TPU v7x, 32 devices: a whole 2x2x4 slice. The times are simulated.
32 devices in a mesh: grp: 4 (over y, x), tp: 8 (over z, core).
Axes of the slice: x: 2, y: 2, z: 4, core: 2. Of those that a mesh axis runs over, the one named last changes fastest.
Arguments:
- vision_in: bfloat16 [2048, 3200], P(('grp', 'tp')), may hold values from -6 to 6
- vis_gain: float32 [3200], replicated, may hold values from 0.5 to 2
- first_weight: bfloat16 [3200, 12800], P(None, 'tp'), may hold values from -0.109375 to 0.109375
- second_weight: bfloat16 [12800, 3200], P('tp'), may hold values from -0.0546875 to 0.0546875
- layer_scale: float32 [3200], replicated, may hold values from 0.3 to 1.5
- proj_gain: float32 [12800], replicated, may hold values from 0.5 to 2
- proj_weight: bfloat16 [12800, 8192], P(None, 'tp'), may hold values from -0.0546875 to 0.0546875
- text_embed: bfloat16 [4608, 8192], P('grp', 'tp'), may hold values from -6 to 6
- dest_row: int32 [512], replicated, may hold values from 0 to 4607, as said below
- cotangent: bfloat16 [4608, 8192], P('grp', 'tp'), may hold values from -6 to 6
Outputs:
- seq_embed: bfloat16 [4608, 8192], P('grp', 'tp')
- grad_vision: bfloat16 [2048, 3200], P(('grp', 'tp'))
Inputs may be any that keep to these rules, and one draw needn't show every extreme that they name: `dest_row`: all values distinct. Sequence h is rows h * 1152 to (h + 1) * 1152 - 1. The 128 merged rows of index g of grp form four images of 32 rows each; each image fills consecutive token rows of its own sequence, four different sequences for one index of grp, inside positions g * (288) to (g + 1) * 288 - 1 of that sequence. Image j of index g goes to sequence (g + k_j) mod 4 with four distinct shifts k_j common to all g, among them 1 and 2; so at most, and exactly, 32 rows go from one index of grp to one sequence, and every sequence receives four images from four different indices of grp.
All inputs are finite; a program needn't handle non-finite values.
Results may differ from a plain program's by a relative error of at most 0.025.
Values may be sent and summed in bfloat16 or wider, within the bound.
No kernel may reach another device: no remote copies, remote signals or barrier semaphores. Data moves between devices by JAX's collectives and lax.ppermute only.
A program may use at most 128 MiB of HBM per device.

v0:
```python
import jax
import jax.numpy as jnp
from jax import lax
from jax.sharding import PartitionSpec as P

vis_eps = 1e-06
proj_eps = 1e-05


def layer_norm(values, scale_vec, epsilon):
    mean_val = jnp.mean(values, -1, keepdims=True)
    centred = values - mean_val
    inv_std = lax.rsqrt(jnp.mean(centred * centred, -1, keepdims=True) + epsilon)
    normed = centred * inv_std
    return (normed * scale_vec, normed, inv_std)


def norm_back(upstream, scale_vec, normed, inv_std):
    scaled = upstream * scale_vec
    return inv_std * (
        scaled
        - jnp.mean(scaled, -1, keepdims=True)
        - normed * jnp.mean(scaled * normed, -1, keepdims=True)
    )


def gelu_slope(values):
    cumul = 0.5 * (1.0 + lax.erf(values * 0.7071067811865476))
    dense = jnp.exp(-0.5 * values * values) * 0.3989422804014327
    return cumul + values * dense


def times_transposed(left, right):
    return lax.dot_general(
        left, right, (((1,), (1,)), ((), ())), preferred_element_type=jnp.float32
    )


def run_ranks(targets):
    length = targets.shape[-1]
    same = targets[:, :, None] == targets[:, None, :]
    earlier = jnp.arange(length)[None, :] < jnp.arange(length)[:, None]
    return jnp.sum(jnp.logical_and(same, earlier[None]), -1)


def per_device(
    vision_in,
    vis_gain,
    first_weight,
    second_weight,
    layer_scale,
    proj_gain,
    proj_weight,
    text_embed,
    dest_row,
    cotangent,
):
    own_rows = vision_in.shape[0]
    groups = lax.axis_size("grp")
    tp_rank = lax.axis_index("tp")
    grp_rank = lax.axis_index("grp")
    seq_len = text_embed.shape[0]
    width = proj_weight.shape[1]
    merged_width = proj_gain.shape[0]
    vis_width = vis_gain.shape[0]
    merged_total = dest_row.shape[0] // groups
    capacity = merged_total // 4
    merged_own = own_rows // 4
    own_float = vision_in.astype(jnp.float32)
    own_parts = layer_norm(own_float, vis_gain, vis_eps)
    own_hat = own_parts[1]
    own_inv = own_parts[2]
    patches = lax.all_gather(vision_in, "tp", axis=0, tiled=True)
    patch_float = patches.astype(jnp.float32)
    normed_in = layer_norm(patch_float, vis_gain, vis_eps)[0].astype(jnp.bfloat16)
    first_pre = jnp.dot(normed_in, first_weight, preferred_element_type=jnp.float32)
    hidden = jax.nn.gelu(first_pre, approximate=False).astype(jnp.bfloat16)
    summed = lax.psum_scatter(
        jnp.dot(hidden, second_weight, preferred_element_type=jnp.float32).astype(jnp.bfloat16),
        "tp",
        scatter_dimension=0,
        tiled=True,
    ).astype(jnp.float32)
    outputs = (own_float + layer_scale * summed).astype(jnp.bfloat16)
    merged = lax.all_gather(outputs.reshape(merged_own, merged_width), "tp", axis=0, tiled=True)
    merged_norm, merged_hat, merged_inv = layer_norm(
        merged.astype(jnp.float32), proj_gain, proj_eps
    )
    proj_pre = jnp.dot(
        merged_norm.astype(jnp.bfloat16), proj_weight, preferred_element_type=jnp.float32
    )
    projected = jax.nn.gelu(proj_pre, approximate=False).astype(jnp.bfloat16)
    all_dest = dest_row.reshape(groups, merged_total)
    all_seq = all_dest // seq_len
    all_pos = all_dest % seq_len
    all_rank = run_ranks(all_seq)
    mine_seq = lax.dynamic_index_in_dim(all_seq, grp_rank, 0, False)
    mine_rank = lax.dynamic_index_in_dim(all_rank, grp_rank, 0, False)
    outgoing = (
        jnp.zeros((groups, capacity, width), jnp.bfloat16).at[mine_seq, mine_rank].set(projected)
    )
    arrived = lax.all_to_all(outgoing, "grp", split_axis=0, concat_axis=0, tiled=True)
    slot_rank = jnp.where(all_seq == grp_rank, all_rank, capacity)
    sources = jnp.broadcast_to(jnp.arange(groups, dtype=jnp.int32)[:, None], all_seq.shape)
    targets = (
        jnp.full((groups, capacity), seq_len, jnp.int32)
        .at[sources, slot_rank]
        .set(all_pos, mode="drop")
    )
    flat_targets = targets.reshape(-1)
    seq_embed = text_embed.at[flat_targets].set(arrived.reshape(-1, width), mode="drop")
    live = flat_targets < seq_len
    picked = jnp.take(cotangent, jnp.minimum(flat_targets, seq_len - 1), axis=0)
    picked = jnp.where(live[:, None], picked, jnp.zeros_like(picked)).reshape(
        groups, capacity, width
    )
    returned = lax.all_to_all(picked, "grp", split_axis=0, concat_axis=0, tiled=True)
    grad_proj = returned[mine_seq, mine_rank]
    proj_delta = (grad_proj.astype(jnp.float32) * gelu_slope(proj_pre)).astype(jnp.bfloat16)
    back_sum = lax.psum_scatter(
        times_transposed(proj_delta, proj_weight).astype(jnp.bfloat16),
        "tp",
        scatter_dimension=0,
        tiled=True,
    ).astype(jnp.float32)
    hat_mine = lax.dynamic_slice_in_dim(merged_hat, tp_rank * merged_own, merged_own, 0)
    inv_mine = lax.dynamic_slice_in_dim(merged_inv, tp_rank * merged_own, merged_own, 0)
    merged_grad = norm_back(back_sum, proj_gain, hat_mine, inv_mine).astype(jnp.bfloat16)
    own_grad = merged_grad.reshape(own_rows, vis_width)
    grad_out = lax.all_gather(own_grad, "tp", axis=0, tiled=True)
    scaled_grad = (grad_out.astype(jnp.float32) * layer_scale).astype(jnp.bfloat16)
    hidden_grad = times_transposed(scaled_grad, second_weight)
    first_delta = (hidden_grad * gelu_slope(first_pre)).astype(jnp.bfloat16)
    normed_grad = lax.psum_scatter(
        times_transposed(first_delta, first_weight).astype(jnp.bfloat16),
        "tp",
        scatter_dimension=0,
        tiled=True,
    ).astype(jnp.float32)
    grad_vision = (
        own_grad.astype(jnp.float32) + norm_back(normed_grad, vis_gain, own_hat, own_inv)
    ).astype(jnp.bfloat16)
    return (seq_embed, grad_vision)


def solution(mesh):
    placed = (
        P(("grp", "tp"), None),
        P(),
        P(None, "tp"),
        P("tp", None),
        P(),
        P(),
        P(None, "tp"),
        P("grp", "tp"),
        P(),
        P("grp", "tp"),
    )
    return jax.shard_map(
        per_device,
        mesh=mesh,
        in_specs=placed,
        out_specs=(P("grp", "tp"), P(("grp", "tp"), None)),
        check_vma=False,
    )
```

profile of v0, /device:TPU:0, one launch (start us, length us, event | category | flops | bytes accessed | tf_op | source)
XLA Modules:
  0.0 349.9 jit_solution(13138204232093086160)
XLA Ops:
  7.2 0.0 copy-start
  7.2 0.0 all-gather.4.cloned.1.call-start
  7.2 3.4 copy.16
  10.7 0.0 all-gather.4.cloned.1.call-update
  10.7 0.0 reduce-scatter.4.cloned.1.call-start
  10.7 42.2 %all-gather.4.cloned.1.call-done = bf16[512,3200]{1,0:T(8,128)(2,1)} async-done(((bf16[64,3200]{1,0:T(8,128)(2,1)}), bf16[512,3200]{1,0:T(8,128)(2,1)}) %all-gather.4.cloned.1.call-update) | async-done | bytes 3276816 | tf_op jit(solution)/shard_map/all_gather | solution.py:73
  52.9 2.6 convert_reduce_fusion.1
  55.5 0.3 copy-done.3
  55.8 1.0 fusion.5
  56.8 0.0 copy-done.7
  56.8 0.0 slice-start.1
  56.8 0.0 slice-start.2
  56.8 9.1 %fusion.16 = f32[512,1600]{0,1:T(8,128)S(1)} fusion(bf16[3200,1600]{0,1:T(8,128)(2,1)} %param.12, bf16[512,3200]{1,0:T(8,128)(2,1)S(1)} %copy-done.3, f32[3200]{0:T(1024)S(1)} %copy-done.7, f32[512]{0:T(512)S(1)} %add_rsqrt_fusion, f32[512]{0:T(512)S(1)} %broadcast_multiply_fusion), kind=kOutput, calls=%fused_computation.33 | convolution fusion | flops 5251072000 | bytes 16810496 | tf_op jit(solution)/shard_map/dot_general | solution.py:76
  65.9 0.0 copy-start.10
  66.0 1.7 copy-done.10
  67.7 0.0 slice-done.2
  67.7 14.1 %convolution_convert_fusion.2 = bf16[512,3200]{1,0:T(8,128)(2,1)} fusion(bf16[1600,3200]{1,0:T(8,128)(2,1)S(1)} %bitcast.72, f32[512,1600]{0,1:T(8,128)S(1)} %fusion.16), kind=kOutput, calls=%fused_computation.21 | convolution fusion | flops 5297766400 | bytes 16793600 | tf_op jit(solution)/shard_map/dot_general | solution.py:79
  81.8 0.0 reduce-scatter.4.cloned.1.call-update
  81.8 0.0 all-gather.6.cloned.1.call-start
  81.9 0.9 copy-done.4
  82.8 0.2 convert_reduce_fusion.2
  82.9 39.2 %reduce-scatter.4.cloned.1.call-done = bf16[64,3200]{1,0:T(8,128)(2,1)} async-done(((bf16[512,3200]{1,0:T(8,128)(2,1)}), bf16[64,3200]{1,0:T(8,128)(2,1)}) %reduce-scatter.4.cloned.1.call-update) | async-done | bytes 409616 | tf_op jit(solution)/shard_map/reduce_scatter | solution.py:78
  122.2 1.3 fusion.71
  123.5 1.1 reshape.340
  124.6 0.0 all-gather.6.cloned.1.call-update
  124.7 0.0 copy-done.9
  124.7 0.2 convert_reduce_fusion.3
  125.0 22.7 %scatter_fusion = s32[4,32]{1,0:T(4,128)S(1)} fusion(s32[4,32]{1,0:T(4,128)S(1)} %broadcast_in_dim.22, s32[512]{0:T(512)S(1)} %fusion.100, s32[512]{0:T(512)S(1)} %get-tuple-element.12), kind=kCustom, calls=%fused_computation.2 | custom fusion | bytes 10240 | tf_op jit(solution)/shard_map/scatter | solution.py:108
  147.7 0.1 reshape.339
  147.8 0.9 gather_fusion
  148.7 0.8 select_select_fusion
  149.5 3.7 %all-to-all-start.1 = ((bf16[4,32,1024]{2,1,0:T(8,128)(2,1)}), bf16[4,32,1024]{2,1,0:T(8,128)(2,1)S(1)}, u32[]{:S(2)}, u32[]{:S(2)}) async-start(bf16[4,32,1024]{2,1,0:T(8,128)(2,1)} %select_select_fusion), calls=%async_computation.2 | async-start | bytes 524288 | tf_op jit(solution)/shard_map/all_to_all | solution.py:117
  153.1 0.0 reduce-scatter.6.cloned.1.call-start
  153.1 5.4 %all-to-all-done.1 = bf16[4,32,1024]{2,1,0:T(8,128)(2,1)S(1)} async-done(((bf16[4,32,1024]{2,1,0:T(8,128)(2,1)}), bf16[4,32,1024]{2,1,0:T(8,128)(2,1)S(1)}, u32[]{:S(2)}, u32[]{:S(2)}) %all-to-all-start.1) | async-done | bytes 262176 | tf_op jit(solution)/shard_map/all_to_all | solution.py:117
  158.5 1.7 gather_fusion.1
  160.1 2.8 all-gather.6.cloned.1.call-done
  162.9 2.6 convert_reduce_fusion
  165.5 0.3 copy-done.2
  165.9 1.1 fusion.4
  166.9 11.1 %fusion.77 = (bf16[128,1024]{1,0:T(8,128)(2,1)S(1)}, f32[128,1024]{1,0:T(8,128)S(1)}) fusion(bf16[12800,1024]{1,0:T(8,128)(2,1)} %param.16, f32[12800]{0:T(1024)S(1)} %copy-done.6, f32[128]{0:T(128)S(1)} %add_rsqrt_fusion.2, f32[128]{0:T(128)S(1)} %broadcast_multiply_fusion.6, bf16[128,12800]{1,0:T(8,128)(2,1)S(1)} %copy-done.2), kind=kOutput, calls=%fused_computation.109 | convolution fusion | flops 3372154880 | bytes 30329856 | tf_op jit(solution)/shard_map/dot_general | solution.py:89
  178.0 15.0 %convolution_convert_fusion = bf16[128,12800]{1,0:T(8,128)(2,1)} fusion(bf16[12800,1024]{1,0:T(8,128)(2,1)} %param.16, f32[128,1024]{1,0:T(8,128)S(1)} %get-tuple-element.17, bf16[128,1024]{1,0:T(8,128)(2,1)S(1)} %gather_fusion.1), kind=kOutput, calls=%fused_computation.5 | convolution fusion | flops 3358523392 | bytes 30277632 | tf_op jit(solution)/shard_map/dot_general | solution.py:34
  193.0 0.0 reduce-scatter.6.cloned.1.call-update
  193.0 0.0 all-gather.8.cloned.1.call-start
  193.0 0.1 dynamic-slice.3
  193.1 5.6 %fusion.2 = f32[128,12800]{1,0:T(8,128)} fusion(bf16[128,12800]{1,0:T(8,128)(2,1)} %all-gather.6.cloned.1.call-done, f32[128]{0:T(128)S(1)} %add_rsqrt_fusion.2, f32[128]{0:T(128)S(1)} %broadcast_multiply_fusion.6), kind=kLoop, calls=%fused_computation.12 | loop fusion | flops 4915200 | bytes 9831424 | tf_op jit(solution)/shard_map/mul | solution.py:14
  198.8 34.6 %reduce-scatter.6.cloned.1.call-done = bf16[16,12800]{1,0:T(8,128)(2,1)} async-done(((bf16[128,12800]{1,0:T(8,128)(2,1)}), bf16[16,12800]{1,0:T(8,128)(2,1)}) %reduce-scatter.6.cloned.1.call-update) | async-done | bytes 409616 | tf_op jit(solution)/shard_map/reduce_scatter | solution.py:120
  233.3 1.5 fusion.74
  234.9 1.5 multiply_convert_fusion.6
  236.4 1.1 reshape.342
  237.5 0.0 all-gather.8.cloned.1.call-update
  237.5 0.3 reduce-scatter.8.cloned.1.call-start
  237.7 38.0 %all-gather.8.cloned.1.call-done = bf16[512,3200]{1,0:T(8,128)(2,1)} async-done(((bf16[64,3200]{1,0:T(8,128)(2,1)}), bf16[512,3200]{1,0:T(8,128)(2,1)}) %all-gather.8.cloned.1.call-update) | async-done | bytes 3276816 | tf_op jit(solution)/shard_map/all_gather | solution.py:130
  275.8 11.7 %fusion.30 = bf16[512,1600]{0,1:T(8,128)(2,1)S(1)} fusion(f32[512,1600]{0,1:T(8,128)} %copy-done.10, bf16[1600,3200]{1,0:T(8,128)(2,1)} %param.13, bf16[512,3200]{1,0:T(8,128)(2,1)} %all-gather.8.cloned.1.call-done, f32[3200]{0:T(1024)S(1)} %copy-done.8), kind=kOutput, calls=%fused_computation.54 | convolution fusion | flops 5255987200 | bytes 18444800 | tf_op jit(solution)/shard_map/dot_general | solution.py:34
  287.5 11.7 %convolution_convert_fusion.1 = bf16[512,3200]{1,0:T(8,128)(2,1)} fusion(bf16[512,1600]{0,1:T(8,128)(2,1)S(1)} %fusion.30, bf16[3200,1600]{0,1:T(8,128)(2,1)} %param.12), kind=kOutput, calls=%fused_computation.20 | convolution fusion | flops 5244518400 | bytes 15155200 | tf_op jit(solution)/shard_map/dot_general | solution.py:34
  299.2 0.0 reduce-scatter.8.cloned.1.call-update
  299.2 0.7 broadcast_in_dim.25
  299.9 19.8 %scatter_fusion.1 = bf16[4,32,1024]{2,1,0:T(8,128)(2,1)} fusion(bf16[4,32,1024]{2,1,0:T(8,128)(2,1)} %broadcast_in_dim.25, s32[128]{0:T(128)S(1)} %get-tuple-element.9, bf16[128,1024]{1,0:T(8,128)(2,1)S(1)} %get-tuple-element.16), kind=kCustom, calls=%fused_computation.3 | custom fusion | bytes 787456 | tf_op jit(solution)/shard_map/scatter | solution.py:100
  319.7 3.8 %all-to-all-start = ((bf16[4,32,1024]{2,1,0:T(8,128)(2,1)}), bf16[4,32,1024]{2,1,0:T(8,128)(2,1)S(1)}, u32[]{:S(2)}, u32[]{:S(2)}) async-start(bf16[4,32,1024]{2,1,0:T(8,128)(2,1)} %scatter_fusion.1), calls=%async_computation.1 | async-start | bytes 524288 | tf_op jit(solution)/shard_map/all_to_all | solution.py:102
  323.5 5.8 %all-to-all-done = bf16[4,32,1024]{2,1,0:T(8,128)(2,1)S(1)} async-done(((bf16[4,32,1024]{2,1,0:T(8,128)(2,1)}), bf16[4,32,1024]{2,1,0:T(8,128)(2,1)S(1)}, u32[]{:S(2)}, u32[]{:S(2)}) %all-to-all-start) | async-done | bytes 262176 | tf_op jit(solution)/shard_map/all_to_all | solution.py:102
  329.3 4.8 %scatter_fusion.2 = bf16[1152,1024]{1,0:T(8,128)(2,1)} fusion(bf16[1152,1024]{1,0:T(8,128)(2,1)} %copy.16, s32[128]{0:T(128)S(1)} %get-tuple-element.15, bf16[128,1024]{1,0:T(8,128)(2,1)S(1)} %bitcast.69), kind=kCustom, calls=%fused_computation.4 | custom fusion | bytes 786944 | tf_op jit(solution)/shard_map/scatter | solution.py:111
  334.0 5.5 %reduce-scatter.8.cloned.1.call-done = bf16[64,3200]{1,0:T(8,128)(2,1)} async-done(((bf16[512,3200]{1,0:T(8,128)(2,1)}), bf16[64,3200]{1,0:T(8,128)(2,1)}) %reduce-scatter.8.cloned.1.call-update) | async-done | bytes 409616 | tf_op jit(solution)/shard_map/reduce_scatter | solution.py:134
  339.5 1.3 fusion.73
  340.9 2.1 fusion.70
  343.0 0.0 copy-done.1
  (34 shorter events, 0.2 us)
Async XLA Ops:
  7.2 140.6 %copy-start = (bf16[1152,1024]{1,0:T(8,128)(2,1)S(1)}, bf16[1152,1024]{1,0:T(8,128)(2,1)}, u32[]{:S(2)}) copy-start(bf16[1152,1024]{1,0:T(8,128)(2,1)} %param.19) | copy-start | bytes 7077892
  7.2 45.7 %all-gather.4.cloned.1.call-start = ((), (), s32[]{:S(2)}) async-start(), calls=%async_computation.5 | async-start | bytes 3686400 | tf_op jit(solution)/shard_map/all_gather | solution.py:73
  10.7 46.2 %copy-start.7 = (f32[3200]{0:T(1024)S(1)}, f32[3200]{0:T(1024)}, u32[]{:S(2)}) copy-start(f32[3200]{0:T(1024)} %param.11) | copy-start | bytes 38404
  10.7 111.5 %reduce-scatter.4.cloned.1.call-start = ((), (), s32[]{:S(2)}) async-start(), calls=%async_computation.6 | async-start | bytes 3686400 | tf_op jit(solution)/shard_map/reduce_scatter | solution.py:78
  52.9 2.9 copy-start.3
  55.8 11.9 %slice-start = ((s8[10240000]{0:T(1024)(128)(4,1)}), s8[4194304]{0:T(1024)(128)(4,1)S(1)}, s32[]{:S(2)}) async-start(s8[10240000]{0:T(1024)(128)(4,1)} %bitcast.71), calls=%async_computation.11 | async-start | bytes 8388608
  56.8 10.9 %slice-start.1 = ((s8[10240000]{0:T(1024)(128)(4,1)}), s8[4194304]{0:T(1024)(128)(4,1)S(1)}, s32[]{:S(2)}) async-start(s8[10240000]{0:T(1024)(128)(4,1)} %bitcast.71), calls=%async_computation.12 | async-start | bytes 8388608
  56.8 10.9 %slice-start.2 = ((s8[10240000]{0:T(1024)(128)(4,1)}), s8[1851392]{0:T(1024)(128)(4,1)S(1)}, s32[]{:S(2)}) async-start(s8[10240000]{0:T(1024)(128)(4,1)} %bitcast.71), calls=%async_computation.13 | async-start | bytes 3702784
  65.9 1.7 copy-start.10
  81.8 1.0 copy-start.4
  81.8 40.4 %copy-start.8 = (f32[3200]{0:T(1024)S(1)}, f32[3200]{0:T(1024)}, u32[]{:S(2)}) copy-start(f32[3200]{0:T(1024)} %param.14) | copy-start | bytes 38404
  81.8 42.9 %copy-start.9 = (s32[512]{0:T(512)S(1)}, s32[512]{0:T(512)}, u32[]{:S(2)}) copy-start(s32[512]{0:T(512)} %param.18) | copy-start | bytes 6148
  81.8 81.1 %all-gather.6.cloned.1.call-start = ((), (), s32[]{:S(2)}) async-start(), calls=%async_computation.7 | async-start | bytes 3686400 | tf_op jit(solution)/shard_map/all_gather | solution.py:85
  149.5 9.0 %all-to-all-start.1 = ((bf16[4,32,1024]{2,1,0:T(8,128)(2,1)}), bf16[4,32,1024]{2,1,0:T(8,128)(2,1)S(1)}, u32[]{:S(2)}, u32[]{:S(2)}) async-start(bf16[4,32,1024]{2,1,0:T(8,128)(2,1)} %select_select_fusion), calls=%async_computation.2 | async-start | bytes 524288 | tf_op jit(solution)/shard_map/all_to_all | solution.py:117
  153.1 80.2 %reduce-scatter.6.cloned.1.call-start = ((), (), s32[]{:S(2)}) async-start(), calls=%async_computation.8 | async-start | bytes 3686400 | tf_op jit(solution)/shard_map/reduce_scatter | solution.py:120
  162.9 2.9 copy-start.2
  162.9 4.0 %copy-start.6 = (f32[12800]{0:T(1024)S(1)}, f32[12800]{0:T(1024)}, u32[]{:S(2)}) copy-start(f32[12800]{0:T(1024)} %param.15) | copy-start | bytes 153604
  193.0 82.8 %all-gather.8.cloned.1.call-start = ((), (), s32[]{:S(2)}) async-start(), calls=%async_computation.9 | async-start | bytes 3686400 | tf_op jit(solution)/shard_map/all_gather | solution.py:130
  237.5 102.1 %reduce-scatter.8.cloned.1.call-start = ((), (), s32[]{:S(2)}) async-start(), calls=%async_computation.10 | async-start | bytes 3686400 | tf_op jit(solution)/shard_map/reduce_scatter | solution.py:134
  319.7 21.2 %copy-start.5 = (bf16[64,3200]{1,0:T(8,128)(2,1)S(1)}, bf16[64,3200]{1,0:T(8,128)(2,1)}, u32[]{:S(2)}) copy-start(bf16[64,3200]{1,0:T(8,128)(2,1)} %reshape.342) | copy-start | bytes 1228804
  319.7 9.6 %all-to-all-start = ((bf16[4,32,1024]{2,1,0:T(8,128)(2,1)}), bf16[4,32,1024]{2,1,0:T(8,128)(2,1)S(1)}, u32[]{:S(2)}, u32[]{:S(2)}) async-start(bf16[4,32,1024]{2,1,0:T(8,128)(2,1)} %scatter_fusion.1), calls=%async_computation.1 | async-start | bytes 524288 | tf_op jit(solution)/shard_map/all_to_all | solution.py:102
  329.3 13.8 %copy-start.1 = (bf16[1152,1024]{1,0:T(8,128)(2,1)S(1)}, bf16[1152,1024]{1,0:T(8,128)(2,1)}, u32[]{:S(2)}) copy-start(bf16[1152,1024]{1,0:T(8,128)(2,1)} %param.19) | copy-start | bytes 7077892
Sparse Core Ops, SparseCore 0:
  10.8 42.0 all-gather.3
  81.9 40.1 reduce-scatter.3
  124.7 38.1 all-gather.5
  193.1 40.1 reduce-scatter.5
  237.6 38.1 all-gather.7
  299.3 40.1 reduce-scatter.7
where the time goes:
time: 351 us; the launch traced here: 350 us
  waiting for transfers between devices  174 us (50%)
  matrix products  72.6 us (21%)
  local copies, waits for them, and re-layouts  59.6 us (17%)
  other arithmetic  22 us (6%)
  between operations  14.3 us (4%)
  starting transfers between devices  7.86 us (2%)
    all_gather x1, waiting for transfers between devices, per_device(): patches = lax.all_gather(vision_in, 'tp', axis=0, tiled=True)  42.2 us
    reduce_scatter x1, waiting for transfers between devices, per_device(): lax.psum_scatter(jnp.dot(hidden, second_weight, preferred_element_type=jn...  39.2 us
    dot_general x3, matrix products, times_transposed(): lax.dot_general(left, right, (((1,), (1,)), ((), ())), preferred_element_...  38.3 us
    all_gather x1, waiting for transfers between devices, per_device(): grad_out = lax.all_gather(own_grad, 'tp', axis=0, tiled=True)  38 us
    reduce_scatter x1, waiting for transfers between devices, per_device(): lax.psum_scatter(times_transposed(proj_delta, proj_weight).astype(jnp.bfl...  34.6 us
    scatter x1, local copies, waits for them, and re-layouts, per_device(): targets = jnp.full((groups, capacity), seq_len, jnp.int32).at[sources, sl...  22.7 us
    scatter x1, local copies, waits for them, and re-layouts, per_device(): jnp.zeros((groups, capacity, width), jnp.bfloat16).at[mine_seq, mine_rank]  19.8 us
    dot_general x1, matrix products, per_device(): jnp.dot(hidden, second_weight, preferred_element_type=jnp.float32)  14.1 us
  transfers between devices with their start and end apart: 8, of which 8 were waited for; matrix products, arithmetic and copies ran while one was open for 16% of the time, Pallas kernels for 0%

commit v1 on v0

v1 whole, which is shorter than its diff:
```python
import jax
import jax.numpy as jnp
from jax import lax
from jax.sharding import PartitionSpec as P

vis_eps = 1e-06
proj_eps = 1e-05
chunks = 2
images = 4
cores = 2


def layer_norm(values, scale_vec, epsilon):
    mean_val = jnp.mean(values, -1, keepdims=True)
    centred = values - mean_val
    inv_std = lax.rsqrt(jnp.mean(centred * centred, -1, keepdims=True) + epsilon)
    normed = centred * inv_std
    return (normed * scale_vec, normed, inv_std)


def norm_back(upstream, scale_vec, normed, inv_std):
    scaled = upstream * scale_vec
    return inv_std * (
        scaled
        - jnp.mean(scaled, -1, keepdims=True)
        - normed * jnp.mean(scaled * normed, -1, keepdims=True)
    )


def gelu_slope(values):
    cumul = 0.5 * (1.0 + lax.erf(values * 0.7071067811865476))
    dense = jnp.exp(-0.5 * values * values) * 0.3989422804014327
    return cumul + values * dense


def times_transposed(left, right):
    return lax.dot_general(
        left, right, (((1,), (1,)), ((), ())), preferred_element_type=jnp.float32
    )


class Line:
    def __init__(self):
        self.places = lax.axis_size("tp") // cores
        rank = lax.axis_index("tp")
        self.place = rank // cores
        self.core = rank % cores
        self.order = sorted(
            range(self.places), key=lambda k: max(k, self.places - k) if k else 0
        )
        self.swap_pairs = [
            (p * cores + c, p * cores + 1 - c) for p in range(self.places) for c in range(cores)
        ]

    def move(self, block, step, sources):
        pairs = [
            (p * cores + c, (p + step) * cores + c) for p in sources for c in range(cores)
        ]
        return lax.ppermute(block, "tp", pairs)

    def swap(self, block):
        return lax.ppermute(block, "tp", self.swap_pairs)

    def gather(self, block):
        n = self.places
        up, down = [block], [block]
        for s in range(1, n):
            up.append(self.move(up[-1], 1, range(s - 1, n - 1)))
            down.append(self.move(down[-1], -1, range(1, n - s + 1)))
        slots = [block] + [
            jnp.where(self.place >= k, up[k], down[n - k]) for k in range(1, n)
        ]
        mine = [slots[k] for k in self.order]
        head = [self.swap(m) for m in mine[:-2]]
        tail = self.swap(jnp.concatenate(mine[-2:], 0))
        return jnp.concatenate(mine + head + [tail], 0), (up[-1], down[-1])

    def scatter(self, partial):
        n = self.places
        half = partial.shape[0] // cores
        got = self.swap(partial[half:])
        both = partial[:half].astype(jnp.float32) + got.astype(jnp.float32)
        both = both.reshape(n, half // n, partial.shape[1])
        part = {k: both[i] for i, k in enumerate(self.order)}

        def travel(step):
            slot = lambda d: part[(-d * step) % n]
            total = slot(n - 1)
            for d in range(n - 1, 0, -1):
                sources = range(n - d) if step == 1 else range(d, n)
                came = self.move(total.astype(jnp.bfloat16), step, sources).astype(jnp.float32)
                total = came + slot(d - 1) if d > 1 else came
            return total

        return part[0] + travel(1) + travel(-1)


def per_device(
    vision_in,
    vis_gain,
    first_weight,
    second_weight,
    layer_scale,
    proj_gain,
    proj_weight,
    text_embed,
    dest_row,
    cotangent,
):
    line = Line()
    groups = lax.axis_size("grp")
    grp_rank = lax.axis_index("grp")
    seq_len, width = text_embed.shape
    merged_total = dest_row.shape[0] // groups
    image_rows = merged_total // images
    own_rows, vis_width = vision_in.shape
    merged_width = proj_gain.shape[0]
    fold = merged_width // vis_width
    merged_own = own_rows // fold
    rows = own_rows // chunks
    merged_rows = rows // fold

    starts = dest_row.reshape(groups, images, image_rows)[:, :, 0]
    start_seq = starts // seq_len
    start_pos = starts % seq_len
    mine_seq = lax.dynamic_index_in_dim(start_seq, grp_rank, 0, False)
    shift = (mine_seq - grp_rank) % groups
    matches = shift[None, :] == jnp.arange(groups)[:, None]
    image_of = jnp.argmax(matches, 1)
    used = jnp.any(matches, 1)
    spot = [start_pos[(grp_rank - s) % groups, image_of[s]] for s in range(groups)]
    span = jnp.arange(image_rows)

    picked = []
    for s in range(groups):
        block = jnp.take(cotangent, spot[s] + span, axis=0)
        if s:
            block = lax.ppermute(block, "grp", [(g, (g - s) % groups) for g in range(groups)])
        picked.append(block)
    returned = jnp.concatenate(picked, 0)

    ordering = jnp.array(line.order)
    held_place = (line.place - ordering) % line.places
    held_core = (line.core + jnp.arange(cores)) % cores
    held_rank = held_place[None, :] * cores + held_core[:, None]
    held_row = held_rank[:, :, None] * merged_own + jnp.arange(merged_rows)
    held_row = held_row.reshape(-1)
    natural = jnp.arange(merged_total)
    rank_of = natural // merged_own
    inside = natural % merged_own
    back_order = jnp.array([line.order.index(k) for k in range(line.places)])
    slot_of = jnp.take(back_order, (line.place - rank_of // cores) % line.places)
    far = (rank_of % cores + line.core) % cores
    row_in = (far * line.places + slot_of) * merged_rows + inside % merged_rows
    row_at = inside // merged_rows * (merged_total // chunks) + row_in

    x, hat, inv, normed = [], [], [], []
    for c in range(chunks):
        x.append(vision_in[c * rows : (c + 1) * rows].astype(jnp.float32))
        scaled, own_hat, own_inv = layer_norm(x[c], vis_gain, vis_eps)
        normed.append(scaled.astype(jnp.bfloat16))
        hat.append(own_hat)
        inv.append(own_inv)

    first_pre, merged_hat, merged_inv, merged_norm = [], [], [], []
    ends = None
    for c in range(chunks):
        block = normed[c]
        if ends is not None:
            block, _ = lax.optimization_barrier((block, ends))
        patches, ends = line.gather(block)
        first_pre.append(jnp.dot(patches, first_weight, preferred_element_type=jnp.float32))
        hidden = jax.nn.gelu(first_pre[c], approximate=False).astype(jnp.bfloat16)
        summed = line.scatter(
            jnp.dot(hidden, second_weight, preferred_element_type=jnp.float32).astype(jnp.bfloat16)
        )
        outputs = (x[c] + layer_scale * summed).astype(jnp.bfloat16)
        merged = outputs.reshape(merged_rows, merged_width).astype(jnp.float32)
        scaled, own_hat, own_inv = layer_norm(merged, proj_gain, proj_eps)
        merged_norm.append(scaled.astype(jnp.bfloat16))
        merged_hat.append(own_hat)
        merged_inv.append(own_inv)

    projected, own_grad = [], []
    for c in range(chunks):
        merged, _ = line.gather(merged_norm[c])
        proj_pre = jnp.dot(merged, proj_weight, preferred_element_type=jnp.float32)
        projected.append(jax.nn.gelu(proj_pre, approximate=False).astype(jnp.bfloat16))
        row = held_row + c * merged_rows
        from_row = jnp.take(shift, row // image_rows) * image_rows + row % image_rows
        grad_proj = jnp.take(returned, from_row, axis=0).astype(jnp.float32)
        proj_delta = (grad_proj * gelu_slope(proj_pre)).astype(jnp.bfloat16)
        back_sum = line.scatter(times_transposed(proj_delta, proj_weight).astype(jnp.bfloat16))
        merged_grad = norm_back(back_sum, proj_gain, merged_hat[c], merged_inv[c])
        own_grad.append(merged_grad.astype(jnp.bfloat16).reshape(rows, vis_width))

    projected = jnp.concatenate(projected, 0)
    seq_embed = text_embed
    for s in range(groups):
        block = jnp.take(projected, jnp.take(row_at, image_of[s] * image_rows + span), axis=0)
        if s:
            block = lax.ppermute(block, "grp", [(g, (g + s) % groups) for g in range(groups)])
        if groups > images:
            there = lax.dynamic_slice_in_dim(seq_embed, spot[s], image_rows, 0)
            block = jnp.where(used[s], block, there)
        seq_embed = lax.dynamic_update_slice_in_dim(seq_embed, block, spot[s], 0)

    grads = []
    for c in range(chunks):
        grad_float = own_grad[c].astype(jnp.float32)
        grad_out, _ = line.gather((grad_float * layer_scale).astype(jnp.bfloat16))
        hidden_grad = times_transposed(grad_out, second_weight)
        first_delta = (hidden_grad * gelu_slope(first_pre[c])).astype(jnp.bfloat16)
        normed_grad = line.scatter(times_transposed(first_delta, first_weight).astype(jnp.bfloat16))
        grads.append(grad_float + norm_back(normed_grad, vis_gain, hat[c], inv[c]))
    grad_vision = jnp.concatenate(grads, 0).astype(jnp.bfloat16)
    return (seq_embed, grad_vision)


def solution(mesh):
    placed = (
        P(("grp", "tp"), None),
        P(),
        P(None, "tp"),
        P("tp", None),
        P(),
        P(),
        P(None, "tp"),
        P("grp", "tp"),
        P(),
        P("grp", "tp"),
    )
    return jax.shard_map(
        per_device,
        mesh=mesh,
        in_specs=placed,
        out_specs=(P("grp", "tp"), P(("grp", "tp"), None)),
        check_vma=False,
    )
```

time: 351 us -> 572 us (1.63); the launches traced: 350 us -> 562 us
  starting transfers between devices: 7.86 us -> 194 us
  matrix products: 72.6 us -> 119 us
  waiting for transfers between devices: 174 us -> 143 us
  other arithmetic: 22 us -> 46.3 us
  local copies, waits for them, and re-layouts: 59.6 us -> 38.5 us
  between operations: 14.3 us -> 20.9 us
    ppermute x0 -> x102, starting transfers between devices: none -> 194 us  [the longest x72 182 us: move(): return lax.ppermute(block, 'tp', pairs)]
    ppermute x0 -> x102, waiting for transfers between devices: none -> 143 us  [the longest x72 132 us: move(): return lax.ppermute(block, 'tp', pairs)]
    all_gather x3 -> x0, waiting for transfers between devices: 83 us -> none  [the longest x1 42.2 us: per_device(): patches = lax.all_gather(vision_in, 'tp', axis=0, tiled=True)]
    reduce_scatter x3 -> x0, waiting for transfers between devices: 79.3 us -> none  [the longest x1 39.2 us: per_device(): lax.psum_scatter(jnp.dot(hidden, second_weight, preferred_element_type=jn...]
    scatter x3 -> x0, local copies, waits for them, and re-layouts: 47.3 us -> none  [the longest x1 22.7 us: per_device(): targets = jnp.full((groups, capacity), seq_len, jnp.int32).at[sources, sl...]
    dot_general x3 -> x4, matrix products: 38.3 us -> 65.2 us  [times_transposed(): lax.dot_general(left, right, (((1,), (1,)), ((), ())), preferred_element_...]
    dot_general x2 -> x4, matrix products: 20.1 us -> 41.1 us  [the longest x2 28.6 us: per_device(): proj_pre = jnp.dot(merged, proj_weight, preferred_element_type=jnp.float32)]
    unnamed x1 -> x25, other arithmetic: 0.01 us -> 15.3 us
  transfers between devices with their start and end apart: 8 -> 102, of which waited for: 8 -> 51; matrix products, arithmetic and copies ran while one was open for 16% -> 13% of each run, Pallas kernels for 0% -> 0%
where the time goes in v1:
time: 572 us; the launch traced here: 562 us
  starting transfers between devices  194 us (34%)
  waiting for transfers between devices  143 us (25%)
  matrix products  119 us (21%)
  other arithmetic  46.3 us (8%)
  local copies, waits for them, and re-layouts  38.5 us (7%)
  between operations  20.9 us (4%)
    ppermute x72, starting transfers between devices, move(): return lax.ppermute(block, 'tp', pairs)  182 us
    ppermute x72, waiting for transfers between devices, move(): return lax.ppermute(block, 'tp', pairs)  132 us
    dot_general x4, matrix products, times_transposed(): lax.dot_general(left, right, (((1,), (1,)), ((), ())), preferred_element_...  65.2 us
    dot_general x2, matrix products, per_device(): proj_pre = jnp.dot(merged, proj_weight, preferred_element_type=jnp.float32)  28.6 us
    unnamed x25, other arithmetic  15.3 us
    dot_general x2, matrix products, per_device(): jnp.dot(hidden, second_weight, preferred_element_type=jnp.float32)  13.2 us
    dot_general x2, matrix products, per_device(): jnp.dot(patches, first_weight, preferred_element_type=jnp.float32)  12.5 us
    unnamed x64, local copies, waits for them, and re-layouts  12.3 us
  transfers between devices with their start and end apart: 102, of which 51 were waited for; matrix products, arithmetic and copies ran while one was open for 13% of the time, Pallas kernels for 0%

profile of v1, /device:TPU:0, one launch (start us, length us, event | category | flops | bytes accessed | tf_op | source)
XLA Modules:
  0.0 562.5 jit_solution(17901665283704688319)
XLA Ops:
  0.7 3.4 copy.55
  7.1 5.8 %collective-permute-start = (bf16[32,3200]{1,0:T(8,128)(2,1)S(1)}, bf16[32,3200]{1,0:T(8,128)(2,1)}, u32[]{:S(2)}, u32[]{:S(2)}) collective-permute-start(bf16[32,3200]{1,0:T(8,128)(2,1)S(1)} %get-tuple-element.89), channel_id=1, source_target_pairs={{0,2},{1,3},{2,4},{3,5},{4,6},{5,7},{8,10},{9,11},{10,12},{11,13},... | collective-permute-start | bytes 614408 | tf_op jit(solution)/shard_map/ppermute | solution.py:59
  25.7 2.0 collective-permute-start.54
  34.5 4.7 collective-permute-done.3
  42.2 4.9 collective-permute-done.4
  52.7 6.7 %fusion.308 = f32[256,1600]{0,1:T(8,128)S(1)} fusion(bf16[256,3200]{1,0:T(8,128)(2,1)} %constant_dynamic-update-slice_fusion, bf16[3200,1600]{0,1:T(8,128)(2,1)} %param.24), kind=kOutput, calls=%fused_computation.640 | convolution fusion | flops 2621440000 | bytes 13516800 | tf_op jit(solution)/shard_map/dot_general | solution.py:172
  59.7 6.6 %convolution_convert_fusion.5 = bf16[256,3200]{1,0:T(8,128)(2,1)S(1)} fusion(bf16[1600,3200]{1,0:T(8,128)(2,1)S(1)} %bitcast.45, f32[256,1600]{0,1:T(8,128)S(1)} %fusion.308), kind=kOutput, calls=%fused_computation.19 | convolution fusion | flops 2648883200 | bytes 13516800 | tf_op jit(solution)/shard_map/dot_general | solution.py:175
  75.8 2.5 collective-permute-start.10
  79.8 3.3 collective-permute-done.10
  84.2 4.3 collective-permute-start.11
  93.4 11.5 %collective-permute-start.12 = (bf16[32,3200]{1,0:T(8,128)(2,1)S(1)}, bf16[32,3200]{1,0:T(8,128)(2,1)S(1)}, u32[]{:S(2)}, u32[]{:S(2)}) collective-permute-start(bf16[32,3200]{1,0:T(8,128)(2,1)S(1)} %get-tuple-element.120), channel_id=1, source_target_pairs={{0,2},{1,3},{2,4},{3,5},{4,6},{5,7},{8,10},{9,11},{10,12},{11,13},... | collective-permute-start | bytes 614408 | tf_op jit(solution)/shard_map/ppermute | solution.py:59
  108.2 4.4 collective-permute-done.15
  116.1 5.2 collective-permute-start.16
  121.4 2.6 compare_and_fusion
  128.3 3.6 collective-permute-done.19
  135.2 4.6 collective-permute-done.20
  142.7 14.3 %fusion.132 = (bf16[64,1024]{1,0:T(8,128)(2,1)}, f32[64,1024]{1,0:T(8,128)S(1)}) fusion(bf16[64,12800]{1,0:T(8,128)(2,1)S(1)} %constant_dynamic-update-slice_fusion.7, bf16[12800,1024]{1,0:T(8,128)(2,1)} %param.28), kind=kOutput, calls=%fused_computation.249 | convolution fusion | flops 1681981440 | bytes 28246016 | tf_op jit(solution)/shard_map/dot_general | solution.py:187
  157.0 13.1 %convolution_convert_fusion.1 = bf16[64,12800]{1,0:T(8,128)(2,1)S(1)} fusion(bf16[12800,1024]{1,0:T(8,128)(2,1)} %param.28, f32[64,1024]{1,0:T(8,128)S(1)} %get-tuple-element.146, bf16[64,1024]{1,0:T(8,128)(2,1)S(1)} %gather_fusion.12, pred[64]{0:T(512)(128)(4,1)S(1)} %get-tuple-element.133), kind=kOutput, calls=%fused_computation.15 | convolution fusion | flops 1679327232 | bytes 28246080 | tf_op jit(solution)/shard_map/dot_general | solution.py:37
  173.9 2.5 collective-permute-start.57
  177.1 3.9 collective-permute-done.57
  181.1 4.4 collective-permute-start.58
  186.2 3.1 collective-permute-done.58
  189.4 10.4 %collective-permute-start.59 = (bf16[8,12800]{1,0:T(8,128)(2,1)S(1)}, bf16[8,12800]{1,0:T(8,128)(2,1)S(1)}, u32[]{:S(2)}, u32[]{:S(2)}) collective-permute-start(bf16[8,12800]{1,0:T(8,128)(2,1)S(1)} %get-tuple-element.114), channel_id=1, source_target_pairs={{0,2},{1,3},{2,4},{3,5},{4,6},{5,7},{8,10},{9,11},{10,12},{11,13},... | collective-permute-start | bytes 614408 | tf_op jit(solution)/shard_map/ppermute | solution.py:59
  201.1 1.9 collective-permute-done.59
  203.0 4.4 collective-permute-done.62
  210.0 4.6 collective-permute-start.63
  218.6 5.4 collective-permute-done.66
  227.1 4.5 collective-permute-done.67
  235.8 19.5 %convolution_convert_fusion.3 = bf16[256,3200]{1,0:T(8,128)(2,1)S(1)} fusion(bf16[3200,1600]{0,1:T(8,128)(2,1)} %param.24, bf16[256,3200]{1,0:T(8,128)(2,1)} %constant_dynamic-update-slice_fusion.28, bf16[1600,3200]{1,0:T(8,128)(2,1)} %param.25, f32[256,1600]{0,1:T(8,128)} %copy-done.17), kind=kOutput, calls=%fused_computation.17 | convolution fusion | flops 5247795200 | bytes 25395200 | tf_op jit(solution)/shard_map/dot_general | solution.py:37
  261.3 4.1 collective-permute-done.73
  265.5 4.4 collective-permute-start.74
  270.6 3.3 collective-permute-done.74
  273.9 10.4 %collective-permute-start.75 = (bf16[32,3200]{1,0:T(8,128)(2,1)S(1)}, bf16[32,3200]{1,0:T(8,128)(2,1)S(1)}, u32[]{:S(2)}, u32[]{:S(2)}) collective-permute-start(bf16[32,3200]{1,0:T(8,128)(2,1)S(1)} %get-tuple-element.108), channel_id=1, source_target_pairs={{0,2},{1,3},{2,4},{3,5},{4,6},{5,7},{8,10},{9,11},{10,12},{11,13},... | collective-permute-start | bytes 614408 | tf_op jit(solution)/shard_map/ppermute | solution.py:59
  285.6 1.9 collective-permute-done.75
  287.5 4.4 collective-permute-done.78
  293.7 4.6 collective-permute-start.25
  302.2 5.5 collective-permute-done.28
  310.0 5.3 collective-permute-done.29
  317.4 5.8 %fusion.309 = f32[256,1600]{0,1:T(8,128)S(1)} fusion(bf16[256,3200]{1,0:T(8,128)(2,1)S(1)} %constant_dynamic-update-slice_fusion.14, bf16[3200,1600]{0,1:T(8,128)(2,1)} %param.24), kind=kOutput, calls=%fused_computation.641 | convolution fusion | flops 2621440000 | bytes 13516800 | tf_op jit(solution)/shard_map/dot_general | solution.py:172
  323.3 6.6 %convolution_convert_fusion.4 = bf16[256,3200]{1,0:T(8,128)(2,1)S(1)} fusion(bf16[1600,3200]{1,0:T(8,128)(2,1)S(1)} %bitcast.47, f32[256,1600]{0,1:T(8,128)S(1)} %fusion.309), kind=kOutput, calls=%fused_computation.18 | convolution fusion | flops 2648883200 | bytes 13516800 | tf_op jit(solution)/shard_map/dot_general | solution.py:175
  330.2 2.2 collective-permute-done.34
  334.8 4.0 collective-permute-done.35
  338.9 4.4 collective-permute-start.36
  344.0 3.2 collective-permute-done.36
  347.3 10.4 %collective-permute-start.37 = (bf16[32,3200]{1,0:T(8,128)(2,1)S(1)}, bf16[32,3200]{1,0:T(8,128)(2,1)S(1)}, u32[]{:S(2)}, u32[]{:S(2)}) collective-permute-start(bf16[32,3200]{1,0:T(8,128)(2,1)S(1)} %get-tuple-element.102), channel_id=1, source_target_pairs={{0,2},{1,3},{2,4},{3,5},{4,6},{5,7},{8,10},{9,11},{10,12},{11,13},... | collective-permute-start | bytes 614408 | tf_op jit(solution)/shard_map/ppermute | solution.py:59
  361.0 4.4 collective-permute-done.40
  368.0 5.2 collective-permute-start.41
  378.0 4.5 collective-permute-done.44
  385.7 4.6 collective-permute-done.45
  393.3 14.3 %fusion.135 = (bf16[64,1024]{1,0:T(8,128)(2,1)}, f32[64,1024]{1,0:T(8,128)S(1)}) fusion(bf16[64,12800]{1,0:T(8,128)(2,1)S(1)} %constant_dynamic-update-slice_fusion.21, bf16[12800,1024]{1,0:T(8,128)(2,1)} %param.28), kind=kOutput, calls=%fused_computation.252 | convolution fusion | flops 1681981440 | bytes 28246016 | tf_op jit(solution)/shard_map/dot_general | solution.py:187
  407.6 13.1 %convolution_convert_fusion = bf16[64,12800]{1,0:T(8,128)(2,1)S(1)} fusion(bf16[12800,1024]{1,0:T(8,128)(2,1)} %param.28, f32[64,1024]{1,0:T(8,128)S(1)} %get-tuple-element.144, bf16[64,1024]{1,0:T(8,128)(2,1)S(1)} %gather_fusion.13, pred[64]{0:T(512)(128)(4,1)S(1)} %get-tuple-element.34), kind=kOutput, calls=%fused_computation.14 | convolution fusion | flops 1679327232 | bytes 28246080 | tf_op jit(solution)/shard_map/dot_general | solution.py:37
  427.4 2.5 collective-permute-start.80
  431.3 3.7 collective-permute-done.80
  435.8 4.3 collective-permute-start.81
  441.5 2.9 collective-permute-done.81
  444.6 10.5 %collective-permute-start.82 = (bf16[8,12800]{1,0:T(8,128)(2,1)S(1)}, bf16[8,12800]{1,0:T(8,128)(2,1)S(1)}, u32[]{:S(2)}, u32[]{:S(2)}) collective-permute-start(bf16[8,12800]{1,0:T(8,128)(2,1)S(1)} %get-tuple-element.96), channel_id=1, source_target_pairs={{0,2},{1,3},{2,4},{3,5},{4,6},{5,7},{8,10},{9,11},{10,12},{11,13},... | collective-permute-start | bytes 614408 | tf_op jit(solution)/shard_map/ppermute | solution.py:59
  458.4 4.4 collective-permute-done.85
  465.4 4.6 collective-permute-start.86
  473.9 5.4 collective-permute-done.89
  482.3 4.7 collective-permute-done.90
  491.1 19.5 %convolution_convert_fusion.2 = bf16[256,3200]{1,0:T(8,128)(2,1)S(1)} fusion(bf16[3200,1600]{0,1:T(8,128)(2,1)} %param.24, bf16[256,3200]{1,0:T(8,128)(2,1)} %constant_dynamic-update-slice_fusion.35, bf16[1600,3200]{1,0:T(8,128)(2,1)} %param.25, f32[256,1600]{0,1:T(8,128)} %copy-done.18), kind=kOutput, calls=%fused_computation.16 | convolution fusion | flops 5247795200 | bytes 25395200 | tf_op jit(solution)/shard_map/dot_general | solution.py:37
  531.5 4.4 collective-permute-start.97
  536.7 2.4 collective-permute-start.52
  540.6 11.0 %collective-permute-start.98 = (bf16[32,3200]{1,0:T(8,128)(2,1)}, bf16[32,3200]{1,0:T(8,128)(2,1)}, u32[]{:S(2)}, u32[]{:S(2)}) collective-permute-start(bf16[32,3200]{1,0:T(8,128)(2,1)} %get-tuple-element.90), channel_id=1, source_target_pairs={{0,2},{1,3},{2,4},{3,5},{4,6},{5,7},{8,10},{9,11},{10,12},{11,13},... | collective-permute-start | bytes 614408 | tf_op jit(solution)/shard_map/ppermute | solution.py:59
  (399 shorter events, 166.6 us)
Async XLA Ops:
  5.3 44.9 %collective-permute-start.6 = (bf16[32,3200]{1,0:T(8,128)(2,1)S(1)}, bf16[32,3200]{1,0:T(8,128)(2,1)S(1)}, u32[]{:S(2)}, u32[]{:S(2)}) collective-permute-start(bf16[32,3200]{1,0:T(8,128)(2,1)S(1)} %get-tuple-element.89), channel_id=1, source_target_pairs={{0,1},{1,0},{2,3},{3,2},{4,5},{5,4},{6,7},{7,6},{8,9},{9,8},{10,11... | collective-permute-start | bytes 614408 | tf_op jit(solution)/shard_map/ppermute | solution.py:62
  5.8 24.5 %collective-permute-start.2 = (bf16[32,3200]{1,0:T(8,128)(2,1)S(1)}, bf16[32,3200]{1,0:T(8,128)(2,1)}, u32[]{:S(2)}, u32[]{:S(2)}) collective-permute-start(bf16[32,3200]{1,0:T(8,128)(2,1)S(1)} %get-tuple-element.89), channel_id=1, source_target_pairs={{2,0},{3,1},{4,2},{5,3},{6,4},{7,5},{10,8},{11,9},{12,10},{13,11},... | collective-permute-start | bytes 614408 | tf_op jit(solution)/shard_map/ppermute | solution.py:59
  7.1 24.6 %collective-permute-start = (bf16[32,3200]{1,0:T(8,128)(2,1)S(1)}, bf16[32,3200]{1,0:T(8,128)(2,1)}, u32[]{:S(2)}, u32[]{:S(2)}) collective-permute-start(bf16[32,3200]{1,0:T(8,128)(2,1)S(1)} %get-tuple-element.89), channel_id=1, source_target_pairs={{0,2},{1,3},{2,4},{3,5},{4,6},{5,7},{8,10},{9,11},{10,12},{11,13},... | collective-permute-start | bytes 614408 | tf_op jit(solution)/shard_map/ppermute | solution.py:59
  25.7 100.9 %collective-permute-start.54 = (bf16[32,1024]{1,0:T(8,128)(2,1)S(1)}, bf16[32,1024]{1,0:T(8,128)(2,1)}, u32[]{:S(2)}, u32[]{:S(2)}) collective-permute-start(bf16[32,1024]{1,0:T(8,128)(2,1)S(1)} %broadcast_select_fusion.19), channel_id=1, source_target_pairs={{0,16},{8,24},{16,0},{24,8},{1,17},{9,25},{17,1},{25,9},{2,18},{10... | collective-permute-start | bytes 196616 | tf_op jit(solution)/shard_map/ppermute | solution.py:138
  30.3 8.9 %collective-permute-start.3 = (bf16[32,3200]{1,0:T(8,128)(2,1)}, bf16[32,3200]{1,0:T(8,128)(2,1)}, u32[]{:S(2)}, u32[]{:S(2)}) collective-permute-start(bf16[32,3200]{1,0:T(8,128)(2,1)} %collective-permute-done.2), channel_id=1, source_target_pairs={{2,0},{3,1},{4,2},{5,3},{10,8},{11,9},{12,10},{13,11},{18,16},{19,... | collective-permute-start | bytes 614408 | tf_op jit(solution)/shard_map/ppermute | solution.py:59
  31.6 8.8 %collective-permute-start.1 = (bf16[32,3200]{1,0:T(8,128)(2,1)}, bf16[32,3200]{1,0:T(8,128)(2,1)}, u32[]{:S(2)}, u32[]{:S(2)}) collective-permute-start(bf16[32,3200]{1,0:T(8,128)(2,1)} %collective-permute-done), channel_id=1, source_target_pairs={{2,4},{3,5},{4,6},{5,7},{10,12},{11,13},{12,14},{13,15},{18,20},{1... | collective-permute-start | bytes 614408 | tf_op jit(solution)/shard_map/ppermute | solution.py:59
  33.1 93.5 %collective-permute-start.53 = (bf16[32,1024]{1,0:T(8,128)(2,1)S(1)}, bf16[32,1024]{1,0:T(8,128)(2,1)}, u32[]{:S(2)}, u32[]{:S(2)}) collective-permute-start(bf16[32,1024]{1,0:T(8,128)(2,1)S(1)} %broadcast_select_fusion.20), channel_id=1, source_target_pairs={{0,24},{8,0},{16,8},{24,16},{1,25},{9,1},{17,9},{25,17},{2,26},{10... | collective-permute-start | bytes 196616 | tf_op jit(solution)/shard_map/ppermute | solution.py:138
  39.2 7.8 %collective-permute-start.4 = (bf16[32,3200]{1,0:T(8,128)(2,1)}, bf16[32,3200]{1,0:T(8,128)(2,1)S(1)}, u32[]{:S(2)}, u32[]{:S(2)}) collective-permute-start(bf16[32,3200]{1,0:T(8,128)(2,1)} %collective-permute-done.3), channel_id=1, source_target_pairs={{2,0},{3,1},{10,8},{11,9},{18,16},{19,17},{26,24},{27,25}} | collective-permute-start | bytes 614408 | tf_op jit(solution)/shard_map/ppermute | solution.py:59
  42.2 8.7 %collective-permute-start.7 = (bf16[32,3200]{1,0:T(8,128)(2,1)S(1)}, bf16[32,3200]{1,0:T(8,128)(2,1)S(1)}, u32[]{:S(2)}, u32[]{:S(2)}) collective-permute-start(bf16[32,3200]{1,0:T(8,128)(2,1)S(1)} %get-tuple-element.87), channel_id=1, source_target_pairs={{0,1},{1,0},{2,3},{3,2},{4,5},{5,4},{6,7},{7,6},{8,9},{9,8},{10,11... | collective-permute-start | bytes 614408 | tf_op jit(solution)/shard_map/ppermute | solution.py:62
  70.7 56.0 %collective-permute-start.55 = (bf16[32,1024]{1,0:T(8,128)(2,1)}, bf16[32,1024]{1,0:T(8,128)(2,1)}, u32[]{:S(2)}, u32[]{:S(2)}) collective-permute-start(bf16[32,1024]{1,0:T(8,128)(2,1)} %broadcast_select_fusion.18), channel_id=1, source_target_pairs={{0,8},{8,16},{16,24},{24,0},{1,9},{9,17},{17,25},{25,1},{2,10},{10... | collective-permute-start | bytes 196616 | tf_op jit(solution)/shard_map/ppermute | solution.py:138
  84.2 8.0 %collective-permute-start.11 = (bf16[32,3200]{1,0:T(8,128)(2,1)S(1)}, bf16[32,3200]{1,0:T(8,128)(2,1)S(1)}, u32[]{:S(2)}, u32[]{:S(2)}) collective-permute-start(bf16[32,3200]{1,0:T(8,128)(2,1)S(1)} %get-tuple-element.122), channel_id=1, source_target_pairs={{0,2},{1,3},{2,4},{3,5},{8,10},{9,11},{10,12},{11,13},{16,18},{17,... | collective-permute-start | bytes 614408 | tf_op jit(solution)/shard_map/ppermute | solution.py:59
  93.4 14.7 %collective-permute-start.12 = (bf16[32,3200]{1,0:T(8,128)(2,1)S(1)}, bf16[32,3200]{1,0:T(8,128)(2,1)S(1)}, u32[]{:S(2)}, u32[]{:S(2)}) collective-permute-start(bf16[32,3200]{1,0:T(8,128)(2,1)S(1)} %get-tuple-element.120), channel_id=1, source_target_pairs={{0,2},{1,3},{2,4},{3,5},{4,6},{5,7},{8,10},{9,11},{10,12},{11,13},... | collective-permute-start | bytes 614408 | tf_op jit(solution)/shard_map/ppermute | solution.py:59
  104.9 7.7 %collective-permute-start.15 = (bf16[32,3200]{1,0:T(8,128)(2,1)S(1)}, bf16[32,3200]{1,0:T(8,128)(2,1)S(1)}, u32[]{:S(2)}, u32[]{:S(2)}) collective-permute-start(bf16[32,3200]{1,0:T(8,128)(2,1)S(1)} %get-tuple-element.121), channel_id=1, source_target_pairs={{2,0},{3,1},{4,2},{5,3},{6,4},{7,5},{10,8},{11,9},{12,10},{13,11},... | collective-permute-start | bytes 614408 | tf_op jit(solution)/shard_map/ppermute | solution.py:59
  114.8 9.1 %collective-permute-start.18 = (bf16[8,12800]{1,0:T(8,128)(2,1)S(1)}, bf16[8,12800]{1,0:T(8,128)(2,1)}, u32[]{:S(2)}, u32[]{:S(2)}) collective-permute-start(bf16[8,12800]{1,0:T(8,128)(2,1)S(1)} %get-tuple-element.79), channel_id=1, source_target_pairs={{2,0},{3,1},{4,2},{5,3},{6,4},{7,5},{10,8},{11,9},{12,10},{13,11},... | collective-permute-start | bytes 614408 | tf_op jit(solution)/shard_map/ppermute | solution.py:59
  116.1 9.1 %collective-permute-start.16 = (bf16[8,12800]{1,0:T(8,128)(2,1)S(1)}, bf16[8,12800]{1,0:T(8,128)(2,1)}, u32[]{:S(2)}, u32[]{:S(2)}) collective-permute-start(bf16[8,12800]{1,0:T(8,128)(2,1)S(1)} %get-tuple-element.79), channel_id=1, source_target_pairs={{0,2},{1,3},{2,4},{3,5},{4,6},{5,7},{8,10},{9,11},{10,12},{11,13},... | collective-permute-start | bytes 614408 | tf_op jit(solution)/shard_map/ppermute | solution.py:59
  123.9 8.0 %collective-permute-start.19 = (bf16[8,12800]{1,0:T(8,128)(2,1)}, bf16[8,12800]{1,0:T(8,128)(2,1)}, u32[]{:S(2)}, u32[]{:S(2)}) collective-permute-start(bf16[8,12800]{1,0:T(8,128)(2,1)} %collective-permute-done.18), channel_id=1, source_target_pairs={{2,0},{3,1},{4,2},{5,3},{10,8},{11,9},{12,10},{13,11},{18,16},{19,... | collective-permute-start | bytes 614408 | tf_op jit(solution)/shard_map/ppermute | solution.py:59
  125.2 7.9 %collective-permute-start.17 = (bf16[8,12800]{1,0:T(8,128)(2,1)}, bf16[8,12800]{1,0:T(8,128)(2,1)}, u32[]{:S(2)}, u32[]{:S(2)}) collective-permute-start(bf16[8,12800]{1,0:T(8,128)(2,1)} %collective-permute-done.16), channel_id=1, source_target_pairs={{2,4},{3,5},{4,6},{5,7},{10,12},{11,13},{12,14},{13,15},{18,20},{1... | collective-permute-start | bytes 614408 | tf_op jit(solution)/shard_map/ppermute | solution.py:59
  128.3 12.7 %collective-permute-start.22 = (bf16[8,12800]{1,0:T(8,128)(2,1)S(1)}, bf16[8,12800]{1,0:T(8,128)(2,1)S(1)}, u32[]{:S(2)}, u32[]{:S(2)}) collective-permute-start(bf16[8,12800]{1,0:T(8,128)(2,1)S(1)} %get-tuple-element.79), channel_id=1, source_target_pairs={{0,1},{1,0},{2,3},{3,2},{4,5},{5,4},{6,7},{7,6},{8,9},{9,8},{10,11... | collective-permute-start | bytes 614408 | tf_op jit(solution)/shard_map/ppermute | solution.py:62
  131.9 7.8 %collective-permute-start.20 = (bf16[8,12800]{1,0:T(8,128)(2,1)}, bf16[8,12800]{1,0:T(8,128)(2,1)S(1)}, u32[]{:S(2)}, u32[]{:S(2)}) collective-permute-start(bf16[8,12800]{1,0:T(8,128)(2,1)} %collective-permute-done.19), channel_id=1, source_target_pairs={{2,0},{3,1},{10,8},{11,9},{18,16},{19,17},{26,24},{27,25}} | collective-permute-start | bytes 614408 | tf_op jit(solution)/shard_map/ppermute | solution.py:59
  181.1 8.2 %collective-permute-start.58 = (bf16[8,12800]{1,0:T(8,128)(2,1)S(1)}, bf16[8,12800]{1,0:T(8,128)(2,1)S(1)}, u32[]{:S(2)}, u32[]{:S(2)}) collective-permute-start(bf16[8,12800]{1,0:T(8,128)(2,1)S(1)} %get-tuple-element.116), channel_id=1, source_target_pairs={{0,2},{1,3},{2,4},{3,5},{8,10},{9,11},{10,12},{11,13},{16,18},{17,... | collective-permute-start | bytes 614408 | tf_op jit(solution)/shard_map/ppermute | solution.py:59
  189.4 13.7 %collective-permute-start.59 = (bf16[8,12800]{1,0:T(8,128)(2,1)S(1)}, bf16[8,12800]{1,0:T(8,128)(2,1)S(1)}, u32[]{:S(2)}, u32[]{:S(2)}) collective-permute-start(bf16[8,12800]{1,0:T(8,128)(2,1)S(1)} %get-tuple-element.114), channel_id=1, source_target_pairs={{0,2},{1,3},{2,4},{3,5},{4,6},{5,7},{8,10},{9,11},{10,12},{11,13},... | collective-permute-start | bytes 614408 | tf_op jit(solution)/shard_map/ppermute | solution.py:59
  199.8 7.7 %collective-permute-start.62 = (bf16[8,12800]{1,0:T(8,128)(2,1)S(1)}, bf16[8,12800]{1,0:T(8,128)(2,1)S(1)}, u32[]{:S(2)}, u32[]{:S(2)}) collective-permute-start(bf16[8,12800]{1,0:T(8,128)(2,1)S(1)} %get-tuple-element.115), channel_id=1, source_target_pairs={{2,0},{3,1},{4,2},{5,3},{6,4},{7,5},{10,8},{11,9},{12,10},{13,11},... | collective-permute-start | bytes 614408 | tf_op jit(solution)/shard_map/ppermute | solution.py:59
  208.8 7.6 %collective-permute-start.65 = (bf16[32,3200]{1,0:T(8,128)(2,1)S(1)}, bf16[32,3200]{1,0:T(8,128)(2,1)S(1)}, u32[]{:S(2)}, u32[]{:S(2)}) collective-permute-start(bf16[32,3200]{1,0:T(8,128)(2,1)S(1)} %get-tuple-element.68), channel_id=1, source_target_pairs={{2,0},{3,1},{4,2},{5,3},{6,4},{7,5},{10,8},{11,9},{12,10},{13,11},... | collective-permute-start | bytes 614408 | tf_op jit(solution)/shard_map/ppermute | solution.py:59
  210.0 7.8 %collective-permute-start.63 = (bf16[32,3200]{1,0:T(8,128)(2,1)S(1)}, bf16[32,3200]{1,0:T(8,128)(2,1)S(1)}, u32[]{:S(2)}, u32[]{:S(2)}) collective-permute-start(bf16[32,3200]{1,0:T(8,128)(2,1)S(1)} %get-tuple-element.68), channel_id=1, source_target_pairs={{0,2},{1,3},{2,4},{3,5},{4,6},{5,7},{8,10},{9,11},{10,12},{11,13},... | collective-permute-start | bytes 614408 | tf_op jit(solution)/shard_map/ppermute | solution.py:59
  216.4 7.6 %collective-permute-start.66 = (bf16[32,3200]{1,0:T(8,128)(2,1)S(1)}, bf16[32,3200]{1,0:T(8,128)(2,1)S(1)}, u32[]{:S(2)}, u32[]{:S(2)}) collective-permute-start(bf16[32,3200]{1,0:T(8,128)(2,1)S(1)} %collective-permute-done.65), channel_id=1, source_target_pairs={{2,0},{3,1},{4,2},{5,3},{10,8},{11,9},{12,10},{13,11},{18,16},{19,... | collective-permute-start | bytes 614408 | tf_op jit(solution)/shard_map/ppermute | solution.py:59
  218.5 14.7 %collective-permute-start.69 = (bf16[32,3200]{1,0:T(8,128)(2,1)S(1)}, bf16[32,3200]{1,0:T(8,128)(2,1)S(1)}, u32[]{:S(2)}, u32[]{:S(2)}) collective-permute-start(bf16[32,3200]{1,0:T(8,128)(2,1)S(1)} %get-tuple-element.68), channel_id=1, source_target_pairs={{0,1},{1,0},{2,3},{3,2},{4,5},{5,4},{6,7},{7,6},{8,9},{9,8},{10,11... | collective-permute-start | bytes 614408 | tf_op jit(solution)/shard_map/ppermute | solution.py:62
  224.0 7.6 %collective-permute-start.67 = (bf16[32,3200]{1,0:T(8,128)(2,1)S(1)}, bf16[32,3200]{1,0:T(8,128)(2,1)S(1)}, u32[]{:S(2)}, u32[]{:S(2)}) collective-permute-start(bf16[32,3200]{1,0:T(8,128)(2,1)S(1)} %collective-permute-done.66), channel_id=1, source_target_pairs={{2,0},{3,1},{10,8},{11,9},{18,16},{19,17},{26,24},{27,25}} | collective-permute-start | bytes 614408 | tf_op jit(solution)/shard_map/ppermute | solution.py:59
  226.1 7.9 %collective-permute-start.70 = (bf16[32,3200]{1,0:T(8,128)(2,1)S(1)}, bf16[32,3200]{1,0:T(8,128)(2,1)S(1)}, u32[]{:S(2)}, u32[]{:S(2)}) collective-permute-start(bf16[32,3200]{1,0:T(8,128)(2,1)S(1)} %get-tuple-element.66), channel_id=1, source_target_pairs={{0,1},{1,0},{2,3},{3,2},{4,5},{5,4},{6,7},{7,6},{8,9},{9,8},{10,11... | collective-permute-start | bytes 614408 | tf_op jit(solution)/shard_map/ppermute | solution.py:62
  265.5 8.4 %collective-permute-start.74 = (bf16[32,3200]{1,0:T(8,128)(2,1)S(1)}, bf16[32,3200]{1,0:T(8,128)(2,1)S(1)}, u32[]{:S(2)}, u32[]{:S(2)}) collective-permute-start(bf16[32,3200]{1,0:T(8,128)(2,1)S(1)} %get-tuple-element.110), channel_id=1, source_target_pairs={{0,2},{1,3},{2,4},{3,5},{8,10},{9,11},{10,12},{11,13},{16,18},{17,... | collective-permute-start | bytes 614408 | tf_op jit(solution)/shard_map/ppermute | solution.py:59
  273.9 13.6 %collective-permute-start.75 = (bf16[32,3200]{1,0:T(8,128)(2,1)S(1)}, bf16[32,3200]{1,0:T(8,128)(2,1)S(1)}, u32[]{:S(2)}, u32[]{:S(2)}) collective-permute-start(bf16[32,3200]{1,0:T(8,128)(2,1)S(1)} %get-tuple-element.108), channel_id=1, source_target_pairs={{0,2},{1,3},{2,4},{3,5},{4,6},{5,7},{8,10},{9,11},{10,12},{11,13},... | collective-permute-start | bytes 614408 | tf_op jit(solution)/shard_map/ppermute | solution.py:59
  284.3 7.7 %collective-permute-start.78 = (bf16[32,3200]{1,0:T(8,128)(2,1)S(1)}, bf16[32,3200]{1,0:T(8,128)(2,1)S(1)}, u32[]{:S(2)}, u32[]{:S(2)}) collective-permute-start(bf16[32,3200]{1,0:T(8,128)(2,1)S(1)} %get-tuple-element.109), channel_id=1, source_target_pairs={{2,0},{3,1},{4,2},{5,3},{6,4},{7,5},{10,8},{11,9},{12,10},{13,11},... | collective-permute-start | bytes 614408 | tf_op jit(solution)/shard_map/ppermute | solution.py:59
  292.4 7.7 %collective-permute-start.27 = (bf16[32,3200]{1,0:T(8,128)(2,1)S(1)}, bf16[32,3200]{1,0:T(8,128)(2,1)S(1)}, u32[]{:S(2)}, u32[]{:S(2)}) collective-permute-start(bf16[32,3200]{1,0:T(8,128)(2,1)S(1)} %fusion.102), channel_id=1, source_target_pairs={{2,0},{3,1},{4,2},{5,3},{6,4},{7,5},{10,8},{11,9},{12,10},{13,11},... | collective-permute-start | bytes 614408 | tf_op jit(solution)/shard_map/ppermute | solution.py:59
  293.7 7.8 %collective-permute-start.25 = (bf16[32,3200]{1,0:T(8,128)(2,1)S(1)}, bf16[32,3200]{1,0:T(8,128)(2,1)S(1)}, u32[]{:S(2)}, u32[]{:S(2)}) collective-permute-start(bf16[32,3200]{1,0:T(8,128)(2,1)S(1)} %fusion.102), channel_id=1, source_target_pairs={{0,2},{1,3},{2,4},{3,5},{4,6},{5,7},{8,10},{9,11},{10,12},{11,13},... | collective-permute-start | bytes 614408 | tf_op jit(solution)/shard_map/ppermute | solution.py:59
  298.3 17.4 %collective-permute-start.31 = (bf16[32,3200]{1,0:T(8,128)(2,1)S(1)}, bf16[32,3200]{1,0:T(8,128)(2,1)S(1)}, u32[]{:S(2)}, u32[]{:S(2)}) collective-permute-start(bf16[32,3200]{1,0:T(8,128)(2,1)S(1)} %fusion.102), channel_id=1, source_target_pairs={{0,1},{1,0},{2,3},{3,2},{4,5},{5,4},{6,7},{7,6},{8,9},{9,8},{10,11... | collective-permute-start | bytes 614408 | tf_op jit(solution)/shard_map/ppermute | solution.py:62
  300.1 7.7 %collective-permute-start.28 = (bf16[32,3200]{1,0:T(8,128)(2,1)S(1)}, bf16[32,3200]{1,0:T(8,128)(2,1)S(1)}, u32[]{:S(2)}, u32[]{:S(2)}) collective-permute-start(bf16[32,3200]{1,0:T(8,128)(2,1)S(1)} %collective-permute-done.27), channel_id=1, source_target_pairs={{2,0},{3,1},{4,2},{5,3},{10,8},{11,9},{12,10},{13,11},{18,16},{19,... | collective-permute-start | bytes 614408 | tf_op jit(solution)/shard_map/ppermute | solution.py:59
  301.5 7.5 %collective-permute-start.26 = (bf16[32,3200]{1,0:T(8,128)(2,1)S(1)}, bf16[32,3200]{1,0:T(8,128)(2,1)S(1)}, u32[]{:S(2)}, u32[]{:S(2)}) collective-permute-start(bf16[32,3200]{1,0:T(8,128)(2,1)S(1)} %collective-permute-done.25), channel_id=1, source_target_pairs={{2,4},{3,5},{4,6},{5,7},{10,12},{11,13},{12,14},{13,15},{18,20},{1... | collective-permute-start | bytes 614408 | tf_op jit(solution)/shard_map/ppermute | solution.py:59
  307.7 7.6 %collective-permute-start.29 = (bf16[32,3200]{1,0:T(8,128)(2,1)S(1)}, bf16[32,3200]{1,0:T(8,128)(2,1)S(1)}, u32[]{:S(2)}, u32[]{:S(2)}) collective-permute-start(bf16[32,3200]{1,0:T(8,128)(2,1)S(1)} %collective-permute-done.28), channel_id=1, source_target_pairs={{2,0},{3,1},{10,8},{11,9},{18,16},{19,17},{26,24},{27,25}} | collective-permute-start | bytes 614408 | tf_op jit(solution)/shard_map/ppermute | solution.py:59
  338.9 8.3 %collective-permute-start.36 = (bf16[32,3200]{1,0:T(8,128)(2,1)S(1)}, bf16[32,3200]{1,0:T(8,128)(2,1)S(1)}, u32[]{:S(2)}, u32[]{:S(2)}) collective-permute-start(bf16[32,3200]{1,0:T(8,128)(2,1)S(1)} %get-tuple-element.104), channel_id=1, source_target_pairs={{0,2},{1,3},{2,4},{3,5},{8,10},{9,11},{10,12},{11,13},{16,18},{17,... | collective-permute-start | bytes 614408 | tf_op jit(solution)/shard_map/ppermute | solution.py:59
  347.3 13.7 %collective-permute-start.37 = (bf16[32,3200]{1,0:T(8,128)(2,1)S(1)}, bf16[32,3200]{1,0:T(8,128)(2,1)S(1)}, u32[]{:S(2)}, u32[]{:S(2)}) collective-permute-start(bf16[32,3200]{1,0:T(8,128)(2,1)S(1)} %get-tuple-element.102), channel_id=1, source_target_pairs={{0,2},{1,3},{2,4},{3,5},{4,6},{5,7},{8,10},{9,11},{10,12},{11,13},... | collective-permute-start | bytes 614408 | tf_op jit(solution)/shard_map/ppermute | solution.py:59
  357.8 7.7 %collective-permute-start.40 = (bf16[32,3200]{1,0:T(8,128)(2,1)S(1)}, bf16[32,3200]{1,0:T(8,128)(2,1)S(1)}, u32[]{:S(2)}, u32[]{:S(2)}) collective-permute-start(bf16[32,3200]{1,0:T(8,128)(2,1)S(1)} %get-tuple-element.103), channel_id=1, source_target_pairs={{2,0},{3,1},{4,2},{5,3},{6,4},{7,5},{10,8},{11,9},{12,10},{13,11},... | collective-permute-start | bytes 614408 | tf_op jit(solution)/shard_map/ppermute | solution.py:59
  366.7 7.8 %collective-permute-start.43 = (bf16[8,12800]{1,0:T(8,128)(2,1)S(1)}, bf16[8,12800]{1,0:T(8,128)(2,1)}, u32[]{:S(2)}, u32[]{:S(2)}) collective-permute-start(bf16[8,12800]{1,0:T(8,128)(2,1)S(1)} %get-tuple-element.51), channel_id=1, source_target_pairs={{2,0},{3,1},{4,2},{5,3},{6,4},{7,5},{10,8},{11,9},{12,10},{13,11},... | collective-permute-start | bytes 614408 | tf_op jit(solution)/shard_map/ppermute | solution.py:59
  368.0 7.8 %collective-permute-start.41 = (bf16[8,12800]{1,0:T(8,128)(2,1)S(1)}, bf16[8,12800]{1,0:T(8,128)(2,1)}, u32[]{:S(2)}, u32[]{:S(2)}) collective-permute-start(bf16[8,12800]{1,0:T(8,128)(2,1)S(1)} %get-tuple-element.51), channel_id=1, source_target_pairs={{0,2},{1,3},{2,4},{3,5},{4,6},{5,7},{8,10},{9,11},{10,12},{11,13},... | collective-permute-start | bytes 614408 | tf_op jit(solution)/shard_map/ppermute | solution.py:59
  374.5 8.0 %collective-permute-start.44 = (bf16[8,12800]{1,0:T(8,128)(2,1)}, bf16[8,12800]{1,0:T(8,128)(2,1)}, u32[]{:S(2)}, u32[]{:S(2)}) collective-permute-start(bf16[8,12800]{1,0:T(8,128)(2,1)} %collective-permute-done.43), channel_id=1, source_target_pairs={{2,0},{3,1},{4,2},{5,3},{10,8},{11,9},{12,10},{13,11},{18,16},{19,... | collective-permute-start | bytes 614408 | tf_op jit(solution)/shard_map/ppermute | solution.py:59
  375.8 7.9 %collective-permute-start.42 = (bf16[8,12800]{1,0:T(8,128)(2,1)}, bf16[8,12800]{1,0:T(8,128)(2,1)}, u32[]{:S(2)}, u32[]{:S(2)}) collective-permute-start(bf16[8,12800]{1,0:T(8,128)(2,1)} %collective-permute-done.41), channel_id=1, source_target_pairs={{2,4},{3,5},{4,6},{5,7},{10,12},{11,13},{12,14},{13,15},{18,20},{1... | collective-permute-start | bytes 614408 | tf_op jit(solution)/shard_map/ppermute | solution.py:59
  377.9 13.6 %collective-permute-start.47 = (bf16[8,12800]{1,0:T(8,128)(2,1)S(1)}, bf16[8,12800]{1,0:T(8,128)(2,1)S(1)}, u32[]{:S(2)}, u32[]{:S(2)}) collective-permute-start(bf16[8,12800]{1,0:T(8,128)(2,1)S(1)} %get-tuple-element.51), channel_id=1, source_target_pairs={{0,1},{1,0},{2,3},{3,2},{4,5},{5,4},{6,7},{7,6},{8,9},{9,8},{10,11... | collective-permute-start | bytes 614408 | tf_op jit(solution)/shard_map/ppermute | solution.py:62
  382.4 7.8 %collective-permute-start.45 = (bf16[8,12800]{1,0:T(8,128)(2,1)}, bf16[8,12800]{1,0:T(8,128)(2,1)S(1)}, u32[]{:S(2)}, u32[]{:S(2)}) collective-permute-start(bf16[8,12800]{1,0:T(8,128)(2,1)} %collective-permute-done.44), channel_id=1, source_target_pairs={{2,0},{3,1},{10,8},{11,9},{18,16},{19,17},{26,24},{27,25}} | collective-permute-start | bytes 614408 | tf_op jit(solution)/shard_map/ppermute | solution.py:59
  427.4 7.6 %collective-permute-start.80 = (bf16[8,12800]{1,0:T(8,128)(2,1)}, bf16[8,12800]{1,0:T(8,128)(2,1)S(1)}, u32[]{:S(2)}, u32[]{:S(2)}) collective-permute-start(bf16[8,12800]{1,0:T(8,128)(2,1)} %get-tuple-element.100), channel_id=1, source_target_pairs={{0,2},{1,3},{8,10},{9,11},{16,18},{17,19},{24,26},{25,27}} | collective-permute-start | bytes 614408 | tf_op jit(solution)/shard_map/ppermute | solution.py:59
  435.8 8.6 %collective-permute-start.81 = (bf16[8,12800]{1,0:T(8,128)(2,1)}, bf16[8,12800]{1,0:T(8,128)(2,1)S(1)}, u32[]{:S(2)}, u32[]{:S(2)}) collective-permute-start(bf16[8,12800]{1,0:T(8,128)(2,1)} %get-tuple-element.98), channel_id=1, source_target_pairs={{0,2},{1,3},{2,4},{3,5},{8,10},{9,11},{10,12},{11,13},{16,18},{17,... | collective-permute-start | bytes 614408 | tf_op jit(solution)/shard_map/ppermute | solution.py:59
  444.6 13.8 %collective-permute-start.82 = (bf16[8,12800]{1,0:T(8,128)(2,1)S(1)}, bf16[8,12800]{1,0:T(8,128)(2,1)S(1)}, u32[]{:S(2)}, u32[]{:S(2)}) collective-permute-start(bf16[8,12800]{1,0:T(8,128)(2,1)S(1)} %get-tuple-element.96), channel_id=1, source_target_pairs={{0,2},{1,3},{2,4},{3,5},{4,6},{5,7},{8,10},{9,11},{10,12},{11,13},... | collective-permute-start | bytes 614408 | tf_op jit(solution)/shard_map/ppermute | solution.py:59
  455.1 7.7 %collective-permute-start.85 = (bf16[8,12800]{1,0:T(8,128)(2,1)S(1)}, bf16[8,12800]{1,0:T(8,128)(2,1)S(1)}, u32[]{:S(2)}, u32[]{:S(2)}) collective-permute-start(bf16[8,12800]{1,0:T(8,128)(2,1)S(1)} %get-tuple-element.97), channel_id=1, source_target_pairs={{2,0},{3,1},{4,2},{5,3},{6,4},{7,5},{10,8},{11,9},{12,10},{13,11},... | collective-permute-start | bytes 614408 | tf_op jit(solution)/shard_map/ppermute | solution.py:59
  464.1 7.6 %collective-permute-start.88 = (bf16[32,3200]{1,0:T(8,128)(2,1)S(1)}, bf16[32,3200]{1,0:T(8,128)(2,1)S(1)}, u32[]{:S(2)}, u32[]{:S(2)}) collective-permute-start(bf16[32,3200]{1,0:T(8,128)(2,1)S(1)} %get-tuple-element.32), channel_id=1, source_target_pairs={{2,0},{3,1},{4,2},{5,3},{6,4},{7,5},{10,8},{11,9},{12,10},{13,11},... | collective-permute-start | bytes 614408 | tf_op jit(solution)/shard_map/ppermute | solution.py:59
  465.4 7.8 %collective-permute-start.86 = (bf16[32,3200]{1,0:T(8,128)(2,1)S(1)}, bf16[32,3200]{1,0:T(8,128)(2,1)S(1)}, u32[]{:S(2)}, u32[]{:S(2)}) collective-permute-start(bf16[32,3200]{1,0:T(8,128)(2,1)S(1)} %get-tuple-element.32), channel_id=1, source_target_pairs={{0,2},{1,3},{2,4},{3,5},{4,6},{5,7},{8,10},{9,11},{10,12},{11,13},... | collective-permute-start | bytes 614408 | tf_op jit(solution)/shard_map/ppermute | solution.py:59
  471.7 7.6 %collective-permute-start.89 = (bf16[32,3200]{1,0:T(8,128)(2,1)S(1)}, bf16[32,3200]{1,0:T(8,128)(2,1)S(1)}, u32[]{:S(2)}, u32[]{:S(2)}) collective-permute-start(bf16[32,3200]{1,0:T(8,128)(2,1)S(1)} %collective-permute-done.88), channel_id=1, source_target_pairs={{2,0},{3,1},{4,2},{5,3},{10,8},{11,9},{12,10},{13,11},{18,16},{19,... | collective-permute-start | bytes 614408 | tf_op jit(solution)/shard_map/ppermute | solution.py:59
  473.2 7.5 %collective-permute-start.87 = (bf16[32,3200]{1,0:T(8,128)(2,1)S(1)}, bf16[32,3200]{1,0:T(8,128)(2,1)S(1)}, u32[]{:S(2)}, u32[]{:S(2)}) collective-permute-start(bf16[32,3200]{1,0:T(8,128)(2,1)S(1)} %collective-permute-done.86), channel_id=1, source_target_pairs={{2,4},{3,5},{4,6},{5,7},{10,12},{11,13},{12,14},{13,15},{18,20},{1... | collective-permute-start | bytes 614408 | tf_op jit(solution)/shard_map/ppermute | solution.py:59
  473.9 14.7 %collective-permute-start.92 = (bf16[32,3200]{1,0:T(8,128)(2,1)S(1)}, bf16[32,3200]{1,0:T(8,128)(2,1)S(1)}, u32[]{:S(2)}, u32[]{:S(2)}) collective-permute-start(bf16[32,3200]{1,0:T(8,128)(2,1)S(1)} %get-tuple-element.32), channel_id=1, source_target_pairs={{0,1},{1,0},{2,3},{3,2},{4,5},{5,4},{6,7},{7,6},{8,9},{9,8},{10,11... | collective-permute-start | bytes 614408 | tf_op jit(solution)/shard_map/ppermute | solution.py:62
  479.4 7.6 %collective-permute-start.90 = (bf16[32,3200]{1,0:T(8,128)(2,1)S(1)}, bf16[32,3200]{1,0:T(8,128)(2,1)S(1)}, u32[]{:S(2)}, u32[]{:S(2)}) collective-permute-start(bf16[32,3200]{1,0:T(8,128)(2,1)S(1)} %collective-permute-done.89), channel_id=1, source_target_pairs={{2,0},{3,1},{10,8},{11,9},{18,16},{19,17},{26,24},{27,25}} | collective-permute-start | bytes 614408 | tf_op jit(solution)/shard_map/ppermute | solution.py:59
  481.4 7.9 %collective-permute-start.93 = (bf16[32,3200]{1,0:T(8,128)(2,1)S(1)}, bf16[32,3200]{1,0:T(8,128)(2,1)S(1)}, u32[]{:S(2)}, u32[]{:S(2)}) collective-permute-start(bf16[32,3200]{1,0:T(8,128)(2,1)S(1)} %get-tuple-element.30), channel_id=1, source_target_pairs={{0,1},{1,0},{2,3},{3,2},{4,5},{5,4},{6,7},{7,6},{8,9},{9,8},{10,11... | collective-permute-start | bytes 614408 | tf_op jit(solution)/shard_map/ppermute | solution.py:62
  511.6 12.0 %collective-permute-start.95 = (bf16[128,3200]{1,0:T(8,128)(2,1)}, bf16[128,3200]{1,0:T(8,128)(2,1)}, u32[]{:S(2)}, u32[]{:S(2)}) collective-permute-start(bf16[128,3200]{1,0:T(8,128)(2,1)} %slice.283), channel_id=1, source_target_pairs={{0,1},{1,0},{2,3},{3,2},{4,5},{5,4},{6,7},{7,6},{8,9},{9,8},{10,11... | collective-permute-start | bytes 2457608 | tf_op jit(solution)/shard_map/ppermute | solution.py:62
  523.1 31.4 %collective-permute-start.50 = (bf16[32,1024]{1,0:T(8,128)(2,1)S(1)}, bf16[32,1024]{1,0:T(8,128)(2,1)S(1)}, u32[]{:S(2)}, u32[]{:S(2)}) collective-permute-start(bf16[32,1024]{1,0:T(8,128)(2,1)S(1)} %broadcast_select_fusion.24), channel_id=1, source_target_pairs={{0,8},{8,16},{16,24},{24,0},{1,9},{9,17},{17,25},{25,1},{2,10},{10... | collective-permute-start | bytes 196616 | tf_op jit(solution)/shard_map/ppermute | solution.py:202
  528.1 28.0 %collective-permute-start.51 = (bf16[32,1024]{1,0:T(8,128)(2,1)}, bf16[32,1024]{1,0:T(8,128)(2,1)}, u32[]{:S(2)}, u32[]{:S(2)}) collective-permute-start(bf16[32,1024]{1,0:T(8,128)(2,1)} %broadcast_select_fusion.23), channel_id=1, source_target_pairs={{0,16},{8,24},{16,0},{24,8},{1,17},{9,25},{17,1},{25,9},{2,18},{10... | collective-permute-start | bytes 196616 | tf_op jit(solution)/shard_map/ppermute | solution.py:202
  531.5 8.2 %collective-permute-start.97 = (bf16[32,3200]{1,0:T(8,128)(2,1)S(1)}, bf16[32,3200]{1,0:T(8,128)(2,1)S(1)}, u32[]{:S(2)}, u32[]{:S(2)}) collective-permute-start(bf16[32,3200]{1,0:T(8,128)(2,1)S(1)} %get-tuple-element.92), channel_id=1, source_target_pairs={{0,2},{1,3},{2,4},{3,5},{8,10},{9,11},{10,12},{11,13},{16,18},{17,... | collective-permute-start | bytes 614408 | tf_op jit(solution)/shard_map/ppermute | solution.py:59
  536.7 21.1 %collective-permute-start.52 = (bf16[32,1024]{1,0:T(8,128)(2,1)S(1)}, bf16[32,1024]{1,0:T(8,128)(2,1)}, u32[]{:S(2)}, u32[]{:S(2)}) collective-permute-start(bf16[32,1024]{1,0:T(8,128)(2,1)S(1)} %broadcast_select_fusion.22), channel_id=1, source_target_pairs={{0,24},{8,0},{16,8},{24,16},{1,25},{9,1},{17,9},{25,17},{2,26},{10... | collective-permute-start | bytes 196616 | tf_op jit(solution)/shard_map/ppermute | solution.py:202
  540.6 19.0 %collective-permute-start.98 = (bf16[32,3200]{1,0:T(8,128)(2,1)}, bf16[32,3200]{1,0:T(8,128)(2,1)}, u32[]{:S(2)}, u32[]{:S(2)}) collective-permute-start(bf16[32,3200]{1,0:T(8,128)(2,1)} %get-tuple-element.90), channel_id=1, source_target_pairs={{0,2},{1,3},{2,4},{3,5},{4,6},{5,7},{8,10},{9,11},{10,12},{11,13},... | collective-permute-start | bytes 614408 | tf_op jit(solution)/shard_map/ppermute | solution.py:59
  551.6 8.0 %collective-permute-start.101 = (bf16[32,3200]{1,0:T(8,128)(2,1)}, bf16[32,3200]{1,0:T(8,128)(2,1)}, u32[]{:S(2)}, u32[]{:S(2)}) collective-permute-start(bf16[32,3200]{1,0:T(8,128)(2,1)} %get-tuple-element.91), channel_id=1, source_target_pairs={{2,0},{3,1},{4,2},{5,3},{6,4},{7,5},{10,8},{11,9},{12,10},{13,11},... | collective-permute-start | bytes 614408 | tf_op jit(solution)/shard_map/ppermute | solution.py:59
  (63 other events, 384.5 us)

commit v2 on v1

v2 whole, which is shorter than its diff:
```python
import jax
import jax.numpy as jnp
from jax import lax
from jax.sharding import PartitionSpec as P

vis_eps = 1e-06
proj_eps = 1e-05
chunks = 2
images = 4
cores = 2


def layer_norm(values, scale_vec, epsilon):
    mean_val = jnp.mean(values, -1, keepdims=True)
    centred = values - mean_val
    inv_std = lax.rsqrt(jnp.mean(centred * centred, -1, keepdims=True) + epsilon)
    normed = centred * inv_std
    return (normed * scale_vec, normed, inv_std)


def norm_back(upstream, scale_vec, normed, inv_std):
    scaled = upstream * scale_vec
    return inv_std * (
        scaled
        - jnp.mean(scaled, -1, keepdims=True)
        - normed * jnp.mean(scaled * normed, -1, keepdims=True)
    )


def gelu_slope(values):
    cumul = 0.5 * (1.0 + lax.erf(values * 0.7071067811865476))
    dense = jnp.exp(-0.5 * values * values) * 0.3989422804014327
    return cumul + values * dense


def times_transposed(left, right):
    return lax.dot_general(
        left, right, (((1,), (1,)), ((), ())), preferred_element_type=jnp.float32
    )


def after(values, *tokens):
    return lax.optimization_barrier((values, tokens))[0]


class Whole:
    def gather(self, block):
        return lax.all_gather(block, "tp", axis=0, tiled=True)

    def scatter(self, partial):
        summed = lax.psum_scatter(partial, "tp", scatter_dimension=0, tiled=True)
        return summed.astype(jnp.float32)

    def by_rank(self, rows, size):
        return rows.reshape(size, -1, rows.shape[-1])

    def by_row(self, ranks):
        return ranks.reshape(-1, ranks.shape[-1])


class Rails:
    def __init__(self):
        size = lax.axis_size("tp")
        self.places = size // cores
        self.lead = lax.axis_index("tp") % cores == 0
        self.groups = [list(range(c, size, cores)) for c in range(cores)]
        self.pairs = [(a, a + 1 - 2 * (a % cores)) for a in range(size)]

    def exchange(self, blocks):
        return lax.all_to_all(
            blocks, "tp", split_axis=0, concat_axis=0, axis_index_groups=self.groups, tiled=True
        )

    def gather(self, block):
        mine = self.exchange(jnp.concatenate([block] * self.places, 0))
        other = lax.ppermute(mine, "tp", self.pairs)
        return jnp.concatenate(
            [jnp.where(self.lead, mine, other), jnp.where(self.lead, other, mine)], 0
        )

    def scatter(self, partial):
        half = partial.shape[0] // cores
        low, high = partial[:half], partial[half:]
        got = lax.ppermute(jnp.where(self.lead, high, low), "tp", self.pairs)
        mine = jnp.where(self.lead, low, high).astype(jnp.float32) + got.astype(jnp.float32)
        came = self.exchange(mine.astype(jnp.bfloat16)).astype(jnp.float32)
        return jnp.sum(came.reshape(self.places, half // self.places, -1), 0)

    def by_rank(self, rows, size):
        width = rows.shape[-1]
        split = rows.reshape(cores, self.places, -1, width)
        return jnp.swapaxes(split, 0, 1).reshape(size, -1, width)

    def by_row(self, ranks):
        size, _, width = ranks.shape
        split = ranks.reshape(self.places, cores, -1, width)
        return jnp.swapaxes(split, 0, 1).reshape(-1, width)


def per_device(
    vision_in,
    vis_gain,
    first_weight,
    second_weight,
    layer_scale,
    proj_gain,
    proj_weight,
    text_embed,
    dest_row,
    cotangent,
):
    moves = [Whole(), Rails()]
    groups = lax.axis_size("grp")
    size = lax.axis_size("tp")
    grp_rank = lax.axis_index("grp")
    seq_len, width = text_embed.shape
    merged_total = dest_row.shape[0] // groups
    image_rows = merged_total // images
    own_rows, vis_width = vision_in.shape
    merged_width = proj_gain.shape[0]
    fold = merged_width // vis_width
    rows = own_rows // chunks
    merged_rows = rows // fold

    x, hat, inv, normed = [], [], [], []
    for c in range(chunks):
        x.append(vision_in[c * rows : (c + 1) * rows].astype(jnp.float32))
        scaled, own_hat, own_inv = layer_norm(x[c], vis_gain, vis_eps)
        normed.append(scaled.astype(jnp.bfloat16))
        hat.append(own_hat)
        inv.append(own_inv)
    patches_a = moves[0].gather(normed[0])
    patches_b = moves[1].gather(normed[1])

    starts = dest_row.reshape(groups, images, image_rows)[:, :, 0]
    start_pos = starts % seq_len
    shift = starts[0] // seq_len
    matches = (shift[None, :] == jnp.arange(groups)[:, None]).astype(jnp.int32)
    image_of = jnp.sum(matches * jnp.arange(images), 1)
    used = jnp.sum(matches, 1) > 0
    source = (grp_rank - jnp.arange(groups)) % groups
    from_group = (source[:, None] == jnp.arange(groups)).astype(jnp.int32)
    spot = jnp.sum(matches[:, None, :] * from_group[:, :, None] * start_pos[None], (1, 2))

    picked = []
    for s in range(groups):
        block = lax.dynamic_slice_in_dim(cotangent, spot[s], image_rows, 0)
        if s:
            block = lax.ppermute(block, "grp", [(g, (g - s) % groups) for g in range(groups)])
        picked.append(block)
    returned = jnp.take(jnp.stack(picked), shift, axis=0).reshape(size, -1, width)
    grad_proj = [
        moves[c].by_row(returned[:, c * merged_rows : (c + 1) * merged_rows]) for c in range(chunks)
    ]

    def vision_mlp(patches):
        pre = jnp.dot(patches, first_weight, preferred_element_type=jnp.float32)
        hidden = jax.nn.gelu(pre, approximate=False).astype(jnp.bfloat16)
        summed = jnp.dot(hidden, second_weight, preferred_element_type=jnp.float32)
        return summed.astype(jnp.bfloat16), pre

    def merge(c, summed):
        outputs = (x[c] + layer_scale * summed).astype(jnp.bfloat16)
        merged = outputs.reshape(merged_rows, merged_width).astype(jnp.float32)
        scaled, own_hat, own_inv = layer_norm(merged, proj_gain, proj_eps)
        return scaled.astype(jnp.bfloat16), own_hat, own_inv

    def project(c, merged):
        pre = jnp.dot(merged, proj_weight, preferred_element_type=jnp.float32)
        projected = jax.nn.gelu(pre, approximate=False).astype(jnp.bfloat16)
        delta = (grad_proj[c].astype(jnp.float32) * gelu_slope(pre)).astype(jnp.bfloat16)
        return times_transposed(delta, proj_weight).astype(jnp.bfloat16), projected

    def unmerge(back_sum, own_hat, own_inv):
        merged_grad = norm_back(back_sum, proj_gain, own_hat, own_inv).astype(jnp.bfloat16)
        own_grad = merged_grad.reshape(rows, vis_width).astype(jnp.float32)
        return own_grad, (own_grad * layer_scale).astype(jnp.bfloat16)

    def vision_back(grad_out, pre):
        hidden_grad = times_transposed(grad_out, second_weight)
        delta = (hidden_grad * gelu_slope(pre)).astype(jnp.bfloat16)
        return times_transposed(delta, first_weight).astype(jnp.bfloat16)

    part_b, pre_b = vision_mlp(patches_b)
    summed_b = moves[1].scatter(part_b)
    part_a, pre_a = vision_mlp(after(patches_a, part_b))
    summed_a = moves[0].scatter(part_a)
    mixed_b, *stats_b = merge(1, after(summed_b, part_a))
    merged_b = moves[1].gather(mixed_b)
    mixed_a, *stats_a = merge(0, after(summed_a, mixed_b))
    merged_a = moves[0].gather(mixed_a)
    back_b, projected_b = project(1, after(merged_b, mixed_a))
    summed_b = moves[1].scatter(back_b)
    back_a, projected_a = project(0, after(merged_a, back_b))
    summed_a = moves[0].scatter(back_a)

    projected = jnp.concatenate(
        [moves[0].by_rank(projected_a, size), moves[1].by_rank(projected_b, size)], 1
    ).reshape(images, image_rows, width)
    seq_embed = text_embed
    for s in range(groups):
        block = lax.dynamic_index_in_dim(projected, image_of[s], 0, False)
        if s:
            block = lax.ppermute(block, "grp", [(g, (g + s) % groups) for g in range(groups)])
        if groups > images:
            there = lax.dynamic_slice_in_dim(seq_embed, spot[s], image_rows, 0)
            block = jnp.where(used[s], block, there)
        seq_embed = lax.dynamic_update_slice_in_dim(seq_embed, block, spot[s], 0)

    own_b, scaled_b = unmerge(after(summed_b, back_a), *stats_b)
    grad_out_b = moves[1].gather(scaled_b)
    own_a, scaled_a = unmerge(after(summed_a, scaled_b), *stats_a)
    grad_out_a = moves[0].gather(scaled_a)
    deep_b = vision_back(after(grad_out_b, scaled_a), pre_b)
    normed_b = moves[1].scatter(deep_b)
    deep_a = vision_back(after(grad_out_a, deep_b), pre_a)
    normed_a = moves[0].scatter(deep_a)
    normed_b, seq_embed = after((normed_b, seq_embed), deep_a)
    grads = [
        own_a + norm_back(normed_a, vis_gain, hat[0], inv[0]),
        own_b + norm_back(normed_b, vis_gain, hat[1], inv[1]),
    ]
    grad_vision = jnp.concatenate(grads, 0).astype(jnp.bfloat16)
    return (seq_embed, grad_vision)


def solution(mesh):
    placed = (
        P(("grp", "tp"), None),
        P(),
        P(None, "tp"),
        P("tp", None),
        P(),
        P(),
        P(None, "tp"),
        P("grp", "tp"),
        P(),
        P("grp", "tp"),
    )
    return jax.shard_map(
        per_device,
        mesh=mesh,
        in_specs=placed,
        out_specs=(P("grp", "tp"), P(("grp", "tp"), None)),
        check_vma=False,
    )
```

time: 572 us -> 392 us (0.69)
  the two profiles are of different devices: /device:TPU:0 before, /device:TPU:9 now
where the time goes in v2:
time: 392 us; the launch traced here: 385 us
  matrix products  126 us (32%)
  waiting for transfers between devices  78.5 us (20%)
  blocking collectives  67.6 us (17%)
  starting transfers between devices  42.9 us (11%)
  between operations  30.4 us (8%)
  other arithmetic  24.6 us (6%)
  local copies, waits for them, and re-layouts  15 us (4%)
    dot_general x4, matrix products, times_transposed(): lax.dot_general(left, right, (((1,), (1,)), ((), ())), preferred_element_...  67.6 us
    all_to_all x2, blocking collectives, exchange(): lax.all_to_all(blocks, 'tp', split_axis=0, concat_axis=0, axis_index_grou...  67.6 us
    all_to_all x4, waiting for transfers between devices, exchange(): lax.all_to_all(blocks, 'tp', split_axis=0, concat_axis=0, axis_index_grou...  43.1 us
    dot_general x2, matrix products, project(): pre = jnp.dot(merged, proj_weight, preferred_element_type=jnp.float32)  25.7 us
    reduce_scatter x3, waiting for transfers between devices, scatter(): summed = lax.psum_scatter(partial, 'tp', scatter_dimension=0, tiled=True)  23 us
    all_to_all x4, starting transfers between devices, exchange(): lax.all_to_all(blocks, 'tp', split_axis=0, concat_axis=0, axis_index_grou...  22.3 us
    dot_general x2, matrix products, vision_mlp(): summed = jnp.dot(hidden, second_weight, preferred_element_type=jnp.float32)  18.1 us
    dot_general x2, matrix products, vision_mlp(): pre = jnp.dot(patches, first_weight, preferred_element_type=jnp.float32)  14.4 us
  transfers between devices with their start and end apart: 22, of which 14 were waited for; matrix products, arithmetic and copies ran while one was open for 20% of the time, Pallas kernels for 0%

profile of v2, /device:TPU:9, one launch (start us, length us, event | category | flops | bytes accessed | tf_op | source)
XLA Modules:
  0.0 384.8 jit_solution(13653382546215566448)
XLA Ops:
  7.2 3.3 copy.24
  11.0 0.9 fusion.107
  11.9 0.9 pad_maximum_fusion.2
  12.8 4.8 %all-to-all-start = ((bf16[4,32,3200]{2,1,0:T(8,128)(2,1)}), bf16[4,32,3200]{2,1,0:T(8,128)(2,1)S(1)}, u32[]{:S(2)}, u32[]{:S(2)}) async-start(bf16[4,32,3200]{2,1,0:T(8,128)(2,1)} %bitcast), calls=%async_computation | async-start | bytes 1638400 | tf_op jit(solution)/shard_map/all_to_all | solution.py:70
  17.6 0.7 all-gather.4.cloned.1.call-update
  18.6 21.1 %all-to-all-done = bf16[4,32,3200]{2,1,0:T(8,128)(2,1)S(1)} async-done(((bf16[4,32,3200]{2,1,0:T(8,128)(2,1)}), bf16[4,32,3200]{2,1,0:T(8,128)(2,1)S(1)}, u32[]{:S(2)}, u32[]{:S(2)}) %all-to-all-start) | async-done | bytes 819232 | tf_op jit(solution)/shard_map/all_to_all | solution.py:70
  39.7 6.9 %collective-permute-start = (bf16[128,3200]{1,0:T(8,128)(2,1)S(1)}, bf16[128,3200]{1,0:T(8,128)(2,1)S(1)}, u32[]{:S(2)}, u32[]{:S(2)}) collective-permute-start(bf16[128,3200]{1,0:T(8,128)(2,1)S(1)} %bitcast.90), channel_id=1, source_target_pairs={{0,1},{1,0},{2,3},{3,2},{4,5},{5,4},{6,7},{7,6},{8,9},{9,8},{10,11... | collective-permute-start | bytes 2457608 | tf_op jit(solution)/shard_map/ppermute | solution.py:76
  46.9 1.7 collective-permute-done
  48.8 5.8 %fusion.16 = f32[256,1600]{0,1:T(8,128)S(1)} fusion(bf16[3200,1600]{0,1:T(8,128)(2,1)} %param.12, bf16[128,3200]{1,0:T(8,128)(2,1)S(1)} %get-tuple-element.51, bf16[128,3200]{1,0:T(8,128)(2,1)S(1)} %get-tuple-element.50), kind=kOutput, calls=%fused_computation.29 | convolution fusion | flops 2624716800 | bytes 13516800 | tf_op jit(solution)/shard_map/dot_general | solution.py:157
  55.6 6.6 %convolution_convert_fusion.5 = bf16[256,3200]{1,0:T(8,128)(2,1)S(1)} fusion(bf16[1600,3200]{1,0:T(8,128)(2,1)S(1)} %bitcast.102, f32[256,1600]{0,1:T(8,128)S(1)} %fusion.16), kind=kOutput, calls=%fused_computation.6 | convolution fusion | flops 2648883200 | bytes 13516800 | tf_op jit(solution)/shard_map/dot_general | solution.py:159
  62.2 1.0 broadcast_select_fusion.6
  63.6 8.6 %fusion.256 = f32[256,1600]{0,1:T(8,128)} fusion(bf16[256,3200]{1,0:T(8,128)(2,1)} %all-gather.4.cloned.1.call-done, bf16[3200,1600]{0,1:T(8,128)(2,1)} %param.12), kind=kOutput, calls=%fused_computation.389 | convolution fusion | flops 2621440000 | bytes 13516800 | tf_op jit(solution)/shard_map/dot_general | solution.py:157
  72.2 1.2 add_convert_fusion.2
  73.4 7.3 %all-to-all-start.1 = ((bf16[4,32,3200]{2,1,0:T(8,128)(2,1)}), bf16[4,32,3200]{2,1,0:T(8,128)(2,1)S(1)}, u32[]{:S(2)}, u32[]{:S(2)}) async-start(bf16[4,32,3200]{2,1,0:T(8,128)(2,1)} %bitcast.2), calls=%async_computation.1 | async-start | bytes 1638400 | tf_op jit(solution)/shard_map/all_to_all | solution.py:70
  81.2 11.6 %convolution_convert_fusion.4 = bf16[256,3200]{1,0:T(8,128)(2,1)} fusion(bf16[1600,3200]{1,0:T(8,128)(2,1)} %param.13, f32[256,1600]{0,1:T(8,128)S(1)} %copy-done.6), kind=kOutput, calls=%fused_computation.5 | convolution fusion | flops 2648883200 | bytes 13516800 | tf_op jit(solution)/shard_map/dot_general | solution.py:159
  92.8 5.7 %all-to-all-done.1 = bf16[4,32,3200]{2,1,0:T(8,128)(2,1)S(1)} async-done(((bf16[4,32,3200]{2,1,0:T(8,128)(2,1)}), bf16[4,32,3200]{2,1,0:T(8,128)(2,1)S(1)}, u32[]{:S(2)}, u32[]{:S(2)}) %all-to-all-start.1) | async-done | bytes 819232 | tf_op jit(solution)/shard_map/all_to_all | solution.py:70
  99.9 1.0 maximum_bitcast_fusion
  100.9 6.5 %all-to-all-start.2 = ((bf16[4,8,12800]{2,1,0:T(8,128)(2,1)}), bf16[4,8,12800]{2,1,0:T(8,128)(2,1)S(1)}, u32[]{:S(2)}, u32[]{:S(2)}) async-start(bf16[4,8,12800]{2,1,0:T(8,128)(2,1)} %maximum_bitcast_fusion), calls=%async_computation.2 | async-start | bytes 1638400 | tf_op jit(solution)/shard_map/all_to_all | solution.py:70
  107.6 0.7 fusion.255
  116.0 1.1 dynamic-slice_bitcast_fusion.4
  117.0 1.3 collective-permute-start.4
  118.3 1.3 collective-permute-start.2
  119.6 1.2 collective-permute-start.3
  121.1 1.2 collective-permute-done.2
  122.3 1.6 collective-permute-done.3
  124.6 8.9 %all-to-all-done.2 = bf16[4,8,12800]{2,1,0:T(8,128)(2,1)S(1)} async-done(((bf16[4,8,12800]{2,1,0:T(8,128)(2,1)}), bf16[4,8,12800]{2,1,0:T(8,128)(2,1)S(1)}, u32[]{:S(2)}, u32[]{:S(2)}) %all-to-all-start.2) | async-done | bytes 819232 | tf_op jit(solution)/shard_map/all_to_all | solution.py:70
  133.5 1.6 collective-permute-start.5
  135.1 3.7 reduce-scatter.4.cloned.1.call-done
  138.9 1.0 convert_element_type.214
  140.9 0.8 multiply_convert_fusion.4
  141.7 1.3 broadcast_select_fusion.2
  143.1 14.4 %fusion.141 = (bf16[64,1024]{1,0:T(8,128)(2,1)}, bf16[64,1024]{1,0:T(8,128)(2,1)}) fusion(f32[4,2,8,1024]{3,2,0,1:T(8,128)S(1)} %copy.17, bf16[64,12800]{1,0:T(8,128)(2,1)S(1)} %pad_maximum_fusion, bf16[12800,1024]{1,0:T(8,128)(2,1)} %param.16), kind=kOutput, calls=%fused_computation.215 | convolution fusion | flops 1682636800 | bytes 28377088 | tf_op jit(solution)/shard_map/dot_general | solution.py:169
  157.5 12.9 %convolution_convert_fusion.1 = bf16[64,12800]{1,0:T(8,128)(2,1)S(1)} fusion(bf16[64,1024]{1,0:T(8,128)(2,1)} %get-tuple-element.61, bf16[12800,1024]{1,0:T(8,128)(2,1)} %param.16), kind=kOutput, calls=%fused_computation.2 | convolution fusion | flops 1678540800 | bytes 27983872 | tf_op jit(solution)/shard_map/dot_general | solution.py:37
  170.4 1.0 broadcast_select_fusion
  171.5 2.6 collective-permute-done.6
  174.1 1.4 fusion.36
  175.6 35.2 %all_to_all.63 = bf16[4,8,12800]{2,1,0:T(8,128)(2,1)S(1)} all-to-all(bf16[4,8,12800]{2,1,0:T(8,128)(2,1)S(1)} %fusion.36), channel_id=1, replica_groups={{0,2,4,6},{1,3,5,7},{8,10,12,14},{9,11,13,15},{16,18,20,22},{17,19,21,2..., dimensions={0} | all-to-all | bytes 1638400 | tf_op jit(solution)/shard_map/all_to_all | solution.py:70
  210.9 11.3 %fusion.257 = f32[64,1024]{1,0:T(8,128)S(1)} fusion(bf16[64,12800]{1,0:T(8,128)(2,1)} %all-gather.6.cloned.1.call-done, bf16[12800,1024]{1,0:T(8,128)(2,1)} %param.16), kind=kOutput, calls=%fused_computation.390 | convolution fusion | flops 1677721600 | bytes 28114944 | tf_op jit(solution)/shard_map/dot_general | solution.py:169
  222.2 14.2 %convolution_convert_fusion = bf16[64,12800]{1,0:T(8,128)(2,1)} fusion(bf16[12800,1024]{1,0:T(8,128)(2,1)} %param.16, f32[64,1024]{1,0:T(8,128)S(1)} %fusion.257, bf16[8,16,1024]{2,1,0:T(8,128)(2,1)S(1)} %broadcast_select_fusion.9), kind=kOutput, calls=%fused_computation.1 | convolution fusion | flops 1679261696 | bytes 28246016 | tf_op jit(solution)/shard_map/dot_general | solution.py:37
  237.2 32.4 %all_to_all.64 = bf16[4,32,3200]{2,1,0:T(8,128)(2,1)S(1)} all-to-all(bf16[4,32,3200]{2,1,0:T(8,128)(2,1)S(1)} %bitcast.92), channel_id=1, replica_groups={{0,2,4,6},{1,3,5,7},{8,10,12,14},{9,11,13,15},{16,18,20,22},{17,19,21,2..., dimensions={0} | all-to-all | bytes 1638400 | tf_op jit(solution)/shard_map/all_to_all | solution.py:70
  269.5 3.2 collective-permute-start.7
  272.8 8.3 %reduce-scatter.6.cloned.1.call-done = bf16[8,12800]{1,0:T(8,128)(2,1)} async-done(((bf16[64,12800]{1,0:T(8,128)(2,1)}), bf16[8,12800]{1,0:T(8,128)(2,1)}) %reduce-scatter.6.cloned.1.call-update) | async-done | bytes 204816 | tf_op jit(solution)/shard_map/reduce_scatter | solution.py:51
  281.1 1.0 convert_element_type.234
  282.7 0.7 multiply_convert_fusion
  283.7 1.3 broadcast_select_fusion.5
  285.0 1.3 pad_maximum_fusion.1
  286.3 19.6 %convolution_convert_fusion.3 = bf16[256,3200]{1,0:T(8,128)(2,1)S(1)} fusion(bf16[3200,1600]{0,1:T(8,128)(2,1)} %param.12, bf16[256,3200]{1,0:T(8,128)(2,1)} %pad_maximum_fusion.1, bf16[1600,3200]{1,0:T(8,128)(2,1)} %param.13, f32[256,1600]{0,1:T(8,128)} %copy-done.7), kind=kOutput, calls=%fused_computation.4 | convolution fusion | flops 5247795200 | bytes 25395200 | tf_op jit(solution)/shard_map/dot_general | solution.py:37
  306.0 2.3 all-gather.8.cloned.1.call-done
  308.3 20.9 %convolution_convert_fusion.2 = bf16[256,3200]{1,0:T(8,128)(2,1)} fusion(bf16[3200,1600]{0,1:T(8,128)(2,1)} %param.12, bf16[256,3200]{1,0:T(8,128)(2,1)} %all-gather.8.cloned.1.call-done, bf16[1600,3200]{1,0:T(8,128)(2,1)} %param.13, f32[256,1600]{0,1:T(8,128)} %fusion.256), kind=kOutput, calls=%fused_computation.3 | convolution fusion | flops 5247795200 | bytes 25395200 | tf_op jit(solution)/shard_map/dot_general | solution.py:37
  329.6 2.1 collective-permute-done.8
  331.7 1.2 add_convert_fusion
  332.9 3.8 all-to-all-start.5
  345.8 1.2 collective-permute-start.9
  347.0 1.2 collective-permute-start.10
  348.2 1.2 collective-permute-start.11
  349.4 1.6 dynamic_update_slice.12
  351.0 1.6 dynamic_update_slice.13
  352.6 1.6 dynamic_update_slice.14
  354.1 1.6 dynamic_update_slice.15
  355.7 7.4 %all-to-all-done.5 = bf16[4,32,3200]{2,1,0:T(8,128)(2,1)S(1)} async-done(((bf16[4,32,3200]{2,1,0:T(8,128)(2,1)}), bf16[4,32,3200]{2,1,0:T(8,128)(2,1)S(1)}, u32[]{:S(2)}, u32[]{:S(2)}) %all-to-all-start.5) | async-done | bytes 819232 | tf_op jit(solution)/shard_map/all_to_all | solution.py:70
  363.2 11.0 %reduce-scatter.8.cloned.1.call-done = bf16[32,3200]{1,0:T(8,128)(2,1)} async-done(((bf16[256,3200]{1,0:T(8,128)(2,1)}), bf16[32,3200]{1,0:T(8,128)(2,1)}) %reduce-scatter.8.cloned.1.call-update) | async-done | bytes 204816 | tf_op jit(solution)/shard_map/reduce_scatter | solution.py:51
  374.1 1.3 fusion.108
  375.5 1.3 fusion.112
  376.7 0.8 pad_maximum_fusion.4
  (120 shorter events, 10.6 us)
Async XLA Ops:
  7.2 3.3 copy-start
  7.2 3.8 copy-start.4
  11.9 6.4 %copy-start.5 = (s32[512]{0:T(512)S(1)}, s32[512]{0:T(512)}, u32[]{:S(2)}) copy-start(s32[512]{0:T(512)} %param.18) | copy-start | bytes 6148
  12.8 26.9 %all-to-all-start = ((bf16[4,32,3200]{2,1,0:T(8,128)(2,1)}), bf16[4,32,3200]{2,1,0:T(8,128)(2,1)S(1)}, u32[]{:S(2)}, u32[]{:S(2)}) async-start(bf16[4,32,3200]{2,1,0:T(8,128)(2,1)} %bitcast), calls=%async_computation | async-start | bytes 1638400 | tf_op jit(solution)/shard_map/all_to_all | solution.py:70
  17.6 46.0 %all-gather.4.cloned.1.call-start = ((), (), s32[]{:S(2)}) async-start(), calls=%async_computation.9 | async-start | bytes 1843200 | tf_op jit(solution)/shard_map/all_gather | solution.py:48
  39.7 8.8 %collective-permute-start = (bf16[128,3200]{1,0:T(8,128)(2,1)S(1)}, bf16[128,3200]{1,0:T(8,128)(2,1)S(1)}, u32[]{:S(2)}, u32[]{:S(2)}) collective-permute-start(bf16[128,3200]{1,0:T(8,128)(2,1)S(1)} %bitcast.90), channel_id=1, source_target_pairs={{0,1},{1,0},{2,3},{3,2},{4,5},{5,4},{6,7},{7,6},{8,9},{9,8},{10,11... | collective-permute-start | bytes 2457608 | tf_op jit(solution)/shard_map/ppermute | solution.py:76
  48.5 6.1 %slice-start = ((s8[10240000]{0:T(1024)(128)(4,1)}), s8[4194304]{0:T(1024)(128)(4,1)S(1)}, s32[]{:S(2)}) async-start(s8[10240000]{0:T(1024)(128)(4,1)} %bitcast.101), calls=%async_computation.15 | async-start | bytes 8388608
  48.7 6.3 %slice-start.1 = ((s8[10240000]{0:T(1024)(128)(4,1)}), s8[4194304]{0:T(1024)(128)(4,1)S(1)}, s32[]{:S(2)}) async-start(s8[10240000]{0:T(1024)(128)(4,1)} %bitcast.101), calls=%async_computation.16 | async-start | bytes 8388608
  48.8 6.8 %slice-start.2 = ((s8[10240000]{0:T(1024)(128)(4,1)}), s8[1851392]{0:T(1024)(128)(4,1)S(1)}, s32[]{:S(2)}) async-start(s8[10240000]{0:T(1024)(128)(4,1)} %bitcast.101), calls=%async_computation.17 | async-start | bytes 3702784
  55.6 6.6 %copy-start.7 = (f32[256,1600]{0,1:T(8,128)}, f32[256,1600]{0,1:T(8,128)S(1)}, u32[]{:S(2)}) copy-start(f32[256,1600]{0,1:T(8,128)S(1)} %fusion.16) | copy-start | bytes 4915204
  63.2 9.0 %collective-permute-start.1 = (bf16[128,3200]{1,0:T(8,128)(2,1)}, bf16[128,3200]{1,0:T(8,128)(2,1)S(1)}, u32[]{:S(2)}, u32[]{:S(2)}) collective-permute-start(bf16[128,3200]{1,0:T(8,128)(2,1)} %broadcast_select_fusion.6), channel_id=1, source_target_pairs={{0,1},{1,0},{2,3},{3,2},{4,5},{5,4},{6,7},{7,6},{8,9},{9,8},{10,11... | collective-permute-start | bytes 2457608 | tf_op jit(solution)/shard_map/ppermute | solution.py:84
  73.4 7.8 %copy-start.6 = (f32[256,1600]{0,1:T(8,128)S(1)}, f32[256,1600]{0,1:T(8,128)}, u32[]{:S(2)}) copy-start(f32[256,1600]{0,1:T(8,128)} %fusion.256) | copy-start | bytes 4915204
  73.4 25.1 %all-to-all-start.1 = ((bf16[4,32,3200]{2,1,0:T(8,128)(2,1)}), bf16[4,32,3200]{2,1,0:T(8,128)(2,1)S(1)}, u32[]{:S(2)}, u32[]{:S(2)}) async-start(bf16[4,32,3200]{2,1,0:T(8,128)(2,1)} %bitcast.2), calls=%async_computation.1 | async-start | bytes 1638400 | tf_op jit(solution)/shard_map/all_to_all | solution.py:70
  80.7 58.1 %reduce-scatter.4.cloned.1.call-start = ((), (), s32[]{:S(2)}) async-start(), calls=%async_computation.10 | async-start | bytes 1843200 | tf_op jit(solution)/shard_map/reduce_scatter | solution.py:51
  92.8 5.9 %copy-start.3 = (f32[3200]{0:T(1024)S(1)}, f32[3200]{0:T(1024)}, u32[]{:S(2)}) copy-start(f32[3200]{0:T(1024)} %param.14) | copy-start | bytes 38404
  92.8 6.9 %copy-start.1 = (f32[12800]{0:T(1024)S(1)}, f32[12800]{0:T(1024)}, u32[]{:S(2)}) copy-start(f32[12800]{0:T(1024)} %param.15) | copy-start | bytes 153604
  100.9 32.7 %all-to-all-start.2 = ((bf16[4,8,12800]{2,1,0:T(8,128)(2,1)}), bf16[4,8,12800]{2,1,0:T(8,128)(2,1)S(1)}, u32[]{:S(2)}, u32[]{:S(2)}) async-start(bf16[4,8,12800]{2,1,0:T(8,128)(2,1)} %maximum_bitcast_fusion), calls=%async_computation.2 | async-start | bytes 1638400 | tf_op jit(solution)/shard_map/all_to_all | solution.py:70
  107.3 103.6 %all-gather.6.cloned.1.call-start = ((), (), s32[]{:S(2)}) async-start(), calls=%async_computation.11 | async-start | bytes 1843200 | tf_op jit(solution)/shard_map/all_gather | solution.py:48
  117.0 4.1 %collective-permute-start.4 = (bf16[32,1024]{1,0:T(8,128)(2,1)S(1)}, bf16[32,1024]{1,0:T(8,128)(2,1)S(1)}, u32[]{:S(2)}, u32[]{:S(2)}) collective-permute-start(bf16[32,1024]{1,0:T(8,128)(2,1)S(1)} %get-tuple-element.44), channel_id=1, source_target_pairs={{0,8},{8,16},{16,24},{24,0},{1,9},{9,17},{17,25},{25,1},{2,10},{10... | collective-permute-start | bytes 196616 | tf_op jit(solution)/shard_map/ppermute | solution.py:149
  118.3 4.0 %collective-permute-start.2 = (bf16[32,1024]{1,0:T(8,128)(2,1)S(1)}, bf16[32,1024]{1,0:T(8,128)(2,1)S(1)}, u32[]{:S(2)}, u32[]{:S(2)}) collective-permute-start(bf16[32,1024]{1,0:T(8,128)(2,1)S(1)} %get-tuple-element.43), channel_id=1, source_target_pairs={{0,24},{8,0},{16,8},{24,16},{1,25},{9,1},{17,9},{25,17},{2,26},{10... | collective-permute-start | bytes 196616 | tf_op jit(solution)/shard_map/ppermute | solution.py:149
  119.6 4.2 %collective-permute-start.3 = (bf16[32,1024]{1,0:T(8,128)(2,1)S(1)}, bf16[32,1024]{1,0:T(8,128)(2,1)S(1)}, u32[]{:S(2)}, u32[]{:S(2)}) collective-permute-start(bf16[32,1024]{1,0:T(8,128)(2,1)S(1)} %get-tuple-element.45), channel_id=1, source_target_pairs={{0,16},{8,24},{16,0},{24,8},{1,17},{9,25},{17,1},{25,9},{2,18},{10... | collective-permute-start | bytes 196616 | tf_op jit(solution)/shard_map/ppermute | solution.py:149
  133.5 8.2 %collective-permute-start.5 = (bf16[32,12800]{1,0:T(8,128)(2,1)S(1)}, bf16[32,12800]{1,0:T(8,128)(2,1)}, u32[]{:S(2)}, u32[]{:S(2)}) collective-permute-start(bf16[32,12800]{1,0:T(8,128)(2,1)S(1)} %bitcast.88), channel_id=1, source_target_pairs={{0,1},{1,0},{2,3},{3,2},{4,5},{5,4},{6,7},{7,6},{8,9},{9,8},{10,11... | collective-permute-start | bytes 2457608 | tf_op jit(solution)/shard_map/ppermute | solution.py:76
  171.5 2.7 collective-permute-start.6
  171.5 109.6 %reduce-scatter.6.cloned.1.call-start = ((), (), s32[]{:S(2)}) async-start(), calls=%async_computation.12 | async-start | bytes 1843200 | tf_op jit(solution)/shard_map/reduce_scatter | solution.py:51
  236.4 71.9 %all-gather.8.cloned.1.call-start = ((), (), s32[]{:S(2)}) async-start(), calls=%async_computation.13 | async-start | bytes 1843200 | tf_op jit(solution)/shard_map/all_gather | solution.py:48
  269.5 14.1 %collective-permute-start.7 = (bf16[128,3200]{1,0:T(8,128)(2,1)S(1)}, bf16[128,3200]{1,0:T(8,128)(2,1)}, u32[]{:S(2)}, u32[]{:S(2)}) collective-permute-start(bf16[128,3200]{1,0:T(8,128)(2,1)S(1)} %bitcast.91), channel_id=1, source_target_pairs={{0,1},{1,0},{2,3},{3,2},{4,5},{5,4},{6,7},{7,6},{8,9},{9,8},{10,11... | collective-permute-start | bytes 2457608 | tf_op jit(solution)/shard_map/ppermute | solution.py:76
  283.4 90.7 %reduce-scatter.8.cloned.1.call-start = ((), (), s32[]{:S(2)}) async-start(), calls=%async_computation.14 | async-start | bytes 1843200 | tf_op jit(solution)/shard_map/reduce_scatter | solution.py:51
  329.3 2.4 collective-permute-start.8
  332.9 12.2 %copy-start.2 = (bf16[64,1024]{1,0:T(8,128)(2,1)S(1)}, bf16[64,1024]{1,0:T(8,128)(2,1)}, u32[]{:S(2)}) copy-start(bf16[64,1024]{1,0:T(8,128)(2,1)} %get-tuple-element.60) | copy-start | bytes 393220
  332.9 30.1 %all-to-all-start.5 = ((bf16[4,32,3200]{2,1,0:T(8,128)(2,1)}), bf16[4,32,3200]{2,1,0:T(8,128)(2,1)S(1)}, u32[]{:S(2)}, u32[]{:S(2)}) async-start(bf16[4,32,3200]{2,1,0:T(8,128)(2,1)} %bitcast.89), calls=%async_computation.7 | async-start | bytes 1638400 | tf_op jit(solution)/shard_map/all_to_all | solution.py:70
  345.8 5.2 %collective-permute-start.9 = (bf16[32,1024]{1,0:T(8,128)(2,1)S(1)}, bf16[32,1024]{1,0:T(8,128)(2,1)S(1)}, u32[]{:S(2)}, u32[]{:S(2)}) collective-permute-start(bf16[32,1024]{1,0:T(8,128)(2,1)S(1)} %get-tuple-element.58), channel_id=1, source_target_pairs={{0,8},{8,16},{16,24},{24,0},{1,9},{9,17},{17,25},{25,1},{2,10},{10... | collective-permute-start | bytes 196616 | tf_op jit(solution)/shard_map/ppermute | solution.py:204
  347.0 5.5 %collective-permute-start.10 = (bf16[32,1024]{1,0:T(8,128)(2,1)S(1)}, bf16[32,1024]{1,0:T(8,128)(2,1)S(1)}, u32[]{:S(2)}, u32[]{:S(2)}) collective-permute-start(bf16[32,1024]{1,0:T(8,128)(2,1)S(1)} %get-tuple-element.57), channel_id=1, source_target_pairs={{0,16},{8,24},{16,0},{24,8},{1,17},{9,25},{17,1},{25,9},{2,18},{10... | collective-permute-start | bytes 196616 | tf_op jit(solution)/shard_map/ppermute | solution.py:204
  348.2 5.9 %collective-permute-start.11 = (bf16[32,1024]{1,0:T(8,128)(2,1)S(1)}, bf16[32,1024]{1,0:T(8,128)(2,1)S(1)}, u32[]{:S(2)}, u32[]{:S(2)}) collective-permute-start(bf16[32,1024]{1,0:T(8,128)(2,1)S(1)} %get-tuple-element.56), channel_id=1, source_target_pairs={{0,24},{8,0},{16,8},{24,16},{1,25},{9,1},{17,9},{25,17},{2,26},{10... | collective-permute-start | bytes 196616 | tf_op jit(solution)/shard_map/ppermute | solution.py:204
Sparse Core Ops, SparseCore 0:
  20.6 33.3 all-gather.3
  92.9 45.8 reduce-scatter.3
  171.6 36.8 all-gather.5
  236.6 44.5 reduce-scatter.5
  283.5 24.7 all-gather.7
  329.4 44.7 reduce-scatter.7

commit v3 on v2

--- a/solution.py
+++ b/solution.py
@@ -1,6 +1,10 @@
+import functools
+
 import jax
 import jax.numpy as jnp
 from jax import lax
+from jax.experimental import pallas as pl
+from jax.experimental.pallas import tpu as pltpu
 from jax.sharding import PartitionSpec as P
 
 vis_eps = 1e-06
@@ -27,25 +31,236 @@
     )
 
 
-def gelu_slope(values):
-    cumul = 0.5 * (1.0 + lax.erf(values * 0.7071067811865476))
-    dense = jnp.exp(-0.5 * values * values) * 0.3989422804014327
-    return cumul + values * dense
-
-
 def times_transposed(left, right):
     return lax.dot_general(
         left, right, (((1,), (1,)), ((), ())), preferred_element_type=jnp.float32
     )
 
 
+def tile_of(length, most):
+    return max(t for t in range(128, most + 1, 128) if length % t == 0)
+
+
+def laid(pieces):
+    if len(pieces) == 1:
+        return pieces[0][...]
+    if pieces[0].shape[0] % 16 == 0:
+        return jnp.concatenate([p[...] for p in pieces], 0)
+    return jnp.concatenate([p[...].astype(jnp.float32) for p in pieces], 0).astype(jnp.bfloat16)
+
+
+def each_rows(total, body):
+    step = 16 if total % 16 == 0 else total
+
+    def run(i, _):
+        body(pl.ds(pl.multiple_of(i * step, step), step))
+        return 0
+
+    lax.fori_loop(0, total // step, run, 0)
+
+
+def forward_kernel(count, steps, *refs):
+    pieces = refs[:count]
+    first, second, out, slope, pre, hidden = refs[count:]
+    i = pl.program_id(0)
+
+    @pl.when(i == 0)
+    def _():
+        pre[...] = jnp.dot(laid(pieces), first[...], preferred_element_type=jnp.float32)
+
+    @pl.when(jnp.logical_and(i > 0, i < steps))
+    def _():
+        pre[...] += jnp.dot(laid(pieces), first[...], preferred_element_type=jnp.float32)
+
+    @pl.when(i == steps - 1)
+    def _():
+        def act(sel):
+            u = pre[sel, :]
+            cumul = 0.5 * (1.0 + lax.erf(u * 0.7071067811865476))
+            dense = jnp.exp(-0.5 * u * u) * 0.3989422804014327
+            hidden[sel, :] = (u * cumul).astype(jnp.bfloat16)
+            slope[sel, :] = cumul + u * dense
+
+        each_rows(pre.shape[0], act)
+
+    @pl.when(i >= steps)
+    def _():
+        out[...] = jnp.dot(
+            hidden[...], second[...], preferred_element_type=jnp.float32
+        ).astype(jnp.bfloat16)
+
+
+def backward_kernel(count, steps, *refs):
+    pieces = refs[:count]
+    first, second, slope, out, total, delta = refs[count:]
+    i = pl.program_id(0)
+
+    @pl.when(i == 0)
+    def _():
+        total[...] = times_transposed(laid(pieces), second[...])
+
+    @pl.when(jnp.logical_and(i > 0, i < steps))
+    def _():
+        total[...] += times_transposed(laid(pieces), second[...])
+
+    @pl.when(i == steps - 1)
+    def _():
+        def act(sel):
+            delta[sel, :] = (total[sel, :] * slope[sel, :]).astype(jnp.bfloat16)
+
+        each_rows(total.shape[0], act)
+
+    @pl.when(i >= steps)
+    def _():
+        out[...] = times_transposed(delta[...], first[...]).astype(jnp.bfloat16)
+
+
+def project_kernel(count, chunk, *refs):
+    pieces = refs[:count]
+    weight, upstream, projected, back, rows, total = refs[count:]
+    i = pl.program_id(0)
+    depth = weight.shape[0]
+
+    @pl.when(i == 0)
+    def _():
+        total[...] = jnp.zeros_like(total)
+        rows[...] = laid(pieces)
+
+    def ahead(k, pre):
+        sel = pl.ds(pl.multiple_of(k * chunk, 128), chunk)
+        return pre + jnp.dot(rows[:, sel], weight[sel, :], preferred_element_type=jnp.float32)
+
+    u = lax.fori_loop(0, depth // chunk, ahead, jnp.zeros(projected.shape, jnp.float32))
+    cumul = 0.5 * (1.0 + lax.erf(u * 0.7071067811865476))
+    dense = jnp.exp(-0.5 * u * u) * 0.3989422804014327
+    projected[...] = (u * cumul).astype(jnp.bfloat16)
+    delta = (upstream[...].astype(jnp.float32) * (cumul + u * dense)).astype(jnp.bfloat16)
+
+    def behind(k, _):
+        sel = pl.ds(pl.multiple_of(k * chunk, 128), chunk)
+        total[:, sel] += times_transposed(delta, weight[sel, :])
+        return 0
+
+    lax.fori_loop(0, depth // chunk, behind, 0)
+
+    @pl.when(i == pl.num_programs(0) - 1)
+    def _():
+        back[...] = total[...].astype(jnp.bfloat16)
+
+
+def settings(limit):
+    return pltpu.CompilerParams(
+        vmem_limit_bytes=limit * 1024 * 1024, dimension_semantics=("arbitrary",)
+    )
+
+
+def vision_mlp(pieces, first, second):
+    rows = sum(p.shape[0] for p in pieces)
+    width, units = first.shape
+    tile = tile_of(width, 640)
+    steps = width // tile
+    early = lambda i: jnp.minimum(i, steps - 1)
+    late = lambda i: jnp.maximum(i - steps, 0)
+    return pl.pallas_call(
+        functools.partial(forward_kernel, len(pieces), steps),
+        grid=(2 * steps,),
+        in_specs=[pl.BlockSpec((p.shape[0], tile), lambda i: (0, early(i))) for p in pieces]
+        + [
+            pl.BlockSpec((tile, units), lambda i: (early(i), 0)),
+            pl.BlockSpec((units, tile), lambda i: (0, late(i))),
+        ],
+        out_specs=[
+            pl.BlockSpec((rows, tile), lambda i: (0, late(i))),
+            pl.BlockSpec((rows, units), lambda i: (0, 0)),
+        ],
+        out_shape=[
+            jax.ShapeDtypeStruct((rows, width), jnp.bfloat16),
+            jax.ShapeDtypeStruct((rows, units), jnp.float32),
+        ],
+        scratch_shapes=[
+            pltpu.VMEM((rows, units), jnp.float32),
+            pltpu.VMEM((rows, units), jnp.bfloat16),
+        ],
+        compiler_params=settings(28),
+        cost_estimate=pl.CostEstimate(
+            flops=4 * rows * width * units,
+            bytes_accessed=4 * width * units + 4 * rows * (width + units),
+            transcendentals=2 * rows * units,
+        ),
+    )(*pieces, first, second)
+
+
+def vision_back(pieces, first, second, slope):
+    rows = sum(p.shape[0] for p in pieces)
+    width, units = first.shape
+    tile = tile_of(width, 640)
+    steps = width // tile
+    early = lambda i: jnp.minimum(i, steps - 1)
+    late = lambda i: jnp.maximum(i - steps, 0)
+    return pl.pallas_call(
+        functools.partial(backward_kernel, len(pieces), steps),
+        grid=(2 * steps,),
+        in_specs=[pl.BlockSpec((p.shape[0], tile), lambda i: (0, early(i))) for p in pieces]
+        + [
+            pl.BlockSpec((tile, units), lambda i: (late(i), 0)),
+            pl.BlockSpec((units, tile), lambda i: (0, early(i))),
+            pl.BlockSpec((rows, units), lambda i: (0, 0)),
+        ],
+        out_specs=pl.BlockSpec((rows, tile), lambda i: (0, late(i))),
+        out_shape=jax.ShapeDtypeStruct((rows, width), jnp.bfloat16),
+        scratch_shapes=[
+            pltpu.VMEM((rows, units), jnp.float32),
+            pltpu.VMEM((rows, units), jnp.bfloat16),
+        ],
+        compiler_params=settings(28),
+        cost_estimate=pl.CostEstimate(
+            flops=4 * rows * width * units,
+            bytes_accessed=4 * width * units + 4 * rows * (width + units),
+            transcendentals=0,
+        ),
+    )(*pieces, first, second, slope)
+
+
+def project(pieces, weight, upstream):
+    rows = sum(p.shape[0] for p in pieces)
+    depth, units = weight.shape
+    tile = tile_of(units, 256)
+    return pl.pallas_call(
+        functools.partial(project_kernel, len(pieces), tile_of(depth, 2560)),
+        grid=(units // tile,),
+        in_specs=[pl.BlockSpec(p.shape, lambda i: (0, 0)) for p in pieces]
+        + [
+            pl.BlockSpec((depth, tile), lambda i: (0, i)),
+            pl.BlockSpec((rows, tile), lambda i: (0, i)),
+        ],
+        out_specs=[
+            pl.BlockSpec((rows, tile), lambda i: (0, i)),
+            pl.BlockSpec((rows, depth), lambda i: (0, 0)),
+        ],
+        out_shape=[
+            jax.ShapeDtypeStruct((rows, units), jnp.bfloat16),
+            jax.ShapeDtypeStruct((rows, depth), jnp.bfloat16),
+        ],
+        scratch_shapes=[
+            pltpu.VMEM((rows, depth), jnp.bfloat16),
+            pltpu.VMEM((rows, depth), jnp.float32),
+        ],
+        compiler_params=settings(40),
+        cost_estimate=pl.CostEstimate(
+            flops=4 * rows * depth * units,
+            bytes_accessed=2 * depth * units + 4 * rows * (depth + units),
+            transcendentals=2 * rows * units,
+        ),
+    )(*pieces, weight, upstream)
+
+
 def after(values, *tokens):
     return lax.optimization_barrier((values, tokens))[0]
 
 
 class Whole:
     def gather(self, block):
-        return lax.all_gather(block, "tp", axis=0, tiled=True)
+        return [lax.all_gather(block, "tp", axis=0, tiled=True)]
 
     def scatter(self, partial):
         summed = lax.psum_scatter(partial, "tp", scatter_dimension=0, tiled=True)
@@ -58,43 +273,46 @@
         return ranks.reshape(-1, ranks.shape[-1])
 
 
-class Rails:
+class Direct:
     def __init__(self):
-        size = lax.axis_size("tp")
-        self.places = size // cores
-        self.lead = lax.axis_index("tp") % cores == 0
-        self.groups = [list(range(c, size, cores)) for c in range(cores)]
-        self.pairs = [(a, a + 1 - 2 * (a % cores)) for a in range(size)]
-
-    def exchange(self, blocks):
-        return lax.all_to_all(
-            blocks, "tp", split_axis=0, concat_axis=0, axis_index_groups=self.groups, tiled=True
-        )
+        self.size = lax.axis_size("tp")
+        self.places = self.size // cores
+        rank = lax.axis_index("tp")
+        place, core = rank // cores, rank % cores
+        back = (place - jnp.arange(self.places)) % self.places * cores
+        self.ranks = jnp.concatenate([back + core, back + 1 - core])
+        every = jnp.arange(self.size)
+        far = (every + core) % cores * self.places
+        self.blocks = far + (place - every // cores) % self.places
+        self.pairs = [(a, a + 1 - 2 * (a % cores)) for a in range(self.size)]
+
+    def shift(self, block, k):
+        pairs = [(a, (a + k * cores) % self.size) for a in range(self.size)]
+        return lax.ppermute(block, "tp", pairs)
 
     def gather(self, block):
-        mine = self.exchange(jnp.concatenate([block] * self.places, 0))
-        other = lax.ppermute(mine, "tp", self.pairs)
-        return jnp.concatenate(
-            [jnp.where(self.lead, mine, other), jnp.where(self.lead, other, mine)], 0
-        )
+        mine = [block] + [self.shift(block, k) for k in range(1, self.places)]
+        other = [lax.ppermute(m, "tp", self.pairs) for m in mine]
+        if block.shape[0] % 8:
+            return [jnp.concatenate(mine + other, 0)]
+        return mine + other
 
     def scatter(self, partial):
         half = partial.shape[0] // cores
-        low, high = partial[:half], partial[half:]
-        got = lax.ppermute(jnp.where(self.lead, high, low), "tp", self.pairs)
-        mine = jnp.where(self.lead, low, high).astype(jnp.float32) + got.astype(jnp.float32)
-        came = self.exchange(mine.astype(jnp.bfloat16)).astype(jnp.float32)
-        return jnp.sum(came.reshape(self.places, half // self.places, -1), 0)
+        rows = half // self.places
+        got = lax.ppermute(partial[half:], "tp", self.pairs)
+        both = partial[:half].astype(jnp.float32) + got.astype(jnp.float32)
+        total = both[:rows]
+        for k in range(1, self.places):
+            sent = both[k * rows : (k + 1) * rows].astype(jnp.bfloat16)
+            total = total + self.shift(sent, -k).astype(jnp.float32)
+        return total
 
     def by_rank(self, rows, size):
-        width = rows.shape[-1]
-        split = rows.reshape(cores, self.places, -1, width)
-        return jnp.swapaxes(split, 0, 1).reshape(size, -1, width)
+        return jnp.take(rows.reshape(size, -1, rows.shape[-1]), self.blocks, axis=0)
 
     def by_row(self, ranks):
-        size, _, width = ranks.shape
-        split = ranks.reshape(self.places, cores, -1, width)
-        return jnp.swapaxes(split, 0, 1).reshape(-1, width)
+        return jnp.take(ranks, self.ranks, axis=0).reshape(-1, ranks.shape[-1])
 
 
 def per_device(
@@ -109,7 +327,7 @@
     dest_row,
     cotangent,
 ):
-    moves = [Whole(), Rails()]
+    moves = [Whole(), Direct()]
     groups = lax.axis_size("grp")
     size = lax.axis_size("tp")
     grp_rank = lax.axis_index("grp")
@@ -153,45 +371,29 @@
         moves[c].by_row(returned[:, c * merged_rows : (c + 1) * merged_rows]) for c in range(chunks)
     ]
 
-    def vision_mlp(patches):
-        pre = jnp.dot(patches, first_weight, preferred_element_type=jnp.float32)
-        hidden = jax.nn.gelu(pre, approximate=False).astype(jnp.bfloat16)
-        summed = jnp.dot(hidden, second_weight, preferred_element_type=jnp.float32)
-        return summed.astype(jnp.bfloat16), pre
-
     def merge(c, summed):
         outputs = (x[c] + layer_scale * summed).astype(jnp.bfloat16)
         merged = outputs.reshape(merged_rows, merged_width).astype(jnp.float32)
         scaled, own_hat, own_inv = layer_norm(merged, proj_gain, proj_eps)
         return scaled.astype(jnp.bfloat16), own_hat, own_inv
 
-    def project(c, merged):
-        pre = jnp.dot(merged, proj_weight, preferred_element_type=jnp.float32)
-        projected = jax.nn.gelu(pre, approximate=False).astype(jnp.bfloat16)
-        delta = (grad_proj[c].astype(jnp.float32) * gelu_slope(pre)).astype(jnp.bfloat16)
-        return times_transposed(delta, proj_weight).astype(jnp.bfloat16), projected
-
     def unmerge(back_sum, own_hat, own_inv):
         merged_grad = norm_back(back_sum, proj_gain, own_hat, own_inv).astype(jnp.bfloat16)
         own_grad = merged_grad.reshape(rows, vis_width).astype(jnp.float32)
         return own_grad, (own_grad * layer_scale).astype(jnp.bfloat16)
 
-    def vision_back(grad_out, pre):
-        hidden_grad = times_transposed(grad_out, second_weight)
-        delta = (hidden_grad * gelu_slope(pre)).astype(jnp.bfloat16)
-        return times_transposed(delta, first_weight).astype(jnp.bfloat16)
-
-    part_b, pre_b = vision_mlp(patches_b)
+    part_b, slope_b = vision_mlp(patches_b, first_weight, second_weight)
     summed_b = moves[1].scatter(part_b)
-    part_a, pre_a = vision_mlp(after(patches_a, part_b))
+    patches_a = after(patches_a, part_b)
+    part_a, slope_a = vision_mlp(patches_a, first_weight, second_weight)
     summed_a = moves[0].scatter(part_a)
     mixed_b, *stats_b = merge(1, after(summed_b, part_a))
     merged_b = moves[1].gather(mixed_b)
     mixed_a, *stats_a = merge(0, after(summed_a, mixed_b))
     merged_a = moves[0].gather(mixed_a)
-    back_b, projected_b = project(1, after(merged_b, mixed_a))
+    projected_b, back_b = project(after(merged_b, mixed_a), proj_weight, grad_proj[1])
     summed_b = moves[1].scatter(back_b)
-    back_a, projected_a = project(0, after(merged_a, back_b))
+    projected_a, back_a = project(after(merged_a, back_b), proj_weight, grad_proj[0])
     summed_a = moves[0].scatter(back_a)
 
     projected = jnp.concatenate(
@@ -211,9 +413,11 @@
     grad_out_b = moves[1].gather(scaled_b)
     own_a, scaled_a = unmerge(after(summed_a, scaled_b), *stats_a)
     grad_out_a = moves[0].gather(scaled_a)
-    deep_b = vision_back(after(grad_out_b, scaled_a), pre_b)
+    grad_out_b = after(grad_out_b, scaled_a)
+    deep_b = vision_back(grad_out_b, first_weight, second_weight, slope_b)
     normed_b = moves[1].scatter(deep_b)
-    deep_a = vision_back(after(grad_out_a, deep_b), pre_a)
+    grad_out_a = after(grad_out_a, deep_b)
+    deep_a = vision_back(grad_out_a, first_weight, second_weight, slope_a)
     normed_a = moves[0].scatter(deep_a)
     normed_b, seq_embed = after((normed_b, seq_embed), deep_a)
     grads = [

time: 392 us -> 455 us (1.16)
  the two profiles are of different devices: /device:TPU:9 before, /device:TPU:0 now
where the time goes in v3:
time: 455 us; the launch traced here: 453 us
  waiting for transfers between devices  148 us (33%)
  local copies, waits for them, and re-layouts  102 us (22%)
  Pallas kernels  88.9 us (20%)
  starting transfers between devices  52.3 us (11%)
  other arithmetic  32.2 us (7%)
  between operations  29.8 us (7%)
    unnamed x160, local copies, waits for them, and re-layouts  80.9 us
    ppermute x18, waiting for transfers between devices, shift(): return lax.ppermute(block, 'tp', pairs)  74.6 us
    reduce_scatter x3, waiting for transfers between devices, scatter(): summed = lax.psum_scatter(partial, 'tp', scatter_dimension=0, tiled=True)  59.4 us
    pallas_call x2, Pallas kernels, project(): pl.pallas_call(functools.partial(project_kernel, len(pieces), tile_of(dep...  43.6 us
    ppermute x18, starting transfers between devices, shift(): return lax.ppermute(block, 'tp', pairs)  40.8 us
    pallas_call x2, Pallas kernels, vision_mlp(): pl.pallas_call(functools.partial(forward_kernel, len(pieces), steps), gri...  23.1 us
    pallas_call x2, Pallas kernels, vision_back(): pl.pallas_call(functools.partial(backward_kernel, len(pieces), steps), gr...  22.3 us
    all_gather x3, waiting for transfers between devices, gather(): return [lax.all_gather(block, 'tp', axis=0, tiled=True)]  9.37 us
  transfers between devices with their start and end apart: 45, of which 16 were waited for; matrix products, arithmetic and copies ran while one was open for 13% of the time, Pallas kernels for 7%

profile of v3, /device:TPU:0, one launch (start us, length us, event | category | flops | bytes accessed | tf_op | source)
XLA Modules:
  0.0 453.0 jit_solution(3849004526988617967)
XLA Ops:
  7.2 3.3 copy.33
  11.9 3.0 collective-permute-start
  15.0 2.6 collective-permute-start.1
  17.6 1.3 collective-permute-start.2
  29.2 1.8 dynamic-slice_bitcast_fusion.4
  31.0 1.5 collective-permute-start.20
  32.5 16.2 %copy.24.refs_8_.refs_1_ = bf16[3200,1600]{1,0:T(8,128)(2,1)} copy(bf16[3200,1600]{0,1:T(8,128)(2,1)} %param.14) | data formatting | bytes 20480000 | tf_op args[2]
  52.3 1.5 collective-permute-start.19
  53.8 1.4 collective-permute-start.18
  55.3 4.0 copy-done
  59.3 3.9 copy-done.4
  66.9 11.4 %shard_map.113 = (bf16[256,3200]{1,0:T(8,128)(2,1)S(1)}, f32[256,1600]{1,0:T(8,128)S(1)}) custom-call(bf16[32,3200]{1,0:T(8,128)(2,1)S(1)} %get-tuple-element.113.refs_0_, bf16[32,3200]{1,0:T(8,128)(2,1)S(1)} %copy-done.14, bf16[32,3200]{1,0:T(8,128)(2,1)S(1)} %copy-done.16, bf16[32,3200]{1,0:T(8,128)(2,1)S(1)} %copy-done.18, ...), custom_call_target="tpu_custom_call" | custom-call | flops 5242880000 | bytes 25395200 | tf_op jit(solution)/shard_map/pallas_call | solution.py:164
  80.7 1.6 pad_maximum_fusion.1
  82.3 2.2 gather_fusion
  85.6 2.5 fusion.51
  89.2 2.8 collective-permute-start.8
  92.7 5.3 %collective-permute-done.10 = bf16[32,3200]{1,0:T(8,128)(2,1)S(1)} collective-permute-done((bf16[32,3200]{1,0:T(8,128)(2,1)S(1)}, bf16[32,3200]{1,0:T(8,128)(2,1)S(1)}, u32[]{:S(2)}, u32[]{:S(2)}) %collective-permute-start.10) | collective-permute-done | bytes 204832 | tf_op jit(solution)/shard_map/ppermute | solution.py:291
  98.0 8.3 %collective-permute-done.9 = bf16[32,3200]{1,0:T(8,128)(2,1)S(1)} collective-permute-done((bf16[32,3200]{1,0:T(8,128)(2,1)S(1)}, bf16[32,3200]{1,0:T(8,128)(2,1)S(1)}, u32[]{:S(2)}, u32[]{:S(2)}) %collective-permute-start.9) | collective-permute-done | bytes 204832 | tf_op jit(solution)/shard_map/ppermute | solution.py:291
  106.4 1.8 fusion.31
  108.2 4.0 copy-done.1
  112.2 3.9 copy-done.5
  116.2 1.4 copy-done.10
  117.6 11.7 %shard_map.114 = (bf16[256,3200]{1,0:T(8,128)(2,1)}, f32[256,1600]{1,0:T(8,128)S(1)}) custom-call(bf16[256,3200]{1,0:T(8,128)(2,1)S(1)} %copy-done.10, bf16[3200,1600]{1,0:T(8,128)(2,1)S(1)} %copy-done.1, bf16[1600,3200]{1,0:T(8,128)(2,1)S(1)} %copy-done.5), custom_call_target="tpu_custom_call" | custom-call | flops 5242880000 | bytes 25395200 | tf_op jit(solution)/shard_map/pallas_call | solution.py:164
  133.8 4.5 collective-permute-start.11
  138.3 2.4 collective-permute-start.13
  140.9 5.3 %collective-permute-done.11.refs_1_ = bf16[8,12800]{1,0:T(8,128)(2,1)S(1)} collective-permute-done((bf16[8,12800]{1,0:T(8,128)(2,1)S(1)}, bf16[8,12800]{1,0:T(8,128)(2,1)S(1)}, u32[]{:S(2)}, u32[]{:S(2)}) %collective-permute-start.11) | collective-permute-done | bytes 204832 | tf_op jit(solution)/shard_map/ppermute | solution.py:291
  146.3 12.0 %collective-permute-done.12.refs_2_ = bf16[8,12800]{1,0:T(8,128)(2,1)S(1)} collective-permute-done((bf16[8,12800]{1,0:T(8,128)(2,1)S(1)}, bf16[8,12800]{1,0:T(8,128)(2,1)S(1)}, u32[]{:S(2)}, u32[]{:S(2)}) %collective-permute-start.12) | collective-permute-done | bytes 204832 | tf_op jit(solution)/shard_map/ppermute | solution.py:291
  158.8 15.8 %reduce-scatter.4.cloned.1.call-done = bf16[32,3200]{1,0:T(8,128)(2,1)} async-done(((bf16[256,3200]{1,0:T(8,128)(2,1)}), bf16[32,3200]{1,0:T(8,128)(2,1)}) %reduce-scatter.4.cloned.1.call-update) | async-done | bytes 204816 | tf_op jit(solution)/shard_map/reduce_scatter | solution.py:266
  175.6 1.9 fusion.54
  177.5 1.8 reshape.302
  181.1 1.8 multiply_convert_fusion.4
  183.0 21.3 %shard_map.115 = (bf16[64,1024]{1,0:T(8,128)(2,1)S(1)}, bf16[64,12800]{1,0:T(8,128)(2,1)S(1)}) custom-call(bf16[8,12800]{1,0:T(8,128)(2,1)S(1)} %multiply_convert_fusion.5.refs_0_, bf16[8,12800]{1,0:T(8,128)(2,1)S(1)} %collective-permute-done.11.refs_1_, bf16[8,12800]{1,0:T(8,128)(2,1)S(1)} %collective-permute-done.12.refs_2_, ...), custom_call_target="tpu_custom_call" | custom-call | flops 3355443200 | bytes 29753344 | tf_op jit(solution)/shard_map/pallas_call | solution.py:228
  204.8 2.0 collective-permute-done.21
  208.1 2.7 collective-permute-start.24
  211.7 2.8 collective-permute-start.22
  214.6 3.6 collective-permute-done.24
  218.2 14.5 %collective-permute-done.23 = bf16[8,12800]{1,0:T(8,128)(2,1)S(1)} collective-permute-done((bf16[8,12800]{1,0:T(8,128)(2,1)S(1)}, bf16[8,12800]{1,0:T(8,128)(2,1)S(1)}, u32[]{:S(2)}, u32[]{:S(2)}) %collective-permute-start.23) | collective-permute-done | bytes 204832 | tf_op jit(solution)/shard_map/ppermute | solution.py:291
  235.4 9.3 %all-gather.6.cloned.1.call-done.refs_0_ = bf16[64,12800]{1,0:T(8,128)(2,1)} async-done(((bf16[8,12800]{1,0:T(8,128)(2,1)}), bf16[64,12800]{1,0:T(8,128)(2,1)}) %all-gather.6.cloned.1.call-update) | async-done | bytes 1638416 | tf_op jit(solution)/shard_map/all_gather | solution.py:263
  244.7 1.4 copy-done.12
  246.1 22.3 %shard_map.116 = (bf16[64,1024]{1,0:T(8,128)(2,1)S(1)}, bf16[64,12800]{1,0:T(8,128)(2,1)}) custom-call(bf16[64,12800]{1,0:T(8,128)(2,1)S(1)} %copy-done.12, bf16[12800,1024]{1,0:T(8,128)(2,1)} %refs_1_.3, bf16[64,1024]{1,0:T(8,128)(2,1)S(1)} %get-tuple-element.118.refs_2_), custom_call_target="tpu_custom_call" | custom-call | flops 3355443200 | bytes 29753344 | tf_op jit(solution)/shard_map/pallas_call | solution.py:228
  272.5 31.1 %reduce-scatter.6.cloned.1.call-done = bf16[8,12800]{1,0:T(8,128)(2,1)} async-done(((bf16[64,12800]{1,0:T(8,128)(2,1)}), bf16[8,12800]{1,0:T(8,128)(2,1)}) %reduce-scatter.6.cloned.1.call-update) | async-done | bytes 204816 | tf_op jit(solution)/shard_map/reduce_scatter | solution.py:266
  308.0 3.7 collective-permute-start.27
  311.8 6.0 %collective-permute-done.25.refs_1_ = bf16[32,3200]{1,0:T(8,128)(2,1)S(1)} collective-permute-done((bf16[32,3200]{1,0:T(8,128)(2,1)S(1)}, bf16[32,3200]{1,0:T(8,128)(2,1)S(1)}, u32[]{:S(2)}, u32[]{:S(2)}) %collective-permute-start.25) | collective-permute-done | bytes 204832 | tf_op jit(solution)/shard_map/ppermute | solution.py:291
  317.8 11.8 %collective-permute-done.26.refs_2_ = bf16[32,3200]{1,0:T(8,128)(2,1)S(1)} collective-permute-done((bf16[32,3200]{1,0:T(8,128)(2,1)S(1)}, bf16[32,3200]{1,0:T(8,128)(2,1)S(1)}, u32[]{:S(2)}, u32[]{:S(2)}) %collective-permute-start.26) | collective-permute-done | bytes 204832 | tf_op jit(solution)/shard_map/ppermute | solution.py:291
  343.4 4.0 copy-done.2
  347.4 3.9 copy-done.6
  357.9 11.0 %shard_map.117 = bf16[256,3200]{1,0:T(8,128)(2,1)S(1)} custom-call(bf16[32,3200]{1,0:T(8,128)(2,1)S(1)} %multiply_convert_fusion.2.refs_0_, bf16[32,3200]{1,0:T(8,128)(2,1)S(1)} %copy-done.22, bf16[32,3200]{1,0:T(8,128)(2,1)S(1)} %copy-done.24, bf16[32,3200]{1,0:T(8,128)(2,1)S(1)} %copy-done.26, bf16[32,3200]{1,0:T(8,128)(2,1)S(1)} %copy-done.28, ...), custom_call_target="tpu_custom_call" | custom-call | flops 5242880000 | bytes 25395200 | tf_op jit(solution)/shard_map/pallas_call | solution.py:200
  369.1 4.0 copy-done.3
  373.1 3.9 copy-done.7
  377.0 1.5 copy-done.9
  378.4 1.4 copy-done.11
  379.9 11.3 %shard_map.118 = bf16[256,3200]{1,0:T(8,128)(2,1)} custom-call(bf16[256,3200]{1,0:T(8,128)(2,1)S(1)} %copy-done.11, bf16[3200,1600]{1,0:T(8,128)(2,1)S(1)} %copy-done.3, bf16[1600,3200]{1,0:T(8,128)(2,1)S(1)} %copy-done.7, f32[256,1600]{1,0:T(8,128)S(1)} %copy-done.9), custom_call_target="tpu_custom_call" | custom-call | flops 5242880000 | bytes 25395200 | tf_op jit(solution)/shard_map/pallas_call | solution.py:200
  394.4 10.5 %collective-permute-start.35 = (bf16[32,3200]{1,0:T(8,128)(2,1)}, bf16[32,3200]{1,0:T(8,128)(2,1)}, u32[]{:S(2)}, u32[]{:S(2)}) collective-permute-start(bf16[32,3200]{1,0:T(8,128)(2,1)} %get-tuple-element.102), channel_id=1, source_target_pairs={{0,2},{1,3},{2,4},{3,5},{4,6},{5,7},{6,0},{7,1},{8,10},{9,11},{10,... | collective-permute-start | bytes 614408 | tf_op jit(solution)/shard_map/ppermute | solution.py:291
  404.8 2.4 collective-permute-start.33
  407.9 1.4 collective-permute-start.36
  409.3 1.5 collective-permute-start.37
  410.8 2.3 collective-permute-done.36
  413.7 1.4 collective-permute-start.38
  415.1 1.6 dynamic_update_slice.12
  416.7 1.6 dynamic_update_slice.13
  418.3 1.6 dynamic_update_slice.14
  419.9 1.6 dynamic_update_slice.15
  422.1 6.9 %collective-permute-done.33 = bf16[32,3200]{1,0:T(8,128)(2,1)} collective-permute-done((bf16[32,3200]{1,0:T(8,128)(2,1)S(1)}, bf16[32,3200]{1,0:T(8,128)(2,1)}, u32[]{:S(2)}, u32[]{:S(2)}) %collective-permute-start.33) | collective-permute-done | bytes 204832 | tf_op jit(solution)/shard_map/ppermute | solution.py:291
  430.2 12.5 %reduce-scatter.8.cloned.1.call-done = bf16[32,3200]{1,0:T(8,128)(2,1)} async-done(((bf16[256,3200]{1,0:T(8,128)(2,1)}), bf16[32,3200]{1,0:T(8,128)(2,1)}) %reduce-scatter.8.cloned.1.call-update) | async-done | bytes 204816 | tf_op jit(solution)/shard_map/reduce_scatter | solution.py:266
  (296 shorter events, 61.0 us)
Async XLA Ops:
  7.2 101.0 %all-gather.4.cloned.1.call-start = ((), (), s32[]{:S(2)}) async-start(), calls=%async_computation.3 | async-start | bytes 1843200 | tf_op jit(solution)/shard_map/all_gather | solution.py:263
  10.6 8.4 %copy-start.72 = (s32[512]{0:T(512)S(1)}, s32[512]{0:T(512)}, u32[]{:S(2)}) copy-start(s32[512]{0:T(512)} %param.20) | copy-start | bytes 6148
  11.9 36.8 %collective-permute-start = (bf16[32,3200]{1,0:T(8,128)(2,1)S(1)}, bf16[32,3200]{1,0:T(8,128)(2,1)S(1)}, u32[]{:S(2)}, u32[]{:S(2)}) collective-permute-start(bf16[32,3200]{1,0:T(8,128)(2,1)S(1)} %get-tuple-element.113.refs_0_), channel_id=1, source_target_pairs={{0,2},{1,3},{2,4},{3,5},{4,6},{5,7},{6,0},{7,1},{8,10},{9,11},{10,... | collective-permute-start | bytes 614408 | tf_op jit(solution)/shard_map/ppermute | solution.py:291
  15.0 34.7 %collective-permute-start.1 = (bf16[32,3200]{1,0:T(8,128)(2,1)S(1)}, bf16[32,3200]{1,0:T(8,128)(2,1)S(1)}, u32[]{:S(2)}, u32[]{:S(2)}) collective-permute-start(bf16[32,3200]{1,0:T(8,128)(2,1)S(1)} %get-tuple-element.113.refs_0_), channel_id=1, source_target_pairs={{0,4},{1,5},{2,6},{3,7},{4,0},{5,1},{6,2},{7,3},{8,12},{9,13},{10,... | collective-permute-start | bytes 614408 | tf_op jit(solution)/shard_map/ppermute | solution.py:291
  17.6 33.0 %collective-permute-start.2 = (bf16[32,3200]{1,0:T(8,128)(2,1)S(1)}, bf16[32,3200]{1,0:T(8,128)(2,1)S(1)}, u32[]{:S(2)}, u32[]{:S(2)}) collective-permute-start(bf16[32,3200]{1,0:T(8,128)(2,1)S(1)} %get-tuple-element.113.refs_0_), channel_id=1, source_target_pairs={{0,6},{1,7},{2,0},{3,1},{4,2},{5,3},{6,4},{7,5},{8,14},{9,15},{10,... | collective-permute-start | bytes 614408 | tf_op jit(solution)/shard_map/ppermute | solution.py:291
  18.9 32.7 %collective-permute-start.3 = (bf16[32,3200]{1,0:T(8,128)(2,1)S(1)}, bf16[32,3200]{1,0:T(8,128)(2,1)S(1)}, u32[]{:S(2)}, u32[]{:S(2)}) collective-permute-start(bf16[32,3200]{1,0:T(8,128)(2,1)S(1)} %get-tuple-element.113.refs_0_), channel_id=1, source_target_pairs={{0,1},{1,0},{2,3},{3,2},{4,5},{5,4},{6,7},{7,6},{8,9},{9,8},{10,11... | collective-permute-start | bytes 614408 | tf_op jit(solution)/shard_map/ppermute | solution.py:295
  18.9 155.7 %reduce-scatter.4.cloned.1.call-start = ((), (), s32[]{:S(2)}) async-start(), calls=%async_computation.4 | async-start | bytes 1843200 | tf_op jit(solution)/shard_map/reduce_scatter | solution.py:266
  19.5 29.2 %copy-start.75 = (s32[4]{0:T(128)}, s32[4]{0:T(128)S(1)}, u32[]{:S(2)}) copy-start(s32[4]{0:T(128)S(1)} %divide_reduce_fusion) | copy-start | bytes 52
  31.0 49.7 %collective-permute-start.20 = (bf16[32,1024]{1,0:T(8,128)(2,1)}, bf16[32,1024]{1,0:T(8,128)(2,1)}, u32[]{:S(2)}, u32[]{:S(2)}) collective-permute-start(bf16[32,1024]{1,0:T(8,128)(2,1)} %get-tuple-element.99), channel_id=1, source_target_pairs={{0,8},{8,16},{16,24},{24,0},{1,9},{9,17},{17,25},{25,1},{2,10},{10... | collective-permute-start | bytes 196616 | tf_op jit(solution)/shard_map/ppermute | solution.py:367
  48.7 5.1 %collective-permute-start.4 = (bf16[32,3200]{1,0:T(8,128)(2,1)S(1)}, bf16[32,3200]{1,0:T(8,128)(2,1)S(1)}, u32[]{:S(2)}, u32[]{:S(2)}) collective-permute-start(bf16[32,3200]{1,0:T(8,128)(2,1)S(1)} %collective-permute-done.refs_1_), channel_id=1, source_target_pairs={{0,1},{1,0},{2,3},{3,2},{4,5},{5,4},{6,7},{7,6},{8,9},{9,8},{10,11... | collective-permute-start | bytes 614408 | tf_op jit(solution)/shard_map/ppermute | solution.py:295
  49.7 5.6 %collective-permute-start.5 = (bf16[32,3200]{1,0:T(8,128)(2,1)S(1)}, bf16[32,3200]{1,0:T(8,128)(2,1)S(1)}, u32[]{:S(2)}, u32[]{:S(2)}) collective-permute-start(bf16[32,3200]{1,0:T(8,128)(2,1)S(1)} %collective-permute-done.1.refs_2_), channel_id=1, source_target_pairs={{0,1},{1,0},{2,3},{3,2},{4,5},{5,4},{6,7},{7,6},{8,9},{9,8},{10,11... | collective-permute-start | bytes 614408 | tf_op jit(solution)/shard_map/ppermute | solution.py:295
  50.6 4.7 %collective-permute-start.6 = (bf16[32,3200]{1,0:T(8,128)(2,1)S(1)}, bf16[32,3200]{1,0:T(8,128)(2,1)S(1)}, u32[]{:S(2)}, u32[]{:S(2)}) collective-permute-start(bf16[32,3200]{1,0:T(8,128)(2,1)S(1)} %collective-permute-done.2.refs_3_), channel_id=1, source_target_pairs={{0,1},{1,0},{2,3},{3,2},{4,5},{5,4},{6,7},{7,6},{8,9},{9,8},{10,11... | collective-permute-start | bytes 614408 | tf_op jit(solution)/shard_map/ppermute | solution.py:295
  52.3 28.4 %collective-permute-start.19 = (bf16[32,1024]{1,0:T(8,128)(2,1)}, bf16[32,1024]{1,0:T(8,128)(2,1)}, u32[]{:S(2)}, u32[]{:S(2)}) collective-permute-start(bf16[32,1024]{1,0:T(8,128)(2,1)} %get-tuple-element.100), channel_id=1, source_target_pairs={{0,16},{8,24},{16,0},{24,8},{1,17},{9,25},{17,1},{25,9},{2,18},{10... | collective-permute-start | bytes 196616 | tf_op jit(solution)/shard_map/ppermute | solution.py:367
  53.8 26.9 %collective-permute-start.18 = (bf16[32,1024]{1,0:T(8,128)(2,1)}, bf16[32,1024]{1,0:T(8,128)(2,1)}, u32[]{:S(2)}, u32[]{:S(2)}) collective-permute-start(bf16[32,1024]{1,0:T(8,128)(2,1)} %get-tuple-element.98), channel_id=1, source_target_pairs={{0,24},{8,0},{16,8},{24,16},{1,25},{9,1},{17,9},{25,17},{2,26},{10... | collective-permute-start | bytes 196616 | tf_op jit(solution)/shard_map/ppermute | solution.py:367
  55.3 4.0 copy-start
  79.3 6.3 %collective-permute-start.7 = (bf16[128,3200]{1,0:T(8,128)(2,1)}, bf16[128,3200]{1,0:T(8,128)(2,1)}, u32[]{:S(2)}, u32[]{:S(2)}) collective-permute-start(bf16[128,3200]{1,0:T(8,128)(2,1)} %slice.113), channel_id=1, source_target_pairs={{0,1},{1,0},{2,3},{3,2},{4,5},{5,4},{6,7},{7,6},{8,9},{9,8},{10,11... | collective-permute-start | bytes 2457608 | tf_op jit(solution)/shard_map/ppermute | solution.py:303
  88.2 9.9 %collective-permute-start.10 = (bf16[32,3200]{1,0:T(8,128)(2,1)S(1)}, bf16[32,3200]{1,0:T(8,128)(2,1)S(1)}, u32[]{:S(2)}, u32[]{:S(2)}) collective-permute-start(bf16[32,3200]{1,0:T(8,128)(2,1)S(1)} %get-tuple-element.108), channel_id=1, source_target_pairs={{0,2},{1,3},{2,4},{3,5},{4,6},{5,7},{6,0},{7,1},{8,10},{9,11},{10,... | collective-permute-start | bytes 614408 | tf_op jit(solution)/shard_map/ppermute | solution.py:291
  88.9 17.4 %collective-permute-start.9 = (bf16[32,3200]{1,0:T(8,128)(2,1)S(1)}, bf16[32,3200]{1,0:T(8,128)(2,1)S(1)}, u32[]{:S(2)}, u32[]{:S(2)}) collective-permute-start(bf16[32,3200]{1,0:T(8,128)(2,1)S(1)} %get-tuple-element.109), channel_id=1, source_target_pairs={{0,4},{1,5},{2,6},{3,7},{4,0},{5,1},{6,2},{7,3},{8,12},{9,13},{10,... | collective-permute-start | bytes 614408 | tf_op jit(solution)/shard_map/ppermute | solution.py:291
  89.2 17.2 %collective-permute-start.8 = (bf16[32,3200]{1,0:T(8,128)(2,1)S(1)}, bf16[32,3200]{1,0:T(8,128)(2,1)S(1)}, u32[]{:S(2)}, u32[]{:S(2)}) collective-permute-start(bf16[32,3200]{1,0:T(8,128)(2,1)S(1)} %get-tuple-element.107), channel_id=1, source_target_pairs={{0,6},{1,7},{2,0},{3,1},{4,2},{5,3},{6,4},{7,5},{8,14},{9,15},{10,... | collective-permute-start | bytes 614408 | tf_op jit(solution)/shard_map/ppermute | solution.py:291
  130.6 10.1 %copy-start.71 = (pred[8]{0:T(512)(128)(4,1)S(1)}, pred[8]{0:T(512)(128)(4,1)}, u32[]{:S(2)}) copy-start(pred[8]{0:T(512)(128)(4,1)} %get-tuple-element.132) | copy-start | bytes 28
  130.6 114.1 %all-gather.6.cloned.1.call-start = ((), (), s32[]{:S(2)}) async-start(), calls=%async_computation.5 | async-start | bytes 1843200 | tf_op jit(solution)/shard_map/all_gather | solution.py:263
  133.1 7.9 %copy-start.58 = (f32[8]{0:T(128)}, f32[8]{0:T(128)S(1)}, u32[]{:S(2)}) copy-start(f32[8]{0:T(128)S(1)} %broadcast_multiply_fusion.5) | copy-start | bytes 100
  133.7 7.3 %copy-start.66 = (f32[8]{0:T(128)}, f32[8]{0:T(128)S(1)}, u32[]{:S(2)}) copy-start(f32[8]{0:T(128)S(1)} %add_rsqrt_fusion.1) | copy-start | bytes 100
  133.8 12.5 %collective-permute-start.11 = (bf16[8,12800]{1,0:T(8,128)(2,1)S(1)}, bf16[8,12800]{1,0:T(8,128)(2,1)S(1)}, u32[]{:S(2)}, u32[]{:S(2)}) collective-permute-start(bf16[8,12800]{1,0:T(8,128)(2,1)S(1)} %multiply_convert_fusion.5.refs_0_), channel_id=1, source_target_pairs={{0,2},{1,3},{2,4},{3,5},{4,6},{5,7},{6,0},{7,1},{8,10},{9,11},{10,... | collective-permute-start | bytes 614408 | tf_op jit(solution)/shard_map/ppermute | solution.py:291
  138.3 20.0 %collective-permute-start.12 = (bf16[8,12800]{1,0:T(8,128)(2,1)S(1)}, bf16[8,12800]{1,0:T(8,128)(2,1)S(1)}, u32[]{:S(2)}, u32[]{:S(2)}) collective-permute-start(bf16[8,12800]{1,0:T(8,128)(2,1)S(1)} %multiply_convert_fusion.5.refs_0_), channel_id=1, source_target_pairs={{0,4},{1,5},{2,6},{3,7},{4,0},{5,1},{6,2},{7,3},{8,12},{9,13},{10,... | collective-permute-start | bytes 614408 | tf_op jit(solution)/shard_map/ppermute | solution.py:291
  138.3 20.0 %collective-permute-start.13 = (bf16[8,12800]{1,0:T(8,128)(2,1)S(1)}, bf16[8,12800]{1,0:T(8,128)(2,1)S(1)}, u32[]{:S(2)}, u32[]{:S(2)}) collective-permute-start(bf16[8,12800]{1,0:T(8,128)(2,1)S(1)} %multiply_convert_fusion.5.refs_0_), channel_id=1, source_target_pairs={{0,6},{1,7},{2,0},{3,1},{4,2},{5,3},{6,4},{7,5},{8,14},{9,15},{10,... | collective-permute-start | bytes 614408 | tf_op jit(solution)/shard_map/ppermute | solution.py:291
  140.8 42.1 %collective-permute-start.14 = (bf16[8,12800]{1,0:T(8,128)(2,1)S(1)}, bf16[8,12800]{1,0:T(8,128)(2,1)S(1)}, u32[]{:S(2)}, u32[]{:S(2)}) collective-permute-start(bf16[8,12800]{1,0:T(8,128)(2,1)S(1)} %multiply_convert_fusion.5.refs_0_), channel_id=1, source_target_pairs={{0,1},{1,0},{2,3},{3,2},{4,5},{5,4},{6,7},{7,6},{8,9},{9,8},{10,11... | collective-permute-start | bytes 614408 | tf_op jit(solution)/shard_map/ppermute | solution.py:295
  146.3 36.6 %collective-permute-start.15 = (bf16[8,12800]{1,0:T(8,128)(2,1)S(1)}, bf16[8,12800]{1,0:T(8,128)(2,1)S(1)}, u32[]{:S(2)}, u32[]{:S(2)}) collective-permute-start(bf16[8,12800]{1,0:T(8,128)(2,1)S(1)} %collective-permute-done.11.refs_1_), channel_id=1, source_target_pairs={{0,1},{1,0},{2,3},{3,2},{4,5},{5,4},{6,7},{7,6},{8,9},{9,8},{10,11... | collective-permute-start | bytes 614408 | tf_op jit(solution)/shard_map/ppermute | solution.py:295
  158.3 24.6 %collective-permute-start.16 = (bf16[8,12800]{1,0:T(8,128)(2,1)S(1)}, bf16[8,12800]{1,0:T(8,128)(2,1)S(1)}, u32[]{:S(2)}, u32[]{:S(2)}) collective-permute-start(bf16[8,12800]{1,0:T(8,128)(2,1)S(1)} %collective-permute-done.12.refs_2_), channel_id=1, source_target_pairs={{0,1},{1,0},{2,3},{3,2},{4,5},{5,4},{6,7},{7,6},{8,9},{9,8},{10,11... | collective-permute-start | bytes 614408 | tf_op jit(solution)/shard_map/ppermute | solution.py:295
  158.3 24.6 %collective-permute-start.17 = (bf16[8,12800]{1,0:T(8,128)(2,1)S(1)}, bf16[8,12800]{1,0:T(8,128)(2,1)}, u32[]{:S(2)}, u32[]{:S(2)}) collective-permute-start(bf16[8,12800]{1,0:T(8,128)(2,1)S(1)} %collective-permute-done.13.refs_3_), channel_id=1, source_target_pairs={{0,1},{1,0},{2,3},{3,2},{4,5},{5,4},{6,7},{7,6},{8,9},{9,8},{10,11... | collective-permute-start | bytes 614408 | tf_op jit(solution)/shard_map/ppermute | solution.py:295
  204.3 2.4 collective-permute-start.21
  208.1 10.1 %collective-permute-start.24 = (bf16[8,12800]{1,0:T(8,128)(2,1)S(1)}, bf16[8,12800]{1,0:T(8,128)(2,1)S(1)}, u32[]{:S(2)}, u32[]{:S(2)}) collective-permute-start(bf16[8,12800]{1,0:T(8,128)(2,1)S(1)} %get-tuple-element.105), channel_id=1, source_target_pairs={{0,2},{1,3},{2,4},{3,5},{4,6},{5,7},{6,0},{7,1},{8,10},{9,11},{10,... | collective-permute-start | bytes 614408 | tf_op jit(solution)/shard_map/ppermute | solution.py:291
  210.8 21.9 %collective-permute-start.23 = (bf16[8,12800]{1,0:T(8,128)(2,1)S(1)}, bf16[8,12800]{1,0:T(8,128)(2,1)S(1)}, u32[]{:S(2)}, u32[]{:S(2)}) collective-permute-start(bf16[8,12800]{1,0:T(8,128)(2,1)S(1)} %get-tuple-element.106), channel_id=1, source_target_pairs={{0,4},{1,5},{2,6},{3,7},{4,0},{5,1},{6,2},{7,3},{8,12},{9,13},{10,... | collective-permute-start | bytes 614408 | tf_op jit(solution)/shard_map/ppermute | solution.py:291
  211.7 21.1 %collective-permute-start.22 = (bf16[8,12800]{1,0:T(8,128)(2,1)S(1)}, bf16[8,12800]{1,0:T(8,128)(2,1)S(1)}, u32[]{:S(2)}, u32[]{:S(2)}) collective-permute-start(bf16[8,12800]{1,0:T(8,128)(2,1)S(1)} %get-tuple-element.104), channel_id=1, source_target_pairs={{0,6},{1,7},{2,0},{3,1},{4,2},{5,3},{6,4},{7,5},{8,14},{9,15},{10,... | collective-permute-start | bytes 614408 | tf_op jit(solution)/shard_map/ppermute | solution.py:291
  214.5 89.1 %reduce-scatter.6.cloned.1.call-start = ((), (), s32[]{:S(2)}) async-start(), calls=%async_computation.6 | async-start | bytes 1843200 | tf_op jit(solution)/shard_map/reduce_scatter | solution.py:266
  269.1 99.9 %all-gather.8.cloned.1.call-start = ((), (), s32[]{:S(2)}) async-start(), calls=%async_computation.7 | async-start | bytes 1843200 | tf_op jit(solution)/shard_map/all_gather | solution.py:263
  270.4 34.2 %copy-start.42 = (f32[8,12800]{1,0:T(8,128)S(1)}, f32[8,12800]{1,0:T(8,128)}, u32[]{:S(2)}) copy-start(f32[8,12800]{1,0:T(8,128)} %reshape.302) | copy-start | bytes 1228804
  270.4 34.2 %copy-start.61 = (f32[8]{0:T(128)S(1)}, f32[8]{0:T(128)}, u32[]{:S(2)}) copy-start(f32[8]{0:T(128)} %copy-done.60) | copy-start | bytes 100
  270.5 34.2 %copy-start.69 = (f32[8]{0:T(128)S(1)}, f32[8]{0:T(128)}, u32[]{:S(2)}) copy-start(f32[8]{0:T(128)} %copy-done.68) | copy-start | bytes 100
  272.5 33.4 %copy-start.43 = (f32[32,3200]{1,0:T(8,128)}, f32[32,3200]{1,0:T(8,128)S(1)}, u32[]{:S(2)}) copy-start(f32[32,3200]{1,0:T(8,128)S(1)} %reshape.303) | copy-start | bytes 1228804
  305.0 26.5 %copy-start.57 = (s32[4]{0:T(128)S(1)}, s32[4]{0:T(128)}, u32[]{:S(2)}) copy-start(s32[4]{0:T(128)} %get-tuple-element.131) | copy-start | bytes 52
  305.0 34.5 %copy-start.77 = (s32[8]{0:T(128)S(1)}, s32[8]{0:T(128)}, u32[]{:S(2)}) copy-start(s32[8]{0:T(128)} %get-tuple-element.82) | copy-start | bytes 100
  307.8 134.8 %reduce-scatter.8.cloned.1.call-start = ((), (), s32[]{:S(2)}) async-start(), calls=%async_computation.8 | async-start | bytes 1843200 | tf_op jit(solution)/shard_map/reduce_scatter | solution.py:266
  307.9 9.9 %collective-permute-start.25 = (bf16[32,3200]{1,0:T(8,128)(2,1)S(1)}, bf16[32,3200]{1,0:T(8,128)(2,1)S(1)}, u32[]{:S(2)}, u32[]{:S(2)}) collective-permute-start(bf16[32,3200]{1,0:T(8,128)(2,1)S(1)} %multiply_convert_fusion.2.refs_0_), channel_id=1, source_target_pairs={{0,2},{1,3},{2,4},{3,5},{4,6},{5,7},{6,0},{7,1},{8,10},{9,11},{10,... | collective-permute-start | bytes 614408 | tf_op jit(solution)/shard_map/ppermute | solution.py:291
  308.0 21.6 %collective-permute-start.26 = (bf16[32,3200]{1,0:T(8,128)(2,1)S(1)}, bf16[32,3200]{1,0:T(8,128)(2,1)S(1)}, u32[]{:S(2)}, u32[]{:S(2)}) collective-permute-start(bf16[32,3200]{1,0:T(8,128)(2,1)S(1)} %multiply_convert_fusion.2.refs_0_), channel_id=1, source_target_pairs={{0,4},{1,5},{2,6},{3,7},{4,0},{5,1},{6,2},{7,3},{8,12},{9,13},{10,... | collective-permute-start | bytes 614408 | tf_op jit(solution)/shard_map/ppermute | solution.py:291
  308.0 22.3 %collective-permute-start.27 = (bf16[32,3200]{1,0:T(8,128)(2,1)S(1)}, bf16[32,3200]{1,0:T(8,128)(2,1)S(1)}, u32[]{:S(2)}, u32[]{:S(2)}) collective-permute-start(bf16[32,3200]{1,0:T(8,128)(2,1)S(1)} %multiply_convert_fusion.2.refs_0_), channel_id=1, source_target_pairs={{0,6},{1,7},{2,0},{3,1},{4,2},{5,3},{6,4},{7,5},{8,14},{9,15},{10,... | collective-permute-start | bytes 614408 | tf_op jit(solution)/shard_map/ppermute | solution.py:291
  311.8 28.9 %collective-permute-start.28 = (bf16[32,3200]{1,0:T(8,128)(2,1)S(1)}, bf16[32,3200]{1,0:T(8,128)(2,1)S(1)}, u32[]{:S(2)}, u32[]{:S(2)}) collective-permute-start(bf16[32,3200]{1,0:T(8,128)(2,1)S(1)} %multiply_convert_fusion.2.refs_0_), channel_id=1, source_target_pairs={{0,1},{1,0},{2,3},{3,2},{4,5},{5,4},{6,7},{7,6},{8,9},{9,8},{10,11... | collective-permute-start | bytes 614408 | tf_op jit(solution)/shard_map/ppermute | solution.py:295
  317.8 24.9 %copy-start.21 = (bf16[32,3200]{1,0:T(8,128)(2,1)}, bf16[32,3200]{1,0:T(8,128)(2,1)S(1)}, u32[]{:S(2)}) copy-start(bf16[32,3200]{1,0:T(8,128)(2,1)S(1)} %collective-permute-done.25.refs_1_) | copy-start | bytes 614404
  317.8 23.5 %collective-permute-start.29 = (bf16[32,3200]{1,0:T(8,128)(2,1)S(1)}, bf16[32,3200]{1,0:T(8,128)(2,1)S(1)}, u32[]{:S(2)}, u32[]{:S(2)}) collective-permute-start(bf16[32,3200]{1,0:T(8,128)(2,1)S(1)} %collective-permute-done.25.refs_1_), channel_id=1, source_target_pairs={{0,1},{1,0},{2,3},{3,2},{4,5},{5,4},{6,7},{7,6},{8,9},{9,8},{10,11... | collective-permute-start | bytes 614408 | tf_op jit(solution)/shard_map/ppermute | solution.py:295
  329.6 12.4 %collective-permute-start.30 = (bf16[32,3200]{1,0:T(8,128)(2,1)S(1)}, bf16[32,3200]{1,0:T(8,128)(2,1)S(1)}, u32[]{:S(2)}, u32[]{:S(2)}) collective-permute-start(bf16[32,3200]{1,0:T(8,128)(2,1)S(1)} %collective-permute-done.26.refs_2_), channel_id=1, source_target_pairs={{0,1},{1,0},{2,3},{3,2},{4,5},{5,4},{6,7},{7,6},{8,9},{9,8},{10,11... | collective-permute-start | bytes 614408 | tf_op jit(solution)/shard_map/ppermute | solution.py:295
  330.3 12.4 %collective-permute-start.31 = (bf16[32,3200]{1,0:T(8,128)(2,1)S(1)}, bf16[32,3200]{1,0:T(8,128)(2,1)S(1)}, u32[]{:S(2)}, u32[]{:S(2)}) collective-permute-start(bf16[32,3200]{1,0:T(8,128)(2,1)S(1)} %collective-permute-done.27.refs_3_), channel_id=1, source_target_pairs={{0,1},{1,0},{2,3},{3,2},{4,5},{5,4},{6,7},{7,6},{8,9},{9,8},{10,11... | collective-permute-start | bytes 614408 | tf_op jit(solution)/shard_map/ppermute | solution.py:295
  368.9 23.3 %collective-permute-start.32 = (bf16[128,3200]{1,0:T(8,128)(2,1)S(1)}, bf16[128,3200]{1,0:T(8,128)(2,1)}, u32[]{:S(2)}, u32[]{:S(2)}) collective-permute-start(bf16[128,3200]{1,0:T(8,128)(2,1)S(1)} %slice.162), channel_id=1, source_target_pairs={{0,1},{1,0},{2,3},{3,2},{4,5},{5,4},{6,7},{7,6},{8,9},{9,8},{10,11... | collective-permute-start | bytes 2457608 | tf_op jit(solution)/shard_map/ppermute | solution.py:303
  393.5 49.1 %copy-start.39 = (bf16[64,3200]{1,0:T(8,128)(2,1)S(1)}, bf16[64,3200]{1,0:T(8,128)(2,1)}, u32[]{:S(2)}) copy-start(bf16[64,3200]{1,0:T(8,128)(2,1)} %param.12) | copy-start | bytes 1228804
  393.6 49.1 %copy-start.55 = (f32[3200]{0:T(1024)S(1)}, f32[3200]{0:T(1024)}, u32[]{:S(2)}) copy-start(f32[3200]{0:T(1024)} %param.13) | copy-start | bytes 38404
  393.6 49.1 %copy-start.63 = (f32[32]{0:T(128)S(1)}, f32[32]{0:T(128)}, u32[]{:S(2)}) copy-start(f32[32]{0:T(128)} %copy-done.62) | copy-start | bytes 388
  393.6 49.1 %copy-start.65 = (f32[32]{0:T(128)S(1)}, f32[32]{0:T(128)}, u32[]{:S(2)}) copy-start(f32[32]{0:T(128)} %copy-done.64) | copy-start | bytes 388
  394.4 27.1 %collective-permute-start.35 = (bf16[32,3200]{1,0:T(8,128)(2,1)}, bf16[32,3200]{1,0:T(8,128)(2,1)}, u32[]{:S(2)}, u32[]{:S(2)}) collective-permute-start(bf16[32,3200]{1,0:T(8,128)(2,1)} %get-tuple-element.102), channel_id=1, source_target_pairs={{0,2},{1,3},{2,4},{3,5},{4,6},{5,7},{6,0},{7,1},{8,10},{9,11},{10,... | collective-permute-start | bytes 614408 | tf_op jit(solution)/shard_map/ppermute | solution.py:291
  404.8 17.3 %collective-permute-start.34 = (bf16[32,3200]{1,0:T(8,128)(2,1)S(1)}, bf16[32,3200]{1,0:T(8,128)(2,1)}, u32[]{:S(2)}, u32[]{:S(2)}) collective-permute-start(bf16[32,3200]{1,0:T(8,128)(2,1)S(1)} %get-tuple-element.103), channel_id=1, source_target_pairs={{0,4},{1,5},{2,6},{3,7},{4,0},{5,1},{6,2},{7,3},{8,12},{9,13},{10,... | collective-permute-start | bytes 614408 | tf_op jit(solution)/shard_map/ppermute | solution.py:291
  404.8 24.2 %collective-permute-start.33 = (bf16[32,3200]{1,0:T(8,128)(2,1)S(1)}, bf16[32,3200]{1,0:T(8,128)(2,1)}, u32[]{:S(2)}, u32[]{:S(2)}) collective-permute-start(bf16[32,3200]{1,0:T(8,128)(2,1)S(1)} %get-tuple-element.101), channel_id=1, source_target_pairs={{0,6},{1,7},{2,0},{3,1},{4,2},{5,3},{6,4},{7,5},{8,14},{9,15},{10,... | collective-permute-start | bytes 614408 | tf_op jit(solution)/shard_map/ppermute | solution.py:291
  407.9 36.2 %copy-start.44 = (f32[32,3200]{1,0:T(8,128)S(1)}, f32[32,3200]{1,0:T(8,128)}, u32[]{:S(2)}) copy-start(f32[32,3200]{1,0:T(8,128)} %copy-done.43) | copy-start | bytes 1228804
  407.9 36.2 %copy-start.46 = (f32[32,3200]{1,0:T(8,128)S(1)}, f32[32,3200]{1,0:T(8,128)}, u32[]{:S(2)}) copy-start(f32[32,3200]{1,0:T(8,128)} %copy-done.45) | copy-start | bytes 1228804
  407.9 5.2 %collective-permute-start.36 = (bf16[32,1024]{1,0:T(8,128)(2,1)S(1)}, bf16[32,1024]{1,0:T(8,128)(2,1)S(1)}, u32[]{:S(2)}, u32[]{:S(2)}) collective-permute-start(bf16[32,1024]{1,0:T(8,128)(2,1)S(1)} %get-tuple-element.116), channel_id=1, source_target_pairs={{0,8},{8,16},{16,24},{24,0},{1,9},{9,17},{17,25},{25,1},{2,10},{10... | collective-permute-start | bytes 196616 | tf_op jit(solution)/shard_map/ppermute | solution.py:406
  409.3 9.0 %collective-permute-start.37 = (bf16[32,1024]{1,0:T(8,128)(2,1)}, bf16[32,1024]{1,0:T(8,128)(2,1)S(1)}, u32[]{:S(2)}, u32[]{:S(2)}) collective-permute-start(bf16[32,1024]{1,0:T(8,128)(2,1)} %get-tuple-element.115), channel_id=1, source_target_pairs={{0,16},{8,24},{16,0},{24,8},{1,17},{9,25},{17,1},{25,9},{2,18},{10... | collective-permute-start | bytes 196616 | tf_op jit(solution)/shard_map/ppermute | solution.py:406
  413.7 6.2 %collective-permute-start.38 = (bf16[32,1024]{1,0:T(8,128)(2,1)}, bf16[32,1024]{1,0:T(8,128)(2,1)S(1)}, u32[]{:S(2)}, u32[]{:S(2)}) collective-permute-start(bf16[32,1024]{1,0:T(8,128)(2,1)} %get-tuple-element.114), channel_id=1, source_target_pairs={{0,24},{8,0},{16,8},{24,16},{1,25},{9,1},{17,9},{25,17},{2,26},{10... | collective-permute-start | bytes 196616 | tf_op jit(solution)/shard_map/ppermute | solution.py:406
  (60 other events, 96.6 us)
Sparse Core Ops, SparseCore 0:
  19.1 30.6 all-gather.3
  130.7 43.8 reduce-scatter.3
  214.6 30.0 all-gather.5
  269.3 34.3 reduce-scatter.5
  308.0 33.0 all-gather.7
  391.3 51.3 reduce-scatter.7

commit v4 on v3

--- a/solution.py
+++ b/solution.py
@@ -61,16 +61,16 @@
 
 def forward_kernel(count, steps, *refs):
     pieces = refs[:count]
-    first, second, out, slope, pre, hidden = refs[count:]
+    first, second, near, far, slope, pre, hidden = refs[count:]
     i = pl.program_id(0)
 
     @pl.when(i == 0)
     def _():
-        pre[...] = jnp.dot(laid(pieces), first[...], preferred_element_type=jnp.float32)
+        pre[...] = times_transposed(laid(pieces), first[...])
 
     @pl.when(jnp.logical_and(i > 0, i < steps))
     def _():
-        pre[...] += jnp.dot(laid(pieces), first[...], preferred_element_type=jnp.float32)
+        pre[...] += times_transposed(laid(pieces), first[...])
 
     @pl.when(i == steps - 1)
     def _():
@@ -85,14 +85,14 @@
 
     @pl.when(i >= steps)
     def _():
-        out[...] = jnp.dot(
-            hidden[...], second[...], preferred_element_type=jnp.float32
-        ).astype(jnp.bfloat16)
+        both = jnp.dot(hidden[...], second[...], preferred_element_type=jnp.float32)
+        near[...] = both[: near.shape[0]].astype(jnp.bfloat16)
+        far[...] = both[near.shape[0] :].astype(jnp.bfloat16)
 
 
 def backward_kernel(count, steps, *refs):
     pieces = refs[:count]
-    first, second, slope, out, total, delta = refs[count:]
+    second, first, slope, near, far, total, delta = refs[count:]
     i = pl.program_id(0)
 
     @pl.when(i == 0)
@@ -112,12 +112,14 @@
 
     @pl.when(i >= steps)
     def _():
-        out[...] = times_transposed(delta[...], first[...]).astype(jnp.bfloat16)
+        both = jnp.dot(delta[...], first[...], preferred_element_type=jnp.float32)
+        near[...] = both[: near.shape[0]].astype(jnp.bfloat16)
+        far[...] = both[near.shape[0] :].astype(jnp.bfloat16)
 
 
 def project_kernel(count, chunk, *refs):
     pieces = refs[:count]
-    weight, upstream, projected, back, rows, total = refs[count:]
+    weight, upstream, projected, near, far, rows, total = refs[count:]
     i = pl.program_id(0)
     depth = weight.shape[0]
 
@@ -145,80 +147,47 @@
 
     @pl.when(i == pl.num_programs(0) - 1)
     def _():
-        back[...] = total[...].astype(jnp.bfloat16)
-
-
-def settings(limit):
+        half = near.shape[0]
+        near[...] = total[:half].astype(jnp.bfloat16)
+        far[...] = total[half:].astype(jnp.bfloat16)
+
+
+def settings():
     return pltpu.CompilerParams(
-        vmem_limit_bytes=limit * 1024 * 1024, dimension_semantics=("arbitrary",)
+        vmem_limit_bytes=56 * 1024 * 1024, dimension_semantics=("arbitrary",)
     )
 
 
-def vision_mlp(pieces, first, second):
+def vision_pass(kernel, pieces, early, late, slope=None):
     rows = sum(p.shape[0] for p in pieces)
-    width, units = first.shape
+    units, width = early.shape
     tile = tile_of(width, 640)
     steps = width // tile
-    early = lambda i: jnp.minimum(i, steps - 1)
-    late = lambda i: jnp.maximum(i - steps, 0)
+    soon = lambda i: (0, jnp.minimum(i, steps - 1))
+    then = lambda i: (0, jnp.maximum(i - steps, 0))
+    slopes = pl.BlockSpec((rows, units), lambda i: (0, 0))
+    sums = [pl.BlockSpec((rows // 2, tile), then)] * 2
+    shapes = [jax.ShapeDtypeStruct((rows // 2, width), jnp.bfloat16)] * 2
+    given = [] if slope is None else [slope]
     return pl.pallas_call(
-        functools.partial(forward_kernel, len(pieces), steps),
+        functools.partial(kernel, len(pieces), steps),
         grid=(2 * steps,),
-        in_specs=[pl.BlockSpec((p.shape[0], tile), lambda i: (0, early(i))) for p in pieces]
-        + [
-            pl.BlockSpec((tile, units), lambda i: (early(i), 0)),
-            pl.BlockSpec((units, tile), lambda i: (0, late(i))),
-        ],
-        out_specs=[
-            pl.BlockSpec((rows, tile), lambda i: (0, late(i))),
-            pl.BlockSpec((rows, units), lambda i: (0, 0)),
-        ],
-        out_shape=[
-            jax.ShapeDtypeStruct((rows, width), jnp.bfloat16),
-            jax.ShapeDtypeStruct((rows, units), jnp.float32),
-        ],
+        in_specs=[pl.BlockSpec((p.shape[0], tile), soon) for p in pieces]
+        + [pl.BlockSpec((units, tile), soon), pl.BlockSpec((units, tile), then)]
+        + [slopes] * len(given),
+        out_specs=sums + [slopes] * (1 - len(given)),
+        out_shape=shapes + [jax.ShapeDtypeStruct((rows, units), jnp.float32)] * (1 - len(given)),
         scratch_shapes=[
             pltpu.VMEM((rows, units), jnp.float32),
             pltpu.VMEM((rows, units), jnp.bfloat16),
         ],
-        compiler_params=settings(28),
+        compiler_params=settings(),
         cost_estimate=pl.CostEstimate(
             flops=4 * rows * width * units,
             bytes_accessed=4 * width * units + 4 * rows * (width + units),
             transcendentals=2 * rows * units,
         ),
-    )(*pieces, first, second)
-
-
-def vision_back(pieces, first, second, slope):
-    rows = sum(p.shape[0] for p in pieces)
-    width, units = first.shape
-    tile = tile_of(width, 640)
-    steps = width // tile
-    early = lambda i: jnp.minimum(i, steps - 1)
-    late = lambda i: jnp.maximum(i - steps, 0)
-    return pl.pallas_call(
-        functools.partial(backward_kernel, len(pieces), steps),
-        grid=(2 * steps,),
-        in_specs=[pl.BlockSpec((p.shape[0], tile), lambda i: (0, early(i))) for p in pieces]
-        + [
-            pl.BlockSpec((tile, units), lambda i: (late(i), 0)),
-            pl.BlockSpec((units, tile), lambda i: (0, early(i))),
-            pl.BlockSpec((rows, units), lambda i: (0, 0)),
-        ],
-        out_specs=pl.BlockSpec((rows, tile), lambda i: (0, late(i))),
-        out_shape=jax.ShapeDtypeStruct((rows, width), jnp.bfloat16),
-        scratch_shapes=[
-            pltpu.VMEM((rows, units), jnp.float32),
-            pltpu.VMEM((rows, units), jnp.bfloat16),
-        ],
-        compiler_params=settings(28),
-        cost_estimate=pl.CostEstimate(
-            flops=4 * rows * width * units,
-            bytes_accessed=4 * width * units + 4 * rows * (width + units),
-            transcendentals=0,
-        ),
-    )(*pieces, first, second, slope)
+    )(*pieces, early, late, *given)
 
 
 def project(pieces, weight, upstream):
@@ -235,42 +204,22 @@
         ],
         out_specs=[
             pl.BlockSpec((rows, tile), lambda i: (0, i)),
-            pl.BlockSpec((rows, depth), lambda i: (0, 0)),
+            pl.BlockSpec((rows // 2, depth), lambda i: (0, 0)),
+            pl.BlockSpec((rows // 2, depth), lambda i: (0, 0)),
         ],
-        out_shape=[
-            jax.ShapeDtypeStruct((rows, units), jnp.bfloat16),
-            jax.ShapeDtypeStruct((rows, depth), jnp.bfloat16),
-        ],
+        out_shape=[jax.ShapeDtypeStruct((rows, units), jnp.bfloat16)]
+        + [jax.ShapeDtypeStruct((rows // 2, depth), jnp.bfloat16)] * 2,
         scratch_shapes=[
             pltpu.VMEM((rows, depth), jnp.bfloat16),
             pltpu.VMEM((rows, depth), jnp.float32),
         ],
-        compiler_params=settings(40),
+        compiler_params=settings(),
         cost_estimate=pl.CostEstimate(
             flops=4 * rows * depth * units,
             bytes_accessed=2 * depth * units + 4 * rows * (depth + units),
             transcendentals=2 * rows * units,
         ),
     )(*pieces, weight, upstream)
-
-
-def after(values, *tokens):
-    return lax.optimization_barrier((values, tokens))[0]
-
-
-class Whole:
-    def gather(self, block):
-        return [lax.all_gather(block, "tp", axis=0, tiled=True)]
-
-    def scatter(self, partial):
-        summed = lax.psum_scatter(partial, "tp", scatter_dimension=0, tiled=True)
-        return summed.astype(jnp.float32)
-
-    def by_rank(self, rows, size):
-        return rows.reshape(size, -1, rows.shape[-1])
-
-    def by_row(self, ranks):
-        return ranks.reshape(-1, ranks.shape[-1])
 
 
 class Direct:
@@ -290,23 +239,26 @@
         pairs = [(a, (a + k * cores) % self.size) for a in range(self.size)]
         return lax.ppermute(block, "tp", pairs)
 
-    def gather(self, block):
-        mine = [block] + [self.shift(block, k) for k in range(1, self.places)]
+    def spread(self, block):
+        return [block] + [self.shift(block, k) for k in range(1, self.places)]
+
+    def gathered(self, mine):
         other = [lax.ppermute(m, "tp", self.pairs) for m in mine]
-        if block.shape[0] % 8:
+        if mine[0].shape[0] % 8:
             return [jnp.concatenate(mine + other, 0)]
         return mine + other
 
-    def scatter(self, partial):
-        half = partial.shape[0] // cores
-        rows = half // self.places
-        got = lax.ppermute(partial[half:], "tp", self.pairs)
-        both = partial[:half].astype(jnp.float32) + got.astype(jnp.float32)
-        total = both[:rows]
-        for k in range(1, self.places):
-            sent = both[k * rows : (k + 1) * rows].astype(jnp.bfloat16)
-            total = total + self.shift(sent, -k).astype(jnp.float32)
-        return total
+    def send(self, near, far):
+        rows = near.shape[0] // self.places
+        got = lax.ppermute(far, "tp", self.pairs)
+        both = near.astype(jnp.float32) + got.astype(jnp.float32)
+        cut = [both[k * rows : (k + 1) * rows] for k in range(self.places)]
+        return cut[:1] + [
+            self.shift(cut[k].astype(jnp.bfloat16), -k) for k in range(1, self.places)
+        ]
+
+    def summed(self, terms):
+        return sum([t.astype(jnp.float32) for t in terms[1:]], terms[0])
 
     def by_rank(self, rows, size):
         return jnp.take(rows.reshape(size, -1, rows.shape[-1]), self.blocks, axis=0)
@@ -327,7 +279,7 @@
     dest_row,
     cotangent,
 ):
-    moves = [Whole(), Direct()]
+    moves = Direct()
     groups = lax.axis_size("grp")
     size = lax.axis_size("tp")
     grp_rank = lax.axis_index("grp")
@@ -347,8 +299,11 @@
         normed.append(scaled.astype(jnp.bfloat16))
         hat.append(own_hat)
         inv.append(own_inv)
-    patches_a = moves[0].gather(normed[0])
-    patches_b = moves[1].gather(normed[1])
+    tied = lax.optimization_barrier
+    rail_b = moves.spread(normed[1])
+    normed[0], rail_b = tied((normed[0], rail_b))
+    rail_a = moves.spread(normed[0])
+    patches_b = moves.gathered(rail_b)
 
     starts = dest_row.reshape(groups, images, image_rows)[:, :, 0]
     start_pos = starts % seq_len
@@ -368,7 +323,7 @@
         picked.append(block)
     returned = jnp.take(jnp.stack(picked), shift, axis=0).reshape(size, -1, width)
     grad_proj = [
-        moves[c].by_row(returned[:, c * merged_rows : (c + 1) * merged_rows]) for c in range(chunks)
+        moves.by_row(returned[:, c * merged_rows : (c + 1) * merged_rows]) for c in range(chunks)
     ]
 
     def merge(c, summed):
@@ -382,22 +337,30 @@
         own_grad = merged_grad.reshape(rows, vis_width).astype(jnp.float32)
         return own_grad, (own_grad * layer_scale).astype(jnp.bfloat16)
 
-    part_b, slope_b = vision_mlp(patches_b, first_weight, second_weight)
-    summed_b = moves[1].scatter(part_b)
-    patches_a = after(patches_a, part_b)
-    part_a, slope_a = vision_mlp(patches_a, first_weight, second_weight)
-    summed_a = moves[0].scatter(part_a)
-    mixed_b, *stats_b = merge(1, after(summed_b, part_a))
-    merged_b = moves[1].gather(mixed_b)
-    mixed_a, *stats_a = merge(0, after(summed_a, mixed_b))
-    merged_a = moves[0].gather(mixed_a)
-    projected_b, back_b = project(after(merged_b, mixed_a), proj_weight, grad_proj[1])
-    summed_b = moves[1].scatter(back_b)
-    projected_a, back_a = project(after(merged_a, back_b), proj_weight, grad_proj[0])
-    summed_a = moves[0].scatter(back_a)
+    early, late = first_weight.T, second_weight
+    near_b, far_b, slope_b = vision_pass(forward_kernel, patches_b, early, late)
+    near_b, far_b, rail_a = tied((near_b, far_b, rail_a))
+    patches_a = moves.gathered(rail_a)
+    terms_b = moves.send(near_b, far_b)
+    near_a, far_a, slope_a = vision_pass(forward_kernel, patches_a, early, late)
+    near_a, far_a, terms_b = tied((near_a, far_a, terms_b))
+    terms_a = moves.send(near_a, far_a)
+    mixed_b, *stats_b = merge(1, moves.summed(terms_b))
+    rail_b = moves.spread(mixed_b)
+    rail_b, terms_a = tied((rail_b, terms_a))
+    mixed_a, *stats_a = merge(0, moves.summed(terms_a))
+    rail_a = moves.spread(mixed_a)
+    merged_b = moves.gathered(rail_b)
+    projected_b, near_b, far_b = project(merged_b, proj_weight, grad_proj[1])
+    near_b, far_b, rail_a = tied((near_b, far_b, rail_a))
+    merged_a = moves.gathered(rail_a)
+    terms_b = moves.send(near_b, far_b)
+    projected_a, near_a, far_a = project(merged_a, proj_weight, grad_proj[0])
+    near_a, far_a, terms_b = tied((near_a, far_a, terms_b))
+    terms_a = moves.send(near_a, far_a)
 
     projected = jnp.concatenate(
-        [moves[0].by_rank(projected_a, size), moves[1].by_rank(projected_b, size)], 1
+        [moves.by_rank(projected_a, size), moves.by_rank(projected_b, size)], 1
     ).reshape(images, image_rows, width)
     seq_embed = text_embed
     for s in range(groups):
@@ -409,17 +372,20 @@
             block = jnp.where(used[s], block, there)
         seq_embed = lax.dynamic_update_slice_in_dim(seq_embed, block, spot[s], 0)
 
-    own_b, scaled_b = unmerge(after(summed_b, back_a), *stats_b)
-    grad_out_b = moves[1].gather(scaled_b)
-    own_a, scaled_a = unmerge(after(summed_a, scaled_b), *stats_a)
-    grad_out_a = moves[0].gather(scaled_a)
-    grad_out_b = after(grad_out_b, scaled_a)
-    deep_b = vision_back(grad_out_b, first_weight, second_weight, slope_b)
-    normed_b = moves[1].scatter(deep_b)
-    grad_out_a = after(grad_out_a, deep_b)
-    deep_a = vision_back(grad_out_a, first_weight, second_weight, slope_a)
-    normed_a = moves[0].scatter(deep_a)
-    normed_b, seq_embed = after((normed_b, seq_embed), deep_a)
+    own_b, scaled_b = unmerge(moves.summed(terms_b), *stats_b)
+    rail_b = moves.spread(scaled_b)
+    rail_b, terms_a = tied((rail_b, terms_a))
+    own_a, scaled_a = unmerge(moves.summed(terms_a), *stats_a)
+    rail_a = moves.spread(scaled_a)
+    grad_out_b = moves.gathered(rail_b)
+    near_b, far_b = vision_pass(backward_kernel, grad_out_b, late, early, slope_b)
+    near_b, far_b, rail_a = tied((near_b, far_b, rail_a))
+    grad_out_a = moves.gathered(rail_a)
+    terms_b = moves.send(near_b, far_b)
+    near_a, far_a = vision_pass(backward_kernel, grad_out_a, late, early, slope_a)
+    near_a, far_a, terms_b, seq_embed = tied((near_a, far_a, terms_b, seq_embed))
+    normed_a = moves.summed(moves.send(near_a, far_a))
+    normed_b = moves.summed(terms_b)
     grads = [
         own_a + norm_back(normed_a, vis_gain, hat[0], inv[0]),
         own_b + norm_back(normed_b, vis_gain, hat[1], inv[1]),

time: 455 us -> 322 us (0.71)
  local copies, waits for them, and re-layouts: 102 us -> 24 us
  waiting for transfers between devices: 148 us -> 75.1 us
  starting transfers between devices: 52.3 us -> 79 us
  Pallas kernels: 88.9 us -> 113 us
  other arithmetic: 32.2 us -> 12.5 us
  between operations: 29.8 us -> 16.6 us
    unnamed x160 -> x141, local copies, waits for them, and re-layouts: 80.9 us -> 8.63 us
    reduce_scatter x3 -> x0, waiting for transfers between devices: 59.4 us -> none  [scatter(): summed = lax.psum_scatter(partial, 'tp', scatter_dimension=0, tiled=True)]
    pallas_call x4, Pallas kernels: 45.4 us -> 67.6 us  [vision_pass(): pl.pallas_call(functools.partial(kernel, len(pieces), steps), grid=(2 * s...]
    ppermute x18 -> x36, starting transfers between devices: 40.8 us -> 62.3 us  [shift(): return lax.ppermute(block, 'tp', pairs)]
    all_gather x3 -> x0, waiting for transfers between devices: 9.37 us -> none  [gather(): return [lax.all_gather(block, 'tp', axis=0, tiled=True)]]
    ppermute x18 -> x36, waiting for transfers between devices: 74.6 us -> 68.4 us  [shift(): return lax.ppermute(block, 'tp', pairs)]
  transfers between devices with their start and end apart: 45 -> 72, of which waited for: 16 -> 15; matrix products, arithmetic and copies ran while one was open for 13% -> 6% of each run, Pallas kernels for 7% -> 35%
where the time goes in v4:
time: 322 us; the launch traced here: 321 us
  Pallas kernels  113 us (35%)
  starting transfers between devices  79 us (25%)
  waiting for transfers between devices  75.1 us (23%)
  local copies, waits for them, and re-layouts  24 us (7%)
  between operations  16.6 us (5%)
  other arithmetic  12.5 us (4%)
    ppermute x36, waiting for transfers between devices, shift(): return lax.ppermute(block, 'tp', pairs)  68.4 us
    pallas_call x4, Pallas kernels, vision_pass(): pl.pallas_call(functools.partial(kernel, len(pieces), steps), grid=(2 * s...  67.6 us
    ppermute x36, starting transfers between devices, shift(): return lax.ppermute(block, 'tp', pairs)  62.3 us
    pallas_call x2, Pallas kernels, project(): pl.pallas_call(functools.partial(project_kernel, len(pieces), tile_of(dep...  45.8 us
    unnamed x141, local copies, waits for them, and re-layouts  8.63 us
  transfers between devices with their start and end apart: 72, of which 15 were waited for; matrix products, arithmetic and copies ran while one was open for 6% of the time, Pallas kernels for 35%

profile of v4, /device:TPU:0, one launch (start us, length us, event | category | flops | bytes accessed | tf_op | source)
XLA Modules:
  0.0 320.6 jit_solution(9827981863464488662)
XLA Ops:
  0.7 3.3 %copy.17 = bf16[1152,1024]{1,0:T(8,128)(2,1)} copy(bf16[1152,1024]{1,0:T(8,128)(2,1)} %param.19) | data formatting | bytes 4718592
  4.7 5.1 %collective-permute-start.2 = (bf16[32,3200]{1,0:T(8,128)(2,1)S(1)}, bf16[32,3200]{1,0:T(8,128)(2,1)S(1)}, u32[]{:S(2)}, u32[]{:S(2)}) collective-permute-start(bf16[32,3200]{1,0:T(8,128)(2,1)S(1)} %get-tuple-element.77.refs_0_), channel_id=1, source_target_pairs={{0,6},{1,7},{2,0},{3,1},{4,2},{5,3},{6,4},{7,5},{8,14},{9,15},{10,... | collective-permute-start | bytes 614408 | tf_op jit(solution)/shard_map/ppermute | solution.py:240
  9.8 1.0 collective-permute-start
  20.5 1.8 dynamic-slice_bitcast_fusion.4
  22.3 2.4 collective-permute-start.29
  24.8 2.5 collective-permute-done.1.refs_2_
  28.8 1.5 collective-permute-start.31
  30.4 2.6 collective-permute-start.8
  33.1 1.9 collective-permute-start.7
  35.1 17.3 %shard_map.113 = (bf16[128,3200]{1,0:T(8,128)(2,1)}, bf16[128,3200]{1,0:T(8,128)(2,1)}, f32[256,1600]{1,0:T(8,128)}) custom-call(bf16[32,3200]{1,0:T(8,128)(2,1)} %copy-done.8, bf16[32,3200]{1,0:T(8,128)(2,1)} %copy-done.18, bf16[32,3200]{1,0:T(8,128)(2,1)} %copy-done.17, bf16[32,3200]{1,0:T(8,128)(2,1)} %copy-done.16, bf16[32,3200]{1,0:T(8,128)(2,1)} %copy-done.41, ...), custom_call_target="tpu_custom_call" | custom-call | flops 5242880000 | bytes 25395200 | tf_op jit(solution)/shard_map/pallas_call | solution.py:172
  52.4 1.6 collective-permute-start.30
  54.8 1.9 collective-permute-done.30
  56.7 0.9 pad_maximum_fusion.1
  61.4 1.8 collective-permute-start.16
  63.3 1.5 collective-permute-start.15
  66.1 17.2 %shard_map.114 = (bf16[128,3200]{1,0:T(8,128)(2,1)}, bf16[128,3200]{1,0:T(8,128)(2,1)}, f32[256,1600]{1,0:T(8,128)}) custom-call(bf16[32,3200]{1,0:T(8,128)(2,1)} %copy-done.6, bf16[32,3200]{1,0:T(8,128)(2,1)} %copy-done.21, bf16[32,3200]{1,0:T(8,128)(2,1)} %copy-done.20, bf16[32,3200]{1,0:T(8,128)(2,1)} %copy-done.19, bf16[32,3200]{1,0:T(8,128)(2,1)} %copy-done.33, ...), custom_call_target="tpu_custom_call" | custom-call | flops 5242880000 | bytes 25395200 | tf_op jit(solution)/shard_map/pallas_call | solution.py:172
  84.8 1.1 collective-permute-start.20
  85.9 0.9 collective-permute-start.19
  86.9 1.9 collective-permute-start.18
  89.7 1.8 collective-permute-start.23
  91.6 0.8 collective-permute-done.20.refs_3_
  92.4 3.3 %collective-permute-start.22 = (bf16[32,3200]{1,0:T(8,128)(2,1)S(1)}, bf16[32,3200]{1,0:T(8,128)(2,1)S(1)}, u32[]{:S(2)}, u32[]{:S(2)}) collective-permute-start(bf16[32,3200]{1,0:T(8,128)(2,1)S(1)} %get-tuple-element.207), channel_id=1, source_target_pairs={{0,6},{1,7},{2,0},{3,1},{4,2},{5,3},{6,4},{7,5},{8,14},{9,15},{10,... | collective-permute-start | bytes 614408 | tf_op jit(solution)/shard_map/ppermute | solution.py:240
  95.7 0.8 select_bitcast_fusion
  96.6 18.2 %collective-permute-done.19.refs_2_ = bf16[8,12800]{1,0:T(8,128)(2,1)S(1)} collective-permute-done((bf16[8,12800]{1,0:T(8,128)(2,1)S(1)}, bf16[8,12800]{1,0:T(8,128)(2,1)S(1)}, u32[]{:S(2)}, u32[]{:S(2)}) %collective-permute-start.19) | collective-permute-done | bytes 204832 | tf_op jit(solution)/shard_map/ppermute | solution.py:240
  114.8 4.4 %collective-permute-done.23 = bf16[32,3200]{1,0:T(8,128)(2,1)S(1)} collective-permute-done((bf16[32,3200]{1,0:T(8,128)(2,1)S(1)}, bf16[32,3200]{1,0:T(8,128)(2,1)S(1)}, u32[]{:S(2)}, u32[]{:S(2)}) %collective-permute-start.23) | collective-permute-done | bytes 204832 | tf_op jit(solution)/shard_map/ppermute | solution.py:240
  121.6 6.9 %collective-permute-start.34 = (bf16[8,12800]{1,0:T(8,128)(2,1)S(1)}, bf16[8,12800]{1,0:T(8,128)(2,1)S(1)}, u32[]{:S(2)}, u32[]{:S(2)}) collective-permute-start(bf16[8,12800]{1,0:T(8,128)(2,1)S(1)} %multiply_convert_fusion.4.refs_0_), channel_id=1, source_target_pairs={{0,6},{1,7},{2,0},{3,1},{4,2},{5,3},{6,4},{7,5},{8,14},{9,15},{10,... | collective-permute-start | bytes 614408 | tf_op jit(solution)/shard_map/ppermute | solution.py:240
  128.5 0.8 collective-permute-start.32
  130.0 22.9 %shard_map.115 = (bf16[64,1024]{1,0:T(8,128)(2,1)}, bf16[32,12800]{1,0:T(8,128)(2,1)}, bf16[32,12800]{1,0:T(8,128)(2,1)}) custom-call(bf16[8,12800]{1,0:T(8,128)(2,1)} %copy-done.10, bf16[8,12800]{1,0:T(8,128)(2,1)} %copy-done.24, bf16[8,12800]{1,0:T(8,128)(2,1)} %copy-done.23, bf16[8,12800]{1,0:T(8,128)(2,1)} %copy-done.22, bf16[8,12800]{1,0:T(8,128)(2,1)} %copy-done.45, ...), custom_call_target="tpu_custom_call" | custom-call | flops 3355443200 | bytes 29753344 | tf_op jit(solution)/shard_map/pallas_call | solution.py:197
  154.2 1.7 collective-permute-done.39
  155.9 1.4 fusion.49
  157.3 2.8 collective-permute-start.42
  160.1 1.2 collective-permute-start.41
  161.3 1.3 collective-permute-start.40
  163.3 22.9 %shard_map.116 = (bf16[64,1024]{1,0:T(8,128)(2,1)}, bf16[32,12800]{1,0:T(8,128)(2,1)}, bf16[32,12800]{1,0:T(8,128)(2,1)}) custom-call(bf16[8,12800]{1,0:T(8,128)(2,1)} %copy-done.11, bf16[8,12800]{1,0:T(8,128)(2,1)} %copy-done.30, bf16[8,12800]{1,0:T(8,128)(2,1)} %copy-done.29, bf16[8,12800]{1,0:T(8,128)(2,1)} %copy-done.28, bf16[8,12800]{1,0:T(8,128)(2,1)} %copy-done.31, ...), custom_call_target="tpu_custom_call" | custom-call | flops 3355443200 | bytes 29753344 | tf_op jit(solution)/shard_map/pallas_call | solution.py:197
  187.1 2.0 collective-permute-start.45
  190.1 2.8 collective-permute-start.49
  192.9 1.2 collective-permute-start.48
  194.0 0.7 collective-permute-done.45.refs_3_
  194.7 4.2 %collective-permute-start.47 = (bf16[8,12800]{1,0:T(8,128)(2,1)S(1)}, bf16[8,12800]{1,0:T(8,128)(2,1)S(1)}, u32[]{:S(2)}, u32[]{:S(2)}) collective-permute-start(bf16[8,12800]{1,0:T(8,128)(2,1)S(1)} %get-tuple-element.201), channel_id=1, source_target_pairs={{0,6},{1,7},{2,0},{3,1},{4,2},{5,3},{6,4},{7,5},{8,14},{9,15},{10,... | collective-permute-start | bytes 614408 | tf_op jit(solution)/shard_map/ppermute | solution.py:240
  198.9 18.3 %collective-permute-done.44.refs_2_ = bf16[32,3200]{1,0:T(8,128)(2,1)S(1)} collective-permute-done((bf16[32,3200]{1,0:T(8,128)(2,1)S(1)}, bf16[32,3200]{1,0:T(8,128)(2,1)S(1)}, u32[]{:S(2)}, u32[]{:S(2)}) %collective-permute-start.44) | collective-permute-done | bytes 204832 | tf_op jit(solution)/shard_map/ppermute | solution.py:240
  217.2 4.3 %collective-permute-done.48 = bf16[8,12800]{1,0:T(8,128)(2,1)S(1)} collective-permute-done((bf16[8,12800]{1,0:T(8,128)(2,1)S(1)}, bf16[8,12800]{1,0:T(8,128)(2,1)S(1)}, u32[]{:S(2)}, u32[]{:S(2)}) %collective-permute-start.48) | collective-permute-done | bytes 204832 | tf_op jit(solution)/shard_map/ppermute | solution.py:240
  221.5 1.7 collective-permute-done.47
  225.1 5.1 %collective-permute-start.56 = (bf16[32,3200]{1,0:T(8,128)(2,1)S(1)}, bf16[32,3200]{1,0:T(8,128)(2,1)S(1)}, u32[]{:S(2)}, u32[]{:S(2)}) collective-permute-start(bf16[32,3200]{1,0:T(8,128)(2,1)S(1)} %multiply_convert_fusion.refs_0_), channel_id=1, source_target_pairs={{0,6},{1,7},{2,0},{3,1},{4,2},{5,3},{6,4},{7,5},{8,14},{9,15},{10,... | collective-permute-start | bytes 614408 | tf_op jit(solution)/shard_map/ppermute | solution.py:240
  230.2 0.9 collective-permute-start.54
  231.9 16.6 %shard_map.117 = (bf16[128,3200]{1,0:T(8,128)(2,1)}, bf16[128,3200]{1,0:T(8,128)(2,1)}) custom-call(bf16[32,3200]{1,0:T(8,128)(2,1)} %copy-done.9, bf16[32,3200]{1,0:T(8,128)(2,1)} %copy-done.27, bf16[32,3200]{1,0:T(8,128)(2,1)} %copy-done.26, bf16[32,3200]{1,0:T(8,128)(2,1)} %copy-done.25, bf16[32,3200]{1,0:T(8,128)(2,1)} %copy-done.46, ...), custom_call_target="tpu_custom_call" | custom-call | flops 5242880000 | bytes 25395200 | tf_op jit(solution)/shard_map/pallas_call | solution.py:172
  257.6 1.5 gather_fusion.3
  259.3 0.7 dynamic-slice_bitcast_fusion
  260.0 1.5 collective-permute-start.65
  262.0 2.4 collective-permute-start.67
  264.4 1.6 dynamic_update_slice.12
  266.0 1.6 dynamic_update_slice.13
  267.6 1.6 dynamic_update_slice.14
  269.1 1.6 dynamic_update_slice.15
  272.0 2.7 collective-permute-start.64
  274.6 1.0 collective-permute-start.63
  275.6 1.6 collective-permute-start.62
  278.0 16.6 %shard_map.118 = (bf16[128,3200]{1,0:T(8,128)(2,1)}, bf16[128,3200]{1,0:T(8,128)(2,1)}) custom-call(bf16[32,3200]{1,0:T(8,128)(2,1)} %copy-done.7, bf16[32,3200]{1,0:T(8,128)(2,1)} %copy-done.15, bf16[32,3200]{1,0:T(8,128)(2,1)} %copy-done.14, bf16[32,3200]{1,0:T(8,128)(2,1)} %copy-done.13, bf16[32,3200]{1,0:T(8,128)(2,1)} %copy-done.32, ...), custom_call_target="tpu_custom_call" | custom-call | flops 5242880000 | bytes 25395200 | tf_op jit(solution)/shard_map/pallas_call | solution.py:172
  294.8 2.5 collective-permute-done.68
  297.3 1.3 convert_add_fusion
  298.7 1.9 collective-permute-start.69
  301.5 8.9 %collective-permute-done.69 = bf16[32,3200]{1,0:T(8,128)(2,1)S(1)} collective-permute-done((bf16[32,3200]{1,0:T(8,128)(2,1)S(1)}, bf16[32,3200]{1,0:T(8,128)(2,1)S(1)}, u32[]{:S(2)}, u32[]{:S(2)}) %collective-permute-start.69) | collective-permute-done | bytes 204832 | tf_op jit(solution)/shard_map/ppermute | solution.py:240
  310.4 0.9 collective-permute-done.71
  311.3 7.6 %collective-permute-done.70 = bf16[32,3200]{1,0:T(8,128)(2,1)S(1)} collective-permute-done((bf16[32,3200]{1,0:T(8,128)(2,1)S(1)}, bf16[32,3200]{1,0:T(8,128)(2,1)S(1)}, u32[]{:S(2)}, u32[]{:S(2)}) %collective-permute-start.70) | collective-permute-done | bytes 204832 | tf_op jit(solution)/shard_map/ppermute | solution.py:240
  319.8 0.8 pad_maximum_fusion
  (330 shorter events, 28.8 us)
Async XLA Ops:
  4.7 20.0 %collective-permute-start.2 = (bf16[32,3200]{1,0:T(8,128)(2,1)S(1)}, bf16[32,3200]{1,0:T(8,128)(2,1)S(1)}, u32[]{:S(2)}, u32[]{:S(2)}) collective-permute-start(bf16[32,3200]{1,0:T(8,128)(2,1)S(1)} %get-tuple-element.77.refs_0_), channel_id=1, source_target_pairs={{0,6},{1,7},{2,0},{3,1},{4,2},{5,3},{6,4},{7,5},{8,14},{9,15},{10,... | collective-permute-start | bytes 614408 | tf_op jit(solution)/shard_map/ppermute | solution.py:240
  9.8 17.4 %collective-permute-start.1 = (bf16[32,3200]{1,0:T(8,128)(2,1)S(1)}, bf16[32,3200]{1,0:T(8,128)(2,1)S(1)}, u32[]{:S(2)}, u32[]{:S(2)}) collective-permute-start(bf16[32,3200]{1,0:T(8,128)(2,1)S(1)} %get-tuple-element.77.refs_0_), channel_id=1, source_target_pairs={{0,4},{1,5},{2,6},{3,7},{4,0},{5,1},{6,2},{7,3},{8,12},{9,13},{10,... | collective-permute-start | bytes 614408 | tf_op jit(solution)/shard_map/ppermute | solution.py:240
  9.8 17.4 %collective-permute-start = (bf16[32,3200]{1,0:T(8,128)(2,1)S(1)}, bf16[32,3200]{1,0:T(8,128)(2,1)S(1)}, u32[]{:S(2)}, u32[]{:S(2)}) collective-permute-start(bf16[32,3200]{1,0:T(8,128)(2,1)S(1)} %get-tuple-element.77.refs_0_), channel_id=1, source_target_pairs={{0,2},{1,3},{2,4},{3,5},{4,6},{5,7},{6,0},{7,1},{8,10},{9,11},{10,... | collective-permute-start | bytes 614408 | tf_op jit(solution)/shard_map/ppermute | solution.py:240
  22.3 32.5 %collective-permute-start.29 = (bf16[32,1024]{1,0:T(8,128)(2,1)}, bf16[32,1024]{1,0:T(8,128)(2,1)S(1)}, u32[]{:S(2)}, u32[]{:S(2)}) collective-permute-start(bf16[32,1024]{1,0:T(8,128)(2,1)} %get-tuple-element.178), channel_id=1, source_target_pairs={{0,24},{8,0},{16,8},{24,16},{1,25},{9,1},{17,9},{25,17},{2,26},{10... | collective-permute-start | bytes 196616 | tf_op jit(solution)/shard_map/ppermute | solution.py:322
  27.9 5.2 %collective-permute-start.6 = (bf16[32,3200]{1,0:T(8,128)(2,1)S(1)}, bf16[32,3200]{1,0:T(8,128)(2,1)S(1)}, u32[]{:S(2)}, u32[]{:S(2)}) collective-permute-start(bf16[32,3200]{1,0:T(8,128)(2,1)S(1)} %collective-permute-done.2.refs_3_), channel_id=1, source_target_pairs={{0,1},{1,0},{2,3},{3,2},{4,5},{5,4},{6,7},{7,6},{8,9},{9,8},{10,11... | collective-permute-start | bytes 614408 | tf_op jit(solution)/shard_map/ppermute | solution.py:246
  28.8 26.1 %collective-permute-start.31 = (bf16[32,1024]{1,0:T(8,128)(2,1)}, bf16[32,1024]{1,0:T(8,128)(2,1)}, u32[]{:S(2)}, u32[]{:S(2)}) collective-permute-start(bf16[32,1024]{1,0:T(8,128)(2,1)} %get-tuple-element.179), channel_id=1, source_target_pairs={{0,8},{8,16},{16,24},{24,0},{1,9},{9,17},{17,25},{25,1},{2,10},{10... | collective-permute-start | bytes 196616 | tf_op jit(solution)/shard_map/ppermute | solution.py:322
  30.2 22.1 %collective-permute-start.9 = (bf16[32,3200]{1,0:T(8,128)(2,1)S(1)}, bf16[32,3200]{1,0:T(8,128)(2,1)S(1)}, u32[]{:S(2)}, u32[]{:S(2)}) collective-permute-start(bf16[32,3200]{1,0:T(8,128)(2,1)S(1)} %get-tuple-element.84.refs_0_), channel_id=1, source_target_pairs={{0,6},{1,7},{2,0},{3,1},{4,2},{5,3},{6,4},{7,5},{8,14},{9,15},{10,... | collective-permute-start | bytes 614408 | tf_op jit(solution)/shard_map/ppermute | solution.py:240
  30.4 23.5 %collective-permute-start.8 = (bf16[32,3200]{1,0:T(8,128)(2,1)S(1)}, bf16[32,3200]{1,0:T(8,128)(2,1)S(1)}, u32[]{:S(2)}, u32[]{:S(2)}) collective-permute-start(bf16[32,3200]{1,0:T(8,128)(2,1)S(1)} %get-tuple-element.84.refs_0_), channel_id=1, source_target_pairs={{0,4},{1,5},{2,6},{3,7},{4,0},{5,1},{6,2},{7,3},{8,12},{9,13},{10,... | collective-permute-start | bytes 614408 | tf_op jit(solution)/shard_map/ppermute | solution.py:240
  33.1 20.9 %collective-permute-start.7 = (bf16[32,3200]{1,0:T(8,128)(2,1)S(1)}, bf16[32,3200]{1,0:T(8,128)(2,1)S(1)}, u32[]{:S(2)}, u32[]{:S(2)}) collective-permute-start(bf16[32,3200]{1,0:T(8,128)(2,1)S(1)} %get-tuple-element.84.refs_0_), channel_id=1, source_target_pairs={{0,2},{1,3},{2,4},{3,5},{4,6},{5,7},{6,0},{7,1},{8,10},{9,11},{10,... | collective-permute-start | bytes 614408 | tf_op jit(solution)/shard_map/ppermute | solution.py:240
  52.4 4.3 %collective-permute-start.30 = (bf16[32,1024]{1,0:T(8,128)(2,1)S(1)}, bf16[32,1024]{1,0:T(8,128)(2,1)S(1)}, u32[]{:S(2)}, u32[]{:S(2)}) collective-permute-start(bf16[32,1024]{1,0:T(8,128)(2,1)S(1)} %get-tuple-element.180), channel_id=1, source_target_pairs={{0,16},{8,24},{16,0},{24,8},{1,17},{9,25},{17,1},{25,9},{2,18},{10... | collective-permute-start | bytes 196616 | tf_op jit(solution)/shard_map/ppermute | solution.py:322
  54.0 6.5 %collective-permute-start.14 = (bf16[128,3200]{1,0:T(8,128)(2,1)}, bf16[128,3200]{1,0:T(8,128)(2,1)S(1)}, u32[]{:S(2)}, u32[]{:S(2)}) collective-permute-start(bf16[128,3200]{1,0:T(8,128)(2,1)} %get-tuple-element.91), channel_id=1, source_target_pairs={{0,1},{1,0},{2,3},{3,2},{4,5},{5,4},{6,7},{7,6},{8,9},{9,8},{10,11... | collective-permute-start | bytes 2457608 | tf_op jit(solution)/shard_map/ppermute | solution.py:253
  60.0 4.8 %collective-permute-start.12 = (bf16[32,3200]{1,0:T(8,128)(2,1)S(1)}, bf16[32,3200]{1,0:T(8,128)(2,1)S(1)}, u32[]{:S(2)}, u32[]{:S(2)}) collective-permute-start(bf16[32,3200]{1,0:T(8,128)(2,1)S(1)} %collective-permute-done.8.refs_2_), channel_id=1, source_target_pairs={{0,1},{1,0},{2,3},{3,2},{4,5},{5,4},{6,7},{7,6},{8,9},{9,8},{10,11... | collective-permute-start | bytes 614408 | tf_op jit(solution)/shard_map/ppermute | solution.py:246
  60.1 4.7 %collective-permute-start.13 = (bf16[32,3200]{1,0:T(8,128)(2,1)S(1)}, bf16[32,3200]{1,0:T(8,128)(2,1)S(1)}, u32[]{:S(2)}, u32[]{:S(2)}) collective-permute-start(bf16[32,3200]{1,0:T(8,128)(2,1)S(1)} %collective-permute-done.9.refs_3_), channel_id=1, source_target_pairs={{0,1},{1,0},{2,3},{3,2},{4,5},{5,4},{6,7},{7,6},{8,9},{9,8},{10,11... | collective-permute-start | bytes 614408 | tf_op jit(solution)/shard_map/ppermute | solution.py:246
  60.8 22.6 %collective-permute-start.17 = (bf16[32,3200]{1,0:T(8,128)(2,1)S(1)}, bf16[32,3200]{1,0:T(8,128)(2,1)S(1)}, u32[]{:S(2)}, u32[]{:S(2)}) collective-permute-start(bf16[32,3200]{1,0:T(8,128)(2,1)S(1)} %get-tuple-element.208), channel_id=1, source_target_pairs={{0,2},{1,3},{2,4},{3,5},{4,6},{5,7},{6,0},{7,1},{8,10},{9,11},{10,... | collective-permute-start | bytes 614408 | tf_op jit(solution)/shard_map/ppermute | solution.py:240
  61.4 21.9 %collective-permute-start.16 = (bf16[32,3200]{1,0:T(8,128)(2,1)S(1)}, bf16[32,3200]{1,0:T(8,128)(2,1)S(1)}, u32[]{:S(2)}, u32[]{:S(2)}) collective-permute-start(bf16[32,3200]{1,0:T(8,128)(2,1)S(1)} %get-tuple-element.209), channel_id=1, source_target_pairs={{0,4},{1,5},{2,6},{3,7},{4,0},{5,1},{6,2},{7,3},{8,12},{9,13},{10,... | collective-permute-start | bytes 614408 | tf_op jit(solution)/shard_map/ppermute | solution.py:240
  63.3 20.1 %collective-permute-start.15 = (bf16[32,3200]{1,0:T(8,128)(2,1)S(1)}, bf16[32,3200]{1,0:T(8,128)(2,1)S(1)}, u32[]{:S(2)}, u32[]{:S(2)}) collective-permute-start(bf16[32,3200]{1,0:T(8,128)(2,1)S(1)} %get-tuple-element.210), channel_id=1, source_target_pairs={{0,6},{1,7},{2,0},{3,1},{4,2},{5,3},{6,4},{7,5},{8,14},{9,15},{10,... | collective-permute-start | bytes 614408 | tf_op jit(solution)/shard_map/ppermute | solution.py:240
  84.6 4.2 %collective-permute-start.21 = (bf16[128,3200]{1,0:T(8,128)(2,1)}, bf16[128,3200]{1,0:T(8,128)(2,1)S(1)}, u32[]{:S(2)}, u32[]{:S(2)}) collective-permute-start(bf16[128,3200]{1,0:T(8,128)(2,1)} %get-tuple-element.97), channel_id=1, source_target_pairs={{0,1},{1,0},{2,3},{3,2},{4,5},{5,4},{6,7},{7,6},{8,9},{9,8},{10,11... | collective-permute-start | bytes 2457608 | tf_op jit(solution)/shard_map/ppermute | solution.py:253
  84.8 7.6 %collective-permute-start.20 = (bf16[8,12800]{1,0:T(8,128)(2,1)S(1)}, bf16[8,12800]{1,0:T(8,128)(2,1)S(1)}, u32[]{:S(2)}, u32[]{:S(2)}) collective-permute-start(bf16[8,12800]{1,0:T(8,128)(2,1)S(1)} %multiply_convert_fusion.5.refs_0_), channel_id=1, source_target_pairs={{0,6},{1,7},{2,0},{3,1},{4,2},{5,3},{6,4},{7,5},{8,14},{9,15},{10,... | collective-permute-start | bytes 614408 | tf_op jit(solution)/shard_map/ppermute | solution.py:240
  85.9 28.9 %collective-permute-start.19 = (bf16[8,12800]{1,0:T(8,128)(2,1)S(1)}, bf16[8,12800]{1,0:T(8,128)(2,1)S(1)}, u32[]{:S(2)}, u32[]{:S(2)}) collective-permute-start(bf16[8,12800]{1,0:T(8,128)(2,1)S(1)} %multiply_convert_fusion.5.refs_0_), channel_id=1, source_target_pairs={{0,4},{1,5},{2,6},{3,7},{4,0},{5,1},{6,2},{7,3},{8,12},{9,13},{10,... | collective-permute-start | bytes 614408 | tf_op jit(solution)/shard_map/ppermute | solution.py:240
  86.9 27.9 %collective-permute-start.18 = (bf16[8,12800]{1,0:T(8,128)(2,1)S(1)}, bf16[8,12800]{1,0:T(8,128)(2,1)S(1)}, u32[]{:S(2)}, u32[]{:S(2)}) collective-permute-start(bf16[8,12800]{1,0:T(8,128)(2,1)S(1)} %multiply_convert_fusion.5.refs_0_), channel_id=1, source_target_pairs={{0,2},{1,3},{2,4},{3,5},{4,6},{5,7},{6,0},{7,1},{8,10},{9,11},{10,... | collective-permute-start | bytes 614408 | tf_op jit(solution)/shard_map/ppermute | solution.py:240
  89.1 25.7 %collective-permute-start.24 = (bf16[32,3200]{1,0:T(8,128)(2,1)S(1)}, bf16[32,3200]{1,0:T(8,128)(2,1)S(1)}, u32[]{:S(2)}, u32[]{:S(2)}) collective-permute-start(bf16[32,3200]{1,0:T(8,128)(2,1)S(1)} %get-tuple-element.205), channel_id=1, source_target_pairs={{0,2},{1,3},{2,4},{3,5},{4,6},{5,7},{6,0},{7,1},{8,10},{9,11},{10,... | collective-permute-start | bytes 614408 | tf_op jit(solution)/shard_map/ppermute | solution.py:240
  89.7 29.5 %collective-permute-start.23 = (bf16[32,3200]{1,0:T(8,128)(2,1)S(1)}, bf16[32,3200]{1,0:T(8,128)(2,1)S(1)}, u32[]{:S(2)}, u32[]{:S(2)}) collective-permute-start(bf16[32,3200]{1,0:T(8,128)(2,1)S(1)} %get-tuple-element.206), channel_id=1, source_target_pairs={{0,4},{1,5},{2,6},{3,7},{4,0},{5,1},{6,2},{7,3},{8,12},{9,13},{10,... | collective-permute-start | bytes 614408 | tf_op jit(solution)/shard_map/ppermute | solution.py:240
  92.4 26.8 %collective-permute-start.22 = (bf16[32,3200]{1,0:T(8,128)(2,1)S(1)}, bf16[32,3200]{1,0:T(8,128)(2,1)S(1)}, u32[]{:S(2)}, u32[]{:S(2)}) collective-permute-start(bf16[32,3200]{1,0:T(8,128)(2,1)S(1)} %get-tuple-element.207), channel_id=1, source_target_pairs={{0,6},{1,7},{2,0},{3,1},{4,2},{5,3},{6,4},{7,5},{8,14},{9,15},{10,... | collective-permute-start | bytes 614408 | tf_op jit(solution)/shard_map/ppermute | solution.py:240
  120.3 8.1 %collective-permute-start.25 = (bf16[8,12800]{1,0:T(8,128)(2,1)S(1)}, bf16[8,12800]{1,0:T(8,128)(2,1)S(1)}, u32[]{:S(2)}, u32[]{:S(2)}) collective-permute-start(bf16[8,12800]{1,0:T(8,128)(2,1)S(1)} %multiply_convert_fusion.5.refs_0_), channel_id=1, source_target_pairs={{0,1},{1,0},{2,3},{3,2},{4,5},{5,4},{6,7},{7,6},{8,9},{9,8},{10,11... | collective-permute-start | bytes 614408 | tf_op jit(solution)/shard_map/ppermute | solution.py:246
  120.4 8.1 %collective-permute-start.26 = (bf16[8,12800]{1,0:T(8,128)(2,1)S(1)}, bf16[8,12800]{1,0:T(8,128)(2,1)S(1)}, u32[]{:S(2)}, u32[]{:S(2)}) collective-permute-start(bf16[8,12800]{1,0:T(8,128)(2,1)S(1)} %collective-permute-done.18.refs_1_), channel_id=1, source_target_pairs={{0,1},{1,0},{2,3},{3,2},{4,5},{5,4},{6,7},{7,6},{8,9},{9,8},{10,11... | collective-permute-start | bytes 614408 | tf_op jit(solution)/shard_map/ppermute | solution.py:246
  120.9 8.3 %collective-permute-start.27 = (bf16[8,12800]{1,0:T(8,128)(2,1)S(1)}, bf16[8,12800]{1,0:T(8,128)(2,1)S(1)}, u32[]{:S(2)}, u32[]{:S(2)}) collective-permute-start(bf16[8,12800]{1,0:T(8,128)(2,1)S(1)} %collective-permute-done.19.refs_2_), channel_id=1, source_target_pairs={{0,1},{1,0},{2,3},{3,2},{4,5},{5,4},{6,7},{7,6},{8,9},{9,8},{10,11... | collective-permute-start | bytes 614408 | tf_op jit(solution)/shard_map/ppermute | solution.py:246
  121.0 8.3 %collective-permute-start.28 = (bf16[8,12800]{1,0:T(8,128)(2,1)S(1)}, bf16[8,12800]{1,0:T(8,128)(2,1)S(1)}, u32[]{:S(2)}, u32[]{:S(2)}) collective-permute-start(bf16[8,12800]{1,0:T(8,128)(2,1)S(1)} %collective-permute-done.20.refs_3_), channel_id=1, source_target_pairs={{0,1},{1,0},{2,3},{3,2},{4,5},{5,4},{6,7},{7,6},{8,9},{9,8},{10,11... | collective-permute-start | bytes 614408 | tf_op jit(solution)/shard_map/ppermute | solution.py:246
  121.6 31.4 %collective-permute-start.34 = (bf16[8,12800]{1,0:T(8,128)(2,1)S(1)}, bf16[8,12800]{1,0:T(8,128)(2,1)S(1)}, u32[]{:S(2)}, u32[]{:S(2)}) collective-permute-start(bf16[8,12800]{1,0:T(8,128)(2,1)S(1)} %multiply_convert_fusion.4.refs_0_), channel_id=1, source_target_pairs={{0,6},{1,7},{2,0},{3,1},{4,2},{5,3},{6,4},{7,5},{8,14},{9,15},{10,... | collective-permute-start | bytes 614408 | tf_op jit(solution)/shard_map/ppermute | solution.py:240
  128.4 24.5 %collective-permute-start.33 = (bf16[8,12800]{1,0:T(8,128)(2,1)S(1)}, bf16[8,12800]{1,0:T(8,128)(2,1)S(1)}, u32[]{:S(2)}, u32[]{:S(2)}) collective-permute-start(bf16[8,12800]{1,0:T(8,128)(2,1)S(1)} %multiply_convert_fusion.4.refs_0_), channel_id=1, source_target_pairs={{0,4},{1,5},{2,6},{3,7},{4,0},{5,1},{6,2},{7,3},{8,12},{9,13},{10,... | collective-permute-start | bytes 614408 | tf_op jit(solution)/shard_map/ppermute | solution.py:240
  128.5 24.5 %collective-permute-start.32 = (bf16[8,12800]{1,0:T(8,128)(2,1)S(1)}, bf16[8,12800]{1,0:T(8,128)(2,1)S(1)}, u32[]{:S(2)}, u32[]{:S(2)}) collective-permute-start(bf16[8,12800]{1,0:T(8,128)(2,1)S(1)} %multiply_convert_fusion.4.refs_0_), channel_id=1, source_target_pairs={{0,2},{1,3},{2,4},{3,5},{4,6},{5,7},{6,0},{7,1},{8,10},{9,11},{10,... | collective-permute-start | bytes 614408 | tf_op jit(solution)/shard_map/ppermute | solution.py:240
  153.1 7.0 %collective-permute-start.35 = (bf16[8,12800]{1,0:T(8,128)(2,1)S(1)}, bf16[8,12800]{1,0:T(8,128)(2,1)S(1)}, u32[]{:S(2)}, u32[]{:S(2)}) collective-permute-start(bf16[8,12800]{1,0:T(8,128)(2,1)S(1)} %multiply_convert_fusion.4.refs_0_), channel_id=1, source_target_pairs={{0,1},{1,0},{2,3},{3,2},{4,5},{5,4},{6,7},{7,6},{8,9},{9,8},{10,11... | collective-permute-start | bytes 614408 | tf_op jit(solution)/shard_map/ppermute | solution.py:246
  153.6 7.7 %collective-permute-start.36 = (bf16[8,12800]{1,0:T(8,128)(2,1)S(1)}, bf16[8,12800]{1,0:T(8,128)(2,1)S(1)}, u32[]{:S(2)}, u32[]{:S(2)}) collective-permute-start(bf16[8,12800]{1,0:T(8,128)(2,1)S(1)} %collective-permute-done.32.refs_1_), channel_id=1, source_target_pairs={{0,1},{1,0},{2,3},{3,2},{4,5},{5,4},{6,7},{7,6},{8,9},{9,8},{10,11... | collective-permute-start | bytes 614408 | tf_op jit(solution)/shard_map/ppermute | solution.py:246
  153.7 8.9 %collective-permute-start.37 = (bf16[8,12800]{1,0:T(8,128)(2,1)S(1)}, bf16[8,12800]{1,0:T(8,128)(2,1)S(1)}, u32[]{:S(2)}, u32[]{:S(2)}) collective-permute-start(bf16[8,12800]{1,0:T(8,128)(2,1)S(1)} %collective-permute-done.33.refs_2_), channel_id=1, source_target_pairs={{0,1},{1,0},{2,3},{3,2},{4,5},{5,4},{6,7},{7,6},{8,9},{9,8},{10,11... | collective-permute-start | bytes 614408 | tf_op jit(solution)/shard_map/ppermute | solution.py:246
  154.1 8.5 %collective-permute-start.38 = (bf16[8,12800]{1,0:T(8,128)(2,1)S(1)}, bf16[8,12800]{1,0:T(8,128)(2,1)S(1)}, u32[]{:S(2)}, u32[]{:S(2)}) collective-permute-start(bf16[8,12800]{1,0:T(8,128)(2,1)S(1)} %collective-permute-done.34.refs_3_), channel_id=1, source_target_pairs={{0,1},{1,0},{2,3},{3,2},{4,5},{5,4},{6,7},{7,6},{8,9},{9,8},{10,11... | collective-permute-start | bytes 614408 | tf_op jit(solution)/shard_map/ppermute | solution.py:246
  157.3 28.9 %collective-permute-start.42 = (bf16[8,12800]{1,0:T(8,128)(2,1)S(1)}, bf16[8,12800]{1,0:T(8,128)(2,1)S(1)}, u32[]{:S(2)}, u32[]{:S(2)}) collective-permute-start(bf16[8,12800]{1,0:T(8,128)(2,1)S(1)} %get-tuple-element.202), channel_id=1, source_target_pairs={{0,2},{1,3},{2,4},{3,5},{4,6},{5,7},{6,0},{7,1},{8,10},{9,11},{10,... | collective-permute-start | bytes 614408 | tf_op jit(solution)/shard_map/ppermute | solution.py:240
  160.1 26.1 %collective-permute-start.41 = (bf16[8,12800]{1,0:T(8,128)(2,1)S(1)}, bf16[8,12800]{1,0:T(8,128)(2,1)S(1)}, u32[]{:S(2)}, u32[]{:S(2)}) collective-permute-start(bf16[8,12800]{1,0:T(8,128)(2,1)S(1)} %get-tuple-element.203), channel_id=1, source_target_pairs={{0,4},{1,5},{2,6},{3,7},{4,0},{5,1},{6,2},{7,3},{8,12},{9,13},{10,... | collective-permute-start | bytes 614408 | tf_op jit(solution)/shard_map/ppermute | solution.py:240
  161.3 25.0 %collective-permute-start.40 = (bf16[8,12800]{1,0:T(8,128)(2,1)S(1)}, bf16[8,12800]{1,0:T(8,128)(2,1)S(1)}, u32[]{:S(2)}, u32[]{:S(2)}) collective-permute-start(bf16[8,12800]{1,0:T(8,128)(2,1)S(1)} %get-tuple-element.204), channel_id=1, source_target_pairs={{0,6},{1,7},{2,0},{3,1},{4,2},{5,3},{6,4},{7,5},{8,14},{9,15},{10,... | collective-permute-start | bytes 614408 | tf_op jit(solution)/shard_map/ppermute | solution.py:240
  187.1 7.6 %collective-permute-start.45 = (bf16[32,3200]{1,0:T(8,128)(2,1)S(1)}, bf16[32,3200]{1,0:T(8,128)(2,1)S(1)}, u32[]{:S(2)}, u32[]{:S(2)}) collective-permute-start(bf16[32,3200]{1,0:T(8,128)(2,1)S(1)} %multiply_convert_fusion.2.refs_0_), channel_id=1, source_target_pairs={{0,6},{1,7},{2,0},{3,1},{4,2},{5,3},{6,4},{7,5},{8,14},{9,15},{10,... | collective-permute-start | bytes 614408 | tf_op jit(solution)/shard_map/ppermute | solution.py:240
  189.0 28.1 %collective-permute-start.44 = (bf16[32,3200]{1,0:T(8,128)(2,1)S(1)}, bf16[32,3200]{1,0:T(8,128)(2,1)S(1)}, u32[]{:S(2)}, u32[]{:S(2)}) collective-permute-start(bf16[32,3200]{1,0:T(8,128)(2,1)S(1)} %multiply_convert_fusion.2.refs_0_), channel_id=1, source_target_pairs={{0,4},{1,5},{2,6},{3,7},{4,0},{5,1},{6,2},{7,3},{8,12},{9,13},{10,... | collective-permute-start | bytes 614408 | tf_op jit(solution)/shard_map/ppermute | solution.py:240
  189.3 27.9 %collective-permute-start.43 = (bf16[32,3200]{1,0:T(8,128)(2,1)S(1)}, bf16[32,3200]{1,0:T(8,128)(2,1)S(1)}, u32[]{:S(2)}, u32[]{:S(2)}) collective-permute-start(bf16[32,3200]{1,0:T(8,128)(2,1)S(1)} %multiply_convert_fusion.2.refs_0_), channel_id=1, source_target_pairs={{0,2},{1,3},{2,4},{3,5},{4,6},{5,7},{6,0},{7,1},{8,10},{9,11},{10,... | collective-permute-start | bytes 614408 | tf_op jit(solution)/shard_map/ppermute | solution.py:240
  190.1 27.1 %collective-permute-start.49 = (bf16[8,12800]{1,0:T(8,128)(2,1)S(1)}, bf16[8,12800]{1,0:T(8,128)(2,1)S(1)}, u32[]{:S(2)}, u32[]{:S(2)}) collective-permute-start(bf16[8,12800]{1,0:T(8,128)(2,1)S(1)} %get-tuple-element.199), channel_id=1, source_target_pairs={{0,2},{1,3},{2,4},{3,5},{4,6},{5,7},{6,0},{7,1},{8,10},{9,11},{10,... | collective-permute-start | bytes 614408 | tf_op jit(solution)/shard_map/ppermute | solution.py:240
  192.9 28.7 %collective-permute-start.48 = (bf16[8,12800]{1,0:T(8,128)(2,1)S(1)}, bf16[8,12800]{1,0:T(8,128)(2,1)S(1)}, u32[]{:S(2)}, u32[]{:S(2)}) collective-permute-start(bf16[8,12800]{1,0:T(8,128)(2,1)S(1)} %get-tuple-element.200), channel_id=1, source_target_pairs={{0,4},{1,5},{2,6},{3,7},{4,0},{5,1},{6,2},{7,3},{8,12},{9,13},{10,... | collective-permute-start | bytes 614408 | tf_op jit(solution)/shard_map/ppermute | solution.py:240
  194.7 28.6 %collective-permute-start.47 = (bf16[8,12800]{1,0:T(8,128)(2,1)S(1)}, bf16[8,12800]{1,0:T(8,128)(2,1)S(1)}, u32[]{:S(2)}, u32[]{:S(2)}) collective-permute-start(bf16[8,12800]{1,0:T(8,128)(2,1)S(1)} %get-tuple-element.201), channel_id=1, source_target_pairs={{0,6},{1,7},{2,0},{3,1},{4,2},{5,3},{6,4},{7,5},{8,14},{9,15},{10,... | collective-permute-start | bytes 614408 | tf_op jit(solution)/shard_map/ppermute | solution.py:240
  223.9 6.2 %collective-permute-start.50 = (bf16[32,3200]{1,0:T(8,128)(2,1)S(1)}, bf16[32,3200]{1,0:T(8,128)(2,1)S(1)}, u32[]{:S(2)}, u32[]{:S(2)}) collective-permute-start(bf16[32,3200]{1,0:T(8,128)(2,1)S(1)} %multiply_convert_fusion.2.refs_0_), channel_id=1, source_target_pairs={{0,1},{1,0},{2,3},{3,2},{4,5},{5,4},{6,7},{7,6},{8,9},{9,8},{10,11... | collective-permute-start | bytes 614408 | tf_op jit(solution)/shard_map/ppermute | solution.py:246
  224.0 6.2 %collective-permute-start.51 = (bf16[32,3200]{1,0:T(8,128)(2,1)S(1)}, bf16[32,3200]{1,0:T(8,128)(2,1)S(1)}, u32[]{:S(2)}, u32[]{:S(2)}) collective-permute-start(bf16[32,3200]{1,0:T(8,128)(2,1)S(1)} %collective-permute-done.43.refs_1_), channel_id=1, source_target_pairs={{0,1},{1,0},{2,3},{3,2},{4,5},{5,4},{6,7},{7,6},{8,9},{9,8},{10,11... | collective-permute-start | bytes 614408 | tf_op jit(solution)/shard_map/ppermute | solution.py:246
  224.5 6.6 %collective-permute-start.52 = (bf16[32,3200]{1,0:T(8,128)(2,1)S(1)}, bf16[32,3200]{1,0:T(8,128)(2,1)S(1)}, u32[]{:S(2)}, u32[]{:S(2)}) collective-permute-start(bf16[32,3200]{1,0:T(8,128)(2,1)S(1)} %collective-permute-done.44.refs_2_), channel_id=1, source_target_pairs={{0,1},{1,0},{2,3},{3,2},{4,5},{5,4},{6,7},{7,6},{8,9},{9,8},{10,11... | collective-permute-start | bytes 614408 | tf_op jit(solution)/shard_map/ppermute | solution.py:246
  224.6 6.5 %collective-permute-start.53 = (bf16[32,3200]{1,0:T(8,128)(2,1)S(1)}, bf16[32,3200]{1,0:T(8,128)(2,1)S(1)}, u32[]{:S(2)}, u32[]{:S(2)}) collective-permute-start(bf16[32,3200]{1,0:T(8,128)(2,1)S(1)} %collective-permute-done.45.refs_3_), channel_id=1, source_target_pairs={{0,1},{1,0},{2,3},{3,2},{4,5},{5,4},{6,7},{7,6},{8,9},{9,8},{10,11... | collective-permute-start | bytes 614408 | tf_op jit(solution)/shard_map/ppermute | solution.py:246
  225.1 23.4 %collective-permute-start.56 = (bf16[32,3200]{1,0:T(8,128)(2,1)S(1)}, bf16[32,3200]{1,0:T(8,128)(2,1)S(1)}, u32[]{:S(2)}, u32[]{:S(2)}) collective-permute-start(bf16[32,3200]{1,0:T(8,128)(2,1)S(1)} %multiply_convert_fusion.refs_0_), channel_id=1, source_target_pairs={{0,6},{1,7},{2,0},{3,1},{4,2},{5,3},{6,4},{7,5},{8,14},{9,15},{10,... | collective-permute-start | bytes 614408 | tf_op jit(solution)/shard_map/ppermute | solution.py:240
  230.2 18.4 %collective-permute-start.55 = (bf16[32,3200]{1,0:T(8,128)(2,1)S(1)}, bf16[32,3200]{1,0:T(8,128)(2,1)S(1)}, u32[]{:S(2)}, u32[]{:S(2)}) collective-permute-start(bf16[32,3200]{1,0:T(8,128)(2,1)S(1)} %multiply_convert_fusion.refs_0_), channel_id=1, source_target_pairs={{0,4},{1,5},{2,6},{3,7},{4,0},{5,1},{6,2},{7,3},{8,12},{9,13},{10,... | collective-permute-start | bytes 614408 | tf_op jit(solution)/shard_map/ppermute | solution.py:240
  230.2 18.4 %collective-permute-start.54 = (bf16[32,3200]{1,0:T(8,128)(2,1)S(1)}, bf16[32,3200]{1,0:T(8,128)(2,1)S(1)}, u32[]{:S(2)}, u32[]{:S(2)}) collective-permute-start(bf16[32,3200]{1,0:T(8,128)(2,1)S(1)} %multiply_convert_fusion.refs_0_), channel_id=1, source_target_pairs={{0,2},{1,3},{2,4},{3,5},{4,6},{5,7},{6,0},{7,1},{8,10},{9,11},{10,... | collective-permute-start | bytes 614408 | tf_op jit(solution)/shard_map/ppermute | solution.py:240
  249.3 22.5 %collective-permute-start.61 = (bf16[128,3200]{1,0:T(8,128)(2,1)}, bf16[128,3200]{1,0:T(8,128)(2,1)S(1)}, u32[]{:S(2)}, u32[]{:S(2)}) collective-permute-start(bf16[128,3200]{1,0:T(8,128)(2,1)} %get-tuple-element.141), channel_id=1, source_target_pairs={{0,1},{1,0},{2,3},{3,2},{4,5},{5,4},{6,7},{7,6},{8,9},{9,8},{10,11... | collective-permute-start | bytes 2457608 | tf_op jit(solution)/shard_map/ppermute | solution.py:253
  260.0 6.0 %collective-permute-start.65 = (bf16[32,1024]{1,0:T(8,128)(2,1)}, bf16[32,1024]{1,0:T(8,128)(2,1)S(1)}, u32[]{:S(2)}, u32[]{:S(2)}) collective-permute-start(bf16[32,1024]{1,0:T(8,128)(2,1)} %get-tuple-element.217), channel_id=1, source_target_pairs={{0,8},{8,16},{16,24},{24,0},{1,9},{9,17},{17,25},{25,1},{2,10},{10... | collective-permute-start | bytes 196616 | tf_op jit(solution)/shard_map/ppermute | solution.py:369
  261.5 6.1 %collective-permute-start.66 = (bf16[32,1024]{1,0:T(8,128)(2,1)}, bf16[32,1024]{1,0:T(8,128)(2,1)S(1)}, u32[]{:S(2)}, u32[]{:S(2)}) collective-permute-start(bf16[32,1024]{1,0:T(8,128)(2,1)} %get-tuple-element.216), channel_id=1, source_target_pairs={{0,16},{8,24},{16,0},{24,8},{1,17},{9,25},{17,1},{25,9},{2,18},{10... | collective-permute-start | bytes 196616 | tf_op jit(solution)/shard_map/ppermute | solution.py:369
  262.0 7.2 %collective-permute-start.67 = (bf16[32,1024]{1,0:T(8,128)(2,1)}, bf16[32,1024]{1,0:T(8,128)(2,1)S(1)}, u32[]{:S(2)}, u32[]{:S(2)}) collective-permute-start(bf16[32,1024]{1,0:T(8,128)(2,1)} %get-tuple-element.215), channel_id=1, source_target_pairs={{0,24},{8,0},{16,8},{24,16},{1,25},{9,1},{17,9},{25,17},{2,26},{10... | collective-permute-start | bytes 196616 | tf_op jit(solution)/shard_map/ppermute | solution.py:369
  270.7 3.9 %collective-permute-start.57 = (bf16[32,3200]{1,0:T(8,128)(2,1)S(1)}, bf16[32,3200]{1,0:T(8,128)(2,1)S(1)}, u32[]{:S(2)}, u32[]{:S(2)}) collective-permute-start(bf16[32,3200]{1,0:T(8,128)(2,1)S(1)} %multiply_convert_fusion.refs_0_), channel_id=1, source_target_pairs={{0,1},{1,0},{2,3},{3,2},{4,5},{5,4},{6,7},{7,6},{8,9},{9,8},{10,11... | collective-permute-start | bytes 614408 | tf_op jit(solution)/shard_map/ppermute | solution.py:246
  270.7 4.9 %collective-permute-start.58 = (bf16[32,3200]{1,0:T(8,128)(2,1)}, bf16[32,3200]{1,0:T(8,128)(2,1)S(1)}, u32[]{:S(2)}, u32[]{:S(2)}) collective-permute-start(bf16[32,3200]{1,0:T(8,128)(2,1)} %copy-done.15), channel_id=1, source_target_pairs={{0,1},{1,0},{2,3},{3,2},{4,5},{5,4},{6,7},{7,6},{8,9},{9,8},{10,11... | collective-permute-start | bytes 614408 | tf_op jit(solution)/shard_map/ppermute | solution.py:246
  271.2 6.0 %collective-permute-start.59 = (bf16[32,3200]{1,0:T(8,128)(2,1)}, bf16[32,3200]{1,0:T(8,128)(2,1)S(1)}, u32[]{:S(2)}, u32[]{:S(2)}) collective-permute-start(bf16[32,3200]{1,0:T(8,128)(2,1)} %copy-done.14), channel_id=1, source_target_pairs={{0,1},{1,0},{2,3},{3,2},{4,5},{5,4},{6,7},{7,6},{8,9},{9,8},{10,11... | collective-permute-start | bytes 614408 | tf_op jit(solution)/shard_map/ppermute | solution.py:246
  271.3 5.9 %collective-permute-start.60 = (bf16[32,3200]{1,0:T(8,128)(2,1)S(1)}, bf16[32,3200]{1,0:T(8,128)(2,1)S(1)}, u32[]{:S(2)}, u32[]{:S(2)}) collective-permute-start(bf16[32,3200]{1,0:T(8,128)(2,1)S(1)} %collective-permute-done.56.refs_3_), channel_id=1, source_target_pairs={{0,1},{1,0},{2,3},{3,2},{4,5},{5,4},{6,7},{7,6},{8,9},{9,8},{10,11... | collective-permute-start | bytes 614408 | tf_op jit(solution)/shard_map/ppermute | solution.py:246
  272.0 22.6 %collective-permute-start.64 = (bf16[32,3200]{1,0:T(8,128)(2,1)S(1)}, bf16[32,3200]{1,0:T(8,128)(2,1)S(1)}, u32[]{:S(2)}, u32[]{:S(2)}) collective-permute-start(bf16[32,3200]{1,0:T(8,128)(2,1)S(1)} %get-tuple-element.196), channel_id=1, source_target_pairs={{0,2},{1,3},{2,4},{3,5},{4,6},{5,7},{6,0},{7,1},{8,10},{9,11},{10,... | collective-permute-start | bytes 614408 | tf_op jit(solution)/shard_map/ppermute | solution.py:240
  274.6 20.0 %collective-permute-start.63 = (bf16[32,3200]{1,0:T(8,128)(2,1)S(1)}, bf16[32,3200]{1,0:T(8,128)(2,1)S(1)}, u32[]{:S(2)}, u32[]{:S(2)}) collective-permute-start(bf16[32,3200]{1,0:T(8,128)(2,1)S(1)} %get-tuple-element.197), channel_id=1, source_target_pairs={{0,4},{1,5},{2,6},{3,7},{4,0},{5,1},{6,2},{7,3},{8,12},{9,13},{10,... | collective-permute-start | bytes 614408 | tf_op jit(solution)/shard_map/ppermute | solution.py:240
  275.6 19.0 %collective-permute-start.62 = (bf16[32,3200]{1,0:T(8,128)(2,1)S(1)}, bf16[32,3200]{1,0:T(8,128)(2,1)S(1)}, u32[]{:S(2)}, u32[]{:S(2)}) collective-permute-start(bf16[32,3200]{1,0:T(8,128)(2,1)S(1)} %get-tuple-element.198), channel_id=1, source_target_pairs={{0,6},{1,7},{2,0},{3,1},{4,2},{5,3},{6,4},{7,5},{8,14},{9,15},{10,... | collective-permute-start | bytes 614408 | tf_op jit(solution)/shard_map/ppermute | solution.py:240
  298.7 11.7 %collective-permute-start.69 = (bf16[32,3200]{1,0:T(8,128)(2,1)S(1)}, bf16[32,3200]{1,0:T(8,128)(2,1)S(1)}, u32[]{:S(2)}, u32[]{:S(2)}) collective-permute-start(bf16[32,3200]{1,0:T(8,128)(2,1)S(1)} %get-tuple-element.193), channel_id=1, source_target_pairs={{0,6},{1,7},{2,0},{3,1},{4,2},{5,3},{6,4},{7,5},{8,14},{9,15},{10,... | collective-permute-start | bytes 614408 | tf_op jit(solution)/shard_map/ppermute | solution.py:240
  300.6 10.7 %collective-permute-start.71 = (bf16[32,3200]{1,0:T(8,128)(2,1)S(1)}, bf16[32,3200]{1,0:T(8,128)(2,1)S(1)}, u32[]{:S(2)}, u32[]{:S(2)}) collective-permute-start(bf16[32,3200]{1,0:T(8,128)(2,1)S(1)} %get-tuple-element.194), channel_id=1, source_target_pairs={{0,2},{1,3},{2,4},{3,5},{4,6},{5,7},{6,0},{7,1},{8,10},{9,11},{10,... | collective-permute-start | bytes 614408 | tf_op jit(solution)/shard_map/ppermute | solution.py:240
  300.8 18.1 %collective-permute-start.70 = (bf16[32,3200]{1,0:T(8,128)(2,1)S(1)}, bf16[32,3200]{1,0:T(8,128)(2,1)S(1)}, u32[]{:S(2)}, u32[]{:S(2)}) collective-permute-start(bf16[32,3200]{1,0:T(8,128)(2,1)S(1)} %get-tuple-element.195), channel_id=1, source_target_pairs={{0,4},{1,5},{2,6},{3,7},{4,0},{5,1},{6,2},{7,3},{8,12},{9,13},{10,... | collective-permute-start | bytes 614408 | tf_op jit(solution)/shard_map/ppermute | solution.py:240
  (78 other events, 786.8 us)

commit v5 on v4

--- a/solution.py
+++ b/solution.py
@@ -59,127 +59,131 @@
     lax.fori_loop(0, total // step, run, 0)
 
 
-def forward_kernel(count, steps, *refs):
+def fetch(source, held, sems):
+    count, rows = held.shape[:2]
+    for j in range(count):
+        pltpu.make_async_copy(source.at[pl.ds(j * rows, rows)], held.at[j], sems.at[j]).start()
+
+
+def arrive(source, held, sems, j):
+    rows = held.shape[1]
+    pltpu.make_async_copy(source.at[pl.ds(0, rows)], held.at[j], sems.at[j]).wait()
+
+
+def vision_kernel(count, ahead, *refs):
     pieces = refs[:count]
-    first, second, near, far, slope, pre, hidden = refs[count:]
-    i = pl.program_id(0)
-
-    @pl.when(i == 0)
-    def _():
-        pre[...] = times_transposed(laid(pieces), first[...])
-
-    @pl.when(jnp.logical_and(i > 0, i < steps))
-    def _():
-        pre[...] += times_transposed(laid(pieces), first[...])
-
-    @pl.when(i == steps - 1)
-    def _():
+    if ahead:
+        early, late, near, far, slope = refs[count : count + 5]
+    else:
+        early, late, slope, near, far = refs[count : count + 5]
+    first, second, rows, total, pre, hidden, first_sems, second_sems = refs[count + 5 :]
+    fetch(early, first, first_sems)
+    fetch(late, second, second_sems)
+    rows[...] = laid(pieces)
+    total[...] = jnp.zeros_like(total)
+    tile = tile_of(rows.shape[1], 640)
+
+    def block(j, _):
+        arrive(early, first, first_sems, j)
+        pre[...] = times_transposed(rows[...], first[j])
+
         def act(sel):
             u = pre[sel, :]
-            cumul = 0.5 * (1.0 + lax.erf(u * 0.7071067811865476))
-            dense = jnp.exp(-0.5 * u * u) * 0.3989422804014327
-            hidden[sel, :] = (u * cumul).astype(jnp.bfloat16)
-            slope[sel, :] = cumul + u * dense
+            if ahead:
+                cumul = 0.5 * (1.0 + lax.erf(u * 0.7071067811865476))
+                dense = jnp.exp(-0.5 * u * u) * 0.3989422804014327
+                hidden[sel, :] = (u * cumul).astype(jnp.bfloat16)
+                slope[j, sel, :] = cumul + u * dense
+            else:
+                hidden[sel, :] = (u * slope[j, sel, :]).astype(jnp.bfloat16)
 
         each_rows(pre.shape[0], act)
-
-    @pl.when(i >= steps)
-    def _():
-        both = jnp.dot(hidden[...], second[...], preferred_element_type=jnp.float32)
-        near[...] = both[: near.shape[0]].astype(jnp.bfloat16)
-        far[...] = both[near.shape[0] :].astype(jnp.bfloat16)
-
-
-def backward_kernel(count, steps, *refs):
+        arrive(late, second, second_sems, j)
+
+        def columns(k, _):
+            sel = pl.ds(pl.multiple_of(k * tile, 128), tile)
+            total[:, sel] += jnp.dot(
+                hidden[...], second[j, :, sel], preferred_element_type=jnp.float32
+            )
+            return 0
+
+        lax.fori_loop(0, rows.shape[1] // tile, columns, 0)
+        return 0
+
+    lax.fori_loop(0, first.shape[0], block, 0)
+    half = near.shape[0]
+    near[...] = total[:half].astype(jnp.bfloat16)
+    far[...] = total[half:].astype(jnp.bfloat16)
+
+
+def project_kernel(count, *refs):
     pieces = refs[:count]
-    second, first, slope, near, far, total, delta = refs[count:]
-    i = pl.program_id(0)
-
-    @pl.when(i == 0)
-    def _():
-        total[...] = times_transposed(laid(pieces), second[...])
-
-    @pl.when(jnp.logical_and(i > 0, i < steps))
-    def _():
-        total[...] += times_transposed(laid(pieces), second[...])
-
-    @pl.when(i == steps - 1)
-    def _():
-        def act(sel):
-            delta[sel, :] = (total[sel, :] * slope[sel, :]).astype(jnp.bfloat16)
-
-        each_rows(total.shape[0], act)
-
-    @pl.when(i >= steps)
-    def _():
-        both = jnp.dot(delta[...], first[...], preferred_element_type=jnp.float32)
-        near[...] = both[: near.shape[0]].astype(jnp.bfloat16)
-        far[...] = both[near.shape[0] :].astype(jnp.bfloat16)
-
-
-def project_kernel(count, chunk, *refs):
-    pieces = refs[:count]
-    weight, upstream, projected, near, far, rows, total = refs[count:]
-    i = pl.program_id(0)
-    depth = weight.shape[0]
-
-    @pl.when(i == 0)
-    def _():
-        total[...] = jnp.zeros_like(total)
-        rows[...] = laid(pieces)
-
-    def ahead(k, pre):
-        sel = pl.ds(pl.multiple_of(k * chunk, 128), chunk)
-        return pre + jnp.dot(rows[:, sel], weight[sel, :], preferred_element_type=jnp.float32)
-
-    u = lax.fori_loop(0, depth // chunk, ahead, jnp.zeros(projected.shape, jnp.float32))
-    cumul = 0.5 * (1.0 + lax.erf(u * 0.7071067811865476))
-    dense = jnp.exp(-0.5 * u * u) * 0.3989422804014327
-    projected[...] = (u * cumul).astype(jnp.bfloat16)
-    delta = (upstream[...].astype(jnp.float32) * (cumul + u * dense)).astype(jnp.bfloat16)
-
-    def behind(k, _):
-        sel = pl.ds(pl.multiple_of(k * chunk, 128), chunk)
-        total[:, sel] += times_transposed(delta, weight[sel, :])
+    weight, upstream, projected, near, far, held, rows, pre, delta, sems = refs[count:]
+    fetch(weight, held, sems)
+    rows[...] = laid(pieces)
+    pre[...] = jnp.zeros_like(pre)
+    chunk = held.shape[1]
+    half = near.shape[0]
+
+    def ahead(j, _):
+        arrive(weight, held, sems, j)
+        sel = pl.ds(pl.multiple_of(j * chunk, 128), chunk)
+        pre[...] += jnp.dot(rows[:, sel], held[j], preferred_element_type=jnp.float32)
         return 0
 
-    lax.fori_loop(0, depth // chunk, behind, 0)
-
-    @pl.when(i == pl.num_programs(0) - 1)
-    def _():
-        half = near.shape[0]
-        near[...] = total[:half].astype(jnp.bfloat16)
-        far[...] = total[half:].astype(jnp.bfloat16)
+    lax.fori_loop(0, held.shape[0], ahead, 0)
+
+    def act(sel):
+        u = pre[sel, :]
+        cumul = 0.5 * (1.0 + lax.erf(u * 0.7071067811865476))
+        dense = jnp.exp(-0.5 * u * u) * 0.3989422804014327
+        projected[sel, :] = (u * cumul).astype(jnp.bfloat16)
+        grad = upstream[sel, :].astype(jnp.float32)
+        delta[sel, :] = (grad * (cumul + u * dense)).astype(jnp.bfloat16)
+
+    each_rows(pre.shape[0], act)
+
+    def behind(j, _):
+        sel = pl.ds(pl.multiple_of(j * chunk, 128), chunk)
+        back = times_transposed(delta[...], held[j]).astype(jnp.bfloat16)
+        near[:, sel] = back[:half]
+        far[:, sel] = back[half:]
+        return 0
+
+    lax.fori_loop(0, held.shape[0], behind, 0)
 
 
 def settings():
-    return pltpu.CompilerParams(
-        vmem_limit_bytes=56 * 1024 * 1024, dimension_semantics=("arbitrary",)
-    )
-
-
-def vision_pass(kernel, pieces, early, late, slope=None):
+    return pltpu.CompilerParams(vmem_limit_bytes=56 * 1024 * 1024)
+
+
+def whole_blocks(count):
+    return [pl.BlockSpec(memory_space=pltpu.VMEM)] * count
+
+
+def vision_pass(pieces, early, late, slope=None):
     rows = sum(p.shape[0] for p in pieces)
     units, width = early.shape
-    tile = tile_of(width, 640)
-    steps = width // tile
-    soon = lambda i: (0, jnp.minimum(i, steps - 1))
-    then = lambda i: (0, jnp.maximum(i - steps, 0))
-    slopes = pl.BlockSpec((rows, units), lambda i: (0, 0))
-    sums = [pl.BlockSpec((rows // 2, tile), then)] * 2
-    shapes = [jax.ShapeDtypeStruct((rows // 2, width), jnp.bfloat16)] * 2
+    size = max(t for t in range(16, 401, 16) if units % t == 0)
+    blocks = units // size
     given = [] if slope is None else [slope]
+    slopes = [jax.ShapeDtypeStruct((blocks, rows, size), jnp.float32)] * (1 - len(given))
     return pl.pallas_call(
-        functools.partial(kernel, len(pieces), steps),
-        grid=(2 * steps,),
-        in_specs=[pl.BlockSpec((p.shape[0], tile), soon) for p in pieces]
-        + [pl.BlockSpec((units, tile), soon), pl.BlockSpec((units, tile), then)]
-        + [slopes] * len(given),
-        out_specs=sums + [slopes] * (1 - len(given)),
-        out_shape=shapes + [jax.ShapeDtypeStruct((rows, units), jnp.float32)] * (1 - len(given)),
+        functools.partial(vision_kernel, len(pieces), slope is None),
+        in_specs=whole_blocks(len(pieces))
+        + [pl.BlockSpec(memory_space=pl.ANY)] * 2
+        + whole_blocks(len(given)),
+        out_specs=whole_blocks(2 + len(slopes)),
+        out_shape=[jax.ShapeDtypeStruct((rows // 2, width), jnp.bfloat16)] * 2 + slopes,
         scratch_shapes=[
-            pltpu.VMEM((rows, units), jnp.float32),
-            pltpu.VMEM((rows, units), jnp.bfloat16),
+            pltpu.VMEM((blocks, size, width), jnp.bfloat16),
+            pltpu.VMEM((blocks, size, width), jnp.bfloat16),
+            pltpu.VMEM((rows, width), jnp.bfloat16),
+            pltpu.VMEM((rows, width), jnp.float32),
+            pltpu.VMEM((rows, size), jnp.float32),
+            pltpu.VMEM((rows, size), jnp.bfloat16),
+            pltpu.SemaphoreType.DMA((blocks,)),
+            pltpu.SemaphoreType.DMA((blocks,)),
         ],
         compiler_params=settings(),
         cost_estimate=pl.CostEstimate(
@@ -193,25 +197,19 @@
 def project(pieces, weight, upstream):
     rows = sum(p.shape[0] for p in pieces)
     depth, units = weight.shape
-    tile = tile_of(units, 256)
+    size = tile_of(depth, 1280)
     return pl.pallas_call(
-        functools.partial(project_kernel, len(pieces), tile_of(depth, 2560)),
-        grid=(units // tile,),
-        in_specs=[pl.BlockSpec(p.shape, lambda i: (0, 0)) for p in pieces]
-        + [
-            pl.BlockSpec((depth, tile), lambda i: (0, i)),
-            pl.BlockSpec((rows, tile), lambda i: (0, i)),
-        ],
-        out_specs=[
-            pl.BlockSpec((rows, tile), lambda i: (0, i)),
-            pl.BlockSpec((rows // 2, depth), lambda i: (0, 0)),
-            pl.BlockSpec((rows // 2, depth), lambda i: (0, 0)),
-        ],
+        functools.partial(project_kernel, len(pieces)),
+        in_specs=whole_blocks(len(pieces)) + [pl.BlockSpec(memory_space=pl.ANY)] + whole_blocks(1),
+        out_specs=whole_blocks(3),
         out_shape=[jax.ShapeDtypeStruct((rows, units), jnp.bfloat16)]
         + [jax.ShapeDtypeStruct((rows // 2, depth), jnp.bfloat16)] * 2,
         scratch_shapes=[
+            pltpu.VMEM((depth // size, size, units), jnp.bfloat16),
             pltpu.VMEM((rows, depth), jnp.bfloat16),
-            pltpu.VMEM((rows, depth), jnp.float32),
+            pltpu.VMEM((rows, units), jnp.float32),
+            pltpu.VMEM((rows, units), jnp.bfloat16),
+            pltpu.SemaphoreType.DMA((depth // size,)),
         ],
         compiler_params=settings(),
         cost_estimate=pl.CostEstimate(
@@ -321,10 +319,10 @@
         if s:
             block = lax.ppermute(block, "grp", [(g, (g - s) % groups) for g in range(groups)])
         picked.append(block)
-    returned = jnp.take(jnp.stack(picked), shift, axis=0).reshape(size, -1, width)
-    grad_proj = [
-        moves.by_row(returned[:, c * merged_rows : (c + 1) * merged_rows]) for c in range(chunks)
-    ]
+
+    def grad_of(picked, c):
+        returned = jnp.take(jnp.stack(picked), shift, axis=0).reshape(size, -1, width)
+        return moves.by_row(returned[:, c * merged_rows : (c + 1) * merged_rows])
 
     def merge(c, summed):
         outputs = (x[c] + layer_scale * summed).astype(jnp.bfloat16)
@@ -338,12 +336,12 @@
         return own_grad, (own_grad * layer_scale).astype(jnp.bfloat16)
 
     early, late = first_weight.T, second_weight
-    near_b, far_b, slope_b = vision_pass(forward_kernel, patches_b, early, late)
+    near_b, far_b, slope_b = vision_pass(patches_b, early, late)
     near_b, far_b, rail_a = tied((near_b, far_b, rail_a))
     patches_a = moves.gathered(rail_a)
     terms_b = moves.send(near_b, far_b)
-    near_a, far_a, slope_a = vision_pass(forward_kernel, patches_a, early, late)
-    near_a, far_a, terms_b = tied((near_a, far_a, terms_b))
+    near_a, far_a, slope_a = vision_pass(patches_a, early, late)
+    near_a, far_a, terms_b, picked = tied((near_a, far_a, terms_b, picked))
     terms_a = moves.send(near_a, far_a)
     mixed_b, *stats_b = merge(1, moves.summed(terms_b))
     rail_b = moves.spread(mixed_b)
@@ -351,41 +349,49 @@
     mixed_a, *stats_a = merge(0, moves.summed(terms_a))
     rail_a = moves.spread(mixed_a)
     merged_b = moves.gathered(rail_b)
-    projected_b, near_b, far_b = project(merged_b, proj_weight, grad_proj[1])
+    projected_b, near_b, far_b = project(merged_b, proj_weight, grad_of(picked, 1))
     near_b, far_b, rail_a = tied((near_b, far_b, rail_a))
     merged_a = moves.gathered(rail_a)
     terms_b = moves.send(near_b, far_b)
-    projected_a, near_a, far_a = project(merged_a, proj_weight, grad_proj[0])
+    projected_a, near_a, far_a = project(merged_a, proj_weight, grad_of(picked, 0))
     near_a, far_a, terms_b = tied((near_a, far_a, terms_b))
     terms_a = moves.send(near_a, far_a)
 
     projected = jnp.concatenate(
         [moves.by_rank(projected_a, size), moves.by_rank(projected_b, size)], 1
     ).reshape(images, image_rows, width)
-    seq_embed = text_embed
+    arrived = []
     for s in range(groups):
         block = lax.dynamic_index_in_dim(projected, image_of[s], 0, False)
         if s:
             block = lax.ppermute(block, "grp", [(g, (g + s) % groups) for g in range(groups)])
-        if groups > images:
-            there = lax.dynamic_slice_in_dim(seq_embed, spot[s], image_rows, 0)
-            block = jnp.where(used[s], block, there)
-        seq_embed = lax.dynamic_update_slice_in_dim(seq_embed, block, spot[s], 0)
+        arrived.append(block)
+
+    def embed(text, arrived):
+        for s in range(groups):
+            block = arrived[s]
+            if groups > images:
+                there = lax.dynamic_slice_in_dim(text, spot[s], image_rows, 0)
+                block = jnp.where(used[s], block, there)
+            text = lax.dynamic_update_slice_in_dim(text, block, spot[s], 0)
+        return text
 
     own_b, scaled_b = unmerge(moves.summed(terms_b), *stats_b)
     rail_b = moves.spread(scaled_b)
-    rail_b, terms_a = tied((rail_b, terms_a))
+    rail_b, terms_a, arrived = tied((rail_b, terms_a, arrived))
     own_a, scaled_a = unmerge(moves.summed(terms_a), *stats_a)
     rail_a = moves.spread(scaled_a)
     grad_out_b = moves.gathered(rail_b)
-    near_b, far_b = vision_pass(backward_kernel, grad_out_b, late, early, slope_b)
+    near_b, far_b = vision_pass(grad_out_b, late, early, slope_b)
     near_b, far_b, rail_a = tied((near_b, far_b, rail_a))
     grad_out_a = moves.gathered(rail_a)
     terms_b = moves.send(near_b, far_b)
-    near_a, far_a = vision_pass(backward_kernel, grad_out_a, late, early, slope_a)
-    near_a, far_a, terms_b, seq_embed = tied((near_a, far_a, terms_b, seq_embed))
-    normed_a = moves.summed(moves.send(near_a, far_a))
+    near_a, far_a = vision_pass(grad_out_a, late, early, slope_a)
+    near_a, far_a, terms_b, text = tied((near_a, far_a, terms_b, text_embed))
+    terms_a = moves.send(near_a, far_a)
     normed_b = moves.summed(terms_b)
+    terms_a, seq_embed, normed_b = tied((terms_a, embed(text, arrived), normed_b))
+    normed_a = moves.summed(terms_a)
     grads = [
         own_a + norm_back(normed_a, vis_gain, hat[0], inv[0]),
         own_b + norm_back(normed_b, vis_gain, hat[1], inv[1]),

time: 322 us -> 338 us (1.050)
  waiting for transfers between devices: 75.1 us -> 85.5 us
  other arithmetic: 12.5 us -> 16 us
    ppermute x36, waiting for transfers between devices: 68.4 us -> 81 us  [shift(): return lax.ppermute(block, 'tp', pairs)]
    unnamed x141 -> x154, local copies, waits for them, and re-layouts: 8.63 us -> 4.57 us
  transfers between devices with their start and end apart: 72 -> 72, of which waited for: 15 -> 14; matrix products, arithmetic and copies ran while one was open for 6% -> 7% of each run, Pallas kernels for 35% -> 34%
where the time goes in v5:
time: 338 us; the launch traced here: 336 us
  Pallas kernels  114 us (34%)
  waiting for transfers between devices  85.5 us (25%)
  starting transfers between devices  79.3 us (23%)
  local copies, waits for them, and re-layouts  24.5 us (7%)
  between operations  16.3 us (5%)
  other arithmetic  16 us (5%)
    ppermute x36, waiting for transfers between devices, shift(): return lax.ppermute(block, 'tp', pairs)  81 us
    pallas_call x4, Pallas kernels, vision_pass(): pl.pallas_call(functools.partial(vision_kernel, len(pieces), slope is Non...  71.7 us
    ppermute x36, starting transfers between devices, shift(): return lax.ppermute(block, 'tp', pairs)  65.2 us
    pallas_call x2, Pallas kernels, project(): pl.pallas_call(functools.partial(project_kernel, len(pieces)), in_specs=w...  42.6 us
  transfers between devices with their start and end apart: 72, of which 14 were waited for; matrix products, arithmetic and copies ran while one was open for 7% of the time, Pallas kernels for 34%

profile of v5, /device:TPU:0, one launch (start us, length us, event | category | flops | bytes accessed | tf_op | source)
XLA Modules:
  0.0 335.9 jit_solution(16007676186549539948)
XLA Ops:
  0.7 3.3 copy.17
  5.0 5.0 %collective-permute-start.2 = (bf16[32,3200]{1,0:T(8,128)(2,1)S(1)}, bf16[32,3200]{1,0:T(8,128)(2,1)S(1)}, u32[]{:S(2)}, u32[]{:S(2)}) collective-permute-start(bf16[32,3200]{1,0:T(8,128)(2,1)S(1)} %get-tuple-element.92.refs_0_), channel_id=1, source_target_pairs={{0,6},{1,7},{2,0},{3,1},{4,2},{5,3},{6,4},{7,5},{8,14},{9,15},{10,... | collective-permute-start | bytes 614408 | tf_op jit(solution)/shard_map/ppermute | solution.py:238
  10.1 1.0 collective-permute-start
  12.7 2.9 collective-permute-done.2.refs_3_
  15.6 11.9 %collective-permute-done.1.refs_2_ = bf16[32,3200]{1,0:T(8,128)(2,1)S(1)} collective-permute-done((bf16[32,3200]{1,0:T(8,128)(2,1)S(1)}, bf16[32,3200]{1,0:T(8,128)(2,1)S(1)}, u32[]{:S(2)}, u32[]{:S(2)}) %collective-permute-start.1) | collective-permute-done | bytes 204832 | tf_op jit(solution)/shard_map/ppermute | solution.py:238
  29.0 2.7 collective-permute-start.8
  31.7 1.7 collective-permute-start.7
  34.2 18.3 %shard_map.113 = (bf16[128,3200]{1,0:T(8,128)(2,1)}, bf16[128,3200]{1,0:T(8,128)(2,1)}, f32[4,256,400]{2,1,0:T(8,128)}) custom-call(bf16[32,3200]{1,0:T(8,128)(2,1)} %copy-done.8, bf16[32,3200]{1,0:T(8,128)(2,1)} %copy-done.26, bf16[32,3200]{1,0:T(8,128)(2,1)} %copy-done.25, bf16[32,3200]{1,0:T(8,128)(2,1)} %copy-done.24, bf16[32,3200]{1,0:T(8,128)(2,1)} %copy-done.37, ...), custom_call_target="tpu_custom_call" | custom-call | flops 5242880000 | bytes 25395200 | tf_op jit(solution)/shard_map/pallas_call | solution.py:171
  60.9 1.7 constant_dynamic-slice_fusion
  62.6 1.5 collective-permute-start.20
  67.0 1.3 fusion.43
  68.4 1.5 collective-permute-start.18
  69.9 1.5 collective-permute-start.19
  71.5 2.6 collective-permute-start.16
  74.1 1.2 collective-permute-start.15
  75.3 18.3 %shard_map.114 = (bf16[128,3200]{1,0:T(8,128)(2,1)}, bf16[128,3200]{1,0:T(8,128)(2,1)}, f32[4,256,400]{2,1,0:T(8,128)}) custom-call(bf16[32,3200]{1,0:T(8,128)(2,1)} %copy-done.5, bf16[32,3200]{1,0:T(8,128)(2,1)} %copy-done.14, bf16[32,3200]{1,0:T(8,128)(2,1)} %copy-done.13, bf16[32,3200]{1,0:T(8,128)(2,1)} %copy-done.12, bf16[32,3200]{1,0:T(8,128)(2,1)} %copy-done.28, ...), custom_call_target="tpu_custom_call" | custom-call | flops 5242880000 | bytes 25395200 | tf_op jit(solution)/shard_map/pallas_call | solution.py:171
  95.5 0.7 collective-permute-start.23
  96.2 1.9 collective-permute-start.22
  98.2 1.4 collective-permute-start.21
  102.3 2.8 collective-permute-start.26
  105.2 1.0 collective-permute-start.25
  106.2 0.8 select_bitcast_fusion
  107.0 19.1 %collective-permute-done.22.refs_2_ = bf16[8,12800]{1,0:T(8,128)(2,1)} collective-permute-done((bf16[8,12800]{1,0:T(8,128)(2,1)S(1)}, bf16[8,12800]{1,0:T(8,128)(2,1)}, u32[]{:S(2)}, u32[]{:S(2)}) %collective-permute-start.22) | collective-permute-done | bytes 204832 | tf_op jit(solution)/shard_map/ppermute | solution.py:238
  126.1 4.3 %collective-permute-done.26 = bf16[32,3200]{1,0:T(8,128)(2,1)S(1)} collective-permute-done((bf16[32,3200]{1,0:T(8,128)(2,1)S(1)}, bf16[32,3200]{1,0:T(8,128)(2,1)S(1)}, u32[]{:S(2)}, u32[]{:S(2)}) %collective-permute-start.26) | collective-permute-done | bytes 204832 | tf_op jit(solution)/shard_map/ppermute | solution.py:238
  132.8 6.0 %collective-permute-start.34 = (bf16[8,12800]{1,0:T(8,128)(2,1)S(1)}, bf16[8,12800]{1,0:T(8,128)(2,1)S(1)}, u32[]{:S(2)}, u32[]{:S(2)}) collective-permute-start(bf16[8,12800]{1,0:T(8,128)(2,1)S(1)} %multiply_convert_fusion.4.refs_0_), channel_id=1, source_target_pairs={{0,6},{1,7},{2,0},{3,1},{4,2},{5,3},{6,4},{7,5},{8,14},{9,15},{10,... | collective-permute-start | bytes 614408 | tf_op jit(solution)/shard_map/ppermute | solution.py:238
  138.9 0.7 collective-permute-start.32
  140.4 21.2 %shard_map.115 = (bf16[64,1024]{1,0:T(8,128)(2,1)}, bf16[32,12800]{1,0:T(8,128)(2,1)}, bf16[32,12800]{1,0:T(8,128)(2,1)}) custom-call(bf16[8,12800]{1,0:T(8,128)(2,1)} %copy-done.9, bf16[8,12800]{1,0:T(8,128)(2,1)} %collective-permute-done.21.refs_1_, bf16[8,12800]{1,0:T(8,128)(2,1)} %collective-permute-done.22.refs_2_, ...), custom_call_target="tpu_custom_call" | custom-call | flops 3355443200 | bytes 29753344 | tf_op jit(solution)/shard_map/pallas_call | solution.py:201
  170.9 1.5 gather_fusion.4
  173.2 21.3 %shard_map.116 = (bf16[64,1024]{1,0:T(8,128)(2,1)}, bf16[32,12800]{1,0:T(8,128)(2,1)}, bf16[32,12800]{1,0:T(8,128)(2,1)}) custom-call(bf16[8,12800]{1,0:T(8,128)(2,1)} %copy-done.10, bf16[8,12800]{1,0:T(8,128)(2,1)} %copy-done.21, bf16[8,12800]{1,0:T(8,128)(2,1)} %copy-done.19, bf16[8,12800]{1,0:T(8,128)(2,1)} %copy-done.17, bf16[8,12800]{1,0:T(8,128)(2,1)} %copy-done.27, ...), custom_call_target="tpu_custom_call" | custom-call | flops 3355443200 | bytes 29753344 | tf_op jit(solution)/shard_map/pallas_call | solution.py:201
  194.5 1.5 gather_fusion.3
  196.4 2.7 collective-permute-start.42
  199.1 1.2 collective-permute-start.41
  200.3 1.3 collective-permute-start.40
  202.2 1.5 collective-permute-start.51
  203.8 2.5 collective-permute-done.42
  206.8 7.7 %collective-permute-done.41 = bf16[8,12800]{1,0:T(8,128)(2,1)S(1)} collective-permute-done((bf16[8,12800]{1,0:T(8,128)(2,1)S(1)}, bf16[8,12800]{1,0:T(8,128)(2,1)S(1)}, u32[]{:S(2)}, u32[]{:S(2)}) %collective-permute-start.41) | collective-permute-done | bytes 204832 | tf_op jit(solution)/shard_map/ppermute | solution.py:238
  215.3 5.8 %collective-permute-start.45 = (bf16[32,3200]{1,0:T(8,128)(2,1)S(1)}, bf16[32,3200]{1,0:T(8,128)(2,1)S(1)}, u32[]{:S(2)}, u32[]{:S(2)}) collective-permute-start(bf16[32,3200]{1,0:T(8,128)(2,1)S(1)} %multiply_convert_fusion.2.refs_0_), channel_id=1, source_target_pairs={{0,6},{1,7},{2,0},{3,1},{4,2},{5,3},{6,4},{7,5},{8,14},{9,15},{10,... | collective-permute-start | bytes 614408 | tf_op jit(solution)/shard_map/ppermute | solution.py:238
  222.1 2.5 collective-permute-start.43
  225.0 1.5 collective-permute-start.48
  226.6 4.3 %collective-permute-start.47 = (bf16[8,12800]{1,0:T(8,128)(2,1)S(1)}, bf16[8,12800]{1,0:T(8,128)(2,1)S(1)}, u32[]{:S(2)}, u32[]{:S(2)}) collective-permute-start(bf16[8,12800]{1,0:T(8,128)(2,1)S(1)} %get-tuple-element.229), channel_id=1, source_target_pairs={{0,6},{1,7},{2,0},{3,1},{4,2},{5,3},{6,4},{7,5},{8,14},{9,15},{10,... | collective-permute-start | bytes 614408 | tf_op jit(solution)/shard_map/ppermute | solution.py:238
  231.0 18.6 %collective-permute-done.44.refs_2_ = bf16[32,3200]{1,0:T(8,128)(2,1)S(1)} collective-permute-done((bf16[32,3200]{1,0:T(8,128)(2,1)S(1)}, bf16[32,3200]{1,0:T(8,128)(2,1)S(1)}, u32[]{:S(2)}, u32[]{:S(2)}) %collective-permute-start.44) | collective-permute-done | bytes 204832 | tf_op jit(solution)/shard_map/ppermute | solution.py:238
  249.6 4.3 %collective-permute-done.48 = bf16[8,12800]{1,0:T(8,128)(2,1)S(1)} collective-permute-done((bf16[8,12800]{1,0:T(8,128)(2,1)S(1)}, bf16[8,12800]{1,0:T(8,128)(2,1)S(1)}, u32[]{:S(2)}, u32[]{:S(2)}) %collective-permute-start.48) | collective-permute-done | bytes 204832 | tf_op jit(solution)/shard_map/ppermute | solution.py:238
  254.0 1.7 collective-permute-done.47
  257.5 5.6 %collective-permute-start.59 = (bf16[32,3200]{1,0:T(8,128)(2,1)S(1)}, bf16[32,3200]{1,0:T(8,128)(2,1)S(1)}, u32[]{:S(2)}, u32[]{:S(2)}) collective-permute-start(bf16[32,3200]{1,0:T(8,128)(2,1)S(1)} %multiply_convert_fusion.refs_0_), channel_id=1, source_target_pairs={{0,6},{1,7},{2,0},{3,1},{4,2},{5,3},{6,4},{7,5},{8,14},{9,15},{10,... | collective-permute-start | bytes 614408 | tf_op jit(solution)/shard_map/ppermute | solution.py:238
  263.2 0.9 collective-permute-start.57
  264.8 17.6 %shard_map.117 = (bf16[128,3200]{1,0:T(8,128)(2,1)}, bf16[128,3200]{1,0:T(8,128)(2,1)}) custom-call(bf16[32,3200]{1,0:T(8,128)(2,1)} %copy-done.6, bf16[32,3200]{1,0:T(8,128)(2,1)} %copy-done.18, bf16[32,3200]{1,0:T(8,128)(2,1)} %copy-done.16, bf16[32,3200]{1,0:T(8,128)(2,1)} %copy-done.15, bf16[32,3200]{1,0:T(8,128)(2,1)} %copy-done.39, ...), custom_call_target="tpu_custom_call" | custom-call | flops 5242880000 | bytes 25395200 | tf_op jit(solution)/shard_map/pallas_call | solution.py:171
  283.7 1.7 collective-permute-done.64
  285.4 1.3 fusion.47
  286.8 2.6 collective-permute-start.67
  289.5 1.0 collective-permute-start.66
  290.4 1.5 collective-permute-start.65
  292.7 17.5 %shard_map.118 = (bf16[128,3200]{1,0:T(8,128)(2,1)}, bf16[128,3200]{1,0:T(8,128)(2,1)}) custom-call(bf16[32,3200]{1,0:T(8,128)(2,1)} %copy-done.7, bf16[32,3200]{1,0:T(8,128)(2,1)} %copy-done.23, bf16[32,3200]{1,0:T(8,128)(2,1)} %copy-done.22, bf16[32,3200]{1,0:T(8,128)(2,1)} %copy-done.20, bf16[32,3200]{1,0:T(8,128)(2,1)} %copy-done.32, ...), custom_call_target="tpu_custom_call" | custom-call | flops 5242880000 | bytes 25395200 | tf_op jit(solution)/shard_map/pallas_call | solution.py:171
  310.4 2.5 collective-permute-done.68
  312.9 1.3 fusion.48
  314.2 0.8 fusion.55
  315.6 2.0 collective-permute-start.70
  317.6 1.3 collective-permute-start.69
  319.0 1.6 dynamic_update_slice.12
  320.6 1.6 dynamic_update_slice.13
  322.2 1.6 dynamic_update_slice.14
  323.8 1.6 dynamic_update_slice.15
  325.5 7.8 %collective-permute-done.70 = bf16[32,3200]{1,0:T(8,128)(2,1)} collective-permute-done((bf16[32,3200]{1,0:T(8,128)(2,1)}, bf16[32,3200]{1,0:T(8,128)(2,1)}, u32[]{:S(2)}, u32[]{:S(2)}) %collective-permute-start.70) | collective-permute-done | bytes 204832 | tf_op jit(solution)/shard_map/ppermute | solution.py:238
  333.2 1.5 multiply_reduce_fusion.4
  335.1 0.8 pad_maximum_fusion
  (344 shorter events, 28.9 us)
Async XLA Ops:
  5.0 10.6 %collective-permute-start.2 = (bf16[32,3200]{1,0:T(8,128)(2,1)S(1)}, bf16[32,3200]{1,0:T(8,128)(2,1)S(1)}, u32[]{:S(2)}, u32[]{:S(2)}) collective-permute-start(bf16[32,3200]{1,0:T(8,128)(2,1)S(1)} %get-tuple-element.92.refs_0_), channel_id=1, source_target_pairs={{0,6},{1,7},{2,0},{3,1},{4,2},{5,3},{6,4},{7,5},{8,14},{9,15},{10,... | collective-permute-start | bytes 614408 | tf_op jit(solution)/shard_map/ppermute | solution.py:238
  10.1 17.4 %collective-permute-start.1 = (bf16[32,3200]{1,0:T(8,128)(2,1)S(1)}, bf16[32,3200]{1,0:T(8,128)(2,1)S(1)}, u32[]{:S(2)}, u32[]{:S(2)}) collective-permute-start(bf16[32,3200]{1,0:T(8,128)(2,1)S(1)} %get-tuple-element.92.refs_0_), channel_id=1, source_target_pairs={{0,4},{1,5},{2,6},{3,7},{4,0},{5,1},{6,2},{7,3},{8,12},{9,13},{10,... | collective-permute-start | bytes 614408 | tf_op jit(solution)/shard_map/ppermute | solution.py:238
  10.1 17.4 %collective-permute-start = (bf16[32,3200]{1,0:T(8,128)(2,1)S(1)}, bf16[32,3200]{1,0:T(8,128)(2,1)S(1)}, u32[]{:S(2)}, u32[]{:S(2)}) collective-permute-start(bf16[32,3200]{1,0:T(8,128)(2,1)S(1)} %get-tuple-element.92.refs_0_), channel_id=1, source_target_pairs={{0,2},{1,3},{2,4},{3,5},{4,6},{5,7},{6,0},{7,1},{8,10},{9,11},{10,... | collective-permute-start | bytes 614408 | tf_op jit(solution)/shard_map/ppermute | solution.py:238
  28.0 5.4 %collective-permute-start.5 = (bf16[32,3200]{1,0:T(8,128)(2,1)S(1)}, bf16[32,3200]{1,0:T(8,128)(2,1)S(1)}, u32[]{:S(2)}, u32[]{:S(2)}) collective-permute-start(bf16[32,3200]{1,0:T(8,128)(2,1)S(1)} %collective-permute-done.1.refs_2_), channel_id=1, source_target_pairs={{0,1},{1,0},{2,3},{3,2},{4,5},{5,4},{6,7},{7,6},{8,9},{9,8},{10,11... | collective-permute-start | bytes 614408 | tf_op jit(solution)/shard_map/ppermute | solution.py:244
  28.6 23.9 %collective-permute-start.9 = (bf16[32,3200]{1,0:T(8,128)(2,1)S(1)}, bf16[32,3200]{1,0:T(8,128)(2,1)S(1)}, u32[]{:S(2)}, u32[]{:S(2)}) collective-permute-start(bf16[32,3200]{1,0:T(8,128)(2,1)S(1)} %get-tuple-element.99.refs_0_), channel_id=1, source_target_pairs={{0,6},{1,7},{2,0},{3,1},{4,2},{5,3},{6,4},{7,5},{8,14},{9,15},{10,... | collective-permute-start | bytes 614408 | tf_op jit(solution)/shard_map/ppermute | solution.py:238
  29.0 23.5 %collective-permute-start.8 = (bf16[32,3200]{1,0:T(8,128)(2,1)S(1)}, bf16[32,3200]{1,0:T(8,128)(2,1)S(1)}, u32[]{:S(2)}, u32[]{:S(2)}) collective-permute-start(bf16[32,3200]{1,0:T(8,128)(2,1)S(1)} %get-tuple-element.99.refs_0_), channel_id=1, source_target_pairs={{0,4},{1,5},{2,6},{3,7},{4,0},{5,1},{6,2},{7,3},{8,12},{9,13},{10,... | collective-permute-start | bytes 614408 | tf_op jit(solution)/shard_map/ppermute | solution.py:238
  31.7 20.8 %collective-permute-start.7 = (bf16[32,3200]{1,0:T(8,128)(2,1)S(1)}, bf16[32,3200]{1,0:T(8,128)(2,1)S(1)}, u32[]{:S(2)}, u32[]{:S(2)}) collective-permute-start(bf16[32,3200]{1,0:T(8,128)(2,1)S(1)} %get-tuple-element.99.refs_0_), channel_id=1, source_target_pairs={{0,2},{1,3},{2,4},{3,5},{4,6},{5,7},{6,0},{7,1},{8,10},{9,11},{10,... | collective-permute-start | bytes 614408 | tf_op jit(solution)/shard_map/ppermute | solution.py:238
  52.5 14.1 %collective-permute-start.14 = (bf16[128,3200]{1,0:T(8,128)(2,1)}, bf16[128,3200]{1,0:T(8,128)(2,1)S(1)}, u32[]{:S(2)}, u32[]{:S(2)}) collective-permute-start(bf16[128,3200]{1,0:T(8,128)(2,1)} %get-tuple-element.106), channel_id=1, source_target_pairs={{0,1},{1,0},{2,3},{3,2},{4,5},{5,4},{6,7},{7,6},{8,9},{9,8},{10,11... | collective-permute-start | bytes 2457608 | tf_op jit(solution)/shard_map/ppermute | solution.py:251
  62.6 5.7 %collective-permute-start.20 = (bf16[32,1024]{1,0:T(8,128)(2,1)S(1)}, bf16[32,1024]{1,0:T(8,128)(2,1)S(1)}, u32[]{:S(2)}, u32[]{:S(2)}) collective-permute-start(bf16[32,1024]{1,0:T(8,128)(2,1)S(1)} %get-tuple-element.205), channel_id=1, source_target_pairs={{0,8},{8,16},{16,24},{24,0},{1,9},{9,17},{17,25},{25,1},{2,10},{10... | collective-permute-start | bytes 196616 | tf_op jit(solution)/shard_map/ppermute | solution.py:320
  66.7 7.5 %collective-permute-start.13 = (bf16[32,3200]{1,0:T(8,128)(2,1)S(1)}, bf16[32,3200]{1,0:T(8,128)(2,1)S(1)}, u32[]{:S(2)}, u32[]{:S(2)}) collective-permute-start(bf16[32,3200]{1,0:T(8,128)(2,1)S(1)} %collective-permute-done.9.refs_3_), channel_id=1, source_target_pairs={{0,1},{1,0},{2,3},{3,2},{4,5},{5,4},{6,7},{7,6},{8,9},{9,8},{10,11... | collective-permute-start | bytes 614408 | tf_op jit(solution)/shard_map/ppermute | solution.py:244
  68.4 25.4 %collective-permute-start.18 = (bf16[32,1024]{1,0:T(8,128)(2,1)}, bf16[32,1024]{1,0:T(8,128)(2,1)S(1)}, u32[]{:S(2)}, u32[]{:S(2)}) collective-permute-start(bf16[32,1024]{1,0:T(8,128)(2,1)} %get-tuple-element.206), channel_id=1, source_target_pairs={{0,24},{8,0},{16,8},{24,16},{1,25},{9,1},{17,9},{25,17},{2,26},{10... | collective-permute-start | bytes 196616 | tf_op jit(solution)/shard_map/ppermute | solution.py:320
  69.9 23.9 %collective-permute-start.19 = (bf16[32,1024]{1,0:T(8,128)(2,1)S(1)}, bf16[32,1024]{1,0:T(8,128)(2,1)S(1)}, u32[]{:S(2)}, u32[]{:S(2)}) collective-permute-start(bf16[32,1024]{1,0:T(8,128)(2,1)S(1)} %get-tuple-element.208), channel_id=1, source_target_pairs={{0,16},{8,24},{16,0},{24,8},{1,17},{9,25},{17,1},{25,9},{2,18},{10... | collective-permute-start | bytes 196616 | tf_op jit(solution)/shard_map/ppermute | solution.py:320
  71.4 22.4 %collective-permute-start.17 = (bf16[32,3200]{1,0:T(8,128)(2,1)S(1)}, bf16[32,3200]{1,0:T(8,128)(2,1)S(1)}, u32[]{:S(2)}, u32[]{:S(2)}) collective-permute-start(bf16[32,3200]{1,0:T(8,128)(2,1)S(1)} %get-tuple-element.236), channel_id=1, source_target_pairs={{0,2},{1,3},{2,4},{3,5},{4,6},{5,7},{6,0},{7,1},{8,10},{9,11},{10,... | collective-permute-start | bytes 614408 | tf_op jit(solution)/shard_map/ppermute | solution.py:238
  71.5 22.3 %collective-permute-start.16 = (bf16[32,3200]{1,0:T(8,128)(2,1)S(1)}, bf16[32,3200]{1,0:T(8,128)(2,1)S(1)}, u32[]{:S(2)}, u32[]{:S(2)}) collective-permute-start(bf16[32,3200]{1,0:T(8,128)(2,1)S(1)} %get-tuple-element.237), channel_id=1, source_target_pairs={{0,4},{1,5},{2,6},{3,7},{4,0},{5,1},{6,2},{7,3},{8,12},{9,13},{10,... | collective-permute-start | bytes 614408 | tf_op jit(solution)/shard_map/ppermute | solution.py:238
  74.1 19.7 %collective-permute-start.15 = (bf16[32,3200]{1,0:T(8,128)(2,1)S(1)}, bf16[32,3200]{1,0:T(8,128)(2,1)S(1)}, u32[]{:S(2)}, u32[]{:S(2)}) collective-permute-start(bf16[32,3200]{1,0:T(8,128)(2,1)S(1)} %get-tuple-element.238), channel_id=1, source_target_pairs={{0,6},{1,7},{2,0},{3,1},{4,2},{5,3},{6,4},{7,5},{8,14},{9,15},{10,... | collective-permute-start | bytes 614408 | tf_op jit(solution)/shard_map/ppermute | solution.py:238
  95.3 6.5 %collective-permute-start.24 = (bf16[128,3200]{1,0:T(8,128)(2,1)}, bf16[128,3200]{1,0:T(8,128)(2,1)S(1)}, u32[]{:S(2)}, u32[]{:S(2)}) collective-permute-start(bf16[128,3200]{1,0:T(8,128)(2,1)} %get-tuple-element.112), channel_id=1, source_target_pairs={{0,1},{1,0},{2,3},{3,2},{4,5},{5,4},{6,7},{7,6},{8,9},{9,8},{10,11... | collective-permute-start | bytes 2457608 | tf_op jit(solution)/shard_map/ppermute | solution.py:251
  95.5 9.6 %collective-permute-start.23 = (bf16[8,12800]{1,0:T(8,128)(2,1)S(1)}, bf16[8,12800]{1,0:T(8,128)(2,1)}, u32[]{:S(2)}, u32[]{:S(2)}) collective-permute-start(bf16[8,12800]{1,0:T(8,128)(2,1)S(1)} %multiply_convert_fusion.5.refs_0_), channel_id=1, source_target_pairs={{0,6},{1,7},{2,0},{3,1},{4,2},{5,3},{6,4},{7,5},{8,14},{9,15},{10,... | collective-permute-start | bytes 614408 | tf_op jit(solution)/shard_map/ppermute | solution.py:238
  96.2 29.9 %collective-permute-start.22 = (bf16[8,12800]{1,0:T(8,128)(2,1)S(1)}, bf16[8,12800]{1,0:T(8,128)(2,1)}, u32[]{:S(2)}, u32[]{:S(2)}) collective-permute-start(bf16[8,12800]{1,0:T(8,128)(2,1)S(1)} %multiply_convert_fusion.5.refs_0_), channel_id=1, source_target_pairs={{0,4},{1,5},{2,6},{3,7},{4,0},{5,1},{6,2},{7,3},{8,12},{9,13},{10,... | collective-permute-start | bytes 614408 | tf_op jit(solution)/shard_map/ppermute | solution.py:238
  98.2 27.9 %collective-permute-start.21 = (bf16[8,12800]{1,0:T(8,128)(2,1)S(1)}, bf16[8,12800]{1,0:T(8,128)(2,1)}, u32[]{:S(2)}, u32[]{:S(2)}) collective-permute-start(bf16[8,12800]{1,0:T(8,128)(2,1)S(1)} %multiply_convert_fusion.5.refs_0_), channel_id=1, source_target_pairs={{0,2},{1,3},{2,4},{3,5},{4,6},{5,7},{6,0},{7,1},{8,10},{9,11},{10,... | collective-permute-start | bytes 614408 | tf_op jit(solution)/shard_map/ppermute | solution.py:238
  102.1 24.0 %collective-permute-start.27 = (bf16[32,3200]{1,0:T(8,128)(2,1)S(1)}, bf16[32,3200]{1,0:T(8,128)(2,1)S(1)}, u32[]{:S(2)}, u32[]{:S(2)}) collective-permute-start(bf16[32,3200]{1,0:T(8,128)(2,1)S(1)} %get-tuple-element.233), channel_id=1, source_target_pairs={{0,2},{1,3},{2,4},{3,5},{4,6},{5,7},{6,0},{7,1},{8,10},{9,11},{10,... | collective-permute-start | bytes 614408 | tf_op jit(solution)/shard_map/ppermute | solution.py:238
  102.3 28.1 %collective-permute-start.26 = (bf16[32,3200]{1,0:T(8,128)(2,1)S(1)}, bf16[32,3200]{1,0:T(8,128)(2,1)S(1)}, u32[]{:S(2)}, u32[]{:S(2)}) collective-permute-start(bf16[32,3200]{1,0:T(8,128)(2,1)S(1)} %get-tuple-element.234), channel_id=1, source_target_pairs={{0,4},{1,5},{2,6},{3,7},{4,0},{5,1},{6,2},{7,3},{8,12},{9,13},{10,... | collective-permute-start | bytes 614408 | tf_op jit(solution)/shard_map/ppermute | solution.py:238
  105.2 25.2 %collective-permute-start.25 = (bf16[32,3200]{1,0:T(8,128)(2,1)S(1)}, bf16[32,3200]{1,0:T(8,128)(2,1)S(1)}, u32[]{:S(2)}, u32[]{:S(2)}) collective-permute-start(bf16[32,3200]{1,0:T(8,128)(2,1)S(1)} %get-tuple-element.235), channel_id=1, source_target_pairs={{0,6},{1,7},{2,0},{3,1},{4,2},{5,3},{6,4},{7,5},{8,14},{9,15},{10,... | collective-permute-start | bytes 614408 | tf_op jit(solution)/shard_map/ppermute | solution.py:238
  131.6 7.2 %collective-permute-start.28 = (bf16[8,12800]{1,0:T(8,128)(2,1)S(1)}, bf16[8,12800]{1,0:T(8,128)(2,1)S(1)}, u32[]{:S(2)}, u32[]{:S(2)}) collective-permute-start(bf16[8,12800]{1,0:T(8,128)(2,1)S(1)} %multiply_convert_fusion.5.refs_0_), channel_id=1, source_target_pairs={{0,1},{1,0},{2,3},{3,2},{4,5},{5,4},{6,7},{7,6},{8,9},{9,8},{10,11... | collective-permute-start | bytes 614408 | tf_op jit(solution)/shard_map/ppermute | solution.py:244
  131.6 7.2 %collective-permute-start.29 = (bf16[8,12800]{1,0:T(8,128)(2,1)}, bf16[8,12800]{1,0:T(8,128)(2,1)S(1)}, u32[]{:S(2)}, u32[]{:S(2)}) collective-permute-start(bf16[8,12800]{1,0:T(8,128)(2,1)} %collective-permute-done.21.refs_1_), channel_id=1, source_target_pairs={{0,1},{1,0},{2,3},{3,2},{4,5},{5,4},{6,7},{7,6},{8,9},{9,8},{10,11... | collective-permute-start | bytes 614408 | tf_op jit(solution)/shard_map/ppermute | solution.py:244
  132.1 7.4 %collective-permute-start.30 = (bf16[8,12800]{1,0:T(8,128)(2,1)}, bf16[8,12800]{1,0:T(8,128)(2,1)S(1)}, u32[]{:S(2)}, u32[]{:S(2)}) collective-permute-start(bf16[8,12800]{1,0:T(8,128)(2,1)} %collective-permute-done.22.refs_2_), channel_id=1, source_target_pairs={{0,1},{1,0},{2,3},{3,2},{4,5},{5,4},{6,7},{7,6},{8,9},{9,8},{10,11... | collective-permute-start | bytes 614408 | tf_op jit(solution)/shard_map/ppermute | solution.py:244
  132.2 7.4 %collective-permute-start.31 = (bf16[8,12800]{1,0:T(8,128)(2,1)}, bf16[8,12800]{1,0:T(8,128)(2,1)S(1)}, u32[]{:S(2)}, u32[]{:S(2)}) collective-permute-start(bf16[8,12800]{1,0:T(8,128)(2,1)} %collective-permute-done.23.refs_3_), channel_id=1, source_target_pairs={{0,1},{1,0},{2,3},{3,2},{4,5},{5,4},{6,7},{7,6},{8,9},{9,8},{10,11... | collective-permute-start | bytes 614408 | tf_op jit(solution)/shard_map/ppermute | solution.py:244
  132.8 28.8 %collective-permute-start.34 = (bf16[8,12800]{1,0:T(8,128)(2,1)S(1)}, bf16[8,12800]{1,0:T(8,128)(2,1)S(1)}, u32[]{:S(2)}, u32[]{:S(2)}) collective-permute-start(bf16[8,12800]{1,0:T(8,128)(2,1)S(1)} %multiply_convert_fusion.4.refs_0_), channel_id=1, source_target_pairs={{0,6},{1,7},{2,0},{3,1},{4,2},{5,3},{6,4},{7,5},{8,14},{9,15},{10,... | collective-permute-start | bytes 614408 | tf_op jit(solution)/shard_map/ppermute | solution.py:238
  138.8 22.9 %collective-permute-start.33 = (bf16[8,12800]{1,0:T(8,128)(2,1)S(1)}, bf16[8,12800]{1,0:T(8,128)(2,1)S(1)}, u32[]{:S(2)}, u32[]{:S(2)}) collective-permute-start(bf16[8,12800]{1,0:T(8,128)(2,1)S(1)} %multiply_convert_fusion.4.refs_0_), channel_id=1, source_target_pairs={{0,4},{1,5},{2,6},{3,7},{4,0},{5,1},{6,2},{7,3},{8,12},{9,13},{10,... | collective-permute-start | bytes 614408 | tf_op jit(solution)/shard_map/ppermute | solution.py:238
  138.9 22.8 %collective-permute-start.32 = (bf16[8,12800]{1,0:T(8,128)(2,1)S(1)}, bf16[8,12800]{1,0:T(8,128)(2,1)S(1)}, u32[]{:S(2)}, u32[]{:S(2)}) collective-permute-start(bf16[8,12800]{1,0:T(8,128)(2,1)S(1)} %multiply_convert_fusion.4.refs_0_), channel_id=1, source_target_pairs={{0,2},{1,3},{2,4},{3,5},{4,6},{5,7},{6,0},{7,1},{8,10},{9,11},{10,... | collective-permute-start | bytes 614408 | tf_op jit(solution)/shard_map/ppermute | solution.py:238
  161.7 34.4 %collective-permute-start.39 = (bf16[32,12800]{1,0:T(8,128)(2,1)}, bf16[32,12800]{1,0:T(8,128)(2,1)S(1)}, u32[]{:S(2)}, u32[]{:S(2)}) collective-permute-start(bf16[32,12800]{1,0:T(8,128)(2,1)} %get-tuple-element.134), channel_id=1, source_target_pairs={{0,1},{1,0},{2,3},{3,2},{4,5},{5,4},{6,7},{7,6},{8,9},{9,8},{10,11... | collective-permute-start | bytes 2457608 | tf_op jit(solution)/shard_map/ppermute | solution.py:251
  161.8 10.6 %collective-permute-start.35 = (bf16[8,12800]{1,0:T(8,128)(2,1)S(1)}, bf16[8,12800]{1,0:T(8,128)(2,1)S(1)}, u32[]{:S(2)}, u32[]{:S(2)}) collective-permute-start(bf16[8,12800]{1,0:T(8,128)(2,1)S(1)} %multiply_convert_fusion.4.refs_0_), channel_id=1, source_target_pairs={{0,1},{1,0},{2,3},{3,2},{4,5},{5,4},{6,7},{7,6},{8,9},{9,8},{10,11... | collective-permute-start | bytes 614408 | tf_op jit(solution)/shard_map/ppermute | solution.py:244
  162.3 10.1 %collective-permute-start.36 = (bf16[8,12800]{1,0:T(8,128)(2,1)S(1)}, bf16[8,12800]{1,0:T(8,128)(2,1)S(1)}, u32[]{:S(2)}, u32[]{:S(2)}) collective-permute-start(bf16[8,12800]{1,0:T(8,128)(2,1)S(1)} %collective-permute-done.32.refs_1_), channel_id=1, source_target_pairs={{0,1},{1,0},{2,3},{3,2},{4,5},{5,4},{6,7},{7,6},{8,9},{9,8},{10,11... | collective-permute-start | bytes 614408 | tf_op jit(solution)/shard_map/ppermute | solution.py:244
  162.3 10.0 %collective-permute-start.37 = (bf16[8,12800]{1,0:T(8,128)(2,1)S(1)}, bf16[8,12800]{1,0:T(8,128)(2,1)}, u32[]{:S(2)}, u32[]{:S(2)}) collective-permute-start(bf16[8,12800]{1,0:T(8,128)(2,1)S(1)} %collective-permute-done.33.refs_2_), channel_id=1, source_target_pairs={{0,1},{1,0},{2,3},{3,2},{4,5},{5,4},{6,7},{7,6},{8,9},{9,8},{10,11... | collective-permute-start | bytes 614408 | tf_op jit(solution)/shard_map/ppermute | solution.py:244
  162.8 9.6 %collective-permute-start.38 = (bf16[8,12800]{1,0:T(8,128)(2,1)S(1)}, bf16[8,12800]{1,0:T(8,128)(2,1)}, u32[]{:S(2)}, u32[]{:S(2)}) collective-permute-start(bf16[8,12800]{1,0:T(8,128)(2,1)S(1)} %collective-permute-done.34.refs_3_), channel_id=1, source_target_pairs={{0,1},{1,0},{2,3},{3,2},{4,5},{5,4},{6,7},{7,6},{8,9},{9,8},{10,11... | collective-permute-start | bytes 614408 | tf_op jit(solution)/shard_map/ppermute | solution.py:244
  196.4 9.9 %collective-permute-start.42 = (bf16[8,12800]{1,0:T(8,128)(2,1)S(1)}, bf16[8,12800]{1,0:T(8,128)(2,1)S(1)}, u32[]{:S(2)}, u32[]{:S(2)}) collective-permute-start(bf16[8,12800]{1,0:T(8,128)(2,1)S(1)} %get-tuple-element.230), channel_id=1, source_target_pairs={{0,2},{1,3},{2,4},{3,5},{4,6},{5,7},{6,0},{7,1},{8,10},{9,11},{10,... | collective-permute-start | bytes 614408 | tf_op jit(solution)/shard_map/ppermute | solution.py:238
  199.1 15.4 %collective-permute-start.41 = (bf16[8,12800]{1,0:T(8,128)(2,1)S(1)}, bf16[8,12800]{1,0:T(8,128)(2,1)S(1)}, u32[]{:S(2)}, u32[]{:S(2)}) collective-permute-start(bf16[8,12800]{1,0:T(8,128)(2,1)S(1)} %get-tuple-element.231), channel_id=1, source_target_pairs={{0,4},{1,5},{2,6},{3,7},{4,0},{5,1},{6,2},{7,3},{8,12},{9,13},{10,... | collective-permute-start | bytes 614408 | tf_op jit(solution)/shard_map/ppermute | solution.py:238
  200.3 14.3 %collective-permute-start.40 = (bf16[8,12800]{1,0:T(8,128)(2,1)S(1)}, bf16[8,12800]{1,0:T(8,128)(2,1)S(1)}, u32[]{:S(2)}, u32[]{:S(2)}) collective-permute-start(bf16[8,12800]{1,0:T(8,128)(2,1)S(1)} %get-tuple-element.232), channel_id=1, source_target_pairs={{0,6},{1,7},{2,0},{3,1},{4,2},{5,3},{6,4},{7,5},{8,14},{9,15},{10,... | collective-permute-start | bytes 614408 | tf_op jit(solution)/shard_map/ppermute | solution.py:238
  201.6 20.4 %collective-permute-start.52 = (bf16[32,1024]{1,0:T(8,128)(2,1)S(1)}, bf16[32,1024]{1,0:T(8,128)(2,1)S(1)}, u32[]{:S(2)}, u32[]{:S(2)}) collective-permute-start(bf16[32,1024]{1,0:T(8,128)(2,1)S(1)} %get-tuple-element.243), channel_id=1, source_target_pairs={{0,24},{8,0},{16,8},{24,16},{1,25},{9,1},{17,9},{25,17},{2,26},{10... | collective-permute-start | bytes 196616 | tf_op jit(solution)/shard_map/ppermute | solution.py:367
  202.2 22.3 %collective-permute-start.51 = (bf16[32,1024]{1,0:T(8,128)(2,1)S(1)}, bf16[32,1024]{1,0:T(8,128)(2,1)S(1)}, u32[]{:S(2)}, u32[]{:S(2)}) collective-permute-start(bf16[32,1024]{1,0:T(8,128)(2,1)S(1)} %get-tuple-element.244), channel_id=1, source_target_pairs={{0,16},{8,24},{16,0},{24,8},{1,17},{9,25},{17,1},{25,9},{2,18},{10... | collective-permute-start | bytes 196616 | tf_op jit(solution)/shard_map/ppermute | solution.py:367
  206.2 18.8 %collective-permute-start.50 = (bf16[32,1024]{1,0:T(8,128)(2,1)S(1)}, bf16[32,1024]{1,0:T(8,128)(2,1)S(1)}, u32[]{:S(2)}, u32[]{:S(2)}) collective-permute-start(bf16[32,1024]{1,0:T(8,128)(2,1)S(1)} %get-tuple-element.245), channel_id=1, source_target_pairs={{0,8},{8,16},{16,24},{24,0},{1,9},{9,17},{17,25},{25,1},{2,10},{10... | collective-permute-start | bytes 196616 | tf_op jit(solution)/shard_map/ppermute | solution.py:367
  215.2 6.0 %collective-permute-start.46 = (bf16[32,12800]{1,0:T(8,128)(2,1)}, bf16[32,12800]{1,0:T(8,128)(2,1)S(1)}, u32[]{:S(2)}, u32[]{:S(2)}) collective-permute-start(bf16[32,12800]{1,0:T(8,128)(2,1)} %get-tuple-element.140), channel_id=1, source_target_pairs={{0,1},{1,0},{2,3},{3,2},{4,5},{5,4},{6,7},{7,6},{8,9},{9,8},{10,11... | collective-permute-start | bytes 2457608 | tf_op jit(solution)/shard_map/ppermute | solution.py:251
  215.3 11.3 %collective-permute-start.45 = (bf16[32,3200]{1,0:T(8,128)(2,1)S(1)}, bf16[32,3200]{1,0:T(8,128)(2,1)S(1)}, u32[]{:S(2)}, u32[]{:S(2)}) collective-permute-start(bf16[32,3200]{1,0:T(8,128)(2,1)S(1)} %multiply_convert_fusion.2.refs_0_), channel_id=1, source_target_pairs={{0,6},{1,7},{2,0},{3,1},{4,2},{5,3},{6,4},{7,5},{8,14},{9,15},{10,... | collective-permute-start | bytes 614408 | tf_op jit(solution)/shard_map/ppermute | solution.py:238
  221.2 28.5 %collective-permute-start.44 = (bf16[32,3200]{1,0:T(8,128)(2,1)S(1)}, bf16[32,3200]{1,0:T(8,128)(2,1)S(1)}, u32[]{:S(2)}, u32[]{:S(2)}) collective-permute-start(bf16[32,3200]{1,0:T(8,128)(2,1)S(1)} %multiply_convert_fusion.2.refs_0_), channel_id=1, source_target_pairs={{0,4},{1,5},{2,6},{3,7},{4,0},{5,1},{6,2},{7,3},{8,12},{9,13},{10,... | collective-permute-start | bytes 614408 | tf_op jit(solution)/shard_map/ppermute | solution.py:238
  222.1 27.6 %collective-permute-start.43 = (bf16[32,3200]{1,0:T(8,128)(2,1)S(1)}, bf16[32,3200]{1,0:T(8,128)(2,1)S(1)}, u32[]{:S(2)}, u32[]{:S(2)}) collective-permute-start(bf16[32,3200]{1,0:T(8,128)(2,1)S(1)} %multiply_convert_fusion.2.refs_0_), channel_id=1, source_target_pairs={{0,2},{1,3},{2,4},{3,5},{4,6},{5,7},{6,0},{7,1},{8,10},{9,11},{10,... | collective-permute-start | bytes 614408 | tf_op jit(solution)/shard_map/ppermute | solution.py:238
  224.5 25.1 %collective-permute-start.49 = (bf16[8,12800]{1,0:T(8,128)(2,1)S(1)}, bf16[8,12800]{1,0:T(8,128)(2,1)S(1)}, u32[]{:S(2)}, u32[]{:S(2)}) collective-permute-start(bf16[8,12800]{1,0:T(8,128)(2,1)S(1)} %get-tuple-element.227), channel_id=1, source_target_pairs={{0,2},{1,3},{2,4},{3,5},{4,6},{5,7},{6,0},{7,1},{8,10},{9,11},{10,... | collective-permute-start | bytes 614408 | tf_op jit(solution)/shard_map/ppermute | solution.py:238
  225.0 28.9 %collective-permute-start.48 = (bf16[8,12800]{1,0:T(8,128)(2,1)S(1)}, bf16[8,12800]{1,0:T(8,128)(2,1)S(1)}, u32[]{:S(2)}, u32[]{:S(2)}) collective-permute-start(bf16[8,12800]{1,0:T(8,128)(2,1)S(1)} %get-tuple-element.228), channel_id=1, source_target_pairs={{0,4},{1,5},{2,6},{3,7},{4,0},{5,1},{6,2},{7,3},{8,12},{9,13},{10,... | collective-permute-start | bytes 614408 | tf_op jit(solution)/shard_map/ppermute | solution.py:238
  226.6 29.1 %collective-permute-start.47 = (bf16[8,12800]{1,0:T(8,128)(2,1)S(1)}, bf16[8,12800]{1,0:T(8,128)(2,1)S(1)}, u32[]{:S(2)}, u32[]{:S(2)}) collective-permute-start(bf16[8,12800]{1,0:T(8,128)(2,1)S(1)} %get-tuple-element.229), channel_id=1, source_target_pairs={{0,6},{1,7},{2,0},{3,1},{4,2},{5,3},{6,4},{7,5},{8,14},{9,15},{10,... | collective-permute-start | bytes 614408 | tf_op jit(solution)/shard_map/ppermute | solution.py:238
  256.4 6.7 %collective-permute-start.53 = (bf16[32,3200]{1,0:T(8,128)(2,1)S(1)}, bf16[32,3200]{1,0:T(8,128)(2,1)S(1)}, u32[]{:S(2)}, u32[]{:S(2)}) collective-permute-start(bf16[32,3200]{1,0:T(8,128)(2,1)S(1)} %multiply_convert_fusion.2.refs_0_), channel_id=1, source_target_pairs={{0,1},{1,0},{2,3},{3,2},{4,5},{5,4},{6,7},{7,6},{8,9},{9,8},{10,11... | collective-permute-start | bytes 614408 | tf_op jit(solution)/shard_map/ppermute | solution.py:244
  256.5 6.7 %collective-permute-start.54 = (bf16[32,3200]{1,0:T(8,128)(2,1)S(1)}, bf16[32,3200]{1,0:T(8,128)(2,1)S(1)}, u32[]{:S(2)}, u32[]{:S(2)}) collective-permute-start(bf16[32,3200]{1,0:T(8,128)(2,1)S(1)} %collective-permute-done.43.refs_1_), channel_id=1, source_target_pairs={{0,1},{1,0},{2,3},{3,2},{4,5},{5,4},{6,7},{7,6},{8,9},{9,8},{10,11... | collective-permute-start | bytes 614408 | tf_op jit(solution)/shard_map/ppermute | solution.py:244
  257.0 7.1 %collective-permute-start.55 = (bf16[32,3200]{1,0:T(8,128)(2,1)}, bf16[32,3200]{1,0:T(8,128)(2,1)S(1)}, u32[]{:S(2)}, u32[]{:S(2)}) collective-permute-start(bf16[32,3200]{1,0:T(8,128)(2,1)} %copy-done.16), channel_id=1, source_target_pairs={{0,1},{1,0},{2,3},{3,2},{4,5},{5,4},{6,7},{7,6},{8,9},{9,8},{10,11... | collective-permute-start | bytes 614408 | tf_op jit(solution)/shard_map/ppermute | solution.py:244
  257.1 7.0 %collective-permute-start.56 = (bf16[32,3200]{1,0:T(8,128)(2,1)}, bf16[32,3200]{1,0:T(8,128)(2,1)S(1)}, u32[]{:S(2)}, u32[]{:S(2)}) collective-permute-start(bf16[32,3200]{1,0:T(8,128)(2,1)} %copy-done.15), channel_id=1, source_target_pairs={{0,1},{1,0},{2,3},{3,2},{4,5},{5,4},{6,7},{7,6},{8,9},{9,8},{10,11... | collective-permute-start | bytes 614408 | tf_op jit(solution)/shard_map/ppermute | solution.py:244
  257.5 24.9 %collective-permute-start.59 = (bf16[32,3200]{1,0:T(8,128)(2,1)S(1)}, bf16[32,3200]{1,0:T(8,128)(2,1)S(1)}, u32[]{:S(2)}, u32[]{:S(2)}) collective-permute-start(bf16[32,3200]{1,0:T(8,128)(2,1)S(1)} %multiply_convert_fusion.refs_0_), channel_id=1, source_target_pairs={{0,6},{1,7},{2,0},{3,1},{4,2},{5,3},{6,4},{7,5},{8,14},{9,15},{10,... | collective-permute-start | bytes 614408 | tf_op jit(solution)/shard_map/ppermute | solution.py:238
  263.1 19.3 %collective-permute-start.58 = (bf16[32,3200]{1,0:T(8,128)(2,1)S(1)}, bf16[32,3200]{1,0:T(8,128)(2,1)S(1)}, u32[]{:S(2)}, u32[]{:S(2)}) collective-permute-start(bf16[32,3200]{1,0:T(8,128)(2,1)S(1)} %multiply_convert_fusion.refs_0_), channel_id=1, source_target_pairs={{0,4},{1,5},{2,6},{3,7},{4,0},{5,1},{6,2},{7,3},{8,12},{9,13},{10,... | collective-permute-start | bytes 614408 | tf_op jit(solution)/shard_map/ppermute | solution.py:238
  263.2 19.3 %collective-permute-start.57 = (bf16[32,3200]{1,0:T(8,128)(2,1)S(1)}, bf16[32,3200]{1,0:T(8,128)(2,1)S(1)}, u32[]{:S(2)}, u32[]{:S(2)}) collective-permute-start(bf16[32,3200]{1,0:T(8,128)(2,1)S(1)} %multiply_convert_fusion.refs_0_), channel_id=1, source_target_pairs={{0,2},{1,3},{2,4},{3,5},{4,6},{5,7},{6,0},{7,1},{8,10},{9,11},{10,... | collective-permute-start | bytes 614408 | tf_op jit(solution)/shard_map/ppermute | solution.py:238
  282.6 6.9 %collective-permute-start.60 = (bf16[32,3200]{1,0:T(8,128)(2,1)S(1)}, bf16[32,3200]{1,0:T(8,128)(2,1)S(1)}, u32[]{:S(2)}, u32[]{:S(2)}) collective-permute-start(bf16[32,3200]{1,0:T(8,128)(2,1)S(1)} %multiply_convert_fusion.refs_0_), channel_id=1, source_target_pairs={{0,1},{1,0},{2,3},{3,2},{4,5},{5,4},{6,7},{7,6},{8,9},{9,8},{10,11... | collective-permute-start | bytes 614408 | tf_op jit(solution)/shard_map/ppermute | solution.py:244
  283.1 7.4 %collective-permute-start.61 = (bf16[32,3200]{1,0:T(8,128)(2,1)S(1)}, bf16[32,3200]{1,0:T(8,128)(2,1)S(1)}, u32[]{:S(2)}, u32[]{:S(2)}) collective-permute-start(bf16[32,3200]{1,0:T(8,128)(2,1)S(1)} %collective-permute-done.57.refs_1_), channel_id=1, source_target_pairs={{0,1},{1,0},{2,3},{3,2},{4,5},{5,4},{6,7},{7,6},{8,9},{9,8},{10,11... | collective-permute-start | bytes 614408 | tf_op jit(solution)/shard_map/ppermute | solution.py:244
  283.1 8.8 %collective-permute-start.62 = (bf16[32,3200]{1,0:T(8,128)(2,1)S(1)}, bf16[32,3200]{1,0:T(8,128)(2,1)S(1)}, u32[]{:S(2)}, u32[]{:S(2)}) collective-permute-start(bf16[32,3200]{1,0:T(8,128)(2,1)S(1)} %collective-permute-done.58.refs_2_), channel_id=1, source_target_pairs={{0,1},{1,0},{2,3},{3,2},{4,5},{5,4},{6,7},{7,6},{8,9},{9,8},{10,11... | collective-permute-start | bytes 614408 | tf_op jit(solution)/shard_map/ppermute | solution.py:244
  283.6 8.4 %collective-permute-start.63 = (bf16[32,3200]{1,0:T(8,128)(2,1)S(1)}, bf16[32,3200]{1,0:T(8,128)(2,1)S(1)}, u32[]{:S(2)}, u32[]{:S(2)}) collective-permute-start(bf16[32,3200]{1,0:T(8,128)(2,1)S(1)} %collective-permute-done.59.refs_3_), channel_id=1, source_target_pairs={{0,1},{1,0},{2,3},{3,2},{4,5},{5,4},{6,7},{7,6},{8,9},{9,8},{10,11... | collective-permute-start | bytes 614408 | tf_op jit(solution)/shard_map/ppermute | solution.py:244
  286.8 23.5 %collective-permute-start.67 = (bf16[32,3200]{1,0:T(8,128)(2,1)S(1)}, bf16[32,3200]{1,0:T(8,128)(2,1)S(1)}, u32[]{:S(2)}, u32[]{:S(2)}) collective-permute-start(bf16[32,3200]{1,0:T(8,128)(2,1)S(1)} %get-tuple-element.224), channel_id=1, source_target_pairs={{0,2},{1,3},{2,4},{3,5},{4,6},{5,7},{6,0},{7,1},{8,10},{9,11},{10,... | collective-permute-start | bytes 614408 | tf_op jit(solution)/shard_map/ppermute | solution.py:238
  289.5 20.8 %collective-permute-start.66 = (bf16[32,3200]{1,0:T(8,128)(2,1)S(1)}, bf16[32,3200]{1,0:T(8,128)(2,1)S(1)}, u32[]{:S(2)}, u32[]{:S(2)}) collective-permute-start(bf16[32,3200]{1,0:T(8,128)(2,1)S(1)} %get-tuple-element.225), channel_id=1, source_target_pairs={{0,4},{1,5},{2,6},{3,7},{4,0},{5,1},{6,2},{7,3},{8,12},{9,13},{10,... | collective-permute-start | bytes 614408 | tf_op jit(solution)/shard_map/ppermute | solution.py:238
  290.4 19.9 %collective-permute-start.65 = (bf16[32,3200]{1,0:T(8,128)(2,1)S(1)}, bf16[32,3200]{1,0:T(8,128)(2,1)S(1)}, u32[]{:S(2)}, u32[]{:S(2)}) collective-permute-start(bf16[32,3200]{1,0:T(8,128)(2,1)S(1)} %get-tuple-element.226), channel_id=1, source_target_pairs={{0,6},{1,7},{2,0},{3,1},{4,2},{5,3},{6,4},{7,5},{8,14},{9,15},{10,... | collective-permute-start | bytes 614408 | tf_op jit(solution)/shard_map/ppermute | solution.py:238
  315.1 10.4 %collective-permute-start.71 = (bf16[32,3200]{1,0:T(8,128)(2,1)}, bf16[32,3200]{1,0:T(8,128)(2,1)S(1)}, u32[]{:S(2)}, u32[]{:S(2)}) collective-permute-start(bf16[32,3200]{1,0:T(8,128)(2,1)} %get-tuple-element.221), channel_id=1, source_target_pairs={{0,2},{1,3},{2,4},{3,5},{4,6},{5,7},{6,0},{7,1},{8,10},{9,11},{10,... | collective-permute-start | bytes 614408 | tf_op jit(solution)/shard_map/ppermute | solution.py:238
  315.6 17.6 %collective-permute-start.70 = (bf16[32,3200]{1,0:T(8,128)(2,1)}, bf16[32,3200]{1,0:T(8,128)(2,1)}, u32[]{:S(2)}, u32[]{:S(2)}) collective-permute-start(bf16[32,3200]{1,0:T(8,128)(2,1)} %get-tuple-element.222), channel_id=1, source_target_pairs={{0,4},{1,5},{2,6},{3,7},{4,0},{5,1},{6,2},{7,3},{8,12},{9,13},{10,... | collective-permute-start | bytes 614408 | tf_op jit(solution)/shard_map/ppermute | solution.py:238
  317.6 15.7 %collective-permute-start.69 = (bf16[32,3200]{1,0:T(8,128)(2,1)}, bf16[32,3200]{1,0:T(8,128)(2,1)}, u32[]{:S(2)}, u32[]{:S(2)}) collective-permute-start(bf16[32,3200]{1,0:T(8,128)(2,1)} %get-tuple-element.223), channel_id=1, source_target_pairs={{0,6},{1,7},{2,0},{3,1},{4,2},{5,3},{6,4},{7,5},{8,14},{9,15},{10,... | collective-permute-start | bytes 614408 | tf_op jit(solution)/shard_map/ppermute | solution.py:238
  (85 other events, 860.3 us)

commit v6 on v5

--- a/solution.py
+++ b/solution.py
@@ -62,7 +62,8 @@
 def fetch(source, held, sems):
     count, rows = held.shape[:2]
     for j in range(count):
-        pltpu.make_async_copy(source.at[pl.ds(j * rows, rows)], held.at[j], sems.at[j]).start()
+        copy = pltpu.make_async_copy(source.at[pl.ds(j * rows, rows)], held.at[j], sems.at[j])
+        copy.start(priority=j % 2)
 
 
 def arrive(source, held, sems, j):
@@ -259,10 +260,10 @@
         return sum([t.astype(jnp.float32) for t in terms[1:]], terms[0])
 
     def by_rank(self, rows, size):
-        return jnp.take(rows.reshape(size, -1, rows.shape[-1]), self.blocks, axis=0)
+        return jnp.take(rows.reshape(size, -1, rows.shape[-1]), self.blocks, axis=0, mode="clip")
 
     def by_row(self, ranks):
-        return jnp.take(ranks, self.ranks, axis=0).reshape(-1, ranks.shape[-1])
+        return jnp.take(ranks, self.ranks, axis=0, mode="clip").reshape(-1, ranks.shape[-1])
 
 
 def per_device(
@@ -299,9 +300,6 @@
         inv.append(own_inv)
     tied = lax.optimization_barrier
     rail_b = moves.spread(normed[1])
-    normed[0], rail_b = tied((normed[0], rail_b))
-    rail_a = moves.spread(normed[0])
-    patches_b = moves.gathered(rail_b)
 
     starts = dest_row.reshape(groups, images, image_rows)[:, :, 0]
     start_pos = starts % seq_len
@@ -313,15 +311,19 @@
     from_group = (source[:, None] == jnp.arange(groups)).astype(jnp.int32)
     spot = jnp.sum(matches[:, None, :] * from_group[:, :, None] * start_pos[None], (1, 2))
 
-    picked = []
-    for s in range(groups):
-        block = lax.dynamic_slice_in_dim(cotangent, spot[s], image_rows, 0)
-        if s:
-            block = lax.ppermute(block, "grp", [(g, (g - s) % groups) for g in range(groups)])
-        picked.append(block)
+    span = jnp.arange(image_rows)
+    picked = jnp.take(cotangent, (spot[:, None] + span).reshape(-1), axis=0, mode="clip")
+    picked = [picked[s * image_rows : (s + 1) * image_rows] for s in range(groups)]
+    for s in range(1, groups):
+        pairs = [(g, (g - s) % groups) for g in range(groups)]
+        picked[s] = lax.ppermute(picked[s], "grp", pairs)
+
+    normed[0], rail_b, picked = tied((normed[0], rail_b, picked))
+    rail_a = moves.spread(normed[0])
+    patches_b = moves.gathered(rail_b)
 
     def grad_of(picked, c):
-        returned = jnp.take(jnp.stack(picked), shift, axis=0).reshape(size, -1, width)
+        returned = jnp.take(jnp.stack(picked), shift, axis=0, mode="clip").reshape(size, -1, width)
         return moves.by_row(returned[:, c * merged_rows : (c + 1) * merged_rows])
 
     def merge(c, summed):
@@ -354,27 +356,29 @@
     merged_a = moves.gathered(rail_a)
     terms_b = moves.send(near_b, far_b)
     projected_a, near_a, far_a = project(merged_a, proj_weight, grad_of(picked, 0))
-    near_a, far_a, terms_b = tied((near_a, far_a, terms_b))
+    near_a, far_a, terms_b, projected_a, projected_b = tied(
+        (near_a, far_a, terms_b, projected_a, projected_b)
+    )
     terms_a = moves.send(near_a, far_a)
 
     projected = jnp.concatenate(
         [moves.by_rank(projected_a, size), moves.by_rank(projected_b, size)], 1
     ).reshape(images, image_rows, width)
-    arrived = []
-    for s in range(groups):
-        block = lax.dynamic_index_in_dim(projected, image_of[s], 0, False)
-        if s:
-            block = lax.ppermute(block, "grp", [(g, (g + s) % groups) for g in range(groups)])
-        arrived.append(block)
+    chosen = jnp.take(projected, image_of, axis=0, mode="clip")
+    arrived = [chosen[s] for s in range(groups)]
+    for s in range(1, groups):
+        pairs = [(g, (g + s) % groups) for g in range(groups)]
+        arrived[s] = lax.ppermute(arrived[s], "grp", pairs)
 
     def embed(text, arrived):
-        for s in range(groups):
-            block = arrived[s]
-            if groups > images:
-                there = lax.dynamic_slice_in_dim(text, spot[s], image_rows, 0)
-                block = jnp.where(used[s], block, there)
-            text = lax.dynamic_update_slice_in_dim(text, block, spot[s], 0)
-        return text
+        goes_to = jnp.where(used[:, None], spot[:, None] + span, seq_len).reshape(-1)
+        picks = jnp.arange(seq_len)[:, None] == goes_to[None, :]
+        placed = jnp.dot(
+            picks.astype(jnp.bfloat16),
+            jnp.concatenate(arrived, 0),
+            preferred_element_type=jnp.float32,
+        ).astype(jnp.bfloat16)
+        return jnp.where(jnp.any(picks, 1, keepdims=True), placed, text)
 
     own_b, scaled_b = unmerge(moves.summed(terms_b), *stats_b)
     rail_b = moves.spread(scaled_b)
@@ -387,10 +391,10 @@
     grad_out_a = moves.gathered(rail_a)
     terms_b = moves.send(near_b, far_b)
     near_a, far_a = vision_pass(grad_out_a, late, early, slope_a)
-    near_a, far_a, terms_b, text = tied((near_a, far_a, terms_b, text_embed))
+    near_a, far_a, terms_b, arrived = tied((near_a, far_a, terms_b, arrived))
     terms_a = moves.send(near_a, far_a)
     normed_b = moves.summed(terms_b)
-    terms_a, seq_embed, normed_b = tied((terms_a, embed(text, arrived), normed_b))
+    terms_a, seq_embed, normed_b = tied((terms_a, embed(text_embed, arrived), normed_b))
     normed_a = moves.summed(terms_a)
     grads = [
         own_a + norm_back(normed_a, vis_gain, hat[0], inv[0]),

time: 338 us -> 300 us (0.89)
  between operations: 16.3 us -> 1.88 us
  starting transfers between devices: 79.3 us -> 68.5 us
  local copies, waits for them, and re-layouts: 24.5 us -> 14.1 us
  waiting for transfers between devices: 85.5 us -> 75.8 us
  Pallas kernels: 114 us -> 118 us
    ppermute x36, waiting for transfers between devices: 81 us -> 64.7 us  [shift(): return lax.ppermute(block, 'tp', pairs)]
    ppermute x36, starting transfers between devices: 65.2 us -> 51.6 us  [shift(): return lax.ppermute(block, 'tp', pairs)]
    dynamic_update_slice x4 -> x0, local copies, waits for them, and re-layouts: 6.42 us -> none  [embed(): text = lax.dynamic_update_slice_in_dim(text, block, spot[s], 0)]
    another operation x7, other arithmetic: 4.9 us -> 9.63 us
    ppermute x6, waiting for transfers between devices: 0.02 us -> 4.6 us  [the longest x3 4.59 us: per_device(): picked[s] = lax.ppermute(picked[s], 'grp', pairs)]
  transfers between devices with their start and end apart: 72 -> 72, of which waited for: 14 -> 21; matrix products, arithmetic and copies ran while one was open for 7% -> 7% of each run, Pallas kernels for 34% -> 39%
where the time goes in v6:
time: 300 us; the launch traced here: 299 us
  Pallas kernels  118 us (39%)
  waiting for transfers between devices  75.8 us (25%)
  starting transfers between devices  68.5 us (23%)
  other arithmetic  19.1 us (6%)
  local copies, waits for them, and re-layouts  14.1 us (5%)
    pallas_call x4, Pallas kernels, vision_pass(): pl.pallas_call(functools.partial(vision_kernel, len(pieces), slope is Non...  71.8 us
    ppermute x36, waiting for transfers between devices, shift(): return lax.ppermute(block, 'tp', pairs)  64.7 us
    ppermute x36, starting transfers between devices, shift(): return lax.ppermute(block, 'tp', pairs)  51.6 us
    pallas_call x2, Pallas kernels, project(): pl.pallas_call(functools.partial(project_kernel, len(pieces)), in_specs=w...  45.7 us
    another operation x7, other arithmetic  9.63 us
    ppermute x24, starting transfers between devices, gathered(): other = [lax.ppermute(m, 'tp', self.pairs) for m in mine]  6.47 us
  transfers between devices with their start and end apart: 72, of which 21 were waited for; matrix products, arithmetic and copies ran while one was open for 7% of the time, Pallas kernels for 39%

profile of v6, /device:TPU:0, one launch (start us, length us, event | category | flops | bytes accessed | tf_op | source)
XLA Modules:
  0.0 299.0 jit_solution(5241073349856243798)
XLA Ops:
  0.7 1.3 convert_reduce_fusion.1
  2.0 1.3 fusion.25
  3.3 1.2 fusion.19
  4.6 3.1 %collective-permute-start = (bf16[32,3200]{1,0:T(8,128)(2,1)S(1)}, bf16[32,3200]{1,0:T(8,128)(2,1)}, u32[]{:S(2)}, u32[]{:S(2)}) collective-permute-start(bf16[32,3200]{1,0:T(8,128)(2,1)S(1)} %get-tuple-element.99.refs_0_), channel_id=1, source_target_pairs={{0,2},{1,3},{2,4},{3,5},{4,6},{5,7},{6,0},{7,1},{8,10},{9,11},{10,... | collective-permute-start | bytes 614408 | tf_op jit(solution)/shard_map/ppermute | solution.py:239
  7.7 2.6 collective-permute-start.1
  10.3 1.3 collective-permute-start.2
  12.8 0.9 gather_fusion
  13.7 2.5 collective-permute-start.3
  16.7 1.4 collective-permute-done.3
  18.1 2.4 collective-permute-start.5
  21.1 2.5 collective-permute-done.5
  24.8 4.9 %collective-permute-start.10 = (bf16[32,3200]{1,0:T(8,128)(2,1)S(1)}, bf16[32,3200]{1,0:T(8,128)(2,1)S(1)}, u32[]{:S(2)}, u32[]{:S(2)}) collective-permute-start(bf16[32,3200]{1,0:T(8,128)(2,1)S(1)} %get-tuple-element.106.refs_0_), channel_id=1, source_target_pairs={{0,2},{1,3},{2,4},{3,5},{4,6},{5,7},{6,0},{7,1},{8,10},{9,11},{10,... | collective-permute-start | bytes 614408 | tf_op jit(solution)/shard_map/ppermute | solution.py:239
  29.7 1.6 collective-permute-start.11
  31.3 1.3 collective-permute-start.12
  33.4 18.3 %shard_map.113 = (bf16[128,3200]{1,0:T(8,128)(2,1)}, bf16[128,3200]{1,0:T(8,128)(2,1)}, f32[4,256,400]{2,1,0:T(8,128)}) custom-call(bf16[32,3200]{1,0:T(8,128)(2,1)} %copy-done.10, bf16[32,3200]{1,0:T(8,128)(2,1)} %collective-permute-done.refs_1_, bf16[32,3200]{1,0:T(8,128)(2,1)} %collective-permute-done.1.refs_2_, ...), custom_call_target="tpu_custom_call" | custom-call | flops 5242880000 | bytes 25395200 | tf_op jit(solution)/shard_map/pallas_call | solution.py:172
  53.1 1.4 collective-permute-done.17
  54.5 1.6 fusion.57
  56.2 1.5 collective-permute-start.18
  60.5 18.3 %shard_map.114 = (bf16[128,3200]{1,0:T(8,128)(2,1)}, bf16[128,3200]{1,0:T(8,128)(2,1)}, f32[4,256,400]{2,1,0:T(8,128)}) custom-call(bf16[32,3200]{1,0:T(8,128)(2,1)} %copy-done.8, bf16[32,3200]{1,0:T(8,128)(2,1)} %copy-done.16, bf16[32,3200]{1,0:T(8,128)(2,1)} %collective-permute-done.11.refs_2_, bf16[32,3200]{1,0:T(8,128)(2,1)} %collective-permute-done.12.refs_3_, ...), custom_call_target="tpu_custom_call" | custom-call | flops 5242880000 | bytes 25395200 | tf_op jit(solution)/shard_map/pallas_call | solution.py:172
  80.3 2.2 collective-permute-start.21
  82.5 1.6 collective-permute-start.22
  84.1 1.3 collective-permute-start.23
  86.1 2.8 fusion.58
  88.9 1.5 collective-permute-start.25
  91.8 1.2 gather_fusion.2
  93.0 1.0 slice.196
  94.1 4.6 %collective-permute-done.22.refs_2_ = bf16[8,12800]{1,0:T(8,128)(2,1)} collective-permute-done((bf16[8,12800]{1,0:T(8,128)(2,1)S(1)}, bf16[8,12800]{1,0:T(8,128)(2,1)}, u32[]{:S(2)}, u32[]{:S(2)}) %collective-permute-start.22) | collective-permute-done | bytes 204832 | tf_op jit(solution)/shard_map/ppermute | solution.py:239
  98.7 4.1 %collective-permute-done.25 = bf16[32,3200]{1,0:T(8,128)(2,1)S(1)} collective-permute-done((bf16[32,3200]{1,0:T(8,128)(2,1)S(1)}, bf16[32,3200]{1,0:T(8,128)(2,1)S(1)}, u32[]{:S(2)}, u32[]{:S(2)}) %collective-permute-start.25) | collective-permute-done | bytes 204832 | tf_op jit(solution)/shard_map/ppermute | solution.py:239
  102.8 17.6 %collective-permute-done.26 = bf16[32,3200]{1,0:T(8,128)(2,1)S(1)} collective-permute-done((bf16[32,3200]{1,0:T(8,128)(2,1)S(1)}, bf16[32,3200]{1,0:T(8,128)(2,1)S(1)}, u32[]{:S(2)}, u32[]{:S(2)}) %collective-permute-start.26) | collective-permute-done | bytes 204832 | tf_op jit(solution)/shard_map/ppermute | solution.py:239
  123.6 3.2 %collective-permute-start.34 = (bf16[8,12800]{1,0:T(8,128)(2,1)S(1)}, bf16[8,12800]{1,0:T(8,128)(2,1)S(1)}, u32[]{:S(2)}, u32[]{:S(2)}) collective-permute-start(bf16[8,12800]{1,0:T(8,128)(2,1)S(1)} %multiply_convert_fusion.4.refs_0_), channel_id=1, source_target_pairs={{0,6},{1,7},{2,0},{3,1},{4,2},{5,3},{6,4},{7,5},{8,14},{9,15},{10,... | collective-permute-start | bytes 614408 | tf_op jit(solution)/shard_map/ppermute | solution.py:239
  127.6 22.9 %shard_map.115 = (bf16[64,1024]{1,0:T(8,128)(2,1)}, bf16[32,12800]{1,0:T(8,128)(2,1)}, bf16[32,12800]{1,0:T(8,128)(2,1)}) custom-call(bf16[8,12800]{1,0:T(8,128)(2,1)} %copy-done.12, bf16[8,12800]{1,0:T(8,128)(2,1)} %copy-done.17, bf16[8,12800]{1,0:T(8,128)(2,1)} %collective-permute-done.22.refs_2_, bf16[8,12800]{1,0:T(8,128)(2,1)} %collective-permute-done.23.refs_3_, ...), custom_call_target="tpu_custom_call" | custom-call | flops 3355443200 | bytes 29753344 | tf_op jit(solution)/shard_map/pallas_call | solution.py:202
  150.6 1.2 gather_fusion.3
  153.3 1.6 fusion.59
  154.9 0.8 collective-permute-start.40
  155.7 1.3 collective-permute-start.41
  157.0 1.9 collective-permute-start.42
  159.7 22.9 %shard_map.116 = (bf16[64,1024]{1,0:T(8,128)(2,1)}, bf16[32,12800]{1,0:T(8,128)(2,1)}, bf16[32,12800]{1,0:T(8,128)(2,1)}) custom-call(bf16[8,12800]{1,0:T(8,128)(2,1)} %copy-done.13, bf16[8,12800]{1,0:T(8,128)(2,1)} %copy-done.18, bf16[8,12800]{1,0:T(8,128)(2,1)} %copy-done.21, bf16[8,12800]{1,0:T(8,128)(2,1)} %copy-done.22, bf16[8,12800]{1,0:T(8,128)(2,1)} %copy-done.24, ...), custom_call_target="tpu_custom_call" | custom-call | flops 3355443200 | bytes 29753344 | tf_op jit(solution)/shard_map/pallas_call | solution.py:202
  183.8 2.2 collective-permute-start.44
  187.7 1.5 collective-permute-start.50
  189.3 1.5 collective-permute-start.51
  190.8 1.4 collective-permute-start.52
  192.3 1.6 fusion.60
  193.9 1.5 collective-permute-start.45
  196.1 1.3 collective-permute-start.48
  197.5 1.9 collective-permute-start.49
  199.4 2.1 collective-permute-done.44.refs_2_
  201.5 3.7 %collective-permute-done.45.refs_3_ = bf16[32,3200]{1,0:T(8,128)(2,1)S(1)} collective-permute-done((bf16[32,3200]{1,0:T(8,128)(2,1)S(1)}, bf16[32,3200]{1,0:T(8,128)(2,1)S(1)}, u32[]{:S(2)}, u32[]{:S(2)}) %collective-permute-start.45) | collective-permute-done | bytes 204832 | tf_op jit(solution)/shard_map/ppermute | solution.py:239
  205.2 2.9 collective-permute-done.47
  208.1 14.7 %collective-permute-done.48 = bf16[8,12800]{1,0:T(8,128)(2,1)S(1)} collective-permute-done((bf16[8,12800]{1,0:T(8,128)(2,1)S(1)}, bf16[8,12800]{1,0:T(8,128)(2,1)S(1)}, u32[]{:S(2)}, u32[]{:S(2)}) %collective-permute-start.48) | collective-permute-done | bytes 204832 | tf_op jit(solution)/shard_map/ppermute | solution.py:239
  225.2 3.3 %collective-permute-start.59 = (bf16[32,3200]{1,0:T(8,128)(2,1)S(1)}, bf16[32,3200]{1,0:T(8,128)(2,1)S(1)}, u32[]{:S(2)}, u32[]{:S(2)}) collective-permute-start(bf16[32,3200]{1,0:T(8,128)(2,1)S(1)} %multiply_convert_fusion.refs_0_), channel_id=1, source_target_pairs={{0,6},{1,7},{2,0},{3,1},{4,2},{5,3},{6,4},{7,5},{8,14},{9,15},{10,... | collective-permute-start | bytes 614408 | tf_op jit(solution)/shard_map/ppermute | solution.py:239
  229.3 17.6 %shard_map.117 = (bf16[128,3200]{1,0:T(8,128)(2,1)}, bf16[128,3200]{1,0:T(8,128)(2,1)}) custom-call(bf16[32,3200]{1,0:T(8,128)(2,1)} %copy-done.9, bf16[32,3200]{1,0:T(8,128)(2,1)} %copy-done.15, bf16[32,3200]{1,0:T(8,128)(2,1)} %collective-permute-done.44.refs_2_, bf16[32,3200]{1,0:T(8,128)(2,1)} %copy-done.19, bf16[32,3200]{1,0:T(8,128)(2,1)} %copy-done.37, ...), custom_call_target="tpu_custom_call" | custom-call | flops 5242880000 | bytes 25395200 | tf_op jit(solution)/shard_map/pallas_call | solution.py:172
  248.5 1.2 collective-permute-done.64
  249.7 1.6 fusion.61
  251.3 0.9 collective-permute-start.65
  252.2 1.2 collective-permute-start.66
  253.4 1.9 collective-permute-start.67
  256.1 17.5 %shard_map.118 = (bf16[128,3200]{1,0:T(8,128)(2,1)}, bf16[128,3200]{1,0:T(8,128)(2,1)}) custom-call(bf16[32,3200]{1,0:T(8,128)(2,1)} %copy-done.11, bf16[32,3200]{1,0:T(8,128)(2,1)} %collective-permute-done.57.refs_1_, bf16[32,3200]{1,0:T(8,128)(2,1)} %collective-permute-done.58.refs_2_, bf16[32,3200]{1,0:T(8,128)(2,1)} %copy-done.23, ...), custom_call_target="tpu_custom_call" | custom-call | flops 5242880000 | bytes 25395200 | tf_op jit(solution)/shard_map/pallas_call | solution.py:172
  274.0 2.4 collective-permute-done.68
  276.6 1.9 collective-permute-start.69
  278.6 1.1 collective-permute-start.71
  279.7 2.2 fusion
  281.9 2.5 collective-permute-done.69
  284.4 12.4 %collective-permute-done.70 = bf16[32,3200]{1,0:T(8,128)(2,1)S(1)} collective-permute-done((bf16[32,3200]{1,0:T(8,128)(2,1)S(1)}, bf16[32,3200]{1,0:T(8,128)(2,1)S(1)}, u32[]{:S(2)}, u32[]{:S(2)}) %collective-permute-start.70) | collective-permute-done | bytes 204832 | tf_op jit(solution)/shard_map/ppermute | solution.py:239
  297.6 0.8 pad_maximum_fusion
  (311 shorter events, 29.1 us)
Async XLA Ops:
  4.6 19.1 %collective-permute-start = (bf16[32,3200]{1,0:T(8,128)(2,1)S(1)}, bf16[32,3200]{1,0:T(8,128)(2,1)}, u32[]{:S(2)}, u32[]{:S(2)}) collective-permute-start(bf16[32,3200]{1,0:T(8,128)(2,1)S(1)} %get-tuple-element.99.refs_0_), channel_id=1, source_target_pairs={{0,2},{1,3},{2,4},{3,5},{4,6},{5,7},{6,0},{7,1},{8,10},{9,11},{10,... | collective-permute-start | bytes 614408 | tf_op jit(solution)/shard_map/ppermute | solution.py:239
  7.7 16.1 %collective-permute-start.1 = (bf16[32,3200]{1,0:T(8,128)(2,1)S(1)}, bf16[32,3200]{1,0:T(8,128)(2,1)}, u32[]{:S(2)}, u32[]{:S(2)}) collective-permute-start(bf16[32,3200]{1,0:T(8,128)(2,1)S(1)} %get-tuple-element.99.refs_0_), channel_id=1, source_target_pairs={{0,4},{1,5},{2,6},{3,7},{4,0},{5,1},{6,2},{7,3},{8,12},{9,13},{10,... | collective-permute-start | bytes 614408 | tf_op jit(solution)/shard_map/ppermute | solution.py:239
  10.3 13.5 %collective-permute-start.2 = (bf16[32,3200]{1,0:T(8,128)(2,1)S(1)}, bf16[32,3200]{1,0:T(8,128)(2,1)}, u32[]{:S(2)}, u32[]{:S(2)}) collective-permute-start(bf16[32,3200]{1,0:T(8,128)(2,1)S(1)} %get-tuple-element.99.refs_0_), channel_id=1, source_target_pairs={{0,6},{1,7},{2,0},{3,1},{4,2},{5,3},{6,4},{7,5},{8,14},{9,15},{10,... | collective-permute-start | bytes 614408 | tf_op jit(solution)/shard_map/ppermute | solution.py:239
  13.7 4.4 %collective-permute-start.3 = (bf16[32,1024]{1,0:T(8,128)(2,1)S(1)}, bf16[32,1024]{1,0:T(8,128)(2,1)S(1)}, u32[]{:S(2)}, u32[]{:S(2)}) collective-permute-start(bf16[32,1024]{1,0:T(8,128)(2,1)S(1)} %get-tuple-element.259), channel_id=1, source_target_pairs={{0,24},{8,0},{16,8},{24,16},{1,25},{9,1},{17,9},{25,17},{2,26},{10... | collective-permute-start | bytes 196616 | tf_op jit(solution)/shard_map/ppermute | solution.py:319
  16.2 5.0 %collective-permute-start.4 = (bf16[32,1024]{1,0:T(8,128)(2,1)S(1)}, bf16[32,1024]{1,0:T(8,128)(2,1)S(1)}, u32[]{:S(2)}, u32[]{:S(2)}) collective-permute-start(bf16[32,1024]{1,0:T(8,128)(2,1)S(1)} %get-tuple-element.258), channel_id=1, source_target_pairs={{0,16},{8,24},{16,0},{24,8},{1,17},{9,25},{17,1},{25,9},{2,18},{10... | collective-permute-start | bytes 196616 | tf_op jit(solution)/shard_map/ppermute | solution.py:319
  18.1 5.6 %collective-permute-start.5 = (bf16[32,1024]{1,0:T(8,128)(2,1)S(1)}, bf16[32,1024]{1,0:T(8,128)(2,1)S(1)}, u32[]{:S(2)}, u32[]{:S(2)}) collective-permute-start(bf16[32,1024]{1,0:T(8,128)(2,1)S(1)} %get-tuple-element.257), channel_id=1, source_target_pairs={{0,8},{8,16},{16,24},{24,0},{1,9},{9,17},{17,25},{25,1},{2,10},{10... | collective-permute-start | bytes 196616 | tf_op jit(solution)/shard_map/ppermute | solution.py:319
  23.8 5.9 %collective-permute-start.6 = (bf16[32,3200]{1,0:T(8,128)(2,1)S(1)}, bf16[32,3200]{1,0:T(8,128)(2,1)S(1)}, u32[]{:S(2)}, u32[]{:S(2)}) collective-permute-start(bf16[32,3200]{1,0:T(8,128)(2,1)S(1)} %get-tuple-element.99.refs_0_), channel_id=1, source_target_pairs={{0,1},{1,0},{2,3},{3,2},{4,5},{5,4},{6,7},{7,6},{8,9},{9,8},{10,11... | collective-permute-start | bytes 614408 | tf_op jit(solution)/shard_map/ppermute | solution.py:245
  23.8 7.5 %collective-permute-start.7 = (bf16[32,3200]{1,0:T(8,128)(2,1)}, bf16[32,3200]{1,0:T(8,128)(2,1)S(1)}, u32[]{:S(2)}, u32[]{:S(2)}) collective-permute-start(bf16[32,3200]{1,0:T(8,128)(2,1)} %collective-permute-done.refs_1_), channel_id=1, source_target_pairs={{0,1},{1,0},{2,3},{3,2},{4,5},{5,4},{6,7},{7,6},{8,9},{9,8},{10,11... | collective-permute-start | bytes 614408 | tf_op jit(solution)/shard_map/ppermute | solution.py:245
  24.3 8.3 %collective-permute-start.8 = (bf16[32,3200]{1,0:T(8,128)(2,1)}, bf16[32,3200]{1,0:T(8,128)(2,1)S(1)}, u32[]{:S(2)}, u32[]{:S(2)}) collective-permute-start(bf16[32,3200]{1,0:T(8,128)(2,1)} %collective-permute-done.1.refs_2_), channel_id=1, source_target_pairs={{0,1},{1,0},{2,3},{3,2},{4,5},{5,4},{6,7},{7,6},{8,9},{9,8},{10,11... | collective-permute-start | bytes 614408 | tf_op jit(solution)/shard_map/ppermute | solution.py:245
  24.4 8.2 %collective-permute-start.9 = (bf16[32,3200]{1,0:T(8,128)(2,1)}, bf16[32,3200]{1,0:T(8,128)(2,1)S(1)}, u32[]{:S(2)}, u32[]{:S(2)}) collective-permute-start(bf16[32,3200]{1,0:T(8,128)(2,1)} %collective-permute-done.2.refs_3_), channel_id=1, source_target_pairs={{0,1},{1,0},{2,3},{3,2},{4,5},{5,4},{6,7},{7,6},{8,9},{9,8},{10,11... | collective-permute-start | bytes 614408 | tf_op jit(solution)/shard_map/ppermute | solution.py:245
  24.8 26.9 %collective-permute-start.10 = (bf16[32,3200]{1,0:T(8,128)(2,1)S(1)}, bf16[32,3200]{1,0:T(8,128)(2,1)S(1)}, u32[]{:S(2)}, u32[]{:S(2)}) collective-permute-start(bf16[32,3200]{1,0:T(8,128)(2,1)S(1)} %get-tuple-element.106.refs_0_), channel_id=1, source_target_pairs={{0,2},{1,3},{2,4},{3,5},{4,6},{5,7},{6,0},{7,1},{8,10},{9,11},{10,... | collective-permute-start | bytes 614408 | tf_op jit(solution)/shard_map/ppermute | solution.py:239
  29.7 22.1 %collective-permute-start.11 = (bf16[32,3200]{1,0:T(8,128)(2,1)S(1)}, bf16[32,3200]{1,0:T(8,128)(2,1)}, u32[]{:S(2)}, u32[]{:S(2)}) collective-permute-start(bf16[32,3200]{1,0:T(8,128)(2,1)S(1)} %get-tuple-element.106.refs_0_), channel_id=1, source_target_pairs={{0,4},{1,5},{2,6},{3,7},{4,0},{5,1},{6,2},{7,3},{8,12},{9,13},{10,... | collective-permute-start | bytes 614408 | tf_op jit(solution)/shard_map/ppermute | solution.py:239
  31.3 20.5 %collective-permute-start.12 = (bf16[32,3200]{1,0:T(8,128)(2,1)S(1)}, bf16[32,3200]{1,0:T(8,128)(2,1)}, u32[]{:S(2)}, u32[]{:S(2)}) collective-permute-start(bf16[32,3200]{1,0:T(8,128)(2,1)S(1)} %get-tuple-element.106.refs_0_), channel_id=1, source_target_pairs={{0,6},{1,7},{2,0},{3,1},{4,2},{5,3},{6,4},{7,5},{8,14},{9,15},{10,... | collective-permute-start | bytes 614408 | tf_op jit(solution)/shard_map/ppermute | solution.py:239
  52.0 5.7 %collective-permute-start.13 = (bf16[32,3200]{1,0:T(8,128)(2,1)S(1)}, bf16[32,3200]{1,0:T(8,128)(2,1)S(1)}, u32[]{:S(2)}, u32[]{:S(2)}) collective-permute-start(bf16[32,3200]{1,0:T(8,128)(2,1)S(1)} %get-tuple-element.106.refs_0_), channel_id=1, source_target_pairs={{0,1},{1,0},{2,3},{3,2},{4,5},{5,4},{6,7},{7,6},{8,9},{9,8},{10,11... | collective-permute-start | bytes 614408 | tf_op jit(solution)/shard_map/ppermute | solution.py:245
  52.5 5.9 %collective-permute-start.14 = (bf16[32,3200]{1,0:T(8,128)(2,1)S(1)}, bf16[32,3200]{1,0:T(8,128)(2,1)S(1)}, u32[]{:S(2)}, u32[]{:S(2)}) collective-permute-start(bf16[32,3200]{1,0:T(8,128)(2,1)S(1)} %collective-permute-done.10.refs_1_), channel_id=1, source_target_pairs={{0,1},{1,0},{2,3},{3,2},{4,5},{5,4},{6,7},{7,6},{8,9},{9,8},{10,11... | collective-permute-start | bytes 614408 | tf_op jit(solution)/shard_map/ppermute | solution.py:245
  52.6 6.5 %collective-permute-start.15 = (bf16[32,3200]{1,0:T(8,128)(2,1)}, bf16[32,3200]{1,0:T(8,128)(2,1)S(1)}, u32[]{:S(2)}, u32[]{:S(2)}) collective-permute-start(bf16[32,3200]{1,0:T(8,128)(2,1)} %collective-permute-done.11.refs_2_), channel_id=1, source_target_pairs={{0,1},{1,0},{2,3},{3,2},{4,5},{5,4},{6,7},{7,6},{8,9},{9,8},{10,11... | collective-permute-start | bytes 614408 | tf_op jit(solution)/shard_map/ppermute | solution.py:245
  53.0 6.1 %collective-permute-start.16 = (bf16[32,3200]{1,0:T(8,128)(2,1)}, bf16[32,3200]{1,0:T(8,128)(2,1)S(1)}, u32[]{:S(2)}, u32[]{:S(2)}) collective-permute-start(bf16[32,3200]{1,0:T(8,128)(2,1)} %collective-permute-done.12.refs_3_), channel_id=1, source_target_pairs={{0,1},{1,0},{2,3},{3,2},{4,5},{5,4},{6,7},{7,6},{8,9},{9,8},{10,11... | collective-permute-start | bytes 614408 | tf_op jit(solution)/shard_map/ppermute | solution.py:245
  56.2 22.7 %collective-permute-start.18 = (bf16[32,3200]{1,0:T(8,128)(2,1)S(1)}, bf16[32,3200]{1,0:T(8,128)(2,1)S(1)}, u32[]{:S(2)}, u32[]{:S(2)}) collective-permute-start(bf16[32,3200]{1,0:T(8,128)(2,1)S(1)} %get-tuple-element.246), channel_id=1, source_target_pairs={{0,6},{1,7},{2,0},{3,1},{4,2},{5,3},{6,4},{7,5},{8,14},{9,15},{10,... | collective-permute-start | bytes 614408 | tf_op jit(solution)/shard_map/ppermute | solution.py:239
  57.7 21.2 %collective-permute-start.19 = (bf16[32,3200]{1,0:T(8,128)(2,1)S(1)}, bf16[32,3200]{1,0:T(8,128)(2,1)S(1)}, u32[]{:S(2)}, u32[]{:S(2)}) collective-permute-start(bf16[32,3200]{1,0:T(8,128)(2,1)S(1)} %get-tuple-element.245), channel_id=1, source_target_pairs={{0,4},{1,5},{2,6},{3,7},{4,0},{5,1},{6,2},{7,3},{8,12},{9,13},{10,... | collective-permute-start | bytes 614408 | tf_op jit(solution)/shard_map/ppermute | solution.py:239
  58.4 20.5 %collective-permute-start.20 = (bf16[32,3200]{1,0:T(8,128)(2,1)S(1)}, bf16[32,3200]{1,0:T(8,128)(2,1)S(1)}, u32[]{:S(2)}, u32[]{:S(2)}) collective-permute-start(bf16[32,3200]{1,0:T(8,128)(2,1)S(1)} %get-tuple-element.244), channel_id=1, source_target_pairs={{0,2},{1,3},{2,4},{3,5},{4,6},{5,7},{6,0},{7,1},{8,10},{9,11},{10,... | collective-permute-start | bytes 614408 | tf_op jit(solution)/shard_map/ppermute | solution.py:239
  79.0 7.1 %collective-permute-start.24 = (bf16[128,3200]{1,0:T(8,128)(2,1)}, bf16[128,3200]{1,0:T(8,128)(2,1)}, u32[]{:S(2)}, u32[]{:S(2)}) collective-permute-start(bf16[128,3200]{1,0:T(8,128)(2,1)} %get-tuple-element.123), channel_id=1, source_target_pairs={{0,1},{1,0},{2,3},{3,2},{4,5},{5,4},{6,7},{7,6},{8,9},{9,8},{10,11... | collective-permute-start | bytes 2457608 | tf_op jit(solution)/shard_map/ppermute | solution.py:252
  80.3 10.8 %collective-permute-start.21 = (bf16[8,12800]{1,0:T(8,128)(2,1)S(1)}, bf16[8,12800]{1,0:T(8,128)(2,1)S(1)}, u32[]{:S(2)}, u32[]{:S(2)}) collective-permute-start(bf16[8,12800]{1,0:T(8,128)(2,1)S(1)} %multiply_convert_fusion.5.refs_0_), channel_id=1, source_target_pairs={{0,2},{1,3},{2,4},{3,5},{4,6},{5,7},{6,0},{7,1},{8,10},{9,11},{10,... | collective-permute-start | bytes 614408 | tf_op jit(solution)/shard_map/ppermute | solution.py:239
  82.5 16.2 %collective-permute-start.22 = (bf16[8,12800]{1,0:T(8,128)(2,1)S(1)}, bf16[8,12800]{1,0:T(8,128)(2,1)}, u32[]{:S(2)}, u32[]{:S(2)}) collective-permute-start(bf16[8,12800]{1,0:T(8,128)(2,1)S(1)} %multiply_convert_fusion.5.refs_0_), channel_id=1, source_target_pairs={{0,4},{1,5},{2,6},{3,7},{4,0},{5,1},{6,2},{7,3},{8,12},{9,13},{10,... | collective-permute-start | bytes 614408 | tf_op jit(solution)/shard_map/ppermute | solution.py:239
  84.1 14.6 %collective-permute-start.23 = (bf16[8,12800]{1,0:T(8,128)(2,1)S(1)}, bf16[8,12800]{1,0:T(8,128)(2,1)}, u32[]{:S(2)}, u32[]{:S(2)}) collective-permute-start(bf16[8,12800]{1,0:T(8,128)(2,1)S(1)} %multiply_convert_fusion.5.refs_0_), channel_id=1, source_target_pairs={{0,6},{1,7},{2,0},{3,1},{4,2},{5,3},{6,4},{7,5},{8,14},{9,15},{10,... | collective-permute-start | bytes 614408 | tf_op jit(solution)/shard_map/ppermute | solution.py:239
  88.9 13.9 %collective-permute-start.25 = (bf16[32,3200]{1,0:T(8,128)(2,1)S(1)}, bf16[32,3200]{1,0:T(8,128)(2,1)S(1)}, u32[]{:S(2)}, u32[]{:S(2)}) collective-permute-start(bf16[32,3200]{1,0:T(8,128)(2,1)S(1)} %get-tuple-element.243), channel_id=1, source_target_pairs={{0,6},{1,7},{2,0},{3,1},{4,2},{5,3},{6,4},{7,5},{8,14},{9,15},{10,... | collective-permute-start | bytes 614408 | tf_op jit(solution)/shard_map/ppermute | solution.py:239
  90.4 30.0 %collective-permute-start.26 = (bf16[32,3200]{1,0:T(8,128)(2,1)S(1)}, bf16[32,3200]{1,0:T(8,128)(2,1)S(1)}, u32[]{:S(2)}, u32[]{:S(2)}) collective-permute-start(bf16[32,3200]{1,0:T(8,128)(2,1)S(1)} %get-tuple-element.242), channel_id=1, source_target_pairs={{0,4},{1,5},{2,6},{3,7},{4,0},{5,1},{6,2},{7,3},{8,12},{9,13},{10,... | collective-permute-start | bytes 614408 | tf_op jit(solution)/shard_map/ppermute | solution.py:239
  91.1 29.4 %collective-permute-start.27 = (bf16[32,3200]{1,0:T(8,128)(2,1)S(1)}, bf16[32,3200]{1,0:T(8,128)(2,1)S(1)}, u32[]{:S(2)}, u32[]{:S(2)}) collective-permute-start(bf16[32,3200]{1,0:T(8,128)(2,1)S(1)} %get-tuple-element.241), channel_id=1, source_target_pairs={{0,2},{1,3},{2,4},{3,5},{4,6},{5,7},{6,0},{7,1},{8,10},{9,11},{10,... | collective-permute-start | bytes 614408 | tf_op jit(solution)/shard_map/ppermute | solution.py:239
  122.2 4.6 %collective-permute-start.30 = (bf16[8,12800]{1,0:T(8,128)(2,1)}, bf16[8,12800]{1,0:T(8,128)(2,1)S(1)}, u32[]{:S(2)}, u32[]{:S(2)}) collective-permute-start(bf16[8,12800]{1,0:T(8,128)(2,1)} %collective-permute-done.22.refs_2_), channel_id=1, source_target_pairs={{0,1},{1,0},{2,3},{3,2},{4,5},{5,4},{6,7},{7,6},{8,9},{9,8},{10,11... | collective-permute-start | bytes 614408 | tf_op jit(solution)/shard_map/ppermute | solution.py:245
  122.3 4.5 %collective-permute-start.31 = (bf16[8,12800]{1,0:T(8,128)(2,1)}, bf16[8,12800]{1,0:T(8,128)(2,1)S(1)}, u32[]{:S(2)}, u32[]{:S(2)}) collective-permute-start(bf16[8,12800]{1,0:T(8,128)(2,1)} %collective-permute-done.23.refs_3_), channel_id=1, source_target_pairs={{0,1},{1,0},{2,3},{3,2},{4,5},{5,4},{6,7},{7,6},{8,9},{9,8},{10,11... | collective-permute-start | bytes 614408 | tf_op jit(solution)/shard_map/ppermute | solution.py:245
  122.8 27.6 %collective-permute-start.32 = (bf16[8,12800]{1,0:T(8,128)(2,1)S(1)}, bf16[8,12800]{1,0:T(8,128)(2,1)S(1)}, u32[]{:S(2)}, u32[]{:S(2)}) collective-permute-start(bf16[8,12800]{1,0:T(8,128)(2,1)S(1)} %multiply_convert_fusion.4.refs_0_), channel_id=1, source_target_pairs={{0,2},{1,3},{2,4},{3,5},{4,6},{5,7},{6,0},{7,1},{8,10},{9,11},{10,... | collective-permute-start | bytes 614408 | tf_op jit(solution)/shard_map/ppermute | solution.py:239
  123.1 27.3 %collective-permute-start.33 = (bf16[8,12800]{1,0:T(8,128)(2,1)S(1)}, bf16[8,12800]{1,0:T(8,128)(2,1)S(1)}, u32[]{:S(2)}, u32[]{:S(2)}) collective-permute-start(bf16[8,12800]{1,0:T(8,128)(2,1)S(1)} %multiply_convert_fusion.4.refs_0_), channel_id=1, source_target_pairs={{0,4},{1,5},{2,6},{3,7},{4,0},{5,1},{6,2},{7,3},{8,12},{9,13},{10,... | collective-permute-start | bytes 614408 | tf_op jit(solution)/shard_map/ppermute | solution.py:239
  123.6 26.9 %collective-permute-start.34 = (bf16[8,12800]{1,0:T(8,128)(2,1)S(1)}, bf16[8,12800]{1,0:T(8,128)(2,1)S(1)}, u32[]{:S(2)}, u32[]{:S(2)}) collective-permute-start(bf16[8,12800]{1,0:T(8,128)(2,1)S(1)} %multiply_convert_fusion.4.refs_0_), channel_id=1, source_target_pairs={{0,6},{1,7},{2,0},{3,1},{4,2},{5,3},{6,4},{7,5},{8,14},{9,15},{10,... | collective-permute-start | bytes 614408 | tf_op jit(solution)/shard_map/ppermute | solution.py:239
  151.9 3.8 %collective-permute-start.35 = (bf16[8,12800]{1,0:T(8,128)(2,1)S(1)}, bf16[8,12800]{1,0:T(8,128)(2,1)S(1)}, u32[]{:S(2)}, u32[]{:S(2)}) collective-permute-start(bf16[8,12800]{1,0:T(8,128)(2,1)S(1)} %multiply_convert_fusion.4.refs_0_), channel_id=1, source_target_pairs={{0,1},{1,0},{2,3},{3,2},{4,5},{5,4},{6,7},{7,6},{8,9},{9,8},{10,11... | collective-permute-start | bytes 614408 | tf_op jit(solution)/shard_map/ppermute | solution.py:245
  152.3 4.7 %collective-permute-start.36 = (bf16[8,12800]{1,0:T(8,128)(2,1)S(1)}, bf16[8,12800]{1,0:T(8,128)(2,1)S(1)}, u32[]{:S(2)}, u32[]{:S(2)}) collective-permute-start(bf16[8,12800]{1,0:T(8,128)(2,1)S(1)} %collective-permute-done.32.refs_1_), channel_id=1, source_target_pairs={{0,1},{1,0},{2,3},{3,2},{4,5},{5,4},{6,7},{7,6},{8,9},{9,8},{10,11... | collective-permute-start | bytes 614408 | tf_op jit(solution)/shard_map/ppermute | solution.py:245
  152.4 6.6 %collective-permute-start.37 = (bf16[8,12800]{1,0:T(8,128)(2,1)S(1)}, bf16[8,12800]{1,0:T(8,128)(2,1)S(1)}, u32[]{:S(2)}, u32[]{:S(2)}) collective-permute-start(bf16[8,12800]{1,0:T(8,128)(2,1)S(1)} %collective-permute-done.33.refs_2_), channel_id=1, source_target_pairs={{0,1},{1,0},{2,3},{3,2},{4,5},{5,4},{6,7},{7,6},{8,9},{9,8},{10,11... | collective-permute-start | bytes 614408 | tf_op jit(solution)/shard_map/ppermute | solution.py:245
  152.9 6.1 %collective-permute-start.38 = (bf16[8,12800]{1,0:T(8,128)(2,1)S(1)}, bf16[8,12800]{1,0:T(8,128)(2,1)S(1)}, u32[]{:S(2)}, u32[]{:S(2)}) collective-permute-start(bf16[8,12800]{1,0:T(8,128)(2,1)S(1)} %collective-permute-done.34.refs_3_), channel_id=1, source_target_pairs={{0,1},{1,0},{2,3},{3,2},{4,5},{5,4},{6,7},{7,6},{8,9},{9,8},{10,11... | collective-permute-start | bytes 614408 | tf_op jit(solution)/shard_map/ppermute | solution.py:245
  154.9 27.7 %collective-permute-start.40 = (bf16[8,12800]{1,0:T(8,128)(2,1)S(1)}, bf16[8,12800]{1,0:T(8,128)(2,1)S(1)}, u32[]{:S(2)}, u32[]{:S(2)}) collective-permute-start(bf16[8,12800]{1,0:T(8,128)(2,1)S(1)} %get-tuple-element.240), channel_id=1, source_target_pairs={{0,6},{1,7},{2,0},{3,1},{4,2},{5,3},{6,4},{7,5},{8,14},{9,15},{10,... | collective-permute-start | bytes 614408 | tf_op jit(solution)/shard_map/ppermute | solution.py:239
  155.7 27.0 %collective-permute-start.41 = (bf16[8,12800]{1,0:T(8,128)(2,1)S(1)}, bf16[8,12800]{1,0:T(8,128)(2,1)S(1)}, u32[]{:S(2)}, u32[]{:S(2)}) collective-permute-start(bf16[8,12800]{1,0:T(8,128)(2,1)S(1)} %get-tuple-element.239), channel_id=1, source_target_pairs={{0,4},{1,5},{2,6},{3,7},{4,0},{5,1},{6,2},{7,3},{8,12},{9,13},{10,... | collective-permute-start | bytes 614408 | tf_op jit(solution)/shard_map/ppermute | solution.py:239
  157.0 25.6 %collective-permute-start.42 = (bf16[8,12800]{1,0:T(8,128)(2,1)S(1)}, bf16[8,12800]{1,0:T(8,128)(2,1)S(1)}, u32[]{:S(2)}, u32[]{:S(2)}) collective-permute-start(bf16[8,12800]{1,0:T(8,128)(2,1)S(1)} %get-tuple-element.238), channel_id=1, source_target_pairs={{0,2},{1,3},{2,4},{3,5},{4,6},{5,7},{6,0},{7,1},{8,10},{9,11},{10,... | collective-permute-start | bytes 614408 | tf_op jit(solution)/shard_map/ppermute | solution.py:239
  182.7 8.1 %collective-permute-start.46 = (bf16[32,12800]{1,0:T(8,128)(2,1)}, bf16[32,12800]{1,0:T(8,128)(2,1)}, u32[]{:S(2)}, u32[]{:S(2)}) collective-permute-start(bf16[32,12800]{1,0:T(8,128)(2,1)} %get-tuple-element.153), channel_id=1, source_target_pairs={{0,1},{1,0},{2,3},{3,2},{4,5},{5,4},{6,7},{7,6},{8,9},{9,8},{10,11... | collective-permute-start | bytes 2457608 | tf_op jit(solution)/shard_map/ppermute | solution.py:252
  183.5 14.0 %collective-permute-start.43 = (bf16[32,3200]{1,0:T(8,128)(2,1)S(1)}, bf16[32,3200]{1,0:T(8,128)(2,1)S(1)}, u32[]{:S(2)}, u32[]{:S(2)}) collective-permute-start(bf16[32,3200]{1,0:T(8,128)(2,1)S(1)} %multiply_convert_fusion.2.refs_0_), channel_id=1, source_target_pairs={{0,2},{1,3},{2,4},{3,5},{4,6},{5,7},{6,0},{7,1},{8,10},{9,11},{10,... | collective-permute-start | bytes 614408 | tf_op jit(solution)/shard_map/ppermute | solution.py:239
  183.8 17.7 %collective-permute-start.44 = (bf16[32,3200]{1,0:T(8,128)(2,1)S(1)}, bf16[32,3200]{1,0:T(8,128)(2,1)}, u32[]{:S(2)}, u32[]{:S(2)}) collective-permute-start(bf16[32,3200]{1,0:T(8,128)(2,1)S(1)} %multiply_convert_fusion.2.refs_0_), channel_id=1, source_target_pairs={{0,4},{1,5},{2,6},{3,7},{4,0},{5,1},{6,2},{7,3},{8,12},{9,13},{10,... | collective-permute-start | bytes 614408 | tf_op jit(solution)/shard_map/ppermute | solution.py:239
  187.7 6.1 %collective-permute-start.50 = (bf16[32,1024]{1,0:T(8,128)(2,1)S(1)}, bf16[32,1024]{1,0:T(8,128)(2,1)S(1)}, u32[]{:S(2)}, u32[]{:S(2)}) collective-permute-start(bf16[32,1024]{1,0:T(8,128)(2,1)S(1)} %get-tuple-element.253), channel_id=1, source_target_pairs={{0,8},{8,16},{16,24},{24,0},{1,9},{9,17},{17,25},{25,1},{2,10},{10... | collective-permute-start | bytes 196616 | tf_op jit(solution)/shard_map/ppermute | solution.py:371
  189.3 6.1 %collective-permute-start.51 = (bf16[32,1024]{1,0:T(8,128)(2,1)S(1)}, bf16[32,1024]{1,0:T(8,128)(2,1)S(1)}, u32[]{:S(2)}, u32[]{:S(2)}) collective-permute-start(bf16[32,1024]{1,0:T(8,128)(2,1)S(1)} %get-tuple-element.252), channel_id=1, source_target_pairs={{0,16},{8,24},{16,0},{24,8},{1,17},{9,25},{17,1},{25,9},{2,18},{10... | collective-permute-start | bytes 196616 | tf_op jit(solution)/shard_map/ppermute | solution.py:371
  190.8 5.3 %collective-permute-start.52 = (bf16[32,1024]{1,0:T(8,128)(2,1)S(1)}, bf16[32,1024]{1,0:T(8,128)(2,1)S(1)}, u32[]{:S(2)}, u32[]{:S(2)}) collective-permute-start(bf16[32,1024]{1,0:T(8,128)(2,1)S(1)} %get-tuple-element.251), channel_id=1, source_target_pairs={{0,24},{8,0},{16,8},{24,16},{1,25},{9,1},{17,9},{25,17},{2,26},{10... | collective-permute-start | bytes 196616 | tf_op jit(solution)/shard_map/ppermute | solution.py:371
  193.9 11.3 %collective-permute-start.45 = (bf16[32,3200]{1,0:T(8,128)(2,1)S(1)}, bf16[32,3200]{1,0:T(8,128)(2,1)S(1)}, u32[]{:S(2)}, u32[]{:S(2)}) collective-permute-start(bf16[32,3200]{1,0:T(8,128)(2,1)S(1)} %multiply_convert_fusion.2.refs_0_), channel_id=1, source_target_pairs={{0,6},{1,7},{2,0},{3,1},{4,2},{5,3},{6,4},{7,5},{8,14},{9,15},{10,... | collective-permute-start | bytes 614408 | tf_op jit(solution)/shard_map/ppermute | solution.py:239
  195.4 12.7 %collective-permute-start.47 = (bf16[8,12800]{1,0:T(8,128)(2,1)S(1)}, bf16[8,12800]{1,0:T(8,128)(2,1)S(1)}, u32[]{:S(2)}, u32[]{:S(2)}) collective-permute-start(bf16[8,12800]{1,0:T(8,128)(2,1)S(1)} %get-tuple-element.237), channel_id=1, source_target_pairs={{0,6},{1,7},{2,0},{3,1},{4,2},{5,3},{6,4},{7,5},{8,14},{9,15},{10,... | collective-permute-start | bytes 614408 | tf_op jit(solution)/shard_map/ppermute | solution.py:239
  196.1 26.6 %collective-permute-start.48 = (bf16[8,12800]{1,0:T(8,128)(2,1)S(1)}, bf16[8,12800]{1,0:T(8,128)(2,1)S(1)}, u32[]{:S(2)}, u32[]{:S(2)}) collective-permute-start(bf16[8,12800]{1,0:T(8,128)(2,1)S(1)} %get-tuple-element.236), channel_id=1, source_target_pairs={{0,4},{1,5},{2,6},{3,7},{4,0},{5,1},{6,2},{7,3},{8,12},{9,13},{10,... | collective-permute-start | bytes 614408 | tf_op jit(solution)/shard_map/ppermute | solution.py:239
  197.5 25.3 %collective-permute-start.49 = (bf16[8,12800]{1,0:T(8,128)(2,1)S(1)}, bf16[8,12800]{1,0:T(8,128)(2,1)S(1)}, u32[]{:S(2)}, u32[]{:S(2)}) collective-permute-start(bf16[8,12800]{1,0:T(8,128)(2,1)S(1)} %get-tuple-element.235), channel_id=1, source_target_pairs={{0,2},{1,3},{2,4},{3,5},{4,6},{5,7},{6,0},{7,1},{8,10},{9,11},{10,... | collective-permute-start | bytes 614408 | tf_op jit(solution)/shard_map/ppermute | solution.py:239
  224.0 4.5 %collective-permute-start.55 = (bf16[32,3200]{1,0:T(8,128)(2,1)}, bf16[32,3200]{1,0:T(8,128)(2,1)S(1)}, u32[]{:S(2)}, u32[]{:S(2)}) collective-permute-start(bf16[32,3200]{1,0:T(8,128)(2,1)} %collective-permute-done.44.refs_2_), channel_id=1, source_target_pairs={{0,1},{1,0},{2,3},{3,2},{4,5},{5,4},{6,7},{7,6},{8,9},{9,8},{10,11... | collective-permute-start | bytes 614408 | tf_op jit(solution)/shard_map/ppermute | solution.py:245
  224.1 4.4 %collective-permute-start.56 = (bf16[32,3200]{1,0:T(8,128)(2,1)S(1)}, bf16[32,3200]{1,0:T(8,128)(2,1)S(1)}, u32[]{:S(2)}, u32[]{:S(2)}) collective-permute-start(bf16[32,3200]{1,0:T(8,128)(2,1)S(1)} %copy-done.20), channel_id=1, source_target_pairs={{0,1},{1,0},{2,3},{3,2},{4,5},{5,4},{6,7},{7,6},{8,9},{9,8},{10,11... | collective-permute-start | bytes 614408 | tf_op jit(solution)/shard_map/ppermute | solution.py:245
  224.6 22.3 %collective-permute-start.57 = (bf16[32,3200]{1,0:T(8,128)(2,1)S(1)}, bf16[32,3200]{1,0:T(8,128)(2,1)}, u32[]{:S(2)}, u32[]{:S(2)}) collective-permute-start(bf16[32,3200]{1,0:T(8,128)(2,1)S(1)} %multiply_convert_fusion.refs_0_), channel_id=1, source_target_pairs={{0,2},{1,3},{2,4},{3,5},{4,6},{5,7},{6,0},{7,1},{8,10},{9,11},{10,... | collective-permute-start | bytes 614408 | tf_op jit(solution)/shard_map/ppermute | solution.py:239
  225.0 21.9 %collective-permute-start.58 = (bf16[32,3200]{1,0:T(8,128)(2,1)S(1)}, bf16[32,3200]{1,0:T(8,128)(2,1)}, u32[]{:S(2)}, u32[]{:S(2)}) collective-permute-start(bf16[32,3200]{1,0:T(8,128)(2,1)S(1)} %multiply_convert_fusion.refs_0_), channel_id=1, source_target_pairs={{0,4},{1,5},{2,6},{3,7},{4,0},{5,1},{6,2},{7,3},{8,12},{9,13},{10,... | collective-permute-start | bytes 614408 | tf_op jit(solution)/shard_map/ppermute | solution.py:239
  225.2 21.7 %collective-permute-start.59 = (bf16[32,3200]{1,0:T(8,128)(2,1)S(1)}, bf16[32,3200]{1,0:T(8,128)(2,1)S(1)}, u32[]{:S(2)}, u32[]{:S(2)}) collective-permute-start(bf16[32,3200]{1,0:T(8,128)(2,1)S(1)} %multiply_convert_fusion.refs_0_), channel_id=1, source_target_pairs={{0,6},{1,7},{2,0},{3,1},{4,2},{5,3},{6,4},{7,5},{8,14},{9,15},{10,... | collective-permute-start | bytes 614408 | tf_op jit(solution)/shard_map/ppermute | solution.py:239
  247.3 4.8 %collective-permute-start.60 = (bf16[32,3200]{1,0:T(8,128)(2,1)S(1)}, bf16[32,3200]{1,0:T(8,128)(2,1)S(1)}, u32[]{:S(2)}, u32[]{:S(2)}) collective-permute-start(bf16[32,3200]{1,0:T(8,128)(2,1)S(1)} %multiply_convert_fusion.refs_0_), channel_id=1, source_target_pairs={{0,1},{1,0},{2,3},{3,2},{4,5},{5,4},{6,7},{7,6},{8,9},{9,8},{10,11... | collective-permute-start | bytes 614408 | tf_op jit(solution)/shard_map/ppermute | solution.py:245
  247.9 5.5 %collective-permute-start.61 = (bf16[32,3200]{1,0:T(8,128)(2,1)}, bf16[32,3200]{1,0:T(8,128)(2,1)S(1)}, u32[]{:S(2)}, u32[]{:S(2)}) collective-permute-start(bf16[32,3200]{1,0:T(8,128)(2,1)} %collective-permute-done.57.refs_1_), channel_id=1, source_target_pairs={{0,1},{1,0},{2,3},{3,2},{4,5},{5,4},{6,7},{7,6},{8,9},{9,8},{10,11... | collective-permute-start | bytes 614408 | tf_op jit(solution)/shard_map/ppermute | solution.py:245
  248.0 7.4 %collective-permute-start.62 = (bf16[32,3200]{1,0:T(8,128)(2,1)}, bf16[32,3200]{1,0:T(8,128)(2,1)S(1)}, u32[]{:S(2)}, u32[]{:S(2)}) collective-permute-start(bf16[32,3200]{1,0:T(8,128)(2,1)} %collective-permute-done.58.refs_2_), channel_id=1, source_target_pairs={{0,1},{1,0},{2,3},{3,2},{4,5},{5,4},{6,7},{7,6},{8,9},{9,8},{10,11... | collective-permute-start | bytes 614408 | tf_op jit(solution)/shard_map/ppermute | solution.py:245
  248.4 7.0 %collective-permute-start.63 = (bf16[32,3200]{1,0:T(8,128)(2,1)S(1)}, bf16[32,3200]{1,0:T(8,128)(2,1)S(1)}, u32[]{:S(2)}, u32[]{:S(2)}) collective-permute-start(bf16[32,3200]{1,0:T(8,128)(2,1)S(1)} %collective-permute-done.59.refs_3_), channel_id=1, source_target_pairs={{0,1},{1,0},{2,3},{3,2},{4,5},{5,4},{6,7},{7,6},{8,9},{9,8},{10,11... | collective-permute-start | bytes 614408 | tf_op jit(solution)/shard_map/ppermute | solution.py:245
  251.3 22.4 %collective-permute-start.65 = (bf16[32,3200]{1,0:T(8,128)(2,1)S(1)}, bf16[32,3200]{1,0:T(8,128)(2,1)S(1)}, u32[]{:S(2)}, u32[]{:S(2)}) collective-permute-start(bf16[32,3200]{1,0:T(8,128)(2,1)S(1)} %get-tuple-element.234), channel_id=1, source_target_pairs={{0,6},{1,7},{2,0},{3,1},{4,2},{5,3},{6,4},{7,5},{8,14},{9,15},{10,... | collective-permute-start | bytes 614408 | tf_op jit(solution)/shard_map/ppermute | solution.py:239
  252.2 21.6 %collective-permute-start.66 = (bf16[32,3200]{1,0:T(8,128)(2,1)S(1)}, bf16[32,3200]{1,0:T(8,128)(2,1)S(1)}, u32[]{:S(2)}, u32[]{:S(2)}) collective-permute-start(bf16[32,3200]{1,0:T(8,128)(2,1)S(1)} %get-tuple-element.233), channel_id=1, source_target_pairs={{0,4},{1,5},{2,6},{3,7},{4,0},{5,1},{6,2},{7,3},{8,12},{9,13},{10,... | collective-permute-start | bytes 614408 | tf_op jit(solution)/shard_map/ppermute | solution.py:239
  253.4 20.3 %collective-permute-start.67 = (bf16[32,3200]{1,0:T(8,128)(2,1)S(1)}, bf16[32,3200]{1,0:T(8,128)(2,1)S(1)}, u32[]{:S(2)}, u32[]{:S(2)}) collective-permute-start(bf16[32,3200]{1,0:T(8,128)(2,1)S(1)} %get-tuple-element.232), channel_id=1, source_target_pairs={{0,2},{1,3},{2,4},{3,5},{4,6},{5,7},{6,0},{7,1},{8,10},{9,11},{10,... | collective-permute-start | bytes 614408 | tf_op jit(solution)/shard_map/ppermute | solution.py:239
  276.6 7.7 %collective-permute-start.69 = (bf16[32,3200]{1,0:T(8,128)(2,1)S(1)}, bf16[32,3200]{1,0:T(8,128)(2,1)S(1)}, u32[]{:S(2)}, u32[]{:S(2)}) collective-permute-start(bf16[32,3200]{1,0:T(8,128)(2,1)S(1)} %get-tuple-element.231), channel_id=1, source_target_pairs={{0,6},{1,7},{2,0},{3,1},{4,2},{5,3},{6,4},{7,5},{8,14},{9,15},{10,... | collective-permute-start | bytes 614408 | tf_op jit(solution)/shard_map/ppermute | solution.py:239
  278.6 18.1 %collective-permute-start.70 = (bf16[32,3200]{1,0:T(8,128)(2,1)S(1)}, bf16[32,3200]{1,0:T(8,128)(2,1)S(1)}, u32[]{:S(2)}, u32[]{:S(2)}) collective-permute-start(bf16[32,3200]{1,0:T(8,128)(2,1)S(1)} %get-tuple-element.230), channel_id=1, source_target_pairs={{0,4},{1,5},{2,6},{3,7},{4,0},{5,1},{6,2},{7,3},{8,12},{9,13},{10,... | collective-permute-start | bytes 614408 | tf_op jit(solution)/shard_map/ppermute | solution.py:239
  278.6 18.1 %collective-permute-start.71 = (bf16[32,3200]{1,0:T(8,128)(2,1)S(1)}, bf16[32,3200]{1,0:T(8,128)(2,1)S(1)}, u32[]{:S(2)}, u32[]{:S(2)}) collective-permute-start(bf16[32,3200]{1,0:T(8,128)(2,1)S(1)} %get-tuple-element.229), channel_id=1, source_target_pairs={{0,2},{1,3},{2,4},{3,5},{4,6},{5,7},{6,0},{7,1},{8,10},{9,11},{10,... | collective-permute-start | bytes 614408 | tf_op jit(solution)/shard_map/ppermute | solution.py:239
  (68 other events, 555.0 us)

commit v7 on v6

--- a/solution.py
+++ b/solution.py
@@ -59,11 +59,13 @@
     lax.fori_loop(0, total // step, run, 0)
 
 
-def fetch(source, held, sems):
+def fetch(source, held, sems, j):
     count, rows = held.shape[:2]
-    for j in range(count):
-        copy = pltpu.make_async_copy(source.at[pl.ds(j * rows, rows)], held.at[j], sems.at[j])
-        copy.start(priority=j % 2)
+
+    @pl.when(j < count)
+    def _():
+        start = pl.multiple_of(j * rows, 16)
+        pltpu.make_async_copy(source.at[pl.ds(start, rows)], held.at[j], sems.at[j]).start()
 
 
 def arrive(source, held, sems, j):
@@ -78,14 +80,15 @@
     else:
         early, late, slope, near, far = refs[count : count + 5]
     first, second, rows, total, pre, hidden, first_sems, second_sems = refs[count + 5 :]
-    fetch(early, first, first_sems)
-    fetch(late, second, second_sems)
+    fetch(early, first, first_sems, 0)
+    fetch(late, second, second_sems, 0)
     rows[...] = laid(pieces)
     total[...] = jnp.zeros_like(total)
     tile = tile_of(rows.shape[1], 640)
 
     def block(j, _):
         arrive(early, first, first_sems, j)
+        fetch(early, first, first_sems, j + 1)
         pre[...] = times_transposed(rows[...], first[j])
 
         def act(sel):
@@ -100,6 +103,7 @@
 
         each_rows(pre.shape[0], act)
         arrive(late, second, second_sems, j)
+        fetch(late, second, second_sems, j + 1)
 
         def columns(k, _):
             sel = pl.ds(pl.multiple_of(k * tile, 128), tile)
@@ -120,7 +124,8 @@
 def project_kernel(count, *refs):
     pieces = refs[:count]
     weight, upstream, projected, near, far, held, rows, pre, delta, sems = refs[count:]
-    fetch(weight, held, sems)
+    for j in range(3):
+        fetch(weight, held, sems, j)
     rows[...] = laid(pieces)
     pre[...] = jnp.zeros_like(pre)
     chunk = held.shape[1]
@@ -128,6 +133,7 @@
 
     def ahead(j, _):
         arrive(weight, held, sems, j)
+        fetch(weight, held, sems, j + 3)
         sel = pl.ds(pl.multiple_of(j * chunk, 128), chunk)
         pre[...] += jnp.dot(rows[:, sel], held[j], preferred_element_type=jnp.float32)
         return 0
@@ -227,15 +233,14 @@
         self.places = self.size // cores
         rank = lax.axis_index("tp")
         place, core = rank // cores, rank % cores
-        back = (place - jnp.arange(self.places)) % self.places * cores
-        self.ranks = jnp.concatenate([back + core, back + 1 - core])
+        partner = (place ^ jnp.arange(self.places)) * cores
+        self.ranks = jnp.concatenate([partner + core, partner + 1 - core])
         every = jnp.arange(self.size)
-        far = (every + core) % cores * self.places
-        self.blocks = far + (place - every // cores) % self.places
+        self.blocks = (every + core) % cores * self.places + (every // cores ^ place)
         self.pairs = [(a, a + 1 - 2 * (a % cores)) for a in range(self.size)]
 
     def shift(self, block, k):
-        pairs = [(a, (a + k * cores) % self.size) for a in range(self.size)]
+        pairs = [(a, (a // cores ^ k) * cores + a % cores) for a in range(self.size)]
         return lax.ppermute(block, "tp", pairs)
 
     def spread(self, block):
@@ -253,7 +258,7 @@
         both = near.astype(jnp.float32) + got.astype(jnp.float32)
         cut = [both[k * rows : (k + 1) * rows] for k in range(self.places)]
         return cut[:1] + [
-            self.shift(cut[k].astype(jnp.bfloat16), -k) for k in range(1, self.places)
+            self.shift(cut[k].astype(jnp.bfloat16), k) for k in range(1, self.places)
         ]
 
     def summed(self, terms):

time: 300 us -> 296 us (0.987)
  waiting for transfers between devices: 75.8 us -> 64 us
  starting transfers between devices: 68.5 us -> 78.6 us
  Pallas kernels: 118 us -> 115 us
    ppermute x36, waiting for transfers between devices: 64.7 us -> 54 us  [shift(): return lax.ppermute(block, 'tp', pairs)]
    ppermute x36, starting transfers between devices: 51.6 us -> 61.6 us  [shift(): return lax.ppermute(block, 'tp', pairs)]
  transfers between devices with their start and end apart: 72 -> 72, of which waited for: 21 -> 16; matrix products, arithmetic and copies ran while one was open for 7% -> 7% of each run, Pallas kernels for 39% -> 39%
where the time goes in v7:
time: 296 us; the launch traced here: 295 us
  Pallas kernels  115 us (39%)
  starting transfers between devices  78.6 us (27%)
  waiting for transfers between devices  64 us (22%)
  other arithmetic  19.1 us (6%)
  local copies, waits for them, and re-layouts  14.1 us (5%)
    pallas_call x4, Pallas kernels, vision_pass(): pl.pallas_call(functools.partial(vision_kernel, len(pieces), slope is Non...  71.8 us
    ppermute x36, starting transfers between devices, shift(): return lax.ppermute(block, 'tp', pairs)  61.6 us
    ppermute x36, waiting for transfers between devices, shift(): return lax.ppermute(block, 'tp', pairs)  54 us
    pallas_call x2, Pallas kernels, project(): pl.pallas_call(functools.partial(project_kernel, len(pieces)), in_specs=w...  42.9 us
    another operation x7, other arithmetic  9.63 us
    ppermute x24, starting transfers between devices, gathered(): other = [lax.ppermute(m, 'tp', self.pairs) for m in mine]  6.46 us
  transfers between devices with their start and end apart: 72, of which 16 were waited for; matrix products, arithmetic and copies ran while one was open for 7% of the time, Pallas kernels for 39%

profile of v7, /device:TPU:0, one launch (start us, length us, event | category | flops | bytes accessed | tf_op | source)
XLA Modules:
  0.0 294.7 jit_solution(11973393520521655040)
XLA Ops:
  0.7 1.3 convert_reduce_fusion.1
  2.0 1.3 fusion.25
  3.3 1.2 fusion.19
  4.6 3.1 %collective-permute-start = (bf16[32,3200]{1,0:T(8,128)(2,1)S(1)}, bf16[32,3200]{1,0:T(8,128)(2,1)}, u32[]{:S(2)}, u32[]{:S(2)}) collective-permute-start(bf16[32,3200]{1,0:T(8,128)(2,1)S(1)} %get-tuple-element.99.refs_0_), channel_id=1, source_target_pairs={{0,2},{1,3},{2,0},{3,1},{4,6},{5,7},{6,4},{7,5},{8,10},{9,11},{10,... | collective-permute-start | bytes 614408 | tf_op jit(solution)/shard_map/ppermute | solution.py:244
  7.7 2.6 collective-permute-start.1
  12.3 2.7 collective-permute-start.3
  15.6 1.4 collective-permute-done.3
  17.0 2.4 collective-permute-start.5
  19.4 3.2 %collective-permute-done.5 = bf16[32,1024]{1,0:T(8,128)(2,1)S(1)} collective-permute-done((bf16[32,1024]{1,0:T(8,128)(2,1)S(1)}, bf16[32,1024]{1,0:T(8,128)(2,1)S(1)}, u32[]{:S(2)}, u32[]{:S(2)}) %collective-permute-start.5) | collective-permute-done | bytes 65568 | tf_op jit(solution)/shard_map/ppermute | solution.py:324
  22.6 2.9 collective-permute-done.1.refs_2_
  26.5 3.5 %collective-permute-start.10 = (bf16[32,3200]{1,0:T(8,128)(2,1)S(1)}, bf16[32,3200]{1,0:T(8,128)(2,1)S(1)}, u32[]{:S(2)}, u32[]{:S(2)}) collective-permute-start(bf16[32,3200]{1,0:T(8,128)(2,1)S(1)} %get-tuple-element.106.refs_0_), channel_id=1, source_target_pairs={{0,2},{1,3},{2,0},{3,1},{4,6},{5,7},{6,4},{7,5},{8,10},{9,11},{10,... | collective-permute-start | bytes 614408 | tf_op jit(solution)/shard_map/ppermute | solution.py:244
  30.0 1.7 collective-permute-start.11
  31.7 1.3 collective-permute-start.12
  33.9 18.4 %shard_map.113 = (bf16[128,3200]{1,0:T(8,128)(2,1)}, bf16[128,3200]{1,0:T(8,128)(2,1)}, f32[4,256,400]{2,1,0:T(8,128)}) custom-call(bf16[32,3200]{1,0:T(8,128)(2,1)} %copy-done.10, bf16[32,3200]{1,0:T(8,128)(2,1)} %collective-permute-done.refs_1_, bf16[32,3200]{1,0:T(8,128)(2,1)} %collective-permute-done.1.refs_2_, ...), custom_call_target="tpu_custom_call" | custom-call | flops 5242880000 | bytes 25395200 | tf_op jit(solution)/shard_map/pallas_call | solution.py:178
  53.6 1.4 collective-permute-done.17
  55.0 1.6 fusion.55
  57.2 2.6 collective-permute-start.19
  59.8 1.4 collective-permute-start.20
  62.6 18.3 %shard_map.114 = (bf16[128,3200]{1,0:T(8,128)(2,1)}, bf16[128,3200]{1,0:T(8,128)(2,1)}, f32[4,256,400]{2,1,0:T(8,128)}) custom-call(bf16[32,3200]{1,0:T(8,128)(2,1)} %copy-done.8, bf16[32,3200]{1,0:T(8,128)(2,1)} %copy-done.16, bf16[32,3200]{1,0:T(8,128)(2,1)} %collective-permute-done.11.refs_2_, bf16[32,3200]{1,0:T(8,128)(2,1)} %collective-permute-done.12.refs_3_, ...), custom_call_target="tpu_custom_call" | custom-call | flops 5242880000 | bytes 25395200 | tf_op jit(solution)/shard_map/pallas_call | solution.py:178
  82.5 3.0 %collective-permute-start.22 = (bf16[8,12800]{1,0:T(8,128)(2,1)S(1)}, bf16[8,12800]{1,0:T(8,128)(2,1)}, u32[]{:S(2)}, u32[]{:S(2)}) collective-permute-start(bf16[8,12800]{1,0:T(8,128)(2,1)S(1)} %multiply_convert_fusion.5.refs_0_), channel_id=1, source_target_pairs={{0,4},{1,5},{2,6},{3,7},{4,0},{5,1},{6,2},{7,3},{8,12},{9,13},{10,... | collective-permute-start | bytes 614408 | tf_op jit(solution)/shard_map/ppermute | solution.py:244
  85.5 1.4 collective-permute-start.23
  87.5 2.8 fusion.56
  90.4 3.0 %collective-permute-start.26 = (bf16[32,3200]{1,0:T(8,128)(2,1)S(1)}, bf16[32,3200]{1,0:T(8,128)(2,1)S(1)}, u32[]{:S(2)}, u32[]{:S(2)}) collective-permute-start(bf16[32,3200]{1,0:T(8,128)(2,1)S(1)} %get-tuple-element.242), channel_id=1, source_target_pairs={{0,4},{1,5},{2,6},{3,7},{4,0},{5,1},{6,2},{7,3},{8,12},{9,13},{10,... | collective-permute-start | bytes 614408 | tf_op jit(solution)/shard_map/ppermute | solution.py:244
  94.4 1.4 collective-permute-start.27
  95.9 1.2 gather_fusion.2
  97.1 1.0 slice.196
  98.1 2.3 collective-permute-done.22.refs_2_
  100.4 2.8 collective-permute-done.25
  103.1 14.7 %collective-permute-done.26 = bf16[32,3200]{1,0:T(8,128)(2,1)S(1)} collective-permute-done((bf16[32,3200]{1,0:T(8,128)(2,1)S(1)}, bf16[32,3200]{1,0:T(8,128)(2,1)S(1)}, u32[]{:S(2)}, u32[]{:S(2)}) %collective-permute-start.26) | collective-permute-done | bytes 204832 | tf_op jit(solution)/shard_map/ppermute | solution.py:244
  120.2 4.6 %collective-permute-start.32 = (bf16[8,12800]{1,0:T(8,128)(2,1)S(1)}, bf16[8,12800]{1,0:T(8,128)(2,1)S(1)}, u32[]{:S(2)}, u32[]{:S(2)}) collective-permute-start(bf16[8,12800]{1,0:T(8,128)(2,1)S(1)} %multiply_convert_fusion.4.refs_0_), channel_id=1, source_target_pairs={{0,2},{1,3},{2,0},{3,1},{4,6},{5,7},{6,4},{7,5},{8,10},{9,11},{10,... | collective-permute-start | bytes 614408 | tf_op jit(solution)/shard_map/ppermute | solution.py:244
  124.8 1.2 collective-permute-start.33
  126.0 1.4 collective-permute-start.34
  128.1 21.5 %shard_map.115 = (bf16[64,1024]{1,0:T(8,128)(2,1)}, bf16[32,12800]{1,0:T(8,128)(2,1)}, bf16[32,12800]{1,0:T(8,128)(2,1)}) custom-call(bf16[8,12800]{1,0:T(8,128)(2,1)} %copy-done.12, bf16[8,12800]{1,0:T(8,128)(2,1)} %copy-done.17, bf16[8,12800]{1,0:T(8,128)(2,1)} %collective-permute-done.22.refs_2_, bf16[8,12800]{1,0:T(8,128)(2,1)} %collective-permute-done.23.refs_3_, ...), custom_call_target="tpu_custom_call" | custom-call | flops 3355443200 | bytes 29753344 | tf_op jit(solution)/shard_map/pallas_call | solution.py:208
  149.8 1.2 gather_fusion.3
  152.4 1.6 fusion.57
  155.0 2.1 collective-permute-start.41
  157.2 1.4 collective-permute-start.42
  159.3 21.5 %shard_map.116 = (bf16[64,1024]{1,0:T(8,128)(2,1)}, bf16[32,12800]{1,0:T(8,128)(2,1)}, bf16[32,12800]{1,0:T(8,128)(2,1)}) custom-call(bf16[8,12800]{1,0:T(8,128)(2,1)} %copy-done.13, bf16[8,12800]{1,0:T(8,128)(2,1)} %copy-done.18, bf16[8,12800]{1,0:T(8,128)(2,1)} %copy-done.21, bf16[8,12800]{1,0:T(8,128)(2,1)} %copy-done.22, bf16[8,12800]{1,0:T(8,128)(2,1)} %copy-done.24, ...), custom_call_target="tpu_custom_call" | custom-call | flops 3355443200 | bytes 29753344 | tf_op jit(solution)/shard_map/pallas_call | solution.py:208
  181.7 3.0 %collective-permute-start.44 = (bf16[32,3200]{1,0:T(8,128)(2,1)S(1)}, bf16[32,3200]{1,0:T(8,128)(2,1)}, u32[]{:S(2)}, u32[]{:S(2)}) collective-permute-start(bf16[32,3200]{1,0:T(8,128)(2,1)S(1)} %multiply_convert_fusion.2.refs_0_), channel_id=1, source_target_pairs={{0,4},{1,5},{2,6},{3,7},{4,0},{5,1},{6,2},{7,3},{8,12},{9,13},{10,... | collective-permute-start | bytes 614408 | tf_op jit(solution)/shard_map/ppermute | solution.py:244
  186.5 1.5 collective-permute-start.50
  188.0 1.5 collective-permute-start.51
  189.6 1.4 collective-permute-start.52
  191.0 1.6 fusion.58
  192.6 1.5 collective-permute-start.45
  194.1 3.0 %collective-permute-start.48 = (bf16[8,12800]{1,0:T(8,128)(2,1)S(1)}, bf16[8,12800]{1,0:T(8,128)(2,1)S(1)}, u32[]{:S(2)}, u32[]{:S(2)}) collective-permute-start(bf16[8,12800]{1,0:T(8,128)(2,1)S(1)} %get-tuple-element.236), channel_id=1, source_target_pairs={{0,4},{1,5},{2,6},{3,7},{4,0},{5,1},{6,2},{7,3},{8,12},{9,13},{10,... | collective-permute-start | bytes 614408 | tf_op jit(solution)/shard_map/ppermute | solution.py:244
  197.1 1.4 collective-permute-start.49
  198.5 4.0 %collective-permute-done.45.refs_3_ = bf16[32,3200]{1,0:T(8,128)(2,1)S(1)} collective-permute-done((bf16[32,3200]{1,0:T(8,128)(2,1)S(1)}, bf16[32,3200]{1,0:T(8,128)(2,1)S(1)}, u32[]{:S(2)}, u32[]{:S(2)}) %collective-permute-start.45) | collective-permute-done | bytes 204832 | tf_op jit(solution)/shard_map/ppermute | solution.py:244
  202.5 2.8 collective-permute-done.47
  205.3 12.5 %collective-permute-done.48 = bf16[8,12800]{1,0:T(8,128)(2,1)S(1)} collective-permute-done((bf16[8,12800]{1,0:T(8,128)(2,1)S(1)}, bf16[8,12800]{1,0:T(8,128)(2,1)S(1)}, u32[]{:S(2)}, u32[]{:S(2)}) %collective-permute-start.48) | collective-permute-done | bytes 204832 | tf_op jit(solution)/shard_map/ppermute | solution.py:244
  219.6 3.8 %collective-permute-start.57 = (bf16[32,3200]{1,0:T(8,128)(2,1)S(1)}, bf16[32,3200]{1,0:T(8,128)(2,1)}, u32[]{:S(2)}, u32[]{:S(2)}) collective-permute-start(bf16[32,3200]{1,0:T(8,128)(2,1)S(1)} %multiply_convert_fusion.refs_0_), channel_id=1, source_target_pairs={{0,2},{1,3},{2,0},{3,1},{4,6},{5,7},{6,4},{7,5},{8,10},{9,11},{10,... | collective-permute-start | bytes 614408 | tf_op jit(solution)/shard_map/ppermute | solution.py:244
  223.4 1.3 collective-permute-start.58
  224.7 1.4 collective-permute-start.59
  226.8 17.6 %shard_map.117 = (bf16[128,3200]{1,0:T(8,128)(2,1)}, bf16[128,3200]{1,0:T(8,128)(2,1)}) custom-call(bf16[32,3200]{1,0:T(8,128)(2,1)} %copy-done.9, bf16[32,3200]{1,0:T(8,128)(2,1)} %copy-done.15, bf16[32,3200]{1,0:T(8,128)(2,1)} %collective-permute-done.44.refs_2_, bf16[32,3200]{1,0:T(8,128)(2,1)} %copy-done.19, bf16[32,3200]{1,0:T(8,128)(2,1)} %copy-done.37, ...), custom_call_target="tpu_custom_call" | custom-call | flops 5242880000 | bytes 25395200 | tf_op jit(solution)/shard_map/pallas_call | solution.py:178
  246.1 1.2 collective-permute-done.64
  247.2 1.6 fusion.59
  249.8 2.2 collective-permute-start.66
  251.9 1.4 collective-permute-start.67
  254.1 17.6 %shard_map.118 = (bf16[128,3200]{1,0:T(8,128)(2,1)}, bf16[128,3200]{1,0:T(8,128)(2,1)}) custom-call(bf16[32,3200]{1,0:T(8,128)(2,1)} %copy-done.11, bf16[32,3200]{1,0:T(8,128)(2,1)} %collective-permute-done.57.refs_1_, bf16[32,3200]{1,0:T(8,128)(2,1)} %collective-permute-done.58.refs_2_, bf16[32,3200]{1,0:T(8,128)(2,1)} %copy-done.23, ...), custom_call_target="tpu_custom_call" | custom-call | flops 5242880000 | bytes 25395200 | tf_op jit(solution)/shard_map/pallas_call | solution.py:178
  272.0 2.4 collective-permute-done.68
  274.7 3.0 %collective-permute-start.70 = (bf16[32,3200]{1,0:T(8,128)(2,1)S(1)}, bf16[32,3200]{1,0:T(8,128)(2,1)S(1)}, u32[]{:S(2)}, u32[]{:S(2)}) collective-permute-start(bf16[32,3200]{1,0:T(8,128)(2,1)S(1)} %get-tuple-element.230), channel_id=1, source_target_pairs={{0,4},{1,5},{2,6},{3,7},{4,0},{5,1},{6,2},{7,3},{8,12},{9,13},{10,... | collective-permute-start | bytes 614408 | tf_op jit(solution)/shard_map/ppermute | solution.py:244
  277.7 1.4 collective-permute-start.71
  279.1 2.2 fusion
  281.3 4.4 %collective-permute-done.69 = bf16[32,3200]{1,0:T(8,128)(2,1)S(1)} collective-permute-done((bf16[32,3200]{1,0:T(8,128)(2,1)S(1)}, bf16[32,3200]{1,0:T(8,128)(2,1)S(1)}, u32[]{:S(2)}, u32[]{:S(2)}) %collective-permute-start.69) | collective-permute-done | bytes 204832 | tf_op jit(solution)/shard_map/ppermute | solution.py:244
  285.7 6.7 %collective-permute-done.70 = bf16[32,3200]{1,0:T(8,128)(2,1)S(1)} collective-permute-done((bf16[32,3200]{1,0:T(8,128)(2,1)S(1)}, bf16[32,3200]{1,0:T(8,128)(2,1)S(1)}, u32[]{:S(2)}, u32[]{:S(2)}) %collective-permute-start.70) | collective-permute-done | bytes 204832 | tf_op jit(solution)/shard_map/ppermute | solution.py:244
  (311 shorter events, 28.3 us)
Async XLA Ops:
  4.6 18.0 %collective-permute-start = (bf16[32,3200]{1,0:T(8,128)(2,1)S(1)}, bf16[32,3200]{1,0:T(8,128)(2,1)}, u32[]{:S(2)}, u32[]{:S(2)}) collective-permute-start(bf16[32,3200]{1,0:T(8,128)(2,1)S(1)} %get-tuple-element.99.refs_0_), channel_id=1, source_target_pairs={{0,2},{1,3},{2,0},{3,1},{4,6},{5,7},{6,4},{7,5},{8,10},{9,11},{10,... | collective-permute-start | bytes 614408 | tf_op jit(solution)/shard_map/ppermute | solution.py:244
  7.7 17.8 %collective-permute-start.1 = (bf16[32,3200]{1,0:T(8,128)(2,1)S(1)}, bf16[32,3200]{1,0:T(8,128)(2,1)}, u32[]{:S(2)}, u32[]{:S(2)}) collective-permute-start(bf16[32,3200]{1,0:T(8,128)(2,1)S(1)} %get-tuple-element.99.refs_0_), channel_id=1, source_target_pairs={{0,4},{1,5},{2,6},{3,7},{4,0},{5,1},{6,2},{7,3},{8,12},{9,13},{10,... | collective-permute-start | bytes 614408 | tf_op jit(solution)/shard_map/ppermute | solution.py:244
  10.3 15.2 %collective-permute-start.2 = (bf16[32,3200]{1,0:T(8,128)(2,1)S(1)}, bf16[32,3200]{1,0:T(8,128)(2,1)}, u32[]{:S(2)}, u32[]{:S(2)}) collective-permute-start(bf16[32,3200]{1,0:T(8,128)(2,1)S(1)} %get-tuple-element.99.refs_0_), channel_id=1, source_target_pairs={{0,6},{1,7},{2,4},{3,5},{4,2},{5,3},{6,0},{7,1},{8,14},{9,15},{10,... | collective-permute-start | bytes 614408 | tf_op jit(solution)/shard_map/ppermute | solution.py:244
  12.3 4.6 %collective-permute-start.3 = (bf16[32,1024]{1,0:T(8,128)(2,1)S(1)}, bf16[32,1024]{1,0:T(8,128)(2,1)S(1)}, u32[]{:S(2)}, u32[]{:S(2)}) collective-permute-start(bf16[32,1024]{1,0:T(8,128)(2,1)S(1)} %get-tuple-element.259), channel_id=1, source_target_pairs={{0,24},{8,0},{16,8},{24,16},{1,25},{9,1},{17,9},{25,17},{2,26},{10... | collective-permute-start | bytes 196616 | tf_op jit(solution)/shard_map/ppermute | solution.py:324
  17.0 5.6 %collective-permute-start.5 = (bf16[32,1024]{1,0:T(8,128)(2,1)S(1)}, bf16[32,1024]{1,0:T(8,128)(2,1)S(1)}, u32[]{:S(2)}, u32[]{:S(2)}) collective-permute-start(bf16[32,1024]{1,0:T(8,128)(2,1)S(1)} %get-tuple-element.257), channel_id=1, source_target_pairs={{0,8},{8,16},{16,24},{24,0},{1,9},{9,17},{17,25},{25,1},{2,10},{10... | collective-permute-start | bytes 196616 | tf_op jit(solution)/shard_map/ppermute | solution.py:324
  25.5 6.2 %collective-permute-start.7 = (bf16[32,3200]{1,0:T(8,128)(2,1)}, bf16[32,3200]{1,0:T(8,128)(2,1)S(1)}, u32[]{:S(2)}, u32[]{:S(2)}) collective-permute-start(bf16[32,3200]{1,0:T(8,128)(2,1)} %collective-permute-done.refs_1_), channel_id=1, source_target_pairs={{0,1},{1,0},{2,3},{3,2},{4,5},{5,4},{6,7},{7,6},{8,9},{9,8},{10,11... | collective-permute-start | bytes 614408 | tf_op jit(solution)/shard_map/ppermute | solution.py:250
  26.0 7.1 %collective-permute-start.8 = (bf16[32,3200]{1,0:T(8,128)(2,1)}, bf16[32,3200]{1,0:T(8,128)(2,1)S(1)}, u32[]{:S(2)}, u32[]{:S(2)}) collective-permute-start(bf16[32,3200]{1,0:T(8,128)(2,1)} %collective-permute-done.1.refs_2_), channel_id=1, source_target_pairs={{0,1},{1,0},{2,3},{3,2},{4,5},{5,4},{6,7},{7,6},{8,9},{9,8},{10,11... | collective-permute-start | bytes 614408 | tf_op jit(solution)/shard_map/ppermute | solution.py:250
  26.0 7.1 %collective-permute-start.9 = (bf16[32,3200]{1,0:T(8,128)(2,1)}, bf16[32,3200]{1,0:T(8,128)(2,1)S(1)}, u32[]{:S(2)}, u32[]{:S(2)}) collective-permute-start(bf16[32,3200]{1,0:T(8,128)(2,1)} %collective-permute-done.2.refs_3_), channel_id=1, source_target_pairs={{0,1},{1,0},{2,3},{3,2},{4,5},{5,4},{6,7},{7,6},{8,9},{9,8},{10,11... | collective-permute-start | bytes 614408 | tf_op jit(solution)/shard_map/ppermute | solution.py:250
  26.5 25.7 %collective-permute-start.10 = (bf16[32,3200]{1,0:T(8,128)(2,1)S(1)}, bf16[32,3200]{1,0:T(8,128)(2,1)S(1)}, u32[]{:S(2)}, u32[]{:S(2)}) collective-permute-start(bf16[32,3200]{1,0:T(8,128)(2,1)S(1)} %get-tuple-element.106.refs_0_), channel_id=1, source_target_pairs={{0,2},{1,3},{2,0},{3,1},{4,6},{5,7},{6,4},{7,5},{8,10},{9,11},{10,... | collective-permute-start | bytes 614408 | tf_op jit(solution)/shard_map/ppermute | solution.py:244
  30.0 22.2 %collective-permute-start.11 = (bf16[32,3200]{1,0:T(8,128)(2,1)S(1)}, bf16[32,3200]{1,0:T(8,128)(2,1)}, u32[]{:S(2)}, u32[]{:S(2)}) collective-permute-start(bf16[32,3200]{1,0:T(8,128)(2,1)S(1)} %get-tuple-element.106.refs_0_), channel_id=1, source_target_pairs={{0,4},{1,5},{2,6},{3,7},{4,0},{5,1},{6,2},{7,3},{8,12},{9,13},{10,... | collective-permute-start | bytes 614408 | tf_op jit(solution)/shard_map/ppermute | solution.py:244
  31.7 20.5 %collective-permute-start.12 = (bf16[32,3200]{1,0:T(8,128)(2,1)S(1)}, bf16[32,3200]{1,0:T(8,128)(2,1)}, u32[]{:S(2)}, u32[]{:S(2)}) collective-permute-start(bf16[32,3200]{1,0:T(8,128)(2,1)S(1)} %get-tuple-element.106.refs_0_), channel_id=1, source_target_pairs={{0,6},{1,7},{2,4},{3,5},{4,2},{5,3},{6,0},{7,1},{8,14},{9,15},{10,... | collective-permute-start | bytes 614408 | tf_op jit(solution)/shard_map/ppermute | solution.py:244
  52.5 4.7 %collective-permute-start.13 = (bf16[32,3200]{1,0:T(8,128)(2,1)S(1)}, bf16[32,3200]{1,0:T(8,128)(2,1)S(1)}, u32[]{:S(2)}, u32[]{:S(2)}) collective-permute-start(bf16[32,3200]{1,0:T(8,128)(2,1)S(1)} %get-tuple-element.106.refs_0_), channel_id=1, source_target_pairs={{0,1},{1,0},{2,3},{3,2},{4,5},{5,4},{6,7},{7,6},{8,9},{9,8},{10,11... | collective-permute-start | bytes 614408 | tf_op jit(solution)/shard_map/ppermute | solution.py:250
  53.0 6.7 %collective-permute-start.14 = (bf16[32,3200]{1,0:T(8,128)(2,1)S(1)}, bf16[32,3200]{1,0:T(8,128)(2,1)S(1)}, u32[]{:S(2)}, u32[]{:S(2)}) collective-permute-start(bf16[32,3200]{1,0:T(8,128)(2,1)S(1)} %collective-permute-done.10.refs_1_), channel_id=1, source_target_pairs={{0,1},{1,0},{2,3},{3,2},{4,5},{5,4},{6,7},{7,6},{8,9},{9,8},{10,11... | collective-permute-start | bytes 614408 | tf_op jit(solution)/shard_map/ppermute | solution.py:250
  53.1 8.1 %collective-permute-start.15 = (bf16[32,3200]{1,0:T(8,128)(2,1)}, bf16[32,3200]{1,0:T(8,128)(2,1)S(1)}, u32[]{:S(2)}, u32[]{:S(2)}) collective-permute-start(bf16[32,3200]{1,0:T(8,128)(2,1)} %collective-permute-done.11.refs_2_), channel_id=1, source_target_pairs={{0,1},{1,0},{2,3},{3,2},{4,5},{5,4},{6,7},{7,6},{8,9},{9,8},{10,11... | collective-permute-start | bytes 614408 | tf_op jit(solution)/shard_map/ppermute | solution.py:250
  53.5 7.7 %collective-permute-start.16 = (bf16[32,3200]{1,0:T(8,128)(2,1)}, bf16[32,3200]{1,0:T(8,128)(2,1)S(1)}, u32[]{:S(2)}, u32[]{:S(2)}) collective-permute-start(bf16[32,3200]{1,0:T(8,128)(2,1)} %collective-permute-done.12.refs_3_), channel_id=1, source_target_pairs={{0,1},{1,0},{2,3},{3,2},{4,5},{5,4},{6,7},{7,6},{8,9},{9,8},{10,11... | collective-permute-start | bytes 614408 | tf_op jit(solution)/shard_map/ppermute | solution.py:250
  56.7 24.3 %collective-permute-start.18 = (bf16[32,3200]{1,0:T(8,128)(2,1)S(1)}, bf16[32,3200]{1,0:T(8,128)(2,1)S(1)}, u32[]{:S(2)}, u32[]{:S(2)}) collective-permute-start(bf16[32,3200]{1,0:T(8,128)(2,1)S(1)} %get-tuple-element.246), channel_id=1, source_target_pairs={{0,2},{1,3},{2,0},{3,1},{4,6},{5,7},{6,4},{7,5},{8,10},{9,11},{10,... | collective-permute-start | bytes 614408 | tf_op jit(solution)/shard_map/ppermute | solution.py:244
  57.2 23.8 %collective-permute-start.19 = (bf16[32,3200]{1,0:T(8,128)(2,1)S(1)}, bf16[32,3200]{1,0:T(8,128)(2,1)S(1)}, u32[]{:S(2)}, u32[]{:S(2)}) collective-permute-start(bf16[32,3200]{1,0:T(8,128)(2,1)S(1)} %get-tuple-element.245), channel_id=1, source_target_pairs={{0,4},{1,5},{2,6},{3,7},{4,0},{5,1},{6,2},{7,3},{8,12},{9,13},{10,... | collective-permute-start | bytes 614408 | tf_op jit(solution)/shard_map/ppermute | solution.py:244
  59.8 21.2 %collective-permute-start.20 = (bf16[32,3200]{1,0:T(8,128)(2,1)S(1)}, bf16[32,3200]{1,0:T(8,128)(2,1)S(1)}, u32[]{:S(2)}, u32[]{:S(2)}) collective-permute-start(bf16[32,3200]{1,0:T(8,128)(2,1)S(1)} %get-tuple-element.244), channel_id=1, source_target_pairs={{0,6},{1,7},{2,4},{3,5},{4,2},{5,3},{6,0},{7,1},{8,14},{9,15},{10,... | collective-permute-start | bytes 614408 | tf_op jit(solution)/shard_map/ppermute | solution.py:244
  81.0 6.5 %collective-permute-start.24 = (bf16[128,3200]{1,0:T(8,128)(2,1)}, bf16[128,3200]{1,0:T(8,128)(2,1)}, u32[]{:S(2)}, u32[]{:S(2)}) collective-permute-start(bf16[128,3200]{1,0:T(8,128)(2,1)} %get-tuple-element.123), channel_id=1, source_target_pairs={{0,1},{1,0},{2,3},{3,2},{4,5},{5,4},{6,7},{7,6},{8,9},{9,8},{10,11... | collective-permute-start | bytes 2457608 | tf_op jit(solution)/shard_map/ppermute | solution.py:257
  82.4 12.0 %collective-permute-start.21 = (bf16[8,12800]{1,0:T(8,128)(2,1)S(1)}, bf16[8,12800]{1,0:T(8,128)(2,1)S(1)}, u32[]{:S(2)}, u32[]{:S(2)}) collective-permute-start(bf16[8,12800]{1,0:T(8,128)(2,1)S(1)} %multiply_convert_fusion.5.refs_0_), channel_id=1, source_target_pairs={{0,2},{1,3},{2,0},{3,1},{4,6},{5,7},{6,4},{7,5},{8,10},{9,11},{10,... | collective-permute-start | bytes 614408 | tf_op jit(solution)/shard_map/ppermute | solution.py:244
  82.5 17.8 %collective-permute-start.22 = (bf16[8,12800]{1,0:T(8,128)(2,1)S(1)}, bf16[8,12800]{1,0:T(8,128)(2,1)}, u32[]{:S(2)}, u32[]{:S(2)}) collective-permute-start(bf16[8,12800]{1,0:T(8,128)(2,1)S(1)} %multiply_convert_fusion.5.refs_0_), channel_id=1, source_target_pairs={{0,4},{1,5},{2,6},{3,7},{4,0},{5,1},{6,2},{7,3},{8,12},{9,13},{10,... | collective-permute-start | bytes 614408 | tf_op jit(solution)/shard_map/ppermute | solution.py:244
  85.5 14.8 %collective-permute-start.23 = (bf16[8,12800]{1,0:T(8,128)(2,1)S(1)}, bf16[8,12800]{1,0:T(8,128)(2,1)}, u32[]{:S(2)}, u32[]{:S(2)}) collective-permute-start(bf16[8,12800]{1,0:T(8,128)(2,1)S(1)} %multiply_convert_fusion.5.refs_0_), channel_id=1, source_target_pairs={{0,6},{1,7},{2,4},{3,5},{4,2},{5,3},{6,0},{7,1},{8,14},{9,15},{10,... | collective-permute-start | bytes 614408 | tf_op jit(solution)/shard_map/ppermute | solution.py:244
  90.3 12.8 %collective-permute-start.25 = (bf16[32,3200]{1,0:T(8,128)(2,1)S(1)}, bf16[32,3200]{1,0:T(8,128)(2,1)S(1)}, u32[]{:S(2)}, u32[]{:S(2)}) collective-permute-start(bf16[32,3200]{1,0:T(8,128)(2,1)S(1)} %get-tuple-element.243), channel_id=1, source_target_pairs={{0,2},{1,3},{2,0},{3,1},{4,6},{5,7},{6,4},{7,5},{8,10},{9,11},{10,... | collective-permute-start | bytes 614408 | tf_op jit(solution)/shard_map/ppermute | solution.py:244
  90.4 27.4 %collective-permute-start.26 = (bf16[32,3200]{1,0:T(8,128)(2,1)S(1)}, bf16[32,3200]{1,0:T(8,128)(2,1)S(1)}, u32[]{:S(2)}, u32[]{:S(2)}) collective-permute-start(bf16[32,3200]{1,0:T(8,128)(2,1)S(1)} %get-tuple-element.242), channel_id=1, source_target_pairs={{0,4},{1,5},{2,6},{3,7},{4,0},{5,1},{6,2},{7,3},{8,12},{9,13},{10,... | collective-permute-start | bytes 614408 | tf_op jit(solution)/shard_map/ppermute | solution.py:244
  94.4 23.4 %collective-permute-start.27 = (bf16[32,3200]{1,0:T(8,128)(2,1)S(1)}, bf16[32,3200]{1,0:T(8,128)(2,1)S(1)}, u32[]{:S(2)}, u32[]{:S(2)}) collective-permute-start(bf16[32,3200]{1,0:T(8,128)(2,1)S(1)} %get-tuple-element.241), channel_id=1, source_target_pairs={{0,6},{1,7},{2,4},{3,5},{4,2},{5,3},{6,0},{7,1},{8,14},{9,15},{10,... | collective-permute-start | bytes 614408 | tf_op jit(solution)/shard_map/ppermute | solution.py:244
  118.9 5.8 %collective-permute-start.28 = (bf16[8,12800]{1,0:T(8,128)(2,1)S(1)}, bf16[8,12800]{1,0:T(8,128)(2,1)S(1)}, u32[]{:S(2)}, u32[]{:S(2)}) collective-permute-start(bf16[8,12800]{1,0:T(8,128)(2,1)S(1)} %multiply_convert_fusion.5.refs_0_), channel_id=1, source_target_pairs={{0,1},{1,0},{2,3},{3,2},{4,5},{5,4},{6,7},{7,6},{8,9},{9,8},{10,11... | collective-permute-start | bytes 614408 | tf_op jit(solution)/shard_map/ppermute | solution.py:250
  119.0 7.0 %collective-permute-start.29 = (bf16[8,12800]{1,0:T(8,128)(2,1)}, bf16[8,12800]{1,0:T(8,128)(2,1)S(1)}, u32[]{:S(2)}, u32[]{:S(2)}) collective-permute-start(bf16[8,12800]{1,0:T(8,128)(2,1)} %copy-done.17), channel_id=1, source_target_pairs={{0,1},{1,0},{2,3},{3,2},{4,5},{5,4},{6,7},{7,6},{8,9},{9,8},{10,11... | collective-permute-start | bytes 614408 | tf_op jit(solution)/shard_map/ppermute | solution.py:250
  119.5 7.8 %collective-permute-start.30 = (bf16[8,12800]{1,0:T(8,128)(2,1)}, bf16[8,12800]{1,0:T(8,128)(2,1)S(1)}, u32[]{:S(2)}, u32[]{:S(2)}) collective-permute-start(bf16[8,12800]{1,0:T(8,128)(2,1)} %collective-permute-done.22.refs_2_), channel_id=1, source_target_pairs={{0,1},{1,0},{2,3},{3,2},{4,5},{5,4},{6,7},{7,6},{8,9},{9,8},{10,11... | collective-permute-start | bytes 614408 | tf_op jit(solution)/shard_map/ppermute | solution.py:250
  119.6 7.8 %collective-permute-start.31 = (bf16[8,12800]{1,0:T(8,128)(2,1)}, bf16[8,12800]{1,0:T(8,128)(2,1)S(1)}, u32[]{:S(2)}, u32[]{:S(2)}) collective-permute-start(bf16[8,12800]{1,0:T(8,128)(2,1)} %collective-permute-done.23.refs_3_), channel_id=1, source_target_pairs={{0,1},{1,0},{2,3},{3,2},{4,5},{5,4},{6,7},{7,6},{8,9},{9,8},{10,11... | collective-permute-start | bytes 614408 | tf_op jit(solution)/shard_map/ppermute | solution.py:250
  120.2 29.4 %collective-permute-start.32 = (bf16[8,12800]{1,0:T(8,128)(2,1)S(1)}, bf16[8,12800]{1,0:T(8,128)(2,1)S(1)}, u32[]{:S(2)}, u32[]{:S(2)}) collective-permute-start(bf16[8,12800]{1,0:T(8,128)(2,1)S(1)} %multiply_convert_fusion.4.refs_0_), channel_id=1, source_target_pairs={{0,2},{1,3},{2,0},{3,1},{4,6},{5,7},{6,4},{7,5},{8,10},{9,11},{10,... | collective-permute-start | bytes 614408 | tf_op jit(solution)/shard_map/ppermute | solution.py:244
  124.8 24.9 %collective-permute-start.33 = (bf16[8,12800]{1,0:T(8,128)(2,1)S(1)}, bf16[8,12800]{1,0:T(8,128)(2,1)S(1)}, u32[]{:S(2)}, u32[]{:S(2)}) collective-permute-start(bf16[8,12800]{1,0:T(8,128)(2,1)S(1)} %multiply_convert_fusion.4.refs_0_), channel_id=1, source_target_pairs={{0,4},{1,5},{2,6},{3,7},{4,0},{5,1},{6,2},{7,3},{8,12},{9,13},{10,... | collective-permute-start | bytes 614408 | tf_op jit(solution)/shard_map/ppermute | solution.py:244
  126.0 23.7 %collective-permute-start.34 = (bf16[8,12800]{1,0:T(8,128)(2,1)S(1)}, bf16[8,12800]{1,0:T(8,128)(2,1)S(1)}, u32[]{:S(2)}, u32[]{:S(2)}) collective-permute-start(bf16[8,12800]{1,0:T(8,128)(2,1)S(1)} %multiply_convert_fusion.4.refs_0_), channel_id=1, source_target_pairs={{0,6},{1,7},{2,4},{3,5},{4,2},{5,3},{6,0},{7,1},{8,14},{9,15},{10,... | collective-permute-start | bytes 614408 | tf_op jit(solution)/shard_map/ppermute | solution.py:244
  151.5 5.6 %collective-permute-start.36 = (bf16[8,12800]{1,0:T(8,128)(2,1)S(1)}, bf16[8,12800]{1,0:T(8,128)(2,1)S(1)}, u32[]{:S(2)}, u32[]{:S(2)}) collective-permute-start(bf16[8,12800]{1,0:T(8,128)(2,1)S(1)} %collective-permute-done.32.refs_1_), channel_id=1, source_target_pairs={{0,1},{1,0},{2,3},{3,2},{4,5},{5,4},{6,7},{7,6},{8,9},{9,8},{10,11... | collective-permute-start | bytes 614408 | tf_op jit(solution)/shard_map/ppermute | solution.py:250
  151.5 7.0 %collective-permute-start.37 = (bf16[8,12800]{1,0:T(8,128)(2,1)S(1)}, bf16[8,12800]{1,0:T(8,128)(2,1)S(1)}, u32[]{:S(2)}, u32[]{:S(2)}) collective-permute-start(bf16[8,12800]{1,0:T(8,128)(2,1)S(1)} %collective-permute-done.33.refs_2_), channel_id=1, source_target_pairs={{0,1},{1,0},{2,3},{3,2},{4,5},{5,4},{6,7},{7,6},{8,9},{9,8},{10,11... | collective-permute-start | bytes 614408 | tf_op jit(solution)/shard_map/ppermute | solution.py:250
  152.0 6.5 %collective-permute-start.38 = (bf16[8,12800]{1,0:T(8,128)(2,1)S(1)}, bf16[8,12800]{1,0:T(8,128)(2,1)S(1)}, u32[]{:S(2)}, u32[]{:S(2)}) collective-permute-start(bf16[8,12800]{1,0:T(8,128)(2,1)S(1)} %collective-permute-done.34.refs_3_), channel_id=1, source_target_pairs={{0,1},{1,0},{2,3},{3,2},{4,5},{5,4},{6,7},{7,6},{8,9},{9,8},{10,11... | collective-permute-start | bytes 614408 | tf_op jit(solution)/shard_map/ppermute | solution.py:250
  154.1 26.8 %collective-permute-start.40 = (bf16[8,12800]{1,0:T(8,128)(2,1)S(1)}, bf16[8,12800]{1,0:T(8,128)(2,1)S(1)}, u32[]{:S(2)}, u32[]{:S(2)}) collective-permute-start(bf16[8,12800]{1,0:T(8,128)(2,1)S(1)} %get-tuple-element.240), channel_id=1, source_target_pairs={{0,2},{1,3},{2,0},{3,1},{4,6},{5,7},{6,4},{7,5},{8,10},{9,11},{10,... | collective-permute-start | bytes 614408 | tf_op jit(solution)/shard_map/ppermute | solution.py:244
  155.0 25.8 %collective-permute-start.41 = (bf16[8,12800]{1,0:T(8,128)(2,1)S(1)}, bf16[8,12800]{1,0:T(8,128)(2,1)S(1)}, u32[]{:S(2)}, u32[]{:S(2)}) collective-permute-start(bf16[8,12800]{1,0:T(8,128)(2,1)S(1)} %get-tuple-element.239), channel_id=1, source_target_pairs={{0,4},{1,5},{2,6},{3,7},{4,0},{5,1},{6,2},{7,3},{8,12},{9,13},{10,... | collective-permute-start | bytes 614408 | tf_op jit(solution)/shard_map/ppermute | solution.py:244
  157.2 23.7 %collective-permute-start.42 = (bf16[8,12800]{1,0:T(8,128)(2,1)S(1)}, bf16[8,12800]{1,0:T(8,128)(2,1)S(1)}, u32[]{:S(2)}, u32[]{:S(2)}) collective-permute-start(bf16[8,12800]{1,0:T(8,128)(2,1)S(1)} %get-tuple-element.238), channel_id=1, source_target_pairs={{0,6},{1,7},{2,4},{3,5},{4,2},{5,3},{6,0},{7,1},{8,14},{9,15},{10,... | collective-permute-start | bytes 614408 | tf_op jit(solution)/shard_map/ppermute | solution.py:244
  180.9 8.7 %collective-permute-start.46 = (bf16[32,12800]{1,0:T(8,128)(2,1)}, bf16[32,12800]{1,0:T(8,128)(2,1)}, u32[]{:S(2)}, u32[]{:S(2)}) collective-permute-start(bf16[32,12800]{1,0:T(8,128)(2,1)} %get-tuple-element.153), channel_id=1, source_target_pairs={{0,1},{1,0},{2,3},{3,2},{4,5},{5,4},{6,7},{7,6},{8,9},{9,8},{10,11... | collective-permute-start | bytes 2457608 | tf_op jit(solution)/shard_map/ppermute | solution.py:257
  181.7 15.5 %collective-permute-start.43 = (bf16[32,3200]{1,0:T(8,128)(2,1)S(1)}, bf16[32,3200]{1,0:T(8,128)(2,1)S(1)}, u32[]{:S(2)}, u32[]{:S(2)}) collective-permute-start(bf16[32,3200]{1,0:T(8,128)(2,1)S(1)} %multiply_convert_fusion.2.refs_0_), channel_id=1, source_target_pairs={{0,2},{1,3},{2,0},{3,1},{4,6},{5,7},{6,4},{7,5},{8,10},{9,11},{10,... | collective-permute-start | bytes 614408 | tf_op jit(solution)/shard_map/ppermute | solution.py:244
  181.7 16.8 %collective-permute-start.44 = (bf16[32,3200]{1,0:T(8,128)(2,1)S(1)}, bf16[32,3200]{1,0:T(8,128)(2,1)}, u32[]{:S(2)}, u32[]{:S(2)}) collective-permute-start(bf16[32,3200]{1,0:T(8,128)(2,1)S(1)} %multiply_convert_fusion.2.refs_0_), channel_id=1, source_target_pairs={{0,4},{1,5},{2,6},{3,7},{4,0},{5,1},{6,2},{7,3},{8,12},{9,13},{10,... | collective-permute-start | bytes 614408 | tf_op jit(solution)/shard_map/ppermute | solution.py:244
  186.5 6.1 %collective-permute-start.50 = (bf16[32,1024]{1,0:T(8,128)(2,1)S(1)}, bf16[32,1024]{1,0:T(8,128)(2,1)S(1)}, u32[]{:S(2)}, u32[]{:S(2)}) collective-permute-start(bf16[32,1024]{1,0:T(8,128)(2,1)S(1)} %get-tuple-element.253), channel_id=1, source_target_pairs={{0,8},{8,16},{16,24},{24,0},{1,9},{9,17},{17,25},{25,1},{2,10},{10... | collective-permute-start | bytes 196616 | tf_op jit(solution)/shard_map/ppermute | solution.py:376
  188.0 6.1 %collective-permute-start.51 = (bf16[32,1024]{1,0:T(8,128)(2,1)S(1)}, bf16[32,1024]{1,0:T(8,128)(2,1)S(1)}, u32[]{:S(2)}, u32[]{:S(2)}) collective-permute-start(bf16[32,1024]{1,0:T(8,128)(2,1)S(1)} %get-tuple-element.252), channel_id=1, source_target_pairs={{0,16},{8,24},{16,0},{24,8},{1,17},{9,25},{17,1},{25,9},{2,18},{10... | collective-permute-start | bytes 196616 | tf_op jit(solution)/shard_map/ppermute | solution.py:376
  192.6 9.9 %collective-permute-start.45 = (bf16[32,3200]{1,0:T(8,128)(2,1)S(1)}, bf16[32,3200]{1,0:T(8,128)(2,1)S(1)}, u32[]{:S(2)}, u32[]{:S(2)}) collective-permute-start(bf16[32,3200]{1,0:T(8,128)(2,1)S(1)} %multiply_convert_fusion.2.refs_0_), channel_id=1, source_target_pairs={{0,6},{1,7},{2,4},{3,5},{4,2},{5,3},{6,0},{7,1},{8,14},{9,15},{10,... | collective-permute-start | bytes 614408 | tf_op jit(solution)/shard_map/ppermute | solution.py:244
  194.1 11.2 %collective-permute-start.47 = (bf16[8,12800]{1,0:T(8,128)(2,1)S(1)}, bf16[8,12800]{1,0:T(8,128)(2,1)S(1)}, u32[]{:S(2)}, u32[]{:S(2)}) collective-permute-start(bf16[8,12800]{1,0:T(8,128)(2,1)S(1)} %get-tuple-element.237), channel_id=1, source_target_pairs={{0,2},{1,3},{2,0},{3,1},{4,6},{5,7},{6,4},{7,5},{8,10},{9,11},{10,... | collective-permute-start | bytes 614408 | tf_op jit(solution)/shard_map/ppermute | solution.py:244
  194.1 23.7 %collective-permute-start.48 = (bf16[8,12800]{1,0:T(8,128)(2,1)S(1)}, bf16[8,12800]{1,0:T(8,128)(2,1)S(1)}, u32[]{:S(2)}, u32[]{:S(2)}) collective-permute-start(bf16[8,12800]{1,0:T(8,128)(2,1)S(1)} %get-tuple-element.236), channel_id=1, source_target_pairs={{0,4},{1,5},{2,6},{3,7},{4,0},{5,1},{6,2},{7,3},{8,12},{9,13},{10,... | collective-permute-start | bytes 614408 | tf_op jit(solution)/shard_map/ppermute | solution.py:244
  197.1 20.7 %collective-permute-start.49 = (bf16[8,12800]{1,0:T(8,128)(2,1)S(1)}, bf16[8,12800]{1,0:T(8,128)(2,1)S(1)}, u32[]{:S(2)}, u32[]{:S(2)}) collective-permute-start(bf16[8,12800]{1,0:T(8,128)(2,1)S(1)} %get-tuple-element.235), channel_id=1, source_target_pairs={{0,6},{1,7},{2,4},{3,5},{4,2},{5,3},{6,0},{7,1},{8,14},{9,15},{10,... | collective-permute-start | bytes 614408 | tf_op jit(solution)/shard_map/ppermute | solution.py:244
  218.5 4.9 %collective-permute-start.53 = (bf16[32,3200]{1,0:T(8,128)(2,1)S(1)}, bf16[32,3200]{1,0:T(8,128)(2,1)S(1)}, u32[]{:S(2)}, u32[]{:S(2)}) collective-permute-start(bf16[32,3200]{1,0:T(8,128)(2,1)S(1)} %multiply_convert_fusion.2.refs_0_), channel_id=1, source_target_pairs={{0,1},{1,0},{2,3},{3,2},{4,5},{5,4},{6,7},{7,6},{8,9},{9,8},{10,11... | collective-permute-start | bytes 614408 | tf_op jit(solution)/shard_map/ppermute | solution.py:250
  218.6 6.1 %collective-permute-start.54 = (bf16[32,3200]{1,0:T(8,128)(2,1)S(1)}, bf16[32,3200]{1,0:T(8,128)(2,1)S(1)}, u32[]{:S(2)}, u32[]{:S(2)}) collective-permute-start(bf16[32,3200]{1,0:T(8,128)(2,1)S(1)} %collective-permute-done.43.refs_1_), channel_id=1, source_target_pairs={{0,1},{1,0},{2,3},{3,2},{4,5},{5,4},{6,7},{7,6},{8,9},{9,8},{10,11... | collective-permute-start | bytes 614408 | tf_op jit(solution)/shard_map/ppermute | solution.py:250
  219.1 7.0 %collective-permute-start.55 = (bf16[32,3200]{1,0:T(8,128)(2,1)}, bf16[32,3200]{1,0:T(8,128)(2,1)S(1)}, u32[]{:S(2)}, u32[]{:S(2)}) collective-permute-start(bf16[32,3200]{1,0:T(8,128)(2,1)} %collective-permute-done.44.refs_2_), channel_id=1, source_target_pairs={{0,1},{1,0},{2,3},{3,2},{4,5},{5,4},{6,7},{7,6},{8,9},{9,8},{10,11... | collective-permute-start | bytes 614408 | tf_op jit(solution)/shard_map/ppermute | solution.py:250
  219.1 6.9 %collective-permute-start.56 = (bf16[32,3200]{1,0:T(8,128)(2,1)S(1)}, bf16[32,3200]{1,0:T(8,128)(2,1)S(1)}, u32[]{:S(2)}, u32[]{:S(2)}) collective-permute-start(bf16[32,3200]{1,0:T(8,128)(2,1)S(1)} %copy-done.20), channel_id=1, source_target_pairs={{0,1},{1,0},{2,3},{3,2},{4,5},{5,4},{6,7},{7,6},{8,9},{9,8},{10,11... | collective-permute-start | bytes 614408 | tf_op jit(solution)/shard_map/ppermute | solution.py:250
  219.6 24.8 %collective-permute-start.57 = (bf16[32,3200]{1,0:T(8,128)(2,1)S(1)}, bf16[32,3200]{1,0:T(8,128)(2,1)}, u32[]{:S(2)}, u32[]{:S(2)}) collective-permute-start(bf16[32,3200]{1,0:T(8,128)(2,1)S(1)} %multiply_convert_fusion.refs_0_), channel_id=1, source_target_pairs={{0,2},{1,3},{2,0},{3,1},{4,6},{5,7},{6,4},{7,5},{8,10},{9,11},{10,... | collective-permute-start | bytes 614408 | tf_op jit(solution)/shard_map/ppermute | solution.py:244
  223.4 21.1 %collective-permute-start.58 = (bf16[32,3200]{1,0:T(8,128)(2,1)S(1)}, bf16[32,3200]{1,0:T(8,128)(2,1)}, u32[]{:S(2)}, u32[]{:S(2)}) collective-permute-start(bf16[32,3200]{1,0:T(8,128)(2,1)S(1)} %multiply_convert_fusion.refs_0_), channel_id=1, source_target_pairs={{0,4},{1,5},{2,6},{3,7},{4,0},{5,1},{6,2},{7,3},{8,12},{9,13},{10,... | collective-permute-start | bytes 614408 | tf_op jit(solution)/shard_map/ppermute | solution.py:244
  224.7 19.8 %collective-permute-start.59 = (bf16[32,3200]{1,0:T(8,128)(2,1)S(1)}, bf16[32,3200]{1,0:T(8,128)(2,1)S(1)}, u32[]{:S(2)}, u32[]{:S(2)}) collective-permute-start(bf16[32,3200]{1,0:T(8,128)(2,1)S(1)} %multiply_convert_fusion.refs_0_), channel_id=1, source_target_pairs={{0,6},{1,7},{2,4},{3,5},{4,2},{5,3},{6,0},{7,1},{8,14},{9,15},{10,... | collective-permute-start | bytes 614408 | tf_op jit(solution)/shard_map/ppermute | solution.py:244
  244.9 4.9 %collective-permute-start.60 = (bf16[32,3200]{1,0:T(8,128)(2,1)S(1)}, bf16[32,3200]{1,0:T(8,128)(2,1)S(1)}, u32[]{:S(2)}, u32[]{:S(2)}) collective-permute-start(bf16[32,3200]{1,0:T(8,128)(2,1)S(1)} %multiply_convert_fusion.refs_0_), channel_id=1, source_target_pairs={{0,1},{1,0},{2,3},{3,2},{4,5},{5,4},{6,7},{7,6},{8,9},{9,8},{10,11... | collective-permute-start | bytes 614408 | tf_op jit(solution)/shard_map/ppermute | solution.py:250
  245.5 6.5 %collective-permute-start.61 = (bf16[32,3200]{1,0:T(8,128)(2,1)}, bf16[32,3200]{1,0:T(8,128)(2,1)S(1)}, u32[]{:S(2)}, u32[]{:S(2)}) collective-permute-start(bf16[32,3200]{1,0:T(8,128)(2,1)} %collective-permute-done.57.refs_1_), channel_id=1, source_target_pairs={{0,1},{1,0},{2,3},{3,2},{4,5},{5,4},{6,7},{7,6},{8,9},{9,8},{10,11... | collective-permute-start | bytes 614408 | tf_op jit(solution)/shard_map/ppermute | solution.py:250
  245.5 7.8 %collective-permute-start.62 = (bf16[32,3200]{1,0:T(8,128)(2,1)}, bf16[32,3200]{1,0:T(8,128)(2,1)S(1)}, u32[]{:S(2)}, u32[]{:S(2)}) collective-permute-start(bf16[32,3200]{1,0:T(8,128)(2,1)} %collective-permute-done.58.refs_2_), channel_id=1, source_target_pairs={{0,1},{1,0},{2,3},{3,2},{4,5},{5,4},{6,7},{7,6},{8,9},{9,8},{10,11... | collective-permute-start | bytes 614408 | tf_op jit(solution)/shard_map/ppermute | solution.py:250
  246.0 7.4 %collective-permute-start.63 = (bf16[32,3200]{1,0:T(8,128)(2,1)S(1)}, bf16[32,3200]{1,0:T(8,128)(2,1)S(1)}, u32[]{:S(2)}, u32[]{:S(2)}) collective-permute-start(bf16[32,3200]{1,0:T(8,128)(2,1)S(1)} %collective-permute-done.59.refs_3_), channel_id=1, source_target_pairs={{0,1},{1,0},{2,3},{3,2},{4,5},{5,4},{6,7},{7,6},{8,9},{9,8},{10,11... | collective-permute-start | bytes 614408 | tf_op jit(solution)/shard_map/ppermute | solution.py:250
  248.9 22.9 %collective-permute-start.65 = (bf16[32,3200]{1,0:T(8,128)(2,1)S(1)}, bf16[32,3200]{1,0:T(8,128)(2,1)S(1)}, u32[]{:S(2)}, u32[]{:S(2)}) collective-permute-start(bf16[32,3200]{1,0:T(8,128)(2,1)S(1)} %get-tuple-element.234), channel_id=1, source_target_pairs={{0,2},{1,3},{2,0},{3,1},{4,6},{5,7},{6,4},{7,5},{8,10},{9,11},{10,... | collective-permute-start | bytes 614408 | tf_op jit(solution)/shard_map/ppermute | solution.py:244
  249.8 22.0 %collective-permute-start.66 = (bf16[32,3200]{1,0:T(8,128)(2,1)S(1)}, bf16[32,3200]{1,0:T(8,128)(2,1)S(1)}, u32[]{:S(2)}, u32[]{:S(2)}) collective-permute-start(bf16[32,3200]{1,0:T(8,128)(2,1)S(1)} %get-tuple-element.233), channel_id=1, source_target_pairs={{0,4},{1,5},{2,6},{3,7},{4,0},{5,1},{6,2},{7,3},{8,12},{9,13},{10,... | collective-permute-start | bytes 614408 | tf_op jit(solution)/shard_map/ppermute | solution.py:244
  251.9 19.8 %collective-permute-start.67 = (bf16[32,3200]{1,0:T(8,128)(2,1)S(1)}, bf16[32,3200]{1,0:T(8,128)(2,1)S(1)}, u32[]{:S(2)}, u32[]{:S(2)}) collective-permute-start(bf16[32,3200]{1,0:T(8,128)(2,1)S(1)} %get-tuple-element.232), channel_id=1, source_target_pairs={{0,6},{1,7},{2,4},{3,5},{4,2},{5,3},{6,0},{7,1},{8,14},{9,15},{10,... | collective-permute-start | bytes 614408 | tf_op jit(solution)/shard_map/ppermute | solution.py:244
  274.6 11.1 %collective-permute-start.69 = (bf16[32,3200]{1,0:T(8,128)(2,1)S(1)}, bf16[32,3200]{1,0:T(8,128)(2,1)S(1)}, u32[]{:S(2)}, u32[]{:S(2)}) collective-permute-start(bf16[32,3200]{1,0:T(8,128)(2,1)S(1)} %get-tuple-element.231), channel_id=1, source_target_pairs={{0,2},{1,3},{2,0},{3,1},{4,6},{5,7},{6,4},{7,5},{8,10},{9,11},{10,... | collective-permute-start | bytes 614408 | tf_op jit(solution)/shard_map/ppermute | solution.py:244
  274.7 17.7 %collective-permute-start.70 = (bf16[32,3200]{1,0:T(8,128)(2,1)S(1)}, bf16[32,3200]{1,0:T(8,128)(2,1)S(1)}, u32[]{:S(2)}, u32[]{:S(2)}) collective-permute-start(bf16[32,3200]{1,0:T(8,128)(2,1)S(1)} %get-tuple-element.230), channel_id=1, source_target_pairs={{0,4},{1,5},{2,6},{3,7},{4,0},{5,1},{6,2},{7,3},{8,12},{9,13},{10,... | collective-permute-start | bytes 614408 | tf_op jit(solution)/shard_map/ppermute | solution.py:244
  277.7 14.7 %collective-permute-start.71 = (bf16[32,3200]{1,0:T(8,128)(2,1)S(1)}, bf16[32,3200]{1,0:T(8,128)(2,1)S(1)}, u32[]{:S(2)}, u32[]{:S(2)}) collective-permute-start(bf16[32,3200]{1,0:T(8,128)(2,1)S(1)} %get-tuple-element.229), channel_id=1, source_target_pairs={{0,6},{1,7},{2,4},{3,5},{4,2},{5,3},{6,0},{7,1},{8,14},{9,15},{10,... | collective-permute-start | bytes 614408 | tf_op jit(solution)/shard_map/ppermute | solution.py:244
  (68 other events, 552.2 us)

commit v8 on v7

--- a/solution.py
+++ b/solution.py
@@ -50,7 +50,7 @@
 
 
 def each_rows(total, body):
-    step = 16 if total % 16 == 0 else total
+    step = 32 if total % 32 == 0 else total
 
     def run(i, _):
         body(pl.ds(pl.multiple_of(i * step, step), step))
@@ -59,13 +59,17 @@
     lax.fori_loop(0, total // step, run, 0)
 
 
+def block_start(total, rows, j):
+    return pl.multiple_of(jnp.minimum(j * rows, total - rows), 16)
+
+
 def fetch(source, held, sems, j):
     count, rows = held.shape[:2]
 
     @pl.when(j < count)
     def _():
-        start = pl.multiple_of(j * rows, 16)
-        pltpu.make_async_copy(source.at[pl.ds(start, rows)], held.at[j], sems.at[j]).start()
+        part = source.at[pl.ds(block_start(source.shape[0], rows, j), rows)]
+        pltpu.make_async_copy(part, held.at[j], sems.at[j]).start()
 
 
 def arrive(source, held, sems, j):
@@ -84,35 +88,35 @@
     fetch(late, second, second_sems, 0)
     rows[...] = laid(pieces)
     total[...] = jnp.zeros_like(total)
-    tile = tile_of(rows.shape[1], 640)
+    size = first.shape[1]
+    width = rows.shape[1]
+    tile = min(1280, width)
+    spans = [(k, min(tile, width - k)) for k in range(0, width, tile)]
 
     def block(j, _):
         arrive(early, first, first_sems, j)
         fetch(early, first, first_sems, j + 1)
         pre[...] = times_transposed(rows[...], first[j])
+        repeated = j * size - jnp.minimum(j * size, early.shape[0] - size)
 
         def act(sel):
             u = pre[sel, :]
             if ahead:
+                fresh = lax.broadcasted_iota(jnp.int32, u.shape, 1) >= repeated
                 cumul = 0.5 * (1.0 + lax.erf(u * 0.7071067811865476))
                 dense = jnp.exp(-0.5 * u * u) * 0.3989422804014327
-                hidden[sel, :] = (u * cumul).astype(jnp.bfloat16)
-                slope[j, sel, :] = cumul + u * dense
+                hidden[sel, :] = jnp.where(fresh, u * cumul, 0.0).astype(jnp.bfloat16)
+                slope[j, sel, :] = jnp.where(fresh, cumul + u * dense, 0.0)
             else:
                 hidden[sel, :] = (u * slope[j, sel, :]).astype(jnp.bfloat16)
 
         each_rows(pre.shape[0], act)
         arrive(late, second, second_sems, j)
         fetch(late, second, second_sems, j + 1)
-
-        def columns(k, _):
-            sel = pl.ds(pl.multiple_of(k * tile, 128), tile)
-            total[:, sel] += jnp.dot(
-                hidden[...], second[j, :, sel], preferred_element_type=jnp.float32
+        for k, length in spans:
+            total[:, k : k + length] += jnp.dot(
+                hidden[...], second[j, :, k : k + length], preferred_element_type=jnp.float32
             )
-            return 0
-
-        lax.fori_loop(0, rows.shape[1] // tile, columns, 0)
         return 0
 
     lax.fori_loop(0, first.shape[0], block, 0)
@@ -123,13 +127,12 @@
 
 def project_kernel(count, *refs):
     pieces = refs[:count]
-    weight, upstream, projected, near, far, held, rows, pre, delta, sems = refs[count:]
+    weight, upstream, projected, delta, held, rows, pre, sems = refs[count:]
     for j in range(3):
         fetch(weight, held, sems, j)
     rows[...] = laid(pieces)
     pre[...] = jnp.zeros_like(pre)
     chunk = held.shape[1]
-    half = near.shape[0]
 
     def ahead(j, _):
         arrive(weight, held, sems, j)
@@ -150,7 +153,16 @@
 
     each_rows(pre.shape[0], act)
 
+
+def project_back_kernel(delta, weight, near, far, held, sems):
+    for j in range(3):
+        fetch(weight, held, sems, j)
+    chunk = held.shape[1]
+    half = near.shape[0]
+
     def behind(j, _):
+        arrive(weight, held, sems, j)
+        fetch(weight, held, sems, j + 3)
         sel = pl.ds(pl.multiple_of(j * chunk, 128), chunk)
         back = times_transposed(delta[...], held[j]).astype(jnp.bfloat16)
         near[:, sel] = back[:half]
@@ -171,8 +183,8 @@
 def vision_pass(pieces, early, late, slope=None):
     rows = sum(p.shape[0] for p in pieces)
     units, width = early.shape
-    size = max(t for t in range(16, 401, 16) if units % t == 0)
-    blocks = units // size
+    size = min(256, units)
+    blocks = -(-units // size)
     given = [] if slope is None else [slope]
     slopes = [jax.ShapeDtypeStruct((blocks, rows, size), jnp.float32)] * (1 - len(given))
     return pl.pallas_call(
@@ -201,6 +213,14 @@
     )(*pieces, early, late, *given)
 
 
+def weight_cost(rows, depth, units):
+    return pl.CostEstimate(
+        flops=2 * rows * depth * units,
+        bytes_accessed=2 * depth * units + 4 * rows * (depth + units),
+        transcendentals=2 * rows * units,
+    )
+
+
 def project(pieces, weight, upstream):
     rows = sum(p.shape[0] for p in pieces)
     depth, units = weight.shape
@@ -208,23 +228,35 @@
     return pl.pallas_call(
         functools.partial(project_kernel, len(pieces)),
         in_specs=whole_blocks(len(pieces)) + [pl.BlockSpec(memory_space=pl.ANY)] + whole_blocks(1),
-        out_specs=whole_blocks(3),
-        out_shape=[jax.ShapeDtypeStruct((rows, units), jnp.bfloat16)]
-        + [jax.ShapeDtypeStruct((rows // 2, depth), jnp.bfloat16)] * 2,
+        out_specs=whole_blocks(2),
+        out_shape=[jax.ShapeDtypeStruct((rows, units), jnp.bfloat16)] * 2,
         scratch_shapes=[
             pltpu.VMEM((depth // size, size, units), jnp.bfloat16),
             pltpu.VMEM((rows, depth), jnp.bfloat16),
             pltpu.VMEM((rows, units), jnp.float32),
-            pltpu.VMEM((rows, units), jnp.bfloat16),
             pltpu.SemaphoreType.DMA((depth // size,)),
         ],
         compiler_params=settings(),
-        cost_estimate=pl.CostEstimate(
-            flops=4 * rows * depth * units,
-            bytes_accessed=2 * depth * units + 4 * rows * (depth + units),
-            transcendentals=2 * rows * units,
-        ),
+        cost_estimate=weight_cost(rows, depth, units),
     )(*pieces, weight, upstream)
+
+
+def project_back(delta, weight):
+    rows = delta.shape[0]
+    depth, units = weight.shape
+    size = tile_of(depth, 1280)
+    return pl.pallas_call(
+        project_back_kernel,
+        in_specs=whole_blocks(1) + [pl.BlockSpec(memory_space=pl.ANY)],
+        out_specs=whole_blocks(2),
+        out_shape=[jax.ShapeDtypeStruct((rows // 2, depth), jnp.bfloat16)] * 2,
+        scratch_shapes=[
+            pltpu.VMEM((depth // size, size, units), jnp.bfloat16),
+            pltpu.SemaphoreType.DMA((depth // size,)),
+        ],
+        compiler_params=settings(),
+        cost_estimate=weight_cost(rows, depth, units),
+    )(delta, weight)
 
 
 class Direct:
@@ -252,14 +284,15 @@
             return [jnp.concatenate(mine + other, 0)]
         return mine + other
 
-    def send(self, near, far):
+    def combine(self, near, far):
         rows = near.shape[0] // self.places
         got = lax.ppermute(far, "tp", self.pairs)
         both = near.astype(jnp.float32) + got.astype(jnp.float32)
         cut = [both[k * rows : (k + 1) * rows] for k in range(self.places)]
-        return cut[:1] + [
-            self.shift(cut[k].astype(jnp.bfloat16), k) for k in range(1, self.places)
-        ]
+        return cut[:1] + [c.astype(jnp.bfloat16) for c in cut[1:]]
+
+    def send(self, cut):
+        return cut[:1] + [self.shift(cut[k], k) for k in range(1, self.places)]
 
     def summed(self, terms):
         return sum([t.astype(jnp.float32) for t in terms[1:]], terms[0])
@@ -346,25 +379,42 @@
     near_b, far_b, slope_b = vision_pass(patches_b, early, late)
     near_b, far_b, rail_a = tied((near_b, far_b, rail_a))
     patches_a = moves.gathered(rail_a)
-    terms_b = moves.send(near_b, far_b)
+    terms_b = moves.send(moves.combine(near_b, far_b))
     near_a, far_a, slope_a = vision_pass(patches_a, early, late)
     near_a, far_a, terms_b, picked = tied((near_a, far_a, terms_b, picked))
-    terms_a = moves.send(near_a, far_a)
     mixed_b, *stats_b = merge(1, moves.summed(terms_b))
     rail_b = moves.spread(mixed_b)
-    rail_b, terms_a = tied((rail_b, terms_a))
+    near_a, far_a, mixed_b = tied((near_a, far_a, mixed_b))
+    terms_a = moves.send(moves.combine(near_a, far_a))
+    merged_b = moves.gathered(rail_b)
+    projected_b, delta_b = project(merged_b, proj_weight, grad_of(picked, 1))
+    projected_b, delta_b, terms_a = tied((projected_b, delta_b, terms_a))
     mixed_a, *stats_a = merge(0, moves.summed(terms_a))
     rail_a = moves.spread(mixed_a)
-    merged_b = moves.gathered(rail_b)
-    projected_b, near_b, far_b = project(merged_b, proj_weight, grad_of(picked, 1))
+    delta_b, mixed_a = tied((delta_b, mixed_a))
+    near_b, far_b = project_back(delta_b, proj_weight)
     near_b, far_b, rail_a = tied((near_b, far_b, rail_a))
+    terms_b = moves.send(moves.combine(near_b, far_b))
     merged_a = moves.gathered(rail_a)
-    terms_b = moves.send(near_b, far_b)
-    projected_a, near_a, far_a = project(merged_a, proj_weight, grad_of(picked, 0))
-    near_a, far_a, terms_b, projected_a, projected_b = tied(
-        (near_a, far_a, terms_b, projected_a, projected_b)
-    )
-    terms_a = moves.send(near_a, far_a)
+    projected_a, delta_a = project(merged_a, proj_weight, grad_of(picked, 0))
+    projected_a, delta_a, terms_b = tied((projected_a, delta_a, terms_b))
+    own_b, scaled_b = unmerge(moves.summed(terms_b), *stats_b)
+    rail_b = moves.spread(scaled_b)
+    delta_a, scaled_b = tied((delta_a, scaled_b))
+    near_a, far_a = project_back(delta_a, proj_weight)
+    near_a, far_a, rail_b = tied((near_a, far_a, rail_b))
+    terms_a = moves.send(moves.combine(near_a, far_a))
+    grad_out_b = moves.gathered(rail_b)
+    near_b, far_b = vision_pass(grad_out_b, late, early, slope_b)
+    near_b, far_b, terms_a, projected_a, projected_b = tied(
+        (near_b, far_b, terms_a, projected_a, projected_b)
+    )
+    own_a, scaled_a = unmerge(moves.summed(terms_a), *stats_a)
+    rail_a = moves.spread(scaled_a)
+    near_b, far_b, scaled_a, projected_a, projected_b = tied(
+        (near_b, far_b, scaled_a, projected_a, projected_b)
+    )
+    cut_b = moves.combine(near_b, far_b)
 
     projected = jnp.concatenate(
         [moves.by_rank(projected_a, size), moves.by_rank(projected_b, size)], 1
@@ -385,19 +435,12 @@
         ).astype(jnp.bfloat16)
         return jnp.where(jnp.any(picks, 1, keepdims=True), placed, text)
 
-    own_b, scaled_b = unmerge(moves.summed(terms_b), *stats_b)
-    rail_b = moves.spread(scaled_b)
-    rail_b, terms_a, arrived = tied((rail_b, terms_a, arrived))
-    own_a, scaled_a = unmerge(moves.summed(terms_a), *stats_a)
-    rail_a = moves.spread(scaled_a)
-    grad_out_b = moves.gathered(rail_b)
-    near_b, far_b = vision_pass(grad_out_b, late, early, slope_b)
-    near_b, far_b, rail_a = tied((near_b, far_b, rail_a))
+    cut_b, rail_a, arrived = tied((cut_b, rail_a, arrived))
+    terms_b = moves.send(cut_b)
     grad_out_a = moves.gathered(rail_a)
-    terms_b = moves.send(near_b, far_b)
     near_a, far_a = vision_pass(grad_out_a, late, early, slope_a)
     near_a, far_a, terms_b, arrived = tied((near_a, far_a, terms_b, arrived))
-    terms_a = moves.send(near_a, far_a)
+    terms_a = moves.send(moves.combine(near_a, far_a))
     normed_b = moves.summed(terms_b)
     terms_a, seq_embed, normed_b = tied((terms_a, embed(text_embed, arrived), normed_b))
     normed_a = moves.summed(terms_a)

time: 296 us -> 310 us (1.047)
  Pallas kernels: 115 us -> 132 us
  waiting for transfers between devices: 64 us -> 52.6 us
  starting transfers between devices: 78.6 us -> 84.5 us
    pallas_call x0 -> x2, Pallas kernels: none -> 26.1 us  [project_back(): pl.pallas_call(project_back_kernel, in_specs=whole_blocks(1) + [pl.BlockS...]
    pallas_call x2, Pallas kernels: 42.9 us -> 23.6 us  [project(): pl.pallas_call(functools.partial(project_kernel, len(pieces)), in_specs=w...]
    ppermute x36, waiting for transfers between devices: 54 us -> 38 us  [shift(): return lax.ppermute(block, 'tp', pairs)]
    pallas_call x4, Pallas kernels: 71.8 us -> 82 us  [vision_pass(): pl.pallas_call(functools.partial(vision_kernel, len(pieces), slope is Non...]
    ppermute x36, starting transfers between devices: 61.6 us -> 68.2 us  [shift(): return lax.ppermute(block, 'tp', pairs)]
  transfers between devices with their start and end apart: 72 -> 72, of which waited for: 16 -> 17; matrix products, arithmetic and copies ran while one was open for 7% -> 7% of each run, Pallas kernels for 39% -> 43%
where the time goes in v8:
time: 310 us; the launch traced here: 309 us
  Pallas kernels  132 us (43%)
  starting transfers between devices  84.5 us (27%)
  waiting for transfers between devices  52.6 us (17%)
  other arithmetic  20.3 us (7%)
  local copies, waits for them, and re-layouts  15.9 us (5%)
    pallas_call x4, Pallas kernels, vision_pass(): pl.pallas_call(functools.partial(vision_kernel, len(pieces), slope is Non...  82 us
    ppermute x36, starting transfers between devices, shift(): return lax.ppermute(block, 'tp', pairs)  68.2 us
    ppermute x36, waiting for transfers between devices, shift(): return lax.ppermute(block, 'tp', pairs)  38 us
    pallas_call x2, Pallas kernels, project_back(): pl.pallas_call(project_back_kernel, in_specs=whole_blocks(1) + [pl.BlockS...  26.1 us
    pallas_call x2, Pallas kernels, project(): pl.pallas_call(functools.partial(project_kernel, len(pieces)), in_specs=w...  23.6 us
    another operation x7, other arithmetic  8.85 us
    ppermute x6, waiting for transfers between devices, combine(): got = lax.ppermute(far, 'tp', self.pairs)  7.89 us
  transfers between devices with their start and end apart: 72, of which 17 were waited for; matrix products, arithmetic and copies ran while one was open for 7% of the time, Pallas kernels for 43%

profile of v8, /device:TPU:0, one launch (start us, length us, event | category | flops | bytes accessed | tf_op | source)
XLA Modules:
  0.0 308.9 jit_solution(13007042068933436010)
XLA Ops:
  0.7 1.3 convert_reduce_fusion.1
  2.0 1.3 fusion.25
  4.6 3.1 %collective-permute-start = (bf16[32,3200]{1,0:T(8,128)(2,1)S(1)}, bf16[32,3200]{1,0:T(8,128)(2,1)S(1)}, u32[]{:S(2)}, u32[]{:S(2)}) collective-permute-start(bf16[32,3200]{1,0:T(8,128)(2,1)S(1)} %get-tuple-element.113.refs_0_), channel_id=1, source_target_pairs={{0,2},{1,3},{2,0},{3,1},{4,6},{5,7},{6,4},{7,5},{8,10},{9,11},{10,... | collective-permute-start | bytes 614408 | tf_op jit(solution)/shard_map/ppermute | solution.py:276
  7.7 2.6 collective-permute-start.1
  12.4 2.7 collective-permute-start.3
  15.6 1.4 collective-permute-done.3
  17.0 2.4 collective-permute-start.5
  19.4 3.2 %collective-permute-done.5 = bf16[32,1024]{1,0:T(8,128)(2,1)S(1)} collective-permute-done((bf16[32,1024]{1,0:T(8,128)(2,1)S(1)}, bf16[32,1024]{1,0:T(8,128)(2,1)S(1)}, u32[]{:S(2)}, u32[]{:S(2)}) %collective-permute-start.5) | collective-permute-done | bytes 65568 | tf_op jit(solution)/shard_map/ppermute | solution.py:357
  22.6 2.9 collective-permute-done.1.refs_2_
  26.5 3.5 %collective-permute-start.10 = (bf16[32,3200]{1,0:T(8,128)(2,1)S(1)}, bf16[32,3200]{1,0:T(8,128)(2,1)S(1)}, u32[]{:S(2)}, u32[]{:S(2)}) collective-permute-start(bf16[32,3200]{1,0:T(8,128)(2,1)S(1)} %get-tuple-element.120.refs_0_), channel_id=1, source_target_pairs={{0,2},{1,3},{2,0},{3,1},{4,6},{5,7},{6,4},{7,5},{8,10},{9,11},{10,... | collective-permute-start | bytes 614408 | tf_op jit(solution)/shard_map/ppermute | solution.py:276
  30.0 1.4 collective-permute-start.11
  31.5 1.4 collective-permute-start.12
  33.6 20.9 %shard_map.113 = (bf16[128,3200]{1,0:T(8,128)(2,1)}, bf16[128,3200]{1,0:T(8,128)(2,1)}, f32[7,256,256]{2,1,0:T(8,128)}) custom-call(bf16[32,3200]{1,0:T(8,128)(2,1)} %copy-done.11, bf16[32,3200]{1,0:T(8,128)(2,1)} %copy-done.17, bf16[32,3200]{1,0:T(8,128)(2,1)} %collective-permute-done.1.refs_2_, bf16[32,3200]{1,0:T(8,128)(2,1)} %collective-permute-done.2.refs_3_, ...), custom_call_target="tpu_custom_call" | custom-call | flops 5242880000 | bytes 25395200 | tf_op jit(solution)/shard_map/pallas_call | solution.py:190
  55.8 1.7 collective-permute-done.17
  57.5 1.3 fusion.55
  59.7 2.3 collective-permute-start.19
  62.0 1.4 collective-permute-start.20
  64.8 20.9 %shard_map.114 = (bf16[128,3200]{1,0:T(8,128)(2,1)}, bf16[128,3200]{1,0:T(8,128)(2,1)}, f32[7,256,256]{2,1,0:T(8,128)}) custom-call(bf16[32,3200]{1,0:T(8,128)(2,1)} %copy-done.9, bf16[32,3200]{1,0:T(8,128)(2,1)} %copy-done.18, bf16[32,3200]{1,0:T(8,128)(2,1)} %copy-done.19, bf16[32,3200]{1,0:T(8,128)(2,1)} %copy-done.20, bf16[32,3200]{1,0:T(8,128)(2,1)} %copy-done.28, ...), custom_call_target="tpu_custom_call" | custom-call | flops 5242880000 | bytes 25395200 | tf_op jit(solution)/shard_map/pallas_call | solution.py:190
  87.4 3.0 collective-permute-start.22
  90.4 1.4 collective-permute-start.23
  92.5 6.6 %collective-permute-done.21.refs_1_ = bf16[8,12800]{1,0:T(8,128)(2,1)} collective-permute-done((bf16[8,12800]{1,0:T(8,128)(2,1)S(1)}, bf16[8,12800]{1,0:T(8,128)(2,1)}, u32[]{:S(2)}, u32[]{:S(2)}) %collective-permute-start.21) | collective-permute-done | bytes 204832 | tf_op jit(solution)/shard_map/ppermute | solution.py:276
  99.1 6.1 %collective-permute-done.22.refs_2_ = bf16[8,12800]{1,0:T(8,128)(2,1)} collective-permute-done((bf16[8,12800]{1,0:T(8,128)(2,1)S(1)}, bf16[8,12800]{1,0:T(8,128)(2,1)}, u32[]{:S(2)}, u32[]{:S(2)}) %collective-permute-start.22) | collective-permute-done | bytes 204832 | tf_op jit(solution)/shard_map/ppermute | solution.py:276
  105.7 1.6 fusion.56
  108.2 4.1 %collective-permute-start.29 = (bf16[32,3200]{1,0:T(8,128)(2,1)}, bf16[32,3200]{1,0:T(8,128)(2,1)S(1)}, u32[]{:S(2)}, u32[]{:S(2)}) collective-permute-start(bf16[32,3200]{1,0:T(8,128)(2,1)} %get-tuple-element.271), channel_id=1, source_target_pairs={{0,2},{1,3},{2,0},{3,1},{4,6},{5,7},{6,4},{7,5},{8,10},{9,11},{10,... | collective-permute-start | bytes 614408 | tf_op jit(solution)/shard_map/ppermute | solution.py:276
  113.3 1.5 collective-permute-start.31
  116.0 11.8 %shard_map.115 = (bf16[64,1024]{1,0:T(8,128)(2,1)}, bf16[64,1024]{1,0:T(8,128)(2,1)}) custom-call(bf16[8,12800]{1,0:T(8,128)(2,1)} %copy-done.13, bf16[8,12800]{1,0:T(8,128)(2,1)} %collective-permute-done.21.refs_1_, bf16[8,12800]{1,0:T(8,128)(2,1)} %collective-permute-done.22.refs_2_, bf16[8,12800]{1,0:T(8,128)(2,1)} %collective-permute-done.23.refs_3_, ...), custom_call_target="tpu_custom_call" | custom-call | flops 1677721600 | bytes 29753344 | tf_op jit(solution)/shard_map/pallas_call | solution.py:228
  127.9 2.3 collective-permute-done.30
  130.2 1.3 fusion.63
  132.5 4.3 %collective-permute-start.32 = (bf16[8,12800]{1,0:T(8,128)(2,1)S(1)}, bf16[8,12800]{1,0:T(8,128)(2,1)S(1)}, u32[]{:S(2)}, u32[]{:S(2)}) collective-permute-start(bf16[8,12800]{1,0:T(8,128)(2,1)S(1)} %multiply_convert_fusion.4.refs_0_), channel_id=1, source_target_pairs={{0,2},{1,3},{2,0},{3,1},{4,6},{5,7},{6,4},{7,5},{8,10},{9,11},{10,... | collective-permute-start | bytes 614408 | tf_op jit(solution)/shard_map/ppermute | solution.py:276
  137.9 1.4 collective-permute-start.34
  139.3 13.1 %shard_map.116 = (bf16[32,12800]{1,0:T(8,128)(2,1)}, bf16[32,12800]{1,0:T(8,128)(2,1)}) custom-call(bf16[64,1024]{1,0:T(8,128)(2,1)} %get-tuple-element.151.delta, bf16[12800,1024]{1,0:T(8,128)(2,1)} %weight.3), custom_call_target="tpu_custom_call" | custom-call | flops 1677721600 | bytes 29753344 | tf_op jit(solution)/shard_map/pallas_call | solution.py:248
  152.4 2.3 collective-permute-done.33.refs_2_
  155.7 2.0 collective-permute-done.39
  157.8 2.5 fusion.57
  160.3 3.7 %collective-permute-start.40 = (bf16[8,12800]{1,0:T(8,128)(2,1)S(1)}, bf16[8,12800]{1,0:T(8,128)(2,1)S(1)}, u32[]{:S(2)}, u32[]{:S(2)}) collective-permute-start(bf16[8,12800]{1,0:T(8,128)(2,1)S(1)} %get-tuple-element.268), channel_id=1, source_target_pairs={{0,2},{1,3},{2,0},{3,1},{4,6},{5,7},{6,4},{7,5},{8,10},{9,11},{10,... | collective-permute-start | bytes 614408 | tf_op jit(solution)/shard_map/ppermute | solution.py:276
  165.1 1.5 collective-permute-start.42
  167.8 11.8 %shard_map.117 = (bf16[64,1024]{1,0:T(8,128)(2,1)}, bf16[64,1024]{1,0:T(8,128)(2,1)}) custom-call(bf16[8,12800]{1,0:T(8,128)(2,1)} %copy-done.14, bf16[8,12800]{1,0:T(8,128)(2,1)} %copy-done.21, bf16[8,12800]{1,0:T(8,128)(2,1)} %collective-permute-done.33.refs_2_, bf16[8,12800]{1,0:T(8,128)(2,1)} %collective-permute-done.34.refs_3_, ...), custom_call_target="tpu_custom_call" | custom-call | flops 1677721600 | bytes 29753344 | tf_op jit(solution)/shard_map/pallas_call | solution.py:228
  182.4 1.3 fusion.62
  184.0 3.9 %collective-permute-start.43 = (bf16[32,3200]{1,0:T(8,128)(2,1)S(1)}, bf16[32,3200]{1,0:T(8,128)(2,1)S(1)}, u32[]{:S(2)}, u32[]{:S(2)}) collective-permute-start(bf16[32,3200]{1,0:T(8,128)(2,1)S(1)} %multiply_convert_fusion.2.refs_0_), channel_id=1, source_target_pairs={{0,2},{1,3},{2,0},{3,1},{4,6},{5,7},{6,4},{7,5},{8,10},{9,11},{10,... | collective-permute-start | bytes 614408 | tf_op jit(solution)/shard_map/ppermute | solution.py:276
  189.0 1.4 collective-permute-start.45
  190.4 13.1 %shard_map.118 = (bf16[32,12800]{1,0:T(8,128)(2,1)}, bf16[32,12800]{1,0:T(8,128)(2,1)}) custom-call(bf16[64,1024]{1,0:T(8,128)(2,1)} %get-tuple-element.167.delta, bf16[12800,1024]{1,0:T(8,128)(2,1)} %weight.3), custom_call_target="tpu_custom_call" | custom-call | flops 1677721600 | bytes 29753344 | tf_op jit(solution)/shard_map/pallas_call | solution.py:248
  203.5 2.1 collective-permute-done.44.refs_2_
  206.8 1.7 collective-permute-done.50
  208.5 1.3 fusion.58
  209.9 2.9 collective-permute-start.51
  213.9 1.5 collective-permute-start.53
  216.1 20.1 %shard_map.119 = (bf16[128,3200]{1,0:T(8,128)(2,1)}, bf16[128,3200]{1,0:T(8,128)(2,1)}) custom-call(bf16[32,3200]{1,0:T(8,128)(2,1)} %copy-done.12, bf16[32,3200]{1,0:T(8,128)(2,1)} %copy-done.22, bf16[32,3200]{1,0:T(8,128)(2,1)} %copy-done.23, bf16[32,3200]{1,0:T(8,128)(2,1)} %copy-done.24, bf16[32,3200]{1,0:T(8,128)(2,1)} %copy-done.27, ...), custom_call_target="tpu_custom_call" | custom-call | flops 5242880000 | bytes 25395200 | tf_op jit(solution)/shard_map/pallas_call | solution.py:190
  238.2 2.0 collective-permute-start.56
  240.2 1.5 collective-permute-start.57
  243.4 1.5 collective-permute-start.58
  245.8 1.5 collective-permute-start.59
  247.3 1.6 fusion.59
  248.9 1.5 collective-permute-start.60
  251.3 2.0 collective-permute-done.60
  253.3 2.7 collective-permute-done.56.refs_2_
  257.3 4.3 %collective-permute-start.65 = (bf16[32,3200]{1,0:T(8,128)(2,1)}, bf16[32,3200]{1,0:T(8,128)(2,1)S(1)}, u32[]{:S(2)}, u32[]{:S(2)}) collective-permute-start(bf16[32,3200]{1,0:T(8,128)(2,1)} %get-tuple-element.201), channel_id=1, source_target_pairs={{0,2},{1,3},{2,0},{3,1},{4,6},{5,7},{6,4},{7,5},{8,10},{9,11},{10,... | collective-permute-start | bytes 614408 | tf_op jit(solution)/shard_map/ppermute | solution.py:276
  262.9 1.4 collective-permute-start.67
  265.0 20.1 %shard_map.120 = (bf16[128,3200]{1,0:T(8,128)(2,1)}, bf16[128,3200]{1,0:T(8,128)(2,1)}) custom-call(bf16[32,3200]{1,0:T(8,128)(2,1)} %copy-done.10, bf16[32,3200]{1,0:T(8,128)(2,1)} %collective-permute-done.55.refs_1_, bf16[32,3200]{1,0:T(8,128)(2,1)} %collective-permute-done.56.refs_2_, bf16[32,3200]{1,0:T(8,128)(2,1)} %collective-permute-done.57.refs_3_, ...), custom_call_target="tpu_custom_call" | custom-call | flops 5242880000 | bytes 25395200 | tf_op jit(solution)/shard_map/pallas_call | solution.py:190
  285.3 2.4 collective-permute-done.68
  288.9 2.2 collective-permute-start.70
  291.1 1.4 collective-permute-start.71
  292.5 2.2 fusion
  294.7 4.3 %collective-permute-done.69 = bf16[32,3200]{1,0:T(8,128)(2,1)S(1)} collective-permute-done((bf16[32,3200]{1,0:T(8,128)(2,1)S(1)}, bf16[32,3200]{1,0:T(8,128)(2,1)S(1)}, u32[]{:S(2)}, u32[]{:S(2)}) %collective-permute-start.69) | collective-permute-done | bytes 204832 | tf_op jit(solution)/shard_map/ppermute | solution.py:276
  298.9 7.6 %collective-permute-done.70 = bf16[32,3200]{1,0:T(8,128)(2,1)S(1)} collective-permute-done((bf16[32,3200]{1,0:T(8,128)(2,1)S(1)}, bf16[32,3200]{1,0:T(8,128)(2,1)S(1)}, u32[]{:S(2)}, u32[]{:S(2)}) %collective-permute-start.70) | collective-permute-done | bytes 204832 | tf_op jit(solution)/shard_map/ppermute | solution.py:276
  (303 shorter events, 39.7 us)
Async XLA Ops:
  4.6 18.0 %collective-permute-start = (bf16[32,3200]{1,0:T(8,128)(2,1)S(1)}, bf16[32,3200]{1,0:T(8,128)(2,1)S(1)}, u32[]{:S(2)}, u32[]{:S(2)}) collective-permute-start(bf16[32,3200]{1,0:T(8,128)(2,1)S(1)} %get-tuple-element.113.refs_0_), channel_id=1, source_target_pairs={{0,2},{1,3},{2,0},{3,1},{4,6},{5,7},{6,4},{7,5},{8,10},{9,11},{10,... | collective-permute-start | bytes 614408 | tf_op jit(solution)/shard_map/ppermute | solution.py:276
  7.7 17.8 %collective-permute-start.1 = (bf16[32,3200]{1,0:T(8,128)(2,1)S(1)}, bf16[32,3200]{1,0:T(8,128)(2,1)}, u32[]{:S(2)}, u32[]{:S(2)}) collective-permute-start(bf16[32,3200]{1,0:T(8,128)(2,1)S(1)} %get-tuple-element.113.refs_0_), channel_id=1, source_target_pairs={{0,4},{1,5},{2,6},{3,7},{4,0},{5,1},{6,2},{7,3},{8,12},{9,13},{10,... | collective-permute-start | bytes 614408 | tf_op jit(solution)/shard_map/ppermute | solution.py:276
  10.3 15.2 %collective-permute-start.2 = (bf16[32,3200]{1,0:T(8,128)(2,1)S(1)}, bf16[32,3200]{1,0:T(8,128)(2,1)}, u32[]{:S(2)}, u32[]{:S(2)}) collective-permute-start(bf16[32,3200]{1,0:T(8,128)(2,1)S(1)} %get-tuple-element.113.refs_0_), channel_id=1, source_target_pairs={{0,6},{1,7},{2,4},{3,5},{4,2},{5,3},{6,0},{7,1},{8,14},{9,15},{10,... | collective-permute-start | bytes 614408 | tf_op jit(solution)/shard_map/ppermute | solution.py:276
  17.0 5.6 %collective-permute-start.5 = (bf16[32,1024]{1,0:T(8,128)(2,1)S(1)}, bf16[32,1024]{1,0:T(8,128)(2,1)S(1)}, u32[]{:S(2)}, u32[]{:S(2)}) collective-permute-start(bf16[32,1024]{1,0:T(8,128)(2,1)S(1)} %get-tuple-element.285), channel_id=1, source_target_pairs={{0,8},{8,16},{16,24},{24,0},{1,9},{9,17},{17,25},{25,1},{2,10},{10... | collective-permute-start | bytes 196616 | tf_op jit(solution)/shard_map/ppermute | solution.py:357
  25.5 6.0 %collective-permute-start.7 = (bf16[32,3200]{1,0:T(8,128)(2,1)S(1)}, bf16[32,3200]{1,0:T(8,128)(2,1)S(1)}, u32[]{:S(2)}, u32[]{:S(2)}) collective-permute-start(bf16[32,3200]{1,0:T(8,128)(2,1)S(1)} %collective-permute-done.refs_1_), channel_id=1, source_target_pairs={{0,1},{1,0},{2,3},{3,2},{4,5},{5,4},{6,7},{7,6},{8,9},{9,8},{10,11... | collective-permute-start | bytes 614408 | tf_op jit(solution)/shard_map/ppermute | solution.py:282
  26.0 6.8 %collective-permute-start.8 = (bf16[32,3200]{1,0:T(8,128)(2,1)}, bf16[32,3200]{1,0:T(8,128)(2,1)S(1)}, u32[]{:S(2)}, u32[]{:S(2)}) collective-permute-start(bf16[32,3200]{1,0:T(8,128)(2,1)} %collective-permute-done.1.refs_2_), channel_id=1, source_target_pairs={{0,1},{1,0},{2,3},{3,2},{4,5},{5,4},{6,7},{7,6},{8,9},{9,8},{10,11... | collective-permute-start | bytes 614408 | tf_op jit(solution)/shard_map/ppermute | solution.py:282
  26.0 6.8 %collective-permute-start.9 = (bf16[32,3200]{1,0:T(8,128)(2,1)}, bf16[32,3200]{1,0:T(8,128)(2,1)S(1)}, u32[]{:S(2)}, u32[]{:S(2)}) collective-permute-start(bf16[32,3200]{1,0:T(8,128)(2,1)} %collective-permute-done.2.refs_3_), channel_id=1, source_target_pairs={{0,1},{1,0},{2,3},{3,2},{4,5},{5,4},{6,7},{7,6},{8,9},{9,8},{10,11... | collective-permute-start | bytes 614408 | tf_op jit(solution)/shard_map/ppermute | solution.py:282
  26.5 28.0 %collective-permute-start.10 = (bf16[32,3200]{1,0:T(8,128)(2,1)S(1)}, bf16[32,3200]{1,0:T(8,128)(2,1)S(1)}, u32[]{:S(2)}, u32[]{:S(2)}) collective-permute-start(bf16[32,3200]{1,0:T(8,128)(2,1)S(1)} %get-tuple-element.120.refs_0_), channel_id=1, source_target_pairs={{0,2},{1,3},{2,0},{3,1},{4,6},{5,7},{6,4},{7,5},{8,10},{9,11},{10,... | collective-permute-start | bytes 614408 | tf_op jit(solution)/shard_map/ppermute | solution.py:276
  30.0 24.5 %collective-permute-start.11 = (bf16[32,3200]{1,0:T(8,128)(2,1)S(1)}, bf16[32,3200]{1,0:T(8,128)(2,1)S(1)}, u32[]{:S(2)}, u32[]{:S(2)}) collective-permute-start(bf16[32,3200]{1,0:T(8,128)(2,1)S(1)} %get-tuple-element.120.refs_0_), channel_id=1, source_target_pairs={{0,4},{1,5},{2,6},{3,7},{4,0},{5,1},{6,2},{7,3},{8,12},{9,13},{10,... | collective-permute-start | bytes 614408 | tf_op jit(solution)/shard_map/ppermute | solution.py:276
  31.5 23.1 %collective-permute-start.12 = (bf16[32,3200]{1,0:T(8,128)(2,1)S(1)}, bf16[32,3200]{1,0:T(8,128)(2,1)S(1)}, u32[]{:S(2)}, u32[]{:S(2)}) collective-permute-start(bf16[32,3200]{1,0:T(8,128)(2,1)S(1)} %get-tuple-element.120.refs_0_), channel_id=1, source_target_pairs={{0,6},{1,7},{2,4},{3,5},{4,2},{5,3},{6,0},{7,1},{8,14},{9,15},{10,... | collective-permute-start | bytes 614408 | tf_op jit(solution)/shard_map/ppermute | solution.py:276
  54.7 5.0 %collective-permute-start.13 = (bf16[32,3200]{1,0:T(8,128)(2,1)S(1)}, bf16[32,3200]{1,0:T(8,128)(2,1)S(1)}, u32[]{:S(2)}, u32[]{:S(2)}) collective-permute-start(bf16[32,3200]{1,0:T(8,128)(2,1)S(1)} %get-tuple-element.120.refs_0_), channel_id=1, source_target_pairs={{0,1},{1,0},{2,3},{3,2},{4,5},{5,4},{6,7},{7,6},{8,9},{9,8},{10,11... | collective-permute-start | bytes 614408 | tf_op jit(solution)/shard_map/ppermute | solution.py:282
  55.2 6.8 %collective-permute-start.14 = (bf16[32,3200]{1,0:T(8,128)(2,1)S(1)}, bf16[32,3200]{1,0:T(8,128)(2,1)S(1)}, u32[]{:S(2)}, u32[]{:S(2)}) collective-permute-start(bf16[32,3200]{1,0:T(8,128)(2,1)S(1)} %collective-permute-done.10.refs_1_), channel_id=1, source_target_pairs={{0,1},{1,0},{2,3},{3,2},{4,5},{5,4},{6,7},{7,6},{8,9},{9,8},{10,11... | collective-permute-start | bytes 614408 | tf_op jit(solution)/shard_map/ppermute | solution.py:282
  55.3 8.2 %collective-permute-start.15 = (bf16[32,3200]{1,0:T(8,128)(2,1)S(1)}, bf16[32,3200]{1,0:T(8,128)(2,1)S(1)}, u32[]{:S(2)}, u32[]{:S(2)}) collective-permute-start(bf16[32,3200]{1,0:T(8,128)(2,1)S(1)} %collective-permute-done.11.refs_2_), channel_id=1, source_target_pairs={{0,1},{1,0},{2,3},{3,2},{4,5},{5,4},{6,7},{7,6},{8,9},{9,8},{10,11... | collective-permute-start | bytes 614408 | tf_op jit(solution)/shard_map/ppermute | solution.py:282
  55.7 7.8 %collective-permute-start.16 = (bf16[32,3200]{1,0:T(8,128)(2,1)S(1)}, bf16[32,3200]{1,0:T(8,128)(2,1)S(1)}, u32[]{:S(2)}, u32[]{:S(2)}) collective-permute-start(bf16[32,3200]{1,0:T(8,128)(2,1)S(1)} %collective-permute-done.12.refs_3_), channel_id=1, source_target_pairs={{0,1},{1,0},{2,3},{3,2},{4,5},{5,4},{6,7},{7,6},{8,9},{9,8},{10,11... | collective-permute-start | bytes 614408 | tf_op jit(solution)/shard_map/ppermute | solution.py:282
  58.9 26.8 %collective-permute-start.18 = (bf16[32,3200]{1,0:T(8,128)(2,1)S(1)}, bf16[32,3200]{1,0:T(8,128)(2,1)S(1)}, u32[]{:S(2)}, u32[]{:S(2)}) collective-permute-start(bf16[32,3200]{1,0:T(8,128)(2,1)S(1)} %get-tuple-element.274), channel_id=1, source_target_pairs={{0,2},{1,3},{2,0},{3,1},{4,6},{5,7},{6,4},{7,5},{8,10},{9,11},{10,... | collective-permute-start | bytes 614408 | tf_op jit(solution)/shard_map/ppermute | solution.py:276
  59.7 26.1 %collective-permute-start.19 = (bf16[32,3200]{1,0:T(8,128)(2,1)S(1)}, bf16[32,3200]{1,0:T(8,128)(2,1)S(1)}, u32[]{:S(2)}, u32[]{:S(2)}) collective-permute-start(bf16[32,3200]{1,0:T(8,128)(2,1)S(1)} %get-tuple-element.273), channel_id=1, source_target_pairs={{0,4},{1,5},{2,6},{3,7},{4,0},{5,1},{6,2},{7,3},{8,12},{9,13},{10,... | collective-permute-start | bytes 614408 | tf_op jit(solution)/shard_map/ppermute | solution.py:276
  62.0 23.7 %collective-permute-start.20 = (bf16[32,3200]{1,0:T(8,128)(2,1)S(1)}, bf16[32,3200]{1,0:T(8,128)(2,1)S(1)}, u32[]{:S(2)}, u32[]{:S(2)}) collective-permute-start(bf16[32,3200]{1,0:T(8,128)(2,1)S(1)} %get-tuple-element.272), channel_id=1, source_target_pairs={{0,6},{1,7},{2,4},{3,5},{4,2},{5,3},{6,0},{7,1},{8,14},{9,15},{10,... | collective-permute-start | bytes 614408 | tf_op jit(solution)/shard_map/ppermute | solution.py:276
  87.2 18.5 %collective-permute-start.28 = (bf16[128,3200]{1,0:T(8,128)(2,1)S(1)}, bf16[128,3200]{1,0:T(8,128)(2,1)}, u32[]{:S(2)}, u32[]{:S(2)}) collective-permute-start(bf16[128,3200]{1,0:T(8,128)(2,1)S(1)} %copy-done.54), channel_id=1, source_target_pairs={{0,1},{1,0},{2,3},{3,2},{4,5},{5,4},{6,7},{7,6},{8,9},{9,8},{10,11... | collective-permute-start | bytes 2457608 | tf_op jit(solution)/shard_map/ppermute | solution.py:289
  87.3 11.7 %collective-permute-start.21 = (bf16[8,12800]{1,0:T(8,128)(2,1)S(1)}, bf16[8,12800]{1,0:T(8,128)(2,1)}, u32[]{:S(2)}, u32[]{:S(2)}) collective-permute-start(bf16[8,12800]{1,0:T(8,128)(2,1)S(1)} %multiply_convert_fusion.5.refs_0_), channel_id=1, source_target_pairs={{0,2},{1,3},{2,0},{3,1},{4,6},{5,7},{6,4},{7,5},{8,10},{9,11},{10,... | collective-permute-start | bytes 614408 | tf_op jit(solution)/shard_map/ppermute | solution.py:276
  87.4 17.8 %collective-permute-start.22 = (bf16[8,12800]{1,0:T(8,128)(2,1)S(1)}, bf16[8,12800]{1,0:T(8,128)(2,1)}, u32[]{:S(2)}, u32[]{:S(2)}) collective-permute-start(bf16[8,12800]{1,0:T(8,128)(2,1)S(1)} %multiply_convert_fusion.5.refs_0_), channel_id=1, source_target_pairs={{0,4},{1,5},{2,6},{3,7},{4,0},{5,1},{6,2},{7,3},{8,12},{9,13},{10,... | collective-permute-start | bytes 614408 | tf_op jit(solution)/shard_map/ppermute | solution.py:276
  90.4 14.8 %collective-permute-start.23 = (bf16[8,12800]{1,0:T(8,128)(2,1)S(1)}, bf16[8,12800]{1,0:T(8,128)(2,1)}, u32[]{:S(2)}, u32[]{:S(2)}) collective-permute-start(bf16[8,12800]{1,0:T(8,128)(2,1)S(1)} %multiply_convert_fusion.5.refs_0_), channel_id=1, source_target_pairs={{0,6},{1,7},{2,4},{3,5},{4,2},{5,3},{6,0},{7,1},{8,14},{9,15},{10,... | collective-permute-start | bytes 614408 | tf_op jit(solution)/shard_map/ppermute | solution.py:276
  91.8 20.5 %collective-permute-start.24 = (bf16[8,12800]{1,0:T(8,128)(2,1)S(1)}, bf16[8,12800]{1,0:T(8,128)(2,1)}, u32[]{:S(2)}, u32[]{:S(2)}) collective-permute-start(bf16[8,12800]{1,0:T(8,128)(2,1)S(1)} %multiply_convert_fusion.5.refs_0_), channel_id=1, source_target_pairs={{0,1},{1,0},{2,3},{3,2},{4,5},{5,4},{6,7},{7,6},{8,9},{9,8},{10,11... | collective-permute-start | bytes 614408 | tf_op jit(solution)/shard_map/ppermute | solution.py:282
  99.1 14.2 %collective-permute-start.25 = (bf16[8,12800]{1,0:T(8,128)(2,1)}, bf16[8,12800]{1,0:T(8,128)(2,1)S(1)}, u32[]{:S(2)}, u32[]{:S(2)}) collective-permute-start(bf16[8,12800]{1,0:T(8,128)(2,1)} %collective-permute-done.21.refs_1_), channel_id=1, source_target_pairs={{0,1},{1,0},{2,3},{3,2},{4,5},{5,4},{6,7},{7,6},{8,9},{9,8},{10,11... | collective-permute-start | bytes 614408 | tf_op jit(solution)/shard_map/ppermute | solution.py:282
  105.2 10.8 %collective-permute-start.26 = (bf16[8,12800]{1,0:T(8,128)(2,1)}, bf16[8,12800]{1,0:T(8,128)(2,1)}, u32[]{:S(2)}, u32[]{:S(2)}) collective-permute-start(bf16[8,12800]{1,0:T(8,128)(2,1)} %collective-permute-done.22.refs_2_), channel_id=1, source_target_pairs={{0,1},{1,0},{2,3},{3,2},{4,5},{5,4},{6,7},{7,6},{8,9},{9,8},{10,11... | collective-permute-start | bytes 614408 | tf_op jit(solution)/shard_map/ppermute | solution.py:282
  105.2 10.8 %collective-permute-start.27 = (bf16[8,12800]{1,0:T(8,128)(2,1)}, bf16[8,12800]{1,0:T(8,128)(2,1)}, u32[]{:S(2)}, u32[]{:S(2)}) collective-permute-start(bf16[8,12800]{1,0:T(8,128)(2,1)} %collective-permute-done.23.refs_3_), channel_id=1, source_target_pairs={{0,1},{1,0},{2,3},{3,2},{4,5},{5,4},{6,7},{7,6},{8,9},{9,8},{10,11... | collective-permute-start | bytes 614408 | tf_op jit(solution)/shard_map/ppermute | solution.py:282
  108.2 19.7 %collective-permute-start.29 = (bf16[32,3200]{1,0:T(8,128)(2,1)}, bf16[32,3200]{1,0:T(8,128)(2,1)S(1)}, u32[]{:S(2)}, u32[]{:S(2)}) collective-permute-start(bf16[32,3200]{1,0:T(8,128)(2,1)} %get-tuple-element.271), channel_id=1, source_target_pairs={{0,2},{1,3},{2,0},{3,1},{4,6},{5,7},{6,4},{7,5},{8,10},{9,11},{10,... | collective-permute-start | bytes 614408 | tf_op jit(solution)/shard_map/ppermute | solution.py:276
  112.3 18.0 %collective-permute-start.30 = (bf16[32,3200]{1,0:T(8,128)(2,1)}, bf16[32,3200]{1,0:T(8,128)(2,1)}, u32[]{:S(2)}, u32[]{:S(2)}) collective-permute-start(bf16[32,3200]{1,0:T(8,128)(2,1)} %get-tuple-element.270), channel_id=1, source_target_pairs={{0,4},{1,5},{2,6},{3,7},{4,0},{5,1},{6,2},{7,3},{8,12},{9,13},{10,... | collective-permute-start | bytes 614408 | tf_op jit(solution)/shard_map/ppermute | solution.py:276
  113.3 16.9 %collective-permute-start.31 = (bf16[32,3200]{1,0:T(8,128)(2,1)}, bf16[32,3200]{1,0:T(8,128)(2,1)}, u32[]{:S(2)}, u32[]{:S(2)}) collective-permute-start(bf16[32,3200]{1,0:T(8,128)(2,1)} %get-tuple-element.269), channel_id=1, source_target_pairs={{0,6},{1,7},{2,4},{3,5},{4,2},{5,3},{6,0},{7,1},{8,14},{9,15},{10,... | collective-permute-start | bytes 614408 | tf_op jit(solution)/shard_map/ppermute | solution.py:276
  132.5 19.8 %collective-permute-start.32 = (bf16[8,12800]{1,0:T(8,128)(2,1)S(1)}, bf16[8,12800]{1,0:T(8,128)(2,1)S(1)}, u32[]{:S(2)}, u32[]{:S(2)}) collective-permute-start(bf16[8,12800]{1,0:T(8,128)(2,1)S(1)} %multiply_convert_fusion.4.refs_0_), channel_id=1, source_target_pairs={{0,2},{1,3},{2,0},{3,1},{4,6},{5,7},{6,4},{7,5},{8,10},{9,11},{10,... | collective-permute-start | bytes 614408 | tf_op jit(solution)/shard_map/ppermute | solution.py:276
  136.8 17.8 %collective-permute-start.33 = (bf16[8,12800]{1,0:T(8,128)(2,1)S(1)}, bf16[8,12800]{1,0:T(8,128)(2,1)}, u32[]{:S(2)}, u32[]{:S(2)}) collective-permute-start(bf16[8,12800]{1,0:T(8,128)(2,1)S(1)} %multiply_convert_fusion.4.refs_0_), channel_id=1, source_target_pairs={{0,4},{1,5},{2,6},{3,7},{4,0},{5,1},{6,2},{7,3},{8,12},{9,13},{10,... | collective-permute-start | bytes 614408 | tf_op jit(solution)/shard_map/ppermute | solution.py:276
  137.9 16.7 %collective-permute-start.34 = (bf16[8,12800]{1,0:T(8,128)(2,1)S(1)}, bf16[8,12800]{1,0:T(8,128)(2,1)}, u32[]{:S(2)}, u32[]{:S(2)}) collective-permute-start(bf16[8,12800]{1,0:T(8,128)(2,1)S(1)} %multiply_convert_fusion.4.refs_0_), channel_id=1, source_target_pairs={{0,6},{1,7},{2,4},{3,5},{4,2},{5,3},{6,0},{7,1},{8,14},{9,15},{10,... | collective-permute-start | bytes 614408 | tf_op jit(solution)/shard_map/ppermute | solution.py:276
  154.7 9.4 %collective-permute-start.35 = (bf16[8,12800]{1,0:T(8,128)(2,1)S(1)}, bf16[8,12800]{1,0:T(8,128)(2,1)S(1)}, u32[]{:S(2)}, u32[]{:S(2)}) collective-permute-start(bf16[8,12800]{1,0:T(8,128)(2,1)S(1)} %multiply_convert_fusion.4.refs_0_), channel_id=1, source_target_pairs={{0,1},{1,0},{2,3},{3,2},{4,5},{5,4},{6,7},{7,6},{8,9},{9,8},{10,11... | collective-permute-start | bytes 614408 | tf_op jit(solution)/shard_map/ppermute | solution.py:282
  155.2 10.0 %collective-permute-start.36 = (bf16[8,12800]{1,0:T(8,128)(2,1)S(1)}, bf16[8,12800]{1,0:T(8,128)(2,1)S(1)}, u32[]{:S(2)}, u32[]{:S(2)}) collective-permute-start(bf16[8,12800]{1,0:T(8,128)(2,1)S(1)} %collective-permute-done.32.refs_1_), channel_id=1, source_target_pairs={{0,1},{1,0},{2,3},{3,2},{4,5},{5,4},{6,7},{7,6},{8,9},{9,8},{10,11... | collective-permute-start | bytes 614408 | tf_op jit(solution)/shard_map/ppermute | solution.py:282
  155.2 12.6 %collective-permute-start.37 = (bf16[8,12800]{1,0:T(8,128)(2,1)}, bf16[8,12800]{1,0:T(8,128)(2,1)}, u32[]{:S(2)}, u32[]{:S(2)}) collective-permute-start(bf16[8,12800]{1,0:T(8,128)(2,1)} %collective-permute-done.33.refs_2_), channel_id=1, source_target_pairs={{0,1},{1,0},{2,3},{3,2},{4,5},{5,4},{6,7},{7,6},{8,9},{9,8},{10,11... | collective-permute-start | bytes 614408 | tf_op jit(solution)/shard_map/ppermute | solution.py:282
  155.7 12.1 %collective-permute-start.38 = (bf16[8,12800]{1,0:T(8,128)(2,1)}, bf16[8,12800]{1,0:T(8,128)(2,1)}, u32[]{:S(2)}, u32[]{:S(2)}) collective-permute-start(bf16[8,12800]{1,0:T(8,128)(2,1)} %collective-permute-done.34.refs_3_), channel_id=1, source_target_pairs={{0,1},{1,0},{2,3},{3,2},{4,5},{5,4},{6,7},{7,6},{8,9},{9,8},{10,11... | collective-permute-start | bytes 614408 | tf_op jit(solution)/shard_map/ppermute | solution.py:282
  160.3 20.3 %collective-permute-start.40 = (bf16[8,12800]{1,0:T(8,128)(2,1)S(1)}, bf16[8,12800]{1,0:T(8,128)(2,1)S(1)}, u32[]{:S(2)}, u32[]{:S(2)}) collective-permute-start(bf16[8,12800]{1,0:T(8,128)(2,1)S(1)} %get-tuple-element.268), channel_id=1, source_target_pairs={{0,2},{1,3},{2,0},{3,1},{4,6},{5,7},{6,4},{7,5},{8,10},{9,11},{10,... | collective-permute-start | bytes 614408 | tf_op jit(solution)/shard_map/ppermute | solution.py:276
  164.1 17.6 %collective-permute-start.41 = (bf16[8,12800]{1,0:T(8,128)(2,1)S(1)}, bf16[8,12800]{1,0:T(8,128)(2,1)S(1)}, u32[]{:S(2)}, u32[]{:S(2)}) collective-permute-start(bf16[8,12800]{1,0:T(8,128)(2,1)S(1)} %get-tuple-element.267), channel_id=1, source_target_pairs={{0,4},{1,5},{2,6},{3,7},{4,0},{5,1},{6,2},{7,3},{8,12},{9,13},{10,... | collective-permute-start | bytes 614408 | tf_op jit(solution)/shard_map/ppermute | solution.py:276
  165.1 16.6 %collective-permute-start.42 = (bf16[8,12800]{1,0:T(8,128)(2,1)S(1)}, bf16[8,12800]{1,0:T(8,128)(2,1)S(1)}, u32[]{:S(2)}, u32[]{:S(2)}) collective-permute-start(bf16[8,12800]{1,0:T(8,128)(2,1)S(1)} %get-tuple-element.266), channel_id=1, source_target_pairs={{0,6},{1,7},{2,4},{3,5},{4,2},{5,3},{6,0},{7,1},{8,14},{9,15},{10,... | collective-permute-start | bytes 614408 | tf_op jit(solution)/shard_map/ppermute | solution.py:276
  184.0 19.5 %collective-permute-start.43 = (bf16[32,3200]{1,0:T(8,128)(2,1)S(1)}, bf16[32,3200]{1,0:T(8,128)(2,1)S(1)}, u32[]{:S(2)}, u32[]{:S(2)}) collective-permute-start(bf16[32,3200]{1,0:T(8,128)(2,1)S(1)} %multiply_convert_fusion.2.refs_0_), channel_id=1, source_target_pairs={{0,2},{1,3},{2,0},{3,1},{4,6},{5,7},{6,4},{7,5},{8,10},{9,11},{10,... | collective-permute-start | bytes 614408 | tf_op jit(solution)/shard_map/ppermute | solution.py:276
  187.9 17.7 %collective-permute-start.44 = (bf16[32,3200]{1,0:T(8,128)(2,1)S(1)}, bf16[32,3200]{1,0:T(8,128)(2,1)S(1)}, u32[]{:S(2)}, u32[]{:S(2)}) collective-permute-start(bf16[32,3200]{1,0:T(8,128)(2,1)S(1)} %multiply_convert_fusion.2.refs_0_), channel_id=1, source_target_pairs={{0,4},{1,5},{2,6},{3,7},{4,0},{5,1},{6,2},{7,3},{8,12},{9,13},{10,... | collective-permute-start | bytes 614408 | tf_op jit(solution)/shard_map/ppermute | solution.py:276
  189.0 16.6 %collective-permute-start.45 = (bf16[32,3200]{1,0:T(8,128)(2,1)S(1)}, bf16[32,3200]{1,0:T(8,128)(2,1)S(1)}, u32[]{:S(2)}, u32[]{:S(2)}) collective-permute-start(bf16[32,3200]{1,0:T(8,128)(2,1)S(1)} %multiply_convert_fusion.2.refs_0_), channel_id=1, source_target_pairs={{0,6},{1,7},{2,4},{3,5},{4,2},{5,3},{6,0},{7,1},{8,14},{9,15},{10,... | collective-permute-start | bytes 614408 | tf_op jit(solution)/shard_map/ppermute | solution.py:276
  205.7 7.1 %collective-permute-start.46 = (bf16[32,3200]{1,0:T(8,128)(2,1)S(1)}, bf16[32,3200]{1,0:T(8,128)(2,1)S(1)}, u32[]{:S(2)}, u32[]{:S(2)}) collective-permute-start(bf16[32,3200]{1,0:T(8,128)(2,1)S(1)} %multiply_convert_fusion.2.refs_0_), channel_id=1, source_target_pairs={{0,1},{1,0},{2,3},{3,2},{4,5},{5,4},{6,7},{7,6},{8,9},{9,8},{10,11... | collective-permute-start | bytes 614408 | tf_op jit(solution)/shard_map/ppermute | solution.py:282
  206.2 7.7 %collective-permute-start.47 = (bf16[32,3200]{1,0:T(8,128)(2,1)S(1)}, bf16[32,3200]{1,0:T(8,128)(2,1)S(1)}, u32[]{:S(2)}, u32[]{:S(2)}) collective-permute-start(bf16[32,3200]{1,0:T(8,128)(2,1)S(1)} %collective-permute-done.43.refs_1_), channel_id=1, source_target_pairs={{0,1},{1,0},{2,3},{3,2},{4,5},{5,4},{6,7},{7,6},{8,9},{9,8},{10,11... | collective-permute-start | bytes 614408 | tf_op jit(solution)/shard_map/ppermute | solution.py:282
  206.3 9.1 %collective-permute-start.48 = (bf16[32,3200]{1,0:T(8,128)(2,1)S(1)}, bf16[32,3200]{1,0:T(8,128)(2,1)S(1)}, u32[]{:S(2)}, u32[]{:S(2)}) collective-permute-start(bf16[32,3200]{1,0:T(8,128)(2,1)S(1)} %collective-permute-done.44.refs_2_), channel_id=1, source_target_pairs={{0,1},{1,0},{2,3},{3,2},{4,5},{5,4},{6,7},{7,6},{8,9},{9,8},{10,11... | collective-permute-start | bytes 614408 | tf_op jit(solution)/shard_map/ppermute | solution.py:282
  206.7 8.7 %collective-permute-start.49 = (bf16[32,3200]{1,0:T(8,128)(2,1)S(1)}, bf16[32,3200]{1,0:T(8,128)(2,1)S(1)}, u32[]{:S(2)}, u32[]{:S(2)}) collective-permute-start(bf16[32,3200]{1,0:T(8,128)(2,1)S(1)} %collective-permute-done.45.refs_3_), channel_id=1, source_target_pairs={{0,1},{1,0},{2,3},{3,2},{4,5},{5,4},{6,7},{7,6},{8,9},{9,8},{10,11... | collective-permute-start | bytes 614408 | tf_op jit(solution)/shard_map/ppermute | solution.py:282
  209.9 26.4 %collective-permute-start.51 = (bf16[8,12800]{1,0:T(8,128)(2,1)S(1)}, bf16[8,12800]{1,0:T(8,128)(2,1)S(1)}, u32[]{:S(2)}, u32[]{:S(2)}) collective-permute-start(bf16[8,12800]{1,0:T(8,128)(2,1)S(1)} %get-tuple-element.265), channel_id=1, source_target_pairs={{0,2},{1,3},{2,0},{3,1},{4,6},{5,7},{6,4},{7,5},{8,10},{9,11},{10,... | collective-permute-start | bytes 614408 | tf_op jit(solution)/shard_map/ppermute | solution.py:276
  212.8 23.5 %collective-permute-start.52 = (bf16[8,12800]{1,0:T(8,128)(2,1)S(1)}, bf16[8,12800]{1,0:T(8,128)(2,1)S(1)}, u32[]{:S(2)}, u32[]{:S(2)}) collective-permute-start(bf16[8,12800]{1,0:T(8,128)(2,1)S(1)} %get-tuple-element.264), channel_id=1, source_target_pairs={{0,4},{1,5},{2,6},{3,7},{4,0},{5,1},{6,2},{7,3},{8,12},{9,13},{10,... | collective-permute-start | bytes 614408 | tf_op jit(solution)/shard_map/ppermute | solution.py:276
  213.9 22.4 %collective-permute-start.53 = (bf16[8,12800]{1,0:T(8,128)(2,1)S(1)}, bf16[8,12800]{1,0:T(8,128)(2,1)S(1)}, u32[]{:S(2)}, u32[]{:S(2)}) collective-permute-start(bf16[8,12800]{1,0:T(8,128)(2,1)S(1)} %get-tuple-element.263), channel_id=1, source_target_pairs={{0,6},{1,7},{2,4},{3,5},{4,2},{5,3},{6,0},{7,1},{8,14},{9,15},{10,... | collective-permute-start | bytes 614408 | tf_op jit(solution)/shard_map/ppermute | solution.py:276
  237.0 7.9 %collective-permute-start.54 = (bf16[128,3200]{1,0:T(8,128)(2,1)}, bf16[128,3200]{1,0:T(8,128)(2,1)S(1)}, u32[]{:S(2)}, u32[]{:S(2)}) collective-permute-start(bf16[128,3200]{1,0:T(8,128)(2,1)} %get-tuple-element.190), channel_id=1, source_target_pairs={{0,1},{1,0},{2,3},{3,2},{4,5},{5,4},{6,7},{7,6},{8,9},{9,8},{10,11... | collective-permute-start | bytes 2457608 | tf_op jit(solution)/shard_map/ppermute | solution.py:289
  237.2 16.1 %collective-permute-start.55 = (bf16[32,3200]{1,0:T(8,128)(2,1)S(1)}, bf16[32,3200]{1,0:T(8,128)(2,1)}, u32[]{:S(2)}, u32[]{:S(2)}) collective-permute-start(bf16[32,3200]{1,0:T(8,128)(2,1)S(1)} %multiply_convert_fusion.refs_0_), channel_id=1, source_target_pairs={{0,2},{1,3},{2,0},{3,1},{4,6},{5,7},{6,4},{7,5},{8,10},{9,11},{10,... | collective-permute-start | bytes 614408 | tf_op jit(solution)/shard_map/ppermute | solution.py:276
  238.2 17.7 %collective-permute-start.56 = (bf16[32,3200]{1,0:T(8,128)(2,1)S(1)}, bf16[32,3200]{1,0:T(8,128)(2,1)}, u32[]{:S(2)}, u32[]{:S(2)}) collective-permute-start(bf16[32,3200]{1,0:T(8,128)(2,1)S(1)} %multiply_convert_fusion.refs_0_), channel_id=1, source_target_pairs={{0,4},{1,5},{2,6},{3,7},{4,0},{5,1},{6,2},{7,3},{8,12},{9,13},{10,... | collective-permute-start | bytes 614408 | tf_op jit(solution)/shard_map/ppermute | solution.py:276
  240.2 15.8 %collective-permute-start.57 = (bf16[32,3200]{1,0:T(8,128)(2,1)S(1)}, bf16[32,3200]{1,0:T(8,128)(2,1)}, u32[]{:S(2)}, u32[]{:S(2)}) collective-permute-start(bf16[32,3200]{1,0:T(8,128)(2,1)S(1)} %multiply_convert_fusion.refs_0_), channel_id=1, source_target_pairs={{0,6},{1,7},{2,4},{3,5},{4,2},{5,3},{6,0},{7,1},{8,14},{9,15},{10,... | collective-permute-start | bytes 614408 | tf_op jit(solution)/shard_map/ppermute | solution.py:276
  243.4 5.6 %collective-permute-start.58 = (bf16[32,1024]{1,0:T(8,128)(2,1)S(1)}, bf16[32,1024]{1,0:T(8,128)(2,1)S(1)}, u32[]{:S(2)}, u32[]{:S(2)}) collective-permute-start(bf16[32,1024]{1,0:T(8,128)(2,1)S(1)} %get-tuple-element.281), channel_id=1, source_target_pairs={{0,8},{8,16},{16,24},{24,0},{1,9},{9,17},{17,25},{25,1},{2,10},{10... | collective-permute-start | bytes 196616 | tf_op jit(solution)/shard_map/ppermute | solution.py:426
  245.8 5.4 %collective-permute-start.59 = (bf16[32,1024]{1,0:T(8,128)(2,1)S(1)}, bf16[32,1024]{1,0:T(8,128)(2,1)S(1)}, u32[]{:S(2)}, u32[]{:S(2)}) collective-permute-start(bf16[32,1024]{1,0:T(8,128)(2,1)S(1)} %get-tuple-element.280), channel_id=1, source_target_pairs={{0,16},{8,24},{16,0},{24,8},{1,17},{9,25},{17,1},{25,9},{2,18},{10... | collective-permute-start | bytes 196616 | tf_op jit(solution)/shard_map/ppermute | solution.py:426
  255.9 5.7 %collective-permute-start.61 = (bf16[32,3200]{1,0:T(8,128)(2,1)S(1)}, bf16[32,3200]{1,0:T(8,128)(2,1)S(1)}, u32[]{:S(2)}, u32[]{:S(2)}) collective-permute-start(bf16[32,3200]{1,0:T(8,128)(2,1)S(1)} %multiply_convert_fusion.refs_0_), channel_id=1, source_target_pairs={{0,1},{1,0},{2,3},{3,2},{4,5},{5,4},{6,7},{7,6},{8,9},{9,8},{10,11... | collective-permute-start | bytes 614408 | tf_op jit(solution)/shard_map/ppermute | solution.py:282
  255.9 6.9 %collective-permute-start.62 = (bf16[32,3200]{1,0:T(8,128)(2,1)}, bf16[32,3200]{1,0:T(8,128)(2,1)S(1)}, u32[]{:S(2)}, u32[]{:S(2)}) collective-permute-start(bf16[32,3200]{1,0:T(8,128)(2,1)} %collective-permute-done.55.refs_1_), channel_id=1, source_target_pairs={{0,1},{1,0},{2,3},{3,2},{4,5},{5,4},{6,7},{7,6},{8,9},{9,8},{10,11... | collective-permute-start | bytes 614408 | tf_op jit(solution)/shard_map/ppermute | solution.py:282
  256.4 7.8 %collective-permute-start.63 = (bf16[32,3200]{1,0:T(8,128)(2,1)}, bf16[32,3200]{1,0:T(8,128)(2,1)S(1)}, u32[]{:S(2)}, u32[]{:S(2)}) collective-permute-start(bf16[32,3200]{1,0:T(8,128)(2,1)} %collective-permute-done.56.refs_2_), channel_id=1, source_target_pairs={{0,1},{1,0},{2,3},{3,2},{4,5},{5,4},{6,7},{7,6},{8,9},{9,8},{10,11... | collective-permute-start | bytes 614408 | tf_op jit(solution)/shard_map/ppermute | solution.py:282
  256.5 7.7 %collective-permute-start.64 = (bf16[32,3200]{1,0:T(8,128)(2,1)}, bf16[32,3200]{1,0:T(8,128)(2,1)S(1)}, u32[]{:S(2)}, u32[]{:S(2)}) collective-permute-start(bf16[32,3200]{1,0:T(8,128)(2,1)} %collective-permute-done.57.refs_3_), channel_id=1, source_target_pairs={{0,1},{1,0},{2,3},{3,2},{4,5},{5,4},{6,7},{7,6},{8,9},{9,8},{10,11... | collective-permute-start | bytes 614408 | tf_op jit(solution)/shard_map/ppermute | solution.py:282
  257.3 27.8 %collective-permute-start.65 = (bf16[32,3200]{1,0:T(8,128)(2,1)}, bf16[32,3200]{1,0:T(8,128)(2,1)S(1)}, u32[]{:S(2)}, u32[]{:S(2)}) collective-permute-start(bf16[32,3200]{1,0:T(8,128)(2,1)} %get-tuple-element.201), channel_id=1, source_target_pairs={{0,2},{1,3},{2,0},{3,1},{4,6},{5,7},{6,4},{7,5},{8,10},{9,11},{10,... | collective-permute-start | bytes 614408 | tf_op jit(solution)/shard_map/ppermute | solution.py:276
  261.6 23.5 %collective-permute-start.66 = (bf16[32,3200]{1,0:T(8,128)(2,1)}, bf16[32,3200]{1,0:T(8,128)(2,1)S(1)}, u32[]{:S(2)}, u32[]{:S(2)}) collective-permute-start(bf16[32,3200]{1,0:T(8,128)(2,1)} %get-tuple-element.202), channel_id=1, source_target_pairs={{0,4},{1,5},{2,6},{3,7},{4,0},{5,1},{6,2},{7,3},{8,12},{9,13},{10,... | collective-permute-start | bytes 614408 | tf_op jit(solution)/shard_map/ppermute | solution.py:276
  262.9 22.3 %collective-permute-start.67 = (bf16[32,3200]{1,0:T(8,128)(2,1)S(1)}, bf16[32,3200]{1,0:T(8,128)(2,1)S(1)}, u32[]{:S(2)}, u32[]{:S(2)}) collective-permute-start(bf16[32,3200]{1,0:T(8,128)(2,1)S(1)} %get-tuple-element.203), channel_id=1, source_target_pairs={{0,6},{1,7},{2,4},{3,5},{4,2},{5,3},{6,0},{7,1},{8,14},{9,15},{10,... | collective-permute-start | bytes 614408 | tf_op jit(solution)/shard_map/ppermute | solution.py:276
  288.0 11.0 %collective-permute-start.69 = (bf16[32,3200]{1,0:T(8,128)(2,1)S(1)}, bf16[32,3200]{1,0:T(8,128)(2,1)S(1)}, u32[]{:S(2)}, u32[]{:S(2)}) collective-permute-start(bf16[32,3200]{1,0:T(8,128)(2,1)S(1)} %get-tuple-element.259), channel_id=1, source_target_pairs={{0,2},{1,3},{2,0},{3,1},{4,6},{5,7},{6,4},{7,5},{8,10},{9,11},{10,... | collective-permute-start | bytes 614408 | tf_op jit(solution)/shard_map/ppermute | solution.py:276
  288.9 17.6 %collective-permute-start.70 = (bf16[32,3200]{1,0:T(8,128)(2,1)S(1)}, bf16[32,3200]{1,0:T(8,128)(2,1)S(1)}, u32[]{:S(2)}, u32[]{:S(2)}) collective-permute-start(bf16[32,3200]{1,0:T(8,128)(2,1)S(1)} %get-tuple-element.258), channel_id=1, source_target_pairs={{0,4},{1,5},{2,6},{3,7},{4,0},{5,1},{6,2},{7,3},{8,12},{9,13},{10,... | collective-permute-start | bytes 614408 | tf_op jit(solution)/shard_map/ppermute | solution.py:276
  291.1 15.5 %collective-permute-start.71 = (bf16[32,3200]{1,0:T(8,128)(2,1)S(1)}, bf16[32,3200]{1,0:T(8,128)(2,1)S(1)}, u32[]{:S(2)}, u32[]{:S(2)}) collective-permute-start(bf16[32,3200]{1,0:T(8,128)(2,1)S(1)} %get-tuple-element.257), channel_id=1, source_target_pairs={{0,6},{1,7},{2,4},{3,5},{4,2},{5,3},{6,0},{7,1},{8,14},{9,15},{10,... | collective-permute-start | bytes 614408 | tf_op jit(solution)/shard_map/ppermute | solution.py:276
  (63 other events, 488.5 us)

commit v9 on v8

--- a/solution.py
+++ b/solution.py
@@ -83,21 +83,18 @@
         early, late, near, far, slope = refs[count : count + 5]
     else:
         early, late, slope, near, far = refs[count : count + 5]
-    first, second, rows, total, pre, hidden, first_sems, second_sems = refs[count + 5 :]
-    fetch(early, first, first_sems, 0)
-    fetch(late, second, second_sems, 0)
+    first, second, rows, pre, hidden, first_sems, second_sems = refs[count + 5 :]
+    blocks, size, width = first.shape
+    for j in range(blocks):
+        fetch(early, first, first_sems, j)
     rows[...] = laid(pieces)
-    total[...] = jnp.zeros_like(total)
-    size = first.shape[1]
-    width = rows.shape[1]
-    tile = min(1280, width)
-    spans = [(k, min(tile, width - k)) for k in range(0, width, tile)]
 
     def block(j, _):
         arrive(early, first, first_sems, j)
-        fetch(early, first, first_sems, j + 1)
+        fetch(late, second, second_sems, j)
         pre[...] = times_transposed(rows[...], first[j])
         repeated = j * size - jnp.minimum(j * size, early.shape[0] - size)
+        place = pl.ds(pl.multiple_of(j * size, min(size, 128)), size)
 
         def act(sel):
             u = pre[sel, :]
@@ -105,24 +102,29 @@
                 fresh = lax.broadcasted_iota(jnp.int32, u.shape, 1) >= repeated
                 cumul = 0.5 * (1.0 + lax.erf(u * 0.7071067811865476))
                 dense = jnp.exp(-0.5 * u * u) * 0.3989422804014327
-                hidden[sel, :] = jnp.where(fresh, u * cumul, 0.0).astype(jnp.bfloat16)
+                hidden[sel, place] = jnp.where(fresh, u * cumul, 0.0).astype(jnp.bfloat16)
                 slope[j, sel, :] = jnp.where(fresh, cumul + u * dense, 0.0)
             else:
-                hidden[sel, :] = (u * slope[j, sel, :]).astype(jnp.bfloat16)
+                hidden[sel, place] = (u * slope[j, sel, :]).astype(jnp.bfloat16)
 
         each_rows(pre.shape[0], act)
+        return 0
+
+    lax.fori_loop(0, blocks, block, 0)
+    for j in range(blocks):
         arrive(late, second, second_sems, j)
-        fetch(late, second, second_sems, j + 1)
-        for k, length in spans:
-            total[:, k : k + length] += jnp.dot(
-                hidden[...], second[j, :, k : k + length], preferred_element_type=jnp.float32
-            )
-        return 0
-
-    lax.fori_loop(0, first.shape[0], block, 0)
     half = near.shape[0]
-    near[...] = total[:half].astype(jnp.bfloat16)
-    far[...] = total[half:].astype(jnp.bfloat16)
+    tile = min(1280, width)
+    for k in range(0, width, tile):
+        span = slice(k, min(k + tile, width))
+        held = second[:, :, span]
+        both = jnp.dot(
+            hidden[...],
+            held.reshape(blocks * size, held.shape[2]),
+            preferred_element_type=jnp.float32,
+        ).astype(jnp.bfloat16)
+        near[:, span] = both[:half]
+        far[:, span] = both[half:]
 
 
 def project_kernel(count, *refs):
@@ -198,9 +200,8 @@
             pltpu.VMEM((blocks, size, width), jnp.bfloat16),
             pltpu.VMEM((blocks, size, width), jnp.bfloat16),
             pltpu.VMEM((rows, width), jnp.bfloat16),
-            pltpu.VMEM((rows, width), jnp.float32),
             pltpu.VMEM((rows, size), jnp.float32),
-            pltpu.VMEM((rows, size), jnp.bfloat16),
+            pltpu.VMEM((rows, blocks * size), jnp.bfloat16),
             pltpu.SemaphoreType.DMA((blocks,)),
             pltpu.SemaphoreType.DMA((blocks,)),
         ],
@@ -385,9 +386,12 @@
     mixed_b, *stats_b = merge(1, moves.summed(terms_b))
     rail_b = moves.spread(mixed_b)
     near_a, far_a, mixed_b = tied((near_a, far_a, mixed_b))
-    terms_a = moves.send(moves.combine(near_a, far_a))
+    cut_a, rail_b, upstream = tied(
+        (moves.combine(near_a, far_a), rail_b, [grad_of(picked, c) for c in range(chunks)])
+    )
+    terms_a = moves.send(cut_a)
     merged_b = moves.gathered(rail_b)
-    projected_b, delta_b = project(merged_b, proj_weight, grad_of(picked, 1))
+    projected_b, delta_b = project(merged_b, proj_weight, upstream[1])
     projected_b, delta_b, terms_a = tied((projected_b, delta_b, terms_a))
     mixed_a, *stats_a = merge(0, moves.summed(terms_a))
     rail_a = moves.spread(mixed_a)
@@ -396,7 +400,7 @@
     near_b, far_b, rail_a = tied((near_b, far_b, rail_a))
     terms_b = moves.send(moves.combine(near_b, far_b))
     merged_a = moves.gathered(rail_a)
-    projected_a, delta_a = project(merged_a, proj_weight, grad_of(picked, 0))
+    projected_a, delta_a = project(merged_a, proj_weight, upstream[0])
     projected_a, delta_a, terms_b = tied((projected_a, delta_a, terms_b))
     own_b, scaled_b = unmerge(moves.summed(terms_b), *stats_b)
     rail_b = moves.spread(scaled_b)

time: 310 us -> 289 us (0.932)
  Pallas kernels: 132 us -> 108 us
  starting transfers between devices: 84.5 us -> 90.1 us
  other arithmetic: 20.3 us -> 17.2 us
    pallas_call x4, Pallas kernels: 82 us -> 58.6 us  [vision_pass(): pl.pallas_call(functools.partial(vision_kernel, len(pieces), slope is Non...]
    ppermute x36, starting transfers between devices: 68.2 us -> 73.1 us  [shift(): return lax.ppermute(block, 'tp', pairs)]
    unnamed x110 -> x122, local copies, waits for them, and re-layouts: 6.05 us -> 7.92 us
  transfers between devices with their start and end apart: 72 -> 72, of which waited for: 17 -> 17; matrix products, arithmetic and copies ran while one was open for 7% -> 6% of each run, Pallas kernels for 43% -> 38%
where the time goes in v9:
time: 289 us; the launch traced here: 287 us
  Pallas kernels  108 us (37%)
  starting transfers between devices  90.1 us (31%)
  waiting for transfers between devices  51.6 us (18%)
  other arithmetic  17.2 us (6%)
  local copies, waits for them, and re-layouts  15.9 us (6%)
    ppermute x36, starting transfers between devices, shift(): return lax.ppermute(block, 'tp', pairs)  73.1 us
    pallas_call x4, Pallas kernels, vision_pass(): pl.pallas_call(functools.partial(vision_kernel, len(pieces), slope is Non...  58.6 us
    ppermute x36, waiting for transfers between devices, shift(): return lax.ppermute(block, 'tp', pairs)  37.6 us
    pallas_call x2, Pallas kernels, project_back(): pl.pallas_call(project_back_kernel, in_specs=whole_blocks(1) + [pl.BlockS...  26.1 us
    pallas_call x2, Pallas kernels, project(): pl.pallas_call(functools.partial(project_kernel, len(pieces)), in_specs=w...  23.8 us
    unnamed x122, local copies, waits for them, and re-layouts  7.92 us
    another operation x7, other arithmetic  7.68 us
    ppermute x6, waiting for transfers between devices, combine(): got = lax.ppermute(far, 'tp', self.pairs)  7.39 us
  transfers between devices with their start and end apart: 72, of which 17 were waited for; matrix products, arithmetic and copies ran while one was open for 6% of the time, Pallas kernels for 38%

profile of v9, /device:TPU:0, one launch (start us, length us, event | category | flops | bytes accessed | tf_op | source)
XLA Modules:
  0.0 287.3 jit_solution(12805176217488855925)
XLA Ops:
  0.7 1.3 convert_reduce_fusion
  2.0 1.3 fusion.18
  4.6 3.1 %collective-permute-start = (bf16[32,3200]{1,0:T(8,128)(2,1)S(1)}, bf16[32,3200]{1,0:T(8,128)(2,1)}, u32[]{:S(2)}, u32[]{:S(2)}) collective-permute-start(bf16[32,3200]{1,0:T(8,128)(2,1)S(1)} %get-tuple-element.123.refs_0_), channel_id=1, source_target_pairs={{0,2},{1,3},{2,0},{3,1},{4,6},{5,7},{6,4},{7,5},{8,10},{9,11},{10,... | collective-permute-start | bytes 614408 | tf_op jit(solution)/shard_map/ppermute | solution.py:277
  7.7 2.6 collective-permute-start.1
  12.4 2.7 collective-permute-start.3
  15.6 1.4 collective-permute-done.3
  17.0 2.4 collective-permute-start.5
  19.4 3.2 %collective-permute-done.5 = bf16[32,1024]{1,0:T(8,128)(2,1)S(1)} collective-permute-done((bf16[32,1024]{1,0:T(8,128)(2,1)S(1)}, bf16[32,1024]{1,0:T(8,128)(2,1)S(1)}, u32[]{:S(2)}, u32[]{:S(2)}) %collective-permute-start.5) | collective-permute-done | bytes 65568 | tf_op jit(solution)/shard_map/ppermute | solution.py:358
  22.6 2.9 %collective-permute-done.1.refs_2_ = bf16[32,3200]{1,0:T(8,128)(2,1)} collective-permute-done((bf16[32,3200]{1,0:T(8,128)(2,1)S(1)}, bf16[32,3200]{1,0:T(8,128)(2,1)}, u32[]{:S(2)}, u32[]{:S(2)}) %collective-permute-start.1) | collective-permute-done | bytes 204832 | tf_op jit(solution)/shard_map/ppermute | solution.py:277
  26.5 3.5 %collective-permute-start.10 = (bf16[32,3200]{1,0:T(8,128)(2,1)S(1)}, bf16[32,3200]{1,0:T(8,128)(2,1)S(1)}, u32[]{:S(2)}, u32[]{:S(2)}) collective-permute-start(bf16[32,3200]{1,0:T(8,128)(2,1)S(1)} %get-tuple-element.130.refs_0_), channel_id=1, source_target_pairs={{0,2},{1,3},{2,0},{3,1},{4,6},{5,7},{6,4},{7,5},{8,10},{9,11},{10,... | collective-permute-start | bytes 614408 | tf_op jit(solution)/shard_map/ppermute | solution.py:277
  30.0 1.7 collective-permute-start.11
  31.7 1.3 collective-permute-start.12
  33.8 14.7 %shard_map.113 = (bf16[128,3200]{1,0:T(8,128)(2,1)}, bf16[128,3200]{1,0:T(8,128)(2,1)}, f32[7,256,256]{2,1,0:T(8,128)}) custom-call(bf16[32,3200]{1,0:T(8,128)(2,1)} %copy-done.12, bf16[32,3200]{1,0:T(8,128)(2,1)} %collective-permute-done.refs_1_, bf16[32,3200]{1,0:T(8,128)(2,1)} %collective-permute-done.1.refs_2_, ...), custom_call_target="tpu_custom_call" | custom-call | flops 5242880000 | bytes 25395200 | tf_op jit(solution)/shard_map/pallas_call | solution.py:192
  49.8 1.5 collective-permute-done.17
  51.4 1.6 fusion.55
  53.0 3.3 %collective-permute-start.18 = (bf16[32,3200]{1,0:T(8,128)(2,1)S(1)}, bf16[32,3200]{1,0:T(8,128)(2,1)S(1)}, u32[]{:S(2)}, u32[]{:S(2)}) collective-permute-start(bf16[32,3200]{1,0:T(8,128)(2,1)S(1)} %get-tuple-element.294), channel_id=1, source_target_pairs={{0,2},{1,3},{2,0},{3,1},{4,6},{5,7},{6,4},{7,5},{8,10},{9,11},{10,... | collective-permute-start | bytes 614408 | tf_op jit(solution)/shard_map/ppermute | solution.py:277
  57.4 1.5 collective-permute-start.20
  60.3 14.7 %shard_map.114 = (bf16[128,3200]{1,0:T(8,128)(2,1)}, bf16[128,3200]{1,0:T(8,128)(2,1)}, f32[7,256,256]{2,1,0:T(8,128)}) custom-call(bf16[32,3200]{1,0:T(8,128)(2,1)} %copy-done.10, bf16[32,3200]{1,0:T(8,128)(2,1)} %copy-done.17, bf16[32,3200]{1,0:T(8,128)(2,1)} %collective-permute-done.11.refs_2_, bf16[32,3200]{1,0:T(8,128)(2,1)} %collective-permute-done.12.refs_3_, ...), custom_call_target="tpu_custom_call" | custom-call | flops 5242880000 | bytes 25395200 | tf_op jit(solution)/shard_map/pallas_call | solution.py:192
  76.6 2.8 collective-permute-start.22
  80.5 1.4 collective-permute-start.24
  85.0 1.3 fusion.56
  86.4 2.7 collective-permute-done.22.refs_1_
  89.1 7.9 %collective-permute-done.23.refs_2_ = bf16[8,12800]{1,0:T(8,128)(2,1)S(1)} collective-permute-done((bf16[8,12800]{1,0:T(8,128)(2,1)S(1)}, bf16[8,12800]{1,0:T(8,128)(2,1)S(1)}, u32[]{:S(2)}, u32[]{:S(2)}) %collective-permute-start.23) | collective-permute-done | bytes 204832 | tf_op jit(solution)/shard_map/ppermute | solution.py:277
  98.2 4.2 %collective-permute-start.29 = (bf16[32,3200]{1,0:T(8,128)(2,1)S(1)}, bf16[32,3200]{1,0:T(8,128)(2,1)S(1)}, u32[]{:S(2)}, u32[]{:S(2)}) collective-permute-start(bf16[32,3200]{1,0:T(8,128)(2,1)S(1)} %get-tuple-element.162), channel_id=1, source_target_pairs={{0,2},{1,3},{2,0},{3,1},{4,6},{5,7},{6,4},{7,5},{8,10},{9,11},{10,... | collective-permute-start | bytes 614408 | tf_op jit(solution)/shard_map/ppermute | solution.py:277
  102.3 1.4 collective-permute-start.30
  103.8 1.4 collective-permute-start.31
  106.5 11.8 %shard_map.115 = (bf16[64,1024]{1,0:T(8,128)(2,1)}, bf16[64,1024]{1,0:T(8,128)(2,1)}) custom-call(bf16[8,12800]{1,0:T(8,128)(2,1)} %copy-done.14, bf16[8,12800]{1,0:T(8,128)(2,1)} %copy-done.18, bf16[8,12800]{1,0:T(8,128)(2,1)} %copy-done.19, bf16[8,12800]{1,0:T(8,128)(2,1)} %copy-done.20, bf16[8,12800]{1,0:T(8,128)(2,1)} %copy-done.42, ...), custom_call_target="tpu_custom_call" | custom-call | flops 1677721600 | bytes 29753344 | tf_op jit(solution)/shard_map/pallas_call | solution.py:229
  118.3 1.7 collective-permute-done.30
  121.3 3.9 %collective-permute-start.32 = (bf16[8,12800]{1,0:T(8,128)(2,1)S(1)}, bf16[8,12800]{1,0:T(8,128)(2,1)S(1)}, u32[]{:S(2)}, u32[]{:S(2)}) collective-permute-start(bf16[8,12800]{1,0:T(8,128)(2,1)S(1)} %multiply_convert_fusion.4.refs_0_), channel_id=1, source_target_pairs={{0,2},{1,3},{2,0},{3,1},{4,6},{5,7},{6,4},{7,5},{8,10},{9,11},{10,... | collective-permute-start | bytes 614408 | tf_op jit(solution)/shard_map/ppermute | solution.py:277
  126.2 1.4 collective-permute-start.34
  127.6 13.1 %shard_map.116 = (bf16[32,12800]{1,0:T(8,128)(2,1)}, bf16[32,12800]{1,0:T(8,128)(2,1)}) custom-call(bf16[64,1024]{1,0:T(8,128)(2,1)} %get-tuple-element.170.delta, bf16[12800,1024]{1,0:T(8,128)(2,1)} %weight.3), custom_call_target="tpu_custom_call" | custom-call | flops 1677721600 | bytes 29753344 | tf_op jit(solution)/shard_map/pallas_call | solution.py:249
  140.7 2.0 collective-permute-done.33.refs_2_
  143.9 1.7 collective-permute-done.39
  145.6 1.3 fusion.57
  147.0 2.9 %collective-permute-start.40 = (bf16[8,12800]{1,0:T(8,128)(2,1)S(1)}, bf16[8,12800]{1,0:T(8,128)(2,1)S(1)}, u32[]{:S(2)}, u32[]{:S(2)}) collective-permute-start(bf16[8,12800]{1,0:T(8,128)(2,1)S(1)} %get-tuple-element.288), channel_id=1, source_target_pairs={{0,2},{1,3},{2,0},{3,1},{4,6},{5,7},{6,4},{7,5},{8,10},{9,11},{10,... | collective-permute-start | bytes 614408 | tf_op jit(solution)/shard_map/ppermute | solution.py:277
  151.0 1.5 collective-permute-start.42
  153.9 12.0 %shard_map.117 = (bf16[64,1024]{1,0:T(8,128)(2,1)}, bf16[64,1024]{1,0:T(8,128)(2,1)}) custom-call(bf16[8,12800]{1,0:T(8,128)(2,1)} %copy-done.15, bf16[8,12800]{1,0:T(8,128)(2,1)} %copy-done.22, bf16[8,12800]{1,0:T(8,128)(2,1)} %copy-done.24, bf16[8,12800]{1,0:T(8,128)(2,1)} %copy-done.26, bf16[8,12800]{1,0:T(8,128)(2,1)} %copy-done.29, ...), custom_call_target="tpu_custom_call" | custom-call | flops 1677721600 | bytes 29753344 | tf_op jit(solution)/shard_map/pallas_call | solution.py:229
  165.9 1.7 collective-permute-done.41
  168.3 3.9 %collective-permute-start.43 = (bf16[32,3200]{1,0:T(8,128)(2,1)S(1)}, bf16[32,3200]{1,0:T(8,128)(2,1)S(1)}, u32[]{:S(2)}, u32[]{:S(2)}) collective-permute-start(bf16[32,3200]{1,0:T(8,128)(2,1)S(1)} %multiply_convert_fusion.2.refs_0_), channel_id=1, source_target_pairs={{0,2},{1,3},{2,0},{3,1},{4,6},{5,7},{6,4},{7,5},{8,10},{9,11},{10,... | collective-permute-start | bytes 614408 | tf_op jit(solution)/shard_map/ppermute | solution.py:277
  173.3 1.4 collective-permute-start.45
  174.7 13.1 %shard_map.118 = (bf16[32,12800]{1,0:T(8,128)(2,1)}, bf16[32,12800]{1,0:T(8,128)(2,1)}) custom-call(bf16[64,1024]{1,0:T(8,128)(2,1)} %get-tuple-element.187.delta, bf16[12800,1024]{1,0:T(8,128)(2,1)} %weight.3), custom_call_target="tpu_custom_call" | custom-call | flops 1677721600 | bytes 29753344 | tf_op jit(solution)/shard_map/pallas_call | solution.py:249
  187.8 2.1 collective-permute-done.44.refs_2_
  191.0 1.7 collective-permute-done.50
  192.8 1.3 fusion.58
  194.2 2.9 %collective-permute-start.51 = (bf16[8,12800]{1,0:T(8,128)(2,1)S(1)}, bf16[8,12800]{1,0:T(8,128)(2,1)S(1)}, u32[]{:S(2)}, u32[]{:S(2)}) collective-permute-start(bf16[8,12800]{1,0:T(8,128)(2,1)S(1)} %get-tuple-element.285), channel_id=1, source_target_pairs={{0,2},{1,3},{2,0},{3,1},{4,6},{5,7},{6,4},{7,5},{8,10},{9,11},{10,... | collective-permute-start | bytes 614408 | tf_op jit(solution)/shard_map/ppermute | solution.py:277
  198.2 1.5 collective-permute-start.53
  200.4 14.6 %shard_map.119 = (bf16[128,3200]{1,0:T(8,128)(2,1)}, bf16[128,3200]{1,0:T(8,128)(2,1)}) custom-call(bf16[32,3200]{1,0:T(8,128)(2,1)} %copy-done.13, bf16[32,3200]{1,0:T(8,128)(2,1)} %copy-done.21, bf16[32,3200]{1,0:T(8,128)(2,1)} %copy-done.23, bf16[32,3200]{1,0:T(8,128)(2,1)} %copy-done.25, bf16[32,3200]{1,0:T(8,128)(2,1)} %copy-done.27, ...), custom_call_target="tpu_custom_call" | custom-call | flops 5242880000 | bytes 25395200 | tf_op jit(solution)/shard_map/pallas_call | solution.py:192
  215.9 3.6 %collective-permute-start.55 = (bf16[32,3200]{1,0:T(8,128)(2,1)S(1)}, bf16[32,3200]{1,0:T(8,128)(2,1)}, u32[]{:S(2)}, u32[]{:S(2)}) collective-permute-start(bf16[32,3200]{1,0:T(8,128)(2,1)S(1)} %multiply_convert_fusion.refs_0_), channel_id=1, source_target_pairs={{0,2},{1,3},{2,0},{3,1},{4,6},{5,7},{6,4},{7,5},{8,10},{9,11},{10,... | collective-permute-start | bytes 614408 | tf_op jit(solution)/shard_map/ppermute | solution.py:277
  220.6 1.4 collective-permute-start.57
  223.7 1.5 collective-permute-start.58
  226.2 1.5 collective-permute-start.59
  227.7 1.6 fusion.59
  229.3 1.5 collective-permute-start.60
  231.6 2.0 collective-permute-done.60
  233.6 3.6 %collective-permute-done.56.refs_2_ = bf16[32,3200]{1,0:T(8,128)(2,1)} collective-permute-done((bf16[32,3200]{1,0:T(8,128)(2,1)S(1)}, bf16[32,3200]{1,0:T(8,128)(2,1)}, u32[]{:S(2)}, u32[]{:S(2)}) %collective-permute-start.56) | collective-permute-done | bytes 204832 | tf_op jit(solution)/shard_map/ppermute | solution.py:277
  238.6 4.3 %collective-permute-start.65 = (bf16[32,3200]{1,0:T(8,128)(2,1)}, bf16[32,3200]{1,0:T(8,128)(2,1)S(1)}, u32[]{:S(2)}, u32[]{:S(2)}) collective-permute-start(bf16[32,3200]{1,0:T(8,128)(2,1)} %get-tuple-element.221), channel_id=1, source_target_pairs={{0,2},{1,3},{2,0},{3,1},{4,6},{5,7},{6,4},{7,5},{8,10},{9,11},{10,... | collective-permute-start | bytes 614408 | tf_op jit(solution)/shard_map/ppermute | solution.py:277
  244.2 1.4 collective-permute-start.67
  246.3 14.6 %shard_map.120 = (bf16[128,3200]{1,0:T(8,128)(2,1)}, bf16[128,3200]{1,0:T(8,128)(2,1)}) custom-call(bf16[32,3200]{1,0:T(8,128)(2,1)} %copy-done.11, bf16[32,3200]{1,0:T(8,128)(2,1)} %collective-permute-done.55.refs_1_, bf16[32,3200]{1,0:T(8,128)(2,1)} %collective-permute-done.56.refs_2_, bf16[32,3200]{1,0:T(8,128)(2,1)} %collective-permute-done.57.refs_3_, ...), custom_call_target="tpu_custom_call" | custom-call | flops 5242880000 | bytes 25395200 | tf_op jit(solution)/shard_map/pallas_call | solution.py:192
  261.1 2.4 collective-permute-done.68
  263.8 3.6 %collective-permute-start.69 = (bf16[32,3200]{1,0:T(8,128)(2,1)S(1)}, bf16[32,3200]{1,0:T(8,128)(2,1)S(1)}, u32[]{:S(2)}, u32[]{:S(2)}) collective-permute-start(bf16[32,3200]{1,0:T(8,128)(2,1)S(1)} %get-tuple-element.279), channel_id=1, source_target_pairs={{0,2},{1,3},{2,0},{3,1},{4,6},{5,7},{6,4},{7,5},{8,10},{9,11},{10,... | collective-permute-start | bytes 614408 | tf_op jit(solution)/shard_map/ppermute | solution.py:277
  268.5 1.4 collective-permute-start.71
  269.8 2.2 fusion
  272.1 4.5 %collective-permute-done.69 = bf16[32,3200]{1,0:T(8,128)(2,1)S(1)} collective-permute-done((bf16[32,3200]{1,0:T(8,128)(2,1)S(1)}, bf16[32,3200]{1,0:T(8,128)(2,1)S(1)}, u32[]{:S(2)}, u32[]{:S(2)}) %collective-permute-start.69) | collective-permute-done | bytes 204832 | tf_op jit(solution)/shard_map/ppermute | solution.py:277
  276.5 8.5 %collective-permute-done.70 = bf16[32,3200]{1,0:T(8,128)(2,1)S(1)} collective-permute-done((bf16[32,3200]{1,0:T(8,128)(2,1)S(1)}, bf16[32,3200]{1,0:T(8,128)(2,1)S(1)}, u32[]{:S(2)}, u32[]{:S(2)}) %collective-permute-start.70) | collective-permute-done | bytes 204832 | tf_op jit(solution)/shard_map/ppermute | solution.py:277
  (315 shorter events, 40.7 us)
Async XLA Ops:
  4.6 18.0 %collective-permute-start = (bf16[32,3200]{1,0:T(8,128)(2,1)S(1)}, bf16[32,3200]{1,0:T(8,128)(2,1)}, u32[]{:S(2)}, u32[]{:S(2)}) collective-permute-start(bf16[32,3200]{1,0:T(8,128)(2,1)S(1)} %get-tuple-element.123.refs_0_), channel_id=1, source_target_pairs={{0,2},{1,3},{2,0},{3,1},{4,6},{5,7},{6,4},{7,5},{8,10},{9,11},{10,... | collective-permute-start | bytes 614408 | tf_op jit(solution)/shard_map/ppermute | solution.py:277
  7.7 17.8 %collective-permute-start.1 = (bf16[32,3200]{1,0:T(8,128)(2,1)S(1)}, bf16[32,3200]{1,0:T(8,128)(2,1)}, u32[]{:S(2)}, u32[]{:S(2)}) collective-permute-start(bf16[32,3200]{1,0:T(8,128)(2,1)S(1)} %get-tuple-element.123.refs_0_), channel_id=1, source_target_pairs={{0,4},{1,5},{2,6},{3,7},{4,0},{5,1},{6,2},{7,3},{8,12},{9,13},{10,... | collective-permute-start | bytes 614408 | tf_op jit(solution)/shard_map/ppermute | solution.py:277
  10.3 15.2 %collective-permute-start.2 = (bf16[32,3200]{1,0:T(8,128)(2,1)S(1)}, bf16[32,3200]{1,0:T(8,128)(2,1)}, u32[]{:S(2)}, u32[]{:S(2)}) collective-permute-start(bf16[32,3200]{1,0:T(8,128)(2,1)S(1)} %get-tuple-element.123.refs_0_), channel_id=1, source_target_pairs={{0,6},{1,7},{2,4},{3,5},{4,2},{5,3},{6,0},{7,1},{8,14},{9,15},{10,... | collective-permute-start | bytes 614408 | tf_op jit(solution)/shard_map/ppermute | solution.py:277
  17.0 5.6 %collective-permute-start.5 = (bf16[32,1024]{1,0:T(8,128)(2,1)S(1)}, bf16[32,1024]{1,0:T(8,128)(2,1)S(1)}, u32[]{:S(2)}, u32[]{:S(2)}) collective-permute-start(bf16[32,1024]{1,0:T(8,128)(2,1)S(1)} %get-tuple-element.305), channel_id=1, source_target_pairs={{0,8},{8,16},{16,24},{24,0},{1,9},{9,17},{17,25},{25,1},{2,10},{10... | collective-permute-start | bytes 196616 | tf_op jit(solution)/shard_map/ppermute | solution.py:358
  25.5 6.2 %collective-permute-start.7 = (bf16[32,3200]{1,0:T(8,128)(2,1)}, bf16[32,3200]{1,0:T(8,128)(2,1)S(1)}, u32[]{:S(2)}, u32[]{:S(2)}) collective-permute-start(bf16[32,3200]{1,0:T(8,128)(2,1)} %collective-permute-done.refs_1_), channel_id=1, source_target_pairs={{0,1},{1,0},{2,3},{3,2},{4,5},{5,4},{6,7},{7,6},{8,9},{9,8},{10,11... | collective-permute-start | bytes 614408 | tf_op jit(solution)/shard_map/ppermute | solution.py:283
  26.0 7.1 %collective-permute-start.8 = (bf16[32,3200]{1,0:T(8,128)(2,1)}, bf16[32,3200]{1,0:T(8,128)(2,1)S(1)}, u32[]{:S(2)}, u32[]{:S(2)}) collective-permute-start(bf16[32,3200]{1,0:T(8,128)(2,1)} %collective-permute-done.1.refs_2_), channel_id=1, source_target_pairs={{0,1},{1,0},{2,3},{3,2},{4,5},{5,4},{6,7},{7,6},{8,9},{9,8},{10,11... | collective-permute-start | bytes 614408 | tf_op jit(solution)/shard_map/ppermute | solution.py:283
  26.0 7.1 %collective-permute-start.9 = (bf16[32,3200]{1,0:T(8,128)(2,1)}, bf16[32,3200]{1,0:T(8,128)(2,1)S(1)}, u32[]{:S(2)}, u32[]{:S(2)}) collective-permute-start(bf16[32,3200]{1,0:T(8,128)(2,1)} %collective-permute-done.2.refs_3_), channel_id=1, source_target_pairs={{0,1},{1,0},{2,3},{3,2},{4,5},{5,4},{6,7},{7,6},{8,9},{9,8},{10,11... | collective-permute-start | bytes 614408 | tf_op jit(solution)/shard_map/ppermute | solution.py:283
  26.5 22.1 %collective-permute-start.10 = (bf16[32,3200]{1,0:T(8,128)(2,1)S(1)}, bf16[32,3200]{1,0:T(8,128)(2,1)S(1)}, u32[]{:S(2)}, u32[]{:S(2)}) collective-permute-start(bf16[32,3200]{1,0:T(8,128)(2,1)S(1)} %get-tuple-element.130.refs_0_), channel_id=1, source_target_pairs={{0,2},{1,3},{2,0},{3,1},{4,6},{5,7},{6,4},{7,5},{8,10},{9,11},{10,... | collective-permute-start | bytes 614408 | tf_op jit(solution)/shard_map/ppermute | solution.py:277
  30.0 18.5 %collective-permute-start.11 = (bf16[32,3200]{1,0:T(8,128)(2,1)S(1)}, bf16[32,3200]{1,0:T(8,128)(2,1)}, u32[]{:S(2)}, u32[]{:S(2)}) collective-permute-start(bf16[32,3200]{1,0:T(8,128)(2,1)S(1)} %get-tuple-element.130.refs_0_), channel_id=1, source_target_pairs={{0,4},{1,5},{2,6},{3,7},{4,0},{5,1},{6,2},{7,3},{8,12},{9,13},{10,... | collective-permute-start | bytes 614408 | tf_op jit(solution)/shard_map/ppermute | solution.py:277
  31.7 16.9 %collective-permute-start.12 = (bf16[32,3200]{1,0:T(8,128)(2,1)S(1)}, bf16[32,3200]{1,0:T(8,128)(2,1)}, u32[]{:S(2)}, u32[]{:S(2)}) collective-permute-start(bf16[32,3200]{1,0:T(8,128)(2,1)S(1)} %get-tuple-element.130.refs_0_), channel_id=1, source_target_pairs={{0,6},{1,7},{2,4},{3,5},{4,2},{5,3},{6,0},{7,1},{8,14},{9,15},{10,... | collective-permute-start | bytes 614408 | tf_op jit(solution)/shard_map/ppermute | solution.py:277
  48.7 7.6 %collective-permute-start.13 = (bf16[32,3200]{1,0:T(8,128)(2,1)S(1)}, bf16[32,3200]{1,0:T(8,128)(2,1)S(1)}, u32[]{:S(2)}, u32[]{:S(2)}) collective-permute-start(bf16[32,3200]{1,0:T(8,128)(2,1)S(1)} %get-tuple-element.130.refs_0_), channel_id=1, source_target_pairs={{0,1},{1,0},{2,3},{3,2},{4,5},{5,4},{6,7},{7,6},{8,9},{9,8},{10,11... | collective-permute-start | bytes 614408 | tf_op jit(solution)/shard_map/ppermute | solution.py:283
  49.2 8.2 %collective-permute-start.14 = (bf16[32,3200]{1,0:T(8,128)(2,1)S(1)}, bf16[32,3200]{1,0:T(8,128)(2,1)S(1)}, u32[]{:S(2)}, u32[]{:S(2)}) collective-permute-start(bf16[32,3200]{1,0:T(8,128)(2,1)S(1)} %collective-permute-done.10.refs_1_), channel_id=1, source_target_pairs={{0,1},{1,0},{2,3},{3,2},{4,5},{5,4},{6,7},{7,6},{8,9},{9,8},{10,11... | collective-permute-start | bytes 614408 | tf_op jit(solution)/shard_map/ppermute | solution.py:283
  49.3 9.6 %collective-permute-start.15 = (bf16[32,3200]{1,0:T(8,128)(2,1)}, bf16[32,3200]{1,0:T(8,128)(2,1)S(1)}, u32[]{:S(2)}, u32[]{:S(2)}) collective-permute-start(bf16[32,3200]{1,0:T(8,128)(2,1)} %collective-permute-done.11.refs_2_), channel_id=1, source_target_pairs={{0,1},{1,0},{2,3},{3,2},{4,5},{5,4},{6,7},{7,6},{8,9},{9,8},{10,11... | collective-permute-start | bytes 614408 | tf_op jit(solution)/shard_map/ppermute | solution.py:283
  49.7 9.2 %collective-permute-start.16 = (bf16[32,3200]{1,0:T(8,128)(2,1)}, bf16[32,3200]{1,0:T(8,128)(2,1)S(1)}, u32[]{:S(2)}, u32[]{:S(2)}) collective-permute-start(bf16[32,3200]{1,0:T(8,128)(2,1)} %collective-permute-done.12.refs_3_), channel_id=1, source_target_pairs={{0,1},{1,0},{2,3},{3,2},{4,5},{5,4},{6,7},{7,6},{8,9},{9,8},{10,11... | collective-permute-start | bytes 614408 | tf_op jit(solution)/shard_map/ppermute | solution.py:283
  53.0 22.0 %collective-permute-start.18 = (bf16[32,3200]{1,0:T(8,128)(2,1)S(1)}, bf16[32,3200]{1,0:T(8,128)(2,1)S(1)}, u32[]{:S(2)}, u32[]{:S(2)}) collective-permute-start(bf16[32,3200]{1,0:T(8,128)(2,1)S(1)} %get-tuple-element.294), channel_id=1, source_target_pairs={{0,2},{1,3},{2,0},{3,1},{4,6},{5,7},{6,4},{7,5},{8,10},{9,11},{10,... | collective-permute-start | bytes 614408 | tf_op jit(solution)/shard_map/ppermute | solution.py:277
  56.3 18.7 %collective-permute-start.19 = (bf16[32,3200]{1,0:T(8,128)(2,1)S(1)}, bf16[32,3200]{1,0:T(8,128)(2,1)S(1)}, u32[]{:S(2)}, u32[]{:S(2)}) collective-permute-start(bf16[32,3200]{1,0:T(8,128)(2,1)S(1)} %get-tuple-element.293), channel_id=1, source_target_pairs={{0,4},{1,5},{2,6},{3,7},{4,0},{5,1},{6,2},{7,3},{8,12},{9,13},{10,... | collective-permute-start | bytes 614408 | tf_op jit(solution)/shard_map/ppermute | solution.py:277
  57.4 17.6 %collective-permute-start.20 = (bf16[32,3200]{1,0:T(8,128)(2,1)S(1)}, bf16[32,3200]{1,0:T(8,128)(2,1)S(1)}, u32[]{:S(2)}, u32[]{:S(2)}) collective-permute-start(bf16[32,3200]{1,0:T(8,128)(2,1)S(1)} %get-tuple-element.292), channel_id=1, source_target_pairs={{0,6},{1,7},{2,4},{3,5},{4,2},{5,3},{6,0},{7,1},{8,14},{9,15},{10,... | collective-permute-start | bytes 614408 | tf_op jit(solution)/shard_map/ppermute | solution.py:277
  76.4 8.6 %collective-permute-start.21 = (bf16[128,3200]{1,0:T(8,128)(2,1)}, bf16[128,3200]{1,0:T(8,128)(2,1)}, u32[]{:S(2)}, u32[]{:S(2)}) collective-permute-start(bf16[128,3200]{1,0:T(8,128)(2,1)} %get-tuple-element.149), channel_id=1, source_target_pairs={{0,1},{1,0},{2,3},{3,2},{4,5},{5,4},{6,7},{7,6},{8,9},{9,8},{10,11... | collective-permute-start | bytes 2457608 | tf_op jit(solution)/shard_map/ppermute | solution.py:290
  76.6 12.5 %collective-permute-start.22 = (bf16[8,12800]{1,0:T(8,128)(2,1)S(1)}, bf16[8,12800]{1,0:T(8,128)(2,1)S(1)}, u32[]{:S(2)}, u32[]{:S(2)}) collective-permute-start(bf16[8,12800]{1,0:T(8,128)(2,1)S(1)} %multiply_convert_fusion.5.refs_0_), channel_id=1, source_target_pairs={{0,2},{1,3},{2,0},{3,1},{4,6},{5,7},{6,4},{7,5},{8,10},{9,11},{10,... | collective-permute-start | bytes 614408 | tf_op jit(solution)/shard_map/ppermute | solution.py:277
  79.4 17.6 %collective-permute-start.23 = (bf16[8,12800]{1,0:T(8,128)(2,1)S(1)}, bf16[8,12800]{1,0:T(8,128)(2,1)S(1)}, u32[]{:S(2)}, u32[]{:S(2)}) collective-permute-start(bf16[8,12800]{1,0:T(8,128)(2,1)S(1)} %multiply_convert_fusion.5.refs_0_), channel_id=1, source_target_pairs={{0,4},{1,5},{2,6},{3,7},{4,0},{5,1},{6,2},{7,3},{8,12},{9,13},{10,... | collective-permute-start | bytes 614408 | tf_op jit(solution)/shard_map/ppermute | solution.py:277
  80.5 16.5 %collective-permute-start.24 = (bf16[8,12800]{1,0:T(8,128)(2,1)S(1)}, bf16[8,12800]{1,0:T(8,128)(2,1)S(1)}, u32[]{:S(2)}, u32[]{:S(2)}) collective-permute-start(bf16[8,12800]{1,0:T(8,128)(2,1)S(1)} %multiply_convert_fusion.5.refs_0_), channel_id=1, source_target_pairs={{0,6},{1,7},{2,4},{3,5},{4,2},{5,3},{6,0},{7,1},{8,14},{9,15},{10,... | collective-permute-start | bytes 614408 | tf_op jit(solution)/shard_map/ppermute | solution.py:277
  97.1 5.3 %collective-permute-start.25 = (bf16[8,12800]{1,0:T(8,128)(2,1)S(1)}, bf16[8,12800]{1,0:T(8,128)(2,1)S(1)}, u32[]{:S(2)}, u32[]{:S(2)}) collective-permute-start(bf16[8,12800]{1,0:T(8,128)(2,1)S(1)} %multiply_convert_fusion.5.refs_0_), channel_id=1, source_target_pairs={{0,1},{1,0},{2,3},{3,2},{4,5},{5,4},{6,7},{7,6},{8,9},{9,8},{10,11... | collective-permute-start | bytes 614408 | tf_op jit(solution)/shard_map/ppermute | solution.py:283
  97.1 6.6 %collective-permute-start.26 = (bf16[8,12800]{1,0:T(8,128)(2,1)S(1)}, bf16[8,12800]{1,0:T(8,128)(2,1)S(1)}, u32[]{:S(2)}, u32[]{:S(2)}) collective-permute-start(bf16[8,12800]{1,0:T(8,128)(2,1)S(1)} %collective-permute-done.22.refs_1_), channel_id=1, source_target_pairs={{0,1},{1,0},{2,3},{3,2},{4,5},{5,4},{6,7},{7,6},{8,9},{9,8},{10,11... | collective-permute-start | bytes 614408 | tf_op jit(solution)/shard_map/ppermute | solution.py:283
  97.6 7.5 %collective-permute-start.27 = (bf16[8,12800]{1,0:T(8,128)(2,1)S(1)}, bf16[8,12800]{1,0:T(8,128)(2,1)S(1)}, u32[]{:S(2)}, u32[]{:S(2)}) collective-permute-start(bf16[8,12800]{1,0:T(8,128)(2,1)S(1)} %collective-permute-done.23.refs_2_), channel_id=1, source_target_pairs={{0,1},{1,0},{2,3},{3,2},{4,5},{5,4},{6,7},{7,6},{8,9},{9,8},{10,11... | collective-permute-start | bytes 614408 | tf_op jit(solution)/shard_map/ppermute | solution.py:283
  97.7 7.4 %collective-permute-start.28 = (bf16[8,12800]{1,0:T(8,128)(2,1)S(1)}, bf16[8,12800]{1,0:T(8,128)(2,1)S(1)}, u32[]{:S(2)}, u32[]{:S(2)}) collective-permute-start(bf16[8,12800]{1,0:T(8,128)(2,1)S(1)} %collective-permute-done.24.refs_3_), channel_id=1, source_target_pairs={{0,1},{1,0},{2,3},{3,2},{4,5},{5,4},{6,7},{7,6},{8,9},{9,8},{10,11... | collective-permute-start | bytes 614408 | tf_op jit(solution)/shard_map/ppermute | solution.py:283
  98.2 20.1 %collective-permute-start.29 = (bf16[32,3200]{1,0:T(8,128)(2,1)S(1)}, bf16[32,3200]{1,0:T(8,128)(2,1)S(1)}, u32[]{:S(2)}, u32[]{:S(2)}) collective-permute-start(bf16[32,3200]{1,0:T(8,128)(2,1)S(1)} %get-tuple-element.162), channel_id=1, source_target_pairs={{0,2},{1,3},{2,0},{3,1},{4,6},{5,7},{6,4},{7,5},{8,10},{9,11},{10,... | collective-permute-start | bytes 614408 | tf_op jit(solution)/shard_map/ppermute | solution.py:277
  102.3 17.6 %collective-permute-start.30 = (bf16[32,3200]{1,0:T(8,128)(2,1)S(1)}, bf16[32,3200]{1,0:T(8,128)(2,1)S(1)}, u32[]{:S(2)}, u32[]{:S(2)}) collective-permute-start(bf16[32,3200]{1,0:T(8,128)(2,1)S(1)} %get-tuple-element.163), channel_id=1, source_target_pairs={{0,4},{1,5},{2,6},{3,7},{4,0},{5,1},{6,2},{7,3},{8,12},{9,13},{10,... | collective-permute-start | bytes 614408 | tf_op jit(solution)/shard_map/ppermute | solution.py:277
  103.8 16.2 %collective-permute-start.31 = (bf16[32,3200]{1,0:T(8,128)(2,1)S(1)}, bf16[32,3200]{1,0:T(8,128)(2,1)S(1)}, u32[]{:S(2)}, u32[]{:S(2)}) collective-permute-start(bf16[32,3200]{1,0:T(8,128)(2,1)S(1)} %get-tuple-element.164), channel_id=1, source_target_pairs={{0,6},{1,7},{2,4},{3,5},{4,2},{5,3},{6,0},{7,1},{8,14},{9,15},{10,... | collective-permute-start | bytes 614408 | tf_op jit(solution)/shard_map/ppermute | solution.py:277
  121.3 19.4 %collective-permute-start.32 = (bf16[8,12800]{1,0:T(8,128)(2,1)S(1)}, bf16[8,12800]{1,0:T(8,128)(2,1)S(1)}, u32[]{:S(2)}, u32[]{:S(2)}) collective-permute-start(bf16[8,12800]{1,0:T(8,128)(2,1)S(1)} %multiply_convert_fusion.4.refs_0_), channel_id=1, source_target_pairs={{0,2},{1,3},{2,0},{3,1},{4,6},{5,7},{6,4},{7,5},{8,10},{9,11},{10,... | collective-permute-start | bytes 614408 | tf_op jit(solution)/shard_map/ppermute | solution.py:277
  125.1 17.6 %collective-permute-start.33 = (bf16[8,12800]{1,0:T(8,128)(2,1)S(1)}, bf16[8,12800]{1,0:T(8,128)(2,1)S(1)}, u32[]{:S(2)}, u32[]{:S(2)}) collective-permute-start(bf16[8,12800]{1,0:T(8,128)(2,1)S(1)} %multiply_convert_fusion.4.refs_0_), channel_id=1, source_target_pairs={{0,4},{1,5},{2,6},{3,7},{4,0},{5,1},{6,2},{7,3},{8,12},{9,13},{10,... | collective-permute-start | bytes 614408 | tf_op jit(solution)/shard_map/ppermute | solution.py:277
  126.2 16.5 %collective-permute-start.34 = (bf16[8,12800]{1,0:T(8,128)(2,1)S(1)}, bf16[8,12800]{1,0:T(8,128)(2,1)S(1)}, u32[]{:S(2)}, u32[]{:S(2)}) collective-permute-start(bf16[8,12800]{1,0:T(8,128)(2,1)S(1)} %multiply_convert_fusion.4.refs_0_), channel_id=1, source_target_pairs={{0,6},{1,7},{2,4},{3,5},{4,2},{5,3},{6,0},{7,1},{8,14},{9,15},{10,... | collective-permute-start | bytes 614408 | tf_op jit(solution)/shard_map/ppermute | solution.py:277
  142.8 7.1 %collective-permute-start.35 = (bf16[8,12800]{1,0:T(8,128)(2,1)S(1)}, bf16[8,12800]{1,0:T(8,128)(2,1)S(1)}, u32[]{:S(2)}, u32[]{:S(2)}) collective-permute-start(bf16[8,12800]{1,0:T(8,128)(2,1)S(1)} %multiply_convert_fusion.4.refs_0_), channel_id=1, source_target_pairs={{0,1},{1,0},{2,3},{3,2},{4,5},{5,4},{6,7},{7,6},{8,9},{9,8},{10,11... | collective-permute-start | bytes 614408 | tf_op jit(solution)/shard_map/ppermute | solution.py:283
  143.3 7.8 %collective-permute-start.36 = (bf16[8,12800]{1,0:T(8,128)(2,1)S(1)}, bf16[8,12800]{1,0:T(8,128)(2,1)S(1)}, u32[]{:S(2)}, u32[]{:S(2)}) collective-permute-start(bf16[8,12800]{1,0:T(8,128)(2,1)S(1)} %collective-permute-done.32.refs_1_), channel_id=1, source_target_pairs={{0,1},{1,0},{2,3},{3,2},{4,5},{5,4},{6,7},{7,6},{8,9},{9,8},{10,11... | collective-permute-start | bytes 614408 | tf_op jit(solution)/shard_map/ppermute | solution.py:283
  143.4 9.1 %collective-permute-start.37 = (bf16[8,12800]{1,0:T(8,128)(2,1)S(1)}, bf16[8,12800]{1,0:T(8,128)(2,1)S(1)}, u32[]{:S(2)}, u32[]{:S(2)}) collective-permute-start(bf16[8,12800]{1,0:T(8,128)(2,1)S(1)} %collective-permute-done.33.refs_2_), channel_id=1, source_target_pairs={{0,1},{1,0},{2,3},{3,2},{4,5},{5,4},{6,7},{7,6},{8,9},{9,8},{10,11... | collective-permute-start | bytes 614408 | tf_op jit(solution)/shard_map/ppermute | solution.py:283
  143.8 8.7 %collective-permute-start.38 = (bf16[8,12800]{1,0:T(8,128)(2,1)S(1)}, bf16[8,12800]{1,0:T(8,128)(2,1)S(1)}, u32[]{:S(2)}, u32[]{:S(2)}) collective-permute-start(bf16[8,12800]{1,0:T(8,128)(2,1)S(1)} %collective-permute-done.34.refs_3_), channel_id=1, source_target_pairs={{0,1},{1,0},{2,3},{3,2},{4,5},{5,4},{6,7},{7,6},{8,9},{9,8},{10,11... | collective-permute-start | bytes 614408 | tf_op jit(solution)/shard_map/ppermute | solution.py:283
  147.0 18.9 %collective-permute-start.40 = (bf16[8,12800]{1,0:T(8,128)(2,1)S(1)}, bf16[8,12800]{1,0:T(8,128)(2,1)S(1)}, u32[]{:S(2)}, u32[]{:S(2)}) collective-permute-start(bf16[8,12800]{1,0:T(8,128)(2,1)S(1)} %get-tuple-element.288), channel_id=1, source_target_pairs={{0,2},{1,3},{2,0},{3,1},{4,6},{5,7},{6,4},{7,5},{8,10},{9,11},{10,... | collective-permute-start | bytes 614408 | tf_op jit(solution)/shard_map/ppermute | solution.py:277
  149.9 17.6 %collective-permute-start.41 = (bf16[8,12800]{1,0:T(8,128)(2,1)S(1)}, bf16[8,12800]{1,0:T(8,128)(2,1)S(1)}, u32[]{:S(2)}, u32[]{:S(2)}) collective-permute-start(bf16[8,12800]{1,0:T(8,128)(2,1)S(1)} %get-tuple-element.287), channel_id=1, source_target_pairs={{0,4},{1,5},{2,6},{3,7},{4,0},{5,1},{6,2},{7,3},{8,12},{9,13},{10,... | collective-permute-start | bytes 614408 | tf_op jit(solution)/shard_map/ppermute | solution.py:277
  151.0 16.5 %collective-permute-start.42 = (bf16[8,12800]{1,0:T(8,128)(2,1)S(1)}, bf16[8,12800]{1,0:T(8,128)(2,1)S(1)}, u32[]{:S(2)}, u32[]{:S(2)}) collective-permute-start(bf16[8,12800]{1,0:T(8,128)(2,1)S(1)} %get-tuple-element.286), channel_id=1, source_target_pairs={{0,6},{1,7},{2,4},{3,5},{4,2},{5,3},{6,0},{7,1},{8,14},{9,15},{10,... | collective-permute-start | bytes 614408 | tf_op jit(solution)/shard_map/ppermute | solution.py:277
  168.3 19.5 %collective-permute-start.43 = (bf16[32,3200]{1,0:T(8,128)(2,1)S(1)}, bf16[32,3200]{1,0:T(8,128)(2,1)S(1)}, u32[]{:S(2)}, u32[]{:S(2)}) collective-permute-start(bf16[32,3200]{1,0:T(8,128)(2,1)S(1)} %multiply_convert_fusion.2.refs_0_), channel_id=1, source_target_pairs={{0,2},{1,3},{2,0},{3,1},{4,6},{5,7},{6,4},{7,5},{8,10},{9,11},{10,... | collective-permute-start | bytes 614408 | tf_op jit(solution)/shard_map/ppermute | solution.py:277
  172.2 17.7 %collective-permute-start.44 = (bf16[32,3200]{1,0:T(8,128)(2,1)S(1)}, bf16[32,3200]{1,0:T(8,128)(2,1)S(1)}, u32[]{:S(2)}, u32[]{:S(2)}) collective-permute-start(bf16[32,3200]{1,0:T(8,128)(2,1)S(1)} %multiply_convert_fusion.2.refs_0_), channel_id=1, source_target_pairs={{0,4},{1,5},{2,6},{3,7},{4,0},{5,1},{6,2},{7,3},{8,12},{9,13},{10,... | collective-permute-start | bytes 614408 | tf_op jit(solution)/shard_map/ppermute | solution.py:277
  173.3 16.6 %collective-permute-start.45 = (bf16[32,3200]{1,0:T(8,128)(2,1)S(1)}, bf16[32,3200]{1,0:T(8,128)(2,1)S(1)}, u32[]{:S(2)}, u32[]{:S(2)}) collective-permute-start(bf16[32,3200]{1,0:T(8,128)(2,1)S(1)} %multiply_convert_fusion.2.refs_0_), channel_id=1, source_target_pairs={{0,6},{1,7},{2,4},{3,5},{4,2},{5,3},{6,0},{7,1},{8,14},{9,15},{10,... | collective-permute-start | bytes 614408 | tf_op jit(solution)/shard_map/ppermute | solution.py:277
  189.9 7.1 %collective-permute-start.46 = (bf16[32,3200]{1,0:T(8,128)(2,1)S(1)}, bf16[32,3200]{1,0:T(8,128)(2,1)S(1)}, u32[]{:S(2)}, u32[]{:S(2)}) collective-permute-start(bf16[32,3200]{1,0:T(8,128)(2,1)S(1)} %multiply_convert_fusion.2.refs_0_), channel_id=1, source_target_pairs={{0,1},{1,0},{2,3},{3,2},{4,5},{5,4},{6,7},{7,6},{8,9},{9,8},{10,11... | collective-permute-start | bytes 614408 | tf_op jit(solution)/shard_map/ppermute | solution.py:283
  190.4 7.7 %collective-permute-start.47 = (bf16[32,3200]{1,0:T(8,128)(2,1)S(1)}, bf16[32,3200]{1,0:T(8,128)(2,1)S(1)}, u32[]{:S(2)}, u32[]{:S(2)}) collective-permute-start(bf16[32,3200]{1,0:T(8,128)(2,1)S(1)} %collective-permute-done.43.refs_1_), channel_id=1, source_target_pairs={{0,1},{1,0},{2,3},{3,2},{4,5},{5,4},{6,7},{7,6},{8,9},{9,8},{10,11... | collective-permute-start | bytes 614408 | tf_op jit(solution)/shard_map/ppermute | solution.py:283
  190.5 9.1 %collective-permute-start.48 = (bf16[32,3200]{1,0:T(8,128)(2,1)S(1)}, bf16[32,3200]{1,0:T(8,128)(2,1)S(1)}, u32[]{:S(2)}, u32[]{:S(2)}) collective-permute-start(bf16[32,3200]{1,0:T(8,128)(2,1)S(1)} %collective-permute-done.44.refs_2_), channel_id=1, source_target_pairs={{0,1},{1,0},{2,3},{3,2},{4,5},{5,4},{6,7},{7,6},{8,9},{9,8},{10,11... | collective-permute-start | bytes 614408 | tf_op jit(solution)/shard_map/ppermute | solution.py:283
  191.0 8.7 %collective-permute-start.49 = (bf16[32,3200]{1,0:T(8,128)(2,1)S(1)}, bf16[32,3200]{1,0:T(8,128)(2,1)S(1)}, u32[]{:S(2)}, u32[]{:S(2)}) collective-permute-start(bf16[32,3200]{1,0:T(8,128)(2,1)S(1)} %collective-permute-done.45.refs_3_), channel_id=1, source_target_pairs={{0,1},{1,0},{2,3},{3,2},{4,5},{5,4},{6,7},{7,6},{8,9},{9,8},{10,11... | collective-permute-start | bytes 614408 | tf_op jit(solution)/shard_map/ppermute | solution.py:283
  194.2 20.9 %collective-permute-start.51 = (bf16[8,12800]{1,0:T(8,128)(2,1)S(1)}, bf16[8,12800]{1,0:T(8,128)(2,1)S(1)}, u32[]{:S(2)}, u32[]{:S(2)}) collective-permute-start(bf16[8,12800]{1,0:T(8,128)(2,1)S(1)} %get-tuple-element.285), channel_id=1, source_target_pairs={{0,2},{1,3},{2,0},{3,1},{4,6},{5,7},{6,4},{7,5},{8,10},{9,11},{10,... | collective-permute-start | bytes 614408 | tf_op jit(solution)/shard_map/ppermute | solution.py:277
  197.1 18.0 %collective-permute-start.52 = (bf16[8,12800]{1,0:T(8,128)(2,1)S(1)}, bf16[8,12800]{1,0:T(8,128)(2,1)S(1)}, u32[]{:S(2)}, u32[]{:S(2)}) collective-permute-start(bf16[8,12800]{1,0:T(8,128)(2,1)S(1)} %get-tuple-element.284), channel_id=1, source_target_pairs={{0,4},{1,5},{2,6},{3,7},{4,0},{5,1},{6,2},{7,3},{8,12},{9,13},{10,... | collective-permute-start | bytes 614408 | tf_op jit(solution)/shard_map/ppermute | solution.py:277
  198.2 16.9 %collective-permute-start.53 = (bf16[8,12800]{1,0:T(8,128)(2,1)S(1)}, bf16[8,12800]{1,0:T(8,128)(2,1)S(1)}, u32[]{:S(2)}, u32[]{:S(2)}) collective-permute-start(bf16[8,12800]{1,0:T(8,128)(2,1)S(1)} %get-tuple-element.283), channel_id=1, source_target_pairs={{0,6},{1,7},{2,4},{3,5},{4,2},{5,3},{6,0},{7,1},{8,14},{9,15},{10,... | collective-permute-start | bytes 614408 | tf_op jit(solution)/shard_map/ppermute | solution.py:277
  215.8 9.5 %collective-permute-start.54 = (bf16[128,3200]{1,0:T(8,128)(2,1)}, bf16[128,3200]{1,0:T(8,128)(2,1)S(1)}, u32[]{:S(2)}, u32[]{:S(2)}) collective-permute-start(bf16[128,3200]{1,0:T(8,128)(2,1)} %get-tuple-element.210), channel_id=1, source_target_pairs={{0,1},{1,0},{2,3},{3,2},{4,5},{5,4},{6,7},{7,6},{8,9},{9,8},{10,11... | collective-permute-start | bytes 2457608 | tf_op jit(solution)/shard_map/ppermute | solution.py:290
  215.9 17.7 %collective-permute-start.55 = (bf16[32,3200]{1,0:T(8,128)(2,1)S(1)}, bf16[32,3200]{1,0:T(8,128)(2,1)}, u32[]{:S(2)}, u32[]{:S(2)}) collective-permute-start(bf16[32,3200]{1,0:T(8,128)(2,1)S(1)} %multiply_convert_fusion.refs_0_), channel_id=1, source_target_pairs={{0,2},{1,3},{2,0},{3,1},{4,6},{5,7},{6,4},{7,5},{8,10},{9,11},{10,... | collective-permute-start | bytes 614408 | tf_op jit(solution)/shard_map/ppermute | solution.py:277
  219.5 17.7 %collective-permute-start.56 = (bf16[32,3200]{1,0:T(8,128)(2,1)S(1)}, bf16[32,3200]{1,0:T(8,128)(2,1)}, u32[]{:S(2)}, u32[]{:S(2)}) collective-permute-start(bf16[32,3200]{1,0:T(8,128)(2,1)S(1)} %multiply_convert_fusion.refs_0_), channel_id=1, source_target_pairs={{0,4},{1,5},{2,6},{3,7},{4,0},{5,1},{6,2},{7,3},{8,12},{9,13},{10,... | collective-permute-start | bytes 614408 | tf_op jit(solution)/shard_map/ppermute | solution.py:277
  220.6 16.7 %collective-permute-start.57 = (bf16[32,3200]{1,0:T(8,128)(2,1)S(1)}, bf16[32,3200]{1,0:T(8,128)(2,1)}, u32[]{:S(2)}, u32[]{:S(2)}) collective-permute-start(bf16[32,3200]{1,0:T(8,128)(2,1)S(1)} %multiply_convert_fusion.refs_0_), channel_id=1, source_target_pairs={{0,6},{1,7},{2,4},{3,5},{4,2},{5,3},{6,0},{7,1},{8,14},{9,15},{10,... | collective-permute-start | bytes 614408 | tf_op jit(solution)/shard_map/ppermute | solution.py:277
  223.7 5.6 %collective-permute-start.58 = (bf16[32,1024]{1,0:T(8,128)(2,1)S(1)}, bf16[32,1024]{1,0:T(8,128)(2,1)S(1)}, u32[]{:S(2)}, u32[]{:S(2)}) collective-permute-start(bf16[32,1024]{1,0:T(8,128)(2,1)S(1)} %get-tuple-element.301), channel_id=1, source_target_pairs={{0,8},{8,16},{16,24},{24,0},{1,9},{9,17},{17,25},{25,1},{2,10},{10... | collective-permute-start | bytes 196616 | tf_op jit(solution)/shard_map/ppermute | solution.py:430
  226.2 5.4 %collective-permute-start.59 = (bf16[32,1024]{1,0:T(8,128)(2,1)S(1)}, bf16[32,1024]{1,0:T(8,128)(2,1)S(1)}, u32[]{:S(2)}, u32[]{:S(2)}) collective-permute-start(bf16[32,1024]{1,0:T(8,128)(2,1)S(1)} %get-tuple-element.300), channel_id=1, source_target_pairs={{0,16},{8,24},{16,0},{24,8},{1,17},{9,25},{17,1},{25,9},{2,18},{10... | collective-permute-start | bytes 196616 | tf_op jit(solution)/shard_map/ppermute | solution.py:430
  237.3 5.7 %collective-permute-start.61 = (bf16[32,3200]{1,0:T(8,128)(2,1)S(1)}, bf16[32,3200]{1,0:T(8,128)(2,1)S(1)}, u32[]{:S(2)}, u32[]{:S(2)}) collective-permute-start(bf16[32,3200]{1,0:T(8,128)(2,1)S(1)} %multiply_convert_fusion.refs_0_), channel_id=1, source_target_pairs={{0,1},{1,0},{2,3},{3,2},{4,5},{5,4},{6,7},{7,6},{8,9},{9,8},{10,11... | collective-permute-start | bytes 614408 | tf_op jit(solution)/shard_map/ppermute | solution.py:283
  237.3 6.9 %collective-permute-start.62 = (bf16[32,3200]{1,0:T(8,128)(2,1)}, bf16[32,3200]{1,0:T(8,128)(2,1)S(1)}, u32[]{:S(2)}, u32[]{:S(2)}) collective-permute-start(bf16[32,3200]{1,0:T(8,128)(2,1)} %collective-permute-done.55.refs_1_), channel_id=1, source_target_pairs={{0,1},{1,0},{2,3},{3,2},{4,5},{5,4},{6,7},{7,6},{8,9},{9,8},{10,11... | collective-permute-start | bytes 614408 | tf_op jit(solution)/shard_map/ppermute | solution.py:283
  237.8 7.8 %collective-permute-start.63 = (bf16[32,3200]{1,0:T(8,128)(2,1)}, bf16[32,3200]{1,0:T(8,128)(2,1)S(1)}, u32[]{:S(2)}, u32[]{:S(2)}) collective-permute-start(bf16[32,3200]{1,0:T(8,128)(2,1)} %collective-permute-done.56.refs_2_), channel_id=1, source_target_pairs={{0,1},{1,0},{2,3},{3,2},{4,5},{5,4},{6,7},{7,6},{8,9},{9,8},{10,11... | collective-permute-start | bytes 614408 | tf_op jit(solution)/shard_map/ppermute | solution.py:283
  237.8 7.7 %collective-permute-start.64 = (bf16[32,3200]{1,0:T(8,128)(2,1)}, bf16[32,3200]{1,0:T(8,128)(2,1)S(1)}, u32[]{:S(2)}, u32[]{:S(2)}) collective-permute-start(bf16[32,3200]{1,0:T(8,128)(2,1)} %collective-permute-done.57.refs_3_), channel_id=1, source_target_pairs={{0,1},{1,0},{2,3},{3,2},{4,5},{5,4},{6,7},{7,6},{8,9},{9,8},{10,11... | collective-permute-start | bytes 614408 | tf_op jit(solution)/shard_map/ppermute | solution.py:283
  238.6 22.3 %collective-permute-start.65 = (bf16[32,3200]{1,0:T(8,128)(2,1)}, bf16[32,3200]{1,0:T(8,128)(2,1)S(1)}, u32[]{:S(2)}, u32[]{:S(2)}) collective-permute-start(bf16[32,3200]{1,0:T(8,128)(2,1)} %get-tuple-element.221), channel_id=1, source_target_pairs={{0,2},{1,3},{2,0},{3,1},{4,6},{5,7},{6,4},{7,5},{8,10},{9,11},{10,... | collective-permute-start | bytes 614408 | tf_op jit(solution)/shard_map/ppermute | solution.py:277
  242.9 18.0 %collective-permute-start.66 = (bf16[32,3200]{1,0:T(8,128)(2,1)}, bf16[32,3200]{1,0:T(8,128)(2,1)S(1)}, u32[]{:S(2)}, u32[]{:S(2)}) collective-permute-start(bf16[32,3200]{1,0:T(8,128)(2,1)} %get-tuple-element.222), channel_id=1, source_target_pairs={{0,4},{1,5},{2,6},{3,7},{4,0},{5,1},{6,2},{7,3},{8,12},{9,13},{10,... | collective-permute-start | bytes 614408 | tf_op jit(solution)/shard_map/ppermute | solution.py:277
  244.2 16.7 %collective-permute-start.67 = (bf16[32,3200]{1,0:T(8,128)(2,1)S(1)}, bf16[32,3200]{1,0:T(8,128)(2,1)S(1)}, u32[]{:S(2)}, u32[]{:S(2)}) collective-permute-start(bf16[32,3200]{1,0:T(8,128)(2,1)S(1)} %get-tuple-element.223), channel_id=1, source_target_pairs={{0,6},{1,7},{2,4},{3,5},{4,2},{5,3},{6,0},{7,1},{8,14},{9,15},{10,... | collective-permute-start | bytes 614408 | tf_op jit(solution)/shard_map/ppermute | solution.py:277
  263.8 12.7 %collective-permute-start.69 = (bf16[32,3200]{1,0:T(8,128)(2,1)S(1)}, bf16[32,3200]{1,0:T(8,128)(2,1)S(1)}, u32[]{:S(2)}, u32[]{:S(2)}) collective-permute-start(bf16[32,3200]{1,0:T(8,128)(2,1)S(1)} %get-tuple-element.279), channel_id=1, source_target_pairs={{0,2},{1,3},{2,0},{3,1},{4,6},{5,7},{6,4},{7,5},{8,10},{9,11},{10,... | collective-permute-start | bytes 614408 | tf_op jit(solution)/shard_map/ppermute | solution.py:277
  267.4 17.6 %collective-permute-start.70 = (bf16[32,3200]{1,0:T(8,128)(2,1)S(1)}, bf16[32,3200]{1,0:T(8,128)(2,1)S(1)}, u32[]{:S(2)}, u32[]{:S(2)}) collective-permute-start(bf16[32,3200]{1,0:T(8,128)(2,1)S(1)} %get-tuple-element.278), channel_id=1, source_target_pairs={{0,4},{1,5},{2,6},{3,7},{4,0},{5,1},{6,2},{7,3},{8,12},{9,13},{10,... | collective-permute-start | bytes 614408 | tf_op jit(solution)/shard_map/ppermute | solution.py:277
  268.5 16.6 %collective-permute-start.71 = (bf16[32,3200]{1,0:T(8,128)(2,1)S(1)}, bf16[32,3200]{1,0:T(8,128)(2,1)S(1)}, u32[]{:S(2)}, u32[]{:S(2)}) collective-permute-start(bf16[32,3200]{1,0:T(8,128)(2,1)S(1)} %get-tuple-element.277), channel_id=1, source_target_pairs={{0,6},{1,7},{2,4},{3,5},{4,2},{5,3},{6,0},{7,1},{8,14},{9,15},{10,... | collective-permute-start | bytes 614408 | tf_op jit(solution)/shard_map/ppermute | solution.py:277
  (69 other events, 460.4 us)

commit v10 on v9

--- a/solution.py
+++ b/solution.py
@@ -172,6 +172,26 @@
         return 0
 
     lax.fori_loop(0, held.shape[0], behind, 0)
+
+
+def entry_kernel(source, gain, *normed):
+    rows = normed[0].shape[0]
+    for c, out in enumerate(normed):
+        values = source[c * rows : (c + 1) * rows].astype(jnp.float32)
+        out[...] = layer_norm(values, gain[...], vis_eps)[0].astype(jnp.bfloat16)
+
+
+def entry_norm(source, gain):
+    rows, width = source.shape
+    return pl.pallas_call(
+        entry_kernel,
+        in_specs=whole_blocks(2),
+        out_specs=whole_blocks(chunks),
+        out_shape=[jax.ShapeDtypeStruct((rows // chunks, width), jnp.bfloat16)] * chunks,
+        cost_estimate=pl.CostEstimate(
+            flops=8 * rows * width, bytes_accessed=4 * rows * width, transcendentals=rows
+        ),
+    )(source, gain.reshape(1, width))
 
 
 def settings():
@@ -330,13 +350,9 @@
     rows = own_rows // chunks
     merged_rows = rows // fold
 
-    x, hat, inv, normed = [], [], [], []
-    for c in range(chunks):
-        x.append(vision_in[c * rows : (c + 1) * rows].astype(jnp.float32))
-        scaled, own_hat, own_inv = layer_norm(x[c], vis_gain, vis_eps)
-        normed.append(scaled.astype(jnp.bfloat16))
-        hat.append(own_hat)
-        inv.append(own_inv)
+    normed = list(entry_norm(vision_in, vis_gain))
+    x = [vision_in[c * rows : (c + 1) * rows].astype(jnp.float32) for c in range(chunks)]
+
     tied = lax.optimization_barrier
     rail_b = moves.spread(normed[1])
 
@@ -386,10 +402,11 @@
     mixed_b, *stats_b = merge(1, moves.summed(terms_b))
     rail_b = moves.spread(mixed_b)
     near_a, far_a, mixed_b = tied((near_a, far_a, mixed_b))
-    cut_a, rail_b, upstream = tied(
-        (moves.combine(near_a, far_a), rail_b, [grad_of(picked, c) for c in range(chunks)])
+    cut_a, upstream = tied(
+        (moves.combine(near_a, far_a), [grad_of(picked, c) for c in range(chunks)])
     )
     terms_a = moves.send(cut_a)
+    rail_b, terms_a[1] = tied((rail_b, terms_a[1]))
     merged_b = moves.gathered(rail_b)
     projected_b, delta_b = project(merged_b, proj_weight, upstream[1])
     projected_b, delta_b, terms_a = tied((projected_b, delta_b, terms_a))
@@ -448,9 +465,10 @@
     normed_b = moves.summed(terms_b)
     terms_a, seq_embed, normed_b = tied((terms_a, embed(text_embed, arrived), normed_b))
     normed_a = moves.summed(terms_a)
+    parts = [layer_norm(x[c], vis_gain, vis_eps) for c in range(chunks)]
     grads = [
-        own_a + norm_back(normed_a, vis_gain, hat[0], inv[0]),
-        own_b + norm_back(normed_b, vis_gain, hat[1], inv[1]),
+        own_a + norm_back(normed_a, vis_gain, parts[0][1], parts[0][2]),
+        own_b + norm_back(normed_b, vis_gain, parts[1][1], parts[1][2]),
     ]
     grad_vision = jnp.concatenate(grads, 0).astype(jnp.bfloat16)
     return (seq_embed, grad_vision)

time: 289 us -> 287 us (level)
  other arithmetic: 17.2 us -> 13.8 us
    unnamed x122 -> x118, local copies, waits for them, and re-layouts: 7.92 us -> 7.95 us
where the time goes in v10:
time: 287 us; the launch traced here: 285 us
  Pallas kernels  110 us (38%)
  starting transfers between devices  90.2 us (31%)
  waiting for transfers between devices  49.7 us (17%)
  local copies, waits for them, and re-layouts  17.4 us (6%)
  other arithmetic  13.8 us (5%)
    ppermute x36, starting transfers between devices, shift(): return lax.ppermute(block, 'tp', pairs)  73.2 us
    pallas_call x4, Pallas kernels, vision_pass(): pl.pallas_call(functools.partial(vision_kernel, len(pieces), slope is Non...  58.6 us
    ppermute x36, waiting for transfers between devices, shift(): return lax.ppermute(block, 'tp', pairs)  35.4 us
    pallas_call x2, Pallas kernels, project_back(): pl.pallas_call(project_back_kernel, in_specs=whole_blocks(1) + [pl.BlockS...  26.1 us
    pallas_call x2, Pallas kernels, project(): pl.pallas_call(functools.partial(project_kernel, len(pieces)), in_specs=w...  23.6 us
    unnamed x118, local copies, waits for them, and re-layouts  7.95 us
    another operation x7, other arithmetic  7.93 us
    ppermute x6, waiting for transfers between devices, combine(): got = lax.ppermute(far, 'tp', self.pairs)  6.92 us
  transfers between devices with their start and end apart: 72, of which 17 were waited for; matrix products, arithmetic and copies ran while one was open for 6% of the time, Pallas kernels for 38%

profile of v10, /device:TPU:0, one launch (start us, length us, event | category | flops | bytes accessed | tf_op | source)
XLA Modules:
  0.0 285.5 jit_solution(6663390399753866041)
XLA Ops:
  0.6 1.5 reshape.413.gain
  2.1 2.0 shard_map.113
  4.2 3.0 %collective-permute-start = (bf16[32,3200]{1,0:T(8,128)(2,1)}, bf16[32,3200]{1,0:T(8,128)(2,1)S(1)}, u32[]{:S(2)}, u32[]{:S(2)}) collective-permute-start(bf16[32,3200]{1,0:T(8,128)(2,1)} %get-tuple-element.128.refs_0_), channel_id=1, source_target_pairs={{0,2},{1,3},{2,0},{3,1},{4,6},{5,7},{6,4},{7,5},{8,10},{9,11},{10,... | collective-permute-start | bytes 614408 | tf_op jit(solution)/shard_map/ppermute | solution.py:297
  7.2 2.6 collective-permute-start.1
  12.5 2.7 collective-permute-start.3
  15.8 1.4 collective-permute-done.3
  17.2 2.4 collective-permute-start.5
  19.6 3.2 %collective-permute-done.5 = bf16[32,1024]{1,0:T(8,128)(2,1)S(1)} collective-permute-done((bf16[32,1024]{1,0:T(8,128)(2,1)S(1)}, bf16[32,1024]{1,0:T(8,128)(2,1)S(1)}, u32[]{:S(2)}, u32[]{:S(2)}) %collective-permute-start.5) | collective-permute-done | bytes 65568 | tf_op jit(solution)/shard_map/ppermute | solution.py:374
  22.8 2.4 collective-permute-done.1.refs_2_
  26.2 3.5 %collective-permute-start.10 = (bf16[32,3200]{1,0:T(8,128)(2,1)S(1)}, bf16[32,3200]{1,0:T(8,128)(2,1)S(1)}, u32[]{:S(2)}, u32[]{:S(2)}) collective-permute-start(bf16[32,3200]{1,0:T(8,128)(2,1)S(1)} %copy-done.14), channel_id=1, source_target_pairs={{0,2},{1,3},{2,0},{3,1},{4,6},{5,7},{6,4},{7,5},{8,10},{9,11},{10,... | collective-permute-start | bytes 614408 | tf_op jit(solution)/shard_map/ppermute | solution.py:297
  29.8 1.4 collective-permute-start.11
  31.2 1.4 collective-permute-start.12
  33.4 14.7 %shard_map.114 = (bf16[128,3200]{1,0:T(8,128)(2,1)}, bf16[128,3200]{1,0:T(8,128)(2,1)}, f32[7,256,256]{2,1,0:T(8,128)}) custom-call(bf16[32,3200]{1,0:T(8,128)(2,1)} %get-tuple-element.128.refs_0_, bf16[32,3200]{1,0:T(8,128)(2,1)} %copy-done.19, bf16[32,3200]{1,0:T(8,128)(2,1)} %collective-permute-done.1.refs_2_, ...), custom_call_target="tpu_custom_call" | custom-call | flops 5242880000 | bytes 25395200 | tf_op jit(solution)/shard_map/pallas_call | solution.py:212
  49.6 1.3 collective-permute-done.17
  50.9 1.6 fusion.51
  52.6 3.0 %collective-permute-start.18 = (bf16[32,3200]{1,0:T(8,128)(2,1)S(1)}, bf16[32,3200]{1,0:T(8,128)(2,1)S(1)}, u32[]{:S(2)}, u32[]{:S(2)}) collective-permute-start(bf16[32,3200]{1,0:T(8,128)(2,1)S(1)} %get-tuple-element.300), channel_id=1, source_target_pairs={{0,2},{1,3},{2,0},{3,1},{4,6},{5,7},{6,4},{7,5},{8,10},{9,11},{10,... | collective-permute-start | bytes 614408 | tf_op jit(solution)/shard_map/ppermute | solution.py:297
  56.7 1.5 collective-permute-start.20
  59.5 14.7 %shard_map.115 = (bf16[128,3200]{1,0:T(8,128)(2,1)}, bf16[128,3200]{1,0:T(8,128)(2,1)}, f32[7,256,256]{2,1,0:T(8,128)}) custom-call(bf16[32,3200]{1,0:T(8,128)(2,1)} %get-tuple-element.135.refs_0_, bf16[32,3200]{1,0:T(8,128)(2,1)} %copy-done.15, bf16[32,3200]{1,0:T(8,128)(2,1)} %copy-done.16, bf16[32,3200]{1,0:T(8,128)(2,1)} %copy-done.17, ...), custom_call_target="tpu_custom_call" | custom-call | flops 5242880000 | bytes 25395200 | tf_op jit(solution)/shard_map/pallas_call | solution.py:212
  76.0 2.8 collective-permute-start.21
  79.9 1.4 collective-permute-start.23
  83.1 1.2 gather_fusion.3
  84.3 1.6 fusion.52
  87.1 1.4 collective-permute-done.21.refs_1_
  88.5 8.0 %collective-permute-done.22.refs_2_ = bf16[8,12800]{1,0:T(8,128)(2,1)S(1)} collective-permute-done((bf16[8,12800]{1,0:T(8,128)(2,1)S(1)}, bf16[8,12800]{1,0:T(8,128)(2,1)S(1)}, u32[]{:S(2)}, u32[]{:S(2)}) %collective-permute-start.22) | collective-permute-done | bytes 204832 | tf_op jit(solution)/shard_map/ppermute | solution.py:297
  96.5 1.3 collective-permute-done.25
  98.8 4.0 %collective-permute-start.30 = (bf16[32,3200]{1,0:T(8,128)(2,1)S(1)}, bf16[32,3200]{1,0:T(8,128)(2,1)S(1)}, u32[]{:S(2)}, u32[]{:S(2)}) collective-permute-start(bf16[32,3200]{1,0:T(8,128)(2,1)S(1)} %get-tuple-element.169), channel_id=1, source_target_pairs={{0,4},{1,5},{2,6},{3,7},{4,0},{5,1},{6,2},{7,3},{8,12},{9,13},{10,... | collective-permute-start | bytes 614408 | tf_op jit(solution)/shard_map/ppermute | solution.py:297
  102.8 1.4 collective-permute-start.31
  105.6 11.8 %shard_map.116 = (bf16[64,1024]{1,0:T(8,128)(2,1)}, bf16[64,1024]{1,0:T(8,128)(2,1)}) custom-call(bf16[8,12800]{1,0:T(8,128)(2,1)} %copy-done.11, bf16[8,12800]{1,0:T(8,128)(2,1)} %copy-done.21, bf16[8,12800]{1,0:T(8,128)(2,1)} %copy-done.22, bf16[8,12800]{1,0:T(8,128)(2,1)} %copy-done.23, bf16[8,12800]{1,0:T(8,128)(2,1)} %copy-done.47, ...), custom_call_target="tpu_custom_call" | custom-call | flops 1677721600 | bytes 29753344 | tf_op jit(solution)/shard_map/pallas_call | solution.py:249
  118.7 4.5 %collective-permute-start.32 = (bf16[8,12800]{1,0:T(8,128)(2,1)S(1)}, bf16[8,12800]{1,0:T(8,128)(2,1)S(1)}, u32[]{:S(2)}, u32[]{:S(2)}) collective-permute-start(bf16[8,12800]{1,0:T(8,128)(2,1)S(1)} %multiply_convert_fusion.4.refs_0_), channel_id=1, source_target_pairs={{0,2},{1,3},{2,0},{3,1},{4,6},{5,7},{6,4},{7,5},{8,10},{9,11},{10,... | collective-permute-start | bytes 614408 | tf_op jit(solution)/shard_map/ppermute | solution.py:297
  123.6 2.0 collective-permute-start.34
  125.6 13.1 %shard_map.117 = (bf16[32,12800]{1,0:T(8,128)(2,1)}, bf16[32,12800]{1,0:T(8,128)(2,1)}) custom-call(bf16[64,1024]{1,0:T(8,128)(2,1)} %get-tuple-element.176.delta, bf16[12800,1024]{1,0:T(8,128)(2,1)} %weight.3), custom_call_target="tpu_custom_call" | custom-call | flops 1677721600 | bytes 29753344 | tf_op jit(solution)/shard_map/pallas_call | solution.py:269
  138.7 2.0 collective-permute-done.33.refs_2_
  141.9 1.7 collective-permute-done.39
  143.6 1.3 fusion.53
  145.0 3.6 %collective-permute-start.40 = (bf16[8,12800]{1,0:T(8,128)(2,1)S(1)}, bf16[8,12800]{1,0:T(8,128)(2,1)S(1)}, u32[]{:S(2)}, u32[]{:S(2)}) collective-permute-start(bf16[8,12800]{1,0:T(8,128)(2,1)S(1)} %get-tuple-element.294), channel_id=1, source_target_pairs={{0,2},{1,3},{2,0},{3,1},{4,6},{5,7},{6,4},{7,5},{8,10},{9,11},{10,... | collective-permute-start | bytes 614408 | tf_op jit(solution)/shard_map/ppermute | solution.py:297
  148.7 2.4 collective-permute-start.42
  152.5 11.8 %shard_map.118 = (bf16[64,1024]{1,0:T(8,128)(2,1)}, bf16[64,1024]{1,0:T(8,128)(2,1)}) custom-call(bf16[8,12800]{1,0:T(8,128)(2,1)} %copy-done.12, bf16[8,12800]{1,0:T(8,128)(2,1)} %copy-done.26, bf16[8,12800]{1,0:T(8,128)(2,1)} %copy-done.28, bf16[8,12800]{1,0:T(8,128)(2,1)} %copy-done.29, bf16[8,12800]{1,0:T(8,128)(2,1)} %copy-done.32, ...), custom_call_target="tpu_custom_call" | custom-call | flops 1677721600 | bytes 29753344 | tf_op jit(solution)/shard_map/pallas_call | solution.py:249
  164.3 2.0 collective-permute-done.41
  166.9 3.9 %collective-permute-start.43 = (bf16[32,3200]{1,0:T(8,128)(2,1)S(1)}, bf16[32,3200]{1,0:T(8,128)(2,1)S(1)}, u32[]{:S(2)}, u32[]{:S(2)}) collective-permute-start(bf16[32,3200]{1,0:T(8,128)(2,1)S(1)} %multiply_convert_fusion.2.refs_0_), channel_id=1, source_target_pairs={{0,2},{1,3},{2,0},{3,1},{4,6},{5,7},{6,4},{7,5},{8,10},{9,11},{10,... | collective-permute-start | bytes 614408 | tf_op jit(solution)/shard_map/ppermute | solution.py:297
  170.9 2.4 collective-permute-start.45
  173.3 13.1 %shard_map.119 = (bf16[32,12800]{1,0:T(8,128)(2,1)}, bf16[32,12800]{1,0:T(8,128)(2,1)}) custom-call(bf16[64,1024]{1,0:T(8,128)(2,1)} %get-tuple-element.193.delta, bf16[12800,1024]{1,0:T(8,128)(2,1)} %weight.3), custom_call_target="tpu_custom_call" | custom-call | flops 1677721600 | bytes 29753344 | tf_op jit(solution)/shard_map/pallas_call | solution.py:269
  186.4 1.6 collective-permute-done.44.refs_2_
  189.3 1.5 collective-permute-done.50
  190.8 1.3 fusion.54
  192.2 3.4 %collective-permute-start.51 = (bf16[8,12800]{1,0:T(8,128)(2,1)S(1)}, bf16[8,12800]{1,0:T(8,128)(2,1)S(1)}, u32[]{:S(2)}, u32[]{:S(2)}) collective-permute-start(bf16[8,12800]{1,0:T(8,128)(2,1)S(1)} %get-tuple-element.291), channel_id=1, source_target_pairs={{0,2},{1,3},{2,0},{3,1},{4,6},{5,7},{6,4},{7,5},{8,10},{9,11},{10,... | collective-permute-start | bytes 614408 | tf_op jit(solution)/shard_map/ppermute | solution.py:297
  195.6 2.4 collective-permute-start.53
  198.8 14.6 %shard_map.120 = (bf16[128,3200]{1,0:T(8,128)(2,1)}, bf16[128,3200]{1,0:T(8,128)(2,1)}) custom-call(bf16[32,3200]{1,0:T(8,128)(2,1)} %copy-done.10, bf16[32,3200]{1,0:T(8,128)(2,1)} %copy-done.24, bf16[32,3200]{1,0:T(8,128)(2,1)} %copy-done.25, bf16[32,3200]{1,0:T(8,128)(2,1)} %copy-done.27, bf16[32,3200]{1,0:T(8,128)(2,1)} %copy-done.30, ...), custom_call_target="tpu_custom_call" | custom-call | flops 5242880000 | bytes 25395200 | tf_op jit(solution)/shard_map/pallas_call | solution.py:212
  214.6 3.7 %collective-permute-start.55 = (bf16[32,3200]{1,0:T(8,128)(2,1)S(1)}, bf16[32,3200]{1,0:T(8,128)(2,1)S(1)}, u32[]{:S(2)}, u32[]{:S(2)}) collective-permute-start(bf16[32,3200]{1,0:T(8,128)(2,1)S(1)} %multiply_convert_fusion.refs_0_), channel_id=1, source_target_pairs={{0,2},{1,3},{2,0},{3,1},{4,6},{5,7},{6,4},{7,5},{8,10},{9,11},{10,... | collective-permute-start | bytes 614408 | tf_op jit(solution)/shard_map/ppermute | solution.py:297
  218.3 2.4 collective-permute-start.57
  222.5 1.5 collective-permute-start.58
  224.9 1.5 collective-permute-start.59
  226.5 1.6 fusion.55
  228.1 1.5 collective-permute-start.60
  229.6 2.7 collective-permute-done.60
  232.4 3.6 %collective-permute-done.56.refs_2_ = bf16[32,3200]{1,0:T(8,128)(2,1)} collective-permute-done((bf16[32,3200]{1,0:T(8,128)(2,1)S(1)}, bf16[32,3200]{1,0:T(8,128)(2,1)}, u32[]{:S(2)}, u32[]{:S(2)}) %collective-permute-start.56) | collective-permute-done | bytes 204832 | tf_op jit(solution)/shard_map/ppermute | solution.py:297
  237.1 4.2 %collective-permute-start.65 = (bf16[32,3200]{1,0:T(8,128)(2,1)S(1)}, bf16[32,3200]{1,0:T(8,128)(2,1)S(1)}, u32[]{:S(2)}, u32[]{:S(2)}) collective-permute-start(bf16[32,3200]{1,0:T(8,128)(2,1)S(1)} %get-tuple-element.227), channel_id=1, source_target_pairs={{0,2},{1,3},{2,0},{3,1},{4,6},{5,7},{6,4},{7,5},{8,10},{9,11},{10,... | collective-permute-start | bytes 614408 | tf_op jit(solution)/shard_map/ppermute | solution.py:297
  241.7 2.4 collective-permute-start.67
  244.9 14.6 %shard_map.121 = (bf16[128,3200]{1,0:T(8,128)(2,1)}, bf16[128,3200]{1,0:T(8,128)(2,1)}) custom-call(bf16[32,3200]{1,0:T(8,128)(2,1)} %copy-done.9, bf16[32,3200]{1,0:T(8,128)(2,1)} %copy-done.20, bf16[32,3200]{1,0:T(8,128)(2,1)} %collective-permute-done.56.refs_2_, bf16[32,3200]{1,0:T(8,128)(2,1)} %collective-permute-done.57.refs_3_, ...), custom_call_target="tpu_custom_call" | custom-call | flops 5242880000 | bytes 25395200 | tf_op jit(solution)/shard_map/pallas_call | solution.py:212
  259.7 2.4 collective-permute-done.68
  262.4 3.2 %collective-permute-start.69 = (bf16[32,3200]{1,0:T(8,128)(2,1)S(1)}, bf16[32,3200]{1,0:T(8,128)(2,1)S(1)}, u32[]{:S(2)}, u32[]{:S(2)}) collective-permute-start(bf16[32,3200]{1,0:T(8,128)(2,1)S(1)} %get-tuple-element.285), channel_id=1, source_target_pairs={{0,2},{1,3},{2,0},{3,1},{4,6},{5,7},{6,4},{7,5},{8,10},{9,11},{10,... | collective-permute-start | bytes 614408 | tf_op jit(solution)/shard_map/ppermute | solution.py:297
  265.6 2.4 collective-permute-start.71
  268.0 2.2 fusion
  270.2 3.9 %collective-permute-done.69 = bf16[32,3200]{1,0:T(8,128)(2,1)S(1)} collective-permute-done((bf16[32,3200]{1,0:T(8,128)(2,1)S(1)}, bf16[32,3200]{1,0:T(8,128)(2,1)S(1)}, u32[]{:S(2)}, u32[]{:S(2)}) %collective-permute-start.69) | collective-permute-done | bytes 204832 | tf_op jit(solution)/shard_map/ppermute | solution.py:297
  274.1 9.0 %collective-permute-done.70 = bf16[32,3200]{1,0:T(8,128)(2,1)S(1)} collective-permute-done((bf16[32,3200]{1,0:T(8,128)(2,1)S(1)}, bf16[32,3200]{1,0:T(8,128)(2,1)S(1)}, u32[]{:S(2)}, u32[]{:S(2)}) %collective-permute-start.70) | collective-permute-done | bytes 204832 | tf_op jit(solution)/shard_map/ppermute | solution.py:297
  (311 shorter events, 32.8 us)
Async XLA Ops:
  4.2 18.6 %collective-permute-start = (bf16[32,3200]{1,0:T(8,128)(2,1)}, bf16[32,3200]{1,0:T(8,128)(2,1)S(1)}, u32[]{:S(2)}, u32[]{:S(2)}) collective-permute-start(bf16[32,3200]{1,0:T(8,128)(2,1)} %get-tuple-element.128.refs_0_), channel_id=1, source_target_pairs={{0,2},{1,3},{2,0},{3,1},{4,6},{5,7},{6,4},{7,5},{8,10},{9,11},{10,... | collective-permute-start | bytes 614408 | tf_op jit(solution)/shard_map/ppermute | solution.py:297
  7.2 18.0 %collective-permute-start.1 = (bf16[32,3200]{1,0:T(8,128)(2,1)}, bf16[32,3200]{1,0:T(8,128)(2,1)}, u32[]{:S(2)}, u32[]{:S(2)}) collective-permute-start(bf16[32,3200]{1,0:T(8,128)(2,1)} %get-tuple-element.128.refs_0_), channel_id=1, source_target_pairs={{0,4},{1,5},{2,6},{3,7},{4,0},{5,1},{6,2},{7,3},{8,12},{9,13},{10,... | collective-permute-start | bytes 614408 | tf_op jit(solution)/shard_map/ppermute | solution.py:297
  9.8 15.4 %collective-permute-start.2 = (bf16[32,3200]{1,0:T(8,128)(2,1)}, bf16[32,3200]{1,0:T(8,128)(2,1)}, u32[]{:S(2)}, u32[]{:S(2)}) collective-permute-start(bf16[32,3200]{1,0:T(8,128)(2,1)} %get-tuple-element.128.refs_0_), channel_id=1, source_target_pairs={{0,6},{1,7},{2,4},{3,5},{4,2},{5,3},{6,0},{7,1},{8,14},{9,15},{10,... | collective-permute-start | bytes 614408 | tf_op jit(solution)/shard_map/ppermute | solution.py:297
  17.2 5.6 %collective-permute-start.5 = (bf16[32,1024]{1,0:T(8,128)(2,1)S(1)}, bf16[32,1024]{1,0:T(8,128)(2,1)S(1)}, u32[]{:S(2)}, u32[]{:S(2)}) collective-permute-start(bf16[32,1024]{1,0:T(8,128)(2,1)S(1)} %get-tuple-element.311), channel_id=1, source_target_pairs={{0,8},{8,16},{16,24},{24,0},{1,9},{9,17},{17,25},{25,1},{2,10},{10... | collective-permute-start | bytes 196616 | tf_op jit(solution)/shard_map/ppermute | solution.py:374
  25.2 6.0 %collective-permute-start.7 = (bf16[32,3200]{1,0:T(8,128)(2,1)S(1)}, bf16[32,3200]{1,0:T(8,128)(2,1)S(1)}, u32[]{:S(2)}, u32[]{:S(2)}) collective-permute-start(bf16[32,3200]{1,0:T(8,128)(2,1)S(1)} %collective-permute-done.refs_1_), channel_id=1, source_target_pairs={{0,1},{1,0},{2,3},{3,2},{4,5},{5,4},{6,7},{7,6},{8,9},{9,8},{10,11... | collective-permute-start | bytes 614408 | tf_op jit(solution)/shard_map/ppermute | solution.py:303
  25.7 6.9 %collective-permute-start.8 = (bf16[32,3200]{1,0:T(8,128)(2,1)}, bf16[32,3200]{1,0:T(8,128)(2,1)S(1)}, u32[]{:S(2)}, u32[]{:S(2)}) collective-permute-start(bf16[32,3200]{1,0:T(8,128)(2,1)} %collective-permute-done.1.refs_2_), channel_id=1, source_target_pairs={{0,1},{1,0},{2,3},{3,2},{4,5},{5,4},{6,7},{7,6},{8,9},{9,8},{10,11... | collective-permute-start | bytes 614408 | tf_op jit(solution)/shard_map/ppermute | solution.py:303
  25.8 6.9 %collective-permute-start.9 = (bf16[32,3200]{1,0:T(8,128)(2,1)}, bf16[32,3200]{1,0:T(8,128)(2,1)S(1)}, u32[]{:S(2)}, u32[]{:S(2)}) collective-permute-start(bf16[32,3200]{1,0:T(8,128)(2,1)} %collective-permute-done.2.refs_3_), channel_id=1, source_target_pairs={{0,1},{1,0},{2,3},{3,2},{4,5},{5,4},{6,7},{7,6},{8,9},{9,8},{10,11... | collective-permute-start | bytes 614408 | tf_op jit(solution)/shard_map/ppermute | solution.py:303
  26.2 21.9 %collective-permute-start.10 = (bf16[32,3200]{1,0:T(8,128)(2,1)S(1)}, bf16[32,3200]{1,0:T(8,128)(2,1)S(1)}, u32[]{:S(2)}, u32[]{:S(2)}) collective-permute-start(bf16[32,3200]{1,0:T(8,128)(2,1)S(1)} %copy-done.14), channel_id=1, source_target_pairs={{0,2},{1,3},{2,0},{3,1},{4,6},{5,7},{6,4},{7,5},{8,10},{9,11},{10,... | collective-permute-start | bytes 614408 | tf_op jit(solution)/shard_map/ppermute | solution.py:297
  29.8 18.4 %collective-permute-start.11 = (bf16[32,3200]{1,0:T(8,128)(2,1)S(1)}, bf16[32,3200]{1,0:T(8,128)(2,1)S(1)}, u32[]{:S(2)}, u32[]{:S(2)}) collective-permute-start(bf16[32,3200]{1,0:T(8,128)(2,1)S(1)} %copy-done.14), channel_id=1, source_target_pairs={{0,4},{1,5},{2,6},{3,7},{4,0},{5,1},{6,2},{7,3},{8,12},{9,13},{10,... | collective-permute-start | bytes 614408 | tf_op jit(solution)/shard_map/ppermute | solution.py:297
  31.2 17.0 %collective-permute-start.12 = (bf16[32,3200]{1,0:T(8,128)(2,1)S(1)}, bf16[32,3200]{1,0:T(8,128)(2,1)S(1)}, u32[]{:S(2)}, u32[]{:S(2)}) collective-permute-start(bf16[32,3200]{1,0:T(8,128)(2,1)S(1)} %copy-done.14), channel_id=1, source_target_pairs={{0,6},{1,7},{2,4},{3,5},{4,2},{5,3},{6,0},{7,1},{8,14},{9,15},{10,... | collective-permute-start | bytes 614408 | tf_op jit(solution)/shard_map/ppermute | solution.py:297
  48.5 7.1 %collective-permute-start.13 = (bf16[32,3200]{1,0:T(8,128)(2,1)S(1)}, bf16[32,3200]{1,0:T(8,128)(2,1)S(1)}, u32[]{:S(2)}, u32[]{:S(2)}) collective-permute-start(bf16[32,3200]{1,0:T(8,128)(2,1)S(1)} %copy-done.14), channel_id=1, source_target_pairs={{0,1},{1,0},{2,3},{3,2},{4,5},{5,4},{6,7},{7,6},{8,9},{9,8},{10,11... | collective-permute-start | bytes 614408 | tf_op jit(solution)/shard_map/ppermute | solution.py:303
  49.0 7.6 %collective-permute-start.14 = (bf16[32,3200]{1,0:T(8,128)(2,1)S(1)}, bf16[32,3200]{1,0:T(8,128)(2,1)S(1)}, u32[]{:S(2)}, u32[]{:S(2)}) collective-permute-start(bf16[32,3200]{1,0:T(8,128)(2,1)S(1)} %collective-permute-done.10.refs_1_), channel_id=1, source_target_pairs={{0,1},{1,0},{2,3},{3,2},{4,5},{5,4},{6,7},{7,6},{8,9},{9,8},{10,11... | collective-permute-start | bytes 614408 | tf_op jit(solution)/shard_map/ppermute | solution.py:303
  49.1 9.0 %collective-permute-start.15 = (bf16[32,3200]{1,0:T(8,128)(2,1)S(1)}, bf16[32,3200]{1,0:T(8,128)(2,1)S(1)}, u32[]{:S(2)}, u32[]{:S(2)}) collective-permute-start(bf16[32,3200]{1,0:T(8,128)(2,1)S(1)} %collective-permute-done.11.refs_2_), channel_id=1, source_target_pairs={{0,1},{1,0},{2,3},{3,2},{4,5},{5,4},{6,7},{7,6},{8,9},{9,8},{10,11... | collective-permute-start | bytes 614408 | tf_op jit(solution)/shard_map/ppermute | solution.py:303
  49.5 8.6 %collective-permute-start.16 = (bf16[32,3200]{1,0:T(8,128)(2,1)S(1)}, bf16[32,3200]{1,0:T(8,128)(2,1)S(1)}, u32[]{:S(2)}, u32[]{:S(2)}) collective-permute-start(bf16[32,3200]{1,0:T(8,128)(2,1)S(1)} %collective-permute-done.12.refs_3_), channel_id=1, source_target_pairs={{0,1},{1,0},{2,3},{3,2},{4,5},{5,4},{6,7},{7,6},{8,9},{9,8},{10,11... | collective-permute-start | bytes 614408 | tf_op jit(solution)/shard_map/ppermute | solution.py:303
  52.6 21.6 %collective-permute-start.18 = (bf16[32,3200]{1,0:T(8,128)(2,1)S(1)}, bf16[32,3200]{1,0:T(8,128)(2,1)S(1)}, u32[]{:S(2)}, u32[]{:S(2)}) collective-permute-start(bf16[32,3200]{1,0:T(8,128)(2,1)S(1)} %get-tuple-element.300), channel_id=1, source_target_pairs={{0,2},{1,3},{2,0},{3,1},{4,6},{5,7},{6,4},{7,5},{8,10},{9,11},{10,... | collective-permute-start | bytes 614408 | tf_op jit(solution)/shard_map/ppermute | solution.py:297
  55.6 18.7 %collective-permute-start.19 = (bf16[32,3200]{1,0:T(8,128)(2,1)S(1)}, bf16[32,3200]{1,0:T(8,128)(2,1)S(1)}, u32[]{:S(2)}, u32[]{:S(2)}) collective-permute-start(bf16[32,3200]{1,0:T(8,128)(2,1)S(1)} %get-tuple-element.299), channel_id=1, source_target_pairs={{0,4},{1,5},{2,6},{3,7},{4,0},{5,1},{6,2},{7,3},{8,12},{9,13},{10,... | collective-permute-start | bytes 614408 | tf_op jit(solution)/shard_map/ppermute | solution.py:297
  56.7 17.6 %collective-permute-start.20 = (bf16[32,3200]{1,0:T(8,128)(2,1)S(1)}, bf16[32,3200]{1,0:T(8,128)(2,1)S(1)}, u32[]{:S(2)}, u32[]{:S(2)}) collective-permute-start(bf16[32,3200]{1,0:T(8,128)(2,1)S(1)} %get-tuple-element.298), channel_id=1, source_target_pairs={{0,6},{1,7},{2,4},{3,5},{4,2},{5,3},{6,0},{7,1},{8,14},{9,15},{10,... | collective-permute-start | bytes 614408 | tf_op jit(solution)/shard_map/ppermute | solution.py:297
  75.8 8.6 %collective-permute-start.24 = (bf16[128,3200]{1,0:T(8,128)(2,1)}, bf16[128,3200]{1,0:T(8,128)(2,1)}, u32[]{:S(2)}, u32[]{:S(2)}) collective-permute-start(bf16[128,3200]{1,0:T(8,128)(2,1)} %get-tuple-element.154), channel_id=1, source_target_pairs={{0,1},{1,0},{2,3},{3,2},{4,5},{5,4},{6,7},{7,6},{8,9},{9,8},{10,11... | collective-permute-start | bytes 2457608 | tf_op jit(solution)/shard_map/ppermute | solution.py:310
  76.0 12.5 %collective-permute-start.21 = (bf16[8,12800]{1,0:T(8,128)(2,1)S(1)}, bf16[8,12800]{1,0:T(8,128)(2,1)S(1)}, u32[]{:S(2)}, u32[]{:S(2)}) collective-permute-start(bf16[8,12800]{1,0:T(8,128)(2,1)S(1)} %multiply_convert_fusion.5.refs_0_), channel_id=1, source_target_pairs={{0,2},{1,3},{2,0},{3,1},{4,6},{5,7},{6,4},{7,5},{8,10},{9,11},{10,... | collective-permute-start | bytes 614408 | tf_op jit(solution)/shard_map/ppermute | solution.py:297
  78.8 17.7 %collective-permute-start.22 = (bf16[8,12800]{1,0:T(8,128)(2,1)S(1)}, bf16[8,12800]{1,0:T(8,128)(2,1)S(1)}, u32[]{:S(2)}, u32[]{:S(2)}) collective-permute-start(bf16[8,12800]{1,0:T(8,128)(2,1)S(1)} %multiply_convert_fusion.5.refs_0_), channel_id=1, source_target_pairs={{0,4},{1,5},{2,6},{3,7},{4,0},{5,1},{6,2},{7,3},{8,12},{9,13},{10,... | collective-permute-start | bytes 614408 | tf_op jit(solution)/shard_map/ppermute | solution.py:297
  79.9 16.6 %collective-permute-start.23 = (bf16[8,12800]{1,0:T(8,128)(2,1)S(1)}, bf16[8,12800]{1,0:T(8,128)(2,1)S(1)}, u32[]{:S(2)}, u32[]{:S(2)}) collective-permute-start(bf16[8,12800]{1,0:T(8,128)(2,1)S(1)} %multiply_convert_fusion.5.refs_0_), channel_id=1, source_target_pairs={{0,6},{1,7},{2,4},{3,5},{4,2},{5,3},{6,0},{7,1},{8,14},{9,15},{10,... | collective-permute-start | bytes 614408 | tf_op jit(solution)/shard_map/ppermute | solution.py:297
  86.0 11.8 %collective-permute-start.25 = (bf16[32,3200]{1,0:T(8,128)(2,1)S(1)}, bf16[32,3200]{1,0:T(8,128)(2,1)S(1)}, u32[]{:S(2)}, u32[]{:S(2)}) collective-permute-start(bf16[32,3200]{1,0:T(8,128)(2,1)S(1)} %get-tuple-element.159), channel_id=1, source_target_pairs={{0,2},{1,3},{2,0},{3,1},{4,6},{5,7},{6,4},{7,5},{8,10},{9,11},{10,... | collective-permute-start | bytes 614408 | tf_op jit(solution)/shard_map/ppermute | solution.py:297
  97.8 5.0 %collective-permute-start.26 = (bf16[8,12800]{1,0:T(8,128)(2,1)S(1)}, bf16[8,12800]{1,0:T(8,128)(2,1)S(1)}, u32[]{:S(2)}, u32[]{:S(2)}) collective-permute-start(bf16[8,12800]{1,0:T(8,128)(2,1)S(1)} %multiply_convert_fusion.5.refs_0_), channel_id=1, source_target_pairs={{0,1},{1,0},{2,3},{3,2},{4,5},{5,4},{6,7},{7,6},{8,9},{9,8},{10,11... | collective-permute-start | bytes 614408 | tf_op jit(solution)/shard_map/ppermute | solution.py:303
  97.8 6.4 %collective-permute-start.27 = (bf16[8,12800]{1,0:T(8,128)(2,1)S(1)}, bf16[8,12800]{1,0:T(8,128)(2,1)S(1)}, u32[]{:S(2)}, u32[]{:S(2)}) collective-permute-start(bf16[8,12800]{1,0:T(8,128)(2,1)S(1)} %collective-permute-done.21.refs_1_), channel_id=1, source_target_pairs={{0,1},{1,0},{2,3},{3,2},{4,5},{5,4},{6,7},{7,6},{8,9},{9,8},{10,11... | collective-permute-start | bytes 614408 | tf_op jit(solution)/shard_map/ppermute | solution.py:303
  98.3 5.9 %collective-permute-start.28 = (bf16[8,12800]{1,0:T(8,128)(2,1)S(1)}, bf16[8,12800]{1,0:T(8,128)(2,1)S(1)}, u32[]{:S(2)}, u32[]{:S(2)}) collective-permute-start(bf16[8,12800]{1,0:T(8,128)(2,1)S(1)} %collective-permute-done.22.refs_2_), channel_id=1, source_target_pairs={{0,1},{1,0},{2,3},{3,2},{4,5},{5,4},{6,7},{7,6},{8,9},{9,8},{10,11... | collective-permute-start | bytes 614408 | tf_op jit(solution)/shard_map/ppermute | solution.py:303
  98.3 5.9 %collective-permute-start.29 = (bf16[8,12800]{1,0:T(8,128)(2,1)S(1)}, bf16[8,12800]{1,0:T(8,128)(2,1)S(1)}, u32[]{:S(2)}, u32[]{:S(2)}) collective-permute-start(bf16[8,12800]{1,0:T(8,128)(2,1)S(1)} %collective-permute-done.23.refs_3_), channel_id=1, source_target_pairs={{0,1},{1,0},{2,3},{3,2},{4,5},{5,4},{6,7},{7,6},{8,9},{9,8},{10,11... | collective-permute-start | bytes 614408 | tf_op jit(solution)/shard_map/ppermute | solution.py:303
  98.8 18.6 %collective-permute-start.30 = (bf16[32,3200]{1,0:T(8,128)(2,1)S(1)}, bf16[32,3200]{1,0:T(8,128)(2,1)S(1)}, u32[]{:S(2)}, u32[]{:S(2)}) collective-permute-start(bf16[32,3200]{1,0:T(8,128)(2,1)S(1)} %get-tuple-element.169), channel_id=1, source_target_pairs={{0,4},{1,5},{2,6},{3,7},{4,0},{5,1},{6,2},{7,3},{8,12},{9,13},{10,... | collective-permute-start | bytes 614408 | tf_op jit(solution)/shard_map/ppermute | solution.py:297
  102.8 14.6 %collective-permute-start.31 = (bf16[32,3200]{1,0:T(8,128)(2,1)S(1)}, bf16[32,3200]{1,0:T(8,128)(2,1)S(1)}, u32[]{:S(2)}, u32[]{:S(2)}) collective-permute-start(bf16[32,3200]{1,0:T(8,128)(2,1)S(1)} %get-tuple-element.170), channel_id=1, source_target_pairs={{0,6},{1,7},{2,4},{3,5},{4,2},{5,3},{6,0},{7,1},{8,14},{9,15},{10,... | collective-permute-start | bytes 614408 | tf_op jit(solution)/shard_map/ppermute | solution.py:297
  118.7 20.0 %collective-permute-start.32 = (bf16[8,12800]{1,0:T(8,128)(2,1)S(1)}, bf16[8,12800]{1,0:T(8,128)(2,1)S(1)}, u32[]{:S(2)}, u32[]{:S(2)}) collective-permute-start(bf16[8,12800]{1,0:T(8,128)(2,1)S(1)} %multiply_convert_fusion.4.refs_0_), channel_id=1, source_target_pairs={{0,2},{1,3},{2,0},{3,1},{4,6},{5,7},{6,4},{7,5},{8,10},{9,11},{10,... | collective-permute-start | bytes 614408 | tf_op jit(solution)/shard_map/ppermute | solution.py:297
  123.2 17.5 %collective-permute-start.33 = (bf16[8,12800]{1,0:T(8,128)(2,1)S(1)}, bf16[8,12800]{1,0:T(8,128)(2,1)S(1)}, u32[]{:S(2)}, u32[]{:S(2)}) collective-permute-start(bf16[8,12800]{1,0:T(8,128)(2,1)S(1)} %multiply_convert_fusion.4.refs_0_), channel_id=1, source_target_pairs={{0,4},{1,5},{2,6},{3,7},{4,0},{5,1},{6,2},{7,3},{8,12},{9,13},{10,... | collective-permute-start | bytes 614408 | tf_op jit(solution)/shard_map/ppermute | solution.py:297
  123.6 17.0 %collective-permute-start.34 = (bf16[8,12800]{1,0:T(8,128)(2,1)S(1)}, bf16[8,12800]{1,0:T(8,128)(2,1)S(1)}, u32[]{:S(2)}, u32[]{:S(2)}) collective-permute-start(bf16[8,12800]{1,0:T(8,128)(2,1)S(1)} %multiply_convert_fusion.4.refs_0_), channel_id=1, source_target_pairs={{0,6},{1,7},{2,4},{3,5},{4,2},{5,3},{6,0},{7,1},{8,14},{9,15},{10,... | collective-permute-start | bytes 614408 | tf_op jit(solution)/shard_map/ppermute | solution.py:297
  140.8 7.8 %collective-permute-start.35 = (bf16[8,12800]{1,0:T(8,128)(2,1)S(1)}, bf16[8,12800]{1,0:T(8,128)(2,1)S(1)}, u32[]{:S(2)}, u32[]{:S(2)}) collective-permute-start(bf16[8,12800]{1,0:T(8,128)(2,1)S(1)} %multiply_convert_fusion.4.refs_0_), channel_id=1, source_target_pairs={{0,1},{1,0},{2,3},{3,2},{4,5},{5,4},{6,7},{7,6},{8,9},{9,8},{10,11... | collective-permute-start | bytes 614408 | tf_op jit(solution)/shard_map/ppermute | solution.py:303
  141.3 7.4 %collective-permute-start.36 = (bf16[8,12800]{1,0:T(8,128)(2,1)S(1)}, bf16[8,12800]{1,0:T(8,128)(2,1)S(1)}, u32[]{:S(2)}, u32[]{:S(2)}) collective-permute-start(bf16[8,12800]{1,0:T(8,128)(2,1)S(1)} %collective-permute-done.32.refs_1_), channel_id=1, source_target_pairs={{0,1},{1,0},{2,3},{3,2},{4,5},{5,4},{6,7},{7,6},{8,9},{9,8},{10,11... | collective-permute-start | bytes 614408 | tf_op jit(solution)/shard_map/ppermute | solution.py:303
  141.4 9.7 %collective-permute-start.37 = (bf16[8,12800]{1,0:T(8,128)(2,1)S(1)}, bf16[8,12800]{1,0:T(8,128)(2,1)S(1)}, u32[]{:S(2)}, u32[]{:S(2)}) collective-permute-start(bf16[8,12800]{1,0:T(8,128)(2,1)S(1)} %collective-permute-done.33.refs_2_), channel_id=1, source_target_pairs={{0,1},{1,0},{2,3},{3,2},{4,5},{5,4},{6,7},{7,6},{8,9},{9,8},{10,11... | collective-permute-start | bytes 614408 | tf_op jit(solution)/shard_map/ppermute | solution.py:303
  141.8 9.3 %collective-permute-start.38 = (bf16[8,12800]{1,0:T(8,128)(2,1)S(1)}, bf16[8,12800]{1,0:T(8,128)(2,1)S(1)}, u32[]{:S(2)}, u32[]{:S(2)}) collective-permute-start(bf16[8,12800]{1,0:T(8,128)(2,1)S(1)} %collective-permute-done.34.refs_3_), channel_id=1, source_target_pairs={{0,1},{1,0},{2,3},{3,2},{4,5},{5,4},{6,7},{7,6},{8,9},{9,8},{10,11... | collective-permute-start | bytes 614408 | tf_op jit(solution)/shard_map/ppermute | solution.py:303
  145.0 19.3 %collective-permute-start.40 = (bf16[8,12800]{1,0:T(8,128)(2,1)S(1)}, bf16[8,12800]{1,0:T(8,128)(2,1)S(1)}, u32[]{:S(2)}, u32[]{:S(2)}) collective-permute-start(bf16[8,12800]{1,0:T(8,128)(2,1)S(1)} %get-tuple-element.294), channel_id=1, source_target_pairs={{0,2},{1,3},{2,0},{3,1},{4,6},{5,7},{6,4},{7,5},{8,10},{9,11},{10,... | collective-permute-start | bytes 614408 | tf_op jit(solution)/shard_map/ppermute | solution.py:297
  148.6 17.6 %collective-permute-start.41 = (bf16[8,12800]{1,0:T(8,128)(2,1)S(1)}, bf16[8,12800]{1,0:T(8,128)(2,1)S(1)}, u32[]{:S(2)}, u32[]{:S(2)}) collective-permute-start(bf16[8,12800]{1,0:T(8,128)(2,1)S(1)} %get-tuple-element.293), channel_id=1, source_target_pairs={{0,4},{1,5},{2,6},{3,7},{4,0},{5,1},{6,2},{7,3},{8,12},{9,13},{10,... | collective-permute-start | bytes 614408 | tf_op jit(solution)/shard_map/ppermute | solution.py:297
  148.7 17.6 %collective-permute-start.42 = (bf16[8,12800]{1,0:T(8,128)(2,1)S(1)}, bf16[8,12800]{1,0:T(8,128)(2,1)S(1)}, u32[]{:S(2)}, u32[]{:S(2)}) collective-permute-start(bf16[8,12800]{1,0:T(8,128)(2,1)S(1)} %get-tuple-element.292), channel_id=1, source_target_pairs={{0,6},{1,7},{2,4},{3,5},{4,2},{5,3},{6,0},{7,1},{8,14},{9,15},{10,... | collective-permute-start | bytes 614408 | tf_op jit(solution)/shard_map/ppermute | solution.py:297
  166.9 19.5 %collective-permute-start.43 = (bf16[32,3200]{1,0:T(8,128)(2,1)S(1)}, bf16[32,3200]{1,0:T(8,128)(2,1)S(1)}, u32[]{:S(2)}, u32[]{:S(2)}) collective-permute-start(bf16[32,3200]{1,0:T(8,128)(2,1)S(1)} %multiply_convert_fusion.2.refs_0_), channel_id=1, source_target_pairs={{0,2},{1,3},{2,0},{3,1},{4,6},{5,7},{6,4},{7,5},{8,10},{9,11},{10,... | collective-permute-start | bytes 614408 | tf_op jit(solution)/shard_map/ppermute | solution.py:297
  170.9 17.2 %collective-permute-start.44 = (bf16[32,3200]{1,0:T(8,128)(2,1)S(1)}, bf16[32,3200]{1,0:T(8,128)(2,1)S(1)}, u32[]{:S(2)}, u32[]{:S(2)}) collective-permute-start(bf16[32,3200]{1,0:T(8,128)(2,1)S(1)} %multiply_convert_fusion.2.refs_0_), channel_id=1, source_target_pairs={{0,4},{1,5},{2,6},{3,7},{4,0},{5,1},{6,2},{7,3},{8,12},{9,13},{10,... | collective-permute-start | bytes 614408 | tf_op jit(solution)/shard_map/ppermute | solution.py:297
  170.9 17.1 %collective-permute-start.45 = (bf16[32,3200]{1,0:T(8,128)(2,1)S(1)}, bf16[32,3200]{1,0:T(8,128)(2,1)S(1)}, u32[]{:S(2)}, u32[]{:S(2)}) collective-permute-start(bf16[32,3200]{1,0:T(8,128)(2,1)S(1)} %multiply_convert_fusion.2.refs_0_), channel_id=1, source_target_pairs={{0,6},{1,7},{2,4},{3,5},{4,2},{5,3},{6,0},{7,1},{8,14},{9,15},{10,... | collective-permute-start | bytes 614408 | tf_op jit(solution)/shard_map/ppermute | solution.py:297
  188.2 7.4 %collective-permute-start.46 = (bf16[32,3200]{1,0:T(8,128)(2,1)S(1)}, bf16[32,3200]{1,0:T(8,128)(2,1)S(1)}, u32[]{:S(2)}, u32[]{:S(2)}) collective-permute-start(bf16[32,3200]{1,0:T(8,128)(2,1)S(1)} %multiply_convert_fusion.2.refs_0_), channel_id=1, source_target_pairs={{0,1},{1,0},{2,3},{3,2},{4,5},{5,4},{6,7},{7,6},{8,9},{9,8},{10,11... | collective-permute-start | bytes 614408 | tf_op jit(solution)/shard_map/ppermute | solution.py:303
  188.7 6.9 %collective-permute-start.47 = (bf16[32,3200]{1,0:T(8,128)(2,1)S(1)}, bf16[32,3200]{1,0:T(8,128)(2,1)S(1)}, u32[]{:S(2)}, u32[]{:S(2)}) collective-permute-start(bf16[32,3200]{1,0:T(8,128)(2,1)S(1)} %collective-permute-done.43.refs_1_), channel_id=1, source_target_pairs={{0,1},{1,0},{2,3},{3,2},{4,5},{5,4},{6,7},{7,6},{8,9},{9,8},{10,11... | collective-permute-start | bytes 614408 | tf_op jit(solution)/shard_map/ppermute | solution.py:303
  188.8 9.2 %collective-permute-start.48 = (bf16[32,3200]{1,0:T(8,128)(2,1)S(1)}, bf16[32,3200]{1,0:T(8,128)(2,1)S(1)}, u32[]{:S(2)}, u32[]{:S(2)}) collective-permute-start(bf16[32,3200]{1,0:T(8,128)(2,1)S(1)} %collective-permute-done.44.refs_2_), channel_id=1, source_target_pairs={{0,1},{1,0},{2,3},{3,2},{4,5},{5,4},{6,7},{7,6},{8,9},{9,8},{10,11... | collective-permute-start | bytes 614408 | tf_op jit(solution)/shard_map/ppermute | solution.py:303
  189.2 8.8 %collective-permute-start.49 = (bf16[32,3200]{1,0:T(8,128)(2,1)S(1)}, bf16[32,3200]{1,0:T(8,128)(2,1)S(1)}, u32[]{:S(2)}, u32[]{:S(2)}) collective-permute-start(bf16[32,3200]{1,0:T(8,128)(2,1)S(1)} %collective-permute-done.45.refs_3_), channel_id=1, source_target_pairs={{0,1},{1,0},{2,3},{3,2},{4,5},{5,4},{6,7},{7,6},{8,9},{9,8},{10,11... | collective-permute-start | bytes 614408 | tf_op jit(solution)/shard_map/ppermute | solution.py:303
  192.2 21.2 %collective-permute-start.51 = (bf16[8,12800]{1,0:T(8,128)(2,1)S(1)}, bf16[8,12800]{1,0:T(8,128)(2,1)S(1)}, u32[]{:S(2)}, u32[]{:S(2)}) collective-permute-start(bf16[8,12800]{1,0:T(8,128)(2,1)S(1)} %get-tuple-element.291), channel_id=1, source_target_pairs={{0,2},{1,3},{2,0},{3,1},{4,6},{5,7},{6,4},{7,5},{8,10},{9,11},{10,... | collective-permute-start | bytes 614408 | tf_op jit(solution)/shard_map/ppermute | solution.py:297
  195.6 17.9 %collective-permute-start.52 = (bf16[8,12800]{1,0:T(8,128)(2,1)S(1)}, bf16[8,12800]{1,0:T(8,128)(2,1)S(1)}, u32[]{:S(2)}, u32[]{:S(2)}) collective-permute-start(bf16[8,12800]{1,0:T(8,128)(2,1)S(1)} %get-tuple-element.290), channel_id=1, source_target_pairs={{0,4},{1,5},{2,6},{3,7},{4,0},{5,1},{6,2},{7,3},{8,12},{9,13},{10,... | collective-permute-start | bytes 614408 | tf_op jit(solution)/shard_map/ppermute | solution.py:297
  195.6 17.8 %collective-permute-start.53 = (bf16[8,12800]{1,0:T(8,128)(2,1)S(1)}, bf16[8,12800]{1,0:T(8,128)(2,1)S(1)}, u32[]{:S(2)}, u32[]{:S(2)}) collective-permute-start(bf16[8,12800]{1,0:T(8,128)(2,1)S(1)} %get-tuple-element.289), channel_id=1, source_target_pairs={{0,6},{1,7},{2,4},{3,5},{4,2},{5,3},{6,0},{7,1},{8,14},{9,15},{10,... | collective-permute-start | bytes 614408 | tf_op jit(solution)/shard_map/ppermute | solution.py:297
  214.2 9.9 %collective-permute-start.54 = (bf16[128,3200]{1,0:T(8,128)(2,1)}, bf16[128,3200]{1,0:T(8,128)(2,1)S(1)}, u32[]{:S(2)}, u32[]{:S(2)}) collective-permute-start(bf16[128,3200]{1,0:T(8,128)(2,1)} %get-tuple-element.216), channel_id=1, source_target_pairs={{0,1},{1,0},{2,3},{3,2},{4,5},{5,4},{6,7},{7,6},{8,9},{9,8},{10,11... | collective-permute-start | bytes 2457608 | tf_op jit(solution)/shard_map/ppermute | solution.py:310
  214.6 17.8 %collective-permute-start.55 = (bf16[32,3200]{1,0:T(8,128)(2,1)S(1)}, bf16[32,3200]{1,0:T(8,128)(2,1)S(1)}, u32[]{:S(2)}, u32[]{:S(2)}) collective-permute-start(bf16[32,3200]{1,0:T(8,128)(2,1)S(1)} %multiply_convert_fusion.refs_0_), channel_id=1, source_target_pairs={{0,2},{1,3},{2,0},{3,1},{4,6},{5,7},{6,4},{7,5},{8,10},{9,11},{10,... | collective-permute-start | bytes 614408 | tf_op jit(solution)/shard_map/ppermute | solution.py:297
  218.3 17.7 %collective-permute-start.56 = (bf16[32,3200]{1,0:T(8,128)(2,1)S(1)}, bf16[32,3200]{1,0:T(8,128)(2,1)}, u32[]{:S(2)}, u32[]{:S(2)}) collective-permute-start(bf16[32,3200]{1,0:T(8,128)(2,1)S(1)} %multiply_convert_fusion.refs_0_), channel_id=1, source_target_pairs={{0,4},{1,5},{2,6},{3,7},{4,0},{5,1},{6,2},{7,3},{8,12},{9,13},{10,... | collective-permute-start | bytes 614408 | tf_op jit(solution)/shard_map/ppermute | solution.py:297
  218.3 17.7 %collective-permute-start.57 = (bf16[32,3200]{1,0:T(8,128)(2,1)S(1)}, bf16[32,3200]{1,0:T(8,128)(2,1)}, u32[]{:S(2)}, u32[]{:S(2)}) collective-permute-start(bf16[32,3200]{1,0:T(8,128)(2,1)S(1)} %multiply_convert_fusion.refs_0_), channel_id=1, source_target_pairs={{0,6},{1,7},{2,4},{3,5},{4,2},{5,3},{6,0},{7,1},{8,14},{9,15},{10,... | collective-permute-start | bytes 614408 | tf_op jit(solution)/shard_map/ppermute | solution.py:297
  222.5 5.6 %collective-permute-start.58 = (bf16[32,1024]{1,0:T(8,128)(2,1)S(1)}, bf16[32,1024]{1,0:T(8,128)(2,1)S(1)}, u32[]{:S(2)}, u32[]{:S(2)}) collective-permute-start(bf16[32,1024]{1,0:T(8,128)(2,1)S(1)} %get-tuple-element.307), channel_id=1, source_target_pairs={{0,8},{8,16},{16,24},{24,0},{1,9},{9,17},{17,25},{25,1},{2,10},{10... | collective-permute-start | bytes 196616 | tf_op jit(solution)/shard_map/ppermute | solution.py:447
  224.9 4.7 %collective-permute-start.59 = (bf16[32,1024]{1,0:T(8,128)(2,1)S(1)}, bf16[32,1024]{1,0:T(8,128)(2,1)S(1)}, u32[]{:S(2)}, u32[]{:S(2)}) collective-permute-start(bf16[32,1024]{1,0:T(8,128)(2,1)S(1)} %get-tuple-element.306), channel_id=1, source_target_pairs={{0,16},{8,24},{16,0},{24,8},{1,17},{9,25},{17,1},{25,9},{2,18},{10... | collective-permute-start | bytes 196616 | tf_op jit(solution)/shard_map/ppermute | solution.py:447
  236.0 5.3 %collective-permute-start.61 = (bf16[32,3200]{1,0:T(8,128)(2,1)S(1)}, bf16[32,3200]{1,0:T(8,128)(2,1)S(1)}, u32[]{:S(2)}, u32[]{:S(2)}) collective-permute-start(bf16[32,3200]{1,0:T(8,128)(2,1)S(1)} %multiply_convert_fusion.refs_0_), channel_id=1, source_target_pairs={{0,1},{1,0},{2,3},{3,2},{4,5},{5,4},{6,7},{7,6},{8,9},{9,8},{10,11... | collective-permute-start | bytes 614408 | tf_op jit(solution)/shard_map/ppermute | solution.py:303
  236.1 5.6 %collective-permute-start.62 = (bf16[32,3200]{1,0:T(8,128)(2,1)S(1)}, bf16[32,3200]{1,0:T(8,128)(2,1)S(1)}, u32[]{:S(2)}, u32[]{:S(2)}) collective-permute-start(bf16[32,3200]{1,0:T(8,128)(2,1)S(1)} %collective-permute-done.55.refs_1_), channel_id=1, source_target_pairs={{0,1},{1,0},{2,3},{3,2},{4,5},{5,4},{6,7},{7,6},{8,9},{9,8},{10,11... | collective-permute-start | bytes 614408 | tf_op jit(solution)/shard_map/ppermute | solution.py:303
  236.6 7.5 %collective-permute-start.63 = (bf16[32,3200]{1,0:T(8,128)(2,1)}, bf16[32,3200]{1,0:T(8,128)(2,1)S(1)}, u32[]{:S(2)}, u32[]{:S(2)}) collective-permute-start(bf16[32,3200]{1,0:T(8,128)(2,1)} %collective-permute-done.56.refs_2_), channel_id=1, source_target_pairs={{0,1},{1,0},{2,3},{3,2},{4,5},{5,4},{6,7},{7,6},{8,9},{9,8},{10,11... | collective-permute-start | bytes 614408 | tf_op jit(solution)/shard_map/ppermute | solution.py:303
  236.6 7.5 %collective-permute-start.64 = (bf16[32,3200]{1,0:T(8,128)(2,1)}, bf16[32,3200]{1,0:T(8,128)(2,1)S(1)}, u32[]{:S(2)}, u32[]{:S(2)}) collective-permute-start(bf16[32,3200]{1,0:T(8,128)(2,1)} %collective-permute-done.57.refs_3_), channel_id=1, source_target_pairs={{0,1},{1,0},{2,3},{3,2},{4,5},{5,4},{6,7},{7,6},{8,9},{9,8},{10,11... | collective-permute-start | bytes 614408 | tf_op jit(solution)/shard_map/ppermute | solution.py:303
  237.1 22.4 %collective-permute-start.65 = (bf16[32,3200]{1,0:T(8,128)(2,1)S(1)}, bf16[32,3200]{1,0:T(8,128)(2,1)S(1)}, u32[]{:S(2)}, u32[]{:S(2)}) collective-permute-start(bf16[32,3200]{1,0:T(8,128)(2,1)S(1)} %get-tuple-element.227), channel_id=1, source_target_pairs={{0,2},{1,3},{2,0},{3,1},{4,6},{5,7},{6,4},{7,5},{8,10},{9,11},{10,... | collective-permute-start | bytes 614408 | tf_op jit(solution)/shard_map/ppermute | solution.py:297
  241.3 18.2 %collective-permute-start.66 = (bf16[32,3200]{1,0:T(8,128)(2,1)S(1)}, bf16[32,3200]{1,0:T(8,128)(2,1)S(1)}, u32[]{:S(2)}, u32[]{:S(2)}) collective-permute-start(bf16[32,3200]{1,0:T(8,128)(2,1)S(1)} %get-tuple-element.228), channel_id=1, source_target_pairs={{0,4},{1,5},{2,6},{3,7},{4,0},{5,1},{6,2},{7,3},{8,12},{9,13},{10,... | collective-permute-start | bytes 614408 | tf_op jit(solution)/shard_map/ppermute | solution.py:297
  241.7 17.8 %collective-permute-start.67 = (bf16[32,3200]{1,0:T(8,128)(2,1)S(1)}, bf16[32,3200]{1,0:T(8,128)(2,1)S(1)}, u32[]{:S(2)}, u32[]{:S(2)}) collective-permute-start(bf16[32,3200]{1,0:T(8,128)(2,1)S(1)} %get-tuple-element.229), channel_id=1, source_target_pairs={{0,6},{1,7},{2,4},{3,5},{4,2},{5,3},{6,0},{7,1},{8,14},{9,15},{10,... | collective-permute-start | bytes 614408 | tf_op jit(solution)/shard_map/ppermute | solution.py:297
  262.4 11.8 %collective-permute-start.69 = (bf16[32,3200]{1,0:T(8,128)(2,1)S(1)}, bf16[32,3200]{1,0:T(8,128)(2,1)S(1)}, u32[]{:S(2)}, u32[]{:S(2)}) collective-permute-start(bf16[32,3200]{1,0:T(8,128)(2,1)S(1)} %get-tuple-element.285), channel_id=1, source_target_pairs={{0,2},{1,3},{2,0},{3,1},{4,6},{5,7},{6,4},{7,5},{8,10},{9,11},{10,... | collective-permute-start | bytes 614408 | tf_op jit(solution)/shard_map/ppermute | solution.py:297
  265.5 17.6 %collective-permute-start.70 = (bf16[32,3200]{1,0:T(8,128)(2,1)S(1)}, bf16[32,3200]{1,0:T(8,128)(2,1)S(1)}, u32[]{:S(2)}, u32[]{:S(2)}) collective-permute-start(bf16[32,3200]{1,0:T(8,128)(2,1)S(1)} %get-tuple-element.284), channel_id=1, source_target_pairs={{0,4},{1,5},{2,6},{3,7},{4,0},{5,1},{6,2},{7,3},{8,12},{9,13},{10,... | collective-permute-start | bytes 614408 | tf_op jit(solution)/shard_map/ppermute | solution.py:297
  265.6 17.6 %collective-permute-start.71 = (bf16[32,3200]{1,0:T(8,128)(2,1)S(1)}, bf16[32,3200]{1,0:T(8,128)(2,1)S(1)}, u32[]{:S(2)}, u32[]{:S(2)}) collective-permute-start(bf16[32,3200]{1,0:T(8,128)(2,1)S(1)} %get-tuple-element.283), channel_id=1, source_target_pairs={{0,6},{1,7},{2,4},{3,5},{4,2},{5,3},{6,0},{7,1},{8,14},{9,15},{10,... | collective-permute-start | bytes 614408 | tf_op jit(solution)/shard_map/ppermute | solution.py:297
  (67 other events, 421.2 us)

commit v11 on v10

--- a/solution.py
+++ b/solution.py
@@ -178,7 +178,7 @@
     rows = normed[0].shape[0]
     for c, out in enumerate(normed):
         values = source[c * rows : (c + 1) * rows].astype(jnp.float32)
-        out[...] = layer_norm(values, gain[...], vis_eps)[0].astype(jnp.bfloat16)
+        out[...] = layer_norm(values, gain[...][None, :], vis_eps)[0].astype(jnp.bfloat16)
 
 
 def entry_norm(source, gain):
@@ -191,7 +191,7 @@
         cost_estimate=pl.CostEstimate(
             flops=8 * rows * width, bytes_accessed=4 * rows * width, transcendentals=rows
         ),
-    )(source, gain.reshape(1, width))
+    )(source, gain)
 
 
 def settings():
@@ -398,10 +398,10 @@
     patches_a = moves.gathered(rail_a)
     terms_b = moves.send(moves.combine(near_b, far_b))
     near_a, far_a, slope_a = vision_pass(patches_a, early, late)
-    near_a, far_a, terms_b, picked = tied((near_a, far_a, terms_b, picked))
+    near_a, terms_b, picked = tied((near_a, terms_b, picked))
     mixed_b, *stats_b = merge(1, moves.summed(terms_b))
     rail_b = moves.spread(mixed_b)
-    near_a, far_a, mixed_b = tied((near_a, far_a, mixed_b))
+    near_a, mixed_b = tied((near_a, mixed_b))
     cut_a, upstream = tied(
         (moves.combine(near_a, far_a), [grad_of(picked, c) for c in range(chunks)])
     )
@@ -427,14 +427,10 @@
     terms_a = moves.send(moves.combine(near_a, far_a))
     grad_out_b = moves.gathered(rail_b)
     near_b, far_b = vision_pass(grad_out_b, late, early, slope_b)
-    near_b, far_b, terms_a, projected_a, projected_b = tied(
-        (near_b, far_b, terms_a, projected_a, projected_b)
-    )
+    near_b, terms_a, projected_a, projected_b = tied((near_b, terms_a, projected_a, projected_b))
     own_a, scaled_a = unmerge(moves.summed(terms_a), *stats_a)
     rail_a = moves.spread(scaled_a)
-    near_b, far_b, scaled_a, projected_a, projected_b = tied(
-        (near_b, far_b, scaled_a, projected_a, projected_b)
-    )
+    near_b, scaled_a, projected_a, projected_b = tied((near_b, scaled_a, projected_a, projected_b))
     cut_b = moves.combine(near_b, far_b)
 
     projected = jnp.concatenate(
@@ -460,7 +456,7 @@
     terms_b = moves.send(cut_b)
     grad_out_a = moves.gathered(rail_a)
     near_a, far_a = vision_pass(grad_out_a, late, early, slope_a)
-    near_a, far_a, terms_b, arrived = tied((near_a, far_a, terms_b, arrived))
+    near_a, terms_b, arrived = tied((near_a, terms_b, arrived))
     terms_a = moves.send(moves.combine(near_a, far_a))
     normed_b = moves.summed(terms_b)
     terms_a, seq_embed, normed_b = tied((terms_a, embed(text_embed, arrived), normed_b))

time: 287 us -> 279 us (0.972)
  starting transfers between devices: 90.2 us -> 84.5 us
    ppermute x36, starting transfers between devices: 73.2 us -> 67.4 us  [shift(): return lax.ppermute(block, 'tp', pairs)]
    unnamed x118 -> x110, local copies, waits for them, and re-layouts: 7.95 us -> 8.67 us
  transfers between devices with their start and end apart: 72 -> 72, of which waited for: 17 -> 17; matrix products, arithmetic and copies ran while one was open for 6% -> 8% of each run, Pallas kernels for 38% -> 39%
where the time goes in v11:
time: 279 us; the launch traced here: 278 us
  Pallas kernels  111 us (40%)
  starting transfers between devices  84.5 us (30%)
  waiting for transfers between devices  47.5 us (17%)
  local copies, waits for them, and re-layouts  17.5 us (6%)
  other arithmetic  13.8 us (5%)
    ppermute x36, starting transfers between devices, shift(): return lax.ppermute(block, 'tp', pairs)  67.4 us
    pallas_call x4, Pallas kernels, vision_pass(): pl.pallas_call(functools.partial(vision_kernel, len(pieces), slope is Non...  58.6 us
    ppermute x36, waiting for transfers between devices, shift(): return lax.ppermute(block, 'tp', pairs)  33.8 us
    pallas_call x2, Pallas kernels, project_back(): pl.pallas_call(project_back_kernel, in_specs=whole_blocks(1) + [pl.BlockS...  26.1 us
    pallas_call x2, Pallas kernels, project(): pl.pallas_call(functools.partial(project_kernel, len(pieces)), in_specs=w...  23.6 us
    unnamed x110, local copies, waits for them, and re-layouts  8.67 us
    another operation x7, other arithmetic  7.93 us
    ppermute x24, starting transfers between devices, gathered(): other = [lax.ppermute(m, 'tp', self.pairs) for m in mine]  6.5 us
  transfers between devices with their start and end apart: 72, of which 17 were waited for; matrix products, arithmetic and copies ran while one was open for 8% of the time, Pallas kernels for 39%

profile of v11, /device:TPU:0, one launch (start us, length us, event | category | flops | bytes accessed | tf_op | source)
XLA Modules:
  0.0 277.9 jit_solution(10540880952592996386)
XLA Ops:
  0.6 2.2 shard_map.113
  2.9 3.0 %collective-permute-start = (bf16[32,3200]{1,0:T(8,128)(2,1)}, bf16[32,3200]{1,0:T(8,128)(2,1)S(1)}, u32[]{:S(2)}, u32[]{:S(2)}) collective-permute-start(bf16[32,3200]{1,0:T(8,128)(2,1)} %get-tuple-element.123.refs_0_), channel_id=1, source_target_pairs={{0,2},{1,3},{2,0},{3,1},{4,6},{5,7},{6,4},{7,5},{8,10},{9,11},{10,... | collective-permute-start | bytes 614408 | tf_op jit(solution)/shard_map/ppermute | solution.py:297
  5.9 2.6 collective-permute-start.1
  11.2 2.7 collective-permute-start.3
  14.4 1.4 collective-permute-done.3
  15.8 2.4 collective-permute-start.5
  18.3 3.2 %collective-permute-done.5 = bf16[32,1024]{1,0:T(8,128)(2,1)S(1)} collective-permute-done((bf16[32,1024]{1,0:T(8,128)(2,1)S(1)}, bf16[32,1024]{1,0:T(8,128)(2,1)S(1)}, u32[]{:S(2)}, u32[]{:S(2)}) %collective-permute-start.5) | collective-permute-done | bytes 65568 | tf_op jit(solution)/shard_map/ppermute | solution.py:374
  21.5 2.4 collective-permute-done.1.refs_2_
  25.0 3.5 %collective-permute-start.10 = (bf16[32,3200]{1,0:T(8,128)(2,1)S(1)}, bf16[32,3200]{1,0:T(8,128)(2,1)S(1)}, u32[]{:S(2)}, u32[]{:S(2)}) collective-permute-start(bf16[32,3200]{1,0:T(8,128)(2,1)S(1)} %copy-done.14), channel_id=1, source_target_pairs={{0,2},{1,3},{2,0},{3,1},{4,6},{5,7},{6,4},{7,5},{8,10},{9,11},{10,... | collective-permute-start | bytes 614408 | tf_op jit(solution)/shard_map/ppermute | solution.py:297
  28.5 1.4 collective-permute-start.11
  29.9 1.4 collective-permute-start.12
  32.0 14.7 %shard_map.114 = (bf16[128,3200]{1,0:T(8,128)(2,1)}, bf16[128,3200]{1,0:T(8,128)(2,1)}, f32[7,256,256]{2,1,0:T(8,128)}) custom-call(bf16[32,3200]{1,0:T(8,128)(2,1)} %get-tuple-element.123.refs_0_, bf16[32,3200]{1,0:T(8,128)(2,1)} %copy-done.16, bf16[32,3200]{1,0:T(8,128)(2,1)} %collective-permute-done.1.refs_2_, ...), custom_call_target="tpu_custom_call" | custom-call | flops 5242880000 | bytes 25395200 | tf_op jit(solution)/shard_map/pallas_call | solution.py:212
  49.4 1.3 fusion.51
  50.9 3.1 %collective-permute-start.18 = (bf16[32,3200]{1,0:T(8,128)(2,1)S(1)}, bf16[32,3200]{1,0:T(8,128)(2,1)S(1)}, u32[]{:S(2)}, u32[]{:S(2)}) collective-permute-start(bf16[32,3200]{1,0:T(8,128)(2,1)S(1)} %get-tuple-element.290), channel_id=1, source_target_pairs={{0,2},{1,3},{2,0},{3,1},{4,6},{5,7},{6,4},{7,5},{8,10},{9,11},{10,... | collective-permute-start | bytes 614408 | tf_op jit(solution)/shard_map/ppermute | solution.py:297
  55.1 1.5 collective-permute-start.20
  57.9 14.7 %shard_map.115 = (bf16[128,3200]{1,0:T(8,128)(2,1)}, bf16[128,3200]{1,0:T(8,128)(2,1)}, f32[7,256,256]{2,1,0:T(8,128)}) custom-call(bf16[32,3200]{1,0:T(8,128)(2,1)} %get-tuple-element.130.refs_0_, bf16[32,3200]{1,0:T(8,128)(2,1)} %copy-done.18, bf16[32,3200]{1,0:T(8,128)(2,1)} %copy-done.19, bf16[32,3200]{1,0:T(8,128)(2,1)} %copy-done.20, ...), custom_call_target="tpu_custom_call" | custom-call | flops 5242880000 | bytes 25395200 | tf_op jit(solution)/shard_map/pallas_call | solution.py:212
  74.3 2.7 collective-permute-start.21
  78.1 1.4 collective-permute-start.23
  79.5 1.6 fusion.52
  82.6 1.2 gather_fusion.2
  83.8 1.2 gather_fusion.3
  86.0 8.8 %collective-permute-done.22.refs_2_ = bf16[8,12800]{1,0:T(8,128)(2,1)} collective-permute-done((bf16[8,12800]{1,0:T(8,128)(2,1)S(1)}, bf16[8,12800]{1,0:T(8,128)(2,1)}, u32[]{:S(2)}, u32[]{:S(2)}) %collective-permute-start.22) | collective-permute-done | bytes 204832 | tf_op jit(solution)/shard_map/ppermute | solution.py:297
  94.8 1.4 collective-permute-done.25
  97.2 2.4 collective-permute-start.30
  99.6 1.4 collective-permute-start.31
  102.4 11.8 %shard_map.116 = (bf16[64,1024]{1,0:T(8,128)(2,1)}, bf16[64,1024]{1,0:T(8,128)(2,1)}) custom-call(bf16[8,12800]{1,0:T(8,128)(2,1)} %copy-done.11, bf16[8,12800]{1,0:T(8,128)(2,1)} %collective-permute-done.21.refs_1_, bf16[8,12800]{1,0:T(8,128)(2,1)} %collective-permute-done.22.refs_2_, bf16[8,12800]{1,0:T(8,128)(2,1)} %collective-permute-done.23.refs_3_, ...), custom_call_target="tpu_custom_call" | custom-call | flops 1677721600 | bytes 29753344 | tf_op jit(solution)/shard_map/pallas_call | solution.py:249
  116.1 4.1 %collective-permute-start.32 = (bf16[8,12800]{1,0:T(8,128)(2,1)S(1)}, bf16[8,12800]{1,0:T(8,128)(2,1)S(1)}, u32[]{:S(2)}, u32[]{:S(2)}) collective-permute-start(bf16[8,12800]{1,0:T(8,128)(2,1)S(1)} %multiply_convert_fusion.4.refs_0_), channel_id=1, source_target_pairs={{0,2},{1,3},{2,0},{3,1},{4,6},{5,7},{6,4},{7,5},{8,10},{9,11},{10,... | collective-permute-start | bytes 614408 | tf_op jit(solution)/shard_map/ppermute | solution.py:297
  120.9 1.7 collective-permute-start.34
  122.6 13.1 %shard_map.117 = (bf16[32,12800]{1,0:T(8,128)(2,1)}, bf16[32,12800]{1,0:T(8,128)(2,1)}) custom-call(bf16[64,1024]{1,0:T(8,128)(2,1)} %get-tuple-element.169.delta, bf16[12800,1024]{1,0:T(8,128)(2,1)} %weight.3), custom_call_target="tpu_custom_call" | custom-call | flops 1677721600 | bytes 29753344 | tf_op jit(solution)/shard_map/pallas_call | solution.py:269
  135.7 2.1 collective-permute-done.33.refs_2_
  139.0 1.7 collective-permute-done.39
  140.7 1.3 fusion.53
  142.1 3.0 %collective-permute-start.40 = (bf16[8,12800]{1,0:T(8,128)(2,1)S(1)}, bf16[8,12800]{1,0:T(8,128)(2,1)S(1)}, u32[]{:S(2)}, u32[]{:S(2)}) collective-permute-start(bf16[8,12800]{1,0:T(8,128)(2,1)S(1)} %get-tuple-element.284), channel_id=1, source_target_pairs={{0,2},{1,3},{2,0},{3,1},{4,6},{5,7},{6,4},{7,5},{8,10},{9,11},{10,... | collective-permute-start | bytes 614408 | tf_op jit(solution)/shard_map/ppermute | solution.py:297
  146.0 1.7 collective-permute-start.42
  149.0 11.8 %shard_map.118 = (bf16[64,1024]{1,0:T(8,128)(2,1)}, bf16[64,1024]{1,0:T(8,128)(2,1)}) custom-call(bf16[8,12800]{1,0:T(8,128)(2,1)} %copy-done.12, bf16[8,12800]{1,0:T(8,128)(2,1)} %copy-done.27, bf16[8,12800]{1,0:T(8,128)(2,1)} %copy-done.29, bf16[8,12800]{1,0:T(8,128)(2,1)} %copy-done.30, bf16[8,12800]{1,0:T(8,128)(2,1)} %copy-done.33, ...), custom_call_target="tpu_custom_call" | custom-call | flops 1677721600 | bytes 29753344 | tf_op jit(solution)/shard_map/pallas_call | solution.py:249
  160.8 2.0 collective-permute-done.41
  163.5 3.9 %collective-permute-start.43 = (bf16[32,3200]{1,0:T(8,128)(2,1)S(1)}, bf16[32,3200]{1,0:T(8,128)(2,1)S(1)}, u32[]{:S(2)}, u32[]{:S(2)}) collective-permute-start(bf16[32,3200]{1,0:T(8,128)(2,1)S(1)} %multiply_convert_fusion.2.refs_0_), channel_id=1, source_target_pairs={{0,2},{1,3},{2,0},{3,1},{4,6},{5,7},{6,4},{7,5},{8,10},{9,11},{10,... | collective-permute-start | bytes 614408 | tf_op jit(solution)/shard_map/ppermute | solution.py:297
  168.2 1.7 collective-permute-start.45
  169.9 13.1 %shard_map.119 = (bf16[32,12800]{1,0:T(8,128)(2,1)}, bf16[32,12800]{1,0:T(8,128)(2,1)}) custom-call(bf16[64,1024]{1,0:T(8,128)(2,1)} %get-tuple-element.186.delta, bf16[12800,1024]{1,0:T(8,128)(2,1)} %weight.3), custom_call_target="tpu_custom_call" | custom-call | flops 1677721600 | bytes 29753344 | tf_op jit(solution)/shard_map/pallas_call | solution.py:269
  183.0 2.0 collective-permute-done.44.refs_2_
  186.6 1.1 collective-permute-done.50
  187.7 1.6 fusion.54
  189.4 2.9 %collective-permute-start.51 = (bf16[8,12800]{1,0:T(8,128)(2,1)S(1)}, bf16[8,12800]{1,0:T(8,128)(2,1)S(1)}, u32[]{:S(2)}, u32[]{:S(2)}) collective-permute-start(bf16[8,12800]{1,0:T(8,128)(2,1)S(1)} %get-tuple-element.281), channel_id=1, source_target_pairs={{0,2},{1,3},{2,0},{3,1},{4,6},{5,7},{6,4},{7,5},{8,10},{9,11},{10,... | collective-permute-start | bytes 614408 | tf_op jit(solution)/shard_map/ppermute | solution.py:297
  193.1 1.7 collective-permute-start.53
  195.5 14.6 %shard_map.120 = (bf16[128,3200]{1,0:T(8,128)(2,1)}, bf16[128,3200]{1,0:T(8,128)(2,1)}) custom-call(bf16[32,3200]{1,0:T(8,128)(2,1)} %copy-done.10, bf16[32,3200]{1,0:T(8,128)(2,1)} %copy-done.21, bf16[32,3200]{1,0:T(8,128)(2,1)} %copy-done.22, bf16[32,3200]{1,0:T(8,128)(2,1)} %copy-done.23, bf16[32,3200]{1,0:T(8,128)(2,1)} %copy-done.31, ...), custom_call_target="tpu_custom_call" | custom-call | flops 5242880000 | bytes 25395200 | tf_op jit(solution)/shard_map/pallas_call | solution.py:212
  210.9 3.6 %collective-permute-start.55 = (bf16[32,3200]{1,0:T(8,128)(2,1)S(1)}, bf16[32,3200]{1,0:T(8,128)(2,1)S(1)}, u32[]{:S(2)}, u32[]{:S(2)}) collective-permute-start(bf16[32,3200]{1,0:T(8,128)(2,1)S(1)} %multiply_convert_fusion.refs_0_), channel_id=1, source_target_pairs={{0,2},{1,3},{2,0},{3,1},{4,6},{5,7},{6,4},{7,5},{8,10},{9,11},{10,... | collective-permute-start | bytes 614408 | tf_op jit(solution)/shard_map/ppermute | solution.py:297
  215.3 1.7 collective-permute-start.57
  217.6 1.5 gather_fusion.4
  219.7 1.5 collective-permute-start.58
  222.1 1.5 collective-permute-start.59
  223.6 1.6 fusion.55
  225.2 1.5 collective-permute-start.60
  226.8 2.7 collective-permute-done.60
  229.6 2.6 collective-permute-done.56.refs_2_
  233.2 2.9 %collective-permute-start.65 = (bf16[32,3200]{1,0:T(8,128)(2,1)S(1)}, bf16[32,3200]{1,0:T(8,128)(2,1)S(1)}, u32[]{:S(2)}, u32[]{:S(2)}) collective-permute-start(bf16[32,3200]{1,0:T(8,128)(2,1)S(1)} %get-tuple-element.217), channel_id=1, source_target_pairs={{0,2},{1,3},{2,0},{3,1},{4,6},{5,7},{6,4},{7,5},{8,10},{9,11},{10,... | collective-permute-start | bytes 614408 | tf_op jit(solution)/shard_map/ppermute | solution.py:297
  236.1 1.1 collective-permute-start.66
  237.2 1.7 collective-permute-start.67
  239.7 14.6 %shard_map.121 = (bf16[128,3200]{1,0:T(8,128)(2,1)}, bf16[128,3200]{1,0:T(8,128)(2,1)}) custom-call(bf16[32,3200]{1,0:T(8,128)(2,1)} %copy-done.9, bf16[32,3200]{1,0:T(8,128)(2,1)} %copy-done.17, bf16[32,3200]{1,0:T(8,128)(2,1)} %collective-permute-done.56.refs_2_, bf16[32,3200]{1,0:T(8,128)(2,1)} %collective-permute-done.57.refs_3_, ...), custom_call_target="tpu_custom_call" | custom-call | flops 5242880000 | bytes 25395200 | tf_op jit(solution)/shard_map/pallas_call | solution.py:212
  254.5 2.4 collective-permute-done.68
  258.0 1.9 collective-permute-start.70
  259.9 1.7 collective-permute-start.71
  261.6 2.2 fusion
  263.8 4.1 %collective-permute-done.69 = bf16[32,3200]{1,0:T(8,128)(2,1)S(1)} collective-permute-done((bf16[32,3200]{1,0:T(8,128)(2,1)S(1)}, bf16[32,3200]{1,0:T(8,128)(2,1)S(1)}, u32[]{:S(2)}, u32[]{:S(2)}) %collective-permute-start.69) | collective-permute-done | bytes 204832 | tf_op jit(solution)/shard_map/ppermute | solution.py:297
  267.9 7.7 %collective-permute-done.70 = bf16[32,3200]{1,0:T(8,128)(2,1)S(1)} collective-permute-done((bf16[32,3200]{1,0:T(8,128)(2,1)S(1)}, bf16[32,3200]{1,0:T(8,128)(2,1)S(1)}, u32[]{:S(2)}, u32[]{:S(2)}) %collective-permute-start.70) | collective-permute-done | bytes 204832 | tf_op jit(solution)/shard_map/ppermute | solution.py:297
  (302 shorter events, 37.1 us)
Async XLA Ops:
  2.9 18.6 %collective-permute-start = (bf16[32,3200]{1,0:T(8,128)(2,1)}, bf16[32,3200]{1,0:T(8,128)(2,1)S(1)}, u32[]{:S(2)}, u32[]{:S(2)}) collective-permute-start(bf16[32,3200]{1,0:T(8,128)(2,1)} %get-tuple-element.123.refs_0_), channel_id=1, source_target_pairs={{0,2},{1,3},{2,0},{3,1},{4,6},{5,7},{6,4},{7,5},{8,10},{9,11},{10,... | collective-permute-start | bytes 614408 | tf_op jit(solution)/shard_map/ppermute | solution.py:297
  5.9 18.0 %collective-permute-start.1 = (bf16[32,3200]{1,0:T(8,128)(2,1)}, bf16[32,3200]{1,0:T(8,128)(2,1)}, u32[]{:S(2)}, u32[]{:S(2)}) collective-permute-start(bf16[32,3200]{1,0:T(8,128)(2,1)} %get-tuple-element.123.refs_0_), channel_id=1, source_target_pairs={{0,4},{1,5},{2,6},{3,7},{4,0},{5,1},{6,2},{7,3},{8,12},{9,13},{10,... | collective-permute-start | bytes 614408 | tf_op jit(solution)/shard_map/ppermute | solution.py:297
  8.5 15.4 %collective-permute-start.2 = (bf16[32,3200]{1,0:T(8,128)(2,1)}, bf16[32,3200]{1,0:T(8,128)(2,1)}, u32[]{:S(2)}, u32[]{:S(2)}) collective-permute-start(bf16[32,3200]{1,0:T(8,128)(2,1)} %get-tuple-element.123.refs_0_), channel_id=1, source_target_pairs={{0,6},{1,7},{2,4},{3,5},{4,2},{5,3},{6,0},{7,1},{8,14},{9,15},{10,... | collective-permute-start | bytes 614408 | tf_op jit(solution)/shard_map/ppermute | solution.py:297
  11.2 4.6 %collective-permute-start.3 = (bf16[32,1024]{1,0:T(8,128)(2,1)S(1)}, bf16[32,1024]{1,0:T(8,128)(2,1)S(1)}, u32[]{:S(2)}, u32[]{:S(2)}) collective-permute-start(bf16[32,1024]{1,0:T(8,128)(2,1)S(1)} %get-tuple-element.303), channel_id=1, source_target_pairs={{0,24},{8,0},{16,8},{24,16},{1,25},{9,1},{17,9},{25,17},{2,26},{10... | collective-permute-start | bytes 196616 | tf_op jit(solution)/shard_map/ppermute | solution.py:374
  13.9 4.3 %collective-permute-start.4 = (bf16[32,1024]{1,0:T(8,128)(2,1)S(1)}, bf16[32,1024]{1,0:T(8,128)(2,1)S(1)}, u32[]{:S(2)}, u32[]{:S(2)}) collective-permute-start(bf16[32,1024]{1,0:T(8,128)(2,1)S(1)} %get-tuple-element.302), channel_id=1, source_target_pairs={{0,16},{8,24},{16,0},{24,8},{1,17},{9,25},{17,1},{25,9},{2,18},{10... | collective-permute-start | bytes 196616 | tf_op jit(solution)/shard_map/ppermute | solution.py:374
  15.8 5.6 %collective-permute-start.5 = (bf16[32,1024]{1,0:T(8,128)(2,1)S(1)}, bf16[32,1024]{1,0:T(8,128)(2,1)S(1)}, u32[]{:S(2)}, u32[]{:S(2)}) collective-permute-start(bf16[32,1024]{1,0:T(8,128)(2,1)S(1)} %get-tuple-element.301), channel_id=1, source_target_pairs={{0,8},{8,16},{16,24},{24,0},{1,9},{9,17},{17,25},{25,1},{2,10},{10... | collective-permute-start | bytes 196616 | tf_op jit(solution)/shard_map/ppermute | solution.py:374
  23.9 4.6 %collective-permute-start.6 = (bf16[32,3200]{1,0:T(8,128)(2,1)S(1)}, bf16[32,3200]{1,0:T(8,128)(2,1)S(1)}, u32[]{:S(2)}, u32[]{:S(2)}) collective-permute-start(bf16[32,3200]{1,0:T(8,128)(2,1)S(1)} %copy-done.15), channel_id=1, source_target_pairs={{0,1},{1,0},{2,3},{3,2},{4,5},{5,4},{6,7},{7,6},{8,9},{9,8},{10,11... | collective-permute-start | bytes 614408 | tf_op jit(solution)/shard_map/ppermute | solution.py:303
  24.0 5.9 %collective-permute-start.7 = (bf16[32,3200]{1,0:T(8,128)(2,1)S(1)}, bf16[32,3200]{1,0:T(8,128)(2,1)S(1)}, u32[]{:S(2)}, u32[]{:S(2)}) collective-permute-start(bf16[32,3200]{1,0:T(8,128)(2,1)S(1)} %collective-permute-done.refs_1_), channel_id=1, source_target_pairs={{0,1},{1,0},{2,3},{3,2},{4,5},{5,4},{6,7},{7,6},{8,9},{9,8},{10,11... | collective-permute-start | bytes 614408 | tf_op jit(solution)/shard_map/ppermute | solution.py:303
  24.5 6.8 %collective-permute-start.8 = (bf16[32,3200]{1,0:T(8,128)(2,1)}, bf16[32,3200]{1,0:T(8,128)(2,1)S(1)}, u32[]{:S(2)}, u32[]{:S(2)}) collective-permute-start(bf16[32,3200]{1,0:T(8,128)(2,1)} %collective-permute-done.1.refs_2_), channel_id=1, source_target_pairs={{0,1},{1,0},{2,3},{3,2},{4,5},{5,4},{6,7},{7,6},{8,9},{9,8},{10,11... | collective-permute-start | bytes 614408 | tf_op jit(solution)/shard_map/ppermute | solution.py:303
  24.5 6.7 %collective-permute-start.9 = (bf16[32,3200]{1,0:T(8,128)(2,1)}, bf16[32,3200]{1,0:T(8,128)(2,1)S(1)}, u32[]{:S(2)}, u32[]{:S(2)}) collective-permute-start(bf16[32,3200]{1,0:T(8,128)(2,1)} %collective-permute-done.2.refs_3_), channel_id=1, source_target_pairs={{0,1},{1,0},{2,3},{3,2},{4,5},{5,4},{6,7},{7,6},{8,9},{9,8},{10,11... | collective-permute-start | bytes 614408 | tf_op jit(solution)/shard_map/ppermute | solution.py:303
  25.0 21.8 %collective-permute-start.10 = (bf16[32,3200]{1,0:T(8,128)(2,1)S(1)}, bf16[32,3200]{1,0:T(8,128)(2,1)S(1)}, u32[]{:S(2)}, u32[]{:S(2)}) collective-permute-start(bf16[32,3200]{1,0:T(8,128)(2,1)S(1)} %copy-done.14), channel_id=1, source_target_pairs={{0,2},{1,3},{2,0},{3,1},{4,6},{5,7},{6,4},{7,5},{8,10},{9,11},{10,... | collective-permute-start | bytes 614408 | tf_op jit(solution)/shard_map/ppermute | solution.py:297
  28.5 18.3 %collective-permute-start.11 = (bf16[32,3200]{1,0:T(8,128)(2,1)S(1)}, bf16[32,3200]{1,0:T(8,128)(2,1)S(1)}, u32[]{:S(2)}, u32[]{:S(2)}) collective-permute-start(bf16[32,3200]{1,0:T(8,128)(2,1)S(1)} %copy-done.14), channel_id=1, source_target_pairs={{0,4},{1,5},{2,6},{3,7},{4,0},{5,1},{6,2},{7,3},{8,12},{9,13},{10,... | collective-permute-start | bytes 614408 | tf_op jit(solution)/shard_map/ppermute | solution.py:297
  29.9 16.9 %collective-permute-start.12 = (bf16[32,3200]{1,0:T(8,128)(2,1)S(1)}, bf16[32,3200]{1,0:T(8,128)(2,1)S(1)}, u32[]{:S(2)}, u32[]{:S(2)}) collective-permute-start(bf16[32,3200]{1,0:T(8,128)(2,1)S(1)} %copy-done.14), channel_id=1, source_target_pairs={{0,6},{1,7},{2,4},{3,5},{4,2},{5,3},{6,0},{7,1},{8,14},{9,15},{10,... | collective-permute-start | bytes 614408 | tf_op jit(solution)/shard_map/ppermute | solution.py:297
  47.2 6.8 %collective-permute-start.13 = (bf16[32,3200]{1,0:T(8,128)(2,1)S(1)}, bf16[32,3200]{1,0:T(8,128)(2,1)S(1)}, u32[]{:S(2)}, u32[]{:S(2)}) collective-permute-start(bf16[32,3200]{1,0:T(8,128)(2,1)S(1)} %copy-done.14), channel_id=1, source_target_pairs={{0,1},{1,0},{2,3},{3,2},{4,5},{5,4},{6,7},{7,6},{8,9},{9,8},{10,11... | collective-permute-start | bytes 614408 | tf_op jit(solution)/shard_map/ppermute | solution.py:303
  47.8 7.3 %collective-permute-start.14 = (bf16[32,3200]{1,0:T(8,128)(2,1)S(1)}, bf16[32,3200]{1,0:T(8,128)(2,1)S(1)}, u32[]{:S(2)}, u32[]{:S(2)}) collective-permute-start(bf16[32,3200]{1,0:T(8,128)(2,1)S(1)} %collective-permute-done.10.refs_1_), channel_id=1, source_target_pairs={{0,1},{1,0},{2,3},{3,2},{4,5},{5,4},{6,7},{7,6},{8,9},{9,8},{10,11... | collective-permute-start | bytes 614408 | tf_op jit(solution)/shard_map/ppermute | solution.py:303
  47.8 8.7 %collective-permute-start.15 = (bf16[32,3200]{1,0:T(8,128)(2,1)S(1)}, bf16[32,3200]{1,0:T(8,128)(2,1)S(1)}, u32[]{:S(2)}, u32[]{:S(2)}) collective-permute-start(bf16[32,3200]{1,0:T(8,128)(2,1)S(1)} %collective-permute-done.11.refs_2_), channel_id=1, source_target_pairs={{0,1},{1,0},{2,3},{3,2},{4,5},{5,4},{6,7},{7,6},{8,9},{9,8},{10,11... | collective-permute-start | bytes 614408 | tf_op jit(solution)/shard_map/ppermute | solution.py:303
  48.3 8.3 %collective-permute-start.16 = (bf16[32,3200]{1,0:T(8,128)(2,1)S(1)}, bf16[32,3200]{1,0:T(8,128)(2,1)S(1)}, u32[]{:S(2)}, u32[]{:S(2)}) collective-permute-start(bf16[32,3200]{1,0:T(8,128)(2,1)S(1)} %collective-permute-done.12.refs_3_), channel_id=1, source_target_pairs={{0,1},{1,0},{2,3},{3,2},{4,5},{5,4},{6,7},{7,6},{8,9},{9,8},{10,11... | collective-permute-start | bytes 614408 | tf_op jit(solution)/shard_map/ppermute | solution.py:303
  50.9 21.9 %collective-permute-start.18 = (bf16[32,3200]{1,0:T(8,128)(2,1)S(1)}, bf16[32,3200]{1,0:T(8,128)(2,1)S(1)}, u32[]{:S(2)}, u32[]{:S(2)}) collective-permute-start(bf16[32,3200]{1,0:T(8,128)(2,1)S(1)} %get-tuple-element.290), channel_id=1, source_target_pairs={{0,2},{1,3},{2,0},{3,1},{4,6},{5,7},{6,4},{7,5},{8,10},{9,11},{10,... | collective-permute-start | bytes 614408 | tf_op jit(solution)/shard_map/ppermute | solution.py:297
  54.0 18.8 %collective-permute-start.19 = (bf16[32,3200]{1,0:T(8,128)(2,1)S(1)}, bf16[32,3200]{1,0:T(8,128)(2,1)S(1)}, u32[]{:S(2)}, u32[]{:S(2)}) collective-permute-start(bf16[32,3200]{1,0:T(8,128)(2,1)S(1)} %get-tuple-element.289), channel_id=1, source_target_pairs={{0,4},{1,5},{2,6},{3,7},{4,0},{5,1},{6,2},{7,3},{8,12},{9,13},{10,... | collective-permute-start | bytes 614408 | tf_op jit(solution)/shard_map/ppermute | solution.py:297
  55.1 17.7 %collective-permute-start.20 = (bf16[32,3200]{1,0:T(8,128)(2,1)S(1)}, bf16[32,3200]{1,0:T(8,128)(2,1)S(1)}, u32[]{:S(2)}, u32[]{:S(2)}) collective-permute-start(bf16[32,3200]{1,0:T(8,128)(2,1)S(1)} %get-tuple-element.288), channel_id=1, source_target_pairs={{0,6},{1,7},{2,4},{3,5},{4,2},{5,3},{6,0},{7,1},{8,14},{9,15},{10,... | collective-permute-start | bytes 614408 | tf_op jit(solution)/shard_map/ppermute | solution.py:297
  72.7 6.8 %collective-permute-start.24 = (bf16[128,3200]{1,0:T(8,128)(2,1)}, bf16[128,3200]{1,0:T(8,128)(2,1)}, u32[]{:S(2)}, u32[]{:S(2)}) collective-permute-start(bf16[128,3200]{1,0:T(8,128)(2,1)} %get-tuple-element.147), channel_id=1, source_target_pairs={{0,1},{1,0},{2,3},{3,2},{4,5},{5,4},{6,7},{7,6},{8,9},{9,8},{10,11... | collective-permute-start | bytes 2457608 | tf_op jit(solution)/shard_map/ppermute | solution.py:310
  74.3 11.7 %collective-permute-start.21 = (bf16[8,12800]{1,0:T(8,128)(2,1)S(1)}, bf16[8,12800]{1,0:T(8,128)(2,1)}, u32[]{:S(2)}, u32[]{:S(2)}) collective-permute-start(bf16[8,12800]{1,0:T(8,128)(2,1)S(1)} %multiply_convert_fusion.5.refs_0_), channel_id=1, source_target_pairs={{0,2},{1,3},{2,0},{3,1},{4,6},{5,7},{6,4},{7,5},{8,10},{9,11},{10,... | collective-permute-start | bytes 614408 | tf_op jit(solution)/shard_map/ppermute | solution.py:297
  77.0 17.8 %collective-permute-start.22 = (bf16[8,12800]{1,0:T(8,128)(2,1)S(1)}, bf16[8,12800]{1,0:T(8,128)(2,1)}, u32[]{:S(2)}, u32[]{:S(2)}) collective-permute-start(bf16[8,12800]{1,0:T(8,128)(2,1)S(1)} %multiply_convert_fusion.5.refs_0_), channel_id=1, source_target_pairs={{0,4},{1,5},{2,6},{3,7},{4,0},{5,1},{6,2},{7,3},{8,12},{9,13},{10,... | collective-permute-start | bytes 614408 | tf_op jit(solution)/shard_map/ppermute | solution.py:297
  78.1 16.7 %collective-permute-start.23 = (bf16[8,12800]{1,0:T(8,128)(2,1)S(1)}, bf16[8,12800]{1,0:T(8,128)(2,1)}, u32[]{:S(2)}, u32[]{:S(2)}) collective-permute-start(bf16[8,12800]{1,0:T(8,128)(2,1)S(1)} %multiply_convert_fusion.5.refs_0_), channel_id=1, source_target_pairs={{0,6},{1,7},{2,4},{3,5},{4,2},{5,3},{6,0},{7,1},{8,14},{9,15},{10,... | collective-permute-start | bytes 614408 | tf_op jit(solution)/shard_map/ppermute | solution.py:297
  85.0 11.2 %collective-permute-start.25 = (bf16[32,3200]{1,0:T(8,128)(2,1)S(1)}, bf16[32,3200]{1,0:T(8,128)(2,1)S(1)}, u32[]{:S(2)}, u32[]{:S(2)}) collective-permute-start(bf16[32,3200]{1,0:T(8,128)(2,1)S(1)} %get-tuple-element.152), channel_id=1, source_target_pairs={{0,2},{1,3},{2,0},{3,1},{4,6},{5,7},{6,4},{7,5},{8,10},{9,11},{10,... | collective-permute-start | bytes 614408 | tf_op jit(solution)/shard_map/ppermute | solution.py:297
  96.2 4.8 %collective-permute-start.27 = (bf16[8,12800]{1,0:T(8,128)(2,1)}, bf16[8,12800]{1,0:T(8,128)(2,1)S(1)}, u32[]{:S(2)}, u32[]{:S(2)}) collective-permute-start(bf16[8,12800]{1,0:T(8,128)(2,1)} %collective-permute-done.21.refs_1_), channel_id=1, source_target_pairs={{0,1},{1,0},{2,3},{3,2},{4,5},{5,4},{6,7},{7,6},{8,9},{9,8},{10,11... | collective-permute-start | bytes 614408 | tf_op jit(solution)/shard_map/ppermute | solution.py:303
  97.2 17.6 %collective-permute-start.30 = (bf16[32,3200]{1,0:T(8,128)(2,1)S(1)}, bf16[32,3200]{1,0:T(8,128)(2,1)S(1)}, u32[]{:S(2)}, u32[]{:S(2)}) collective-permute-start(bf16[32,3200]{1,0:T(8,128)(2,1)S(1)} %get-tuple-element.162), channel_id=1, source_target_pairs={{0,4},{1,5},{2,6},{3,7},{4,0},{5,1},{6,2},{7,3},{8,12},{9,13},{10,... | collective-permute-start | bytes 614408 | tf_op jit(solution)/shard_map/ppermute | solution.py:297
  99.6 15.2 %collective-permute-start.31 = (bf16[32,3200]{1,0:T(8,128)(2,1)S(1)}, bf16[32,3200]{1,0:T(8,128)(2,1)S(1)}, u32[]{:S(2)}, u32[]{:S(2)}) collective-permute-start(bf16[32,3200]{1,0:T(8,128)(2,1)S(1)} %get-tuple-element.163), channel_id=1, source_target_pairs={{0,6},{1,7},{2,4},{3,5},{4,2},{5,3},{6,0},{7,1},{8,14},{9,15},{10,... | collective-permute-start | bytes 614408 | tf_op jit(solution)/shard_map/ppermute | solution.py:297
  116.1 19.6 %collective-permute-start.32 = (bf16[8,12800]{1,0:T(8,128)(2,1)S(1)}, bf16[8,12800]{1,0:T(8,128)(2,1)S(1)}, u32[]{:S(2)}, u32[]{:S(2)}) collective-permute-start(bf16[8,12800]{1,0:T(8,128)(2,1)S(1)} %multiply_convert_fusion.4.refs_0_), channel_id=1, source_target_pairs={{0,2},{1,3},{2,0},{3,1},{4,6},{5,7},{6,4},{7,5},{8,10},{9,11},{10,... | collective-permute-start | bytes 614408 | tf_op jit(solution)/shard_map/ppermute | solution.py:297
  120.2 17.6 %collective-permute-start.33 = (bf16[8,12800]{1,0:T(8,128)(2,1)S(1)}, bf16[8,12800]{1,0:T(8,128)(2,1)S(1)}, u32[]{:S(2)}, u32[]{:S(2)}) collective-permute-start(bf16[8,12800]{1,0:T(8,128)(2,1)S(1)} %multiply_convert_fusion.4.refs_0_), channel_id=1, source_target_pairs={{0,4},{1,5},{2,6},{3,7},{4,0},{5,1},{6,2},{7,3},{8,12},{9,13},{10,... | collective-permute-start | bytes 614408 | tf_op jit(solution)/shard_map/ppermute | solution.py:297
  120.9 16.9 %collective-permute-start.34 = (bf16[8,12800]{1,0:T(8,128)(2,1)S(1)}, bf16[8,12800]{1,0:T(8,128)(2,1)S(1)}, u32[]{:S(2)}, u32[]{:S(2)}) collective-permute-start(bf16[8,12800]{1,0:T(8,128)(2,1)S(1)} %multiply_convert_fusion.4.refs_0_), channel_id=1, source_target_pairs={{0,6},{1,7},{2,4},{3,5},{4,2},{5,3},{6,0},{7,1},{8,14},{9,15},{10,... | collective-permute-start | bytes 614408 | tf_op jit(solution)/shard_map/ppermute | solution.py:297
  137.9 7.3 %collective-permute-start.35 = (bf16[8,12800]{1,0:T(8,128)(2,1)S(1)}, bf16[8,12800]{1,0:T(8,128)(2,1)S(1)}, u32[]{:S(2)}, u32[]{:S(2)}) collective-permute-start(bf16[8,12800]{1,0:T(8,128)(2,1)S(1)} %multiply_convert_fusion.4.refs_0_), channel_id=1, source_target_pairs={{0,1},{1,0},{2,3},{3,2},{4,5},{5,4},{6,7},{7,6},{8,9},{9,8},{10,11... | collective-permute-start | bytes 614408 | tf_op jit(solution)/shard_map/ppermute | solution.py:303
  138.4 7.6 %collective-permute-start.36 = (bf16[8,12800]{1,0:T(8,128)(2,1)S(1)}, bf16[8,12800]{1,0:T(8,128)(2,1)S(1)}, u32[]{:S(2)}, u32[]{:S(2)}) collective-permute-start(bf16[8,12800]{1,0:T(8,128)(2,1)S(1)} %collective-permute-done.32.refs_1_), channel_id=1, source_target_pairs={{0,1},{1,0},{2,3},{3,2},{4,5},{5,4},{6,7},{7,6},{8,9},{9,8},{10,11... | collective-permute-start | bytes 614408 | tf_op jit(solution)/shard_map/ppermute | solution.py:303
  138.5 9.2 %collective-permute-start.37 = (bf16[8,12800]{1,0:T(8,128)(2,1)S(1)}, bf16[8,12800]{1,0:T(8,128)(2,1)S(1)}, u32[]{:S(2)}, u32[]{:S(2)}) collective-permute-start(bf16[8,12800]{1,0:T(8,128)(2,1)S(1)} %collective-permute-done.33.refs_2_), channel_id=1, source_target_pairs={{0,1},{1,0},{2,3},{3,2},{4,5},{5,4},{6,7},{7,6},{8,9},{9,8},{10,11... | collective-permute-start | bytes 614408 | tf_op jit(solution)/shard_map/ppermute | solution.py:303
  138.9 8.7 %collective-permute-start.38 = (bf16[8,12800]{1,0:T(8,128)(2,1)S(1)}, bf16[8,12800]{1,0:T(8,128)(2,1)S(1)}, u32[]{:S(2)}, u32[]{:S(2)}) collective-permute-start(bf16[8,12800]{1,0:T(8,128)(2,1)S(1)} %collective-permute-done.34.refs_3_), channel_id=1, source_target_pairs={{0,1},{1,0},{2,3},{3,2},{4,5},{5,4},{6,7},{7,6},{8,9},{9,8},{10,11... | collective-permute-start | bytes 614408 | tf_op jit(solution)/shard_map/ppermute | solution.py:303
  142.1 18.7 %collective-permute-start.40 = (bf16[8,12800]{1,0:T(8,128)(2,1)S(1)}, bf16[8,12800]{1,0:T(8,128)(2,1)S(1)}, u32[]{:S(2)}, u32[]{:S(2)}) collective-permute-start(bf16[8,12800]{1,0:T(8,128)(2,1)S(1)} %get-tuple-element.284), channel_id=1, source_target_pairs={{0,2},{1,3},{2,0},{3,1},{4,6},{5,7},{6,4},{7,5},{8,10},{9,11},{10,... | collective-permute-start | bytes 614408 | tf_op jit(solution)/shard_map/ppermute | solution.py:297
  145.2 17.6 %collective-permute-start.41 = (bf16[8,12800]{1,0:T(8,128)(2,1)S(1)}, bf16[8,12800]{1,0:T(8,128)(2,1)S(1)}, u32[]{:S(2)}, u32[]{:S(2)}) collective-permute-start(bf16[8,12800]{1,0:T(8,128)(2,1)S(1)} %get-tuple-element.283), channel_id=1, source_target_pairs={{0,4},{1,5},{2,6},{3,7},{4,0},{5,1},{6,2},{7,3},{8,12},{9,13},{10,... | collective-permute-start | bytes 614408 | tf_op jit(solution)/shard_map/ppermute | solution.py:297
  146.0 16.9 %collective-permute-start.42 = (bf16[8,12800]{1,0:T(8,128)(2,1)S(1)}, bf16[8,12800]{1,0:T(8,128)(2,1)S(1)}, u32[]{:S(2)}, u32[]{:S(2)}) collective-permute-start(bf16[8,12800]{1,0:T(8,128)(2,1)S(1)} %get-tuple-element.282), channel_id=1, source_target_pairs={{0,6},{1,7},{2,4},{3,5},{4,2},{5,3},{6,0},{7,1},{8,14},{9,15},{10,... | collective-permute-start | bytes 614408 | tf_op jit(solution)/shard_map/ppermute | solution.py:297
  163.5 19.5 %collective-permute-start.43 = (bf16[32,3200]{1,0:T(8,128)(2,1)S(1)}, bf16[32,3200]{1,0:T(8,128)(2,1)S(1)}, u32[]{:S(2)}, u32[]{:S(2)}) collective-permute-start(bf16[32,3200]{1,0:T(8,128)(2,1)S(1)} %multiply_convert_fusion.2.refs_0_), channel_id=1, source_target_pairs={{0,2},{1,3},{2,0},{3,1},{4,6},{5,7},{6,4},{7,5},{8,10},{9,11},{10,... | collective-permute-start | bytes 614408 | tf_op jit(solution)/shard_map/ppermute | solution.py:297
  167.5 17.5 %collective-permute-start.44 = (bf16[32,3200]{1,0:T(8,128)(2,1)S(1)}, bf16[32,3200]{1,0:T(8,128)(2,1)S(1)}, u32[]{:S(2)}, u32[]{:S(2)}) collective-permute-start(bf16[32,3200]{1,0:T(8,128)(2,1)S(1)} %multiply_convert_fusion.2.refs_0_), channel_id=1, source_target_pairs={{0,4},{1,5},{2,6},{3,7},{4,0},{5,1},{6,2},{7,3},{8,12},{9,13},{10,... | collective-permute-start | bytes 614408 | tf_op jit(solution)/shard_map/ppermute | solution.py:297
  168.2 16.8 %collective-permute-start.45 = (bf16[32,3200]{1,0:T(8,128)(2,1)S(1)}, bf16[32,3200]{1,0:T(8,128)(2,1)S(1)}, u32[]{:S(2)}, u32[]{:S(2)}) collective-permute-start(bf16[32,3200]{1,0:T(8,128)(2,1)S(1)} %multiply_convert_fusion.2.refs_0_), channel_id=1, source_target_pairs={{0,6},{1,7},{2,4},{3,5},{4,2},{5,3},{6,0},{7,1},{8,14},{9,15},{10,... | collective-permute-start | bytes 614408 | tf_op jit(solution)/shard_map/ppermute | solution.py:297
  185.5 6.8 %collective-permute-start.46 = (bf16[32,3200]{1,0:T(8,128)(2,1)S(1)}, bf16[32,3200]{1,0:T(8,128)(2,1)S(1)}, u32[]{:S(2)}, u32[]{:S(2)}) collective-permute-start(bf16[32,3200]{1,0:T(8,128)(2,1)S(1)} %multiply_convert_fusion.2.refs_0_), channel_id=1, source_target_pairs={{0,1},{1,0},{2,3},{3,2},{4,5},{5,4},{6,7},{7,6},{8,9},{9,8},{10,11... | collective-permute-start | bytes 614408 | tf_op jit(solution)/shard_map/ppermute | solution.py:303
  186.0 7.0 %collective-permute-start.47 = (bf16[32,3200]{1,0:T(8,128)(2,1)S(1)}, bf16[32,3200]{1,0:T(8,128)(2,1)S(1)}, u32[]{:S(2)}, u32[]{:S(2)}) collective-permute-start(bf16[32,3200]{1,0:T(8,128)(2,1)S(1)} %collective-permute-done.43.refs_1_), channel_id=1, source_target_pairs={{0,1},{1,0},{2,3},{3,2},{4,5},{5,4},{6,7},{7,6},{8,9},{9,8},{10,11... | collective-permute-start | bytes 614408 | tf_op jit(solution)/shard_map/ppermute | solution.py:303
  186.1 8.6 %collective-permute-start.48 = (bf16[32,3200]{1,0:T(8,128)(2,1)S(1)}, bf16[32,3200]{1,0:T(8,128)(2,1)S(1)}, u32[]{:S(2)}, u32[]{:S(2)}) collective-permute-start(bf16[32,3200]{1,0:T(8,128)(2,1)S(1)} %collective-permute-done.44.refs_2_), channel_id=1, source_target_pairs={{0,1},{1,0},{2,3},{3,2},{4,5},{5,4},{6,7},{7,6},{8,9},{9,8},{10,11... | collective-permute-start | bytes 614408 | tf_op jit(solution)/shard_map/ppermute | solution.py:303
  186.5 8.2 %collective-permute-start.49 = (bf16[32,3200]{1,0:T(8,128)(2,1)S(1)}, bf16[32,3200]{1,0:T(8,128)(2,1)S(1)}, u32[]{:S(2)}, u32[]{:S(2)}) collective-permute-start(bf16[32,3200]{1,0:T(8,128)(2,1)S(1)} %collective-permute-done.45.refs_3_), channel_id=1, source_target_pairs={{0,1},{1,0},{2,3},{3,2},{4,5},{5,4},{6,7},{7,6},{8,9},{9,8},{10,11... | collective-permute-start | bytes 614408 | tf_op jit(solution)/shard_map/ppermute | solution.py:303
  189.4 20.8 %collective-permute-start.51 = (bf16[8,12800]{1,0:T(8,128)(2,1)S(1)}, bf16[8,12800]{1,0:T(8,128)(2,1)S(1)}, u32[]{:S(2)}, u32[]{:S(2)}) collective-permute-start(bf16[8,12800]{1,0:T(8,128)(2,1)S(1)} %get-tuple-element.281), channel_id=1, source_target_pairs={{0,2},{1,3},{2,0},{3,1},{4,6},{5,7},{6,4},{7,5},{8,10},{9,11},{10,... | collective-permute-start | bytes 614408 | tf_op jit(solution)/shard_map/ppermute | solution.py:297
  192.3 17.9 %collective-permute-start.52 = (bf16[8,12800]{1,0:T(8,128)(2,1)S(1)}, bf16[8,12800]{1,0:T(8,128)(2,1)S(1)}, u32[]{:S(2)}, u32[]{:S(2)}) collective-permute-start(bf16[8,12800]{1,0:T(8,128)(2,1)S(1)} %get-tuple-element.280), channel_id=1, source_target_pairs={{0,4},{1,5},{2,6},{3,7},{4,0},{5,1},{6,2},{7,3},{8,12},{9,13},{10,... | collective-permute-start | bytes 614408 | tf_op jit(solution)/shard_map/ppermute | solution.py:297
  193.1 17.2 %collective-permute-start.53 = (bf16[8,12800]{1,0:T(8,128)(2,1)S(1)}, bf16[8,12800]{1,0:T(8,128)(2,1)S(1)}, u32[]{:S(2)}, u32[]{:S(2)}) collective-permute-start(bf16[8,12800]{1,0:T(8,128)(2,1)S(1)} %get-tuple-element.279), channel_id=1, source_target_pairs={{0,6},{1,7},{2,4},{3,5},{4,2},{5,3},{6,0},{7,1},{8,14},{9,15},{10,... | collective-permute-start | bytes 614408 | tf_op jit(solution)/shard_map/ppermute | solution.py:297
  210.1 11.1 %collective-permute-start.54 = (bf16[128,3200]{1,0:T(8,128)(2,1)}, bf16[128,3200]{1,0:T(8,128)(2,1)S(1)}, u32[]{:S(2)}, u32[]{:S(2)}) collective-permute-start(bf16[128,3200]{1,0:T(8,128)(2,1)} %get-tuple-element.207), channel_id=1, source_target_pairs={{0,1},{1,0},{2,3},{3,2},{4,5},{5,4},{6,7},{7,6},{8,9},{9,8},{10,11... | collective-permute-start | bytes 2457608 | tf_op jit(solution)/shard_map/ppermute | solution.py:310
  210.9 18.6 %collective-permute-start.55 = (bf16[32,3200]{1,0:T(8,128)(2,1)S(1)}, bf16[32,3200]{1,0:T(8,128)(2,1)S(1)}, u32[]{:S(2)}, u32[]{:S(2)}) collective-permute-start(bf16[32,3200]{1,0:T(8,128)(2,1)S(1)} %multiply_convert_fusion.refs_0_), channel_id=1, source_target_pairs={{0,2},{1,3},{2,0},{3,1},{4,6},{5,7},{6,4},{7,5},{8,10},{9,11},{10,... | collective-permute-start | bytes 614408 | tf_op jit(solution)/shard_map/ppermute | solution.py:297
  214.6 17.6 %collective-permute-start.56 = (bf16[32,3200]{1,0:T(8,128)(2,1)S(1)}, bf16[32,3200]{1,0:T(8,128)(2,1)}, u32[]{:S(2)}, u32[]{:S(2)}) collective-permute-start(bf16[32,3200]{1,0:T(8,128)(2,1)S(1)} %multiply_convert_fusion.refs_0_), channel_id=1, source_target_pairs={{0,4},{1,5},{2,6},{3,7},{4,0},{5,1},{6,2},{7,3},{8,12},{9,13},{10,... | collective-permute-start | bytes 614408 | tf_op jit(solution)/shard_map/ppermute | solution.py:297
  215.3 16.9 %collective-permute-start.57 = (bf16[32,3200]{1,0:T(8,128)(2,1)S(1)}, bf16[32,3200]{1,0:T(8,128)(2,1)}, u32[]{:S(2)}, u32[]{:S(2)}) collective-permute-start(bf16[32,3200]{1,0:T(8,128)(2,1)S(1)} %multiply_convert_fusion.refs_0_), channel_id=1, source_target_pairs={{0,6},{1,7},{2,4},{3,5},{4,2},{5,3},{6,0},{7,1},{8,14},{9,15},{10,... | collective-permute-start | bytes 614408 | tf_op jit(solution)/shard_map/ppermute | solution.py:297
  219.7 5.6 %collective-permute-start.58 = (bf16[32,1024]{1,0:T(8,128)(2,1)S(1)}, bf16[32,1024]{1,0:T(8,128)(2,1)S(1)}, u32[]{:S(2)}, u32[]{:S(2)}) collective-permute-start(bf16[32,1024]{1,0:T(8,128)(2,1)S(1)} %get-tuple-element.297), channel_id=1, source_target_pairs={{0,8},{8,16},{16,24},{24,0},{1,9},{9,17},{17,25},{25,1},{2,10},{10... | collective-permute-start | bytes 196616 | tf_op jit(solution)/shard_map/ppermute | solution.py:443
  222.1 4.7 %collective-permute-start.59 = (bf16[32,1024]{1,0:T(8,128)(2,1)S(1)}, bf16[32,1024]{1,0:T(8,128)(2,1)S(1)}, u32[]{:S(2)}, u32[]{:S(2)}) collective-permute-start(bf16[32,1024]{1,0:T(8,128)(2,1)S(1)} %get-tuple-element.296), channel_id=1, source_target_pairs={{0,16},{8,24},{16,0},{24,8},{1,17},{9,25},{17,1},{25,9},{2,18},{10... | collective-permute-start | bytes 196616 | tf_op jit(solution)/shard_map/ppermute | solution.py:443
  225.2 4.3 %collective-permute-start.60 = (bf16[32,1024]{1,0:T(8,128)(2,1)S(1)}, bf16[32,1024]{1,0:T(8,128)(2,1)S(1)}, u32[]{:S(2)}, u32[]{:S(2)}) collective-permute-start(bf16[32,1024]{1,0:T(8,128)(2,1)S(1)} %get-tuple-element.295), channel_id=1, source_target_pairs={{0,24},{8,0},{16,8},{24,16},{1,25},{9,1},{17,9},{25,17},{2,26},{10... | collective-permute-start | bytes 196616 | tf_op jit(solution)/shard_map/ppermute | solution.py:443
  232.2 5.0 %collective-permute-start.62 = (bf16[32,3200]{1,0:T(8,128)(2,1)S(1)}, bf16[32,3200]{1,0:T(8,128)(2,1)S(1)}, u32[]{:S(2)}, u32[]{:S(2)}) collective-permute-start(bf16[32,3200]{1,0:T(8,128)(2,1)S(1)} %collective-permute-done.55.refs_1_), channel_id=1, source_target_pairs={{0,1},{1,0},{2,3},{3,2},{4,5},{5,4},{6,7},{7,6},{8,9},{9,8},{10,11... | collective-permute-start | bytes 614408 | tf_op jit(solution)/shard_map/ppermute | solution.py:303
  232.7 6.2 %collective-permute-start.63 = (bf16[32,3200]{1,0:T(8,128)(2,1)}, bf16[32,3200]{1,0:T(8,128)(2,1)S(1)}, u32[]{:S(2)}, u32[]{:S(2)}) collective-permute-start(bf16[32,3200]{1,0:T(8,128)(2,1)} %collective-permute-done.56.refs_2_), channel_id=1, source_target_pairs={{0,1},{1,0},{2,3},{3,2},{4,5},{5,4},{6,7},{7,6},{8,9},{9,8},{10,11... | collective-permute-start | bytes 614408 | tf_op jit(solution)/shard_map/ppermute | solution.py:303
  232.8 6.1 %collective-permute-start.64 = (bf16[32,3200]{1,0:T(8,128)(2,1)}, bf16[32,3200]{1,0:T(8,128)(2,1)S(1)}, u32[]{:S(2)}, u32[]{:S(2)}) collective-permute-start(bf16[32,3200]{1,0:T(8,128)(2,1)} %collective-permute-done.57.refs_3_), channel_id=1, source_target_pairs={{0,1},{1,0},{2,3},{3,2},{4,5},{5,4},{6,7},{7,6},{8,9},{9,8},{10,11... | collective-permute-start | bytes 614408 | tf_op jit(solution)/shard_map/ppermute | solution.py:303
  233.2 21.1 %collective-permute-start.65 = (bf16[32,3200]{1,0:T(8,128)(2,1)S(1)}, bf16[32,3200]{1,0:T(8,128)(2,1)S(1)}, u32[]{:S(2)}, u32[]{:S(2)}) collective-permute-start(bf16[32,3200]{1,0:T(8,128)(2,1)S(1)} %get-tuple-element.217), channel_id=1, source_target_pairs={{0,2},{1,3},{2,0},{3,1},{4,6},{5,7},{6,4},{7,5},{8,10},{9,11},{10,... | collective-permute-start | bytes 614408 | tf_op jit(solution)/shard_map/ppermute | solution.py:297
  236.1 18.2 %collective-permute-start.66 = (bf16[32,3200]{1,0:T(8,128)(2,1)S(1)}, bf16[32,3200]{1,0:T(8,128)(2,1)S(1)}, u32[]{:S(2)}, u32[]{:S(2)}) collective-permute-start(bf16[32,3200]{1,0:T(8,128)(2,1)S(1)} %get-tuple-element.218), channel_id=1, source_target_pairs={{0,4},{1,5},{2,6},{3,7},{4,0},{5,1},{6,2},{7,3},{8,12},{9,13},{10,... | collective-permute-start | bytes 614408 | tf_op jit(solution)/shard_map/ppermute | solution.py:297
  237.2 17.2 %collective-permute-start.67 = (bf16[32,3200]{1,0:T(8,128)(2,1)S(1)}, bf16[32,3200]{1,0:T(8,128)(2,1)S(1)}, u32[]{:S(2)}, u32[]{:S(2)}) collective-permute-start(bf16[32,3200]{1,0:T(8,128)(2,1)S(1)} %get-tuple-element.219), channel_id=1, source_target_pairs={{0,6},{1,7},{2,4},{3,5},{4,2},{5,3},{6,0},{7,1},{8,14},{9,15},{10,... | collective-permute-start | bytes 614408 | tf_op jit(solution)/shard_map/ppermute | solution.py:297
  257.1 10.8 %collective-permute-start.69 = (bf16[32,3200]{1,0:T(8,128)(2,1)S(1)}, bf16[32,3200]{1,0:T(8,128)(2,1)S(1)}, u32[]{:S(2)}, u32[]{:S(2)}) collective-permute-start(bf16[32,3200]{1,0:T(8,128)(2,1)S(1)} %get-tuple-element.275), channel_id=1, source_target_pairs={{0,2},{1,3},{2,0},{3,1},{4,6},{5,7},{6,4},{7,5},{8,10},{9,11},{10,... | collective-permute-start | bytes 614408 | tf_op jit(solution)/shard_map/ppermute | solution.py:297
  258.0 17.6 %collective-permute-start.70 = (bf16[32,3200]{1,0:T(8,128)(2,1)S(1)}, bf16[32,3200]{1,0:T(8,128)(2,1)S(1)}, u32[]{:S(2)}, u32[]{:S(2)}) collective-permute-start(bf16[32,3200]{1,0:T(8,128)(2,1)S(1)} %get-tuple-element.274), channel_id=1, source_target_pairs={{0,4},{1,5},{2,6},{3,7},{4,0},{5,1},{6,2},{7,3},{8,12},{9,13},{10,... | collective-permute-start | bytes 614408 | tf_op jit(solution)/shard_map/ppermute | solution.py:297
  259.9 15.7 %collective-permute-start.71 = (bf16[32,3200]{1,0:T(8,128)(2,1)S(1)}, bf16[32,3200]{1,0:T(8,128)(2,1)S(1)}, u32[]{:S(2)}, u32[]{:S(2)}) collective-permute-start(bf16[32,3200]{1,0:T(8,128)(2,1)S(1)} %get-tuple-element.273), channel_id=1, source_target_pairs={{0,6},{1,7},{2,4},{3,5},{4,2},{5,3},{6,0},{7,1},{8,14},{9,15},{10,... | collective-permute-start | bytes 614408 | tf_op jit(solution)/shard_map/ppermute | solution.py:297
  (63 other events, 357.9 us)

commit v12 on v11

--- a/solution.py
+++ b/solution.py
@@ -194,8 +194,8 @@
     )(source, gain)
 
 
-def settings():
-    return pltpu.CompilerParams(vmem_limit_bytes=56 * 1024 * 1024)
+def settings(limit):
+    return pltpu.CompilerParams(vmem_limit_bytes=limit * 1024 * 1024)
 
 
 def whole_blocks(count):
@@ -225,7 +225,7 @@
             pltpu.SemaphoreType.DMA((blocks,)),
             pltpu.SemaphoreType.DMA((blocks,)),
         ],
-        compiler_params=settings(),
+        compiler_params=settings(56),
         cost_estimate=pl.CostEstimate(
             flops=4 * rows * width * units,
             bytes_accessed=4 * width * units + 4 * rows * (width + units),
@@ -257,7 +257,7 @@
             pltpu.VMEM((rows, units), jnp.float32),
             pltpu.SemaphoreType.DMA((depth // size,)),
         ],
-        compiler_params=settings(),
+        compiler_params=settings(40),
         cost_estimate=weight_cost(rows, depth, units),
     )(*pieces, weight, upstream)
 
@@ -275,7 +275,7 @@
             pltpu.VMEM((depth // size, size, units), jnp.bfloat16),
             pltpu.SemaphoreType.DMA((depth // size,)),
         ],
-        compiler_params=settings(),
+        compiler_params=settings(40),
         cost_estimate=weight_cost(rows, depth, units),
     )(delta, weight)
 
@@ -286,10 +286,12 @@
         self.places = self.size // cores
         rank = lax.axis_index("tp")
         place, core = rank // cores, rank % cores
-        partner = (place ^ jnp.arange(self.places)) * cores
+        self.partners = [0, *range(2, self.places), *range(1, min(2, self.places))]
+        partner = (place ^ jnp.array(self.partners)) * cores
         self.ranks = jnp.concatenate([partner + core, partner + 1 - core])
         every = jnp.arange(self.size)
-        self.blocks = (every + core) % cores * self.places + (every // cores ^ place)
+        block = jnp.array([self.partners.index(k) for k in range(self.places)])
+        self.blocks = (every + core) % cores * self.places + block[every // cores ^ place]
         self.pairs = [(a, a + 1 - 2 * (a % cores)) for a in range(self.size)]
 
     def shift(self, block, k):
@@ -297,7 +299,7 @@
         return lax.ppermute(block, "tp", pairs)
 
     def spread(self, block):
-        return [block] + [self.shift(block, k) for k in range(1, self.places)]
+        return [block] + [self.shift(block, k) for k in self.partners[1:]]
 
     def gathered(self, mine):
         other = [lax.ppermute(m, "tp", self.pairs) for m in mine]
@@ -313,7 +315,7 @@
         return cut[:1] + [c.astype(jnp.bfloat16) for c in cut[1:]]
 
     def send(self, cut):
-        return cut[:1] + [self.shift(cut[k], k) for k in range(1, self.places)]
+        return cut[:1] + [self.shift(c, k) for c, k in zip(cut[1:], self.partners[1:])]
 
     def summed(self, terms):
         return sum([t.astype(jnp.float32) for t in terms[1:]], terms[0])
@@ -406,7 +408,7 @@
         (moves.combine(near_a, far_a), [grad_of(picked, c) for c in range(chunks)])
     )
     terms_a = moves.send(cut_a)
-    rail_b, terms_a[1] = tied((rail_b, terms_a[1]))
+    rail_b, terms_a[-1] = tied((rail_b, terms_a[-1]))
     merged_b = moves.gathered(rail_b)
     projected_b, delta_b = project(merged_b, proj_weight, upstream[1])
     projected_b, delta_b, terms_a = tied((projected_b, delta_b, terms_a))
@@ -452,8 +454,9 @@
         ).astype(jnp.bfloat16)
         return jnp.where(jnp.any(picks, 1, keepdims=True), placed, text)
 
-    cut_b, rail_a, arrived = tied((cut_b, rail_a, arrived))
+    cut_b, arrived = tied((cut_b, arrived))
     terms_b = moves.send(cut_b)
+    rail_a, terms_b[-1] = tied((rail_a, terms_b[-1]))
     grad_out_a = moves.gathered(rail_a)
     near_a, far_a = vision_pass(grad_out_a, late, early, slope_a)
     near_a, terms_b, arrived = tied((near_a, terms_b, arrived))

time: 279 us -> 267 us (0.957)
  waiting for transfers between devices: 47.5 us -> 58.4 us
  Pallas kernels: 111 us -> 102 us
  starting transfers between devices: 84.5 us -> 77.1 us
  local copies, waits for them, and re-layouts: 17.5 us -> 12.4 us
    ppermute x36, waiting for transfers between devices: 33.8 us -> 44.6 us  [shift(): return lax.ppermute(block, 'tp', pairs)]
    ppermute x36, starting transfers between devices: 67.4 us -> 60.9 us  [shift(): return lax.ppermute(block, 'tp', pairs)]
    pallas_call x2, Pallas kernels: 23.6 us -> 19.4 us  [project(): pl.pallas_call(functools.partial(project_kernel, len(pieces)), in_specs=w...]
    pallas_call x2, Pallas kernels: 26.1 us -> 22 us  [project_back(): pl.pallas_call(project_back_kernel, in_specs=whole_blocks(1) + [pl.BlockS...]
    unnamed x110 -> x88, local copies, waits for them, and re-layouts: 8.67 us -> 5.18 us
  transfers between devices with their start and end apart: 72 -> 72, of which waited for: 17 -> 28; matrix products, arithmetic and copies ran while one was open for 8% -> 7% of each run, Pallas kernels for 39% -> 38%
where the time goes in v12:
time: 267 us; the launch traced here: 266 us
  Pallas kernels  102 us (38%)
  starting transfers between devices  77.1 us (29%)
  waiting for transfers between devices  58.4 us (22%)
  local copies, waits for them, and re-layouts  12.4 us (5%)
  other arithmetic  12.1 us (5%)
    ppermute x36, starting transfers between devices, shift(): return lax.ppermute(block, 'tp', pairs)  60.9 us
    pallas_call x4, Pallas kernels, vision_pass(): pl.pallas_call(functools.partial(vision_kernel, len(pieces), slope is Non...  58.6 us
    ppermute x36, waiting for transfers between devices, shift(): return lax.ppermute(block, 'tp', pairs)  44.6 us
    pallas_call x2, Pallas kernels, project_back(): pl.pallas_call(project_back_kernel, in_specs=whole_blocks(1) + [pl.BlockS...  22 us
    pallas_call x2, Pallas kernels, project(): pl.pallas_call(functools.partial(project_kernel, len(pieces)), in_specs=w...  19.4 us
    another operation x7, other arithmetic  6.28 us
    ppermute x24, starting transfers between devices, gathered(): other = [lax.ppermute(m, 'tp', self.pairs) for m in mine]  6.05 us
    ppermute x3, starting transfers between devices, per_device(): picked[s] = lax.ppermute(picked[s], 'grp', pairs)  5.42 us
  transfers between devices with their start and end apart: 72, of which 28 were waited for; matrix products, arithmetic and copies ran while one was open for 7% of the time, Pallas kernels for 38%

profile of v12, /device:TPU:0, one launch (start us, length us, event | category | flops | bytes accessed | tf_op | source)
XLA Modules:
  0.0 266.2 jit_solution(13573385459285557421)
XLA Ops:
  0.6 2.2 shard_map.131
  2.8 4.0 %collective-permute-start = (bf16[32,3200]{1,0:T(8,128)(2,1)}, bf16[32,3200]{1,0:T(8,128)(2,1)S(1)}, u32[]{:S(2)}, u32[]{:S(2)}) collective-permute-start(bf16[32,3200]{1,0:T(8,128)(2,1)} %get-tuple-element.124.refs_0_), channel_id=1, source_target_pairs={{0,4},{1,5},{2,6},{3,7},{4,0},{5,1},{6,2},{7,3},{8,12},{9,13},{10,... | collective-permute-start | bytes 614408 | tf_op jit(solution)/shard_map/ppermute | solution.py:299
  6.9 1.3 collective-permute-start.1
  8.5 0.8 reshape.424
  10.3 0.9 gather_fusion
  11.2 2.5 collective-permute-start.3
  14.2 1.4 collective-permute-done.3
  15.6 2.4 collective-permute-start.5
  18.0 3.2 %collective-permute-done.5 = bf16[32,1024]{1,0:T(8,128)(2,1)S(1)} collective-permute-done((bf16[32,1024]{1,0:T(8,128)(2,1)S(1)}, bf16[32,1024]{1,0:T(8,128)(2,1)S(1)}, u32[]{:S(2)}, u32[]{:S(2)}) %collective-permute-start.5) | collective-permute-done | bytes 65568 | tf_op jit(solution)/shard_map/ppermute | solution.py:376
  23.5 5.7 %collective-permute-start.10 = (bf16[32,3200]{1,0:T(8,128)(2,1)}, bf16[32,3200]{1,0:T(8,128)(2,1)S(1)}, u32[]{:S(2)}, u32[]{:S(2)}) collective-permute-start(bf16[32,3200]{1,0:T(8,128)(2,1)} %get-tuple-element.131.refs_0_), channel_id=1, source_target_pairs={{0,4},{1,5},{2,6},{3,7},{4,0},{5,1},{6,2},{7,3},{8,12},{9,13},{10,... | collective-permute-start | bytes 614408 | tf_op jit(solution)/shard_map/ppermute | solution.py:299
  30.9 14.7 %shard_map.132 = (bf16[128,3200]{1,0:T(8,128)(2,1)}, bf16[128,3200]{1,0:T(8,128)(2,1)}, f32[7,256,256]{2,1,0:T(8,128)}) custom-call(bf16[32,3200]{1,0:T(8,128)(2,1)} %get-tuple-element.124.refs_0_, bf16[32,3200]{1,0:T(8,128)(2,1)} %copy-done.17, bf16[32,3200]{1,0:T(8,128)(2,1)} %copy-done.18, bf16[32,3200]{1,0:T(8,128)(2,1)} %copy-done.20, ...), custom_call_target="tpu_custom_call" | custom-call | flops 5242880000 | bytes 25395200 | tf_op jit(solution)/shard_map/pallas_call | solution.py:212
  47.0 1.3 collective-permute-done.17
  48.3 1.3 fusion.52
  49.7 3.5 %collective-permute-start.18 = (bf16[32,3200]{1,0:T(8,128)(2,1)S(1)}, bf16[32,3200]{1,0:T(8,128)(2,1)S(1)}, u32[]{:S(2)}, u32[]{:S(2)}) collective-permute-start(bf16[32,3200]{1,0:T(8,128)(2,1)S(1)} %get-tuple-element.292), channel_id=1, source_target_pairs={{0,4},{1,5},{2,6},{3,7},{4,0},{5,1},{6,2},{7,3},{8,12},{9,13},{10,... | collective-permute-start | bytes 614408 | tf_op jit(solution)/shard_map/ppermute | solution.py:299
  53.2 1.7 collective-permute-start.19
  56.4 14.7 %shard_map.133 = (bf16[128,3200]{1,0:T(8,128)(2,1)}, bf16[128,3200]{1,0:T(8,128)(2,1)}, f32[7,256,256]{2,1,0:T(8,128)}) custom-call(bf16[32,3200]{1,0:T(8,128)(2,1)} %get-tuple-element.131.refs_0_, bf16[32,3200]{1,0:T(8,128)(2,1)} %copy-done.13, bf16[32,3200]{1,0:T(8,128)(2,1)} %copy-done.14, bf16[32,3200]{1,0:T(8,128)(2,1)} %copy-done.15, ...), custom_call_target="tpu_custom_call" | custom-call | flops 5242880000 | bytes 25395200 | tf_op jit(solution)/shard_map/pallas_call | solution.py:212
  72.6 2.7 %collective-permute-start.21 = (bf16[8,12800]{1,0:T(8,128)(2,1)S(1)}, bf16[8,12800]{1,0:T(8,128)(2,1)S(1)}, u32[]{:S(2)}, u32[]{:S(2)}) collective-permute-start(bf16[8,12800]{1,0:T(8,128)(2,1)S(1)} %multiply_convert_fusion.5.refs_0_), channel_id=1, source_target_pairs={{0,4},{1,5},{2,6},{3,7},{4,0},{5,1},{6,2},{7,3},{8,12},{9,13},{10,... | collective-permute-start | bytes 614408 | tf_op jit(solution)/shard_map/ppermute | solution.py:299
  75.3 1.7 collective-permute-start.22
  77.1 1.6 fusion.53
  78.8 0.7 copy-done.40
  81.3 2.1 collective-permute-start.25
  83.4 0.7 collective-permute-start.30
  84.1 6.2 %collective-permute-done.21.refs_1_ = bf16[8,12800]{1,0:T(8,128)(2,1)S(1)} collective-permute-done((bf16[8,12800]{1,0:T(8,128)(2,1)S(1)}, bf16[8,12800]{1,0:T(8,128)(2,1)S(1)}, u32[]{:S(2)}, u32[]{:S(2)}) %collective-permute-start.21) | collective-permute-done | bytes 204832 | tf_op jit(solution)/shard_map/ppermute | solution.py:299
  90.3 2.1 collective-permute-start.31
  92.4 4.8 %collective-permute-done.25 = bf16[32,3200]{1,0:T(8,128)(2,1)S(1)} collective-permute-done((bf16[32,3200]{1,0:T(8,128)(2,1)S(1)}, bf16[32,3200]{1,0:T(8,128)(2,1)S(1)}, u32[]{:S(2)}, u32[]{:S(2)}) %collective-permute-start.25) | collective-permute-done | bytes 204832 | tf_op jit(solution)/shard_map/ppermute | solution.py:299
  97.7 0.9 collective-permute-done.26.refs_4_
  99.2 0.9 collective-permute-done.29.refs_7_
  100.1 9.6 %shard_map.134 = (bf16[64,1024]{1,0:T(8,128)(2,1)S(1)}, bf16[64,1024]{1,0:T(8,128)(2,1)S(1)}) custom-call(bf16[8,12800]{1,0:T(8,128)(2,1)S(1)} %multiply_convert_fusion.5.refs_0_, bf16[8,12800]{1,0:T(8,128)(2,1)S(1)} %collective-permute-done.21.refs_1_, bf16[8,12800]{1,0:T(8,128)(2,1)S(1)} %collective-permute-done.22.refs_2_, ...), custom_call_target="tpu_custom_call" | custom-call | flops 1677721600 | bytes 29753344 | tf_op jit(solution)/shard_map/pallas_call | solution.py:249
  111.2 3.4 %collective-permute-start.32 = (bf16[8,12800]{1,0:T(8,128)(2,1)S(1)}, bf16[8,12800]{1,0:T(8,128)(2,1)S(1)}, u32[]{:S(2)}, u32[]{:S(2)}) collective-permute-start(bf16[8,12800]{1,0:T(8,128)(2,1)S(1)} %multiply_convert_fusion.4.refs_0_), channel_id=1, source_target_pairs={{0,4},{1,5},{2,6},{3,7},{4,0},{5,1},{6,2},{7,3},{8,12},{9,13},{10,... | collective-permute-start | bytes 614408 | tf_op jit(solution)/shard_map/ppermute | solution.py:299
  114.5 1.7 collective-permute-start.33
  116.3 11.0 %shard_map.135 = (bf16[32,12800]{1,0:T(8,128)(2,1)S(1)}, bf16[32,12800]{1,0:T(8,128)(2,1)S(1)}) custom-call(bf16[64,1024]{1,0:T(8,128)(2,1)S(1)} %get-tuple-element.170.delta, bf16[12800,1024]{1,0:T(8,128)(2,1)} %weight.3), custom_call_target="tpu_custom_call" | custom-call | flops 1677721600 | bytes 29753344 | tf_op jit(solution)/shard_map/pallas_call | solution.py:269
  127.3 2.0 collective-permute-done.32.refs_1_
  130.7 1.3 collective-permute-done.39
  132.2 4.1 %collective-permute-start.40 = (bf16[8,12800]{1,0:T(8,128)(2,1)S(1)}, bf16[8,12800]{1,0:T(8,128)(2,1)S(1)}, u32[]{:S(2)}, u32[]{:S(2)}) collective-permute-start(bf16[8,12800]{1,0:T(8,128)(2,1)S(1)} %get-tuple-element.286), channel_id=1, source_target_pairs={{0,4},{1,5},{2,6},{3,7},{4,0},{5,1},{6,2},{7,3},{8,12},{9,13},{10,... | collective-permute-start | bytes 614408 | tf_op jit(solution)/shard_map/ppermute | solution.py:299
  136.3 2.0 collective-permute-start.41
  138.3 9.8 %shard_map.136 = (bf16[64,1024]{1,0:T(8,128)(2,1)S(1)}, bf16[64,1024]{1,0:T(8,128)(2,1)S(1)}) custom-call(bf16[8,12800]{1,0:T(8,128)(2,1)S(1)} %multiply_convert_fusion.4.refs_0_, bf16[8,12800]{1,0:T(8,128)(2,1)S(1)} %collective-permute-done.32.refs_1_, bf16[8,12800]{1,0:T(8,128)(2,1)S(1)} %collective-permute-done.33.refs_2_, ...), custom_call_target="tpu_custom_call" | custom-call | flops 1677721600 | bytes 29753344 | tf_op jit(solution)/shard_map/pallas_call | solution.py:249
  148.2 2.8 %collective-permute-done.40 = bf16[8,12800]{1,0:T(8,128)(2,1)S(1)} collective-permute-done((bf16[8,12800]{1,0:T(8,128)(2,1)S(1)}, bf16[8,12800]{1,0:T(8,128)(2,1)S(1)}, u32[]{:S(2)}, u32[]{:S(2)}) %collective-permute-start.40) | collective-permute-done | bytes 204832 | tf_op jit(solution)/shard_map/ppermute | solution.py:299
  151.0 0.8 collective-permute-done.42
  152.5 4.2 %collective-permute-start.43 = (bf16[32,3200]{1,0:T(8,128)(2,1)S(1)}, bf16[32,3200]{1,0:T(8,128)(2,1)}, u32[]{:S(2)}, u32[]{:S(2)}) collective-permute-start(bf16[32,3200]{1,0:T(8,128)(2,1)S(1)} %multiply_convert_fusion.2.refs_0_), channel_id=1, source_target_pairs={{0,4},{1,5},{2,6},{3,7},{4,0},{5,1},{6,2},{7,3},{8,12},{9,13},{10,... | collective-permute-start | bytes 614408 | tf_op jit(solution)/shard_map/ppermute | solution.py:299
  156.7 1.8 collective-permute-start.44
  158.6 11.0 %shard_map.137 = (bf16[32,12800]{1,0:T(8,128)(2,1)S(1)}, bf16[32,12800]{1,0:T(8,128)(2,1)S(1)}) custom-call(bf16[64,1024]{1,0:T(8,128)(2,1)S(1)} %get-tuple-element.187.delta, bf16[12800,1024]{1,0:T(8,128)(2,1)} %weight.3), custom_call_target="tpu_custom_call" | custom-call | flops 1677721600 | bytes 29753344 | tf_op jit(solution)/shard_map/pallas_call | solution.py:269
  169.6 2.0 collective-permute-done.43.refs_1_
  174.3 1.3 fusion.55
  175.7 4.1 %collective-permute-start.51 = (bf16[8,12800]{1,0:T(8,128)(2,1)S(1)}, bf16[8,12800]{1,0:T(8,128)(2,1)S(1)}, u32[]{:S(2)}, u32[]{:S(2)}) collective-permute-start(bf16[8,12800]{1,0:T(8,128)(2,1)S(1)} %get-tuple-element.283), channel_id=1, source_target_pairs={{0,4},{1,5},{2,6},{3,7},{4,0},{5,1},{6,2},{7,3},{8,12},{9,13},{10,... | collective-permute-start | bytes 614408 | tf_op jit(solution)/shard_map/ppermute | solution.py:299
  179.8 2.0 collective-permute-start.52
  182.6 14.6 %shard_map.138 = (bf16[128,3200]{1,0:T(8,128)(2,1)}, bf16[128,3200]{1,0:T(8,128)(2,1)}) custom-call(bf16[32,3200]{1,0:T(8,128)(2,1)} %copy-done.11, bf16[32,3200]{1,0:T(8,128)(2,1)} %collective-permute-done.43.refs_1_, bf16[32,3200]{1,0:T(8,128)(2,1)} %collective-permute-done.44.refs_2_, bf16[32,3200]{1,0:T(8,128)(2,1)} %collective-permute-done.45.refs_3_, ...), custom_call_target="tpu_custom_call" | custom-call | flops 5242880000 | bytes 25395200 | tf_op jit(solution)/shard_map/pallas_call | solution.py:212
  198.0 2.4 collective-permute-start.54
  200.4 2.0 collective-permute-start.55
  204.2 1.5 collective-permute-start.58
  205.7 1.5 collective-permute-start.59
  207.2 1.4 collective-permute-start.60
  208.7 1.3 fusion.56
  210.5 1.0 collective-permute-done.60
  212.2 3.5 %collective-permute-done.54.refs_1_ = bf16[32,3200]{1,0:T(8,128)(2,1)S(1)} collective-permute-done((bf16[32,3200]{1,0:T(8,128)(2,1)S(1)}, bf16[32,3200]{1,0:T(8,128)(2,1)S(1)}, u32[]{:S(2)}, u32[]{:S(2)}) %collective-permute-start.54) | collective-permute-done | bytes 204832 | tf_op jit(solution)/shard_map/ppermute | solution.py:299
  215.7 4.0 %collective-permute-done.56.refs_3_ = bf16[32,3200]{1,0:T(8,128)(2,1)S(1)} collective-permute-done((bf16[32,3200]{1,0:T(8,128)(2,1)S(1)}, bf16[32,3200]{1,0:T(8,128)(2,1)S(1)}, u32[]{:S(2)}, u32[]{:S(2)}) %collective-permute-start.56) | collective-permute-done | bytes 204832 | tf_op jit(solution)/shard_map/ppermute | solution.py:299
  219.7 4.3 %collective-permute-done.61 = bf16[32,3200]{1,0:T(8,128)(2,1)S(1)} collective-permute-done((bf16[32,3200]{1,0:T(8,128)(2,1)S(1)}, bf16[32,3200]{1,0:T(8,128)(2,1)S(1)}, u32[]{:S(2)}, u32[]{:S(2)}) %collective-permute-start.61) | collective-permute-done | bytes 204832 | tf_op jit(solution)/shard_map/ppermute | solution.py:299
  225.5 1.8 collective-permute-start.67
  228.2 14.6 %shard_map.139 = (bf16[128,3200]{1,0:T(8,128)(2,1)}, bf16[128,3200]{1,0:T(8,128)(2,1)}) custom-call(bf16[32,3200]{1,0:T(8,128)(2,1)} %copy-done.10, bf16[32,3200]{1,0:T(8,128)(2,1)} %copy-done.19, bf16[32,3200]{1,0:T(8,128)(2,1)} %collective-permute-done.55.refs_2_, bf16[32,3200]{1,0:T(8,128)(2,1)} %copy-done.21, bf16[32,3200]{1,0:T(8,128)(2,1)} %copy-done.31, ...), custom_call_target="tpu_custom_call" | custom-call | flops 5242880000 | bytes 25395200 | tf_op jit(solution)/shard_map/pallas_call | solution.py:212
  243.0 2.4 collective-permute-done.68
  245.6 1.7 collective-permute-start.69
  247.3 2.0 collective-permute-start.70
  249.3 2.2 fusion
  251.5 11.8 %collective-permute-done.69 = bf16[32,3200]{1,0:T(8,128)(2,1)S(1)} collective-permute-done((bf16[32,3200]{1,0:T(8,128)(2,1)S(1)}, bf16[32,3200]{1,0:T(8,128)(2,1)S(1)}, u32[]{:S(2)}, u32[]{:S(2)}) %collective-permute-start.69) | collective-permute-done | bytes 204832 | tf_op jit(solution)/shard_map/ppermute | solution.py:299
  264.7 0.8 pad_maximum_fusion
  (283 shorter events, 28.5 us)
Async XLA Ops:
  2.8 19.0 %collective-permute-start = (bf16[32,3200]{1,0:T(8,128)(2,1)}, bf16[32,3200]{1,0:T(8,128)(2,1)S(1)}, u32[]{:S(2)}, u32[]{:S(2)}) collective-permute-start(bf16[32,3200]{1,0:T(8,128)(2,1)} %get-tuple-element.124.refs_0_), channel_id=1, source_target_pairs={{0,4},{1,5},{2,6},{3,7},{4,0},{5,1},{6,2},{7,3},{8,12},{9,13},{10,... | collective-permute-start | bytes 614408 | tf_op jit(solution)/shard_map/ppermute | solution.py:299
  6.9 15.0 %collective-permute-start.1 = (bf16[32,3200]{1,0:T(8,128)(2,1)}, bf16[32,3200]{1,0:T(8,128)(2,1)S(1)}, u32[]{:S(2)}, u32[]{:S(2)}) collective-permute-start(bf16[32,3200]{1,0:T(8,128)(2,1)} %get-tuple-element.124.refs_0_), channel_id=1, source_target_pairs={{0,6},{1,7},{2,4},{3,5},{4,2},{5,3},{6,0},{7,1},{8,14},{9,15},{10,... | collective-permute-start | bytes 614408 | tf_op jit(solution)/shard_map/ppermute | solution.py:299
  8.2 14.1 %collective-permute-start.2 = (bf16[32,3200]{1,0:T(8,128)(2,1)}, bf16[32,3200]{1,0:T(8,128)(2,1)S(1)}, u32[]{:S(2)}, u32[]{:S(2)}) collective-permute-start(bf16[32,3200]{1,0:T(8,128)(2,1)} %get-tuple-element.124.refs_0_), channel_id=1, source_target_pairs={{0,2},{1,3},{2,0},{3,1},{4,6},{5,7},{6,4},{7,5},{8,10},{9,11},{10,... | collective-permute-start | bytes 614408 | tf_op jit(solution)/shard_map/ppermute | solution.py:299
  11.2 4.4 %collective-permute-start.3 = (bf16[32,1024]{1,0:T(8,128)(2,1)S(1)}, bf16[32,1024]{1,0:T(8,128)(2,1)S(1)}, u32[]{:S(2)}, u32[]{:S(2)}) collective-permute-start(bf16[32,1024]{1,0:T(8,128)(2,1)S(1)} %get-tuple-element.307), channel_id=1, source_target_pairs={{0,24},{8,0},{16,8},{24,16},{1,25},{9,1},{17,9},{25,17},{2,26},{10... | collective-permute-start | bytes 196616 | tf_op jit(solution)/shard_map/ppermute | solution.py:376
  13.7 4.3 %collective-permute-start.4 = (bf16[32,1024]{1,0:T(8,128)(2,1)S(1)}, bf16[32,1024]{1,0:T(8,128)(2,1)S(1)}, u32[]{:S(2)}, u32[]{:S(2)}) collective-permute-start(bf16[32,1024]{1,0:T(8,128)(2,1)S(1)} %get-tuple-element.306), channel_id=1, source_target_pairs={{0,16},{8,24},{16,0},{24,8},{1,17},{9,25},{17,1},{25,9},{2,18},{10... | collective-permute-start | bytes 196616 | tf_op jit(solution)/shard_map/ppermute | solution.py:376
  15.6 5.6 %collective-permute-start.5 = (bf16[32,1024]{1,0:T(8,128)(2,1)S(1)}, bf16[32,1024]{1,0:T(8,128)(2,1)S(1)}, u32[]{:S(2)}, u32[]{:S(2)}) collective-permute-start(bf16[32,1024]{1,0:T(8,128)(2,1)S(1)} %get-tuple-element.305), channel_id=1, source_target_pairs={{0,8},{8,16},{16,24},{24,0},{1,9},{9,17},{17,25},{25,1},{2,10},{10... | collective-permute-start | bytes 196616 | tf_op jit(solution)/shard_map/ppermute | solution.py:376
  22.4 6.8 %collective-permute-start.6 = (bf16[32,3200]{1,0:T(8,128)(2,1)S(1)}, bf16[32,3200]{1,0:T(8,128)(2,1)S(1)}, u32[]{:S(2)}, u32[]{:S(2)}) collective-permute-start(bf16[32,3200]{1,0:T(8,128)(2,1)S(1)} %copy-done.16), channel_id=1, source_target_pairs={{0,1},{1,0},{2,3},{3,2},{4,5},{5,4},{6,7},{7,6},{8,9},{9,8},{10,11... | collective-permute-start | bytes 614408 | tf_op jit(solution)/shard_map/ppermute | solution.py:305
  22.4 7.2 %collective-permute-start.7 = (bf16[32,3200]{1,0:T(8,128)(2,1)S(1)}, bf16[32,3200]{1,0:T(8,128)(2,1)S(1)}, u32[]{:S(2)}, u32[]{:S(2)}) collective-permute-start(bf16[32,3200]{1,0:T(8,128)(2,1)S(1)} %collective-permute-done.refs_1_), channel_id=1, source_target_pairs={{0,1},{1,0},{2,3},{3,2},{4,5},{5,4},{6,7},{7,6},{8,9},{9,8},{10,11... | collective-permute-start | bytes 614408 | tf_op jit(solution)/shard_map/ppermute | solution.py:305
  22.9 7.2 %collective-permute-start.8 = (bf16[32,3200]{1,0:T(8,128)(2,1)S(1)}, bf16[32,3200]{1,0:T(8,128)(2,1)S(1)}, u32[]{:S(2)}, u32[]{:S(2)}) collective-permute-start(bf16[32,3200]{1,0:T(8,128)(2,1)S(1)} %collective-permute-done.1.refs_2_), channel_id=1, source_target_pairs={{0,1},{1,0},{2,3},{3,2},{4,5},{5,4},{6,7},{7,6},{8,9},{9,8},{10,11... | collective-permute-start | bytes 614408 | tf_op jit(solution)/shard_map/ppermute | solution.py:305
  23.0 7.1 %collective-permute-start.9 = (bf16[32,3200]{1,0:T(8,128)(2,1)S(1)}, bf16[32,3200]{1,0:T(8,128)(2,1)S(1)}, u32[]{:S(2)}, u32[]{:S(2)}) collective-permute-start(bf16[32,3200]{1,0:T(8,128)(2,1)S(1)} %collective-permute-done.2.refs_3_), channel_id=1, source_target_pairs={{0,1},{1,0},{2,3},{3,2},{4,5},{5,4},{6,7},{7,6},{8,9},{9,8},{10,11... | collective-permute-start | bytes 614408 | tf_op jit(solution)/shard_map/ppermute | solution.py:305
  23.5 22.2 %collective-permute-start.10 = (bf16[32,3200]{1,0:T(8,128)(2,1)}, bf16[32,3200]{1,0:T(8,128)(2,1)S(1)}, u32[]{:S(2)}, u32[]{:S(2)}) collective-permute-start(bf16[32,3200]{1,0:T(8,128)(2,1)} %get-tuple-element.131.refs_0_), channel_id=1, source_target_pairs={{0,4},{1,5},{2,6},{3,7},{4,0},{5,1},{6,2},{7,3},{8,12},{9,13},{10,... | collective-permute-start | bytes 614408 | tf_op jit(solution)/shard_map/ppermute | solution.py:299
  29.1 16.5 %collective-permute-start.11 = (bf16[32,3200]{1,0:T(8,128)(2,1)}, bf16[32,3200]{1,0:T(8,128)(2,1)S(1)}, u32[]{:S(2)}, u32[]{:S(2)}) collective-permute-start(bf16[32,3200]{1,0:T(8,128)(2,1)} %get-tuple-element.131.refs_0_), channel_id=1, source_target_pairs={{0,6},{1,7},{2,4},{3,5},{4,2},{5,3},{6,0},{7,1},{8,14},{9,15},{10,... | collective-permute-start | bytes 614408 | tf_op jit(solution)/shard_map/ppermute | solution.py:299
  29.7 16.0 %collective-permute-start.12 = (bf16[32,3200]{1,0:T(8,128)(2,1)}, bf16[32,3200]{1,0:T(8,128)(2,1)S(1)}, u32[]{:S(2)}, u32[]{:S(2)}) collective-permute-start(bf16[32,3200]{1,0:T(8,128)(2,1)} %get-tuple-element.131.refs_0_), channel_id=1, source_target_pairs={{0,2},{1,3},{2,0},{3,1},{4,6},{5,7},{6,4},{7,5},{8,10},{9,11},{10,... | collective-permute-start | bytes 614408 | tf_op jit(solution)/shard_map/ppermute | solution.py:299
  45.7 2.6 collective-permute-start.17
  45.9 7.3 %collective-permute-start.13 = (bf16[32,3200]{1,0:T(8,128)(2,1)}, bf16[32,3200]{1,0:T(8,128)(2,1)S(1)}, u32[]{:S(2)}, u32[]{:S(2)}) collective-permute-start(bf16[32,3200]{1,0:T(8,128)(2,1)} %get-tuple-element.131.refs_0_), channel_id=1, source_target_pairs={{0,1},{1,0},{2,3},{3,2},{4,5},{5,4},{6,7},{7,6},{8,9},{9,8},{10,11... | collective-permute-start | bytes 614408 | tf_op jit(solution)/shard_map/ppermute | solution.py:305
  46.4 8.5 %collective-permute-start.14 = (bf16[32,3200]{1,0:T(8,128)(2,1)S(1)}, bf16[32,3200]{1,0:T(8,128)(2,1)S(1)}, u32[]{:S(2)}, u32[]{:S(2)}) collective-permute-start(bf16[32,3200]{1,0:T(8,128)(2,1)S(1)} %collective-permute-done.10.refs_1_), channel_id=1, source_target_pairs={{0,1},{1,0},{2,3},{3,2},{4,5},{5,4},{6,7},{7,6},{8,9},{9,8},{10,11... | collective-permute-start | bytes 614408 | tf_op jit(solution)/shard_map/ppermute | solution.py:305
  46.5 8.5 %collective-permute-start.15 = (bf16[32,3200]{1,0:T(8,128)(2,1)S(1)}, bf16[32,3200]{1,0:T(8,128)(2,1)S(1)}, u32[]{:S(2)}, u32[]{:S(2)}) collective-permute-start(bf16[32,3200]{1,0:T(8,128)(2,1)S(1)} %collective-permute-done.11.refs_2_), channel_id=1, source_target_pairs={{0,1},{1,0},{2,3},{3,2},{4,5},{5,4},{6,7},{7,6},{8,9},{9,8},{10,11... | collective-permute-start | bytes 614408 | tf_op jit(solution)/shard_map/ppermute | solution.py:305
  47.0 8.1 %collective-permute-start.16 = (bf16[32,3200]{1,0:T(8,128)(2,1)S(1)}, bf16[32,3200]{1,0:T(8,128)(2,1)S(1)}, u32[]{:S(2)}, u32[]{:S(2)}) collective-permute-start(bf16[32,3200]{1,0:T(8,128)(2,1)S(1)} %collective-permute-done.12.refs_3_), channel_id=1, source_target_pairs={{0,1},{1,0},{2,3},{3,2},{4,5},{5,4},{6,7},{7,6},{8,9},{9,8},{10,11... | collective-permute-start | bytes 614408 | tf_op jit(solution)/shard_map/ppermute | solution.py:305
  49.7 21.5 %collective-permute-start.18 = (bf16[32,3200]{1,0:T(8,128)(2,1)S(1)}, bf16[32,3200]{1,0:T(8,128)(2,1)S(1)}, u32[]{:S(2)}, u32[]{:S(2)}) collective-permute-start(bf16[32,3200]{1,0:T(8,128)(2,1)S(1)} %get-tuple-element.292), channel_id=1, source_target_pairs={{0,4},{1,5},{2,6},{3,7},{4,0},{5,1},{6,2},{7,3},{8,12},{9,13},{10,... | collective-permute-start | bytes 614408 | tf_op jit(solution)/shard_map/ppermute | solution.py:299
  53.2 18.1 %collective-permute-start.19 = (bf16[32,3200]{1,0:T(8,128)(2,1)S(1)}, bf16[32,3200]{1,0:T(8,128)(2,1)S(1)}, u32[]{:S(2)}, u32[]{:S(2)}) collective-permute-start(bf16[32,3200]{1,0:T(8,128)(2,1)S(1)} %get-tuple-element.291), channel_id=1, source_target_pairs={{0,6},{1,7},{2,4},{3,5},{4,2},{5,3},{6,0},{7,1},{8,14},{9,15},{10,... | collective-permute-start | bytes 614408 | tf_op jit(solution)/shard_map/ppermute | solution.py:299
  54.9 16.3 %collective-permute-start.20 = (bf16[32,3200]{1,0:T(8,128)(2,1)S(1)}, bf16[32,3200]{1,0:T(8,128)(2,1)S(1)}, u32[]{:S(2)}, u32[]{:S(2)}) collective-permute-start(bf16[32,3200]{1,0:T(8,128)(2,1)S(1)} %get-tuple-element.290), channel_id=1, source_target_pairs={{0,2},{1,3},{2,0},{3,1},{4,6},{5,7},{6,4},{7,5},{8,10},{9,11},{10,... | collective-permute-start | bytes 614408 | tf_op jit(solution)/shard_map/ppermute | solution.py:299
  71.1 6.0 %collective-permute-start.24 = (bf16[128,3200]{1,0:T(8,128)(2,1)}, bf16[128,3200]{1,0:T(8,128)(2,1)}, u32[]{:S(2)}, u32[]{:S(2)}) collective-permute-start(bf16[128,3200]{1,0:T(8,128)(2,1)} %get-tuple-element.148), channel_id=1, source_target_pairs={{0,1},{1,0},{2,3},{3,2},{4,5},{5,4},{6,7},{7,6},{8,9},{9,8},{10,11... | collective-permute-start | bytes 2457608 | tf_op jit(solution)/shard_map/ppermute | solution.py:312
  72.6 17.7 %collective-permute-start.21 = (bf16[8,12800]{1,0:T(8,128)(2,1)S(1)}, bf16[8,12800]{1,0:T(8,128)(2,1)S(1)}, u32[]{:S(2)}, u32[]{:S(2)}) collective-permute-start(bf16[8,12800]{1,0:T(8,128)(2,1)S(1)} %multiply_convert_fusion.5.refs_0_), channel_id=1, source_target_pairs={{0,4},{1,5},{2,6},{3,7},{4,0},{5,1},{6,2},{7,3},{8,12},{9,13},{10,... | collective-permute-start | bytes 614408 | tf_op jit(solution)/shard_map/ppermute | solution.py:299
  75.3 17.1 %collective-permute-start.22 = (bf16[8,12800]{1,0:T(8,128)(2,1)S(1)}, bf16[8,12800]{1,0:T(8,128)(2,1)S(1)}, u32[]{:S(2)}, u32[]{:S(2)}) collective-permute-start(bf16[8,12800]{1,0:T(8,128)(2,1)S(1)} %multiply_convert_fusion.5.refs_0_), channel_id=1, source_target_pairs={{0,6},{1,7},{2,4},{3,5},{4,2},{5,3},{6,0},{7,1},{8,14},{9,15},{10,... | collective-permute-start | bytes 614408 | tf_op jit(solution)/shard_map/ppermute | solution.py:299
  77.1 15.3 %collective-permute-start.23 = (bf16[8,12800]{1,0:T(8,128)(2,1)S(1)}, bf16[8,12800]{1,0:T(8,128)(2,1)S(1)}, u32[]{:S(2)}, u32[]{:S(2)}) collective-permute-start(bf16[8,12800]{1,0:T(8,128)(2,1)S(1)} %multiply_convert_fusion.5.refs_0_), channel_id=1, source_target_pairs={{0,2},{1,3},{2,0},{3,1},{4,6},{5,7},{6,4},{7,5},{8,10},{9,11},{10,... | collective-permute-start | bytes 614408 | tf_op jit(solution)/shard_map/ppermute | solution.py:299
  81.3 15.9 %collective-permute-start.25 = (bf16[32,3200]{1,0:T(8,128)(2,1)S(1)}, bf16[32,3200]{1,0:T(8,128)(2,1)S(1)}, u32[]{:S(2)}, u32[]{:S(2)}) collective-permute-start(bf16[32,3200]{1,0:T(8,128)(2,1)S(1)} %get-tuple-element.153), channel_id=1, source_target_pairs={{0,2},{1,3},{2,0},{3,1},{4,6},{5,7},{6,4},{7,5},{8,10},{9,11},{10,... | collective-permute-start | bytes 614408 | tf_op jit(solution)/shard_map/ppermute | solution.py:299
  83.4 26.3 %collective-permute-start.30 = (bf16[32,3200]{1,0:T(8,128)(2,1)S(1)}, bf16[32,3200]{1,0:T(8,128)(2,1)S(1)}, u32[]{:S(2)}, u32[]{:S(2)}) collective-permute-start(bf16[32,3200]{1,0:T(8,128)(2,1)S(1)} %get-tuple-element.162), channel_id=1, source_target_pairs={{0,4},{1,5},{2,6},{3,7},{4,0},{5,1},{6,2},{7,3},{8,12},{9,13},{10,... | collective-permute-start | bytes 614408 | tf_op jit(solution)/shard_map/ppermute | solution.py:299
  90.3 19.4 %collective-permute-start.31 = (bf16[32,3200]{1,0:T(8,128)(2,1)S(1)}, bf16[32,3200]{1,0:T(8,128)(2,1)S(1)}, u32[]{:S(2)}, u32[]{:S(2)}) collective-permute-start(bf16[32,3200]{1,0:T(8,128)(2,1)S(1)} %get-tuple-element.163), channel_id=1, source_target_pairs={{0,6},{1,7},{2,4},{3,5},{4,2},{5,3},{6,0},{7,1},{8,14},{9,15},{10,... | collective-permute-start | bytes 614408 | tf_op jit(solution)/shard_map/ppermute | solution.py:299
  111.2 18.1 %collective-permute-start.32 = (bf16[8,12800]{1,0:T(8,128)(2,1)S(1)}, bf16[8,12800]{1,0:T(8,128)(2,1)S(1)}, u32[]{:S(2)}, u32[]{:S(2)}) collective-permute-start(bf16[8,12800]{1,0:T(8,128)(2,1)S(1)} %multiply_convert_fusion.4.refs_0_), channel_id=1, source_target_pairs={{0,4},{1,5},{2,6},{3,7},{4,0},{5,1},{6,2},{7,3},{8,12},{9,13},{10,... | collective-permute-start | bytes 614408 | tf_op jit(solution)/shard_map/ppermute | solution.py:299
  114.5 14.8 %collective-permute-start.33 = (bf16[8,12800]{1,0:T(8,128)(2,1)S(1)}, bf16[8,12800]{1,0:T(8,128)(2,1)S(1)}, u32[]{:S(2)}, u32[]{:S(2)}) collective-permute-start(bf16[8,12800]{1,0:T(8,128)(2,1)S(1)} %multiply_convert_fusion.4.refs_0_), channel_id=1, source_target_pairs={{0,6},{1,7},{2,4},{3,5},{4,2},{5,3},{6,0},{7,1},{8,14},{9,15},{10,... | collective-permute-start | bytes 614408 | tf_op jit(solution)/shard_map/ppermute | solution.py:299
  116.3 13.4 %collective-permute-start.34 = (bf16[8,12800]{1,0:T(8,128)(2,1)S(1)}, bf16[8,12800]{1,0:T(8,128)(2,1)S(1)}, u32[]{:S(2)}, u32[]{:S(2)}) collective-permute-start(bf16[8,12800]{1,0:T(8,128)(2,1)S(1)} %multiply_convert_fusion.4.refs_0_), channel_id=1, source_target_pairs={{0,2},{1,3},{2,0},{3,1},{4,6},{5,7},{6,4},{7,5},{8,10},{9,11},{10,... | collective-permute-start | bytes 614408 | tf_op jit(solution)/shard_map/ppermute | solution.py:299
  129.6 6.7 %collective-permute-start.35 = (bf16[8,12800]{1,0:T(8,128)(2,1)S(1)}, bf16[8,12800]{1,0:T(8,128)(2,1)S(1)}, u32[]{:S(2)}, u32[]{:S(2)}) collective-permute-start(bf16[8,12800]{1,0:T(8,128)(2,1)S(1)} %multiply_convert_fusion.4.refs_0_), channel_id=1, source_target_pairs={{0,1},{1,0},{2,3},{3,2},{4,5},{5,4},{6,7},{7,6},{8,9},{9,8},{10,11... | collective-permute-start | bytes 614408 | tf_op jit(solution)/shard_map/ppermute | solution.py:305
  130.1 8.1 %collective-permute-start.36 = (bf16[8,12800]{1,0:T(8,128)(2,1)S(1)}, bf16[8,12800]{1,0:T(8,128)(2,1)S(1)}, u32[]{:S(2)}, u32[]{:S(2)}) collective-permute-start(bf16[8,12800]{1,0:T(8,128)(2,1)S(1)} %collective-permute-done.32.refs_1_), channel_id=1, source_target_pairs={{0,1},{1,0},{2,3},{3,2},{4,5},{5,4},{6,7},{7,6},{8,9},{9,8},{10,11... | collective-permute-start | bytes 614408 | tf_op jit(solution)/shard_map/ppermute | solution.py:305
  130.1 8.1 %collective-permute-start.37 = (bf16[8,12800]{1,0:T(8,128)(2,1)S(1)}, bf16[8,12800]{1,0:T(8,128)(2,1)S(1)}, u32[]{:S(2)}, u32[]{:S(2)}) collective-permute-start(bf16[8,12800]{1,0:T(8,128)(2,1)S(1)} %collective-permute-done.33.refs_2_), channel_id=1, source_target_pairs={{0,1},{1,0},{2,3},{3,2},{4,5},{5,4},{6,7},{7,6},{8,9},{9,8},{10,11... | collective-permute-start | bytes 614408 | tf_op jit(solution)/shard_map/ppermute | solution.py:305
  130.7 7.6 %collective-permute-start.38 = (bf16[8,12800]{1,0:T(8,128)(2,1)S(1)}, bf16[8,12800]{1,0:T(8,128)(2,1)S(1)}, u32[]{:S(2)}, u32[]{:S(2)}) collective-permute-start(bf16[8,12800]{1,0:T(8,128)(2,1)S(1)} %collective-permute-done.34.refs_3_), channel_id=1, source_target_pairs={{0,1},{1,0},{2,3},{3,2},{4,5},{5,4},{6,7},{7,6},{8,9},{9,8},{10,11... | collective-permute-start | bytes 614408 | tf_op jit(solution)/shard_map/ppermute | solution.py:305
  132.2 18.8 %collective-permute-start.40 = (bf16[8,12800]{1,0:T(8,128)(2,1)S(1)}, bf16[8,12800]{1,0:T(8,128)(2,1)S(1)}, u32[]{:S(2)}, u32[]{:S(2)}) collective-permute-start(bf16[8,12800]{1,0:T(8,128)(2,1)S(1)} %get-tuple-element.286), channel_id=1, source_target_pairs={{0,4},{1,5},{2,6},{3,7},{4,0},{5,1},{6,2},{7,3},{8,12},{9,13},{10,... | collective-permute-start | bytes 614408 | tf_op jit(solution)/shard_map/ppermute | solution.py:299
  136.3 14.7 %collective-permute-start.41 = (bf16[8,12800]{1,0:T(8,128)(2,1)S(1)}, bf16[8,12800]{1,0:T(8,128)(2,1)S(1)}, u32[]{:S(2)}, u32[]{:S(2)}) collective-permute-start(bf16[8,12800]{1,0:T(8,128)(2,1)S(1)} %get-tuple-element.285), channel_id=1, source_target_pairs={{0,6},{1,7},{2,4},{3,5},{4,2},{5,3},{6,0},{7,1},{8,14},{9,15},{10,... | collective-permute-start | bytes 614408 | tf_op jit(solution)/shard_map/ppermute | solution.py:299
  138.3 13.5 %collective-permute-start.42 = (bf16[8,12800]{1,0:T(8,128)(2,1)S(1)}, bf16[8,12800]{1,0:T(8,128)(2,1)S(1)}, u32[]{:S(2)}, u32[]{:S(2)}) collective-permute-start(bf16[8,12800]{1,0:T(8,128)(2,1)S(1)} %get-tuple-element.284), channel_id=1, source_target_pairs={{0,2},{1,3},{2,0},{3,1},{4,6},{5,7},{6,4},{7,5},{8,10},{9,11},{10,... | collective-permute-start | bytes 614408 | tf_op jit(solution)/shard_map/ppermute | solution.py:299
  152.5 19.1 %collective-permute-start.43 = (bf16[32,3200]{1,0:T(8,128)(2,1)S(1)}, bf16[32,3200]{1,0:T(8,128)(2,1)}, u32[]{:S(2)}, u32[]{:S(2)}) collective-permute-start(bf16[32,3200]{1,0:T(8,128)(2,1)S(1)} %multiply_convert_fusion.2.refs_0_), channel_id=1, source_target_pairs={{0,4},{1,5},{2,6},{3,7},{4,0},{5,1},{6,2},{7,3},{8,12},{9,13},{10,... | collective-permute-start | bytes 614408 | tf_op jit(solution)/shard_map/ppermute | solution.py:299
  156.7 14.9 %collective-permute-start.44 = (bf16[32,3200]{1,0:T(8,128)(2,1)S(1)}, bf16[32,3200]{1,0:T(8,128)(2,1)}, u32[]{:S(2)}, u32[]{:S(2)}) collective-permute-start(bf16[32,3200]{1,0:T(8,128)(2,1)S(1)} %multiply_convert_fusion.2.refs_0_), channel_id=1, source_target_pairs={{0,6},{1,7},{2,4},{3,5},{4,2},{5,3},{6,0},{7,1},{8,14},{9,15},{10,... | collective-permute-start | bytes 614408 | tf_op jit(solution)/shard_map/ppermute | solution.py:299
  158.6 13.3 %collective-permute-start.45 = (bf16[32,3200]{1,0:T(8,128)(2,1)S(1)}, bf16[32,3200]{1,0:T(8,128)(2,1)}, u32[]{:S(2)}, u32[]{:S(2)}) collective-permute-start(bf16[32,3200]{1,0:T(8,128)(2,1)S(1)} %multiply_convert_fusion.2.refs_0_), channel_id=1, source_target_pairs={{0,2},{1,3},{2,0},{3,1},{4,6},{5,7},{6,4},{7,5},{8,10},{9,11},{10,... | collective-permute-start | bytes 614408 | tf_op jit(solution)/shard_map/ppermute | solution.py:299
  172.9 6.9 %collective-permute-start.46 = (bf16[32,3200]{1,0:T(8,128)(2,1)S(1)}, bf16[32,3200]{1,0:T(8,128)(2,1)S(1)}, u32[]{:S(2)}, u32[]{:S(2)}) collective-permute-start(bf16[32,3200]{1,0:T(8,128)(2,1)S(1)} %multiply_convert_fusion.2.refs_0_), channel_id=1, source_target_pairs={{0,1},{1,0},{2,3},{3,2},{4,5},{5,4},{6,7},{7,6},{8,9},{9,8},{10,11... | collective-permute-start | bytes 614408 | tf_op jit(solution)/shard_map/ppermute | solution.py:305
  173.5 8.3 %collective-permute-start.47 = (bf16[32,3200]{1,0:T(8,128)(2,1)}, bf16[32,3200]{1,0:T(8,128)(2,1)S(1)}, u32[]{:S(2)}, u32[]{:S(2)}) collective-permute-start(bf16[32,3200]{1,0:T(8,128)(2,1)} %collective-permute-done.43.refs_1_), channel_id=1, source_target_pairs={{0,1},{1,0},{2,3},{3,2},{4,5},{5,4},{6,7},{7,6},{8,9},{9,8},{10,11... | collective-permute-start | bytes 614408 | tf_op jit(solution)/shard_map/ppermute | solution.py:305
  173.6 8.2 %collective-permute-start.48 = (bf16[32,3200]{1,0:T(8,128)(2,1)}, bf16[32,3200]{1,0:T(8,128)(2,1)S(1)}, u32[]{:S(2)}, u32[]{:S(2)}) collective-permute-start(bf16[32,3200]{1,0:T(8,128)(2,1)} %collective-permute-done.44.refs_2_), channel_id=1, source_target_pairs={{0,1},{1,0},{2,3},{3,2},{4,5},{5,4},{6,7},{7,6},{8,9},{9,8},{10,11... | collective-permute-start | bytes 614408 | tf_op jit(solution)/shard_map/ppermute | solution.py:305
  174.0 7.8 %collective-permute-start.49 = (bf16[32,3200]{1,0:T(8,128)(2,1)}, bf16[32,3200]{1,0:T(8,128)(2,1)S(1)}, u32[]{:S(2)}, u32[]{:S(2)}) collective-permute-start(bf16[32,3200]{1,0:T(8,128)(2,1)} %collective-permute-done.45.refs_3_), channel_id=1, source_target_pairs={{0,1},{1,0},{2,3},{3,2},{4,5},{5,4},{6,7},{7,6},{8,9},{9,8},{10,11... | collective-permute-start | bytes 614408 | tf_op jit(solution)/shard_map/ppermute | solution.py:305
  175.7 21.6 %collective-permute-start.51 = (bf16[8,12800]{1,0:T(8,128)(2,1)S(1)}, bf16[8,12800]{1,0:T(8,128)(2,1)S(1)}, u32[]{:S(2)}, u32[]{:S(2)}) collective-permute-start(bf16[8,12800]{1,0:T(8,128)(2,1)S(1)} %get-tuple-element.283), channel_id=1, source_target_pairs={{0,4},{1,5},{2,6},{3,7},{4,0},{5,1},{6,2},{7,3},{8,12},{9,13},{10,... | collective-permute-start | bytes 614408 | tf_op jit(solution)/shard_map/ppermute | solution.py:299
  179.8 17.5 %collective-permute-start.52 = (bf16[8,12800]{1,0:T(8,128)(2,1)S(1)}, bf16[8,12800]{1,0:T(8,128)(2,1)S(1)}, u32[]{:S(2)}, u32[]{:S(2)}) collective-permute-start(bf16[8,12800]{1,0:T(8,128)(2,1)S(1)} %get-tuple-element.282), channel_id=1, source_target_pairs={{0,6},{1,7},{2,4},{3,5},{4,2},{5,3},{6,0},{7,1},{8,14},{9,15},{10,... | collective-permute-start | bytes 614408 | tf_op jit(solution)/shard_map/ppermute | solution.py:299
  181.8 15.6 %collective-permute-start.53 = (bf16[8,12800]{1,0:T(8,128)(2,1)S(1)}, bf16[8,12800]{1,0:T(8,128)(2,1)S(1)}, u32[]{:S(2)}, u32[]{:S(2)}) collective-permute-start(bf16[8,12800]{1,0:T(8,128)(2,1)S(1)} %get-tuple-element.281), channel_id=1, source_target_pairs={{0,2},{1,3},{2,0},{3,1},{4,6},{5,7},{6,4},{7,5},{8,10},{9,11},{10,... | collective-permute-start | bytes 614408 | tf_op jit(solution)/shard_map/ppermute | solution.py:299
  197.2 10.0 %collective-permute-start.57 = (bf16[128,3200]{1,0:T(8,128)(2,1)}, bf16[128,3200]{1,0:T(8,128)(2,1)}, u32[]{:S(2)}, u32[]{:S(2)}) collective-permute-start(bf16[128,3200]{1,0:T(8,128)(2,1)} %get-tuple-element.208), channel_id=1, source_target_pairs={{0,1},{1,0},{2,3},{3,2},{4,5},{5,4},{6,7},{7,6},{8,9},{9,8},{10,11... | collective-permute-start | bytes 2457608 | tf_op jit(solution)/shard_map/ppermute | solution.py:312
  198.0 17.7 %collective-permute-start.54 = (bf16[32,3200]{1,0:T(8,128)(2,1)S(1)}, bf16[32,3200]{1,0:T(8,128)(2,1)S(1)}, u32[]{:S(2)}, u32[]{:S(2)}) collective-permute-start(bf16[32,3200]{1,0:T(8,128)(2,1)S(1)} %multiply_convert_fusion.refs_0_), channel_id=1, source_target_pairs={{0,4},{1,5},{2,6},{3,7},{4,0},{5,1},{6,2},{7,3},{8,12},{9,13},{10,... | collective-permute-start | bytes 614408 | tf_op jit(solution)/shard_map/ppermute | solution.py:299
  200.4 15.3 %collective-permute-start.55 = (bf16[32,3200]{1,0:T(8,128)(2,1)S(1)}, bf16[32,3200]{1,0:T(8,128)(2,1)}, u32[]{:S(2)}, u32[]{:S(2)}) collective-permute-start(bf16[32,3200]{1,0:T(8,128)(2,1)S(1)} %multiply_convert_fusion.refs_0_), channel_id=1, source_target_pairs={{0,6},{1,7},{2,4},{3,5},{4,2},{5,3},{6,0},{7,1},{8,14},{9,15},{10,... | collective-permute-start | bytes 614408 | tf_op jit(solution)/shard_map/ppermute | solution.py:299
  204.2 5.9 %collective-permute-start.58 = (bf16[32,1024]{1,0:T(8,128)(2,1)S(1)}, bf16[32,1024]{1,0:T(8,128)(2,1)S(1)}, u32[]{:S(2)}, u32[]{:S(2)}) collective-permute-start(bf16[32,1024]{1,0:T(8,128)(2,1)S(1)} %get-tuple-element.301), channel_id=1, source_target_pairs={{0,8},{8,16},{16,24},{24,0},{1,9},{9,17},{17,25},{25,1},{2,10},{10... | collective-permute-start | bytes 196616 | tf_op jit(solution)/shard_map/ppermute | solution.py:445
  205.7 4.7 %collective-permute-start.59 = (bf16[32,1024]{1,0:T(8,128)(2,1)S(1)}, bf16[32,1024]{1,0:T(8,128)(2,1)S(1)}, u32[]{:S(2)}, u32[]{:S(2)}) collective-permute-start(bf16[32,1024]{1,0:T(8,128)(2,1)S(1)} %get-tuple-element.300), channel_id=1, source_target_pairs={{0,16},{8,24},{16,0},{24,8},{1,17},{9,25},{17,1},{25,9},{2,18},{10... | collective-permute-start | bytes 196616 | tf_op jit(solution)/shard_map/ppermute | solution.py:445
  207.2 4.3 %collective-permute-start.60 = (bf16[32,1024]{1,0:T(8,128)(2,1)S(1)}, bf16[32,1024]{1,0:T(8,128)(2,1)S(1)}, u32[]{:S(2)}, u32[]{:S(2)}) collective-permute-start(bf16[32,1024]{1,0:T(8,128)(2,1)S(1)} %get-tuple-element.299), channel_id=1, source_target_pairs={{0,24},{8,0},{16,8},{24,16},{1,25},{9,1},{17,9},{25,17},{2,26},{10... | collective-permute-start | bytes 196616 | tf_op jit(solution)/shard_map/ppermute | solution.py:445
  210.1 9.6 %collective-permute-start.56 = (bf16[32,3200]{1,0:T(8,128)(2,1)S(1)}, bf16[32,3200]{1,0:T(8,128)(2,1)S(1)}, u32[]{:S(2)}, u32[]{:S(2)}) collective-permute-start(bf16[32,3200]{1,0:T(8,128)(2,1)S(1)} %multiply_convert_fusion.refs_0_), channel_id=1, source_target_pairs={{0,2},{1,3},{2,0},{3,1},{4,6},{5,7},{6,4},{7,5},{8,10},{9,11},{10,... | collective-permute-start | bytes 614408 | tf_op jit(solution)/shard_map/ppermute | solution.py:299
  211.5 12.5 %collective-permute-start.61 = (bf16[32,3200]{1,0:T(8,128)(2,1)S(1)}, bf16[32,3200]{1,0:T(8,128)(2,1)S(1)}, u32[]{:S(2)}, u32[]{:S(2)}) collective-permute-start(bf16[32,3200]{1,0:T(8,128)(2,1)S(1)} %get-tuple-element.211), channel_id=1, source_target_pairs={{0,2},{1,3},{2,0},{3,1},{4,6},{5,7},{6,4},{7,5},{8,10},{9,11},{10,... | collective-permute-start | bytes 614408 | tf_op jit(solution)/shard_map/ppermute | solution.py:299
  224.0 3.3 %collective-permute-start.63 = (bf16[32,3200]{1,0:T(8,128)(2,1)S(1)}, bf16[32,3200]{1,0:T(8,128)(2,1)S(1)}, u32[]{:S(2)}, u32[]{:S(2)}) collective-permute-start(bf16[32,3200]{1,0:T(8,128)(2,1)S(1)} %collective-permute-done.54.refs_1_), channel_id=1, source_target_pairs={{0,1},{1,0},{2,3},{3,2},{4,5},{5,4},{6,7},{7,6},{8,9},{9,8},{10,11... | collective-permute-start | bytes 614408 | tf_op jit(solution)/shard_map/ppermute | solution.py:305
  224.5 2.8 %collective-permute-start.64 = (bf16[32,3200]{1,0:T(8,128)(2,1)}, bf16[32,3200]{1,0:T(8,128)(2,1)S(1)}, u32[]{:S(2)}, u32[]{:S(2)}) collective-permute-start(bf16[32,3200]{1,0:T(8,128)(2,1)} %collective-permute-done.55.refs_2_), channel_id=1, source_target_pairs={{0,1},{1,0},{2,3},{3,2},{4,5},{5,4},{6,7},{7,6},{8,9},{9,8},{10,11... | collective-permute-start | bytes 614408 | tf_op jit(solution)/shard_map/ppermute | solution.py:305
  224.6 2.8 %collective-permute-start.65 = (bf16[32,3200]{1,0:T(8,128)(2,1)S(1)}, bf16[32,3200]{1,0:T(8,128)(2,1)S(1)}, u32[]{:S(2)}, u32[]{:S(2)}) collective-permute-start(bf16[32,3200]{1,0:T(8,128)(2,1)S(1)} %collective-permute-done.56.refs_3_), channel_id=1, source_target_pairs={{0,1},{1,0},{2,3},{3,2},{4,5},{5,4},{6,7},{7,6},{8,9},{9,8},{10,11... | collective-permute-start | bytes 614408 | tf_op jit(solution)/shard_map/ppermute | solution.py:305
  225.1 17.8 %collective-permute-start.66 = (bf16[32,3200]{1,0:T(8,128)(2,1)S(1)}, bf16[32,3200]{1,0:T(8,128)(2,1)S(1)}, u32[]{:S(2)}, u32[]{:S(2)}) collective-permute-start(bf16[32,3200]{1,0:T(8,128)(2,1)S(1)} %get-tuple-element.219), channel_id=1, source_target_pairs={{0,4},{1,5},{2,6},{3,7},{4,0},{5,1},{6,2},{7,3},{8,12},{9,13},{10,... | collective-permute-start | bytes 614408 | tf_op jit(solution)/shard_map/ppermute | solution.py:299
  225.5 17.4 %collective-permute-start.67 = (bf16[32,3200]{1,0:T(8,128)(2,1)S(1)}, bf16[32,3200]{1,0:T(8,128)(2,1)S(1)}, u32[]{:S(2)}, u32[]{:S(2)}) collective-permute-start(bf16[32,3200]{1,0:T(8,128)(2,1)S(1)} %get-tuple-element.220), channel_id=1, source_target_pairs={{0,6},{1,7},{2,4},{3,5},{4,2},{5,3},{6,0},{7,1},{8,14},{9,15},{10,... | collective-permute-start | bytes 614408 | tf_op jit(solution)/shard_map/ppermute | solution.py:299
  245.6 17.6 %collective-permute-start.69 = (bf16[32,3200]{1,0:T(8,128)(2,1)S(1)}, bf16[32,3200]{1,0:T(8,128)(2,1)S(1)}, u32[]{:S(2)}, u32[]{:S(2)}) collective-permute-start(bf16[32,3200]{1,0:T(8,128)(2,1)S(1)} %get-tuple-element.277), channel_id=1, source_target_pairs={{0,4},{1,5},{2,6},{3,7},{4,0},{5,1},{6,2},{7,3},{8,12},{9,13},{10,... | collective-permute-start | bytes 614408 | tf_op jit(solution)/shard_map/ppermute | solution.py:299
  247.3 16.0 %collective-permute-start.70 = (bf16[32,3200]{1,0:T(8,128)(2,1)S(1)}, bf16[32,3200]{1,0:T(8,128)(2,1)S(1)}, u32[]{:S(2)}, u32[]{:S(2)}) collective-permute-start(bf16[32,3200]{1,0:T(8,128)(2,1)S(1)} %get-tuple-element.276), channel_id=1, source_target_pairs={{0,6},{1,7},{2,4},{3,5},{4,2},{5,3},{6,0},{7,1},{8,14},{9,15},{10,... | collective-permute-start | bytes 614408 | tf_op jit(solution)/shard_map/ppermute | solution.py:299
  249.3 14.6 %collective-permute-start.71 = (bf16[32,3200]{1,0:T(8,128)(2,1)S(1)}, bf16[32,3200]{1,0:T(8,128)(2,1)S(1)}, u32[]{:S(2)}, u32[]{:S(2)}) collective-permute-start(bf16[32,3200]{1,0:T(8,128)(2,1)S(1)} %get-tuple-element.275), channel_id=1, source_target_pairs={{0,2},{1,3},{2,0},{3,1},{4,6},{5,7},{6,4},{7,5},{8,10},{9,11},{10,... | collective-permute-start | bytes 614408 | tf_op jit(solution)/shard_map/ppermute | solution.py:299
  (52 other events, 292.4 us)

commit v13 on v12

--- a/solution.py
+++ b/solution.py
@@ -225,7 +225,7 @@
             pltpu.SemaphoreType.DMA((blocks,)),
             pltpu.SemaphoreType.DMA((blocks,)),
         ],
-        compiler_params=settings(56),
+        compiler_params=settings(53),
         cost_estimate=pl.CostEstimate(
             flops=4 * rows * width * units,
             bytes_accessed=4 * width * units + 4 * rows * (width + units),
@@ -454,9 +454,8 @@
         ).astype(jnp.bfloat16)
         return jnp.where(jnp.any(picks, 1, keepdims=True), placed, text)
 
-    cut_b, arrived = tied((cut_b, arrived))
+    cut_b, rail_a, arrived = tied((cut_b, rail_a, arrived))
     terms_b = moves.send(cut_b)
-    rail_a, terms_b[-1] = tied((rail_a, terms_b[-1]))
     grad_out_a = moves.gathered(rail_a)
     near_a, far_a = vision_pass(grad_out_a, late, early, slope_a)
     near_a, terms_b, arrived = tied((near_a, terms_b, arrived))

time: 267 us -> 269 us (level)
  waiting for transfers between devices: 58.4 us -> 51.9 us
  starting transfers between devices: 77.1 us -> 83.3 us
    ppermute x36, starting transfers between devices: 60.9 us -> 66.6 us  [shift(): return lax.ppermute(block, 'tp', pairs)]
    ppermute x36, waiting for transfers between devices: 44.6 us -> 38.9 us  [shift(): return lax.ppermute(block, 'tp', pairs)]
  transfers between devices with their start and end apart: 72 -> 72, of which waited for: 28 -> 22; matrix products, arithmetic and copies ran while one was open for 7% -> 8% of each run, Pallas kernels for 38% -> 37%
where the time goes in v13:
time: 269 us; the launch traced here: 268 us
  Pallas kernels  101 us (38%)
  starting transfers between devices  83.3 us (31%)
  waiting for transfers between devices  51.9 us (19%)
  local copies, waits for them, and re-layouts  14.9 us (6%)
  other arithmetic  12.4 us (5%)
    ppermute x36, starting transfers between devices, shift(): return lax.ppermute(block, 'tp', pairs)  66.6 us
    pallas_call x4, Pallas kernels, vision_pass(): pl.pallas_call(functools.partial(vision_kernel, len(pieces), slope is Non...  57.7 us
    ppermute x36, waiting for transfers between devices, shift(): return lax.ppermute(block, 'tp', pairs)  38.9 us
    pallas_call x2, Pallas kernels, project_back(): pl.pallas_call(project_back_kernel, in_specs=whole_blocks(1) + [pl.BlockS...  22 us
    pallas_call x2, Pallas kernels, project(): pl.pallas_call(functools.partial(project_kernel, len(pieces)), in_specs=w...  19.4 us
    another operation x7, other arithmetic  6.53 us
    ppermute x24, starting transfers between devices, gathered(): other = [lax.ppermute(m, 'tp', self.pairs) for m in mine]  6.44 us
    ppermute x3, starting transfers between devices, per_device(): picked[s] = lax.ppermute(picked[s], 'grp', pairs)  5.42 us
  transfers between devices with their start and end apart: 72, of which 22 were waited for; matrix products, arithmetic and copies ran while one was open for 8% of the time, Pallas kernels for 37%

profile of v13, /device:TPU:0, one launch (start us, length us, event | category | flops | bytes accessed | tf_op | source)
XLA Modules:
  0.0 267.6 jit_solution(13752842757029336898)
XLA Ops:
  0.7 2.2 shard_map.131
  2.9 4.0 %collective-permute-start = (bf16[32,3200]{1,0:T(8,128)(2,1)}, bf16[32,3200]{1,0:T(8,128)(2,1)S(1)}, u32[]{:S(2)}, u32[]{:S(2)}) collective-permute-start(bf16[32,3200]{1,0:T(8,128)(2,1)} %get-tuple-element.123.refs_0_), channel_id=1, source_target_pairs={{0,4},{1,5},{2,6},{3,7},{4,0},{5,1},{6,2},{7,3},{8,12},{9,13},{10,... | collective-permute-start | bytes 614408 | tf_op jit(solution)/shard_map/ppermute | solution.py:299
  6.9 1.3 collective-permute-start.1
  8.5 0.8 reshape.424
  10.3 1.6 gather_fusion
  11.9 1.0 fusion.71
  12.8 2.5 collective-permute-start.3
  15.8 1.4 collective-permute-done.3
  17.2 2.4 collective-permute-start.5
  19.7 3.2 %collective-permute-done.5 = bf16[32,1024]{1,0:T(8,128)(2,1)S(1)} collective-permute-done((bf16[32,1024]{1,0:T(8,128)(2,1)S(1)}, bf16[32,1024]{1,0:T(8,128)(2,1)S(1)}, u32[]{:S(2)}, u32[]{:S(2)}) %collective-permute-start.5) | collective-permute-done | bytes 65568 | tf_op jit(solution)/shard_map/ppermute | solution.py:376
  24.0 5.1 %collective-permute-start.10 = (bf16[32,3200]{1,0:T(8,128)(2,1)S(1)}, bf16[32,3200]{1,0:T(8,128)(2,1)S(1)}, u32[]{:S(2)}, u32[]{:S(2)}) collective-permute-start(bf16[32,3200]{1,0:T(8,128)(2,1)S(1)} %copy-done.2), channel_id=1, source_target_pairs={{0,4},{1,5},{2,6},{3,7},{4,0},{5,1},{6,2},{7,3},{8,12},{9,13},{10,... | collective-permute-start | bytes 614408 | tf_op jit(solution)/shard_map/ppermute | solution.py:299
  30.8 14.5 %shard_map.132 = (bf16[128,3200]{1,0:T(8,128)(2,1)}, bf16[128,3200]{1,0:T(8,128)(2,1)}, f32[7,256,256]{2,1,0:T(8,128)}) custom-call(bf16[32,3200]{1,0:T(8,128)(2,1)S(1)} %copy-done.3, bf16[32,3200]{1,0:T(8,128)(2,1)S(1)} %collective-permute-done.refs_1_, bf16[32,3200]{1,0:T(8,128)(2,1)S(1)} %collective-permute-done.1.refs_2_, ...), custom_call_target="tpu_custom_call" | custom-call | flops 5242880000 | bytes 25395200 | tf_op jit(solution)/shard_map/pallas_call | solution.py:212
  46.9 1.1 collective-permute-done.17
  48.0 1.3 fusion.52
  49.4 3.6 %collective-permute-start.18 = (bf16[32,3200]{1,0:T(8,128)(2,1)S(1)}, bf16[32,3200]{1,0:T(8,128)(2,1)S(1)}, u32[]{:S(2)}, u32[]{:S(2)}) collective-permute-start(bf16[32,3200]{1,0:T(8,128)(2,1)S(1)} %get-tuple-element.290), channel_id=1, source_target_pairs={{0,4},{1,5},{2,6},{3,7},{4,0},{5,1},{6,2},{7,3},{8,12},{9,13},{10,... | collective-permute-start | bytes 614408 | tf_op jit(solution)/shard_map/ppermute | solution.py:299
  52.9 1.7 collective-permute-start.19
  56.1 14.5 %shard_map.133 = (bf16[128,3200]{1,0:T(8,128)(2,1)}, bf16[128,3200]{1,0:T(8,128)(2,1)}, f32[7,256,256]{2,1,0:T(8,128)}) custom-call(bf16[32,3200]{1,0:T(8,128)(2,1)S(1)} %copy-done.2, bf16[32,3200]{1,0:T(8,128)(2,1)S(1)} %collective-permute-done.10.refs_1_, bf16[32,3200]{1,0:T(8,128)(2,1)S(1)} %collective-permute-done.11.refs_2_, ...), custom_call_target="tpu_custom_call" | custom-call | flops 5242880000 | bytes 25395200 | tf_op jit(solution)/shard_map/pallas_call | solution.py:212
  72.2 2.7 %collective-permute-start.21 = (bf16[8,12800]{1,0:T(8,128)(2,1)S(1)}, bf16[8,12800]{1,0:T(8,128)(2,1)S(1)}, u32[]{:S(2)}, u32[]{:S(2)}) collective-permute-start(bf16[8,12800]{1,0:T(8,128)(2,1)S(1)} %multiply_convert_fusion.5.refs_0_), channel_id=1, source_target_pairs={{0,4},{1,5},{2,6},{3,7},{4,0},{5,1},{6,2},{7,3},{8,12},{9,13},{10,... | collective-permute-start | bytes 614408 | tf_op jit(solution)/shard_map/ppermute | solution.py:299
  74.9 1.7 collective-permute-start.22
  76.6 1.6 fusion.53
  80.8 2.1 collective-permute-start.25
  82.9 7.0 %collective-permute-done.21.refs_1_ = bf16[8,12800]{1,0:T(8,128)(2,1)S(1)} collective-permute-done((bf16[8,12800]{1,0:T(8,128)(2,1)S(1)}, bf16[8,12800]{1,0:T(8,128)(2,1)S(1)}, u32[]{:S(2)}, u32[]{:S(2)}) %collective-permute-start.21) | collective-permute-done | bytes 204832 | tf_op jit(solution)/shard_map/ppermute | solution.py:299
  89.9 2.0 collective-permute-done.23.refs_3_
  91.8 3.3 %collective-permute-done.25 = bf16[32,3200]{1,0:T(8,128)(2,1)S(1)} collective-permute-done((bf16[32,3200]{1,0:T(8,128)(2,1)}, bf16[32,3200]{1,0:T(8,128)(2,1)S(1)}, u32[]{:S(2)}, u32[]{:S(2)}) %collective-permute-start.25) | collective-permute-done | bytes 204832 | tf_op jit(solution)/shard_map/ppermute | solution.py:299
  96.9 2.1 collective-permute-start.31
  99.0 9.6 %shard_map.134 = (bf16[64,1024]{1,0:T(8,128)(2,1)S(1)}, bf16[64,1024]{1,0:T(8,128)(2,1)S(1)}) custom-call(bf16[8,12800]{1,0:T(8,128)(2,1)S(1)} %multiply_convert_fusion.5.refs_0_, bf16[8,12800]{1,0:T(8,128)(2,1)S(1)} %collective-permute-done.21.refs_1_, bf16[8,12800]{1,0:T(8,128)(2,1)S(1)} %collective-permute-done.22.refs_2_, ...), custom_call_target="tpu_custom_call" | custom-call | flops 1677721600 | bytes 29753344 | tf_op jit(solution)/shard_map/pallas_call | solution.py:249
  108.6 4.2 %collective-permute-done.30 = bf16[32,3200]{1,0:T(8,128)(2,1)S(1)} collective-permute-done((bf16[32,3200]{1,0:T(8,128)(2,1)S(1)}, bf16[32,3200]{1,0:T(8,128)(2,1)S(1)}, u32[]{:S(2)}, u32[]{:S(2)}) %collective-permute-start.30) | collective-permute-done | bytes 204832 | tf_op jit(solution)/shard_map/ppermute | solution.py:299
  114.1 5.1 %collective-permute-start.32 = (bf16[8,12800]{1,0:T(8,128)(2,1)S(1)}, bf16[8,12800]{1,0:T(8,128)(2,1)S(1)}, u32[]{:S(2)}, u32[]{:S(2)}) collective-permute-start(bf16[8,12800]{1,0:T(8,128)(2,1)S(1)} %multiply_convert_fusion.4.refs_0_), channel_id=1, source_target_pairs={{0,4},{1,5},{2,6},{3,7},{4,0},{5,1},{6,2},{7,3},{8,12},{9,13},{10,... | collective-permute-start | bytes 614408 | tf_op jit(solution)/shard_map/ppermute | solution.py:299
  119.2 2.1 collective-permute-start.33
  121.4 11.0 %shard_map.135 = (bf16[32,12800]{1,0:T(8,128)(2,1)S(1)}, bf16[32,12800]{1,0:T(8,128)(2,1)S(1)}) custom-call(bf16[64,1024]{1,0:T(8,128)(2,1)S(1)} %get-tuple-element.169.delta, bf16[12800,1024]{1,0:T(8,128)(2,1)} %weight.3), custom_call_target="tpu_custom_call" | custom-call | flops 1677721600 | bytes 29753344 | tf_op jit(solution)/shard_map/pallas_call | solution.py:269
  132.4 1.5 collective-permute-done.32.refs_1_
  135.7 1.3 collective-permute-done.39
  137.2 4.4 %collective-permute-start.40 = (bf16[8,12800]{1,0:T(8,128)(2,1)S(1)}, bf16[8,12800]{1,0:T(8,128)(2,1)S(1)}, u32[]{:S(2)}, u32[]{:S(2)}) collective-permute-start(bf16[8,12800]{1,0:T(8,128)(2,1)S(1)} %get-tuple-element.284), channel_id=1, source_target_pairs={{0,4},{1,5},{2,6},{3,7},{4,0},{5,1},{6,2},{7,3},{8,12},{9,13},{10,... | collective-permute-start | bytes 614408 | tf_op jit(solution)/shard_map/ppermute | solution.py:299
  141.6 1.7 collective-permute-start.41
  143.3 9.8 %shard_map.136 = (bf16[64,1024]{1,0:T(8,128)(2,1)S(1)}, bf16[64,1024]{1,0:T(8,128)(2,1)S(1)}) custom-call(bf16[8,12800]{1,0:T(8,128)(2,1)S(1)} %multiply_convert_fusion.4.refs_0_, bf16[8,12800]{1,0:T(8,128)(2,1)S(1)} %collective-permute-done.32.refs_1_, bf16[8,12800]{1,0:T(8,128)(2,1)S(1)} %collective-permute-done.33.refs_2_, ...), custom_call_target="tpu_custom_call" | custom-call | flops 1677721600 | bytes 29753344 | tf_op jit(solution)/shard_map/pallas_call | solution.py:249
  153.2 3.1 %collective-permute-done.40 = bf16[8,12800]{1,0:T(8,128)(2,1)S(1)} collective-permute-done((bf16[8,12800]{1,0:T(8,128)(2,1)S(1)}, bf16[8,12800]{1,0:T(8,128)(2,1)S(1)}, u32[]{:S(2)}, u32[]{:S(2)}) %collective-permute-start.40) | collective-permute-done | bytes 204832 | tf_op jit(solution)/shard_map/ppermute | solution.py:299
  156.3 0.8 collective-permute-done.42
  157.8 0.7 copy-done.7
  158.5 3.9 %collective-permute-start.43 = (bf16[32,3200]{1,0:T(8,128)(2,1)S(1)}, bf16[32,3200]{1,0:T(8,128)(2,1)S(1)}, u32[]{:S(2)}, u32[]{:S(2)}) collective-permute-start(bf16[32,3200]{1,0:T(8,128)(2,1)S(1)} %multiply_convert_fusion.2.refs_0_), channel_id=1, source_target_pairs={{0,4},{1,5},{2,6},{3,7},{4,0},{5,1},{6,2},{7,3},{8,12},{9,13},{10,... | collective-permute-start | bytes 614408 | tf_op jit(solution)/shard_map/ppermute | solution.py:299
  162.5 2.1 collective-permute-start.44
  164.6 11.0 %shard_map.137 = (bf16[32,12800]{1,0:T(8,128)(2,1)S(1)}, bf16[32,12800]{1,0:T(8,128)(2,1)S(1)}) custom-call(bf16[64,1024]{1,0:T(8,128)(2,1)S(1)} %get-tuple-element.186.delta, bf16[12800,1024]{1,0:T(8,128)(2,1)} %weight.3), custom_call_target="tpu_custom_call" | custom-call | flops 1677721600 | bytes 29753344 | tf_op jit(solution)/shard_map/pallas_call | solution.py:269
  175.7 1.6 collective-permute-done.43.refs_1_
  179.9 1.3 fusion.55
  181.3 4.4 %collective-permute-start.51 = (bf16[8,12800]{1,0:T(8,128)(2,1)S(1)}, bf16[8,12800]{1,0:T(8,128)(2,1)S(1)}, u32[]{:S(2)}, u32[]{:S(2)}) collective-permute-start(bf16[8,12800]{1,0:T(8,128)(2,1)S(1)} %get-tuple-element.281), channel_id=1, source_target_pairs={{0,4},{1,5},{2,6},{3,7},{4,0},{5,1},{6,2},{7,3},{8,12},{9,13},{10,... | collective-permute-start | bytes 614408 | tf_op jit(solution)/shard_map/ppermute | solution.py:299
  185.7 1.7 collective-permute-start.52
  188.2 14.4 %shard_map.138 = (bf16[128,3200]{1,0:T(8,128)(2,1)}, bf16[128,3200]{1,0:T(8,128)(2,1)}) custom-call(bf16[32,3200]{1,0:T(8,128)(2,1)S(1)} %multiply_convert_fusion.2.refs_0_, bf16[32,3200]{1,0:T(8,128)(2,1)S(1)} %collective-permute-done.43.refs_1_, bf16[32,3200]{1,0:T(8,128)(2,1)S(1)} %collective-permute-done.44.refs_2_, ...), custom_call_target="tpu_custom_call" | custom-call | flops 5242880000 | bytes 25395200 | tf_op jit(solution)/shard_map/pallas_call | solution.py:212
  203.4 2.7 %collective-permute-start.55 = (bf16[32,3200]{1,0:T(8,128)(2,1)S(1)}, bf16[32,3200]{1,0:T(8,128)(2,1)S(1)}, u32[]{:S(2)}, u32[]{:S(2)}) collective-permute-start(bf16[32,3200]{1,0:T(8,128)(2,1)S(1)} %multiply_convert_fusion.refs_0_), channel_id=1, source_target_pairs={{0,4},{1,5},{2,6},{3,7},{4,0},{5,1},{6,2},{7,3},{8,12},{9,13},{10,... | collective-permute-start | bytes 614408 | tf_op jit(solution)/shard_map/ppermute | solution.py:299
  206.1 1.9 collective-permute-start.56
  209.8 1.6 collective-permute-start.58
  211.3 1.5 collective-permute-start.59
  212.8 1.6 fusion.56
  215.1 1.5 collective-permute-start.60
  216.6 2.7 %collective-permute-done.60 = bf16[32,1024]{1,0:T(8,128)(2,1)S(1)} collective-permute-done((bf16[32,1024]{1,0:T(8,128)(2,1)S(1)}, bf16[32,1024]{1,0:T(8,128)(2,1)S(1)}, u32[]{:S(2)}, u32[]{:S(2)}) %collective-permute-start.60) | collective-permute-done | bytes 65568 | tf_op jit(solution)/shard_map/ppermute | solution.py:445
  219.4 1.7 collective-permute-done.55.refs_1_
  221.1 0.9 collective-permute-done.57.refs_3_
  223.0 4.3 %collective-permute-start.65 = (bf16[32,3200]{1,0:T(8,128)(2,1)S(1)}, bf16[32,3200]{1,0:T(8,128)(2,1)S(1)}, u32[]{:S(2)}, u32[]{:S(2)}) collective-permute-start(bf16[32,3200]{1,0:T(8,128)(2,1)S(1)} %get-tuple-element.217), channel_id=1, source_target_pairs={{0,4},{1,5},{2,6},{3,7},{4,0},{5,1},{6,2},{7,3},{8,12},{9,13},{10,... | collective-permute-start | bytes 614408 | tf_op jit(solution)/shard_map/ppermute | solution.py:299
  227.4 1.7 collective-permute-start.66
  229.9 14.3 %shard_map.139 = (bf16[128,3200]{1,0:T(8,128)(2,1)}, bf16[128,3200]{1,0:T(8,128)(2,1)}) custom-call(bf16[32,3200]{1,0:T(8,128)(2,1)S(1)} %multiply_convert_fusion.refs_0_, bf16[32,3200]{1,0:T(8,128)(2,1)S(1)} %collective-permute-done.55.refs_1_, bf16[32,3200]{1,0:T(8,128)(2,1)S(1)} %collective-permute-done.56.refs_2_, ...), custom_call_target="tpu_custom_call" | custom-call | flops 5242880000 | bytes 25395200 | tf_op jit(solution)/shard_map/pallas_call | solution.py:212
  244.5 2.4 collective-permute-done.68
  247.1 2.7 %collective-permute-start.69 = (bf16[32,3200]{1,0:T(8,128)(2,1)S(1)}, bf16[32,3200]{1,0:T(8,128)(2,1)S(1)}, u32[]{:S(2)}, u32[]{:S(2)}) collective-permute-start(bf16[32,3200]{1,0:T(8,128)(2,1)S(1)} %get-tuple-element.275), channel_id=1, source_target_pairs={{0,4},{1,5},{2,6},{3,7},{4,0},{5,1},{6,2},{7,3},{8,12},{9,13},{10,... | collective-permute-start | bytes 614408 | tf_op jit(solution)/shard_map/ppermute | solution.py:299
  249.8 1.7 collective-permute-start.70
  251.5 2.2 fusion
  253.7 11.1 %collective-permute-done.69 = bf16[32,3200]{1,0:T(8,128)(2,1)S(1)} collective-permute-done((bf16[32,3200]{1,0:T(8,128)(2,1)S(1)}, bf16[32,3200]{1,0:T(8,128)(2,1)S(1)}, u32[]{:S(2)}, u32[]{:S(2)}) %collective-permute-start.69) | collective-permute-done | bytes 204832 | tf_op jit(solution)/shard_map/ppermute | solution.py:299
  266.2 0.8 pad_maximum_fusion
  (261 shorter events, 28.3 us)
Async XLA Ops:
  2.9 20.0 %collective-permute-start = (bf16[32,3200]{1,0:T(8,128)(2,1)}, bf16[32,3200]{1,0:T(8,128)(2,1)S(1)}, u32[]{:S(2)}, u32[]{:S(2)}) collective-permute-start(bf16[32,3200]{1,0:T(8,128)(2,1)} %get-tuple-element.123.refs_0_), channel_id=1, source_target_pairs={{0,4},{1,5},{2,6},{3,7},{4,0},{5,1},{6,2},{7,3},{8,12},{9,13},{10,... | collective-permute-start | bytes 614408 | tf_op jit(solution)/shard_map/ppermute | solution.py:299
  6.9 16.0 %collective-permute-start.1 = (bf16[32,3200]{1,0:T(8,128)(2,1)}, bf16[32,3200]{1,0:T(8,128)(2,1)S(1)}, u32[]{:S(2)}, u32[]{:S(2)}) collective-permute-start(bf16[32,3200]{1,0:T(8,128)(2,1)} %get-tuple-element.123.refs_0_), channel_id=1, source_target_pairs={{0,6},{1,7},{2,4},{3,5},{4,2},{5,3},{6,0},{7,1},{8,14},{9,15},{10,... | collective-permute-start | bytes 614408 | tf_op jit(solution)/shard_map/ppermute | solution.py:299
  8.2 14.6 %collective-permute-start.2 = (bf16[32,3200]{1,0:T(8,128)(2,1)}, bf16[32,3200]{1,0:T(8,128)(2,1)S(1)}, u32[]{:S(2)}, u32[]{:S(2)}) collective-permute-start(bf16[32,3200]{1,0:T(8,128)(2,1)} %get-tuple-element.123.refs_0_), channel_id=1, source_target_pairs={{0,2},{1,3},{2,0},{3,1},{4,6},{5,7},{6,4},{7,5},{8,10},{9,11},{10,... | collective-permute-start | bytes 614408 | tf_op jit(solution)/shard_map/ppermute | solution.py:299
  12.8 4.4 %collective-permute-start.3 = (bf16[32,1024]{1,0:T(8,128)(2,1)S(1)}, bf16[32,1024]{1,0:T(8,128)(2,1)S(1)}, u32[]{:S(2)}, u32[]{:S(2)}) collective-permute-start(bf16[32,1024]{1,0:T(8,128)(2,1)S(1)} %get-tuple-element.303), channel_id=1, source_target_pairs={{0,24},{8,0},{16,8},{24,16},{1,25},{9,1},{17,9},{25,17},{2,26},{10... | collective-permute-start | bytes 196616 | tf_op jit(solution)/shard_map/ppermute | solution.py:376
  15.3 4.3 %collective-permute-start.4 = (bf16[32,1024]{1,0:T(8,128)(2,1)S(1)}, bf16[32,1024]{1,0:T(8,128)(2,1)S(1)}, u32[]{:S(2)}, u32[]{:S(2)}) collective-permute-start(bf16[32,1024]{1,0:T(8,128)(2,1)S(1)} %get-tuple-element.302), channel_id=1, source_target_pairs={{0,16},{8,24},{16,0},{24,8},{1,17},{9,25},{17,1},{25,9},{2,18},{10... | collective-permute-start | bytes 196616 | tf_op jit(solution)/shard_map/ppermute | solution.py:376
  17.2 5.6 %collective-permute-start.5 = (bf16[32,1024]{1,0:T(8,128)(2,1)S(1)}, bf16[32,1024]{1,0:T(8,128)(2,1)S(1)}, u32[]{:S(2)}, u32[]{:S(2)}) collective-permute-start(bf16[32,1024]{1,0:T(8,128)(2,1)S(1)} %get-tuple-element.301), channel_id=1, source_target_pairs={{0,8},{8,16},{16,24},{24,0},{1,9},{9,17},{17,25},{25,1},{2,10},{10... | collective-permute-start | bytes 196616 | tf_op jit(solution)/shard_map/ppermute | solution.py:376
  22.9 6.3 %collective-permute-start.6 = (bf16[32,3200]{1,0:T(8,128)(2,1)S(1)}, bf16[32,3200]{1,0:T(8,128)(2,1)S(1)}, u32[]{:S(2)}, u32[]{:S(2)}) collective-permute-start(bf16[32,3200]{1,0:T(8,128)(2,1)S(1)} %copy-done.3), channel_id=1, source_target_pairs={{0,1},{1,0},{2,3},{3,2},{4,5},{5,4},{6,7},{7,6},{8,9},{9,8},{10,11... | collective-permute-start | bytes 614408 | tf_op jit(solution)/shard_map/ppermute | solution.py:305
  23.0 6.7 %collective-permute-start.7 = (bf16[32,3200]{1,0:T(8,128)(2,1)S(1)}, bf16[32,3200]{1,0:T(8,128)(2,1)S(1)}, u32[]{:S(2)}, u32[]{:S(2)}) collective-permute-start(bf16[32,3200]{1,0:T(8,128)(2,1)S(1)} %collective-permute-done.refs_1_), channel_id=1, source_target_pairs={{0,1},{1,0},{2,3},{3,2},{4,5},{5,4},{6,7},{7,6},{8,9},{9,8},{10,11... | collective-permute-start | bytes 614408 | tf_op jit(solution)/shard_map/ppermute | solution.py:305
  23.5 6.6 %collective-permute-start.8 = (bf16[32,3200]{1,0:T(8,128)(2,1)S(1)}, bf16[32,3200]{1,0:T(8,128)(2,1)S(1)}, u32[]{:S(2)}, u32[]{:S(2)}) collective-permute-start(bf16[32,3200]{1,0:T(8,128)(2,1)S(1)} %collective-permute-done.1.refs_2_), channel_id=1, source_target_pairs={{0,1},{1,0},{2,3},{3,2},{4,5},{5,4},{6,7},{7,6},{8,9},{9,8},{10,11... | collective-permute-start | bytes 614408 | tf_op jit(solution)/shard_map/ppermute | solution.py:305
  23.5 6.5 %collective-permute-start.9 = (bf16[32,3200]{1,0:T(8,128)(2,1)S(1)}, bf16[32,3200]{1,0:T(8,128)(2,1)S(1)}, u32[]{:S(2)}, u32[]{:S(2)}) collective-permute-start(bf16[32,3200]{1,0:T(8,128)(2,1)S(1)} %collective-permute-done.2.refs_3_), channel_id=1, source_target_pairs={{0,1},{1,0},{2,3},{3,2},{4,5},{5,4},{6,7},{7,6},{8,9},{9,8},{10,11... | collective-permute-start | bytes 614408 | tf_op jit(solution)/shard_map/ppermute | solution.py:305
  24.0 21.3 %collective-permute-start.10 = (bf16[32,3200]{1,0:T(8,128)(2,1)S(1)}, bf16[32,3200]{1,0:T(8,128)(2,1)S(1)}, u32[]{:S(2)}, u32[]{:S(2)}) collective-permute-start(bf16[32,3200]{1,0:T(8,128)(2,1)S(1)} %copy-done.2), channel_id=1, source_target_pairs={{0,4},{1,5},{2,6},{3,7},{4,0},{5,1},{6,2},{7,3},{8,12},{9,13},{10,... | collective-permute-start | bytes 614408 | tf_op jit(solution)/shard_map/ppermute | solution.py:299
  29.2 16.2 %collective-permute-start.11 = (bf16[32,3200]{1,0:T(8,128)(2,1)S(1)}, bf16[32,3200]{1,0:T(8,128)(2,1)S(1)}, u32[]{:S(2)}, u32[]{:S(2)}) collective-permute-start(bf16[32,3200]{1,0:T(8,128)(2,1)S(1)} %copy-done.2), channel_id=1, source_target_pairs={{0,6},{1,7},{2,4},{3,5},{4,2},{5,3},{6,0},{7,1},{8,14},{9,15},{10,... | collective-permute-start | bytes 614408 | tf_op jit(solution)/shard_map/ppermute | solution.py:299
  29.7 15.6 %collective-permute-start.12 = (bf16[32,3200]{1,0:T(8,128)(2,1)S(1)}, bf16[32,3200]{1,0:T(8,128)(2,1)S(1)}, u32[]{:S(2)}, u32[]{:S(2)}) collective-permute-start(bf16[32,3200]{1,0:T(8,128)(2,1)S(1)} %copy-done.2), channel_id=1, source_target_pairs={{0,2},{1,3},{2,0},{3,1},{4,6},{5,7},{6,4},{7,5},{8,10},{9,11},{10,... | collective-permute-start | bytes 614408 | tf_op jit(solution)/shard_map/ppermute | solution.py:299
  45.7 7.2 %collective-permute-start.13 = (bf16[32,3200]{1,0:T(8,128)(2,1)S(1)}, bf16[32,3200]{1,0:T(8,128)(2,1)S(1)}, u32[]{:S(2)}, u32[]{:S(2)}) collective-permute-start(bf16[32,3200]{1,0:T(8,128)(2,1)S(1)} %copy-done.2), channel_id=1, source_target_pairs={{0,1},{1,0},{2,3},{3,2},{4,5},{5,4},{6,7},{7,6},{8,9},{9,8},{10,11... | collective-permute-start | bytes 614408 | tf_op jit(solution)/shard_map/ppermute | solution.py:305
  46.3 8.3 %collective-permute-start.14 = (bf16[32,3200]{1,0:T(8,128)(2,1)S(1)}, bf16[32,3200]{1,0:T(8,128)(2,1)S(1)}, u32[]{:S(2)}, u32[]{:S(2)}) collective-permute-start(bf16[32,3200]{1,0:T(8,128)(2,1)S(1)} %collective-permute-done.10.refs_1_), channel_id=1, source_target_pairs={{0,1},{1,0},{2,3},{3,2},{4,5},{5,4},{6,7},{7,6},{8,9},{9,8},{10,11... | collective-permute-start | bytes 614408 | tf_op jit(solution)/shard_map/ppermute | solution.py:305
  46.4 8.3 %collective-permute-start.15 = (bf16[32,3200]{1,0:T(8,128)(2,1)S(1)}, bf16[32,3200]{1,0:T(8,128)(2,1)S(1)}, u32[]{:S(2)}, u32[]{:S(2)}) collective-permute-start(bf16[32,3200]{1,0:T(8,128)(2,1)S(1)} %collective-permute-done.11.refs_2_), channel_id=1, source_target_pairs={{0,1},{1,0},{2,3},{3,2},{4,5},{5,4},{6,7},{7,6},{8,9},{9,8},{10,11... | collective-permute-start | bytes 614408 | tf_op jit(solution)/shard_map/ppermute | solution.py:305
  46.8 7.8 %collective-permute-start.16 = (bf16[32,3200]{1,0:T(8,128)(2,1)S(1)}, bf16[32,3200]{1,0:T(8,128)(2,1)S(1)}, u32[]{:S(2)}, u32[]{:S(2)}) collective-permute-start(bf16[32,3200]{1,0:T(8,128)(2,1)S(1)} %collective-permute-done.12.refs_3_), channel_id=1, source_target_pairs={{0,1},{1,0},{2,3},{3,2},{4,5},{5,4},{6,7},{7,6},{8,9},{9,8},{10,11... | collective-permute-start | bytes 614408 | tf_op jit(solution)/shard_map/ppermute | solution.py:305
  49.4 21.3 %collective-permute-start.18 = (bf16[32,3200]{1,0:T(8,128)(2,1)S(1)}, bf16[32,3200]{1,0:T(8,128)(2,1)S(1)}, u32[]{:S(2)}, u32[]{:S(2)}) collective-permute-start(bf16[32,3200]{1,0:T(8,128)(2,1)S(1)} %get-tuple-element.290), channel_id=1, source_target_pairs={{0,4},{1,5},{2,6},{3,7},{4,0},{5,1},{6,2},{7,3},{8,12},{9,13},{10,... | collective-permute-start | bytes 614408 | tf_op jit(solution)/shard_map/ppermute | solution.py:299
  52.9 17.8 %collective-permute-start.19 = (bf16[32,3200]{1,0:T(8,128)(2,1)S(1)}, bf16[32,3200]{1,0:T(8,128)(2,1)S(1)}, u32[]{:S(2)}, u32[]{:S(2)}) collective-permute-start(bf16[32,3200]{1,0:T(8,128)(2,1)S(1)} %get-tuple-element.289), channel_id=1, source_target_pairs={{0,6},{1,7},{2,4},{3,5},{4,2},{5,3},{6,0},{7,1},{8,14},{9,15},{10,... | collective-permute-start | bytes 614408 | tf_op jit(solution)/shard_map/ppermute | solution.py:299
  54.6 16.1 %collective-permute-start.20 = (bf16[32,3200]{1,0:T(8,128)(2,1)S(1)}, bf16[32,3200]{1,0:T(8,128)(2,1)S(1)}, u32[]{:S(2)}, u32[]{:S(2)}) collective-permute-start(bf16[32,3200]{1,0:T(8,128)(2,1)S(1)} %get-tuple-element.288), channel_id=1, source_target_pairs={{0,2},{1,3},{2,0},{3,1},{4,6},{5,7},{6,4},{7,5},{8,10},{9,11},{10,... | collective-permute-start | bytes 614408 | tf_op jit(solution)/shard_map/ppermute | solution.py:299
  70.6 6.0 %collective-permute-start.24 = (bf16[128,3200]{1,0:T(8,128)(2,1)}, bf16[128,3200]{1,0:T(8,128)(2,1)}, u32[]{:S(2)}, u32[]{:S(2)}) collective-permute-start(bf16[128,3200]{1,0:T(8,128)(2,1)} %get-tuple-element.147), channel_id=1, source_target_pairs={{0,1},{1,0},{2,3},{3,2},{4,5},{5,4},{6,7},{7,6},{8,9},{9,8},{10,11... | collective-permute-start | bytes 2457608 | tf_op jit(solution)/shard_map/ppermute | solution.py:312
  72.2 17.7 %collective-permute-start.21 = (bf16[8,12800]{1,0:T(8,128)(2,1)S(1)}, bf16[8,12800]{1,0:T(8,128)(2,1)S(1)}, u32[]{:S(2)}, u32[]{:S(2)}) collective-permute-start(bf16[8,12800]{1,0:T(8,128)(2,1)S(1)} %multiply_convert_fusion.5.refs_0_), channel_id=1, source_target_pairs={{0,4},{1,5},{2,6},{3,7},{4,0},{5,1},{6,2},{7,3},{8,12},{9,13},{10,... | collective-permute-start | bytes 614408 | tf_op jit(solution)/shard_map/ppermute | solution.py:299
  74.9 15.0 %collective-permute-start.22 = (bf16[8,12800]{1,0:T(8,128)(2,1)S(1)}, bf16[8,12800]{1,0:T(8,128)(2,1)S(1)}, u32[]{:S(2)}, u32[]{:S(2)}) collective-permute-start(bf16[8,12800]{1,0:T(8,128)(2,1)S(1)} %multiply_convert_fusion.5.refs_0_), channel_id=1, source_target_pairs={{0,6},{1,7},{2,4},{3,5},{4,2},{5,3},{6,0},{7,1},{8,14},{9,15},{10,... | collective-permute-start | bytes 614408 | tf_op jit(solution)/shard_map/ppermute | solution.py:299
  76.6 15.2 %collective-permute-start.23 = (bf16[8,12800]{1,0:T(8,128)(2,1)S(1)}, bf16[8,12800]{1,0:T(8,128)(2,1)S(1)}, u32[]{:S(2)}, u32[]{:S(2)}) collective-permute-start(bf16[8,12800]{1,0:T(8,128)(2,1)S(1)} %multiply_convert_fusion.5.refs_0_), channel_id=1, source_target_pairs={{0,2},{1,3},{2,0},{3,1},{4,6},{5,7},{6,4},{7,5},{8,10},{9,11},{10,... | collective-permute-start | bytes 614408 | tf_op jit(solution)/shard_map/ppermute | solution.py:299
  80.8 14.4 %collective-permute-start.25 = (bf16[32,3200]{1,0:T(8,128)(2,1)}, bf16[32,3200]{1,0:T(8,128)(2,1)S(1)}, u32[]{:S(2)}, u32[]{:S(2)}) collective-permute-start(bf16[32,3200]{1,0:T(8,128)(2,1)} %get-tuple-element.152), channel_id=1, source_target_pairs={{0,2},{1,3},{2,0},{3,1},{4,6},{5,7},{6,4},{7,5},{8,10},{9,11},{10,... | collective-permute-start | bytes 614408 | tf_op jit(solution)/shard_map/ppermute | solution.py:299
  96.2 16.6 %collective-permute-start.30 = (bf16[32,3200]{1,0:T(8,128)(2,1)S(1)}, bf16[32,3200]{1,0:T(8,128)(2,1)S(1)}, u32[]{:S(2)}, u32[]{:S(2)}) collective-permute-start(bf16[32,3200]{1,0:T(8,128)(2,1)S(1)} %get-tuple-element.161), channel_id=1, source_target_pairs={{0,4},{1,5},{2,6},{3,7},{4,0},{5,1},{6,2},{7,3},{8,12},{9,13},{10,... | collective-permute-start | bytes 614408 | tf_op jit(solution)/shard_map/ppermute | solution.py:299
  96.9 16.0 %collective-permute-start.31 = (bf16[32,3200]{1,0:T(8,128)(2,1)S(1)}, bf16[32,3200]{1,0:T(8,128)(2,1)S(1)}, u32[]{:S(2)}, u32[]{:S(2)}) collective-permute-start(bf16[32,3200]{1,0:T(8,128)(2,1)S(1)} %get-tuple-element.162), channel_id=1, source_target_pairs={{0,6},{1,7},{2,4},{3,5},{4,2},{5,3},{6,0},{7,1},{8,14},{9,15},{10,... | collective-permute-start | bytes 614408 | tf_op jit(solution)/shard_map/ppermute | solution.py:299
  114.1 19.8 %collective-permute-start.32 = (bf16[8,12800]{1,0:T(8,128)(2,1)S(1)}, bf16[8,12800]{1,0:T(8,128)(2,1)S(1)}, u32[]{:S(2)}, u32[]{:S(2)}) collective-permute-start(bf16[8,12800]{1,0:T(8,128)(2,1)S(1)} %multiply_convert_fusion.4.refs_0_), channel_id=1, source_target_pairs={{0,4},{1,5},{2,6},{3,7},{4,0},{5,1},{6,2},{7,3},{8,12},{9,13},{10,... | collective-permute-start | bytes 614408 | tf_op jit(solution)/shard_map/ppermute | solution.py:299
  119.2 14.7 %collective-permute-start.33 = (bf16[8,12800]{1,0:T(8,128)(2,1)S(1)}, bf16[8,12800]{1,0:T(8,128)(2,1)S(1)}, u32[]{:S(2)}, u32[]{:S(2)}) collective-permute-start(bf16[8,12800]{1,0:T(8,128)(2,1)S(1)} %multiply_convert_fusion.4.refs_0_), channel_id=1, source_target_pairs={{0,6},{1,7},{2,4},{3,5},{4,2},{5,3},{6,0},{7,1},{8,14},{9,15},{10,... | collective-permute-start | bytes 614408 | tf_op jit(solution)/shard_map/ppermute | solution.py:299
  121.4 13.3 %collective-permute-start.34 = (bf16[8,12800]{1,0:T(8,128)(2,1)S(1)}, bf16[8,12800]{1,0:T(8,128)(2,1)S(1)}, u32[]{:S(2)}, u32[]{:S(2)}) collective-permute-start(bf16[8,12800]{1,0:T(8,128)(2,1)S(1)} %multiply_convert_fusion.4.refs_0_), channel_id=1, source_target_pairs={{0,2},{1,3},{2,0},{3,1},{4,6},{5,7},{6,4},{7,5},{8,10},{9,11},{10,... | collective-permute-start | bytes 614408 | tf_op jit(solution)/shard_map/ppermute | solution.py:299
  134.7 7.0 %collective-permute-start.35 = (bf16[8,12800]{1,0:T(8,128)(2,1)S(1)}, bf16[8,12800]{1,0:T(8,128)(2,1)S(1)}, u32[]{:S(2)}, u32[]{:S(2)}) collective-permute-start(bf16[8,12800]{1,0:T(8,128)(2,1)S(1)} %multiply_convert_fusion.4.refs_0_), channel_id=1, source_target_pairs={{0,1},{1,0},{2,3},{3,2},{4,5},{5,4},{6,7},{7,6},{8,9},{9,8},{10,11... | collective-permute-start | bytes 614408 | tf_op jit(solution)/shard_map/ppermute | solution.py:305
  135.2 8.1 %collective-permute-start.36 = (bf16[8,12800]{1,0:T(8,128)(2,1)S(1)}, bf16[8,12800]{1,0:T(8,128)(2,1)S(1)}, u32[]{:S(2)}, u32[]{:S(2)}) collective-permute-start(bf16[8,12800]{1,0:T(8,128)(2,1)S(1)} %collective-permute-done.32.refs_1_), channel_id=1, source_target_pairs={{0,1},{1,0},{2,3},{3,2},{4,5},{5,4},{6,7},{7,6},{8,9},{9,8},{10,11... | collective-permute-start | bytes 614408 | tf_op jit(solution)/shard_map/ppermute | solution.py:305
  135.2 8.1 %collective-permute-start.37 = (bf16[8,12800]{1,0:T(8,128)(2,1)S(1)}, bf16[8,12800]{1,0:T(8,128)(2,1)S(1)}, u32[]{:S(2)}, u32[]{:S(2)}) collective-permute-start(bf16[8,12800]{1,0:T(8,128)(2,1)S(1)} %collective-permute-done.33.refs_2_), channel_id=1, source_target_pairs={{0,1},{1,0},{2,3},{3,2},{4,5},{5,4},{6,7},{7,6},{8,9},{9,8},{10,11... | collective-permute-start | bytes 614408 | tf_op jit(solution)/shard_map/ppermute | solution.py:305
  135.7 7.6 %collective-permute-start.38 = (bf16[8,12800]{1,0:T(8,128)(2,1)S(1)}, bf16[8,12800]{1,0:T(8,128)(2,1)S(1)}, u32[]{:S(2)}, u32[]{:S(2)}) collective-permute-start(bf16[8,12800]{1,0:T(8,128)(2,1)S(1)} %collective-permute-done.34.refs_3_), channel_id=1, source_target_pairs={{0,1},{1,0},{2,3},{3,2},{4,5},{5,4},{6,7},{7,6},{8,9},{9,8},{10,11... | collective-permute-start | bytes 614408 | tf_op jit(solution)/shard_map/ppermute | solution.py:305
  137.2 19.1 %collective-permute-start.40 = (bf16[8,12800]{1,0:T(8,128)(2,1)S(1)}, bf16[8,12800]{1,0:T(8,128)(2,1)S(1)}, u32[]{:S(2)}, u32[]{:S(2)}) collective-permute-start(bf16[8,12800]{1,0:T(8,128)(2,1)S(1)} %get-tuple-element.284), channel_id=1, source_target_pairs={{0,4},{1,5},{2,6},{3,7},{4,0},{5,1},{6,2},{7,3},{8,12},{9,13},{10,... | collective-permute-start | bytes 614408 | tf_op jit(solution)/shard_map/ppermute | solution.py:299
  141.6 14.7 %collective-permute-start.41 = (bf16[8,12800]{1,0:T(8,128)(2,1)S(1)}, bf16[8,12800]{1,0:T(8,128)(2,1)S(1)}, u32[]{:S(2)}, u32[]{:S(2)}) collective-permute-start(bf16[8,12800]{1,0:T(8,128)(2,1)S(1)} %get-tuple-element.283), channel_id=1, source_target_pairs={{0,6},{1,7},{2,4},{3,5},{4,2},{5,3},{6,0},{7,1},{8,14},{9,15},{10,... | collective-permute-start | bytes 614408 | tf_op jit(solution)/shard_map/ppermute | solution.py:299
  143.3 13.8 %collective-permute-start.42 = (bf16[8,12800]{1,0:T(8,128)(2,1)S(1)}, bf16[8,12800]{1,0:T(8,128)(2,1)S(1)}, u32[]{:S(2)}, u32[]{:S(2)}) collective-permute-start(bf16[8,12800]{1,0:T(8,128)(2,1)S(1)} %get-tuple-element.282), channel_id=1, source_target_pairs={{0,2},{1,3},{2,0},{3,1},{4,6},{5,7},{6,4},{7,5},{8,10},{9,11},{10,... | collective-permute-start | bytes 614408 | tf_op jit(solution)/shard_map/ppermute | solution.py:299
  158.5 18.7 %collective-permute-start.43 = (bf16[32,3200]{1,0:T(8,128)(2,1)S(1)}, bf16[32,3200]{1,0:T(8,128)(2,1)S(1)}, u32[]{:S(2)}, u32[]{:S(2)}) collective-permute-start(bf16[32,3200]{1,0:T(8,128)(2,1)S(1)} %multiply_convert_fusion.2.refs_0_), channel_id=1, source_target_pairs={{0,4},{1,5},{2,6},{3,7},{4,0},{5,1},{6,2},{7,3},{8,12},{9,13},{10,... | collective-permute-start | bytes 614408 | tf_op jit(solution)/shard_map/ppermute | solution.py:299
  162.5 14.8 %collective-permute-start.44 = (bf16[32,3200]{1,0:T(8,128)(2,1)S(1)}, bf16[32,3200]{1,0:T(8,128)(2,1)S(1)}, u32[]{:S(2)}, u32[]{:S(2)}) collective-permute-start(bf16[32,3200]{1,0:T(8,128)(2,1)S(1)} %multiply_convert_fusion.2.refs_0_), channel_id=1, source_target_pairs={{0,6},{1,7},{2,4},{3,5},{4,2},{5,3},{6,0},{7,1},{8,14},{9,15},{10,... | collective-permute-start | bytes 614408 | tf_op jit(solution)/shard_map/ppermute | solution.py:299
  164.6 12.9 %collective-permute-start.45 = (bf16[32,3200]{1,0:T(8,128)(2,1)S(1)}, bf16[32,3200]{1,0:T(8,128)(2,1)S(1)}, u32[]{:S(2)}, u32[]{:S(2)}) collective-permute-start(bf16[32,3200]{1,0:T(8,128)(2,1)S(1)} %multiply_convert_fusion.2.refs_0_), channel_id=1, source_target_pairs={{0,2},{1,3},{2,0},{3,1},{4,6},{5,7},{6,4},{7,5},{8,10},{9,11},{10,... | collective-permute-start | bytes 614408 | tf_op jit(solution)/shard_map/ppermute | solution.py:299
  178.5 7.2 %collective-permute-start.46 = (bf16[32,3200]{1,0:T(8,128)(2,1)S(1)}, bf16[32,3200]{1,0:T(8,128)(2,1)S(1)}, u32[]{:S(2)}, u32[]{:S(2)}) collective-permute-start(bf16[32,3200]{1,0:T(8,128)(2,1)S(1)} %multiply_convert_fusion.2.refs_0_), channel_id=1, source_target_pairs={{0,1},{1,0},{2,3},{3,2},{4,5},{5,4},{6,7},{7,6},{8,9},{9,8},{10,11... | collective-permute-start | bytes 614408 | tf_op jit(solution)/shard_map/ppermute | solution.py:305
  179.1 8.3 %collective-permute-start.47 = (bf16[32,3200]{1,0:T(8,128)(2,1)S(1)}, bf16[32,3200]{1,0:T(8,128)(2,1)S(1)}, u32[]{:S(2)}, u32[]{:S(2)}) collective-permute-start(bf16[32,3200]{1,0:T(8,128)(2,1)S(1)} %collective-permute-done.43.refs_1_), channel_id=1, source_target_pairs={{0,1},{1,0},{2,3},{3,2},{4,5},{5,4},{6,7},{7,6},{8,9},{9,8},{10,11... | collective-permute-start | bytes 614408 | tf_op jit(solution)/shard_map/ppermute | solution.py:305
  179.2 8.2 %collective-permute-start.48 = (bf16[32,3200]{1,0:T(8,128)(2,1)S(1)}, bf16[32,3200]{1,0:T(8,128)(2,1)S(1)}, u32[]{:S(2)}, u32[]{:S(2)}) collective-permute-start(bf16[32,3200]{1,0:T(8,128)(2,1)S(1)} %collective-permute-done.44.refs_2_), channel_id=1, source_target_pairs={{0,1},{1,0},{2,3},{3,2},{4,5},{5,4},{6,7},{7,6},{8,9},{9,8},{10,11... | collective-permute-start | bytes 614408 | tf_op jit(solution)/shard_map/ppermute | solution.py:305
  179.6 7.8 %collective-permute-start.49 = (bf16[32,3200]{1,0:T(8,128)(2,1)S(1)}, bf16[32,3200]{1,0:T(8,128)(2,1)S(1)}, u32[]{:S(2)}, u32[]{:S(2)}) collective-permute-start(bf16[32,3200]{1,0:T(8,128)(2,1)S(1)} %collective-permute-done.45.refs_3_), channel_id=1, source_target_pairs={{0,1},{1,0},{2,3},{3,2},{4,5},{5,4},{6,7},{7,6},{8,9},{9,8},{10,11... | collective-permute-start | bytes 614408 | tf_op jit(solution)/shard_map/ppermute | solution.py:305
  181.3 21.4 %collective-permute-start.51 = (bf16[8,12800]{1,0:T(8,128)(2,1)S(1)}, bf16[8,12800]{1,0:T(8,128)(2,1)S(1)}, u32[]{:S(2)}, u32[]{:S(2)}) collective-permute-start(bf16[8,12800]{1,0:T(8,128)(2,1)S(1)} %get-tuple-element.281), channel_id=1, source_target_pairs={{0,4},{1,5},{2,6},{3,7},{4,0},{5,1},{6,2},{7,3},{8,12},{9,13},{10,... | collective-permute-start | bytes 614408 | tf_op jit(solution)/shard_map/ppermute | solution.py:299
  185.7 17.0 %collective-permute-start.52 = (bf16[8,12800]{1,0:T(8,128)(2,1)S(1)}, bf16[8,12800]{1,0:T(8,128)(2,1)S(1)}, u32[]{:S(2)}, u32[]{:S(2)}) collective-permute-start(bf16[8,12800]{1,0:T(8,128)(2,1)S(1)} %get-tuple-element.280), channel_id=1, source_target_pairs={{0,6},{1,7},{2,4},{3,5},{4,2},{5,3},{6,0},{7,1},{8,14},{9,15},{10,... | collective-permute-start | bytes 614408 | tf_op jit(solution)/shard_map/ppermute | solution.py:299
  187.4 15.3 %collective-permute-start.53 = (bf16[8,12800]{1,0:T(8,128)(2,1)S(1)}, bf16[8,12800]{1,0:T(8,128)(2,1)S(1)}, u32[]{:S(2)}, u32[]{:S(2)}) collective-permute-start(bf16[8,12800]{1,0:T(8,128)(2,1)S(1)} %get-tuple-element.279), channel_id=1, source_target_pairs={{0,2},{1,3},{2,0},{3,1},{4,6},{5,7},{6,4},{7,5},{8,10},{9,11},{10,... | collective-permute-start | bytes 614408 | tf_op jit(solution)/shard_map/ppermute | solution.py:299
  202.6 8.7 %collective-permute-start.54 = (bf16[128,3200]{1,0:T(8,128)(2,1)}, bf16[128,3200]{1,0:T(8,128)(2,1)}, u32[]{:S(2)}, u32[]{:S(2)}) collective-permute-start(bf16[128,3200]{1,0:T(8,128)(2,1)} %get-tuple-element.207), channel_id=1, source_target_pairs={{0,1},{1,0},{2,3},{3,2},{4,5},{5,4},{6,7},{7,6},{8,9},{9,8},{10,11... | collective-permute-start | bytes 2457608 | tf_op jit(solution)/shard_map/ppermute | solution.py:312
  203.4 17.7 %collective-permute-start.55 = (bf16[32,3200]{1,0:T(8,128)(2,1)S(1)}, bf16[32,3200]{1,0:T(8,128)(2,1)S(1)}, u32[]{:S(2)}, u32[]{:S(2)}) collective-permute-start(bf16[32,3200]{1,0:T(8,128)(2,1)S(1)} %multiply_convert_fusion.refs_0_), channel_id=1, source_target_pairs={{0,4},{1,5},{2,6},{3,7},{4,0},{5,1},{6,2},{7,3},{8,12},{9,13},{10,... | collective-permute-start | bytes 614408 | tf_op jit(solution)/shard_map/ppermute | solution.py:299
  206.1 15.0 %collective-permute-start.56 = (bf16[32,3200]{1,0:T(8,128)(2,1)S(1)}, bf16[32,3200]{1,0:T(8,128)(2,1)S(1)}, u32[]{:S(2)}, u32[]{:S(2)}) collective-permute-start(bf16[32,3200]{1,0:T(8,128)(2,1)S(1)} %multiply_convert_fusion.refs_0_), channel_id=1, source_target_pairs={{0,6},{1,7},{2,4},{3,5},{4,2},{5,3},{6,0},{7,1},{8,14},{9,15},{10,... | collective-permute-start | bytes 614408 | tf_op jit(solution)/shard_map/ppermute | solution.py:299
  208.0 14.0 %collective-permute-start.57 = (bf16[32,3200]{1,0:T(8,128)(2,1)S(1)}, bf16[32,3200]{1,0:T(8,128)(2,1)S(1)}, u32[]{:S(2)}, u32[]{:S(2)}) collective-permute-start(bf16[32,3200]{1,0:T(8,128)(2,1)S(1)} %multiply_convert_fusion.refs_0_), channel_id=1, source_target_pairs={{0,2},{1,3},{2,0},{3,1},{4,6},{5,7},{6,4},{7,5},{8,10},{9,11},{10,... | collective-permute-start | bytes 614408 | tf_op jit(solution)/shard_map/ppermute | solution.py:299
  209.8 5.3 %collective-permute-start.58 = (bf16[32,1024]{1,0:T(8,128)(2,1)S(1)}, bf16[32,1024]{1,0:T(8,128)(2,1)S(1)}, u32[]{:S(2)}, u32[]{:S(2)}) collective-permute-start(bf16[32,1024]{1,0:T(8,128)(2,1)S(1)} %get-tuple-element.297), channel_id=1, source_target_pairs={{0,8},{8,16},{16,24},{24,0},{1,9},{9,17},{17,25},{25,1},{2,10},{10... | collective-permute-start | bytes 196616 | tf_op jit(solution)/shard_map/ppermute | solution.py:445
  211.3 5.3 %collective-permute-start.59 = (bf16[32,1024]{1,0:T(8,128)(2,1)S(1)}, bf16[32,1024]{1,0:T(8,128)(2,1)S(1)}, u32[]{:S(2)}, u32[]{:S(2)}) collective-permute-start(bf16[32,1024]{1,0:T(8,128)(2,1)S(1)} %get-tuple-element.296), channel_id=1, source_target_pairs={{0,16},{8,24},{16,0},{24,8},{1,17},{9,25},{17,1},{25,9},{2,18},{10... | collective-permute-start | bytes 196616 | tf_op jit(solution)/shard_map/ppermute | solution.py:445
  215.1 4.3 %collective-permute-start.60 = (bf16[32,1024]{1,0:T(8,128)(2,1)S(1)}, bf16[32,1024]{1,0:T(8,128)(2,1)S(1)}, u32[]{:S(2)}, u32[]{:S(2)}) collective-permute-start(bf16[32,1024]{1,0:T(8,128)(2,1)S(1)} %get-tuple-element.295), channel_id=1, source_target_pairs={{0,24},{8,0},{16,8},{24,16},{1,25},{9,1},{17,9},{25,17},{2,26},{10... | collective-permute-start | bytes 196616 | tf_op jit(solution)/shard_map/ppermute | solution.py:445
  222.0 5.3 %collective-permute-start.61 = (bf16[32,3200]{1,0:T(8,128)(2,1)S(1)}, bf16[32,3200]{1,0:T(8,128)(2,1)S(1)}, u32[]{:S(2)}, u32[]{:S(2)}) collective-permute-start(bf16[32,3200]{1,0:T(8,128)(2,1)S(1)} %multiply_convert_fusion.refs_0_), channel_id=1, source_target_pairs={{0,1},{1,0},{2,3},{3,2},{4,5},{5,4},{6,7},{7,6},{8,9},{9,8},{10,11... | collective-permute-start | bytes 614408 | tf_op jit(solution)/shard_map/ppermute | solution.py:305
  222.0 7.0 %collective-permute-start.62 = (bf16[32,3200]{1,0:T(8,128)(2,1)S(1)}, bf16[32,3200]{1,0:T(8,128)(2,1)S(1)}, u32[]{:S(2)}, u32[]{:S(2)}) collective-permute-start(bf16[32,3200]{1,0:T(8,128)(2,1)S(1)} %collective-permute-done.55.refs_1_), channel_id=1, source_target_pairs={{0,1},{1,0},{2,3},{3,2},{4,5},{5,4},{6,7},{7,6},{8,9},{9,8},{10,11... | collective-permute-start | bytes 614408 | tf_op jit(solution)/shard_map/ppermute | solution.py:305
  222.5 6.5 %collective-permute-start.63 = (bf16[32,3200]{1,0:T(8,128)(2,1)S(1)}, bf16[32,3200]{1,0:T(8,128)(2,1)S(1)}, u32[]{:S(2)}, u32[]{:S(2)}) collective-permute-start(bf16[32,3200]{1,0:T(8,128)(2,1)S(1)} %collective-permute-done.56.refs_2_), channel_id=1, source_target_pairs={{0,1},{1,0},{2,3},{3,2},{4,5},{5,4},{6,7},{7,6},{8,9},{9,8},{10,11... | collective-permute-start | bytes 614408 | tf_op jit(solution)/shard_map/ppermute | solution.py:305
  222.5 6.6 %collective-permute-start.64 = (bf16[32,3200]{1,0:T(8,128)(2,1)S(1)}, bf16[32,3200]{1,0:T(8,128)(2,1)S(1)}, u32[]{:S(2)}, u32[]{:S(2)}) collective-permute-start(bf16[32,3200]{1,0:T(8,128)(2,1)S(1)} %collective-permute-done.57.refs_3_), channel_id=1, source_target_pairs={{0,1},{1,0},{2,3},{3,2},{4,5},{5,4},{6,7},{7,6},{8,9},{9,8},{10,11... | collective-permute-start | bytes 614408 | tf_op jit(solution)/shard_map/ppermute | solution.py:305
  223.0 21.3 %collective-permute-start.65 = (bf16[32,3200]{1,0:T(8,128)(2,1)S(1)}, bf16[32,3200]{1,0:T(8,128)(2,1)S(1)}, u32[]{:S(2)}, u32[]{:S(2)}) collective-permute-start(bf16[32,3200]{1,0:T(8,128)(2,1)S(1)} %get-tuple-element.217), channel_id=1, source_target_pairs={{0,4},{1,5},{2,6},{3,7},{4,0},{5,1},{6,2},{7,3},{8,12},{9,13},{10,... | collective-permute-start | bytes 614408 | tf_op jit(solution)/shard_map/ppermute | solution.py:299
  227.4 17.0 %collective-permute-start.66 = (bf16[32,3200]{1,0:T(8,128)(2,1)S(1)}, bf16[32,3200]{1,0:T(8,128)(2,1)S(1)}, u32[]{:S(2)}, u32[]{:S(2)}) collective-permute-start(bf16[32,3200]{1,0:T(8,128)(2,1)S(1)} %get-tuple-element.218), channel_id=1, source_target_pairs={{0,6},{1,7},{2,4},{3,5},{4,2},{5,3},{6,0},{7,1},{8,14},{9,15},{10,... | collective-permute-start | bytes 614408 | tf_op jit(solution)/shard_map/ppermute | solution.py:299
  229.1 15.3 %collective-permute-start.67 = (bf16[32,3200]{1,0:T(8,128)(2,1)S(1)}, bf16[32,3200]{1,0:T(8,128)(2,1)S(1)}, u32[]{:S(2)}, u32[]{:S(2)}) collective-permute-start(bf16[32,3200]{1,0:T(8,128)(2,1)S(1)} %get-tuple-element.219), channel_id=1, source_target_pairs={{0,2},{1,3},{2,0},{3,1},{4,6},{5,7},{6,4},{7,5},{8,10},{9,11},{10,... | collective-permute-start | bytes 614408 | tf_op jit(solution)/shard_map/ppermute | solution.py:299
  247.1 17.7 %collective-permute-start.69 = (bf16[32,3200]{1,0:T(8,128)(2,1)S(1)}, bf16[32,3200]{1,0:T(8,128)(2,1)S(1)}, u32[]{:S(2)}, u32[]{:S(2)}) collective-permute-start(bf16[32,3200]{1,0:T(8,128)(2,1)S(1)} %get-tuple-element.275), channel_id=1, source_target_pairs={{0,4},{1,5},{2,6},{3,7},{4,0},{5,1},{6,2},{7,3},{8,12},{9,13},{10,... | collective-permute-start | bytes 614408 | tf_op jit(solution)/shard_map/ppermute | solution.py:299
  249.8 15.0 %collective-permute-start.70 = (bf16[32,3200]{1,0:T(8,128)(2,1)S(1)}, bf16[32,3200]{1,0:T(8,128)(2,1)S(1)}, u32[]{:S(2)}, u32[]{:S(2)}) collective-permute-start(bf16[32,3200]{1,0:T(8,128)(2,1)S(1)} %get-tuple-element.274), channel_id=1, source_target_pairs={{0,6},{1,7},{2,4},{3,5},{4,2},{5,3},{6,0},{7,1},{8,14},{9,15},{10,... | collective-permute-start | bytes 614408 | tf_op jit(solution)/shard_map/ppermute | solution.py:299
  251.5 13.8 %collective-permute-start.71 = (bf16[32,3200]{1,0:T(8,128)(2,1)S(1)}, bf16[32,3200]{1,0:T(8,128)(2,1)S(1)}, u32[]{:S(2)}, u32[]{:S(2)}) collective-permute-start(bf16[32,3200]{1,0:T(8,128)(2,1)S(1)} %get-tuple-element.273), channel_id=1, source_target_pairs={{0,2},{1,3},{2,0},{3,1},{4,6},{5,7},{6,4},{7,5},{8,10},{9,11},{10,... | collective-permute-start | bytes 614408 | tf_op jit(solution)/shard_map/ppermute | solution.py:299
  (41 other events, 210.5 us)

commit v14 on v13

--- a/solution.py
+++ b/solution.py
@@ -225,7 +225,7 @@
             pltpu.SemaphoreType.DMA((blocks,)),
             pltpu.SemaphoreType.DMA((blocks,)),
         ],
-        compiler_params=settings(53),
+        compiler_params=settings(56),
         cost_estimate=pl.CostEstimate(
             flops=4 * rows * width * units,
             bytes_accessed=4 * width * units + 4 * rows * (width + units),

time: 269 us -> 269 us (level)
  local copies, waits for them, and re-layouts: 14.9 us -> 11.8 us
  waiting for transfers between devices: 51.9 us -> 54.6 us
  transfers between devices with their start and end apart: 72 -> 72, of which waited for: 22 -> 24; matrix products, arithmetic and copies ran while one was open for 8% -> 7% of each run, Pallas kernels for 37% -> 37%
where the time goes in v14:
time: 269 us; the launch traced here: 268 us
  Pallas kernels  102 us (38%)
  starting transfers between devices  83.6 us (31%)
  waiting for transfers between devices  54.6 us (20%)
  other arithmetic  12.2 us (5%)
  local copies, waits for them, and re-layouts  11.8 us (4%)
    ppermute x36, starting transfers between devices, shift(): return lax.ppermute(block, 'tp', pairs)  67 us
    pallas_call x4, Pallas kernels, vision_pass(): pl.pallas_call(functools.partial(vision_kernel, len(pieces), slope is Non...  58.6 us
    ppermute x36, waiting for transfers between devices, shift(): return lax.ppermute(block, 'tp', pairs)  41.3 us
    pallas_call x2, Pallas kernels, project_back(): pl.pallas_call(project_back_kernel, in_specs=whole_blocks(1) + [pl.BlockS...  22 us
    pallas_call x2, Pallas kernels, project(): pl.pallas_call(functools.partial(project_kernel, len(pieces)), in_specs=w...  19.4 us
    ppermute x24, starting transfers between devices, gathered(): other = [lax.ppermute(m, 'tp', self.pairs) for m in mine]  6.39 us
    another operation x7, other arithmetic  6.28 us
    ppermute x3, starting transfers between devices, per_device(): picked[s] = lax.ppermute(picked[s], 'grp', pairs)  5.42 us
  transfers between devices with their start and end apart: 72, of which 24 were waited for; matrix products, arithmetic and copies ran while one was open for 7% of the time, Pallas kernels for 37%

profile of v14, /device:TPU:0, one launch (start us, length us, event | category | flops | bytes accessed | tf_op | source)
XLA Modules:
  0.0 268.2 jit_solution(17380801881517061370)
XLA Ops:
  0.7 2.2 shard_map.131
  2.9 4.0 %collective-permute-start = (bf16[32,3200]{1,0:T(8,128)(2,1)}, bf16[32,3200]{1,0:T(8,128)(2,1)S(1)}, u32[]{:S(2)}, u32[]{:S(2)}) collective-permute-start(bf16[32,3200]{1,0:T(8,128)(2,1)} %get-tuple-element.123.refs_0_), channel_id=1, source_target_pairs={{0,4},{1,5},{2,6},{3,7},{4,0},{5,1},{6,2},{7,3},{8,12},{9,13},{10,... | collective-permute-start | bytes 614408 | tf_op jit(solution)/shard_map/ppermute | solution.py:299
  6.9 1.3 collective-permute-start.1
  8.5 0.8 reshape.424
  10.3 0.9 gather_fusion
  11.2 2.5 collective-permute-start.3
  14.2 1.4 collective-permute-done.3
  15.6 2.4 collective-permute-start.5
  18.0 3.2 %collective-permute-done.5 = bf16[32,1024]{1,0:T(8,128)(2,1)S(1)} collective-permute-done((bf16[32,1024]{1,0:T(8,128)(2,1)S(1)}, bf16[32,1024]{1,0:T(8,128)(2,1)S(1)}, u32[]{:S(2)}, u32[]{:S(2)}) %collective-permute-start.5) | collective-permute-done | bytes 65568 | tf_op jit(solution)/shard_map/ppermute | solution.py:376
  23.5 5.7 %collective-permute-start.10 = (bf16[32,3200]{1,0:T(8,128)(2,1)S(1)}, bf16[32,3200]{1,0:T(8,128)(2,1)S(1)}, u32[]{:S(2)}, u32[]{:S(2)}) collective-permute-start(bf16[32,3200]{1,0:T(8,128)(2,1)S(1)} %copy-done.13), channel_id=1, source_target_pairs={{0,4},{1,5},{2,6},{3,7},{4,0},{5,1},{6,2},{7,3},{8,12},{9,13},{10,... | collective-permute-start | bytes 614408 | tf_op jit(solution)/shard_map/ppermute | solution.py:299
  30.9 14.8 %shard_map.132 = (bf16[128,3200]{1,0:T(8,128)(2,1)}, bf16[128,3200]{1,0:T(8,128)(2,1)}, f32[7,256,256]{2,1,0:T(8,128)}) custom-call(bf16[32,3200]{1,0:T(8,128)(2,1)} %get-tuple-element.123.refs_0_, bf16[32,3200]{1,0:T(8,128)(2,1)} %copy-done.15, bf16[32,3200]{1,0:T(8,128)(2,1)} %collective-permute-done.1.refs_2_, ...), custom_call_target="tpu_custom_call" | custom-call | flops 5242880000 | bytes 25395200 | tf_op jit(solution)/shard_map/pallas_call | solution.py:212
  47.3 1.1 collective-permute-done.17
  48.4 1.3 fusion.52
  49.8 3.5 %collective-permute-start.18 = (bf16[32,3200]{1,0:T(8,128)(2,1)S(1)}, bf16[32,3200]{1,0:T(8,128)(2,1)S(1)}, u32[]{:S(2)}, u32[]{:S(2)}) collective-permute-start(bf16[32,3200]{1,0:T(8,128)(2,1)S(1)} %get-tuple-element.290), channel_id=1, source_target_pairs={{0,4},{1,5},{2,6},{3,7},{4,0},{5,1},{6,2},{7,3},{8,12},{9,13},{10,... | collective-permute-start | bytes 614408 | tf_op jit(solution)/shard_map/ppermute | solution.py:299
  53.3 1.5 collective-permute-start.19
  56.3 14.7 %shard_map.133 = (bf16[128,3200]{1,0:T(8,128)(2,1)}, bf16[128,3200]{1,0:T(8,128)(2,1)}, f32[7,256,256]{2,1,0:T(8,128)}) custom-call(bf16[32,3200]{1,0:T(8,128)(2,1)} %get-tuple-element.130.refs_0_, bf16[32,3200]{1,0:T(8,128)(2,1)} %copy-done.17, bf16[32,3200]{1,0:T(8,128)(2,1)} %copy-done.18, bf16[32,3200]{1,0:T(8,128)(2,1)} %copy-done.19, ...), custom_call_target="tpu_custom_call" | custom-call | flops 5242880000 | bytes 25395200 | tf_op jit(solution)/shard_map/pallas_call | solution.py:212
  72.6 2.9 %collective-permute-start.21 = (bf16[8,12800]{1,0:T(8,128)(2,1)S(1)}, bf16[8,12800]{1,0:T(8,128)(2,1)S(1)}, u32[]{:S(2)}, u32[]{:S(2)}) collective-permute-start(bf16[8,12800]{1,0:T(8,128)(2,1)S(1)} %multiply_convert_fusion.5.refs_0_), channel_id=1, source_target_pairs={{0,4},{1,5},{2,6},{3,7},{4,0},{5,1},{6,2},{7,3},{8,12},{9,13},{10,... | collective-permute-start | bytes 614408 | tf_op jit(solution)/shard_map/ppermute | solution.py:299
  75.5 1.5 collective-permute-start.22
  77.0 1.6 fusion.53
  80.4 2.1 collective-permute-start.25
  82.5 7.8 %collective-permute-done.21.refs_1_ = bf16[8,12800]{1,0:T(8,128)(2,1)S(1)} collective-permute-done((bf16[8,12800]{1,0:T(8,128)(2,1)S(1)}, bf16[8,12800]{1,0:T(8,128)(2,1)S(1)}, u32[]{:S(2)}, u32[]{:S(2)}) %collective-permute-start.21) | collective-permute-done | bytes 204832 | tf_op jit(solution)/shard_map/ppermute | solution.py:299
  90.4 2.1 collective-permute-done.23.refs_3_
  92.4 3.3 %collective-permute-done.25 = bf16[32,3200]{1,0:T(8,128)(2,1)S(1)} collective-permute-done((bf16[32,3200]{1,0:T(8,128)(2,1)S(1)}, bf16[32,3200]{1,0:T(8,128)(2,1)S(1)}, u32[]{:S(2)}, u32[]{:S(2)}) %collective-permute-start.25) | collective-permute-done | bytes 204832 | tf_op jit(solution)/shard_map/ppermute | solution.py:299
  97.3 2.4 collective-permute-start.31
  99.7 9.6 %shard_map.134 = (bf16[64,1024]{1,0:T(8,128)(2,1)S(1)}, bf16[64,1024]{1,0:T(8,128)(2,1)S(1)}) custom-call(bf16[8,12800]{1,0:T(8,128)(2,1)S(1)} %multiply_convert_fusion.5.refs_0_, bf16[8,12800]{1,0:T(8,128)(2,1)S(1)} %collective-permute-done.21.refs_1_, bf16[8,12800]{1,0:T(8,128)(2,1)S(1)} %collective-permute-done.22.refs_2_, ...), custom_call_target="tpu_custom_call" | custom-call | flops 1677721600 | bytes 29753344 | tf_op jit(solution)/shard_map/pallas_call | solution.py:249
  109.3 4.2 %collective-permute-done.30 = bf16[32,3200]{1,0:T(8,128)(2,1)S(1)} collective-permute-done((bf16[32,3200]{1,0:T(8,128)(2,1)S(1)}, bf16[32,3200]{1,0:T(8,128)(2,1)S(1)}, u32[]{:S(2)}, u32[]{:S(2)}) %collective-permute-start.30) | collective-permute-done | bytes 204832 | tf_op jit(solution)/shard_map/ppermute | solution.py:299
  114.7 4.9 %collective-permute-start.32 = (bf16[8,12800]{1,0:T(8,128)(2,1)S(1)}, bf16[8,12800]{1,0:T(8,128)(2,1)S(1)}, u32[]{:S(2)}, u32[]{:S(2)}) collective-permute-start(bf16[8,12800]{1,0:T(8,128)(2,1)S(1)} %multiply_convert_fusion.4.refs_0_), channel_id=1, source_target_pairs={{0,4},{1,5},{2,6},{3,7},{4,0},{5,1},{6,2},{7,3},{8,12},{9,13},{10,... | collective-permute-start | bytes 614408 | tf_op jit(solution)/shard_map/ppermute | solution.py:299
  119.7 2.4 collective-permute-start.33
  122.0 11.0 %shard_map.135 = (bf16[32,12800]{1,0:T(8,128)(2,1)S(1)}, bf16[32,12800]{1,0:T(8,128)(2,1)S(1)}) custom-call(bf16[64,1024]{1,0:T(8,128)(2,1)S(1)} %get-tuple-element.169.delta, bf16[12800,1024]{1,0:T(8,128)(2,1)} %weight.3), custom_call_target="tpu_custom_call" | custom-call | flops 1677721600 | bytes 29753344 | tf_op jit(solution)/shard_map/pallas_call | solution.py:269
  133.0 1.3 collective-permute-done.32.refs_1_
  134.4 0.7 collective-permute-done.34.refs_3_
  136.1 1.3 collective-permute-done.39
  137.6 4.6 %collective-permute-start.40 = (bf16[8,12800]{1,0:T(8,128)(2,1)S(1)}, bf16[8,12800]{1,0:T(8,128)(2,1)S(1)}, u32[]{:S(2)}, u32[]{:S(2)}) collective-permute-start(bf16[8,12800]{1,0:T(8,128)(2,1)S(1)} %get-tuple-element.284), channel_id=1, source_target_pairs={{0,4},{1,5},{2,6},{3,7},{4,0},{5,1},{6,2},{7,3},{8,12},{9,13},{10,... | collective-permute-start | bytes 614408 | tf_op jit(solution)/shard_map/ppermute | solution.py:299
  142.2 1.5 collective-permute-start.41
  143.7 9.8 %shard_map.136 = (bf16[64,1024]{1,0:T(8,128)(2,1)S(1)}, bf16[64,1024]{1,0:T(8,128)(2,1)S(1)}) custom-call(bf16[8,12800]{1,0:T(8,128)(2,1)S(1)} %multiply_convert_fusion.4.refs_0_, bf16[8,12800]{1,0:T(8,128)(2,1)S(1)} %collective-permute-done.32.refs_1_, bf16[8,12800]{1,0:T(8,128)(2,1)S(1)} %collective-permute-done.33.refs_2_, ...), custom_call_target="tpu_custom_call" | custom-call | flops 1677721600 | bytes 29753344 | tf_op jit(solution)/shard_map/pallas_call | solution.py:249
  153.6 3.3 %collective-permute-done.40 = bf16[8,12800]{1,0:T(8,128)(2,1)S(1)} collective-permute-done((bf16[8,12800]{1,0:T(8,128)(2,1)S(1)}, bf16[8,12800]{1,0:T(8,128)(2,1)S(1)}, u32[]{:S(2)}, u32[]{:S(2)}) %collective-permute-start.40) | collective-permute-done | bytes 204832 | tf_op jit(solution)/shard_map/ppermute | solution.py:299
  156.9 0.8 collective-permute-done.42
  158.5 3.7 %collective-permute-start.43 = (bf16[32,3200]{1,0:T(8,128)(2,1)S(1)}, bf16[32,3200]{1,0:T(8,128)(2,1)}, u32[]{:S(2)}, u32[]{:S(2)}) collective-permute-start(bf16[32,3200]{1,0:T(8,128)(2,1)S(1)} %multiply_convert_fusion.2.refs_0_), channel_id=1, source_target_pairs={{0,4},{1,5},{2,6},{3,7},{4,0},{5,1},{6,2},{7,3},{8,12},{9,13},{10,... | collective-permute-start | bytes 614408 | tf_op jit(solution)/shard_map/ppermute | solution.py:299
  162.2 2.4 collective-permute-start.44
  164.5 11.0 %shard_map.137 = (bf16[32,12800]{1,0:T(8,128)(2,1)S(1)}, bf16[32,12800]{1,0:T(8,128)(2,1)S(1)}) custom-call(bf16[64,1024]{1,0:T(8,128)(2,1)S(1)} %get-tuple-element.186.delta, bf16[12800,1024]{1,0:T(8,128)(2,1)} %weight.3), custom_call_target="tpu_custom_call" | custom-call | flops 1677721600 | bytes 29753344 | tf_op jit(solution)/shard_map/pallas_call | solution.py:269
  175.6 1.5 collective-permute-done.43.refs_1_
  179.7 1.3 fusion.55
  181.1 4.6 %collective-permute-start.51 = (bf16[8,12800]{1,0:T(8,128)(2,1)S(1)}, bf16[8,12800]{1,0:T(8,128)(2,1)S(1)}, u32[]{:S(2)}, u32[]{:S(2)}) collective-permute-start(bf16[8,12800]{1,0:T(8,128)(2,1)S(1)} %get-tuple-element.281), channel_id=1, source_target_pairs={{0,4},{1,5},{2,6},{3,7},{4,0},{5,1},{6,2},{7,3},{8,12},{9,13},{10,... | collective-permute-start | bytes 614408 | tf_op jit(solution)/shard_map/ppermute | solution.py:299
  185.7 1.5 collective-permute-start.52
  188.1 14.6 %shard_map.138 = (bf16[128,3200]{1,0:T(8,128)(2,1)}, bf16[128,3200]{1,0:T(8,128)(2,1)}) custom-call(bf16[32,3200]{1,0:T(8,128)(2,1)} %copy-done.11, bf16[32,3200]{1,0:T(8,128)(2,1)} %collective-permute-done.43.refs_1_, bf16[32,3200]{1,0:T(8,128)(2,1)} %collective-permute-done.44.refs_2_, bf16[32,3200]{1,0:T(8,128)(2,1)} %collective-permute-done.45.refs_3_, ...), custom_call_target="tpu_custom_call" | custom-call | flops 5242880000 | bytes 25395200 | tf_op jit(solution)/shard_map/pallas_call | solution.py:212
  203.5 2.9 %collective-permute-start.55 = (bf16[32,3200]{1,0:T(8,128)(2,1)S(1)}, bf16[32,3200]{1,0:T(8,128)(2,1)S(1)}, u32[]{:S(2)}, u32[]{:S(2)}) collective-permute-start(bf16[32,3200]{1,0:T(8,128)(2,1)S(1)} %multiply_convert_fusion.refs_0_), channel_id=1, source_target_pairs={{0,4},{1,5},{2,6},{3,7},{4,0},{5,1},{6,2},{7,3},{8,12},{9,13},{10,... | collective-permute-start | bytes 614408 | tf_op jit(solution)/shard_map/ppermute | solution.py:299
  206.4 1.7 collective-permute-start.56
  209.8 1.5 collective-permute-start.58
  211.3 1.5 collective-permute-start.59
  212.9 1.3 fusion.56
  214.2 0.9 collective-permute-done.58
  215.1 1.4 collective-permute-start.60
  216.7 2.7 %collective-permute-done.60 = bf16[32,1024]{1,0:T(8,128)(2,1)S(1)} collective-permute-done((bf16[32,1024]{1,0:T(8,128)(2,1)S(1)}, bf16[32,1024]{1,0:T(8,128)(2,1)S(1)}, u32[]{:S(2)}, u32[]{:S(2)}) %collective-permute-start.60) | collective-permute-done | bytes 65568 | tf_op jit(solution)/shard_map/ppermute | solution.py:445
  219.4 1.8 collective-permute-done.55.refs_1_
  221.2 1.1 collective-permute-done.57.refs_3_
  223.4 4.3 %collective-permute-start.65 = (bf16[32,3200]{1,0:T(8,128)(2,1)S(1)}, bf16[32,3200]{1,0:T(8,128)(2,1)S(1)}, u32[]{:S(2)}, u32[]{:S(2)}) collective-permute-start(bf16[32,3200]{1,0:T(8,128)(2,1)S(1)} %get-tuple-element.217), channel_id=1, source_target_pairs={{0,4},{1,5},{2,6},{3,7},{4,0},{5,1},{6,2},{7,3},{8,12},{9,13},{10,... | collective-permute-start | bytes 614408 | tf_op jit(solution)/shard_map/ppermute | solution.py:299
  227.7 1.7 collective-permute-start.66
  230.2 14.6 %shard_map.139 = (bf16[128,3200]{1,0:T(8,128)(2,1)}, bf16[128,3200]{1,0:T(8,128)(2,1)}) custom-call(bf16[32,3200]{1,0:T(8,128)(2,1)} %copy-done.10, bf16[32,3200]{1,0:T(8,128)(2,1)} %copy-done.16, bf16[32,3200]{1,0:T(8,128)(2,1)} %collective-permute-done.56.refs_2_, bf16[32,3200]{1,0:T(8,128)(2,1)} %collective-permute-done.57.refs_3_, ...), custom_call_target="tpu_custom_call" | custom-call | flops 5242880000 | bytes 25395200 | tf_op jit(solution)/shard_map/pallas_call | solution.py:212
  245.1 2.4 collective-permute-done.68
  247.7 2.7 %collective-permute-start.69 = (bf16[32,3200]{1,0:T(8,128)(2,1)S(1)}, bf16[32,3200]{1,0:T(8,128)(2,1)S(1)}, u32[]{:S(2)}, u32[]{:S(2)}) collective-permute-start(bf16[32,3200]{1,0:T(8,128)(2,1)S(1)} %get-tuple-element.275), channel_id=1, source_target_pairs={{0,4},{1,5},{2,6},{3,7},{4,0},{5,1},{6,2},{7,3},{8,12},{9,13},{10,... | collective-permute-start | bytes 614408 | tf_op jit(solution)/shard_map/ppermute | solution.py:299
  250.4 1.7 collective-permute-start.70
  252.1 2.2 fusion
  254.3 11.1 %collective-permute-done.69 = bf16[32,3200]{1,0:T(8,128)(2,1)S(1)} collective-permute-done((bf16[32,3200]{1,0:T(8,128)(2,1)S(1)}, bf16[32,3200]{1,0:T(8,128)(2,1)S(1)}, u32[]{:S(2)}, u32[]{:S(2)}) %collective-permute-start.69) | collective-permute-done | bytes 204832 | tf_op jit(solution)/shard_map/ppermute | solution.py:299
  266.8 0.8 pad_maximum_fusion
  (271 shorter events, 27.2 us)
Async XLA Ops:
  2.9 19.0 %collective-permute-start = (bf16[32,3200]{1,0:T(8,128)(2,1)}, bf16[32,3200]{1,0:T(8,128)(2,1)S(1)}, u32[]{:S(2)}, u32[]{:S(2)}) collective-permute-start(bf16[32,3200]{1,0:T(8,128)(2,1)} %get-tuple-element.123.refs_0_), channel_id=1, source_target_pairs={{0,4},{1,5},{2,6},{3,7},{4,0},{5,1},{6,2},{7,3},{8,12},{9,13},{10,... | collective-permute-start | bytes 614408 | tf_op jit(solution)/shard_map/ppermute | solution.py:299
  6.9 15.0 %collective-permute-start.1 = (bf16[32,3200]{1,0:T(8,128)(2,1)}, bf16[32,3200]{1,0:T(8,128)(2,1)}, u32[]{:S(2)}, u32[]{:S(2)}) collective-permute-start(bf16[32,3200]{1,0:T(8,128)(2,1)} %get-tuple-element.123.refs_0_), channel_id=1, source_target_pairs={{0,6},{1,7},{2,4},{3,5},{4,2},{5,3},{6,0},{7,1},{8,14},{9,15},{10,... | collective-permute-start | bytes 614408 | tf_op jit(solution)/shard_map/ppermute | solution.py:299
  8.2 14.3 %collective-permute-start.2 = (bf16[32,3200]{1,0:T(8,128)(2,1)}, bf16[32,3200]{1,0:T(8,128)(2,1)}, u32[]{:S(2)}, u32[]{:S(2)}) collective-permute-start(bf16[32,3200]{1,0:T(8,128)(2,1)} %get-tuple-element.123.refs_0_), channel_id=1, source_target_pairs={{0,2},{1,3},{2,0},{3,1},{4,6},{5,7},{6,4},{7,5},{8,10},{9,11},{10,... | collective-permute-start | bytes 614408 | tf_op jit(solution)/shard_map/ppermute | solution.py:299
  11.2 4.4 %collective-permute-start.3 = (bf16[32,1024]{1,0:T(8,128)(2,1)S(1)}, bf16[32,1024]{1,0:T(8,128)(2,1)S(1)}, u32[]{:S(2)}, u32[]{:S(2)}) collective-permute-start(bf16[32,1024]{1,0:T(8,128)(2,1)S(1)} %get-tuple-element.303), channel_id=1, source_target_pairs={{0,24},{8,0},{16,8},{24,16},{1,25},{9,1},{17,9},{25,17},{2,26},{10... | collective-permute-start | bytes 196616 | tf_op jit(solution)/shard_map/ppermute | solution.py:376
  13.7 4.3 %collective-permute-start.4 = (bf16[32,1024]{1,0:T(8,128)(2,1)S(1)}, bf16[32,1024]{1,0:T(8,128)(2,1)S(1)}, u32[]{:S(2)}, u32[]{:S(2)}) collective-permute-start(bf16[32,1024]{1,0:T(8,128)(2,1)S(1)} %get-tuple-element.302), channel_id=1, source_target_pairs={{0,16},{8,24},{16,0},{24,8},{1,17},{9,25},{17,1},{25,9},{2,18},{10... | collective-permute-start | bytes 196616 | tf_op jit(solution)/shard_map/ppermute | solution.py:376
  15.6 5.6 %collective-permute-start.5 = (bf16[32,1024]{1,0:T(8,128)(2,1)S(1)}, bf16[32,1024]{1,0:T(8,128)(2,1)S(1)}, u32[]{:S(2)}, u32[]{:S(2)}) collective-permute-start(bf16[32,1024]{1,0:T(8,128)(2,1)S(1)} %get-tuple-element.301), channel_id=1, source_target_pairs={{0,8},{8,16},{16,24},{24,0},{1,9},{9,17},{17,25},{25,1},{2,10},{10... | collective-permute-start | bytes 196616 | tf_op jit(solution)/shard_map/ppermute | solution.py:376
  22.5 6.7 %collective-permute-start.6 = (bf16[32,3200]{1,0:T(8,128)(2,1)S(1)}, bf16[32,3200]{1,0:T(8,128)(2,1)S(1)}, u32[]{:S(2)}, u32[]{:S(2)}) collective-permute-start(bf16[32,3200]{1,0:T(8,128)(2,1)S(1)} %copy-done.14), channel_id=1, source_target_pairs={{0,1},{1,0},{2,3},{3,2},{4,5},{5,4},{6,7},{7,6},{8,9},{9,8},{10,11... | collective-permute-start | bytes 614408 | tf_op jit(solution)/shard_map/ppermute | solution.py:305
  22.5 7.2 %collective-permute-start.7 = (bf16[32,3200]{1,0:T(8,128)(2,1)S(1)}, bf16[32,3200]{1,0:T(8,128)(2,1)S(1)}, u32[]{:S(2)}, u32[]{:S(2)}) collective-permute-start(bf16[32,3200]{1,0:T(8,128)(2,1)S(1)} %collective-permute-done.refs_1_), channel_id=1, source_target_pairs={{0,1},{1,0},{2,3},{3,2},{4,5},{5,4},{6,7},{7,6},{8,9},{9,8},{10,11... | collective-permute-start | bytes 614408 | tf_op jit(solution)/shard_map/ppermute | solution.py:305
  23.0 7.2 %collective-permute-start.8 = (bf16[32,3200]{1,0:T(8,128)(2,1)}, bf16[32,3200]{1,0:T(8,128)(2,1)S(1)}, u32[]{:S(2)}, u32[]{:S(2)}) collective-permute-start(bf16[32,3200]{1,0:T(8,128)(2,1)} %collective-permute-done.1.refs_2_), channel_id=1, source_target_pairs={{0,1},{1,0},{2,3},{3,2},{4,5},{5,4},{6,7},{7,6},{8,9},{9,8},{10,11... | collective-permute-start | bytes 614408 | tf_op jit(solution)/shard_map/ppermute | solution.py:305
  23.0 7.2 %collective-permute-start.9 = (bf16[32,3200]{1,0:T(8,128)(2,1)}, bf16[32,3200]{1,0:T(8,128)(2,1)S(1)}, u32[]{:S(2)}, u32[]{:S(2)}) collective-permute-start(bf16[32,3200]{1,0:T(8,128)(2,1)} %collective-permute-done.2.refs_3_), channel_id=1, source_target_pairs={{0,1},{1,0},{2,3},{3,2},{4,5},{5,4},{6,7},{7,6},{8,9},{9,8},{10,11... | collective-permute-start | bytes 614408 | tf_op jit(solution)/shard_map/ppermute | solution.py:305
  23.5 22.2 %collective-permute-start.10 = (bf16[32,3200]{1,0:T(8,128)(2,1)S(1)}, bf16[32,3200]{1,0:T(8,128)(2,1)S(1)}, u32[]{:S(2)}, u32[]{:S(2)}) collective-permute-start(bf16[32,3200]{1,0:T(8,128)(2,1)S(1)} %copy-done.13), channel_id=1, source_target_pairs={{0,4},{1,5},{2,6},{3,7},{4,0},{5,1},{6,2},{7,3},{8,12},{9,13},{10,... | collective-permute-start | bytes 614408 | tf_op jit(solution)/shard_map/ppermute | solution.py:299
  29.3 16.5 %collective-permute-start.11 = (bf16[32,3200]{1,0:T(8,128)(2,1)S(1)}, bf16[32,3200]{1,0:T(8,128)(2,1)S(1)}, u32[]{:S(2)}, u32[]{:S(2)}) collective-permute-start(bf16[32,3200]{1,0:T(8,128)(2,1)S(1)} %copy-done.13), channel_id=1, source_target_pairs={{0,6},{1,7},{2,4},{3,5},{4,2},{5,3},{6,0},{7,1},{8,14},{9,15},{10,... | collective-permute-start | bytes 614408 | tf_op jit(solution)/shard_map/ppermute | solution.py:299
  29.7 16.0 %collective-permute-start.12 = (bf16[32,3200]{1,0:T(8,128)(2,1)S(1)}, bf16[32,3200]{1,0:T(8,128)(2,1)S(1)}, u32[]{:S(2)}, u32[]{:S(2)}) collective-permute-start(bf16[32,3200]{1,0:T(8,128)(2,1)S(1)} %copy-done.13), channel_id=1, source_target_pairs={{0,2},{1,3},{2,0},{3,1},{4,6},{5,7},{6,4},{7,5},{8,10},{9,11},{10,... | collective-permute-start | bytes 614408 | tf_op jit(solution)/shard_map/ppermute | solution.py:299
  46.1 7.2 %collective-permute-start.13 = (bf16[32,3200]{1,0:T(8,128)(2,1)S(1)}, bf16[32,3200]{1,0:T(8,128)(2,1)S(1)}, u32[]{:S(2)}, u32[]{:S(2)}) collective-permute-start(bf16[32,3200]{1,0:T(8,128)(2,1)S(1)} %copy-done.13), channel_id=1, source_target_pairs={{0,1},{1,0},{2,3},{3,2},{4,5},{5,4},{6,7},{7,6},{8,9},{9,8},{10,11... | collective-permute-start | bytes 614408 | tf_op jit(solution)/shard_map/ppermute | solution.py:305
  46.7 8.1 %collective-permute-start.14 = (bf16[32,3200]{1,0:T(8,128)(2,1)S(1)}, bf16[32,3200]{1,0:T(8,128)(2,1)S(1)}, u32[]{:S(2)}, u32[]{:S(2)}) collective-permute-start(bf16[32,3200]{1,0:T(8,128)(2,1)S(1)} %collective-permute-done.10.refs_1_), channel_id=1, source_target_pairs={{0,1},{1,0},{2,3},{3,2},{4,5},{5,4},{6,7},{7,6},{8,9},{9,8},{10,11... | collective-permute-start | bytes 614408 | tf_op jit(solution)/shard_map/ppermute | solution.py:305
  46.8 8.0 %collective-permute-start.15 = (bf16[32,3200]{1,0:T(8,128)(2,1)S(1)}, bf16[32,3200]{1,0:T(8,128)(2,1)S(1)}, u32[]{:S(2)}, u32[]{:S(2)}) collective-permute-start(bf16[32,3200]{1,0:T(8,128)(2,1)S(1)} %collective-permute-done.11.refs_2_), channel_id=1, source_target_pairs={{0,1},{1,0},{2,3},{3,2},{4,5},{5,4},{6,7},{7,6},{8,9},{9,8},{10,11... | collective-permute-start | bytes 614408 | tf_op jit(solution)/shard_map/ppermute | solution.py:305
  47.2 7.6 %collective-permute-start.16 = (bf16[32,3200]{1,0:T(8,128)(2,1)S(1)}, bf16[32,3200]{1,0:T(8,128)(2,1)S(1)}, u32[]{:S(2)}, u32[]{:S(2)}) collective-permute-start(bf16[32,3200]{1,0:T(8,128)(2,1)S(1)} %collective-permute-done.12.refs_3_), channel_id=1, source_target_pairs={{0,1},{1,0},{2,3},{3,2},{4,5},{5,4},{6,7},{7,6},{8,9},{9,8},{10,11... | collective-permute-start | bytes 614408 | tf_op jit(solution)/shard_map/ppermute | solution.py:305
  49.8 21.4 %collective-permute-start.18 = (bf16[32,3200]{1,0:T(8,128)(2,1)S(1)}, bf16[32,3200]{1,0:T(8,128)(2,1)S(1)}, u32[]{:S(2)}, u32[]{:S(2)}) collective-permute-start(bf16[32,3200]{1,0:T(8,128)(2,1)S(1)} %get-tuple-element.290), channel_id=1, source_target_pairs={{0,4},{1,5},{2,6},{3,7},{4,0},{5,1},{6,2},{7,3},{8,12},{9,13},{10,... | collective-permute-start | bytes 614408 | tf_op jit(solution)/shard_map/ppermute | solution.py:299
  53.3 17.8 %collective-permute-start.19 = (bf16[32,3200]{1,0:T(8,128)(2,1)S(1)}, bf16[32,3200]{1,0:T(8,128)(2,1)S(1)}, u32[]{:S(2)}, u32[]{:S(2)}) collective-permute-start(bf16[32,3200]{1,0:T(8,128)(2,1)S(1)} %get-tuple-element.289), channel_id=1, source_target_pairs={{0,6},{1,7},{2,4},{3,5},{4,2},{5,3},{6,0},{7,1},{8,14},{9,15},{10,... | collective-permute-start | bytes 614408 | tf_op jit(solution)/shard_map/ppermute | solution.py:299
  54.8 16.4 %collective-permute-start.20 = (bf16[32,3200]{1,0:T(8,128)(2,1)S(1)}, bf16[32,3200]{1,0:T(8,128)(2,1)S(1)}, u32[]{:S(2)}, u32[]{:S(2)}) collective-permute-start(bf16[32,3200]{1,0:T(8,128)(2,1)S(1)} %get-tuple-element.288), channel_id=1, source_target_pairs={{0,2},{1,3},{2,0},{3,1},{4,6},{5,7},{6,4},{7,5},{8,10},{9,11},{10,... | collective-permute-start | bytes 614408 | tf_op jit(solution)/shard_map/ppermute | solution.py:299
  71.0 6.0 %collective-permute-start.24 = (bf16[128,3200]{1,0:T(8,128)(2,1)}, bf16[128,3200]{1,0:T(8,128)(2,1)}, u32[]{:S(2)}, u32[]{:S(2)}) collective-permute-start(bf16[128,3200]{1,0:T(8,128)(2,1)} %get-tuple-element.147), channel_id=1, source_target_pairs={{0,1},{1,0},{2,3},{3,2},{4,5},{5,4},{6,7},{7,6},{8,9},{9,8},{10,11... | collective-permute-start | bytes 2457608 | tf_op jit(solution)/shard_map/ppermute | solution.py:312
  72.6 17.7 %collective-permute-start.21 = (bf16[8,12800]{1,0:T(8,128)(2,1)S(1)}, bf16[8,12800]{1,0:T(8,128)(2,1)S(1)}, u32[]{:S(2)}, u32[]{:S(2)}) collective-permute-start(bf16[8,12800]{1,0:T(8,128)(2,1)S(1)} %multiply_convert_fusion.5.refs_0_), channel_id=1, source_target_pairs={{0,4},{1,5},{2,6},{3,7},{4,0},{5,1},{6,2},{7,3},{8,12},{9,13},{10,... | collective-permute-start | bytes 614408 | tf_op jit(solution)/shard_map/ppermute | solution.py:299
  75.5 14.9 %collective-permute-start.22 = (bf16[8,12800]{1,0:T(8,128)(2,1)S(1)}, bf16[8,12800]{1,0:T(8,128)(2,1)S(1)}, u32[]{:S(2)}, u32[]{:S(2)}) collective-permute-start(bf16[8,12800]{1,0:T(8,128)(2,1)S(1)} %multiply_convert_fusion.5.refs_0_), channel_id=1, source_target_pairs={{0,6},{1,7},{2,4},{3,5},{4,2},{5,3},{6,0},{7,1},{8,14},{9,15},{10,... | collective-permute-start | bytes 614408 | tf_op jit(solution)/shard_map/ppermute | solution.py:299
  77.0 15.4 %collective-permute-start.23 = (bf16[8,12800]{1,0:T(8,128)(2,1)S(1)}, bf16[8,12800]{1,0:T(8,128)(2,1)S(1)}, u32[]{:S(2)}, u32[]{:S(2)}) collective-permute-start(bf16[8,12800]{1,0:T(8,128)(2,1)S(1)} %multiply_convert_fusion.5.refs_0_), channel_id=1, source_target_pairs={{0,2},{1,3},{2,0},{3,1},{4,6},{5,7},{6,4},{7,5},{8,10},{9,11},{10,... | collective-permute-start | bytes 614408 | tf_op jit(solution)/shard_map/ppermute | solution.py:299
  80.4 15.3 %collective-permute-start.25 = (bf16[32,3200]{1,0:T(8,128)(2,1)S(1)}, bf16[32,3200]{1,0:T(8,128)(2,1)S(1)}, u32[]{:S(2)}, u32[]{:S(2)}) collective-permute-start(bf16[32,3200]{1,0:T(8,128)(2,1)S(1)} %get-tuple-element.152), channel_id=1, source_target_pairs={{0,2},{1,3},{2,0},{3,1},{4,6},{5,7},{6,4},{7,5},{8,10},{9,11},{10,... | collective-permute-start | bytes 614408 | tf_op jit(solution)/shard_map/ppermute | solution.py:299
  96.8 16.7 %collective-permute-start.30 = (bf16[32,3200]{1,0:T(8,128)(2,1)S(1)}, bf16[32,3200]{1,0:T(8,128)(2,1)S(1)}, u32[]{:S(2)}, u32[]{:S(2)}) collective-permute-start(bf16[32,3200]{1,0:T(8,128)(2,1)S(1)} %get-tuple-element.161), channel_id=1, source_target_pairs={{0,4},{1,5},{2,6},{3,7},{4,0},{5,1},{6,2},{7,3},{8,12},{9,13},{10,... | collective-permute-start | bytes 614408 | tf_op jit(solution)/shard_map/ppermute | solution.py:299
  97.3 16.2 %collective-permute-start.31 = (bf16[32,3200]{1,0:T(8,128)(2,1)S(1)}, bf16[32,3200]{1,0:T(8,128)(2,1)S(1)}, u32[]{:S(2)}, u32[]{:S(2)}) collective-permute-start(bf16[32,3200]{1,0:T(8,128)(2,1)S(1)} %get-tuple-element.162), channel_id=1, source_target_pairs={{0,6},{1,7},{2,4},{3,5},{4,2},{5,3},{6,0},{7,1},{8,14},{9,15},{10,... | collective-permute-start | bytes 614408 | tf_op jit(solution)/shard_map/ppermute | solution.py:299
  114.7 19.6 %collective-permute-start.32 = (bf16[8,12800]{1,0:T(8,128)(2,1)S(1)}, bf16[8,12800]{1,0:T(8,128)(2,1)S(1)}, u32[]{:S(2)}, u32[]{:S(2)}) collective-permute-start(bf16[8,12800]{1,0:T(8,128)(2,1)S(1)} %multiply_convert_fusion.4.refs_0_), channel_id=1, source_target_pairs={{0,4},{1,5},{2,6},{3,7},{4,0},{5,1},{6,2},{7,3},{8,12},{9,13},{10,... | collective-permute-start | bytes 614408 | tf_op jit(solution)/shard_map/ppermute | solution.py:299
  119.7 14.7 %collective-permute-start.33 = (bf16[8,12800]{1,0:T(8,128)(2,1)S(1)}, bf16[8,12800]{1,0:T(8,128)(2,1)S(1)}, u32[]{:S(2)}, u32[]{:S(2)}) collective-permute-start(bf16[8,12800]{1,0:T(8,128)(2,1)S(1)} %multiply_convert_fusion.4.refs_0_), channel_id=1, source_target_pairs={{0,6},{1,7},{2,4},{3,5},{4,2},{5,3},{6,0},{7,1},{8,14},{9,15},{10,... | collective-permute-start | bytes 614408 | tf_op jit(solution)/shard_map/ppermute | solution.py:299
  122.0 13.0 %collective-permute-start.34 = (bf16[8,12800]{1,0:T(8,128)(2,1)S(1)}, bf16[8,12800]{1,0:T(8,128)(2,1)S(1)}, u32[]{:S(2)}, u32[]{:S(2)}) collective-permute-start(bf16[8,12800]{1,0:T(8,128)(2,1)S(1)} %multiply_convert_fusion.4.refs_0_), channel_id=1, source_target_pairs={{0,2},{1,3},{2,0},{3,1},{4,6},{5,7},{6,4},{7,5},{8,10},{9,11},{10,... | collective-permute-start | bytes 614408 | tf_op jit(solution)/shard_map/ppermute | solution.py:299
  135.1 7.2 %collective-permute-start.35 = (bf16[8,12800]{1,0:T(8,128)(2,1)S(1)}, bf16[8,12800]{1,0:T(8,128)(2,1)S(1)}, u32[]{:S(2)}, u32[]{:S(2)}) collective-permute-start(bf16[8,12800]{1,0:T(8,128)(2,1)S(1)} %multiply_convert_fusion.4.refs_0_), channel_id=1, source_target_pairs={{0,1},{1,0},{2,3},{3,2},{4,5},{5,4},{6,7},{7,6},{8,9},{9,8},{10,11... | collective-permute-start | bytes 614408 | tf_op jit(solution)/shard_map/ppermute | solution.py:305
  135.6 8.1 %collective-permute-start.36 = (bf16[8,12800]{1,0:T(8,128)(2,1)S(1)}, bf16[8,12800]{1,0:T(8,128)(2,1)S(1)}, u32[]{:S(2)}, u32[]{:S(2)}) collective-permute-start(bf16[8,12800]{1,0:T(8,128)(2,1)S(1)} %collective-permute-done.32.refs_1_), channel_id=1, source_target_pairs={{0,1},{1,0},{2,3},{3,2},{4,5},{5,4},{6,7},{7,6},{8,9},{9,8},{10,11... | collective-permute-start | bytes 614408 | tf_op jit(solution)/shard_map/ppermute | solution.py:305
  135.6 8.1 %collective-permute-start.37 = (bf16[8,12800]{1,0:T(8,128)(2,1)S(1)}, bf16[8,12800]{1,0:T(8,128)(2,1)S(1)}, u32[]{:S(2)}, u32[]{:S(2)}) collective-permute-start(bf16[8,12800]{1,0:T(8,128)(2,1)S(1)} %collective-permute-done.33.refs_2_), channel_id=1, source_target_pairs={{0,1},{1,0},{2,3},{3,2},{4,5},{5,4},{6,7},{7,6},{8,9},{9,8},{10,11... | collective-permute-start | bytes 614408 | tf_op jit(solution)/shard_map/ppermute | solution.py:305
  136.1 7.6 %collective-permute-start.38 = (bf16[8,12800]{1,0:T(8,128)(2,1)S(1)}, bf16[8,12800]{1,0:T(8,128)(2,1)S(1)}, u32[]{:S(2)}, u32[]{:S(2)}) collective-permute-start(bf16[8,12800]{1,0:T(8,128)(2,1)S(1)} %collective-permute-done.34.refs_3_), channel_id=1, source_target_pairs={{0,1},{1,0},{2,3},{3,2},{4,5},{5,4},{6,7},{7,6},{8,9},{9,8},{10,11... | collective-permute-start | bytes 614408 | tf_op jit(solution)/shard_map/ppermute | solution.py:305
  137.6 19.3 %collective-permute-start.40 = (bf16[8,12800]{1,0:T(8,128)(2,1)S(1)}, bf16[8,12800]{1,0:T(8,128)(2,1)S(1)}, u32[]{:S(2)}, u32[]{:S(2)}) collective-permute-start(bf16[8,12800]{1,0:T(8,128)(2,1)S(1)} %get-tuple-element.284), channel_id=1, source_target_pairs={{0,4},{1,5},{2,6},{3,7},{4,0},{5,1},{6,2},{7,3},{8,12},{9,13},{10,... | collective-permute-start | bytes 614408 | tf_op jit(solution)/shard_map/ppermute | solution.py:299
  142.2 14.7 %collective-permute-start.41 = (bf16[8,12800]{1,0:T(8,128)(2,1)S(1)}, bf16[8,12800]{1,0:T(8,128)(2,1)S(1)}, u32[]{:S(2)}, u32[]{:S(2)}) collective-permute-start(bf16[8,12800]{1,0:T(8,128)(2,1)S(1)} %get-tuple-element.283), channel_id=1, source_target_pairs={{0,6},{1,7},{2,4},{3,5},{4,2},{5,3},{6,0},{7,1},{8,14},{9,15},{10,... | collective-permute-start | bytes 614408 | tf_op jit(solution)/shard_map/ppermute | solution.py:299
  143.7 14.1 %collective-permute-start.42 = (bf16[8,12800]{1,0:T(8,128)(2,1)S(1)}, bf16[8,12800]{1,0:T(8,128)(2,1)S(1)}, u32[]{:S(2)}, u32[]{:S(2)}) collective-permute-start(bf16[8,12800]{1,0:T(8,128)(2,1)S(1)} %get-tuple-element.282), channel_id=1, source_target_pairs={{0,2},{1,3},{2,0},{3,1},{4,6},{5,7},{6,4},{7,5},{8,10},{9,11},{10,... | collective-permute-start | bytes 614408 | tf_op jit(solution)/shard_map/ppermute | solution.py:299
  158.5 18.6 %collective-permute-start.43 = (bf16[32,3200]{1,0:T(8,128)(2,1)S(1)}, bf16[32,3200]{1,0:T(8,128)(2,1)}, u32[]{:S(2)}, u32[]{:S(2)}) collective-permute-start(bf16[32,3200]{1,0:T(8,128)(2,1)S(1)} %multiply_convert_fusion.2.refs_0_), channel_id=1, source_target_pairs={{0,4},{1,5},{2,6},{3,7},{4,0},{5,1},{6,2},{7,3},{8,12},{9,13},{10,... | collective-permute-start | bytes 614408 | tf_op jit(solution)/shard_map/ppermute | solution.py:299
  162.2 14.9 %collective-permute-start.44 = (bf16[32,3200]{1,0:T(8,128)(2,1)S(1)}, bf16[32,3200]{1,0:T(8,128)(2,1)}, u32[]{:S(2)}, u32[]{:S(2)}) collective-permute-start(bf16[32,3200]{1,0:T(8,128)(2,1)S(1)} %multiply_convert_fusion.2.refs_0_), channel_id=1, source_target_pairs={{0,6},{1,7},{2,4},{3,5},{4,2},{5,3},{6,0},{7,1},{8,14},{9,15},{10,... | collective-permute-start | bytes 614408 | tf_op jit(solution)/shard_map/ppermute | solution.py:299
  164.5 12.8 %collective-permute-start.45 = (bf16[32,3200]{1,0:T(8,128)(2,1)S(1)}, bf16[32,3200]{1,0:T(8,128)(2,1)}, u32[]{:S(2)}, u32[]{:S(2)}) collective-permute-start(bf16[32,3200]{1,0:T(8,128)(2,1)S(1)} %multiply_convert_fusion.2.refs_0_), channel_id=1, source_target_pairs={{0,2},{1,3},{2,0},{3,1},{4,6},{5,7},{6,4},{7,5},{8,10},{9,11},{10,... | collective-permute-start | bytes 614408 | tf_op jit(solution)/shard_map/ppermute | solution.py:299
  178.3 7.4 %collective-permute-start.46 = (bf16[32,3200]{1,0:T(8,128)(2,1)S(1)}, bf16[32,3200]{1,0:T(8,128)(2,1)S(1)}, u32[]{:S(2)}, u32[]{:S(2)}) collective-permute-start(bf16[32,3200]{1,0:T(8,128)(2,1)S(1)} %multiply_convert_fusion.2.refs_0_), channel_id=1, source_target_pairs={{0,1},{1,0},{2,3},{3,2},{4,5},{5,4},{6,7},{7,6},{8,9},{9,8},{10,11... | collective-permute-start | bytes 614408 | tf_op jit(solution)/shard_map/ppermute | solution.py:305
  178.9 8.3 %collective-permute-start.47 = (bf16[32,3200]{1,0:T(8,128)(2,1)}, bf16[32,3200]{1,0:T(8,128)(2,1)S(1)}, u32[]{:S(2)}, u32[]{:S(2)}) collective-permute-start(bf16[32,3200]{1,0:T(8,128)(2,1)} %collective-permute-done.43.refs_1_), channel_id=1, source_target_pairs={{0,1},{1,0},{2,3},{3,2},{4,5},{5,4},{6,7},{7,6},{8,9},{9,8},{10,11... | collective-permute-start | bytes 614408 | tf_op jit(solution)/shard_map/ppermute | solution.py:305
  179.0 8.2 %collective-permute-start.48 = (bf16[32,3200]{1,0:T(8,128)(2,1)}, bf16[32,3200]{1,0:T(8,128)(2,1)S(1)}, u32[]{:S(2)}, u32[]{:S(2)}) collective-permute-start(bf16[32,3200]{1,0:T(8,128)(2,1)} %collective-permute-done.44.refs_2_), channel_id=1, source_target_pairs={{0,1},{1,0},{2,3},{3,2},{4,5},{5,4},{6,7},{7,6},{8,9},{9,8},{10,11... | collective-permute-start | bytes 614408 | tf_op jit(solution)/shard_map/ppermute | solution.py:305
  179.4 7.8 %collective-permute-start.49 = (bf16[32,3200]{1,0:T(8,128)(2,1)}, bf16[32,3200]{1,0:T(8,128)(2,1)S(1)}, u32[]{:S(2)}, u32[]{:S(2)}) collective-permute-start(bf16[32,3200]{1,0:T(8,128)(2,1)} %collective-permute-done.45.refs_3_), channel_id=1, source_target_pairs={{0,1},{1,0},{2,3},{3,2},{4,5},{5,4},{6,7},{7,6},{8,9},{9,8},{10,11... | collective-permute-start | bytes 614408 | tf_op jit(solution)/shard_map/ppermute | solution.py:305
  181.1 21.6 %collective-permute-start.51 = (bf16[8,12800]{1,0:T(8,128)(2,1)S(1)}, bf16[8,12800]{1,0:T(8,128)(2,1)S(1)}, u32[]{:S(2)}, u32[]{:S(2)}) collective-permute-start(bf16[8,12800]{1,0:T(8,128)(2,1)S(1)} %get-tuple-element.281), channel_id=1, source_target_pairs={{0,4},{1,5},{2,6},{3,7},{4,0},{5,1},{6,2},{7,3},{8,12},{9,13},{10,... | collective-permute-start | bytes 614408 | tf_op jit(solution)/shard_map/ppermute | solution.py:299
  185.7 17.0 %collective-permute-start.52 = (bf16[8,12800]{1,0:T(8,128)(2,1)S(1)}, bf16[8,12800]{1,0:T(8,128)(2,1)S(1)}, u32[]{:S(2)}, u32[]{:S(2)}) collective-permute-start(bf16[8,12800]{1,0:T(8,128)(2,1)S(1)} %get-tuple-element.280), channel_id=1, source_target_pairs={{0,6},{1,7},{2,4},{3,5},{4,2},{5,3},{6,0},{7,1},{8,14},{9,15},{10,... | collective-permute-start | bytes 614408 | tf_op jit(solution)/shard_map/ppermute | solution.py:299
  187.2 15.6 %collective-permute-start.53 = (bf16[8,12800]{1,0:T(8,128)(2,1)S(1)}, bf16[8,12800]{1,0:T(8,128)(2,1)S(1)}, u32[]{:S(2)}, u32[]{:S(2)}) collective-permute-start(bf16[8,12800]{1,0:T(8,128)(2,1)S(1)} %get-tuple-element.279), channel_id=1, source_target_pairs={{0,2},{1,3},{2,0},{3,1},{4,6},{5,7},{6,4},{7,5},{8,10},{9,11},{10,... | collective-permute-start | bytes 614408 | tf_op jit(solution)/shard_map/ppermute | solution.py:299
  202.6 8.7 %collective-permute-start.54 = (bf16[128,3200]{1,0:T(8,128)(2,1)}, bf16[128,3200]{1,0:T(8,128)(2,1)}, u32[]{:S(2)}, u32[]{:S(2)}) collective-permute-start(bf16[128,3200]{1,0:T(8,128)(2,1)} %get-tuple-element.207), channel_id=1, source_target_pairs={{0,1},{1,0},{2,3},{3,2},{4,5},{5,4},{6,7},{7,6},{8,9},{9,8},{10,11... | collective-permute-start | bytes 2457608 | tf_op jit(solution)/shard_map/ppermute | solution.py:312
  203.5 17.7 %collective-permute-start.55 = (bf16[32,3200]{1,0:T(8,128)(2,1)S(1)}, bf16[32,3200]{1,0:T(8,128)(2,1)S(1)}, u32[]{:S(2)}, u32[]{:S(2)}) collective-permute-start(bf16[32,3200]{1,0:T(8,128)(2,1)S(1)} %multiply_convert_fusion.refs_0_), channel_id=1, source_target_pairs={{0,4},{1,5},{2,6},{3,7},{4,0},{5,1},{6,2},{7,3},{8,12},{9,13},{10,... | collective-permute-start | bytes 614408 | tf_op jit(solution)/shard_map/ppermute | solution.py:299
  206.4 14.8 %collective-permute-start.56 = (bf16[32,3200]{1,0:T(8,128)(2,1)S(1)}, bf16[32,3200]{1,0:T(8,128)(2,1)}, u32[]{:S(2)}, u32[]{:S(2)}) collective-permute-start(bf16[32,3200]{1,0:T(8,128)(2,1)S(1)} %multiply_convert_fusion.refs_0_), channel_id=1, source_target_pairs={{0,6},{1,7},{2,4},{3,5},{4,2},{5,3},{6,0},{7,1},{8,14},{9,15},{10,... | collective-permute-start | bytes 614408 | tf_op jit(solution)/shard_map/ppermute | solution.py:299
  208.0 14.3 %collective-permute-start.57 = (bf16[32,3200]{1,0:T(8,128)(2,1)S(1)}, bf16[32,3200]{1,0:T(8,128)(2,1)}, u32[]{:S(2)}, u32[]{:S(2)}) collective-permute-start(bf16[32,3200]{1,0:T(8,128)(2,1)S(1)} %multiply_convert_fusion.refs_0_), channel_id=1, source_target_pairs={{0,2},{1,3},{2,0},{3,1},{4,6},{5,7},{6,4},{7,5},{8,10},{9,11},{10,... | collective-permute-start | bytes 614408 | tf_op jit(solution)/shard_map/ppermute | solution.py:299
  209.8 5.3 %collective-permute-start.58 = (bf16[32,1024]{1,0:T(8,128)(2,1)S(1)}, bf16[32,1024]{1,0:T(8,128)(2,1)S(1)}, u32[]{:S(2)}, u32[]{:S(2)}) collective-permute-start(bf16[32,1024]{1,0:T(8,128)(2,1)S(1)} %get-tuple-element.297), channel_id=1, source_target_pairs={{0,8},{8,16},{16,24},{24,0},{1,9},{9,17},{17,25},{25,1},{2,10},{10... | collective-permute-start | bytes 196616 | tf_op jit(solution)/shard_map/ppermute | solution.py:445
  211.3 5.3 %collective-permute-start.59 = (bf16[32,1024]{1,0:T(8,128)(2,1)S(1)}, bf16[32,1024]{1,0:T(8,128)(2,1)S(1)}, u32[]{:S(2)}, u32[]{:S(2)}) collective-permute-start(bf16[32,1024]{1,0:T(8,128)(2,1)S(1)} %get-tuple-element.296), channel_id=1, source_target_pairs={{0,16},{8,24},{16,0},{24,8},{1,17},{9,25},{17,1},{25,9},{2,18},{10... | collective-permute-start | bytes 196616 | tf_op jit(solution)/shard_map/ppermute | solution.py:445
  215.1 4.3 %collective-permute-start.60 = (bf16[32,1024]{1,0:T(8,128)(2,1)S(1)}, bf16[32,1024]{1,0:T(8,128)(2,1)S(1)}, u32[]{:S(2)}, u32[]{:S(2)}) collective-permute-start(bf16[32,1024]{1,0:T(8,128)(2,1)S(1)} %get-tuple-element.295), channel_id=1, source_target_pairs={{0,24},{8,0},{16,8},{24,16},{1,25},{9,1},{17,9},{25,17},{2,26},{10... | collective-permute-start | bytes 196616 | tf_op jit(solution)/shard_map/ppermute | solution.py:445
  222.4 5.4 %collective-permute-start.61 = (bf16[32,3200]{1,0:T(8,128)(2,1)S(1)}, bf16[32,3200]{1,0:T(8,128)(2,1)S(1)}, u32[]{:S(2)}, u32[]{:S(2)}) collective-permute-start(bf16[32,3200]{1,0:T(8,128)(2,1)S(1)} %multiply_convert_fusion.refs_0_), channel_id=1, source_target_pairs={{0,1},{1,0},{2,3},{3,2},{4,5},{5,4},{6,7},{7,6},{8,9},{9,8},{10,11... | collective-permute-start | bytes 614408 | tf_op jit(solution)/shard_map/ppermute | solution.py:305
  222.4 7.0 %collective-permute-start.62 = (bf16[32,3200]{1,0:T(8,128)(2,1)S(1)}, bf16[32,3200]{1,0:T(8,128)(2,1)S(1)}, u32[]{:S(2)}, u32[]{:S(2)}) collective-permute-start(bf16[32,3200]{1,0:T(8,128)(2,1)S(1)} %collective-permute-done.55.refs_1_), channel_id=1, source_target_pairs={{0,1},{1,0},{2,3},{3,2},{4,5},{5,4},{6,7},{7,6},{8,9},{9,8},{10,11... | collective-permute-start | bytes 614408 | tf_op jit(solution)/shard_map/ppermute | solution.py:305
  222.9 6.5 %collective-permute-start.63 = (bf16[32,3200]{1,0:T(8,128)(2,1)}, bf16[32,3200]{1,0:T(8,128)(2,1)S(1)}, u32[]{:S(2)}, u32[]{:S(2)}) collective-permute-start(bf16[32,3200]{1,0:T(8,128)(2,1)} %collective-permute-done.56.refs_2_), channel_id=1, source_target_pairs={{0,1},{1,0},{2,3},{3,2},{4,5},{5,4},{6,7},{7,6},{8,9},{9,8},{10,11... | collective-permute-start | bytes 614408 | tf_op jit(solution)/shard_map/ppermute | solution.py:305
  222.9 6.6 %collective-permute-start.64 = (bf16[32,3200]{1,0:T(8,128)(2,1)}, bf16[32,3200]{1,0:T(8,128)(2,1)S(1)}, u32[]{:S(2)}, u32[]{:S(2)}) collective-permute-start(bf16[32,3200]{1,0:T(8,128)(2,1)} %collective-permute-done.57.refs_3_), channel_id=1, source_target_pairs={{0,1},{1,0},{2,3},{3,2},{4,5},{5,4},{6,7},{7,6},{8,9},{9,8},{10,11... | collective-permute-start | bytes 614408 | tf_op jit(solution)/shard_map/ppermute | solution.py:305
  223.4 21.5 %collective-permute-start.65 = (bf16[32,3200]{1,0:T(8,128)(2,1)S(1)}, bf16[32,3200]{1,0:T(8,128)(2,1)S(1)}, u32[]{:S(2)}, u32[]{:S(2)}) collective-permute-start(bf16[32,3200]{1,0:T(8,128)(2,1)S(1)} %get-tuple-element.217), channel_id=1, source_target_pairs={{0,4},{1,5},{2,6},{3,7},{4,0},{5,1},{6,2},{7,3},{8,12},{9,13},{10,... | collective-permute-start | bytes 614408 | tf_op jit(solution)/shard_map/ppermute | solution.py:299
  227.7 17.2 %collective-permute-start.66 = (bf16[32,3200]{1,0:T(8,128)(2,1)S(1)}, bf16[32,3200]{1,0:T(8,128)(2,1)S(1)}, u32[]{:S(2)}, u32[]{:S(2)}) collective-permute-start(bf16[32,3200]{1,0:T(8,128)(2,1)S(1)} %get-tuple-element.218), channel_id=1, source_target_pairs={{0,6},{1,7},{2,4},{3,5},{4,2},{5,3},{6,0},{7,1},{8,14},{9,15},{10,... | collective-permute-start | bytes 614408 | tf_op jit(solution)/shard_map/ppermute | solution.py:299
  229.4 15.5 %collective-permute-start.67 = (bf16[32,3200]{1,0:T(8,128)(2,1)S(1)}, bf16[32,3200]{1,0:T(8,128)(2,1)S(1)}, u32[]{:S(2)}, u32[]{:S(2)}) collective-permute-start(bf16[32,3200]{1,0:T(8,128)(2,1)S(1)} %get-tuple-element.219), channel_id=1, source_target_pairs={{0,2},{1,3},{2,0},{3,1},{4,6},{5,7},{6,4},{7,5},{8,10},{9,11},{10,... | collective-permute-start | bytes 614408 | tf_op jit(solution)/shard_map/ppermute | solution.py:299
  247.7 17.7 %collective-permute-start.69 = (bf16[32,3200]{1,0:T(8,128)(2,1)S(1)}, bf16[32,3200]{1,0:T(8,128)(2,1)S(1)}, u32[]{:S(2)}, u32[]{:S(2)}) collective-permute-start(bf16[32,3200]{1,0:T(8,128)(2,1)S(1)} %get-tuple-element.275), channel_id=1, source_target_pairs={{0,4},{1,5},{2,6},{3,7},{4,0},{5,1},{6,2},{7,3},{8,12},{9,13},{10,... | collective-permute-start | bytes 614408 | tf_op jit(solution)/shard_map/ppermute | solution.py:299
  250.4 15.0 %collective-permute-start.70 = (bf16[32,3200]{1,0:T(8,128)(2,1)S(1)}, bf16[32,3200]{1,0:T(8,128)(2,1)S(1)}, u32[]{:S(2)}, u32[]{:S(2)}) collective-permute-start(bf16[32,3200]{1,0:T(8,128)(2,1)S(1)} %get-tuple-element.274), channel_id=1, source_target_pairs={{0,6},{1,7},{2,4},{3,5},{4,2},{5,3},{6,0},{7,1},{8,14},{9,15},{10,... | collective-permute-start | bytes 614408 | tf_op jit(solution)/shard_map/ppermute | solution.py:299
  252.1 13.8 %collective-permute-start.71 = (bf16[32,3200]{1,0:T(8,128)(2,1)S(1)}, bf16[32,3200]{1,0:T(8,128)(2,1)S(1)}, u32[]{:S(2)}, u32[]{:S(2)}) collective-permute-start(bf16[32,3200]{1,0:T(8,128)(2,1)S(1)} %get-tuple-element.273), channel_id=1, source_target_pairs={{0,2},{1,3},{2,0},{3,1},{4,6},{5,7},{6,4},{7,5},{8,10},{9,11},{10,... | collective-permute-start | bytes 614408 | tf_op jit(solution)/shard_map/ppermute | solution.py:299
  (46 other events, 275.4 us)

commit v15 on v14

--- a/solution.py
+++ b/solution.py
@@ -408,7 +408,6 @@
         (moves.combine(near_a, far_a), [grad_of(picked, c) for c in range(chunks)])
     )
     terms_a = moves.send(cut_a)
-    rail_b, terms_a[-1] = tied((rail_b, terms_a[-1]))
     merged_b = moves.gathered(rail_b)
     projected_b, delta_b = project(merged_b, proj_weight, upstream[1])
     projected_b, delta_b, terms_a = tied((projected_b, delta_b, terms_a))

time: 269 us -> 269 us (level)
  waiting for transfers between devices: 54.6 us -> 50.3 us
    ppermute x36, waiting for transfers between devices: 41.3 us -> 37.3 us  [shift(): return lax.ppermute(block, 'tp', pairs)]
  transfers between devices with their start and end apart: 72 -> 72, of which waited for: 24 -> 24; matrix products, arithmetic and copies ran while one was open for 7% -> 8% of each run, Pallas kernels for 37% -> 37%
where the time goes in v15:
time: 269 us; the launch traced here: 268 us
  Pallas kernels  102 us (38%)
  starting transfers between devices  83.6 us (31%)
  waiting for transfers between devices  50.3 us (19%)
  local copies, waits for them, and re-layouts  13.8 us (5%)
  other arithmetic  13.6 us (5%)
    ppermute x36, starting transfers between devices, shift(): return lax.ppermute(block, 'tp', pairs)  67.4 us
    pallas_call x4, Pallas kernels, vision_pass(): pl.pallas_call(functools.partial(vision_kernel, len(pieces), slope is Non...  58.7 us
    ppermute x36, waiting for transfers between devices, shift(): return lax.ppermute(block, 'tp', pairs)  37.3 us
    pallas_call x2, Pallas kernels, project_back(): pl.pallas_call(project_back_kernel, in_specs=whole_blocks(1) + [pl.BlockS...  22 us
    pallas_call x2, Pallas kernels, project(): pl.pallas_call(functools.partial(project_kernel, len(pieces)), in_specs=w...  19.5 us
    another operation x7, other arithmetic  7.71 us
    ppermute x24, starting transfers between devices, gathered(): other = [lax.ppermute(m, 'tp', self.pairs) for m in mine]  5.88 us
    ppermute x3, starting transfers between devices, per_device(): picked[s] = lax.ppermute(picked[s], 'grp', pairs)  5.42 us
  transfers between devices with their start and end apart: 72, of which 24 were waited for; matrix products, arithmetic and copies ran while one was open for 8% of the time, Pallas kernels for 37%

profile of v15, /device:TPU:0, one launch (start us, length us, event | category | flops | bytes accessed | tf_op | source)
XLA Modules:
  0.0 267.5 jit_solution(1611548831064836334)
XLA Ops:
  0.7 2.2 shard_map.131
  2.9 4.0 %collective-permute-start = (bf16[32,3200]{1,0:T(8,128)(2,1)}, bf16[32,3200]{1,0:T(8,128)(2,1)S(1)}, u32[]{:S(2)}, u32[]{:S(2)}) collective-permute-start(bf16[32,3200]{1,0:T(8,128)(2,1)} %get-tuple-element.118.refs_0_), channel_id=1, source_target_pairs={{0,4},{1,5},{2,6},{3,7},{4,0},{5,1},{6,2},{7,3},{8,12},{9,13},{10,... | collective-permute-start | bytes 614408 | tf_op jit(solution)/shard_map/ppermute | solution.py:299
  6.9 1.3 collective-permute-start.1
  8.5 0.8 reshape.424
  10.3 0.9 gather_fusion
  11.2 2.5 collective-permute-start.3
  14.2 1.4 collective-permute-done.3
  15.6 2.4 collective-permute-start.5
  18.0 3.2 %collective-permute-done.5 = bf16[32,1024]{1,0:T(8,128)(2,1)S(1)} collective-permute-done((bf16[32,1024]{1,0:T(8,128)(2,1)S(1)}, bf16[32,1024]{1,0:T(8,128)(2,1)S(1)}, u32[]{:S(2)}, u32[]{:S(2)}) %collective-permute-start.5) | collective-permute-done | bytes 65568 | tf_op jit(solution)/shard_map/ppermute | solution.py:376
  21.2 0.7 collective-permute-done.refs_1_
  23.5 5.7 %collective-permute-start.10 = (bf16[32,3200]{1,0:T(8,128)(2,1)S(1)}, bf16[32,3200]{1,0:T(8,128)(2,1)S(1)}, u32[]{:S(2)}, u32[]{:S(2)}) collective-permute-start(bf16[32,3200]{1,0:T(8,128)(2,1)S(1)} %copy-done.14), channel_id=1, source_target_pairs={{0,4},{1,5},{2,6},{3,7},{4,0},{5,1},{6,2},{7,3},{8,12},{9,13},{10,... | collective-permute-start | bytes 614408 | tf_op jit(solution)/shard_map/ppermute | solution.py:299
  30.9 14.7 %shard_map.132 = (bf16[128,3200]{1,0:T(8,128)(2,1)}, bf16[128,3200]{1,0:T(8,128)(2,1)}, f32[7,256,256]{2,1,0:T(8,128)}) custom-call(bf16[32,3200]{1,0:T(8,128)(2,1)} %get-tuple-element.118.refs_0_, bf16[32,3200]{1,0:T(8,128)(2,1)} %copy-done.16, bf16[32,3200]{1,0:T(8,128)(2,1)} %collective-permute-done.1.refs_2_, ...), custom_call_target="tpu_custom_call" | custom-call | flops 5242880000 | bytes 25395200 | tf_op jit(solution)/shard_map/pallas_call | solution.py:212
  47.3 1.1 collective-permute-done.17
  48.4 1.3 fusion.52
  49.8 3.5 %collective-permute-start.18 = (bf16[32,3200]{1,0:T(8,128)(2,1)S(1)}, bf16[32,3200]{1,0:T(8,128)(2,1)S(1)}, u32[]{:S(2)}, u32[]{:S(2)}) collective-permute-start(bf16[32,3200]{1,0:T(8,128)(2,1)S(1)} %get-tuple-element.280), channel_id=1, source_target_pairs={{0,4},{1,5},{2,6},{3,7},{4,0},{5,1},{6,2},{7,3},{8,12},{9,13},{10,... | collective-permute-start | bytes 614408 | tf_op jit(solution)/shard_map/ppermute | solution.py:299
  53.3 1.5 collective-permute-start.19
  56.3 14.8 %shard_map.133 = (bf16[128,3200]{1,0:T(8,128)(2,1)}, bf16[128,3200]{1,0:T(8,128)(2,1)}, f32[7,256,256]{2,1,0:T(8,128)}) custom-call(bf16[32,3200]{1,0:T(8,128)(2,1)} %get-tuple-element.125.refs_0_, bf16[32,3200]{1,0:T(8,128)(2,1)} %copy-done.18, bf16[32,3200]{1,0:T(8,128)(2,1)} %copy-done.19, bf16[32,3200]{1,0:T(8,128)(2,1)} %copy-done.20, ...), custom_call_target="tpu_custom_call" | custom-call | flops 5242880000 | bytes 25395200 | tf_op jit(solution)/shard_map/pallas_call | solution.py:212
  73.0 2.9 %collective-permute-start.21 = (bf16[8,12800]{1,0:T(8,128)(2,1)S(1)}, bf16[8,12800]{1,0:T(8,128)(2,1)S(1)}, u32[]{:S(2)}, u32[]{:S(2)}) collective-permute-start(bf16[8,12800]{1,0:T(8,128)(2,1)S(1)} %multiply_convert_fusion.5.refs_0_), channel_id=1, source_target_pairs={{0,4},{1,5},{2,6},{3,7},{4,0},{5,1},{6,2},{7,3},{8,12},{9,13},{10,... | collective-permute-start | bytes 614408 | tf_op jit(solution)/shard_map/ppermute | solution.py:299
  75.9 1.5 collective-permute-start.22
  77.4 2.8 %fusion.53 = (bf16[128,3200]{1,0:T(8,128)(2,1)S(1)}, f32[128,3200]{1,0:T(8,128)}) fusion(bf16[128,3200]{1,0:T(8,128)(2,1)} %collective-permute-done.28, bf16[128,3200]{1,0:T(8,128)(2,1)} %get-tuple-element.141), kind=kLoop, calls=%fused_computation.149 | loop fusion | flops 1638400 | bytes 4096000 | tf_op jit(solution)/shard_map/convert.20
  80.1 0.7 fusion.68
  81.5 9.2 %collective-permute-done.21.refs_1_ = bf16[8,12800]{1,0:T(8,128)(2,1)S(1)} collective-permute-done((bf16[8,12800]{1,0:T(8,128)(2,1)S(1)}, bf16[8,12800]{1,0:T(8,128)(2,1)S(1)}, u32[]{:S(2)}, u32[]{:S(2)}) %collective-permute-start.21) | collective-permute-done | bytes 204832 | tf_op jit(solution)/shard_map/ppermute | solution.py:299
  92.9 1.0 slice.198
  93.9 4.9 %collective-permute-start.29 = (bf16[32,3200]{1,0:T(8,128)(2,1)}, bf16[32,3200]{1,0:T(8,128)(2,1)S(1)}, u32[]{:S(2)}, u32[]{:S(2)}) collective-permute-start(bf16[32,3200]{1,0:T(8,128)(2,1)} %get-tuple-element.151), channel_id=1, source_target_pairs={{0,4},{1,5},{2,6},{3,7},{4,0},{5,1},{6,2},{7,3},{8,12},{9,13},{10,... | collective-permute-start | bytes 614408 | tf_op jit(solution)/shard_map/ppermute | solution.py:299
  98.9 1.7 collective-permute-start.30
  100.5 9.6 %shard_map.134 = (bf16[64,1024]{1,0:T(8,128)(2,1)S(1)}, bf16[64,1024]{1,0:T(8,128)(2,1)S(1)}) custom-call(bf16[8,12800]{1,0:T(8,128)(2,1)S(1)} %multiply_convert_fusion.5.refs_0_, bf16[8,12800]{1,0:T(8,128)(2,1)S(1)} %collective-permute-done.21.refs_1_, bf16[8,12800]{1,0:T(8,128)(2,1)S(1)} %collective-permute-done.22.refs_2_, ...), custom_call_target="tpu_custom_call" | custom-call | flops 1677721600 | bytes 29753344 | tf_op jit(solution)/shard_map/pallas_call | solution.py:249
  110.1 3.6 %collective-permute-done.29 = bf16[32,3200]{1,0:T(8,128)(2,1)S(1)} collective-permute-done((bf16[32,3200]{1,0:T(8,128)(2,1)}, bf16[32,3200]{1,0:T(8,128)(2,1)S(1)}, u32[]{:S(2)}, u32[]{:S(2)}) %collective-permute-start.29) | collective-permute-done | bytes 204832 | tf_op jit(solution)/shard_map/ppermute | solution.py:299
  115.5 4.1 %collective-permute-start.32 = (bf16[8,12800]{1,0:T(8,128)(2,1)S(1)}, bf16[8,12800]{1,0:T(8,128)(2,1)S(1)}, u32[]{:S(2)}, u32[]{:S(2)}) collective-permute-start(bf16[8,12800]{1,0:T(8,128)(2,1)S(1)} %multiply_convert_fusion.4.refs_0_), channel_id=1, source_target_pairs={{0,4},{1,5},{2,6},{3,7},{4,0},{5,1},{6,2},{7,3},{8,12},{9,13},{10,... | collective-permute-start | bytes 614408 | tf_op jit(solution)/shard_map/ppermute | solution.py:299
  119.6 2.2 collective-permute-start.33
  121.8 11.0 %shard_map.135 = (bf16[32,12800]{1,0:T(8,128)(2,1)S(1)}, bf16[32,12800]{1,0:T(8,128)(2,1)S(1)}) custom-call(bf16[64,1024]{1,0:T(8,128)(2,1)S(1)} %get-tuple-element.159.delta, bf16[12800,1024]{1,0:T(8,128)(2,1)} %weight.3), custom_call_target="tpu_custom_call" | custom-call | flops 1677721600 | bytes 29753344 | tf_op jit(solution)/shard_map/pallas_call | solution.py:269
  132.8 1.6 collective-permute-done.32.refs_1_
  135.5 1.3 collective-permute-done.39
  137.0 4.4 %collective-permute-start.40 = (bf16[8,12800]{1,0:T(8,128)(2,1)S(1)}, bf16[8,12800]{1,0:T(8,128)(2,1)S(1)}, u32[]{:S(2)}, u32[]{:S(2)}) collective-permute-start(bf16[8,12800]{1,0:T(8,128)(2,1)S(1)} %get-tuple-element.274), channel_id=1, source_target_pairs={{0,4},{1,5},{2,6},{3,7},{4,0},{5,1},{6,2},{7,3},{8,12},{9,13},{10,... | collective-permute-start | bytes 614408 | tf_op jit(solution)/shard_map/ppermute | solution.py:299
  141.5 1.7 collective-permute-start.41
  143.1 9.9 %shard_map.136 = (bf16[64,1024]{1,0:T(8,128)(2,1)S(1)}, bf16[64,1024]{1,0:T(8,128)(2,1)S(1)}) custom-call(bf16[8,12800]{1,0:T(8,128)(2,1)S(1)} %multiply_convert_fusion.4.refs_0_, bf16[8,12800]{1,0:T(8,128)(2,1)S(1)} %collective-permute-done.32.refs_1_, bf16[8,12800]{1,0:T(8,128)(2,1)S(1)} %collective-permute-done.33.refs_2_, ...), custom_call_target="tpu_custom_call" | custom-call | flops 1677721600 | bytes 29753344 | tf_op jit(solution)/shard_map/pallas_call | solution.py:249
  153.0 3.1 %collective-permute-done.40 = bf16[8,12800]{1,0:T(8,128)(2,1)S(1)} collective-permute-done((bf16[8,12800]{1,0:T(8,128)(2,1)S(1)}, bf16[8,12800]{1,0:T(8,128)(2,1)S(1)}, u32[]{:S(2)}, u32[]{:S(2)}) %collective-permute-start.40) | collective-permute-done | bytes 204832 | tf_op jit(solution)/shard_map/ppermute | solution.py:299
  156.1 0.8 collective-permute-done.42
  157.7 3.9 %collective-permute-start.43 = (bf16[32,3200]{1,0:T(8,128)(2,1)S(1)}, bf16[32,3200]{1,0:T(8,128)(2,1)}, u32[]{:S(2)}, u32[]{:S(2)}) collective-permute-start(bf16[32,3200]{1,0:T(8,128)(2,1)S(1)} %multiply_convert_fusion.2.refs_0_), channel_id=1, source_target_pairs={{0,4},{1,5},{2,6},{3,7},{4,0},{5,1},{6,2},{7,3},{8,12},{9,13},{10,... | collective-permute-start | bytes 614408 | tf_op jit(solution)/shard_map/ppermute | solution.py:299
  161.6 2.2 collective-permute-start.44
  163.8 11.0 %shard_map.137 = (bf16[32,12800]{1,0:T(8,128)(2,1)S(1)}, bf16[32,12800]{1,0:T(8,128)(2,1)S(1)}) custom-call(bf16[64,1024]{1,0:T(8,128)(2,1)S(1)} %get-tuple-element.176.delta, bf16[12800,1024]{1,0:T(8,128)(2,1)} %weight.3), custom_call_target="tpu_custom_call" | custom-call | flops 1677721600 | bytes 29753344 | tf_op jit(solution)/shard_map/pallas_call | solution.py:269
  174.8 1.6 collective-permute-done.43.refs_1_
  179.2 1.3 fusion.55
  180.5 4.4 %collective-permute-start.51 = (bf16[8,12800]{1,0:T(8,128)(2,1)S(1)}, bf16[8,12800]{1,0:T(8,128)(2,1)S(1)}, u32[]{:S(2)}, u32[]{:S(2)}) collective-permute-start(bf16[8,12800]{1,0:T(8,128)(2,1)S(1)} %get-tuple-element.271), channel_id=1, source_target_pairs={{0,4},{1,5},{2,6},{3,7},{4,0},{5,1},{6,2},{7,3},{8,12},{9,13},{10,... | collective-permute-start | bytes 614408 | tf_op jit(solution)/shard_map/ppermute | solution.py:299
  184.9 1.7 collective-permute-start.52
  187.5 14.6 %shard_map.138 = (bf16[128,3200]{1,0:T(8,128)(2,1)}, bf16[128,3200]{1,0:T(8,128)(2,1)}) custom-call(bf16[32,3200]{1,0:T(8,128)(2,1)} %copy-done.12, bf16[32,3200]{1,0:T(8,128)(2,1)} %collective-permute-done.43.refs_1_, bf16[32,3200]{1,0:T(8,128)(2,1)} %collective-permute-done.44.refs_2_, bf16[32,3200]{1,0:T(8,128)(2,1)} %collective-permute-done.45.refs_3_, ...), custom_call_target="tpu_custom_call" | custom-call | flops 5242880000 | bytes 25395200 | tf_op jit(solution)/shard_map/pallas_call | solution.py:212
  202.9 2.7 %collective-permute-start.55 = (bf16[32,3200]{1,0:T(8,128)(2,1)S(1)}, bf16[32,3200]{1,0:T(8,128)(2,1)S(1)}, u32[]{:S(2)}, u32[]{:S(2)}) collective-permute-start(bf16[32,3200]{1,0:T(8,128)(2,1)S(1)} %multiply_convert_fusion.refs_0_), channel_id=1, source_target_pairs={{0,4},{1,5},{2,6},{3,7},{4,0},{5,1},{6,2},{7,3},{8,12},{9,13},{10,... | collective-permute-start | bytes 614408 | tf_op jit(solution)/shard_map/ppermute | solution.py:299
  205.6 1.7 collective-permute-start.56
  209.0 1.6 collective-permute-start.58
  210.6 1.5 collective-permute-start.59
  212.1 1.6 fusion.56
  214.3 1.5 collective-permute-start.60
  215.9 2.7 collective-permute-done.60
  218.6 2.0 collective-permute-done.55.refs_1_
  220.5 1.0 collective-permute-done.57.refs_3_
  222.6 4.3 %collective-permute-start.65 = (bf16[32,3200]{1,0:T(8,128)(2,1)S(1)}, bf16[32,3200]{1,0:T(8,128)(2,1)S(1)}, u32[]{:S(2)}, u32[]{:S(2)}) collective-permute-start(bf16[32,3200]{1,0:T(8,128)(2,1)S(1)} %get-tuple-element.207), channel_id=1, source_target_pairs={{0,4},{1,5},{2,6},{3,7},{4,0},{5,1},{6,2},{7,3},{8,12},{9,13},{10,... | collective-permute-start | bytes 614408 | tf_op jit(solution)/shard_map/ppermute | solution.py:299
  226.9 1.7 collective-permute-start.66
  229.5 14.6 %shard_map.139 = (bf16[128,3200]{1,0:T(8,128)(2,1)}, bf16[128,3200]{1,0:T(8,128)(2,1)}) custom-call(bf16[32,3200]{1,0:T(8,128)(2,1)} %copy-done.11, bf16[32,3200]{1,0:T(8,128)(2,1)} %copy-done.17, bf16[32,3200]{1,0:T(8,128)(2,1)} %collective-permute-done.56.refs_2_, bf16[32,3200]{1,0:T(8,128)(2,1)} %collective-permute-done.57.refs_3_, ...), custom_call_target="tpu_custom_call" | custom-call | flops 5242880000 | bytes 25395200 | tf_op jit(solution)/shard_map/pallas_call | solution.py:212
  244.3 2.4 collective-permute-done.68
  246.9 2.7 %collective-permute-start.69 = (bf16[32,3200]{1,0:T(8,128)(2,1)S(1)}, bf16[32,3200]{1,0:T(8,128)(2,1)S(1)}, u32[]{:S(2)}, u32[]{:S(2)}) collective-permute-start(bf16[32,3200]{1,0:T(8,128)(2,1)S(1)} %get-tuple-element.265), channel_id=1, source_target_pairs={{0,4},{1,5},{2,6},{3,7},{4,0},{5,1},{6,2},{7,3},{8,12},{9,13},{10,... | collective-permute-start | bytes 614408 | tf_op jit(solution)/shard_map/ppermute | solution.py:299
  249.7 1.7 collective-permute-start.70
  251.4 2.2 fusion
  253.6 11.1 %collective-permute-done.69 = bf16[32,3200]{1,0:T(8,128)(2,1)S(1)} collective-permute-done((bf16[32,3200]{1,0:T(8,128)(2,1)S(1)}, bf16[32,3200]{1,0:T(8,128)(2,1)S(1)}, u32[]{:S(2)}, u32[]{:S(2)}) %collective-permute-start.69) | collective-permute-done | bytes 204832 | tf_op jit(solution)/shard_map/ppermute | solution.py:299
  266.0 0.8 pad_maximum_fusion
  266.8 0.7 copy-done.1
  (277 shorter events, 26.8 us)
Async XLA Ops:
  2.9 19.0 %collective-permute-start = (bf16[32,3200]{1,0:T(8,128)(2,1)}, bf16[32,3200]{1,0:T(8,128)(2,1)S(1)}, u32[]{:S(2)}, u32[]{:S(2)}) collective-permute-start(bf16[32,3200]{1,0:T(8,128)(2,1)} %get-tuple-element.118.refs_0_), channel_id=1, source_target_pairs={{0,4},{1,5},{2,6},{3,7},{4,0},{5,1},{6,2},{7,3},{8,12},{9,13},{10,... | collective-permute-start | bytes 614408 | tf_op jit(solution)/shard_map/ppermute | solution.py:299
  6.9 15.0 %collective-permute-start.1 = (bf16[32,3200]{1,0:T(8,128)(2,1)}, bf16[32,3200]{1,0:T(8,128)(2,1)}, u32[]{:S(2)}, u32[]{:S(2)}) collective-permute-start(bf16[32,3200]{1,0:T(8,128)(2,1)} %get-tuple-element.118.refs_0_), channel_id=1, source_target_pairs={{0,6},{1,7},{2,4},{3,5},{4,2},{5,3},{6,0},{7,1},{8,14},{9,15},{10,... | collective-permute-start | bytes 614408 | tf_op jit(solution)/shard_map/ppermute | solution.py:299
  8.3 14.3 %collective-permute-start.2 = (bf16[32,3200]{1,0:T(8,128)(2,1)}, bf16[32,3200]{1,0:T(8,128)(2,1)}, u32[]{:S(2)}, u32[]{:S(2)}) collective-permute-start(bf16[32,3200]{1,0:T(8,128)(2,1)} %get-tuple-element.118.refs_0_), channel_id=1, source_target_pairs={{0,2},{1,3},{2,0},{3,1},{4,6},{5,7},{6,4},{7,5},{8,10},{9,11},{10,... | collective-permute-start | bytes 614408 | tf_op jit(solution)/shard_map/ppermute | solution.py:299
  15.6 5.6 %collective-permute-start.5 = (bf16[32,1024]{1,0:T(8,128)(2,1)S(1)}, bf16[32,1024]{1,0:T(8,128)(2,1)S(1)}, u32[]{:S(2)}, u32[]{:S(2)}) collective-permute-start(bf16[32,1024]{1,0:T(8,128)(2,1)S(1)} %get-tuple-element.291), channel_id=1, source_target_pairs={{0,8},{8,16},{16,24},{24,0},{1,9},{9,17},{17,25},{25,1},{2,10},{10... | collective-permute-start | bytes 196616 | tf_op jit(solution)/shard_map/ppermute | solution.py:376
  22.5 6.7 %collective-permute-start.6 = (bf16[32,3200]{1,0:T(8,128)(2,1)S(1)}, bf16[32,3200]{1,0:T(8,128)(2,1)S(1)}, u32[]{:S(2)}, u32[]{:S(2)}) collective-permute-start(bf16[32,3200]{1,0:T(8,128)(2,1)S(1)} %copy-done.15), channel_id=1, source_target_pairs={{0,1},{1,0},{2,3},{3,2},{4,5},{5,4},{6,7},{7,6},{8,9},{9,8},{10,11... | collective-permute-start | bytes 614408 | tf_op jit(solution)/shard_map/ppermute | solution.py:305
  22.5 7.2 %collective-permute-start.7 = (bf16[32,3200]{1,0:T(8,128)(2,1)S(1)}, bf16[32,3200]{1,0:T(8,128)(2,1)S(1)}, u32[]{:S(2)}, u32[]{:S(2)}) collective-permute-start(bf16[32,3200]{1,0:T(8,128)(2,1)S(1)} %collective-permute-done.refs_1_), channel_id=1, source_target_pairs={{0,1},{1,0},{2,3},{3,2},{4,5},{5,4},{6,7},{7,6},{8,9},{9,8},{10,11... | collective-permute-start | bytes 614408 | tf_op jit(solution)/shard_map/ppermute | solution.py:305
  23.0 7.2 %collective-permute-start.8 = (bf16[32,3200]{1,0:T(8,128)(2,1)}, bf16[32,3200]{1,0:T(8,128)(2,1)S(1)}, u32[]{:S(2)}, u32[]{:S(2)}) collective-permute-start(bf16[32,3200]{1,0:T(8,128)(2,1)} %collective-permute-done.1.refs_2_), channel_id=1, source_target_pairs={{0,1},{1,0},{2,3},{3,2},{4,5},{5,4},{6,7},{7,6},{8,9},{9,8},{10,11... | collective-permute-start | bytes 614408 | tf_op jit(solution)/shard_map/ppermute | solution.py:305
  23.0 7.2 %collective-permute-start.9 = (bf16[32,3200]{1,0:T(8,128)(2,1)}, bf16[32,3200]{1,0:T(8,128)(2,1)S(1)}, u32[]{:S(2)}, u32[]{:S(2)}) collective-permute-start(bf16[32,3200]{1,0:T(8,128)(2,1)} %collective-permute-done.2.refs_3_), channel_id=1, source_target_pairs={{0,1},{1,0},{2,3},{3,2},{4,5},{5,4},{6,7},{7,6},{8,9},{9,8},{10,11... | collective-permute-start | bytes 614408 | tf_op jit(solution)/shard_map/ppermute | solution.py:305
  23.5 22.2 %collective-permute-start.10 = (bf16[32,3200]{1,0:T(8,128)(2,1)S(1)}, bf16[32,3200]{1,0:T(8,128)(2,1)S(1)}, u32[]{:S(2)}, u32[]{:S(2)}) collective-permute-start(bf16[32,3200]{1,0:T(8,128)(2,1)S(1)} %copy-done.14), channel_id=1, source_target_pairs={{0,4},{1,5},{2,6},{3,7},{4,0},{5,1},{6,2},{7,3},{8,12},{9,13},{10,... | collective-permute-start | bytes 614408 | tf_op jit(solution)/shard_map/ppermute | solution.py:299
  29.3 16.5 %collective-permute-start.11 = (bf16[32,3200]{1,0:T(8,128)(2,1)S(1)}, bf16[32,3200]{1,0:T(8,128)(2,1)S(1)}, u32[]{:S(2)}, u32[]{:S(2)}) collective-permute-start(bf16[32,3200]{1,0:T(8,128)(2,1)S(1)} %copy-done.14), channel_id=1, source_target_pairs={{0,6},{1,7},{2,4},{3,5},{4,2},{5,3},{6,0},{7,1},{8,14},{9,15},{10,... | collective-permute-start | bytes 614408 | tf_op jit(solution)/shard_map/ppermute | solution.py:299
  29.7 16.0 %collective-permute-start.12 = (bf16[32,3200]{1,0:T(8,128)(2,1)S(1)}, bf16[32,3200]{1,0:T(8,128)(2,1)S(1)}, u32[]{:S(2)}, u32[]{:S(2)}) collective-permute-start(bf16[32,3200]{1,0:T(8,128)(2,1)S(1)} %copy-done.14), channel_id=1, source_target_pairs={{0,2},{1,3},{2,0},{3,1},{4,6},{5,7},{6,4},{7,5},{8,10},{9,11},{10,... | collective-permute-start | bytes 614408 | tf_op jit(solution)/shard_map/ppermute | solution.py:299
  46.1 7.2 %collective-permute-start.13 = (bf16[32,3200]{1,0:T(8,128)(2,1)S(1)}, bf16[32,3200]{1,0:T(8,128)(2,1)S(1)}, u32[]{:S(2)}, u32[]{:S(2)}) collective-permute-start(bf16[32,3200]{1,0:T(8,128)(2,1)S(1)} %copy-done.14), channel_id=1, source_target_pairs={{0,1},{1,0},{2,3},{3,2},{4,5},{5,4},{6,7},{7,6},{8,9},{9,8},{10,11... | collective-permute-start | bytes 614408 | tf_op jit(solution)/shard_map/ppermute | solution.py:305
  46.7 8.1 %collective-permute-start.14 = (bf16[32,3200]{1,0:T(8,128)(2,1)S(1)}, bf16[32,3200]{1,0:T(8,128)(2,1)S(1)}, u32[]{:S(2)}, u32[]{:S(2)}) collective-permute-start(bf16[32,3200]{1,0:T(8,128)(2,1)S(1)} %collective-permute-done.10.refs_1_), channel_id=1, source_target_pairs={{0,1},{1,0},{2,3},{3,2},{4,5},{5,4},{6,7},{7,6},{8,9},{9,8},{10,11... | collective-permute-start | bytes 614408 | tf_op jit(solution)/shard_map/ppermute | solution.py:305
  46.8 8.1 %collective-permute-start.15 = (bf16[32,3200]{1,0:T(8,128)(2,1)S(1)}, bf16[32,3200]{1,0:T(8,128)(2,1)S(1)}, u32[]{:S(2)}, u32[]{:S(2)}) collective-permute-start(bf16[32,3200]{1,0:T(8,128)(2,1)S(1)} %collective-permute-done.11.refs_2_), channel_id=1, source_target_pairs={{0,1},{1,0},{2,3},{3,2},{4,5},{5,4},{6,7},{7,6},{8,9},{9,8},{10,11... | collective-permute-start | bytes 614408 | tf_op jit(solution)/shard_map/ppermute | solution.py:305
  47.2 7.6 %collective-permute-start.16 = (bf16[32,3200]{1,0:T(8,128)(2,1)S(1)}, bf16[32,3200]{1,0:T(8,128)(2,1)S(1)}, u32[]{:S(2)}, u32[]{:S(2)}) collective-permute-start(bf16[32,3200]{1,0:T(8,128)(2,1)S(1)} %collective-permute-done.12.refs_3_), channel_id=1, source_target_pairs={{0,1},{1,0},{2,3},{3,2},{4,5},{5,4},{6,7},{7,6},{8,9},{9,8},{10,11... | collective-permute-start | bytes 614408 | tf_op jit(solution)/shard_map/ppermute | solution.py:305
  49.8 21.4 %collective-permute-start.18 = (bf16[32,3200]{1,0:T(8,128)(2,1)S(1)}, bf16[32,3200]{1,0:T(8,128)(2,1)S(1)}, u32[]{:S(2)}, u32[]{:S(2)}) collective-permute-start(bf16[32,3200]{1,0:T(8,128)(2,1)S(1)} %get-tuple-element.280), channel_id=1, source_target_pairs={{0,4},{1,5},{2,6},{3,7},{4,0},{5,1},{6,2},{7,3},{8,12},{9,13},{10,... | collective-permute-start | bytes 614408 | tf_op jit(solution)/shard_map/ppermute | solution.py:299
  53.3 17.9 %collective-permute-start.19 = (bf16[32,3200]{1,0:T(8,128)(2,1)S(1)}, bf16[32,3200]{1,0:T(8,128)(2,1)S(1)}, u32[]{:S(2)}, u32[]{:S(2)}) collective-permute-start(bf16[32,3200]{1,0:T(8,128)(2,1)S(1)} %get-tuple-element.279), channel_id=1, source_target_pairs={{0,6},{1,7},{2,4},{3,5},{4,2},{5,3},{6,0},{7,1},{8,14},{9,15},{10,... | collective-permute-start | bytes 614408 | tf_op jit(solution)/shard_map/ppermute | solution.py:299
  54.8 16.4 %collective-permute-start.20 = (bf16[32,3200]{1,0:T(8,128)(2,1)S(1)}, bf16[32,3200]{1,0:T(8,128)(2,1)S(1)}, u32[]{:S(2)}, u32[]{:S(2)}) collective-permute-start(bf16[32,3200]{1,0:T(8,128)(2,1)S(1)} %get-tuple-element.278), channel_id=1, source_target_pairs={{0,2},{1,3},{2,0},{3,1},{4,6},{5,7},{6,4},{7,5},{8,10},{9,11},{10,... | collective-permute-start | bytes 614408 | tf_op jit(solution)/shard_map/ppermute | solution.py:299
  71.1 6.3 %collective-permute-start.28 = (bf16[128,3200]{1,0:T(8,128)(2,1)}, bf16[128,3200]{1,0:T(8,128)(2,1)}, u32[]{:S(2)}, u32[]{:S(2)}) collective-permute-start(bf16[128,3200]{1,0:T(8,128)(2,1)} %get-tuple-element.142), channel_id=1, source_target_pairs={{0,1},{1,0},{2,3},{3,2},{4,5},{5,4},{6,7},{7,6},{8,9},{9,8},{10,11... | collective-permute-start | bytes 2457608 | tf_op jit(solution)/shard_map/ppermute | solution.py:312
  73.0 17.7 %collective-permute-start.21 = (bf16[8,12800]{1,0:T(8,128)(2,1)S(1)}, bf16[8,12800]{1,0:T(8,128)(2,1)S(1)}, u32[]{:S(2)}, u32[]{:S(2)}) collective-permute-start(bf16[8,12800]{1,0:T(8,128)(2,1)S(1)} %multiply_convert_fusion.5.refs_0_), channel_id=1, source_target_pairs={{0,4},{1,5},{2,6},{3,7},{4,0},{5,1},{6,2},{7,3},{8,12},{9,13},{10,... | collective-permute-start | bytes 614408 | tf_op jit(solution)/shard_map/ppermute | solution.py:299
  75.9 14.9 %collective-permute-start.22 = (bf16[8,12800]{1,0:T(8,128)(2,1)S(1)}, bf16[8,12800]{1,0:T(8,128)(2,1)S(1)}, u32[]{:S(2)}, u32[]{:S(2)}) collective-permute-start(bf16[8,12800]{1,0:T(8,128)(2,1)S(1)} %multiply_convert_fusion.5.refs_0_), channel_id=1, source_target_pairs={{0,6},{1,7},{2,4},{3,5},{4,2},{5,3},{6,0},{7,1},{8,14},{9,15},{10,... | collective-permute-start | bytes 614408 | tf_op jit(solution)/shard_map/ppermute | solution.py:299
  77.4 14.4 %collective-permute-start.23 = (bf16[8,12800]{1,0:T(8,128)(2,1)S(1)}, bf16[8,12800]{1,0:T(8,128)(2,1)S(1)}, u32[]{:S(2)}, u32[]{:S(2)}) collective-permute-start(bf16[8,12800]{1,0:T(8,128)(2,1)S(1)} %multiply_convert_fusion.5.refs_0_), channel_id=1, source_target_pairs={{0,2},{1,3},{2,0},{3,1},{4,6},{5,7},{6,4},{7,5},{8,10},{9,11},{10,... | collective-permute-start | bytes 614408 | tf_op jit(solution)/shard_map/ppermute | solution.py:299
  77.4 21.5 %collective-permute-start.24 = (bf16[8,12800]{1,0:T(8,128)(2,1)S(1)}, bf16[8,12800]{1,0:T(8,128)(2,1)S(1)}, u32[]{:S(2)}, u32[]{:S(2)}) collective-permute-start(bf16[8,12800]{1,0:T(8,128)(2,1)S(1)} %multiply_convert_fusion.5.refs_0_), channel_id=1, source_target_pairs={{0,1},{1,0},{2,3},{3,2},{4,5},{5,4},{6,7},{7,6},{8,9},{9,8},{10,11... | collective-permute-start | bytes 614408 | tf_op jit(solution)/shard_map/ppermute | solution.py:305
  90.7 9.8 %collective-permute-start.25 = (bf16[8,12800]{1,0:T(8,128)(2,1)S(1)}, bf16[8,12800]{1,0:T(8,128)(2,1)S(1)}, u32[]{:S(2)}, u32[]{:S(2)}) collective-permute-start(bf16[8,12800]{1,0:T(8,128)(2,1)S(1)} %collective-permute-done.21.refs_1_), channel_id=1, source_target_pairs={{0,1},{1,0},{2,3},{3,2},{4,5},{5,4},{6,7},{7,6},{8,9},{9,8},{10,11... | collective-permute-start | bytes 614408 | tf_op jit(solution)/shard_map/ppermute | solution.py:305
  90.7 9.8 %collective-permute-start.26 = (bf16[8,12800]{1,0:T(8,128)(2,1)S(1)}, bf16[8,12800]{1,0:T(8,128)(2,1)S(1)}, u32[]{:S(2)}, u32[]{:S(2)}) collective-permute-start(bf16[8,12800]{1,0:T(8,128)(2,1)S(1)} %collective-permute-done.22.refs_2_), channel_id=1, source_target_pairs={{0,1},{1,0},{2,3},{3,2},{4,5},{5,4},{6,7},{7,6},{8,9},{9,8},{10,11... | collective-permute-start | bytes 614408 | tf_op jit(solution)/shard_map/ppermute | solution.py:305
  91.8 8.8 %collective-permute-start.27 = (bf16[8,12800]{1,0:T(8,128)(2,1)S(1)}, bf16[8,12800]{1,0:T(8,128)(2,1)S(1)}, u32[]{:S(2)}, u32[]{:S(2)}) collective-permute-start(bf16[8,12800]{1,0:T(8,128)(2,1)S(1)} %collective-permute-done.23.refs_3_), channel_id=1, source_target_pairs={{0,1},{1,0},{2,3},{3,2},{4,5},{5,4},{6,7},{7,6},{8,9},{9,8},{10,11... | collective-permute-start | bytes 614408 | tf_op jit(solution)/shard_map/ppermute | solution.py:305
  93.9 19.8 %collective-permute-start.29 = (bf16[32,3200]{1,0:T(8,128)(2,1)}, bf16[32,3200]{1,0:T(8,128)(2,1)S(1)}, u32[]{:S(2)}, u32[]{:S(2)}) collective-permute-start(bf16[32,3200]{1,0:T(8,128)(2,1)} %get-tuple-element.151), channel_id=1, source_target_pairs={{0,4},{1,5},{2,6},{3,7},{4,0},{5,1},{6,2},{7,3},{8,12},{9,13},{10,... | collective-permute-start | bytes 614408 | tf_op jit(solution)/shard_map/ppermute | solution.py:299
  98.9 14.9 %collective-permute-start.30 = (bf16[32,3200]{1,0:T(8,128)(2,1)S(1)}, bf16[32,3200]{1,0:T(8,128)(2,1)S(1)}, u32[]{:S(2)}, u32[]{:S(2)}) collective-permute-start(bf16[32,3200]{1,0:T(8,128)(2,1)S(1)} %get-tuple-element.152), channel_id=1, source_target_pairs={{0,6},{1,7},{2,4},{3,5},{4,2},{5,3},{6,0},{7,1},{8,14},{9,15},{10,... | collective-permute-start | bytes 614408 | tf_op jit(solution)/shard_map/ppermute | solution.py:299
  100.5 13.7 %collective-permute-start.31 = (bf16[32,3200]{1,0:T(8,128)(2,1)S(1)}, bf16[32,3200]{1,0:T(8,128)(2,1)S(1)}, u32[]{:S(2)}, u32[]{:S(2)}) collective-permute-start(bf16[32,3200]{1,0:T(8,128)(2,1)S(1)} %get-tuple-element.153), channel_id=1, source_target_pairs={{0,2},{1,3},{2,0},{3,1},{4,6},{5,7},{6,4},{7,5},{8,10},{9,11},{10,... | collective-permute-start | bytes 614408 | tf_op jit(solution)/shard_map/ppermute | solution.py:299
  115.5 18.9 %collective-permute-start.32 = (bf16[8,12800]{1,0:T(8,128)(2,1)S(1)}, bf16[8,12800]{1,0:T(8,128)(2,1)S(1)}, u32[]{:S(2)}, u32[]{:S(2)}) collective-permute-start(bf16[8,12800]{1,0:T(8,128)(2,1)S(1)} %multiply_convert_fusion.4.refs_0_), channel_id=1, source_target_pairs={{0,4},{1,5},{2,6},{3,7},{4,0},{5,1},{6,2},{7,3},{8,12},{9,13},{10,... | collective-permute-start | bytes 614408 | tf_op jit(solution)/shard_map/ppermute | solution.py:299
  119.6 14.8 %collective-permute-start.33 = (bf16[8,12800]{1,0:T(8,128)(2,1)S(1)}, bf16[8,12800]{1,0:T(8,128)(2,1)S(1)}, u32[]{:S(2)}, u32[]{:S(2)}) collective-permute-start(bf16[8,12800]{1,0:T(8,128)(2,1)S(1)} %multiply_convert_fusion.4.refs_0_), channel_id=1, source_target_pairs={{0,6},{1,7},{2,4},{3,5},{4,2},{5,3},{6,0},{7,1},{8,14},{9,15},{10,... | collective-permute-start | bytes 614408 | tf_op jit(solution)/shard_map/ppermute | solution.py:299
  121.8 12.7 %collective-permute-start.34 = (bf16[8,12800]{1,0:T(8,128)(2,1)S(1)}, bf16[8,12800]{1,0:T(8,128)(2,1)S(1)}, u32[]{:S(2)}, u32[]{:S(2)}) collective-permute-start(bf16[8,12800]{1,0:T(8,128)(2,1)S(1)} %multiply_convert_fusion.4.refs_0_), channel_id=1, source_target_pairs={{0,2},{1,3},{2,0},{3,1},{4,6},{5,7},{6,4},{7,5},{8,10},{9,11},{10,... | collective-permute-start | bytes 614408 | tf_op jit(solution)/shard_map/ppermute | solution.py:299
  134.5 7.0 %collective-permute-start.35 = (bf16[8,12800]{1,0:T(8,128)(2,1)S(1)}, bf16[8,12800]{1,0:T(8,128)(2,1)S(1)}, u32[]{:S(2)}, u32[]{:S(2)}) collective-permute-start(bf16[8,12800]{1,0:T(8,128)(2,1)S(1)} %multiply_convert_fusion.4.refs_0_), channel_id=1, source_target_pairs={{0,1},{1,0},{2,3},{3,2},{4,5},{5,4},{6,7},{7,6},{8,9},{9,8},{10,11... | collective-permute-start | bytes 614408 | tf_op jit(solution)/shard_map/ppermute | solution.py:305
  135.0 8.1 %collective-permute-start.36 = (bf16[8,12800]{1,0:T(8,128)(2,1)S(1)}, bf16[8,12800]{1,0:T(8,128)(2,1)S(1)}, u32[]{:S(2)}, u32[]{:S(2)}) collective-permute-start(bf16[8,12800]{1,0:T(8,128)(2,1)S(1)} %collective-permute-done.32.refs_1_), channel_id=1, source_target_pairs={{0,1},{1,0},{2,3},{3,2},{4,5},{5,4},{6,7},{7,6},{8,9},{9,8},{10,11... | collective-permute-start | bytes 614408 | tf_op jit(solution)/shard_map/ppermute | solution.py:305
  135.0 8.1 %collective-permute-start.37 = (bf16[8,12800]{1,0:T(8,128)(2,1)S(1)}, bf16[8,12800]{1,0:T(8,128)(2,1)S(1)}, u32[]{:S(2)}, u32[]{:S(2)}) collective-permute-start(bf16[8,12800]{1,0:T(8,128)(2,1)S(1)} %collective-permute-done.33.refs_2_), channel_id=1, source_target_pairs={{0,1},{1,0},{2,3},{3,2},{4,5},{5,4},{6,7},{7,6},{8,9},{9,8},{10,11... | collective-permute-start | bytes 614408 | tf_op jit(solution)/shard_map/ppermute | solution.py:305
  135.5 7.6 %collective-permute-start.38 = (bf16[8,12800]{1,0:T(8,128)(2,1)S(1)}, bf16[8,12800]{1,0:T(8,128)(2,1)S(1)}, u32[]{:S(2)}, u32[]{:S(2)}) collective-permute-start(bf16[8,12800]{1,0:T(8,128)(2,1)S(1)} %collective-permute-done.34.refs_3_), channel_id=1, source_target_pairs={{0,1},{1,0},{2,3},{3,2},{4,5},{5,4},{6,7},{7,6},{8,9},{9,8},{10,11... | collective-permute-start | bytes 614408 | tf_op jit(solution)/shard_map/ppermute | solution.py:305
  137.0 19.1 %collective-permute-start.40 = (bf16[8,12800]{1,0:T(8,128)(2,1)S(1)}, bf16[8,12800]{1,0:T(8,128)(2,1)S(1)}, u32[]{:S(2)}, u32[]{:S(2)}) collective-permute-start(bf16[8,12800]{1,0:T(8,128)(2,1)S(1)} %get-tuple-element.274), channel_id=1, source_target_pairs={{0,4},{1,5},{2,6},{3,7},{4,0},{5,1},{6,2},{7,3},{8,12},{9,13},{10,... | collective-permute-start | bytes 614408 | tf_op jit(solution)/shard_map/ppermute | solution.py:299
  141.5 14.7 %collective-permute-start.41 = (bf16[8,12800]{1,0:T(8,128)(2,1)S(1)}, bf16[8,12800]{1,0:T(8,128)(2,1)S(1)}, u32[]{:S(2)}, u32[]{:S(2)}) collective-permute-start(bf16[8,12800]{1,0:T(8,128)(2,1)S(1)} %get-tuple-element.273), channel_id=1, source_target_pairs={{0,6},{1,7},{2,4},{3,5},{4,2},{5,3},{6,0},{7,1},{8,14},{9,15},{10,... | collective-permute-start | bytes 614408 | tf_op jit(solution)/shard_map/ppermute | solution.py:299
  143.1 13.9 %collective-permute-start.42 = (bf16[8,12800]{1,0:T(8,128)(2,1)S(1)}, bf16[8,12800]{1,0:T(8,128)(2,1)S(1)}, u32[]{:S(2)}, u32[]{:S(2)}) collective-permute-start(bf16[8,12800]{1,0:T(8,128)(2,1)S(1)} %get-tuple-element.272), channel_id=1, source_target_pairs={{0,2},{1,3},{2,0},{3,1},{4,6},{5,7},{6,4},{7,5},{8,10},{9,11},{10,... | collective-permute-start | bytes 614408 | tf_op jit(solution)/shard_map/ppermute | solution.py:299
  157.7 18.7 %collective-permute-start.43 = (bf16[32,3200]{1,0:T(8,128)(2,1)S(1)}, bf16[32,3200]{1,0:T(8,128)(2,1)}, u32[]{:S(2)}, u32[]{:S(2)}) collective-permute-start(bf16[32,3200]{1,0:T(8,128)(2,1)S(1)} %multiply_convert_fusion.2.refs_0_), channel_id=1, source_target_pairs={{0,4},{1,5},{2,6},{3,7},{4,0},{5,1},{6,2},{7,3},{8,12},{9,13},{10,... | collective-permute-start | bytes 614408 | tf_op jit(solution)/shard_map/ppermute | solution.py:299
  161.6 14.9 %collective-permute-start.44 = (bf16[32,3200]{1,0:T(8,128)(2,1)S(1)}, bf16[32,3200]{1,0:T(8,128)(2,1)}, u32[]{:S(2)}, u32[]{:S(2)}) collective-permute-start(bf16[32,3200]{1,0:T(8,128)(2,1)S(1)} %multiply_convert_fusion.2.refs_0_), channel_id=1, source_target_pairs={{0,6},{1,7},{2,4},{3,5},{4,2},{5,3},{6,0},{7,1},{8,14},{9,15},{10,... | collective-permute-start | bytes 614408 | tf_op jit(solution)/shard_map/ppermute | solution.py:299
  163.7 13.0 %collective-permute-start.45 = (bf16[32,3200]{1,0:T(8,128)(2,1)S(1)}, bf16[32,3200]{1,0:T(8,128)(2,1)}, u32[]{:S(2)}, u32[]{:S(2)}) collective-permute-start(bf16[32,3200]{1,0:T(8,128)(2,1)S(1)} %multiply_convert_fusion.2.refs_0_), channel_id=1, source_target_pairs={{0,2},{1,3},{2,0},{3,1},{4,6},{5,7},{6,4},{7,5},{8,10},{9,11},{10,... | collective-permute-start | bytes 614408 | tf_op jit(solution)/shard_map/ppermute | solution.py:299
  177.7 7.2 %collective-permute-start.46 = (bf16[32,3200]{1,0:T(8,128)(2,1)S(1)}, bf16[32,3200]{1,0:T(8,128)(2,1)S(1)}, u32[]{:S(2)}, u32[]{:S(2)}) collective-permute-start(bf16[32,3200]{1,0:T(8,128)(2,1)S(1)} %multiply_convert_fusion.2.refs_0_), channel_id=1, source_target_pairs={{0,1},{1,0},{2,3},{3,2},{4,5},{5,4},{6,7},{7,6},{8,9},{9,8},{10,11... | collective-permute-start | bytes 614408 | tf_op jit(solution)/shard_map/ppermute | solution.py:305
  178.3 8.3 %collective-permute-start.47 = (bf16[32,3200]{1,0:T(8,128)(2,1)}, bf16[32,3200]{1,0:T(8,128)(2,1)S(1)}, u32[]{:S(2)}, u32[]{:S(2)}) collective-permute-start(bf16[32,3200]{1,0:T(8,128)(2,1)} %collective-permute-done.43.refs_1_), channel_id=1, source_target_pairs={{0,1},{1,0},{2,3},{3,2},{4,5},{5,4},{6,7},{7,6},{8,9},{9,8},{10,11... | collective-permute-start | bytes 614408 | tf_op jit(solution)/shard_map/ppermute | solution.py:305
  178.4 8.2 %collective-permute-start.48 = (bf16[32,3200]{1,0:T(8,128)(2,1)}, bf16[32,3200]{1,0:T(8,128)(2,1)S(1)}, u32[]{:S(2)}, u32[]{:S(2)}) collective-permute-start(bf16[32,3200]{1,0:T(8,128)(2,1)} %collective-permute-done.44.refs_2_), channel_id=1, source_target_pairs={{0,1},{1,0},{2,3},{3,2},{4,5},{5,4},{6,7},{7,6},{8,9},{9,8},{10,11... | collective-permute-start | bytes 614408 | tf_op jit(solution)/shard_map/ppermute | solution.py:305
  178.8 7.8 %collective-permute-start.49 = (bf16[32,3200]{1,0:T(8,128)(2,1)}, bf16[32,3200]{1,0:T(8,128)(2,1)S(1)}, u32[]{:S(2)}, u32[]{:S(2)}) collective-permute-start(bf16[32,3200]{1,0:T(8,128)(2,1)} %collective-permute-done.45.refs_3_), channel_id=1, source_target_pairs={{0,1},{1,0},{2,3},{3,2},{4,5},{5,4},{6,7},{7,6},{8,9},{9,8},{10,11... | collective-permute-start | bytes 614408 | tf_op jit(solution)/shard_map/ppermute | solution.py:305
  180.5 21.6 %collective-permute-start.51 = (bf16[8,12800]{1,0:T(8,128)(2,1)S(1)}, bf16[8,12800]{1,0:T(8,128)(2,1)S(1)}, u32[]{:S(2)}, u32[]{:S(2)}) collective-permute-start(bf16[8,12800]{1,0:T(8,128)(2,1)S(1)} %get-tuple-element.271), channel_id=1, source_target_pairs={{0,4},{1,5},{2,6},{3,7},{4,0},{5,1},{6,2},{7,3},{8,12},{9,13},{10,... | collective-permute-start | bytes 614408 | tf_op jit(solution)/shard_map/ppermute | solution.py:299
  184.9 17.2 %collective-permute-start.52 = (bf16[8,12800]{1,0:T(8,128)(2,1)S(1)}, bf16[8,12800]{1,0:T(8,128)(2,1)S(1)}, u32[]{:S(2)}, u32[]{:S(2)}) collective-permute-start(bf16[8,12800]{1,0:T(8,128)(2,1)S(1)} %get-tuple-element.270), channel_id=1, source_target_pairs={{0,6},{1,7},{2,4},{3,5},{4,2},{5,3},{6,0},{7,1},{8,14},{9,15},{10,... | collective-permute-start | bytes 614408 | tf_op jit(solution)/shard_map/ppermute | solution.py:299
  186.6 15.6 %collective-permute-start.53 = (bf16[8,12800]{1,0:T(8,128)(2,1)S(1)}, bf16[8,12800]{1,0:T(8,128)(2,1)S(1)}, u32[]{:S(2)}, u32[]{:S(2)}) collective-permute-start(bf16[8,12800]{1,0:T(8,128)(2,1)S(1)} %get-tuple-element.269), channel_id=1, source_target_pairs={{0,2},{1,3},{2,0},{3,1},{4,6},{5,7},{6,4},{7,5},{8,10},{9,11},{10,... | collective-permute-start | bytes 614408 | tf_op jit(solution)/shard_map/ppermute | solution.py:299
  202.1 8.5 %collective-permute-start.54 = (bf16[128,3200]{1,0:T(8,128)(2,1)}, bf16[128,3200]{1,0:T(8,128)(2,1)}, u32[]{:S(2)}, u32[]{:S(2)}) collective-permute-start(bf16[128,3200]{1,0:T(8,128)(2,1)} %get-tuple-element.197), channel_id=1, source_target_pairs={{0,1},{1,0},{2,3},{3,2},{4,5},{5,4},{6,7},{7,6},{8,9},{9,8},{10,11... | collective-permute-start | bytes 2457608 | tf_op jit(solution)/shard_map/ppermute | solution.py:312
  202.9 17.7 %collective-permute-start.55 = (bf16[32,3200]{1,0:T(8,128)(2,1)S(1)}, bf16[32,3200]{1,0:T(8,128)(2,1)S(1)}, u32[]{:S(2)}, u32[]{:S(2)}) collective-permute-start(bf16[32,3200]{1,0:T(8,128)(2,1)S(1)} %multiply_convert_fusion.refs_0_), channel_id=1, source_target_pairs={{0,4},{1,5},{2,6},{3,7},{4,0},{5,1},{6,2},{7,3},{8,12},{9,13},{10,... | collective-permute-start | bytes 614408 | tf_op jit(solution)/shard_map/ppermute | solution.py:299
  205.6 14.9 %collective-permute-start.56 = (bf16[32,3200]{1,0:T(8,128)(2,1)S(1)}, bf16[32,3200]{1,0:T(8,128)(2,1)}, u32[]{:S(2)}, u32[]{:S(2)}) collective-permute-start(bf16[32,3200]{1,0:T(8,128)(2,1)S(1)} %multiply_convert_fusion.refs_0_), channel_id=1, source_target_pairs={{0,6},{1,7},{2,4},{3,5},{4,2},{5,3},{6,0},{7,1},{8,14},{9,15},{10,... | collective-permute-start | bytes 614408 | tf_op jit(solution)/shard_map/ppermute | solution.py:299
  207.3 14.3 %collective-permute-start.57 = (bf16[32,3200]{1,0:T(8,128)(2,1)S(1)}, bf16[32,3200]{1,0:T(8,128)(2,1)}, u32[]{:S(2)}, u32[]{:S(2)}) collective-permute-start(bf16[32,3200]{1,0:T(8,128)(2,1)S(1)} %multiply_convert_fusion.refs_0_), channel_id=1, source_target_pairs={{0,2},{1,3},{2,0},{3,1},{4,6},{5,7},{6,4},{7,5},{8,10},{9,11},{10,... | collective-permute-start | bytes 614408 | tf_op jit(solution)/shard_map/ppermute | solution.py:299
  210.6 5.3 %collective-permute-start.59 = (bf16[32,1024]{1,0:T(8,128)(2,1)S(1)}, bf16[32,1024]{1,0:T(8,128)(2,1)S(1)}, u32[]{:S(2)}, u32[]{:S(2)}) collective-permute-start(bf16[32,1024]{1,0:T(8,128)(2,1)S(1)} %get-tuple-element.286), channel_id=1, source_target_pairs={{0,16},{8,24},{16,0},{24,8},{1,17},{9,25},{17,1},{25,9},{2,18},{10... | collective-permute-start | bytes 196616 | tf_op jit(solution)/shard_map/ppermute | solution.py:444
  221.6 5.4 %collective-permute-start.61 = (bf16[32,3200]{1,0:T(8,128)(2,1)S(1)}, bf16[32,3200]{1,0:T(8,128)(2,1)S(1)}, u32[]{:S(2)}, u32[]{:S(2)}) collective-permute-start(bf16[32,3200]{1,0:T(8,128)(2,1)S(1)} %multiply_convert_fusion.refs_0_), channel_id=1, source_target_pairs={{0,1},{1,0},{2,3},{3,2},{4,5},{5,4},{6,7},{7,6},{8,9},{9,8},{10,11... | collective-permute-start | bytes 614408 | tf_op jit(solution)/shard_map/ppermute | solution.py:305
  221.6 7.0 %collective-permute-start.62 = (bf16[32,3200]{1,0:T(8,128)(2,1)S(1)}, bf16[32,3200]{1,0:T(8,128)(2,1)S(1)}, u32[]{:S(2)}, u32[]{:S(2)}) collective-permute-start(bf16[32,3200]{1,0:T(8,128)(2,1)S(1)} %collective-permute-done.55.refs_1_), channel_id=1, source_target_pairs={{0,1},{1,0},{2,3},{3,2},{4,5},{5,4},{6,7},{7,6},{8,9},{9,8},{10,11... | collective-permute-start | bytes 614408 | tf_op jit(solution)/shard_map/ppermute | solution.py:305
  222.1 6.5 %collective-permute-start.63 = (bf16[32,3200]{1,0:T(8,128)(2,1)}, bf16[32,3200]{1,0:T(8,128)(2,1)S(1)}, u32[]{:S(2)}, u32[]{:S(2)}) collective-permute-start(bf16[32,3200]{1,0:T(8,128)(2,1)} %collective-permute-done.56.refs_2_), channel_id=1, source_target_pairs={{0,1},{1,0},{2,3},{3,2},{4,5},{5,4},{6,7},{7,6},{8,9},{9,8},{10,11... | collective-permute-start | bytes 614408 | tf_op jit(solution)/shard_map/ppermute | solution.py:305
  222.1 6.6 %collective-permute-start.64 = (bf16[32,3200]{1,0:T(8,128)(2,1)}, bf16[32,3200]{1,0:T(8,128)(2,1)S(1)}, u32[]{:S(2)}, u32[]{:S(2)}) collective-permute-start(bf16[32,3200]{1,0:T(8,128)(2,1)} %collective-permute-done.57.refs_3_), channel_id=1, source_target_pairs={{0,1},{1,0},{2,3},{3,2},{4,5},{5,4},{6,7},{7,6},{8,9},{9,8},{10,11... | collective-permute-start | bytes 614408 | tf_op jit(solution)/shard_map/ppermute | solution.py:305
  222.6 21.4 %collective-permute-start.65 = (bf16[32,3200]{1,0:T(8,128)(2,1)S(1)}, bf16[32,3200]{1,0:T(8,128)(2,1)S(1)}, u32[]{:S(2)}, u32[]{:S(2)}) collective-permute-start(bf16[32,3200]{1,0:T(8,128)(2,1)S(1)} %get-tuple-element.207), channel_id=1, source_target_pairs={{0,4},{1,5},{2,6},{3,7},{4,0},{5,1},{6,2},{7,3},{8,12},{9,13},{10,... | collective-permute-start | bytes 614408 | tf_op jit(solution)/shard_map/ppermute | solution.py:299
  226.9 17.1 %collective-permute-start.66 = (bf16[32,3200]{1,0:T(8,128)(2,1)S(1)}, bf16[32,3200]{1,0:T(8,128)(2,1)S(1)}, u32[]{:S(2)}, u32[]{:S(2)}) collective-permute-start(bf16[32,3200]{1,0:T(8,128)(2,1)S(1)} %get-tuple-element.208), channel_id=1, source_target_pairs={{0,6},{1,7},{2,4},{3,5},{4,2},{5,3},{6,0},{7,1},{8,14},{9,15},{10,... | collective-permute-start | bytes 614408 | tf_op jit(solution)/shard_map/ppermute | solution.py:299
  228.6 15.5 %collective-permute-start.67 = (bf16[32,3200]{1,0:T(8,128)(2,1)S(1)}, bf16[32,3200]{1,0:T(8,128)(2,1)S(1)}, u32[]{:S(2)}, u32[]{:S(2)}) collective-permute-start(bf16[32,3200]{1,0:T(8,128)(2,1)S(1)} %get-tuple-element.209), channel_id=1, source_target_pairs={{0,2},{1,3},{2,0},{3,1},{4,6},{5,7},{6,4},{7,5},{8,10},{9,11},{10,... | collective-permute-start | bytes 614408 | tf_op jit(solution)/shard_map/ppermute | solution.py:299
  246.9 17.7 %collective-permute-start.69 = (bf16[32,3200]{1,0:T(8,128)(2,1)S(1)}, bf16[32,3200]{1,0:T(8,128)(2,1)S(1)}, u32[]{:S(2)}, u32[]{:S(2)}) collective-permute-start(bf16[32,3200]{1,0:T(8,128)(2,1)S(1)} %get-tuple-element.265), channel_id=1, source_target_pairs={{0,4},{1,5},{2,6},{3,7},{4,0},{5,1},{6,2},{7,3},{8,12},{9,13},{10,... | collective-permute-start | bytes 614408 | tf_op jit(solution)/shard_map/ppermute | solution.py:299
  249.7 15.0 %collective-permute-start.70 = (bf16[32,3200]{1,0:T(8,128)(2,1)S(1)}, bf16[32,3200]{1,0:T(8,128)(2,1)S(1)}, u32[]{:S(2)}, u32[]{:S(2)}) collective-permute-start(bf16[32,3200]{1,0:T(8,128)(2,1)S(1)} %get-tuple-element.264), channel_id=1, source_target_pairs={{0,6},{1,7},{2,4},{3,5},{4,2},{5,3},{6,0},{7,1},{8,14},{9,15},{10,... | collective-permute-start | bytes 614408 | tf_op jit(solution)/shard_map/ppermute | solution.py:299
  251.3 13.9 %collective-permute-start.71 = (bf16[32,3200]{1,0:T(8,128)(2,1)S(1)}, bf16[32,3200]{1,0:T(8,128)(2,1)S(1)}, u32[]{:S(2)}, u32[]{:S(2)}) collective-permute-start(bf16[32,3200]{1,0:T(8,128)(2,1)S(1)} %get-tuple-element.263), channel_id=1, source_target_pairs={{0,2},{1,3},{2,0},{3,1},{4,6},{5,7},{6,4},{7,5},{8,10},{9,11},{10,... | collective-permute-start | bytes 614408 | tf_op jit(solution)/shard_map/ppermute | solution.py:299
  (49 other events, 304.3 us)

commit v16 on v12

--- a/solution.py
+++ b/solution.py
@@ -454,7 +454,7 @@
         ).astype(jnp.bfloat16)
         return jnp.where(jnp.any(picks, 1, keepdims=True), placed, text)
 
-    cut_b, arrived = tied((cut_b, arrived))
+    cut_b, arrived, rail_a[-1] = tied((cut_b, arrived, rail_a[-1]))
     terms_b = moves.send(cut_b)
     rail_a, terms_b[-1] = tied((rail_a, terms_b[-1]))
     grad_out_a = moves.gathered(rail_a)

time: 267 us -> 265 us (level)
  waiting for transfers between devices: 58.4 us -> 53.5 us
    ppermute x36, waiting for transfers between devices: 44.6 us -> 41.4 us  [shift(): return lax.ppermute(block, 'tp', pairs)]
  transfers between devices with their start and end apart: 72 -> 72, of which waited for: 28 -> 24; matrix products, arithmetic and copies ran while one was open for 7% -> 7% of each run, Pallas kernels for 38% -> 38%
where the time goes in v16:
time: 265 us; the launch traced here: 263 us
  Pallas kernels  102 us (38%)
  starting transfers between devices  79.2 us (30%)
  waiting for transfers between devices  53.5 us (20%)
  local copies, waits for them, and re-layouts  12.4 us (5%)
  other arithmetic  12.1 us (5%)
    ppermute x36, starting transfers between devices, shift(): return lax.ppermute(block, 'tp', pairs)  63 us
    pallas_call x4, Pallas kernels, vision_pass(): pl.pallas_call(functools.partial(vision_kernel, len(pieces), slope is Non...  58.6 us
    ppermute x36, waiting for transfers between devices, shift(): return lax.ppermute(block, 'tp', pairs)  41.4 us
    pallas_call x2, Pallas kernels, project_back(): pl.pallas_call(project_back_kernel, in_specs=whole_blocks(1) + [pl.BlockS...  22 us
    pallas_call x2, Pallas kernels, project(): pl.pallas_call(functools.partial(project_kernel, len(pieces)), in_specs=w...  19.4 us
    another operation x7, other arithmetic  6.28 us
    ppermute x24, starting transfers between devices, gathered(): other = [lax.ppermute(m, 'tp', self.pairs) for m in mine]  6.05 us
    ppermute x3, starting transfers between devices, per_device(): picked[s] = lax.ppermute(picked[s], 'grp', pairs)  5.42 us
  transfers between devices with their start and end apart: 72, of which 24 were waited for; matrix products, arithmetic and copies ran while one was open for 7% of the time, Pallas kernels for 38%

profile of v16, /device:TPU:0, one launch (start us, length us, event | category | flops | bytes accessed | tf_op | source)
XLA Modules:
  0.0 263.4 jit_solution(11876941298832429802)
XLA Ops:
  0.6 2.2 shard_map.131
  2.8 4.0 %collective-permute-start = (bf16[32,3200]{1,0:T(8,128)(2,1)}, bf16[32,3200]{1,0:T(8,128)(2,1)S(1)}, u32[]{:S(2)}, u32[]{:S(2)}) collective-permute-start(bf16[32,3200]{1,0:T(8,128)(2,1)} %get-tuple-element.125.refs_0_), channel_id=1, source_target_pairs={{0,4},{1,5},{2,6},{3,7},{4,0},{5,1},{6,2},{7,3},{8,12},{9,13},{10,... | collective-permute-start | bytes 614408 | tf_op jit(solution)/shard_map/ppermute | solution.py:299
  6.9 1.3 collective-permute-start.1
  8.5 0.8 reshape.424
  10.3 0.9 gather_fusion
  11.2 2.5 collective-permute-start.3
  14.2 1.4 collective-permute-done.3
  15.6 2.4 collective-permute-start.5
  18.0 3.2 %collective-permute-done.5 = bf16[32,1024]{1,0:T(8,128)(2,1)S(1)} collective-permute-done((bf16[32,1024]{1,0:T(8,128)(2,1)S(1)}, bf16[32,1024]{1,0:T(8,128)(2,1)S(1)}, u32[]{:S(2)}, u32[]{:S(2)}) %collective-permute-start.5) | collective-permute-done | bytes 65568 | tf_op jit(solution)/shard_map/ppermute | solution.py:376
  23.5 5.7 %collective-permute-start.10 = (bf16[32,3200]{1,0:T(8,128)(2,1)}, bf16[32,3200]{1,0:T(8,128)(2,1)S(1)}, u32[]{:S(2)}, u32[]{:S(2)}) collective-permute-start(bf16[32,3200]{1,0:T(8,128)(2,1)} %get-tuple-element.132.refs_0_), channel_id=1, source_target_pairs={{0,4},{1,5},{2,6},{3,7},{4,0},{5,1},{6,2},{7,3},{8,12},{9,13},{10,... | collective-permute-start | bytes 614408 | tf_op jit(solution)/shard_map/ppermute | solution.py:299
  30.9 14.7 %shard_map.132 = (bf16[128,3200]{1,0:T(8,128)(2,1)}, bf16[128,3200]{1,0:T(8,128)(2,1)}, f32[7,256,256]{2,1,0:T(8,128)}) custom-call(bf16[32,3200]{1,0:T(8,128)(2,1)} %get-tuple-element.125.refs_0_, bf16[32,3200]{1,0:T(8,128)(2,1)} %copy-done.17, bf16[32,3200]{1,0:T(8,128)(2,1)} %copy-done.18, bf16[32,3200]{1,0:T(8,128)(2,1)} %copy-done.20, ...), custom_call_target="tpu_custom_call" | custom-call | flops 5242880000 | bytes 25395200 | tf_op jit(solution)/shard_map/pallas_call | solution.py:212
  47.0 1.3 collective-permute-done.17
  48.3 1.3 fusion.52
  49.7 3.5 %collective-permute-start.18 = (bf16[32,3200]{1,0:T(8,128)(2,1)S(1)}, bf16[32,3200]{1,0:T(8,128)(2,1)S(1)}, u32[]{:S(2)}, u32[]{:S(2)}) collective-permute-start(bf16[32,3200]{1,0:T(8,128)(2,1)S(1)} %get-tuple-element.294), channel_id=1, source_target_pairs={{0,4},{1,5},{2,6},{3,7},{4,0},{5,1},{6,2},{7,3},{8,12},{9,13},{10,... | collective-permute-start | bytes 614408 | tf_op jit(solution)/shard_map/ppermute | solution.py:299
  53.2 1.7 collective-permute-start.19
  55.7 0.7 copy-done.29
  56.4 14.7 %shard_map.133 = (bf16[128,3200]{1,0:T(8,128)(2,1)}, bf16[128,3200]{1,0:T(8,128)(2,1)}, f32[7,256,256]{2,1,0:T(8,128)}) custom-call(bf16[32,3200]{1,0:T(8,128)(2,1)} %get-tuple-element.132.refs_0_, bf16[32,3200]{1,0:T(8,128)(2,1)} %copy-done.13, bf16[32,3200]{1,0:T(8,128)(2,1)} %copy-done.14, bf16[32,3200]{1,0:T(8,128)(2,1)} %copy-done.15, ...), custom_call_target="tpu_custom_call" | custom-call | flops 5242880000 | bytes 25395200 | tf_op jit(solution)/shard_map/pallas_call | solution.py:212
  72.6 2.7 %collective-permute-start.21 = (bf16[8,12800]{1,0:T(8,128)(2,1)S(1)}, bf16[8,12800]{1,0:T(8,128)(2,1)S(1)}, u32[]{:S(2)}, u32[]{:S(2)}) collective-permute-start(bf16[8,12800]{1,0:T(8,128)(2,1)S(1)} %multiply_convert_fusion.5.refs_0_), channel_id=1, source_target_pairs={{0,4},{1,5},{2,6},{3,7},{4,0},{5,1},{6,2},{7,3},{8,12},{9,13},{10,... | collective-permute-start | bytes 614408 | tf_op jit(solution)/shard_map/ppermute | solution.py:299
  75.3 1.7 collective-permute-start.22
  77.1 1.6 fusion.53
  78.8 0.7 copy-done.40
  81.3 2.1 collective-permute-start.25
  83.4 0.7 collective-permute-start.30
  84.1 6.2 %collective-permute-done.21.refs_1_ = bf16[8,12800]{1,0:T(8,128)(2,1)S(1)} collective-permute-done((bf16[8,12800]{1,0:T(8,128)(2,1)S(1)}, bf16[8,12800]{1,0:T(8,128)(2,1)S(1)}, u32[]{:S(2)}, u32[]{:S(2)}) %collective-permute-start.21) | collective-permute-done | bytes 204832 | tf_op jit(solution)/shard_map/ppermute | solution.py:299
  90.3 2.1 collective-permute-start.31
  92.4 4.8 %collective-permute-done.25 = bf16[32,3200]{1,0:T(8,128)(2,1)S(1)} collective-permute-done((bf16[32,3200]{1,0:T(8,128)(2,1)S(1)}, bf16[32,3200]{1,0:T(8,128)(2,1)S(1)}, u32[]{:S(2)}, u32[]{:S(2)}) %collective-permute-start.25) | collective-permute-done | bytes 204832 | tf_op jit(solution)/shard_map/ppermute | solution.py:299
  97.7 0.9 collective-permute-done.26.refs_4_
  99.2 0.9 collective-permute-done.29.refs_7_
  100.1 9.6 %shard_map.134 = (bf16[64,1024]{1,0:T(8,128)(2,1)S(1)}, bf16[64,1024]{1,0:T(8,128)(2,1)S(1)}) custom-call(bf16[8,12800]{1,0:T(8,128)(2,1)S(1)} %multiply_convert_fusion.5.refs_0_, bf16[8,12800]{1,0:T(8,128)(2,1)S(1)} %collective-permute-done.21.refs_1_, bf16[8,12800]{1,0:T(8,128)(2,1)S(1)} %collective-permute-done.22.refs_2_, ...), custom_call_target="tpu_custom_call" | custom-call | flops 1677721600 | bytes 29753344 | tf_op jit(solution)/shard_map/pallas_call | solution.py:249
  111.2 3.4 %collective-permute-start.32 = (bf16[8,12800]{1,0:T(8,128)(2,1)S(1)}, bf16[8,12800]{1,0:T(8,128)(2,1)S(1)}, u32[]{:S(2)}, u32[]{:S(2)}) collective-permute-start(bf16[8,12800]{1,0:T(8,128)(2,1)S(1)} %multiply_convert_fusion.4.refs_0_), channel_id=1, source_target_pairs={{0,4},{1,5},{2,6},{3,7},{4,0},{5,1},{6,2},{7,3},{8,12},{9,13},{10,... | collective-permute-start | bytes 614408 | tf_op jit(solution)/shard_map/ppermute | solution.py:299
  114.5 1.7 collective-permute-start.33
  116.3 11.0 %shard_map.135 = (bf16[32,12800]{1,0:T(8,128)(2,1)S(1)}, bf16[32,12800]{1,0:T(8,128)(2,1)S(1)}) custom-call(bf16[64,1024]{1,0:T(8,128)(2,1)S(1)} %get-tuple-element.171.delta, bf16[12800,1024]{1,0:T(8,128)(2,1)} %weight.3), custom_call_target="tpu_custom_call" | custom-call | flops 1677721600 | bytes 29753344 | tf_op jit(solution)/shard_map/pallas_call | solution.py:269
  127.3 2.0 collective-permute-done.32.refs_1_
  130.7 1.3 collective-permute-done.39
  132.2 4.1 %collective-permute-start.40 = (bf16[8,12800]{1,0:T(8,128)(2,1)S(1)}, bf16[8,12800]{1,0:T(8,128)(2,1)S(1)}, u32[]{:S(2)}, u32[]{:S(2)}) collective-permute-start(bf16[8,12800]{1,0:T(8,128)(2,1)S(1)} %get-tuple-element.288), channel_id=1, source_target_pairs={{0,4},{1,5},{2,6},{3,7},{4,0},{5,1},{6,2},{7,3},{8,12},{9,13},{10,... | collective-permute-start | bytes 614408 | tf_op jit(solution)/shard_map/ppermute | solution.py:299
  136.3 2.0 collective-permute-start.41
  138.3 9.8 %shard_map.136 = (bf16[64,1024]{1,0:T(8,128)(2,1)S(1)}, bf16[64,1024]{1,0:T(8,128)(2,1)S(1)}) custom-call(bf16[8,12800]{1,0:T(8,128)(2,1)S(1)} %multiply_convert_fusion.4.refs_0_, bf16[8,12800]{1,0:T(8,128)(2,1)S(1)} %collective-permute-done.32.refs_1_, bf16[8,12800]{1,0:T(8,128)(2,1)S(1)} %collective-permute-done.33.refs_2_, ...), custom_call_target="tpu_custom_call" | custom-call | flops 1677721600 | bytes 29753344 | tf_op jit(solution)/shard_map/pallas_call | solution.py:249
  148.2 2.8 %collective-permute-done.40 = bf16[8,12800]{1,0:T(8,128)(2,1)S(1)} collective-permute-done((bf16[8,12800]{1,0:T(8,128)(2,1)S(1)}, bf16[8,12800]{1,0:T(8,128)(2,1)S(1)}, u32[]{:S(2)}, u32[]{:S(2)}) %collective-permute-start.40) | collective-permute-done | bytes 204832 | tf_op jit(solution)/shard_map/ppermute | solution.py:299
  151.0 0.8 collective-permute-done.42
  152.5 4.2 %collective-permute-start.43 = (bf16[32,3200]{1,0:T(8,128)(2,1)S(1)}, bf16[32,3200]{1,0:T(8,128)(2,1)}, u32[]{:S(2)}, u32[]{:S(2)}) collective-permute-start(bf16[32,3200]{1,0:T(8,128)(2,1)S(1)} %multiply_convert_fusion.2.refs_0_), channel_id=1, source_target_pairs={{0,4},{1,5},{2,6},{3,7},{4,0},{5,1},{6,2},{7,3},{8,12},{9,13},{10,... | collective-permute-start | bytes 614408 | tf_op jit(solution)/shard_map/ppermute | solution.py:299
  156.7 1.8 collective-permute-start.44
  158.6 11.0 %shard_map.137 = (bf16[32,12800]{1,0:T(8,128)(2,1)S(1)}, bf16[32,12800]{1,0:T(8,128)(2,1)S(1)}) custom-call(bf16[64,1024]{1,0:T(8,128)(2,1)S(1)} %get-tuple-element.188.delta, bf16[12800,1024]{1,0:T(8,128)(2,1)} %weight.3), custom_call_target="tpu_custom_call" | custom-call | flops 1677721600 | bytes 29753344 | tf_op jit(solution)/shard_map/pallas_call | solution.py:269
  169.6 2.0 collective-permute-done.43.refs_1_
  174.3 1.3 fusion.55
  175.7 4.1 %collective-permute-start.51 = (bf16[8,12800]{1,0:T(8,128)(2,1)S(1)}, bf16[8,12800]{1,0:T(8,128)(2,1)S(1)}, u32[]{:S(2)}, u32[]{:S(2)}) collective-permute-start(bf16[8,12800]{1,0:T(8,128)(2,1)S(1)} %get-tuple-element.285), channel_id=1, source_target_pairs={{0,4},{1,5},{2,6},{3,7},{4,0},{5,1},{6,2},{7,3},{8,12},{9,13},{10,... | collective-permute-start | bytes 614408 | tf_op jit(solution)/shard_map/ppermute | solution.py:299
  179.8 2.0 collective-permute-start.52
  182.6 14.6 %shard_map.138 = (bf16[128,3200]{1,0:T(8,128)(2,1)}, bf16[128,3200]{1,0:T(8,128)(2,1)}) custom-call(bf16[32,3200]{1,0:T(8,128)(2,1)} %copy-done.11, bf16[32,3200]{1,0:T(8,128)(2,1)} %collective-permute-done.43.refs_1_, bf16[32,3200]{1,0:T(8,128)(2,1)} %collective-permute-done.44.refs_2_, bf16[32,3200]{1,0:T(8,128)(2,1)} %collective-permute-done.45.refs_3_, ...), custom_call_target="tpu_custom_call" | custom-call | flops 5242880000 | bytes 25395200 | tf_op jit(solution)/shard_map/pallas_call | solution.py:212
  198.0 2.4 collective-permute-start.54
  202.3 1.5 collective-permute-start.57
  203.8 1.5 collective-permute-start.58
  205.3 1.4 collective-permute-start.59
  206.8 1.3 fusion.56
  208.2 2.0 collective-permute-start.55
  210.3 2.3 collective-permute-start.61
  212.6 5.5 %collective-permute-done.55.refs_2_ = bf16[32,3200]{1,0:T(8,128)(2,1)S(1)} collective-permute-done((bf16[32,3200]{1,0:T(8,128)(2,1)S(1)}, bf16[32,3200]{1,0:T(8,128)(2,1)S(1)}, u32[]{:S(2)}, u32[]{:S(2)}) %collective-permute-start.55) | collective-permute-done | bytes 204832 | tf_op jit(solution)/shard_map/ppermute | solution.py:299
  218.1 3.1 %collective-permute-done.61 = bf16[32,3200]{1,0:T(8,128)(2,1)S(1)} collective-permute-done((bf16[32,3200]{1,0:T(8,128)(2,1)S(1)}, bf16[32,3200]{1,0:T(8,128)(2,1)S(1)}, u32[]{:S(2)}, u32[]{:S(2)}) %collective-permute-start.61) | collective-permute-done | bytes 204832 | tf_op jit(solution)/shard_map/ppermute | solution.py:299
  222.7 1.8 collective-permute-start.67
  225.4 14.6 %shard_map.139 = (bf16[128,3200]{1,0:T(8,128)(2,1)}, bf16[128,3200]{1,0:T(8,128)(2,1)}) custom-call(bf16[32,3200]{1,0:T(8,128)(2,1)} %copy-done.10, bf16[32,3200]{1,0:T(8,128)(2,1)} %copy-done.19, bf16[32,3200]{1,0:T(8,128)(2,1)} %copy-done.21, bf16[32,3200]{1,0:T(8,128)(2,1)} %collective-permute-done.60.refs_3_, bf16[32,3200]{1,0:T(8,128)(2,1)} %copy-done.31, ...), custom_call_target="tpu_custom_call" | custom-call | flops 5242880000 | bytes 25395200 | tf_op jit(solution)/shard_map/pallas_call | solution.py:212
  240.2 2.4 collective-permute-done.68
  242.9 1.6 collective-permute-start.69
  244.5 2.0 collective-permute-start.70
  246.4 2.2 fusion
  248.7 11.8 %collective-permute-done.69 = bf16[32,3200]{1,0:T(8,128)(2,1)S(1)} collective-permute-done((bf16[32,3200]{1,0:T(8,128)(2,1)S(1)}, bf16[32,3200]{1,0:T(8,128)(2,1)S(1)}, u32[]{:S(2)}, u32[]{:S(2)}) %collective-permute-start.69) | collective-permute-done | bytes 204832 | tf_op jit(solution)/shard_map/ppermute | solution.py:299
  261.9 0.8 pad_maximum_fusion
  (283 shorter events, 27.0 us)
Async XLA Ops:
  2.8 19.0 %collective-permute-start = (bf16[32,3200]{1,0:T(8,128)(2,1)}, bf16[32,3200]{1,0:T(8,128)(2,1)S(1)}, u32[]{:S(2)}, u32[]{:S(2)}) collective-permute-start(bf16[32,3200]{1,0:T(8,128)(2,1)} %get-tuple-element.125.refs_0_), channel_id=1, source_target_pairs={{0,4},{1,5},{2,6},{3,7},{4,0},{5,1},{6,2},{7,3},{8,12},{9,13},{10,... | collective-permute-start | bytes 614408 | tf_op jit(solution)/shard_map/ppermute | solution.py:299
  6.9 15.0 %collective-permute-start.1 = (bf16[32,3200]{1,0:T(8,128)(2,1)}, bf16[32,3200]{1,0:T(8,128)(2,1)S(1)}, u32[]{:S(2)}, u32[]{:S(2)}) collective-permute-start(bf16[32,3200]{1,0:T(8,128)(2,1)} %get-tuple-element.125.refs_0_), channel_id=1, source_target_pairs={{0,6},{1,7},{2,4},{3,5},{4,2},{5,3},{6,0},{7,1},{8,14},{9,15},{10,... | collective-permute-start | bytes 614408 | tf_op jit(solution)/shard_map/ppermute | solution.py:299
  8.2 14.1 %collective-permute-start.2 = (bf16[32,3200]{1,0:T(8,128)(2,1)}, bf16[32,3200]{1,0:T(8,128)(2,1)S(1)}, u32[]{:S(2)}, u32[]{:S(2)}) collective-permute-start(bf16[32,3200]{1,0:T(8,128)(2,1)} %get-tuple-element.125.refs_0_), channel_id=1, source_target_pairs={{0,2},{1,3},{2,0},{3,1},{4,6},{5,7},{6,4},{7,5},{8,10},{9,11},{10,... | collective-permute-start | bytes 614408 | tf_op jit(solution)/shard_map/ppermute | solution.py:299
  11.2 4.4 %collective-permute-start.3 = (bf16[32,1024]{1,0:T(8,128)(2,1)S(1)}, bf16[32,1024]{1,0:T(8,128)(2,1)S(1)}, u32[]{:S(2)}, u32[]{:S(2)}) collective-permute-start(bf16[32,1024]{1,0:T(8,128)(2,1)S(1)} %get-tuple-element.309), channel_id=1, source_target_pairs={{0,24},{8,0},{16,8},{24,16},{1,25},{9,1},{17,9},{25,17},{2,26},{10... | collective-permute-start | bytes 196616 | tf_op jit(solution)/shard_map/ppermute | solution.py:376
  13.7 4.3 %collective-permute-start.4 = (bf16[32,1024]{1,0:T(8,128)(2,1)S(1)}, bf16[32,1024]{1,0:T(8,128)(2,1)S(1)}, u32[]{:S(2)}, u32[]{:S(2)}) collective-permute-start(bf16[32,1024]{1,0:T(8,128)(2,1)S(1)} %get-tuple-element.308), channel_id=1, source_target_pairs={{0,16},{8,24},{16,0},{24,8},{1,17},{9,25},{17,1},{25,9},{2,18},{10... | collective-permute-start | bytes 196616 | tf_op jit(solution)/shard_map/ppermute | solution.py:376
  15.6 5.6 %collective-permute-start.5 = (bf16[32,1024]{1,0:T(8,128)(2,1)S(1)}, bf16[32,1024]{1,0:T(8,128)(2,1)S(1)}, u32[]{:S(2)}, u32[]{:S(2)}) collective-permute-start(bf16[32,1024]{1,0:T(8,128)(2,1)S(1)} %get-tuple-element.307), channel_id=1, source_target_pairs={{0,8},{8,16},{16,24},{24,0},{1,9},{9,17},{17,25},{25,1},{2,10},{10... | collective-permute-start | bytes 196616 | tf_op jit(solution)/shard_map/ppermute | solution.py:376
  22.4 6.8 %collective-permute-start.6 = (bf16[32,3200]{1,0:T(8,128)(2,1)S(1)}, bf16[32,3200]{1,0:T(8,128)(2,1)S(1)}, u32[]{:S(2)}, u32[]{:S(2)}) collective-permute-start(bf16[32,3200]{1,0:T(8,128)(2,1)S(1)} %copy-done.16), channel_id=1, source_target_pairs={{0,1},{1,0},{2,3},{3,2},{4,5},{5,4},{6,7},{7,6},{8,9},{9,8},{10,11... | collective-permute-start | bytes 614408 | tf_op jit(solution)/shard_map/ppermute | solution.py:305
  22.4 7.2 %collective-permute-start.7 = (bf16[32,3200]{1,0:T(8,128)(2,1)S(1)}, bf16[32,3200]{1,0:T(8,128)(2,1)S(1)}, u32[]{:S(2)}, u32[]{:S(2)}) collective-permute-start(bf16[32,3200]{1,0:T(8,128)(2,1)S(1)} %collective-permute-done.refs_1_), channel_id=1, source_target_pairs={{0,1},{1,0},{2,3},{3,2},{4,5},{5,4},{6,7},{7,6},{8,9},{9,8},{10,11... | collective-permute-start | bytes 614408 | tf_op jit(solution)/shard_map/ppermute | solution.py:305
  22.9 7.2 %collective-permute-start.8 = (bf16[32,3200]{1,0:T(8,128)(2,1)S(1)}, bf16[32,3200]{1,0:T(8,128)(2,1)S(1)}, u32[]{:S(2)}, u32[]{:S(2)}) collective-permute-start(bf16[32,3200]{1,0:T(8,128)(2,1)S(1)} %collective-permute-done.1.refs_2_), channel_id=1, source_target_pairs={{0,1},{1,0},{2,3},{3,2},{4,5},{5,4},{6,7},{7,6},{8,9},{9,8},{10,11... | collective-permute-start | bytes 614408 | tf_op jit(solution)/shard_map/ppermute | solution.py:305
  23.0 7.1 %collective-permute-start.9 = (bf16[32,3200]{1,0:T(8,128)(2,1)S(1)}, bf16[32,3200]{1,0:T(8,128)(2,1)S(1)}, u32[]{:S(2)}, u32[]{:S(2)}) collective-permute-start(bf16[32,3200]{1,0:T(8,128)(2,1)S(1)} %collective-permute-done.2.refs_3_), channel_id=1, source_target_pairs={{0,1},{1,0},{2,3},{3,2},{4,5},{5,4},{6,7},{7,6},{8,9},{9,8},{10,11... | collective-permute-start | bytes 614408 | tf_op jit(solution)/shard_map/ppermute | solution.py:305
  23.5 22.2 %collective-permute-start.10 = (bf16[32,3200]{1,0:T(8,128)(2,1)}, bf16[32,3200]{1,0:T(8,128)(2,1)S(1)}, u32[]{:S(2)}, u32[]{:S(2)}) collective-permute-start(bf16[32,3200]{1,0:T(8,128)(2,1)} %get-tuple-element.132.refs_0_), channel_id=1, source_target_pairs={{0,4},{1,5},{2,6},{3,7},{4,0},{5,1},{6,2},{7,3},{8,12},{9,13},{10,... | collective-permute-start | bytes 614408 | tf_op jit(solution)/shard_map/ppermute | solution.py:299
  29.1 16.5 %collective-permute-start.11 = (bf16[32,3200]{1,0:T(8,128)(2,1)}, bf16[32,3200]{1,0:T(8,128)(2,1)S(1)}, u32[]{:S(2)}, u32[]{:S(2)}) collective-permute-start(bf16[32,3200]{1,0:T(8,128)(2,1)} %get-tuple-element.132.refs_0_), channel_id=1, source_target_pairs={{0,6},{1,7},{2,4},{3,5},{4,2},{5,3},{6,0},{7,1},{8,14},{9,15},{10,... | collective-permute-start | bytes 614408 | tf_op jit(solution)/shard_map/ppermute | solution.py:299
  29.7 16.0 %collective-permute-start.12 = (bf16[32,3200]{1,0:T(8,128)(2,1)}, bf16[32,3200]{1,0:T(8,128)(2,1)S(1)}, u32[]{:S(2)}, u32[]{:S(2)}) collective-permute-start(bf16[32,3200]{1,0:T(8,128)(2,1)} %get-tuple-element.132.refs_0_), channel_id=1, source_target_pairs={{0,2},{1,3},{2,0},{3,1},{4,6},{5,7},{6,4},{7,5},{8,10},{9,11},{10,... | collective-permute-start | bytes 614408 | tf_op jit(solution)/shard_map/ppermute | solution.py:299
  45.7 2.6 collective-permute-start.17
  45.9 7.3 %collective-permute-start.13 = (bf16[32,3200]{1,0:T(8,128)(2,1)}, bf16[32,3200]{1,0:T(8,128)(2,1)S(1)}, u32[]{:S(2)}, u32[]{:S(2)}) collective-permute-start(bf16[32,3200]{1,0:T(8,128)(2,1)} %get-tuple-element.132.refs_0_), channel_id=1, source_target_pairs={{0,1},{1,0},{2,3},{3,2},{4,5},{5,4},{6,7},{7,6},{8,9},{9,8},{10,11... | collective-permute-start | bytes 614408 | tf_op jit(solution)/shard_map/ppermute | solution.py:305
  46.4 8.5 %collective-permute-start.14 = (bf16[32,3200]{1,0:T(8,128)(2,1)S(1)}, bf16[32,3200]{1,0:T(8,128)(2,1)S(1)}, u32[]{:S(2)}, u32[]{:S(2)}) collective-permute-start(bf16[32,3200]{1,0:T(8,128)(2,1)S(1)} %collective-permute-done.10.refs_1_), channel_id=1, source_target_pairs={{0,1},{1,0},{2,3},{3,2},{4,5},{5,4},{6,7},{7,6},{8,9},{9,8},{10,11... | collective-permute-start | bytes 614408 | tf_op jit(solution)/shard_map/ppermute | solution.py:305
  46.5 8.5 %collective-permute-start.15 = (bf16[32,3200]{1,0:T(8,128)(2,1)S(1)}, bf16[32,3200]{1,0:T(8,128)(2,1)S(1)}, u32[]{:S(2)}, u32[]{:S(2)}) collective-permute-start(bf16[32,3200]{1,0:T(8,128)(2,1)S(1)} %collective-permute-done.11.refs_2_), channel_id=1, source_target_pairs={{0,1},{1,0},{2,3},{3,2},{4,5},{5,4},{6,7},{7,6},{8,9},{9,8},{10,11... | collective-permute-start | bytes 614408 | tf_op jit(solution)/shard_map/ppermute | solution.py:305
  47.0 8.1 %collective-permute-start.16 = (bf16[32,3200]{1,0:T(8,128)(2,1)S(1)}, bf16[32,3200]{1,0:T(8,128)(2,1)S(1)}, u32[]{:S(2)}, u32[]{:S(2)}) collective-permute-start(bf16[32,3200]{1,0:T(8,128)(2,1)S(1)} %collective-permute-done.12.refs_3_), channel_id=1, source_target_pairs={{0,1},{1,0},{2,3},{3,2},{4,5},{5,4},{6,7},{7,6},{8,9},{9,8},{10,11... | collective-permute-start | bytes 614408 | tf_op jit(solution)/shard_map/ppermute | solution.py:305
  49.7 21.5 %collective-permute-start.18 = (bf16[32,3200]{1,0:T(8,128)(2,1)S(1)}, bf16[32,3200]{1,0:T(8,128)(2,1)S(1)}, u32[]{:S(2)}, u32[]{:S(2)}) collective-permute-start(bf16[32,3200]{1,0:T(8,128)(2,1)S(1)} %get-tuple-element.294), channel_id=1, source_target_pairs={{0,4},{1,5},{2,6},{3,7},{4,0},{5,1},{6,2},{7,3},{8,12},{9,13},{10,... | collective-permute-start | bytes 614408 | tf_op jit(solution)/shard_map/ppermute | solution.py:299
  53.2 18.1 %collective-permute-start.19 = (bf16[32,3200]{1,0:T(8,128)(2,1)S(1)}, bf16[32,3200]{1,0:T(8,128)(2,1)S(1)}, u32[]{:S(2)}, u32[]{:S(2)}) collective-permute-start(bf16[32,3200]{1,0:T(8,128)(2,1)S(1)} %get-tuple-element.293), channel_id=1, source_target_pairs={{0,6},{1,7},{2,4},{3,5},{4,2},{5,3},{6,0},{7,1},{8,14},{9,15},{10,... | collective-permute-start | bytes 614408 | tf_op jit(solution)/shard_map/ppermute | solution.py:299
  54.9 16.3 %collective-permute-start.20 = (bf16[32,3200]{1,0:T(8,128)(2,1)S(1)}, bf16[32,3200]{1,0:T(8,128)(2,1)S(1)}, u32[]{:S(2)}, u32[]{:S(2)}) collective-permute-start(bf16[32,3200]{1,0:T(8,128)(2,1)S(1)} %get-tuple-element.292), channel_id=1, source_target_pairs={{0,2},{1,3},{2,0},{3,1},{4,6},{5,7},{6,4},{7,5},{8,10},{9,11},{10,... | collective-permute-start | bytes 614408 | tf_op jit(solution)/shard_map/ppermute | solution.py:299
  71.1 6.0 %collective-permute-start.24 = (bf16[128,3200]{1,0:T(8,128)(2,1)}, bf16[128,3200]{1,0:T(8,128)(2,1)}, u32[]{:S(2)}, u32[]{:S(2)}) collective-permute-start(bf16[128,3200]{1,0:T(8,128)(2,1)} %get-tuple-element.149), channel_id=1, source_target_pairs={{0,1},{1,0},{2,3},{3,2},{4,5},{5,4},{6,7},{7,6},{8,9},{9,8},{10,11... | collective-permute-start | bytes 2457608 | tf_op jit(solution)/shard_map/ppermute | solution.py:312
  72.6 17.7 %collective-permute-start.21 = (bf16[8,12800]{1,0:T(8,128)(2,1)S(1)}, bf16[8,12800]{1,0:T(8,128)(2,1)S(1)}, u32[]{:S(2)}, u32[]{:S(2)}) collective-permute-start(bf16[8,12800]{1,0:T(8,128)(2,1)S(1)} %multiply_convert_fusion.5.refs_0_), channel_id=1, source_target_pairs={{0,4},{1,5},{2,6},{3,7},{4,0},{5,1},{6,2},{7,3},{8,12},{9,13},{10,... | collective-permute-start | bytes 614408 | tf_op jit(solution)/shard_map/ppermute | solution.py:299
  75.3 17.1 %collective-permute-start.22 = (bf16[8,12800]{1,0:T(8,128)(2,1)S(1)}, bf16[8,12800]{1,0:T(8,128)(2,1)S(1)}, u32[]{:S(2)}, u32[]{:S(2)}) collective-permute-start(bf16[8,12800]{1,0:T(8,128)(2,1)S(1)} %multiply_convert_fusion.5.refs_0_), channel_id=1, source_target_pairs={{0,6},{1,7},{2,4},{3,5},{4,2},{5,3},{6,0},{7,1},{8,14},{9,15},{10,... | collective-permute-start | bytes 614408 | tf_op jit(solution)/shard_map/ppermute | solution.py:299
  77.1 15.3 %collective-permute-start.23 = (bf16[8,12800]{1,0:T(8,128)(2,1)S(1)}, bf16[8,12800]{1,0:T(8,128)(2,1)S(1)}, u32[]{:S(2)}, u32[]{:S(2)}) collective-permute-start(bf16[8,12800]{1,0:T(8,128)(2,1)S(1)} %multiply_convert_fusion.5.refs_0_), channel_id=1, source_target_pairs={{0,2},{1,3},{2,0},{3,1},{4,6},{5,7},{6,4},{7,5},{8,10},{9,11},{10,... | collective-permute-start | bytes 614408 | tf_op jit(solution)/shard_map/ppermute | solution.py:299
  81.3 15.9 %collective-permute-start.25 = (bf16[32,3200]{1,0:T(8,128)(2,1)S(1)}, bf16[32,3200]{1,0:T(8,128)(2,1)S(1)}, u32[]{:S(2)}, u32[]{:S(2)}) collective-permute-start(bf16[32,3200]{1,0:T(8,128)(2,1)S(1)} %get-tuple-element.154), channel_id=1, source_target_pairs={{0,2},{1,3},{2,0},{3,1},{4,6},{5,7},{6,4},{7,5},{8,10},{9,11},{10,... | collective-permute-start | bytes 614408 | tf_op jit(solution)/shard_map/ppermute | solution.py:299
  83.4 26.3 %collective-permute-start.30 = (bf16[32,3200]{1,0:T(8,128)(2,1)S(1)}, bf16[32,3200]{1,0:T(8,128)(2,1)S(1)}, u32[]{:S(2)}, u32[]{:S(2)}) collective-permute-start(bf16[32,3200]{1,0:T(8,128)(2,1)S(1)} %get-tuple-element.163), channel_id=1, source_target_pairs={{0,4},{1,5},{2,6},{3,7},{4,0},{5,1},{6,2},{7,3},{8,12},{9,13},{10,... | collective-permute-start | bytes 614408 | tf_op jit(solution)/shard_map/ppermute | solution.py:299
  90.3 19.4 %collective-permute-start.31 = (bf16[32,3200]{1,0:T(8,128)(2,1)S(1)}, bf16[32,3200]{1,0:T(8,128)(2,1)S(1)}, u32[]{:S(2)}, u32[]{:S(2)}) collective-permute-start(bf16[32,3200]{1,0:T(8,128)(2,1)S(1)} %get-tuple-element.164), channel_id=1, source_target_pairs={{0,6},{1,7},{2,4},{3,5},{4,2},{5,3},{6,0},{7,1},{8,14},{9,15},{10,... | collective-permute-start | bytes 614408 | tf_op jit(solution)/shard_map/ppermute | solution.py:299
  111.2 18.1 %collective-permute-start.32 = (bf16[8,12800]{1,0:T(8,128)(2,1)S(1)}, bf16[8,12800]{1,0:T(8,128)(2,1)S(1)}, u32[]{:S(2)}, u32[]{:S(2)}) collective-permute-start(bf16[8,12800]{1,0:T(8,128)(2,1)S(1)} %multiply_convert_fusion.4.refs_0_), channel_id=1, source_target_pairs={{0,4},{1,5},{2,6},{3,7},{4,0},{5,1},{6,2},{7,3},{8,12},{9,13},{10,... | collective-permute-start | bytes 614408 | tf_op jit(solution)/shard_map/ppermute | solution.py:299
  114.5 14.8 %collective-permute-start.33 = (bf16[8,12800]{1,0:T(8,128)(2,1)S(1)}, bf16[8,12800]{1,0:T(8,128)(2,1)S(1)}, u32[]{:S(2)}, u32[]{:S(2)}) collective-permute-start(bf16[8,12800]{1,0:T(8,128)(2,1)S(1)} %multiply_convert_fusion.4.refs_0_), channel_id=1, source_target_pairs={{0,6},{1,7},{2,4},{3,5},{4,2},{5,3},{6,0},{7,1},{8,14},{9,15},{10,... | collective-permute-start | bytes 614408 | tf_op jit(solution)/shard_map/ppermute | solution.py:299
  116.3 13.4 %collective-permute-start.34 = (bf16[8,12800]{1,0:T(8,128)(2,1)S(1)}, bf16[8,12800]{1,0:T(8,128)(2,1)S(1)}, u32[]{:S(2)}, u32[]{:S(2)}) collective-permute-start(bf16[8,12800]{1,0:T(8,128)(2,1)S(1)} %multiply_convert_fusion.4.refs_0_), channel_id=1, source_target_pairs={{0,2},{1,3},{2,0},{3,1},{4,6},{5,7},{6,4},{7,5},{8,10},{9,11},{10,... | collective-permute-start | bytes 614408 | tf_op jit(solution)/shard_map/ppermute | solution.py:299
  129.6 6.7 %collective-permute-start.35 = (bf16[8,12800]{1,0:T(8,128)(2,1)S(1)}, bf16[8,12800]{1,0:T(8,128)(2,1)S(1)}, u32[]{:S(2)}, u32[]{:S(2)}) collective-permute-start(bf16[8,12800]{1,0:T(8,128)(2,1)S(1)} %multiply_convert_fusion.4.refs_0_), channel_id=1, source_target_pairs={{0,1},{1,0},{2,3},{3,2},{4,5},{5,4},{6,7},{7,6},{8,9},{9,8},{10,11... | collective-permute-start | bytes 614408 | tf_op jit(solution)/shard_map/ppermute | solution.py:305
  130.1 8.1 %collective-permute-start.36 = (bf16[8,12800]{1,0:T(8,128)(2,1)S(1)}, bf16[8,12800]{1,0:T(8,128)(2,1)S(1)}, u32[]{:S(2)}, u32[]{:S(2)}) collective-permute-start(bf16[8,12800]{1,0:T(8,128)(2,1)S(1)} %collective-permute-done.32.refs_1_), channel_id=1, source_target_pairs={{0,1},{1,0},{2,3},{3,2},{4,5},{5,4},{6,7},{7,6},{8,9},{9,8},{10,11... | collective-permute-start | bytes 614408 | tf_op jit(solution)/shard_map/ppermute | solution.py:305
  130.1 8.1 %collective-permute-start.37 = (bf16[8,12800]{1,0:T(8,128)(2,1)S(1)}, bf16[8,12800]{1,0:T(8,128)(2,1)S(1)}, u32[]{:S(2)}, u32[]{:S(2)}) collective-permute-start(bf16[8,12800]{1,0:T(8,128)(2,1)S(1)} %collective-permute-done.33.refs_2_), channel_id=1, source_target_pairs={{0,1},{1,0},{2,3},{3,2},{4,5},{5,4},{6,7},{7,6},{8,9},{9,8},{10,11... | collective-permute-start | bytes 614408 | tf_op jit(solution)/shard_map/ppermute | solution.py:305
  130.7 7.6 %collective-permute-start.38 = (bf16[8,12800]{1,0:T(8,128)(2,1)S(1)}, bf16[8,12800]{1,0:T(8,128)(2,1)S(1)}, u32[]{:S(2)}, u32[]{:S(2)}) collective-permute-start(bf16[8,12800]{1,0:T(8,128)(2,1)S(1)} %collective-permute-done.34.refs_3_), channel_id=1, source_target_pairs={{0,1},{1,0},{2,3},{3,2},{4,5},{5,4},{6,7},{7,6},{8,9},{9,8},{10,11... | collective-permute-start | bytes 614408 | tf_op jit(solution)/shard_map/ppermute | solution.py:305
  132.2 18.8 %collective-permute-start.40 = (bf16[8,12800]{1,0:T(8,128)(2,1)S(1)}, bf16[8,12800]{1,0:T(8,128)(2,1)S(1)}, u32[]{:S(2)}, u32[]{:S(2)}) collective-permute-start(bf16[8,12800]{1,0:T(8,128)(2,1)S(1)} %get-tuple-element.288), channel_id=1, source_target_pairs={{0,4},{1,5},{2,6},{3,7},{4,0},{5,1},{6,2},{7,3},{8,12},{9,13},{10,... | collective-permute-start | bytes 614408 | tf_op jit(solution)/shard_map/ppermute | solution.py:299
  136.3 14.7 %collective-permute-start.41 = (bf16[8,12800]{1,0:T(8,128)(2,1)S(1)}, bf16[8,12800]{1,0:T(8,128)(2,1)S(1)}, u32[]{:S(2)}, u32[]{:S(2)}) collective-permute-start(bf16[8,12800]{1,0:T(8,128)(2,1)S(1)} %get-tuple-element.287), channel_id=1, source_target_pairs={{0,6},{1,7},{2,4},{3,5},{4,2},{5,3},{6,0},{7,1},{8,14},{9,15},{10,... | collective-permute-start | bytes 614408 | tf_op jit(solution)/shard_map/ppermute | solution.py:299
  138.3 13.5 %collective-permute-start.42 = (bf16[8,12800]{1,0:T(8,128)(2,1)S(1)}, bf16[8,12800]{1,0:T(8,128)(2,1)S(1)}, u32[]{:S(2)}, u32[]{:S(2)}) collective-permute-start(bf16[8,12800]{1,0:T(8,128)(2,1)S(1)} %get-tuple-element.286), channel_id=1, source_target_pairs={{0,2},{1,3},{2,0},{3,1},{4,6},{5,7},{6,4},{7,5},{8,10},{9,11},{10,... | collective-permute-start | bytes 614408 | tf_op jit(solution)/shard_map/ppermute | solution.py:299
  152.5 19.1 %collective-permute-start.43 = (bf16[32,3200]{1,0:T(8,128)(2,1)S(1)}, bf16[32,3200]{1,0:T(8,128)(2,1)}, u32[]{:S(2)}, u32[]{:S(2)}) collective-permute-start(bf16[32,3200]{1,0:T(8,128)(2,1)S(1)} %multiply_convert_fusion.2.refs_0_), channel_id=1, source_target_pairs={{0,4},{1,5},{2,6},{3,7},{4,0},{5,1},{6,2},{7,3},{8,12},{9,13},{10,... | collective-permute-start | bytes 614408 | tf_op jit(solution)/shard_map/ppermute | solution.py:299
  156.7 14.9 %collective-permute-start.44 = (bf16[32,3200]{1,0:T(8,128)(2,1)S(1)}, bf16[32,3200]{1,0:T(8,128)(2,1)}, u32[]{:S(2)}, u32[]{:S(2)}) collective-permute-start(bf16[32,3200]{1,0:T(8,128)(2,1)S(1)} %multiply_convert_fusion.2.refs_0_), channel_id=1, source_target_pairs={{0,6},{1,7},{2,4},{3,5},{4,2},{5,3},{6,0},{7,1},{8,14},{9,15},{10,... | collective-permute-start | bytes 614408 | tf_op jit(solution)/shard_map/ppermute | solution.py:299
  158.6 13.3 %collective-permute-start.45 = (bf16[32,3200]{1,0:T(8,128)(2,1)S(1)}, bf16[32,3200]{1,0:T(8,128)(2,1)}, u32[]{:S(2)}, u32[]{:S(2)}) collective-permute-start(bf16[32,3200]{1,0:T(8,128)(2,1)S(1)} %multiply_convert_fusion.2.refs_0_), channel_id=1, source_target_pairs={{0,2},{1,3},{2,0},{3,1},{4,6},{5,7},{6,4},{7,5},{8,10},{9,11},{10,... | collective-permute-start | bytes 614408 | tf_op jit(solution)/shard_map/ppermute | solution.py:299
  172.9 6.9 %collective-permute-start.46 = (bf16[32,3200]{1,0:T(8,128)(2,1)S(1)}, bf16[32,3200]{1,0:T(8,128)(2,1)S(1)}, u32[]{:S(2)}, u32[]{:S(2)}) collective-permute-start(bf16[32,3200]{1,0:T(8,128)(2,1)S(1)} %multiply_convert_fusion.2.refs_0_), channel_id=1, source_target_pairs={{0,1},{1,0},{2,3},{3,2},{4,5},{5,4},{6,7},{7,6},{8,9},{9,8},{10,11... | collective-permute-start | bytes 614408 | tf_op jit(solution)/shard_map/ppermute | solution.py:305
  173.5 8.3 %collective-permute-start.47 = (bf16[32,3200]{1,0:T(8,128)(2,1)}, bf16[32,3200]{1,0:T(8,128)(2,1)S(1)}, u32[]{:S(2)}, u32[]{:S(2)}) collective-permute-start(bf16[32,3200]{1,0:T(8,128)(2,1)} %collective-permute-done.43.refs_1_), channel_id=1, source_target_pairs={{0,1},{1,0},{2,3},{3,2},{4,5},{5,4},{6,7},{7,6},{8,9},{9,8},{10,11... | collective-permute-start | bytes 614408 | tf_op jit(solution)/shard_map/ppermute | solution.py:305
  173.6 8.2 %collective-permute-start.48 = (bf16[32,3200]{1,0:T(8,128)(2,1)}, bf16[32,3200]{1,0:T(8,128)(2,1)S(1)}, u32[]{:S(2)}, u32[]{:S(2)}) collective-permute-start(bf16[32,3200]{1,0:T(8,128)(2,1)} %collective-permute-done.44.refs_2_), channel_id=1, source_target_pairs={{0,1},{1,0},{2,3},{3,2},{4,5},{5,4},{6,7},{7,6},{8,9},{9,8},{10,11... | collective-permute-start | bytes 614408 | tf_op jit(solution)/shard_map/ppermute | solution.py:305
  174.0 7.8 %collective-permute-start.49 = (bf16[32,3200]{1,0:T(8,128)(2,1)}, bf16[32,3200]{1,0:T(8,128)(2,1)S(1)}, u32[]{:S(2)}, u32[]{:S(2)}) collective-permute-start(bf16[32,3200]{1,0:T(8,128)(2,1)} %collective-permute-done.45.refs_3_), channel_id=1, source_target_pairs={{0,1},{1,0},{2,3},{3,2},{4,5},{5,4},{6,7},{7,6},{8,9},{9,8},{10,11... | collective-permute-start | bytes 614408 | tf_op jit(solution)/shard_map/ppermute | solution.py:305
  175.7 21.6 %collective-permute-start.51 = (bf16[8,12800]{1,0:T(8,128)(2,1)S(1)}, bf16[8,12800]{1,0:T(8,128)(2,1)S(1)}, u32[]{:S(2)}, u32[]{:S(2)}) collective-permute-start(bf16[8,12800]{1,0:T(8,128)(2,1)S(1)} %get-tuple-element.285), channel_id=1, source_target_pairs={{0,4},{1,5},{2,6},{3,7},{4,0},{5,1},{6,2},{7,3},{8,12},{9,13},{10,... | collective-permute-start | bytes 614408 | tf_op jit(solution)/shard_map/ppermute | solution.py:299
  179.8 17.5 %collective-permute-start.52 = (bf16[8,12800]{1,0:T(8,128)(2,1)S(1)}, bf16[8,12800]{1,0:T(8,128)(2,1)S(1)}, u32[]{:S(2)}, u32[]{:S(2)}) collective-permute-start(bf16[8,12800]{1,0:T(8,128)(2,1)S(1)} %get-tuple-element.284), channel_id=1, source_target_pairs={{0,6},{1,7},{2,4},{3,5},{4,2},{5,3},{6,0},{7,1},{8,14},{9,15},{10,... | collective-permute-start | bytes 614408 | tf_op jit(solution)/shard_map/ppermute | solution.py:299
  181.8 15.6 %collective-permute-start.53 = (bf16[8,12800]{1,0:T(8,128)(2,1)S(1)}, bf16[8,12800]{1,0:T(8,128)(2,1)S(1)}, u32[]{:S(2)}, u32[]{:S(2)}) collective-permute-start(bf16[8,12800]{1,0:T(8,128)(2,1)S(1)} %get-tuple-element.283), channel_id=1, source_target_pairs={{0,2},{1,3},{2,0},{3,1},{4,6},{5,7},{6,4},{7,5},{8,10},{9,11},{10,... | collective-permute-start | bytes 614408 | tf_op jit(solution)/shard_map/ppermute | solution.py:299
  197.2 8.1 %collective-permute-start.56 = (bf16[128,3200]{1,0:T(8,128)(2,1)}, bf16[128,3200]{1,0:T(8,128)(2,1)}, u32[]{:S(2)}, u32[]{:S(2)}) collective-permute-start(bf16[128,3200]{1,0:T(8,128)(2,1)} %get-tuple-element.209), channel_id=1, source_target_pairs={{0,1},{1,0},{2,3},{3,2},{4,5},{5,4},{6,7},{7,6},{8,9},{9,8},{10,11... | collective-permute-start | bytes 2457608 | tf_op jit(solution)/shard_map/ppermute | solution.py:312
  198.0 14.6 %collective-permute-start.54 = (bf16[32,3200]{1,0:T(8,128)(2,1)S(1)}, bf16[32,3200]{1,0:T(8,128)(2,1)S(1)}, u32[]{:S(2)}, u32[]{:S(2)}) collective-permute-start(bf16[32,3200]{1,0:T(8,128)(2,1)S(1)} %multiply_convert_fusion.refs_0_), channel_id=1, source_target_pairs={{0,4},{1,5},{2,6},{3,7},{4,0},{5,1},{6,2},{7,3},{8,12},{9,13},{10,... | collective-permute-start | bytes 614408 | tf_op jit(solution)/shard_map/ppermute | solution.py:299
  200.4 9.8 %collective-permute-start.60 = (bf16[32,3200]{1,0:T(8,128)(2,1)S(1)}, bf16[32,3200]{1,0:T(8,128)(2,1)}, u32[]{:S(2)}, u32[]{:S(2)}) collective-permute-start(bf16[32,3200]{1,0:T(8,128)(2,1)S(1)} %multiply_convert_fusion.refs_0_), channel_id=1, source_target_pairs={{0,2},{1,3},{2,0},{3,1},{4,6},{5,7},{6,4},{7,5},{8,10},{9,11},{10,... | collective-permute-start | bytes 614408 | tf_op jit(solution)/shard_map/ppermute | solution.py:299
  202.3 5.9 %collective-permute-start.57 = (bf16[32,1024]{1,0:T(8,128)(2,1)S(1)}, bf16[32,1024]{1,0:T(8,128)(2,1)S(1)}, u32[]{:S(2)}, u32[]{:S(2)}) collective-permute-start(bf16[32,1024]{1,0:T(8,128)(2,1)S(1)} %get-tuple-element.303), channel_id=1, source_target_pairs={{0,8},{8,16},{16,24},{24,0},{1,9},{9,17},{17,25},{25,1},{2,10},{10... | collective-permute-start | bytes 196616 | tf_op jit(solution)/shard_map/ppermute | solution.py:445
  203.8 6.4 %collective-permute-start.58 = (bf16[32,1024]{1,0:T(8,128)(2,1)S(1)}, bf16[32,1024]{1,0:T(8,128)(2,1)S(1)}, u32[]{:S(2)}, u32[]{:S(2)}) collective-permute-start(bf16[32,1024]{1,0:T(8,128)(2,1)S(1)} %get-tuple-element.302), channel_id=1, source_target_pairs={{0,16},{8,24},{16,0},{24,8},{1,17},{9,25},{17,1},{25,9},{2,18},{10... | collective-permute-start | bytes 196616 | tf_op jit(solution)/shard_map/ppermute | solution.py:445
  205.3 4.9 %collective-permute-start.59 = (bf16[32,1024]{1,0:T(8,128)(2,1)S(1)}, bf16[32,1024]{1,0:T(8,128)(2,1)S(1)}, u32[]{:S(2)}, u32[]{:S(2)}) collective-permute-start(bf16[32,1024]{1,0:T(8,128)(2,1)S(1)} %get-tuple-element.301), channel_id=1, source_target_pairs={{0,24},{8,0},{16,8},{24,16},{1,25},{9,1},{17,9},{25,17},{2,26},{10... | collective-permute-start | bytes 196616 | tf_op jit(solution)/shard_map/ppermute | solution.py:445
  208.2 9.9 %collective-permute-start.55 = (bf16[32,3200]{1,0:T(8,128)(2,1)S(1)}, bf16[32,3200]{1,0:T(8,128)(2,1)S(1)}, u32[]{:S(2)}, u32[]{:S(2)}) collective-permute-start(bf16[32,3200]{1,0:T(8,128)(2,1)S(1)} %multiply_convert_fusion.refs_0_), channel_id=1, source_target_pairs={{0,6},{1,7},{2,4},{3,5},{4,2},{5,3},{6,0},{7,1},{8,14},{9,15},{10,... | collective-permute-start | bytes 614408 | tf_op jit(solution)/shard_map/ppermute | solution.py:299
  210.3 10.9 %collective-permute-start.61 = (bf16[32,3200]{1,0:T(8,128)(2,1)S(1)}, bf16[32,3200]{1,0:T(8,128)(2,1)S(1)}, u32[]{:S(2)}, u32[]{:S(2)}) collective-permute-start(bf16[32,3200]{1,0:T(8,128)(2,1)S(1)} %get-tuple-element.213), channel_id=1, source_target_pairs={{0,2},{1,3},{2,0},{3,1},{4,6},{5,7},{6,4},{7,5},{8,10},{9,11},{10,... | collective-permute-start | bytes 614408 | tf_op jit(solution)/shard_map/ppermute | solution.py:299
  221.2 3.4 %collective-permute-start.63 = (bf16[32,3200]{1,0:T(8,128)(2,1)S(1)}, bf16[32,3200]{1,0:T(8,128)(2,1)S(1)}, u32[]{:S(2)}, u32[]{:S(2)}) collective-permute-start(bf16[32,3200]{1,0:T(8,128)(2,1)S(1)} %collective-permute-done.54.refs_1_), channel_id=1, source_target_pairs={{0,1},{1,0},{2,3},{3,2},{4,5},{5,4},{6,7},{7,6},{8,9},{9,8},{10,11... | collective-permute-start | bytes 614408 | tf_op jit(solution)/shard_map/ppermute | solution.py:305
  221.7 2.9 %collective-permute-start.64 = (bf16[32,3200]{1,0:T(8,128)(2,1)S(1)}, bf16[32,3200]{1,0:T(8,128)(2,1)S(1)}, u32[]{:S(2)}, u32[]{:S(2)}) collective-permute-start(bf16[32,3200]{1,0:T(8,128)(2,1)S(1)} %collective-permute-done.55.refs_2_), channel_id=1, source_target_pairs={{0,1},{1,0},{2,3},{3,2},{4,5},{5,4},{6,7},{7,6},{8,9},{9,8},{10,11... | collective-permute-start | bytes 614408 | tf_op jit(solution)/shard_map/ppermute | solution.py:305
  221.7 2.9 %collective-permute-start.65 = (bf16[32,3200]{1,0:T(8,128)(2,1)}, bf16[32,3200]{1,0:T(8,128)(2,1)S(1)}, u32[]{:S(2)}, u32[]{:S(2)}) collective-permute-start(bf16[32,3200]{1,0:T(8,128)(2,1)} %collective-permute-done.60.refs_3_), channel_id=1, source_target_pairs={{0,1},{1,0},{2,3},{3,2},{4,5},{5,4},{6,7},{7,6},{8,9},{9,8},{10,11... | collective-permute-start | bytes 614408 | tf_op jit(solution)/shard_map/ppermute | solution.py:305
  222.2 17.9 %collective-permute-start.66 = (bf16[32,3200]{1,0:T(8,128)(2,1)S(1)}, bf16[32,3200]{1,0:T(8,128)(2,1)S(1)}, u32[]{:S(2)}, u32[]{:S(2)}) collective-permute-start(bf16[32,3200]{1,0:T(8,128)(2,1)S(1)} %get-tuple-element.221), channel_id=1, source_target_pairs={{0,4},{1,5},{2,6},{3,7},{4,0},{5,1},{6,2},{7,3},{8,12},{9,13},{10,... | collective-permute-start | bytes 614408 | tf_op jit(solution)/shard_map/ppermute | solution.py:299
  222.7 17.4 %collective-permute-start.67 = (bf16[32,3200]{1,0:T(8,128)(2,1)S(1)}, bf16[32,3200]{1,0:T(8,128)(2,1)S(1)}, u32[]{:S(2)}, u32[]{:S(2)}) collective-permute-start(bf16[32,3200]{1,0:T(8,128)(2,1)S(1)} %get-tuple-element.222), channel_id=1, source_target_pairs={{0,6},{1,7},{2,4},{3,5},{4,2},{5,3},{6,0},{7,1},{8,14},{9,15},{10,... | collective-permute-start | bytes 614408 | tf_op jit(solution)/shard_map/ppermute | solution.py:299
  242.9 17.6 %collective-permute-start.69 = (bf16[32,3200]{1,0:T(8,128)(2,1)S(1)}, bf16[32,3200]{1,0:T(8,128)(2,1)S(1)}, u32[]{:S(2)}, u32[]{:S(2)}) collective-permute-start(bf16[32,3200]{1,0:T(8,128)(2,1)S(1)} %get-tuple-element.279), channel_id=1, source_target_pairs={{0,4},{1,5},{2,6},{3,7},{4,0},{5,1},{6,2},{7,3},{8,12},{9,13},{10,... | collective-permute-start | bytes 614408 | tf_op jit(solution)/shard_map/ppermute | solution.py:299
  244.5 16.0 %collective-permute-start.70 = (bf16[32,3200]{1,0:T(8,128)(2,1)S(1)}, bf16[32,3200]{1,0:T(8,128)(2,1)S(1)}, u32[]{:S(2)}, u32[]{:S(2)}) collective-permute-start(bf16[32,3200]{1,0:T(8,128)(2,1)S(1)} %get-tuple-element.278), channel_id=1, source_target_pairs={{0,6},{1,7},{2,4},{3,5},{4,2},{5,3},{6,0},{7,1},{8,14},{9,15},{10,... | collective-permute-start | bytes 614408 | tf_op jit(solution)/shard_map/ppermute | solution.py:299
  246.4 14.7 %collective-permute-start.71 = (bf16[32,3200]{1,0:T(8,128)(2,1)S(1)}, bf16[32,3200]{1,0:T(8,128)(2,1)S(1)}, u32[]{:S(2)}, u32[]{:S(2)}) collective-permute-start(bf16[32,3200]{1,0:T(8,128)(2,1)S(1)} %get-tuple-element.277), channel_id=1, source_target_pairs={{0,2},{1,3},{2,0},{3,1},{4,6},{5,7},{6,4},{7,5},{8,10},{9,11},{10,... | collective-permute-start | bytes 614408 | tf_op jit(solution)/shard_map/ppermute | solution.py:299
  (52 other events, 287.1 us)
